TPU v7x, 32 devices: a whole 2x2x4 slice. The times are simulated.
32 devices in a mesh: groups: 2 (over x), node: 16 (over z, y, core).
Axes of the slice: x: 2, y: 2, z: 4, core: 2. Of those that a mesh axis runs over, the one named last changes fastest.
Arguments:
- tokens: bfloat16 [1024, 3584], P(('groups', 'node')), parts along dimension 0, may hold values from -6 to 6
- routes: int32 [1024, 8], P(('groups', 'node')), parts along dimension 0, may hold values from 0 to 15, all different within a row; in each aligned block of 32 rows (0 to 31, 32 to 63, ...) at most 32 rows name the same one
- gates: float32 [1024, 8], P(('groups', 'node')), parts along dimension 0, may hold values from 0.1 to 0.5
- w_gate: bfloat16 [16, 3584, 1024], P('node'), may hold values from -0.09375 to 0.09375
- w_up: bfloat16 [16, 3584, 1024], P('node'), may hold values from -0.09375 to 0.09375
- w_down: bfloat16 [16, 1024, 3584], P('node'), may hold values from -0.1875 to 0.1875
Outputs:
- mixed: bfloat16 [1024, 3584], P(('groups', 'node')), parts along dimension 0
There are 2 independent parts, one for each index of `groups`. A program takes and returns all parts, laid end to end along the dimension named above; an argument that names none is the same for every part. Nothing has to cross between parts.
Inputs may be any that keep to these rules, and one draw needn't show every extreme that they name: `routes`: each token names 8 different experts; at most 32 of the tokens of one device name the same expert, and exactly 32 do so for some expert and device.
All inputs are finite; a program needn't handle non-finite values.
Results may differ from a plain program's by a relative error of at most 0.0057.
Values may be sent and summed in bfloat16 or wider, within the bound.
No kernel may reach another device: no remote copies, remote signals or barrier semaphores. Data moves between devices by JAX's collectives and lax.ppermute only.
A program may use at most 128 MiB of HBM per device.

v0:
```python
import jax
import jax.numpy as jnp
from jax import lax
from jax.sharding import PartitionSpec as P


def local(tokens, routes, gates, w_gate, w_up, w_down):
    experts = lax.axis_size("node")
    tok_rows, model_width = tokens.shape
    top_count = routes.shape[1]
    slot_count = 2 * tok_rows * top_count // experts
    gate_mat = w_gate[0]
    up_mat = w_up[0]
    down_mat = w_down[0]
    expert_ids = jnp.arange(experts, dtype=jnp.int32)
    gathered = lax.all_gather(tokens, "node", axis=0, tiled=True)
    table = jnp.sum(
        jnp.where(routes[:, :, None] == expert_ids[None, None, :], gates[:, :, None], 0.0), axis=1
    )
    all_table = lax.all_gather(table, "node", axis=0, tiled=True)
    myself = lax.axis_index("node")
    column = jnp.sum(jnp.where(expert_ids[None, :] == myself, all_table, 0.0), axis=1)
    routed = column > 0.0
    rank = jnp.cumsum(routed.astype(jnp.int32)) - 1
    capacity = experts * slot_count
    cap_range = jnp.arange(capacity, dtype=jnp.int32)
    picker = ((rank[None, :] == cap_range[:, None]) & routed[None, :]).astype(jnp.bfloat16)
    rows = jnp.dot(picker, gathered, preferred_element_type=jnp.float32).astype(jnp.bfloat16)
    gate = jnp.dot(rows, gate_mat, preferred_element_type=jnp.float32)
    upper = jnp.dot(rows, up_mat, preferred_element_type=jnp.float32)
    hidden = (jax.nn.silu(gate) * upper).astype(jnp.bfloat16)
    produced = jnp.dot(hidden, down_mat, preferred_element_type=jnp.float32).astype(jnp.bfloat16)
    chosen = ((rank[:, None] == cap_range[None, :]) & routed[:, None]).astype(jnp.bfloat16)
    picked_rows = jnp.dot(chosen, produced, preferred_element_type=jnp.float32)
    mixed = lax.psum_scatter(column[:, None] * picked_rows, "node", scatter_dimension=0, tiled=True)
    return mixed.astype(jnp.bfloat16)


def solution(mesh):
    in_specs = (
        P(("groups", "node"), None),
        P(("groups", "node"), None),
        P(("groups", "node"), None),
        P("node", None, None),
        P("node", None, None),
        P("node", None, None),
    )
    out_specs = P(("groups", "node"), None)
    return jax.shard_map(local, mesh=mesh, in_specs=in_specs, out_specs=out_specs, check_vma=False)
```

profile of v0, /device:TPU:0, one launch (start us, length us, event | category | flops | bytes accessed | tf_op | source)
XLA Modules:
  0.0 193.0 jit_solution(3109323428464466137)
XLA Ops:
  6.5 0.0 all-gather.3.cloned.1.call-start
  6.5 0.7 all-gather.3.cloned.1.call-update
  7.3 0.0 reduce-scatter.2.cloned.1.call-start
  7.3 0.7 select_reduce_fusion
  8.0 23.5 %all-gather = f32[16,32,16]{1,2,0:T(8,128)S(1)} all-gather(f32[1,32,16]{1,2,0:T(8,128)S(1)} %bitcast.26), channel_id=1, replica_groups=mesh['groups'=2,'node'=16] {'node'}, dimensions={0}, use_global_device_ids=true | all-gather | bytes 34816 | tf_op jit(solution)/shard_map/all_gather | solution.py:20
  31.6 0.1 reshape.57
  31.7 0.1 select_reduce_fusion.1
  31.8 0.3 reduce-window.9
  32.1 0.1 slice.7
  32.2 0.1 slice_reduce_fusion
  32.3 0.1 add_bitcast_fusion
  32.4 28.0 %all-gather.3.cloned.1.call-done = bf16[512,3584]{1,0:T(8,128)(2,1)} async-done(((bf16[32,3584]{1,0:T(8,128)(2,1)}), bf16[512,3584]{1,0:T(8,128)(2,1)}) %all-gather.3.cloned.1.call-update) | async-done | bytes 3670032 | tf_op jit(solution)/shard_map/all_gather | solution.py:16
  60.3 0.0 copy-start
  60.3 4.2 %convolution_convert_fusion = bf16[512,3584]{1,0:T(8,128)(2,1)S(1)} fusion(bf16[512,3584]{1,0:T(8,128)(2,1)} %all-gather.3.cloned.1.call-done, s32[512]{0:T(512)S(1)} %add_bitcast_fusion, pred[512]{0:T(512)(128)(4,1)S(1)} %get-tuple-element.6), kind=kOutput, calls=%fused_computation.8 | convolution fusion | flops 1881407488 | bytes 7342592 | tf_op jit(solution)/shard_map/dot_general | solution.py:28
  64.6 0.0 copy-start.1
  64.6 1.8 copy-done.1
  66.4 0.0 copy-done
  66.4 3.9 %fusion.2 = f32[512,1024]{1,0:T(8,128)S(1)} fusion(bf16[512,3584]{1,0:T(8,128)(2,1)S(1)} %convolution_convert_fusion, bf16[1,3584,1024]{2,1,0:T(8,128)(2,1)S(1)} %copy-done), kind=kOutput, calls=%fused_computation.2 | convolution fusion | flops 3758096384 | bytes 13107200 | tf_op jit(solution)/shard_map/dot_general | solution.py:30
  70.3 16.1 %fusion.6 = bf16[512,3584]{1,0:T(8,128)(2,1)} fusion(bf16[1,1024,3584]{2,1,0:T(8,128)(2,1)} %param.11, f32[512,1024]{1,0:T(8,128)S(1)} %fusion.2, bf16[512,3584]{1,0:T(8,128)(2,1)} %copy-done.1, bf16[1,3584,1024]{2,1,0:T(8,128)(2,1)} %param.9), kind=kOutput, calls=%fused_computation.7 | convolution fusion | flops 7521173504 | bytes 24117248 | tf_op jit(solution)/shard_map/dot_general | solution.py:32
  86.5 7.1 %convolution_multiply_fusion = f32[512,3584]{1,0:T(8,128)} fusion(bf16[512,3584]{1,0:T(8,128)(2,1)} %fusion.6, f32[512]{0:T(512)S(1)} %select_reduce_fusion.1, s32[512]{0:T(512)S(1)} %add_bitcast_fusion, pred[512]{0:T(512)(128)(4,1)S(1)} %get-tuple-element.6), kind=kOutput, calls=%fused_computation.6 | convolution fusion | flops 1881407488 | bytes 11014656 | tf_op jit(solution)/shard_map/dot_general | solution.py:34
  93.6 0.0 reduce-scatter.2.cloned.1.call-update
  93.6 90.8 %reduce-scatter.2.cloned.1.call-done = f32[32,3584]{1,0:T(8,128)} async-done(((f32[512,3584]{1,0:T(8,128)}), f32[32,3584]{1,0:T(8,128)}) %reduce-scatter.2.cloned.1.call-update) | async-done | bytes 458768 | tf_op jit(solution)/shard_map/reduce_scatter | solution.py:35
  184.5 1.7 convert_element_type.26
  (4 shorter events, 0.1 us)
Async XLA Ops:
  6.5 53.8 %all-gather.3.cloned.1.call-start = ((), (), s32[]{:S(2)}) async-start(), calls=%async_computation.1 | async-start | bytes 3899392 | tf_op jit(solution)/shard_map/all_gather | solution.py:16
  7.3 177.2 %reduce-scatter.2.cloned.1.call-start = ((), (), s32[]{:S(2)}) async-start(), calls=%async_computation.2 | async-start | bytes 7798784 | tf_op jit(solution)/shard_map/reduce_scatter | solution.py:35
  60.3 6.1 %copy-start = (bf16[1,3584,1024]{2,1,0:T(8,128)(2,1)S(1)}, bf16[1,3584,1024]{2,1,0:T(8,128)(2,1)}, u32[]{:S(2)}) copy-start(bf16[1,3584,1024]{2,1,0:T(8,128)(2,1)} %param.10) | copy-start | bytes 22020100
  64.6 1.8 copy-start.1
Sparse Core Ops, SparseCore 0:
  9.6 50.6 all-gather.2
  93.8 90.6 reduce-scatter.1
where the time goes:
time: 193 us
  waiting for transfers between devices  120 us (62%)
  matrix products  31.4 us (16%)
  blocking collectives  23.5 us (12%)
  between operations  13.4 us (7%)
  other arithmetic  2.97 us (2%)
  local copies, waits for them, and re-layouts  2.13 us (1%)
    reduce_scatter x1, waiting for transfers between devices, local(): lax.psum_scatter(column[:, None] * picked_rows, 'node', scatter_dimension...  90.8 us
    all_gather x1, waiting for transfers between devices, local(): gathered = lax.all_gather(tokens, 'node', axis=0, tiled=True)  28 us
    all_gather x1, blocking collectives, local(): all_table = lax.all_gather(table, 'node', axis=0, tiled=True)  23.5 us
    dot_general x1, matrix products, local(): jnp.dot(hidden, down_mat, preferred_element_type=jnp.float32)  16.1 us
    dot_general x1, matrix products, local(): picked_rows = jnp.dot(chosen, produced, preferred_element_type=jnp.float32)  7.14 us
    dot_general x1, matrix products, local(): jnp.dot(picker, gathered, preferred_element_type=jnp.float32)  4.24 us
    dot_general x1, matrix products, local(): upper = jnp.dot(rows, up_mat, preferred_element_type=jnp.float32)  3.94 us
  transfers between devices with their start and end apart: 2, of which 2 were waited for; matrix products, arithmetic and copies ran while one was open for 1% of the time, Pallas kernels for 0%

commit v1 on v0

v1 whole, which is shorter than its diff:
```python
import functools

import jax
import jax.numpy as jnp
from jax import lax
from jax.experimental import pallas as pl
from jax.experimental.pallas import tpu as pltpu
from jax.sharding import PartitionSpec as P

F32, BF16 = jnp.float32, jnp.bfloat16


def chip_layout(mesh):
    names = list(mesh.axis_names)
    count = mesh.shape["node"]
    row = mesh.devices.transpose([names.index(n) for n in names if n != "node"] + [names.index("node")])
    row = list(row.reshape(-1, count)[0])
    where = [tuple(getattr(d, "coords", None) or (i // 2,)) for i, d in enumerate(row)]
    cores = 2 if count % 2 == 0 and all(where[i] == where[i + 1] for i in range(0, count, 2)) else 1
    chips = where[::cores]
    order = list(range(len(chips)))
    axes = [a for a in range(len(chips[0])) if len({c[a] for c in chips}) > 1]
    if len(axes) == 2:
        short, long = sorted(axes, key=lambda a: len({c[a] for c in chips}))
        low = min(c[short] for c in chips)
        if len({c[short] for c in chips}) == 2:
            order.sort(key=lambda i: (chips[i][short], chips[i][long] if chips[i][short] == low else -chips[i][long]))
    return cores, order


def pack_kernel(experts, tok_ref, routes_ref, gates_ref, out_ref):
    rows, width = tok_ref.shape
    extra = out_ref.shape[1] - width
    lane = lax.broadcasted_iota(jnp.int32, (rows, extra), 1)
    expert, piece = lax.rem(lane, experts), lax.div(lane, experts)
    weight = jnp.zeros((rows, extra), F32)
    for k in range(routes_ref.shape[1]):
        weight += jnp.where(routes_ref[:, k : k + 1] == expert, gates_ref[:, k : k + 1], 0.0)
    high = weight.astype(BF16).astype(F32)
    middle = (weight - high).astype(BF16).astype(F32)
    low = weight - high - middle
    table = jnp.where(piece == 0, high, jnp.where(piece == 1, middle, jnp.where(piece == 2, low, 0.0)))
    out_ref[:, :width] = tok_ref[...]
    out_ref[:, width:] = table.astype(BF16)


def pack(tokens, routes, gates, experts):
    rows, width = tokens.shape
    extra = pl.cdiv(3 * experts, 128) * 128
    return pl.pallas_call(
        functools.partial(pack_kernel, experts),
        out_shape=jax.ShapeDtypeStruct((rows, width + extra), BF16),
    )(tokens, routes, gates)


def ffn_kernel(count, rows, experts, n_ff, me_ref, *refs):
    blocks, (gate_ref, up_ref, down_ref, mine_ref, other_ref, x_ref, w_ref, h_ref) = refs[:count], refs[count:]
    i = pl.program_id(0)
    width = x_ref.shape[1]
    half = mine_ref.shape[0]

    @pl.when(i == 0)
    def _():
        for at, ref in enumerate(blocks):
            x_ref[at * rows : (at + 1) * rows, :] = ref[:, :width]
            table = ref[:, width:].astype(F32)
            lane = lax.broadcasted_iota(jnp.int32, table.shape, 1)
            own = lax.rem(lane, experts) == me_ref[0]
            w_ref[at * rows : (at + 1) * rows, :] = jnp.sum(jnp.where(own, table, 0.0), axis=1, keepdims=True)

    @pl.when(i < n_ff)
    def _():
        x = x_ref[...]
        gate = jnp.dot(x, gate_ref[0], preferred_element_type=F32)
        upper = jnp.dot(x, up_ref[0], preferred_element_type=F32)
        h_ref[jnp.minimum(i, n_ff - 1)] = (gate / (1.0 + jnp.exp(-gate)) * upper).astype(BF16)

    @pl.when(i >= n_ff)
    def _():
        tile = h_ref.shape[2]
        out = jnp.dot(h_ref[0], down_ref[0, :tile], preferred_element_type=F32)
        for j in range(1, n_ff):
            out += jnp.dot(h_ref[j], down_ref[0, j * tile : (j + 1) * tile], preferred_element_type=F32)
        out = out * w_ref[...]
        mine_ref[...] = out[:half]
        if count * rows > half:
            other_ref[...] = out[half:].astype(BF16)


def ffn(blocks, mine, me, experts, w_gate, w_up, w_down):
    count, rows = len(blocks), blocks[0].shape[0]
    _, width, ff = w_gate.shape
    tile_ff = 256 if ff % 256 == 0 else ff
    tile_d = next(t for t in (512, 256, 128, width) if width % t == 0)
    n_ff, n_d = ff // tile_ff, width // tile_d
    total, half = count * rows, mine * rows
    first = lambda i: (0, 0, jnp.minimum(i, n_ff - 1))
    second = lambda i: (0, jnp.maximum(i - n_ff, 0))
    return pl.pallas_call(
        functools.partial(ffn_kernel, count, rows, experts, n_ff),
        grid=(n_ff + n_d,),
        out_shape=[
            jax.ShapeDtypeStruct((half, width), F32),
            jax.ShapeDtypeStruct((total - half, width), BF16),
        ],
        in_specs=[pl.BlockSpec(memory_space=pltpu.SMEM)]
        + [pl.BlockSpec(b.shape, lambda i: (0, 0)) for b in blocks]
        + [
            pl.BlockSpec((1, width, tile_ff), first),
            pl.BlockSpec((1, width, tile_ff), first),
            pl.BlockSpec((1, ff, tile_d), lambda i: (0, 0, jnp.maximum(i - n_ff, 0))),
        ],
        out_specs=[pl.BlockSpec((half, tile_d), second), pl.BlockSpec((total - half, tile_d), second)],
        scratch_shapes=[
            pltpu.VMEM((total, width), BF16),
            pltpu.VMEM((total, 1), F32),
            pltpu.VMEM((n_ff, total, tile_ff), BF16),
        ],
        compiler_params=pltpu.CompilerParams(vmem_limit_bytes=40 * 2**20),
        cost_estimate=pl.CostEstimate(
            flops=6 * total * width * ff, bytes_accessed=6 * width * ff, transcendentals=total * ff
        ),
    )(me, *blocks, w_gate, w_up, w_down)


def local(cores, order, tokens, routes, gates, w_gate, w_up, w_down):
    chips = len(order)
    experts = chips * cores
    rows, width = tokens.shape
    me = lax.axis_index("node").astype(jnp.int32).reshape(1)
    forth = [(order[i] * cores + c, order[(i + 1) % chips] * cores + c) for i in range(chips) for c in range(cores)]
    back = [(b, a) for a, b in forth]
    swap = [(chip * cores + c, chip * cores + 1 - c) for chip in range(chips) for c in range(cores)]
    right = lambda a: lax.ppermute(a, "node", forth)
    left = lambda a: lax.ppermute(a, "node", back)
    sibling = lambda a: lax.ppermute(a, "node", swap)

    own = pack(tokens, routes, gates, experts)
    far = chips // 2
    cut = rows // 2
    got = {0: own}
    for d in range(1, far):
        got[-d] = right(got[-(d - 1)])
        got[d] = left(got[d - 1])
    ends = (right(got[1 - far][:cut]), left(got[far - 1][cut:]))
    got[far] = jnp.concatenate(ends, axis=0)
    twin = {d: sibling(got[d]) for d in got}

    run = lambda at: ffn([got[d] for d in at] + [twin[d] for d in at], len(at), me, experts, w_gate, w_up, w_down)
    late = [far] + [s * (far - 1) for s in (1, -1)]
    early = [d for d in sorted(got, key=abs) if d not in late]
    mine, theirs = {}, {}
    for at in (early, late):
        kept, sent = run(at)
        sent = sibling(sent)
        for j, d in enumerate(at):
            mine[d] = kept[j * rows : (j + 1) * rows]
            theirs[d] = sent[j * rows : (j + 1) * rows]

    both = lambda d: mine[d] + theirs[d].astype(F32)
    end = both(far).astype(BF16)
    a, b = right(end[:cut]), left(end[cut:])
    for d in range(far - 1, 0, -1):
        up, down = both(d), both(-d)
        if d == far - 1:
            up = jnp.concatenate([up[:cut] + a.astype(F32), up[cut:]], axis=0)
            down = jnp.concatenate([down[:cut], down[cut:] + b.astype(F32)], axis=0)
        else:
            up, down = up + a.astype(F32), down + b.astype(F32)
        a, b = right(up.astype(BF16)), left(down.astype(BF16))
    return (both(0) + a.astype(F32) + b.astype(F32)).astype(BF16)


def solution(mesh):
    cores, order = chip_layout(mesh)
    in_specs = (
        P(("groups", "node"), None),
        P(("groups", "node"), None),
        P(("groups", "node"), None),
        P("node", None, None),
        P("node", None, None),
        P("node", None, None),
    )
    out_specs = P(("groups", "node"), None)
    body = functools.partial(local, cores, order)
    return jax.shard_map(body, mesh=mesh, in_specs=in_specs, out_specs=out_specs, check_vma=False)
```

time: 193 us -> 98.9 us (0.51)
  waiting for transfers between devices: 120 us -> 41.1 us
  matrix products: 31.4 us -> 0 us
  Pallas kernels: 0 us -> 29.3 us
  blocking collectives: 23.5 us -> 0 us
  starting transfers between devices: 0.04 us -> 20.6 us
  between operations: 13.4 us -> 0.16 us
  local copies, waits for them, and re-layouts: 2.13 us -> 5.9 us
    reduce_scatter x1 -> x0, waiting for transfers between devices: 90.8 us -> none  [local(): lax.psum_scatter(column[:, None] * picked_rows, 'node', scatter_dimension...]
    ppermute x0 -> x26, waiting for transfers between devices: none -> 41.1 us  [the longest x8 21.9 us: local(): right = lambda a: lax.ppermute(a, 'node', forth)]
    dot_general x4 -> x0, matrix products: 31.4 us -> none  [the longest x1 16.1 us: local(): jnp.dot(hidden, down_mat, preferred_element_type=jnp.float32)]
    pallas_call x0 -> x3, Pallas kernels: none -> 29.3 us  [the longest x2 27.5 us: ffn(): pl.pallas_call(functools.partial(ffn_kernel, count, rows, experts, n_ff),...]
    all_gather x1 -> x0, waiting for transfers between devices: 28 us -> none  [local(): gathered = lax.all_gather(tokens, 'node', axis=0, tiled=True)]
    all_gather x1 -> x0, blocking collectives: 23.5 us -> none  [local(): all_table = lax.all_gather(table, 'node', axis=0, tiled=True)]
    ppermute x0 -> x26, starting transfers between devices: none -> 20.6 us  [the longest x8 13.8 us: local(): right = lambda a: lax.ppermute(a, 'node', forth)]
    unnamed x5 -> x9, local copies, waits for them, and re-layouts: 1.9 us -> 5.82 us
  transfers between devices with their start and end apart: 2 -> 26, of which waited for: 2 -> 13; matrix products, arithmetic and copies ran while one was open for 1% -> 0% of each run, Pallas kernels for 0% -> 15%
where the time goes in v1:
time: 98.9 us; the launch traced here: 98.4 us
  waiting for transfers between devices  41.1 us (42%)
  Pallas kernels  29.3 us (30%)
  starting transfers between devices  20.6 us (21%)
  local copies, waits for them, and re-layouts  5.9 us (6%)
  other arithmetic  1.27 us (1%)
    pallas_call x2, Pallas kernels, ffn(): pl.pallas_call(functools.partial(ffn_kernel, count, rows, experts, n_ff),...  27.5 us
    ppermute x8, waiting for transfers between devices, local(): right = lambda a: lax.ppermute(a, 'node', forth)  21.9 us
    ppermute x8, waiting for transfers between devices, local(): left = lambda a: lax.ppermute(a, 'node', back)  16.7 us
    ppermute x8, starting transfers between devices, local(): right = lambda a: lax.ppermute(a, 'node', forth)  13.8 us
    unnamed x9, local copies, waits for them, and re-layouts  5.82 us
    ppermute x8, starting transfers between devices, local(): left = lambda a: lax.ppermute(a, 'node', back)  4.75 us
    ppermute x10, waiting for transfers between devices, local(): sibling = lambda a: lax.ppermute(a, 'node', swap)  2.5 us
    ppermute x10, starting transfers between devices, local(): sibling = lambda a: lax.ppermute(a, 'node', swap)  2.1 us
  transfers between devices with their start and end apart: 26, of which 13 were waited for; matrix products, arithmetic and copies ran while one was open for 0% of the time, Pallas kernels for 15%

profile of v1, /device:TPU:0, one launch (start us, length us, event | category | flops | bytes accessed | tf_op | source)
XLA Modules:
  0.0 98.4 jit_solution(10853488395315949797)
XLA Ops:
  0.0 1.4 %copy.7.routes_ref = s32[32,8]{1,0:T(8,128)} copy(s32[32,8]{0,1:T(8,128)} %param.7) | data formatting | bytes 2048 | tf_op args[1]
  1.4 1.4 %copy.8.gates_ref = f32[32,8]{1,0:T(8,128)} copy(f32[32,8]{0,1:T(8,128)} %param.8) | data formatting | bytes 2048 | tf_op args[2]
  2.7 1.8 %shard_map.64.refs_0_ = bf16[32,3712]{1,0:T(8,128)(2,1)} custom-call(bf16[32,3584]{1,0:T(8,128)(2,1)} %tok_ref.1, s32[32,8]{1,0:T(8,128)} %copy.7.routes_ref, f32[32,8]{1,0:T(8,128)} %copy.8.gates_ref), custom_call_target="tpu_custom_call" | custom-call | tf_op jit(solution)/shard_map/pallas_call | solution.py:50
  4.5 3.0 %collective-permute-start = (bf16[32,3712]{1,0:T(8,128)(2,1)}, bf16[32,3712]{1,0:T(8,128)(2,1)S(1)}, u32[]{:S(2)}, u32[]{:S(2)}) collective-permute-start(bf16[32,3712]{1,0:T(8,128)(2,1)} %shard_map.64.refs_0_), channel_id=1, source_target_pairs={{0,4},{1,5},{4,8},{5,9},{8,12},{9,13},{12,14},{13,15},{14,10},{15,... | collective-permute-start | bytes 712712 | tf_op jit(solution)/shard_map/ppermute | solution.py:134
  7.5 5.9 %collective-permute-done.refs_1_ = bf16[32,3712]{1,0:T(8,128)(2,1)S(1)} collective-permute-done((bf16[32,3712]{1,0:T(8,128)(2,1)}, bf16[32,3712]{1,0:T(8,128)(2,1)S(1)}, u32[]{:S(2)}, u32[]{:S(2)}) %collective-permute-start) | collective-permute-done | bytes 237600 | tf_op jit(solution)/shard_map/ppermute | solution.py:134
  13.5 1.8 %collective-permute-start.2 = (bf16[32,3712]{1,0:T(8,128)(2,1)S(1)}, bf16[32,3712]{1,0:T(8,128)(2,1)S(1)}, u32[]{:S(2)}, u32[]{:S(2)}) collective-permute-start(bf16[32,3712]{1,0:T(8,128)(2,1)S(1)} %collective-permute-done.refs_1_), channel_id=1, source_target_pairs={{0,4},{1,5},{4,8},{5,9},{8,12},{9,13},{12,14},{13,15},{14,10},{15,... | collective-permute-start | bytes 712712 | tf_op jit(solution)/shard_map/ppermute | solution.py:134
  15.3 0.2 collective-permute-start.3
  15.5 4.9 %collective-permute-done.2.refs_3_ = bf16[32,3712]{1,0:T(8,128)(2,1)S(1)} collective-permute-done((bf16[32,3712]{1,0:T(8,128)(2,1)S(1)}, bf16[32,3712]{1,0:T(8,128)(2,1)S(1)}, u32[]{:S(2)}, u32[]{:S(2)}) %collective-permute-start.2) | collective-permute-done | bytes 237600 | tf_op jit(solution)/shard_map/ppermute | solution.py:134
  20.4 1.5 %collective-permute-start.10 = (bf16[32,3712]{1,0:T(8,128)(2,1)S(1)}, bf16[32,3712]{1,0:T(8,128)(2,1)S(1)}, u32[]{:S(2)}, u32[]{:S(2)}) collective-permute-start(bf16[32,3712]{1,0:T(8,128)(2,1)S(1)} %collective-permute-done.2.refs_3_), channel_id=1, source_target_pairs={{0,4},{1,5},{4,8},{5,9},{8,12},{9,13},{12,14},{13,15},{14,10},{15,... | collective-permute-start | bytes 712712 | tf_op jit(solution)/shard_map/ppermute | solution.py:134
  21.9 0.5 collective-permute-start.12
  22.5 4.1 %collective-permute-done.10.refs_2_ = bf16[32,3712]{1,0:T(8,128)(2,1)S(1)} collective-permute-done((bf16[32,3712]{1,0:T(8,128)(2,1)S(1)}, bf16[32,3712]{1,0:T(8,128)(2,1)S(1)}, u32[]{:S(2)}, u32[]{:S(2)}) %collective-permute-start.10) | collective-permute-done | bytes 237600 | tf_op jit(solution)/shard_map/ppermute | solution.py:134
  26.6 1.9 %collective-permute-start.11 = (bf16[16,3712]{1,0:T(8,128)(2,1)S(1)}, bf16[16,3712]{1,0:T(8,128)(2,1)S(1)}, u32[]{:S(2)}, u32[]{:S(2)}) collective-permute-start(bf16[16,3712]{1,0:T(8,128)(2,1)S(1)} %slice.101), channel_id=1, source_target_pairs={{0,4},{1,5},{4,8},{5,9},{8,12},{9,13},{12,14},{13,15},{14,10},{15,... | collective-permute-start | bytes 356360 | tf_op jit(solution)/shard_map/ppermute | solution.py:134
  28.5 0.3 collective-permute-start.13
  28.8 0.5 collective-permute-start.16
  29.3 2.2 %collective-permute-done.11 = bf16[16,3712]{1,0:T(8,128)(2,1)S(1)} collective-permute-done((bf16[16,3712]{1,0:T(8,128)(2,1)S(1)}, bf16[16,3712]{1,0:T(8,128)(2,1)S(1)}, u32[]{:S(2)}, u32[]{:S(2)}) %collective-permute-start.11) | collective-permute-done | bytes 118816 | tf_op jit(solution)/shard_map/ppermute | solution.py:134
  31.5 1.9 %collective-permute-done.13 = bf16[16,3712]{1,0:T(8,128)(2,1)S(1)} collective-permute-done((bf16[16,3712]{1,0:T(8,128)(2,1)S(1)}, bf16[16,3712]{1,0:T(8,128)(2,1)S(1)}, u32[]{:S(2)}, u32[]{:S(2)}) %collective-permute-start.13) | collective-permute-done | bytes 118816 | tf_op jit(solution)/shard_map/ppermute | solution.py:135
  33.4 0.1 collective-permute-start.14
  33.5 1.5 %collective-permute-done.14.refs_3_ = bf16[32,3712]{1,0:T(8,128)(2,1)S(1)} collective-permute-done((bf16[32,3712]{1,0:T(8,128)(2,1)S(1)}, bf16[32,3712]{1,0:T(8,128)(2,1)S(1)}, u32[]{:S(2)}, u32[]{:S(2)}) %collective-permute-start.14) | collective-permute-done | bytes 237600 | tf_op jit(solution)/shard_map/ppermute | solution.py:136
  35.0 3.1 %copy-done = bf16[1,3584,1024]{2,1,0:T(8,128)(2,1)S(1)} copy-done((bf16[1,3584,1024]{2,1,0:T(8,128)(2,1)S(1)}, bf16[1,3584,1024]{2,1,0:T(8,128)(2,1)}, u32[]{:S(2)}) %copy-start) | copy-done | bytes 7340056
  38.0 12.9 %shard_map.66 = (f32[96,3584]{1,0:T(8,128)S(1)}, bf16[96,3584]{1,0:T(8,128)(2,1)S(1)}) custom-call(s32[1]{0:T(128)} %bitcast.me_ref, bf16[32,3712]{1,0:T(8,128)(2,1)S(1)} %constant_dynamic-update-slice_fusion.refs_0_, bf16[32,3712]{1,0:T(8,128)(2,1)S(1)} %collective-permute-done.12.refs_1_, bf16[32,3712]{1,0:T(8,128)(2,1)S(1)} %collective-permute-done.10.refs_2_, ...), custom_call_target="tpu_custom_call" | custom-call | flops 4227858432 | bytes 22020096 | tf_op jit(solution)/shard_map/pallas_call | solution.py:99
  50.9 0.2 collective-permute-start.17
  51.2 0.4 collective-permute-start.4
  51.5 0.1 collective-permute-start.6
  51.7 0.4 collective-permute-start.5
  52.0 0.1 collective-permute-start.8
  52.2 1.0 collective-permute-done.17
  53.1 0.1 collective-permute-start.7
  53.3 0.1 convert_add_fusion.1
  53.5 1.6 %collective-permute-start.18 = (bf16[16,3584]{1,0:T(8,128)(2,1)S(1)}, bf16[16,3584]{1,0:T(8,128)(2,1)S(1)}, u32[]{:S(2)}, u32[]{:S(2)}) collective-permute-start(bf16[16,3584]{1,0:T(8,128)(2,1)S(1)} %get-tuple-element.18), channel_id=1, source_target_pairs={{0,4},{1,5},{4,8},{5,9},{8,12},{9,13},{12,14},{13,15},{14,10},{15,... | collective-permute-start | bytes 344072 | tf_op jit(solution)/shard_map/ppermute | solution.py:134
  55.1 14.7 %shard_map.65 = (f32[160,3584]{1,0:T(8,128)S(1)}, bf16[160,3584]{1,0:T(8,128)(2,1)S(1)}) custom-call(s32[1]{0:T(128)} %bitcast.me_ref, bf16[32,3712]{1,0:T(8,128)(2,1)S(1)} %copy-done.2, bf16[32,3712]{1,0:T(8,128)(2,1)S(1)} %collective-permute-done.refs_1_, bf16[32,3712]{1,0:T(8,128)(2,1)S(1)} %collective-permute-done.1.refs_2_, ...), custom_call_target="tpu_custom_call" | custom-call | flops 7046430720 | bytes 22020096 | tf_op jit(solution)/shard_map/pallas_call | solution.py:99
  69.8 0.1 collective-permute-start.9
  70.0 0.5 collective-permute-start.22
  70.5 1.6 %collective-permute-start.19 = (bf16[32,3584]{1,0:T(8,128)(2,1)S(1)}, bf16[32,3584]{1,0:T(8,128)(2,1)S(1)}, u32[]{:S(2)}, u32[]{:S(2)}) collective-permute-start(bf16[32,3584]{1,0:T(8,128)(2,1)S(1)} %pad_maximum_fusion), channel_id=1, source_target_pairs={{0,4},{1,5},{4,8},{5,9},{8,12},{9,13},{12,14},{13,15},{14,10},{15,... | collective-permute-start | bytes 688136 | tf_op jit(solution)/shard_map/ppermute | solution.py:134
  72.2 3.4 %collective-permute-done.22 = bf16[16,3584]{1,0:T(8,128)(2,1)S(1)} collective-permute-done((bf16[16,3584]{1,0:T(8,128)(2,1)S(1)}, bf16[16,3584]{1,0:T(8,128)(2,1)S(1)}, u32[]{:S(2)}, u32[]{:S(2)}) %collective-permute-start.22) | collective-permute-done | bytes 114720 | tf_op jit(solution)/shard_map/ppermute | solution.py:135
  75.6 0.5 collective-permute-start.23
  76.1 2.2 %collective-permute-done.19 = bf16[32,3584]{1,0:T(8,128)(2,1)S(1)} collective-permute-done((bf16[32,3584]{1,0:T(8,128)(2,1)S(1)}, bf16[32,3584]{1,0:T(8,128)(2,1)S(1)}, u32[]{:S(2)}, u32[]{:S(2)}) %collective-permute-start.19) | collective-permute-done | bytes 229408 | tf_op jit(solution)/shard_map/ppermute | solution.py:134
  78.3 0.1 add_convert_fusion.4
  78.3 1.6 %collective-permute-start.20 = (bf16[32,3584]{1,0:T(8,128)(2,1)S(1)}, bf16[32,3584]{1,0:T(8,128)(2,1)S(1)}, u32[]{:S(2)}, u32[]{:S(2)}) collective-permute-start(bf16[32,3584]{1,0:T(8,128)(2,1)S(1)} %add_convert_fusion.4), channel_id=1, source_target_pairs={{0,4},{1,5},{4,8},{5,9},{8,12},{9,13},{12,14},{13,15},{14,10},{15,... | collective-permute-start | bytes 688136 | tf_op jit(solution)/shard_map/ppermute | solution.py:134
  80.0 2.8 %collective-permute-done.23 = bf16[32,3584]{1,0:T(8,128)(2,1)S(1)} collective-permute-done((bf16[32,3584]{1,0:T(8,128)(2,1)S(1)}, bf16[32,3584]{1,0:T(8,128)(2,1)S(1)}, u32[]{:S(2)}, u32[]{:S(2)}) %collective-permute-start.23) | collective-permute-done | bytes 229408 | tf_op jit(solution)/shard_map/ppermute | solution.py:135
  82.8 2.4 %collective-permute-done.20 = bf16[32,3584]{1,0:T(8,128)(2,1)S(1)} collective-permute-done((bf16[32,3584]{1,0:T(8,128)(2,1)S(1)}, bf16[32,3584]{1,0:T(8,128)(2,1)S(1)}, u32[]{:S(2)}, u32[]{:S(2)}) %collective-permute-start.20) | collective-permute-done | bytes 229408 | tf_op jit(solution)/shard_map/ppermute | solution.py:134
  85.2 0.1 add_convert_fusion.3
  85.4 1.3 %collective-permute-start.24 = (bf16[32,3584]{1,0:T(8,128)(2,1)S(1)}, bf16[32,3584]{1,0:T(8,128)(2,1)S(1)}, u32[]{:S(2)}, u32[]{:S(2)}) collective-permute-start(bf16[32,3584]{1,0:T(8,128)(2,1)S(1)} %get-tuple-element.14), channel_id=1, source_target_pairs={{4,0},{5,1},{8,4},{9,5},{12,8},{13,9},{14,12},{15,13},{10,14},{11,... | collective-permute-start | bytes 688136 | tf_op jit(solution)/shard_map/ppermute | solution.py:135
  86.7 0.7 collective-permute-start.21
  87.4 4.0 %collective-permute-done.24 = bf16[32,3584]{1,0:T(8,128)(2,1)S(1)} collective-permute-done((bf16[32,3584]{1,0:T(8,128)(2,1)S(1)}, bf16[32,3584]{1,0:T(8,128)(2,1)S(1)}, u32[]{:S(2)}, u32[]{:S(2)}) %collective-permute-start.24) | collective-permute-done | bytes 229408 | tf_op jit(solution)/shard_map/ppermute | solution.py:135
  91.4 0.1 add_convert_fusion.1
  91.5 1.4 %collective-permute-start.25 = (bf16[32,3584]{1,0:T(8,128)(2,1)S(1)}, bf16[32,3584]{1,0:T(8,128)(2,1)S(1)}, u32[]{:S(2)}, u32[]{:S(2)}) collective-permute-start(bf16[32,3584]{1,0:T(8,128)(2,1)S(1)} %add_convert_fusion.1), channel_id=1, source_target_pairs={{4,0},{5,1},{8,4},{9,5},{12,8},{13,9},{14,12},{15,13},{10,14},{11,... | collective-permute-start | bytes 688136 | tf_op jit(solution)/shard_map/ppermute | solution.py:135
  92.9 4.7 %collective-permute-done.25 = bf16[32,3584]{1,0:T(8,128)(2,1)S(1)} collective-permute-done((bf16[32,3584]{1,0:T(8,128)(2,1)S(1)}, bf16[32,3584]{1,0:T(8,128)(2,1)S(1)}, u32[]{:S(2)}, u32[]{:S(2)}) %collective-permute-start.25) | collective-permute-done | bytes 229408 | tf_op jit(solution)/shard_map/ppermute | solution.py:135
  97.6 0.8 add_convert_fusion
  (31 shorter events, 0.3 us)
Async XLA Ops:
  4.5 9.0 %collective-permute-start = (bf16[32,3712]{1,0:T(8,128)(2,1)}, bf16[32,3712]{1,0:T(8,128)(2,1)S(1)}, u32[]{:S(2)}, u32[]{:S(2)}) collective-permute-start(bf16[32,3712]{1,0:T(8,128)(2,1)} %shard_map.64.refs_0_), channel_id=1, source_target_pairs={{0,4},{1,5},{4,8},{5,9},{8,12},{9,13},{12,14},{13,15},{14,10},{15,... | collective-permute-start | bytes 712712 | tf_op jit(solution)/shard_map/ppermute | solution.py:134
  7.5 7.7 %collective-permute-start.1 = (bf16[32,3712]{1,0:T(8,128)(2,1)}, bf16[32,3712]{1,0:T(8,128)(2,1)S(1)}, u32[]{:S(2)}, u32[]{:S(2)}) collective-permute-start(bf16[32,3712]{1,0:T(8,128)(2,1)} %shard_map.64.refs_0_), channel_id=1, source_target_pairs={{4,0},{5,1},{8,4},{9,5},{12,8},{13,9},{14,12},{15,13},{10,14},{11,... | collective-permute-start | bytes 712712 | tf_op jit(solution)/shard_map/ppermute | solution.py:135
  13.5 7.0 %collective-permute-start.2 = (bf16[32,3712]{1,0:T(8,128)(2,1)S(1)}, bf16[32,3712]{1,0:T(8,128)(2,1)S(1)}, u32[]{:S(2)}, u32[]{:S(2)}) collective-permute-start(bf16[32,3712]{1,0:T(8,128)(2,1)S(1)} %collective-permute-done.refs_1_), channel_id=1, source_target_pairs={{0,4},{1,5},{4,8},{5,9},{8,12},{9,13},{12,14},{13,15},{14,10},{15,... | collective-permute-start | bytes 712712 | tf_op jit(solution)/shard_map/ppermute | solution.py:134
  15.3 6.6 %collective-permute-start.3 = (bf16[32,3712]{1,0:T(8,128)(2,1)S(1)}, bf16[32,3712]{1,0:T(8,128)(2,1)S(1)}, u32[]{:S(2)}, u32[]{:S(2)}) collective-permute-start(bf16[32,3712]{1,0:T(8,128)(2,1)S(1)} %collective-permute-done.1.refs_2_), channel_id=1, source_target_pairs={{4,0},{5,1},{8,4},{9,5},{12,8},{13,9},{14,12},{15,13},{10,14},{11,... | collective-permute-start | bytes 712712 | tf_op jit(solution)/shard_map/ppermute | solution.py:135
  20.4 6.2 %collective-permute-start.10 = (bf16[32,3712]{1,0:T(8,128)(2,1)S(1)}, bf16[32,3712]{1,0:T(8,128)(2,1)S(1)}, u32[]{:S(2)}, u32[]{:S(2)}) collective-permute-start(bf16[32,3712]{1,0:T(8,128)(2,1)S(1)} %collective-permute-done.2.refs_3_), channel_id=1, source_target_pairs={{0,4},{1,5},{4,8},{5,9},{8,12},{9,13},{12,14},{13,15},{14,10},{15,... | collective-permute-start | bytes 712712 | tf_op jit(solution)/shard_map/ppermute | solution.py:134
  21.9 6.6 %collective-permute-start.12 = (bf16[32,3712]{1,0:T(8,128)(2,1)S(1)}, bf16[32,3712]{1,0:T(8,128)(2,1)S(1)}, u32[]{:S(2)}, u32[]{:S(2)}) collective-permute-start(bf16[32,3712]{1,0:T(8,128)(2,1)S(1)} %collective-permute-done.3.refs_4_), channel_id=1, source_target_pairs={{4,0},{5,1},{8,4},{9,5},{12,8},{13,9},{14,12},{15,13},{10,14},{11,... | collective-permute-start | bytes 712712 | tf_op jit(solution)/shard_map/ppermute | solution.py:135
  26.6 4.9 %collective-permute-start.11 = (bf16[16,3712]{1,0:T(8,128)(2,1)S(1)}, bf16[16,3712]{1,0:T(8,128)(2,1)S(1)}, u32[]{:S(2)}, u32[]{:S(2)}) collective-permute-start(bf16[16,3712]{1,0:T(8,128)(2,1)S(1)} %slice.101), channel_id=1, source_target_pairs={{0,4},{1,5},{4,8},{5,9},{8,12},{9,13},{12,14},{13,15},{14,10},{15,... | collective-permute-start | bytes 356360 | tf_op jit(solution)/shard_map/ppermute | solution.py:134
  28.5 4.9 %collective-permute-start.13 = (bf16[16,3712]{1,0:T(8,128)(2,1)S(1)}, bf16[16,3712]{1,0:T(8,128)(2,1)S(1)}, u32[]{:S(2)}, u32[]{:S(2)}) collective-permute-start(bf16[16,3712]{1,0:T(8,128)(2,1)S(1)} %slice.102), channel_id=1, source_target_pairs={{4,0},{5,1},{8,4},{9,5},{12,8},{13,9},{14,12},{15,13},{10,14},{11,... | collective-permute-start | bytes 356360 | tf_op jit(solution)/shard_map/ppermute | solution.py:135
  28.8 4.7 %collective-permute-start.15 = (bf16[32,3712]{1,0:T(8,128)(2,1)S(1)}, bf16[32,3712]{1,0:T(8,128)(2,1)S(1)}, u32[]{:S(2)}, u32[]{:S(2)}) collective-permute-start(bf16[32,3712]{1,0:T(8,128)(2,1)S(1)} %collective-permute-done.12.refs_1_), channel_id=1, source_target_pairs={{0,1},{1,0},{2,3},{3,2},{4,5},{5,4},{6,7},{7,6},{8,9},{9,8},{10,11... | collective-permute-start | bytes 712712 | tf_op jit(solution)/shard_map/ppermute | solution.py:136
  28.8 4.7 %collective-permute-start.16 = (bf16[32,3712]{1,0:T(8,128)(2,1)S(1)}, bf16[32,3712]{1,0:T(8,128)(2,1)S(1)}, u32[]{:S(2)}, u32[]{:S(2)}) collective-permute-start(bf16[32,3712]{1,0:T(8,128)(2,1)S(1)} %collective-permute-done.10.refs_2_), channel_id=1, source_target_pairs={{0,1},{1,0},{2,3},{3,2},{4,5},{5,4},{6,7},{7,6},{8,9},{9,8},{10,11... | collective-permute-start | bytes 712712 | tf_op jit(solution)/shard_map/ppermute | solution.py:136
  33.4 1.6 %collective-permute-start.14 = (bf16[32,3712]{1,0:T(8,128)(2,1)S(1)}, bf16[32,3712]{1,0:T(8,128)(2,1)S(1)}, u32[]{:S(2)}, u32[]{:S(2)}) collective-permute-start(bf16[32,3712]{1,0:T(8,128)(2,1)S(1)} %constant_dynamic-update-slice_fusion.refs_0_), channel_id=1, source_target_pairs={{0,1},{1,0},{2,3},{3,2},{4,5},{5,4},{6,7},{7,6},{8,9},{9,8},{10,11... | collective-permute-start | bytes 712712 | tf_op jit(solution)/shard_map/ppermute | solution.py:136
  35.0 3.1 %copy-start = (bf16[1,3584,1024]{2,1,0:T(8,128)(2,1)S(1)}, bf16[1,3584,1024]{2,1,0:T(8,128)(2,1)}, u32[]{:S(2)}) copy-start(bf16[1,3584,1024]{2,1,0:T(8,128)(2,1)} %refs_6_.1) | copy-start | bytes 22020100
  38.0 13.1 %copy-start.2 = (bf16[32,3712]{1,0:T(8,128)(2,1)S(1)}, bf16[32,3712]{1,0:T(8,128)(2,1)}, u32[]{:S(2)}) copy-start(bf16[32,3712]{1,0:T(8,128)(2,1)} %shard_map.64.refs_0_) | copy-start | bytes 712708
  38.0 17.1 %copy-start.1 = (bf16[1,3584,1024]{2,1,0:T(8,128)(2,1)S(1)}, bf16[1,3584,1024]{2,1,0:T(8,128)(2,1)}, u32[]{:S(2)}) copy-start(bf16[1,3584,1024]{2,1,0:T(8,128)(2,1)} %refs_6_.1) | copy-start | bytes 22020100
  50.9 2.2 %collective-permute-start.17 = (bf16[96,3584]{1,0:T(8,128)(2,1)S(1)}, bf16[96,3584]{1,0:T(8,128)(2,1)S(1)}, u32[]{:S(2)}, u32[]{:S(2)}) collective-permute-start(bf16[96,3584]{1,0:T(8,128)(2,1)S(1)} %get-tuple-element.12), channel_id=1, source_target_pairs={{0,1},{1,0},{2,3},{3,2},{4,5},{5,4},{6,7},{7,6},{8,9},{9,8},{10,11... | collective-permute-start | bytes 2064392 | tf_op jit(solution)/shard_map/ppermute | solution.py:136
  51.2 2.3 %collective-permute-start.4 = (bf16[32,3712]{1,0:T(8,128)(2,1)S(1)}, bf16[32,3712]{1,0:T(8,128)(2,1)S(1)}, u32[]{:S(2)}, u32[]{:S(2)}) collective-permute-start(bf16[32,3712]{1,0:T(8,128)(2,1)S(1)} %copy-done.2), channel_id=1, source_target_pairs={{0,1},{1,0},{2,3},{3,2},{4,5},{5,4},{6,7},{7,6},{8,9},{9,8},{10,11... | collective-permute-start | bytes 712712 | tf_op jit(solution)/shard_map/ppermute | solution.py:136
  51.5 3.6 %collective-permute-start.6 = (bf16[32,3712]{1,0:T(8,128)(2,1)S(1)}, bf16[32,3712]{1,0:T(8,128)(2,1)S(1)}, u32[]{:S(2)}, u32[]{:S(2)}) collective-permute-start(bf16[32,3712]{1,0:T(8,128)(2,1)S(1)} %collective-permute-done.1.refs_2_), channel_id=1, source_target_pairs={{0,1},{1,0},{2,3},{3,2},{4,5},{5,4},{6,7},{7,6},{8,9},{9,8},{10,11... | collective-permute-start | bytes 712712 | tf_op jit(solution)/shard_map/ppermute | solution.py:136
  51.7 3.4 %collective-permute-start.5 = (bf16[32,3712]{1,0:T(8,128)(2,1)S(1)}, bf16[32,3712]{1,0:T(8,128)(2,1)S(1)}, u32[]{:S(2)}, u32[]{:S(2)}) collective-permute-start(bf16[32,3712]{1,0:T(8,128)(2,1)S(1)} %collective-permute-done.refs_1_), channel_id=1, source_target_pairs={{0,1},{1,0},{2,3},{3,2},{4,5},{5,4},{6,7},{7,6},{8,9},{9,8},{10,11... | collective-permute-start | bytes 712712 | tf_op jit(solution)/shard_map/ppermute | solution.py:136
  52.0 3.1 %collective-permute-start.8 = (bf16[32,3712]{1,0:T(8,128)(2,1)S(1)}, bf16[32,3712]{1,0:T(8,128)(2,1)S(1)}, u32[]{:S(2)}, u32[]{:S(2)}) collective-permute-start(bf16[32,3712]{1,0:T(8,128)(2,1)S(1)} %collective-permute-done.3.refs_4_), channel_id=1, source_target_pairs={{0,1},{1,0},{2,3},{3,2},{4,5},{5,4},{6,7},{7,6},{8,9},{9,8},{10,11... | collective-permute-start | bytes 712712 | tf_op jit(solution)/shard_map/ppermute | solution.py:136
  53.1 2.0 %collective-permute-start.7 = (bf16[32,3712]{1,0:T(8,128)(2,1)S(1)}, bf16[32,3712]{1,0:T(8,128)(2,1)S(1)}, u32[]{:S(2)}, u32[]{:S(2)}) collective-permute-start(bf16[32,3712]{1,0:T(8,128)(2,1)S(1)} %collective-permute-done.2.refs_3_), channel_id=1, source_target_pairs={{0,1},{1,0},{2,3},{3,2},{4,5},{5,4},{6,7},{7,6},{8,9},{9,8},{10,11... | collective-permute-start | bytes 712712 | tf_op jit(solution)/shard_map/ppermute | solution.py:136
  53.5 17.0 %collective-permute-start.18 = (bf16[16,3584]{1,0:T(8,128)(2,1)S(1)}, bf16[16,3584]{1,0:T(8,128)(2,1)S(1)}, u32[]{:S(2)}, u32[]{:S(2)}) collective-permute-start(bf16[16,3584]{1,0:T(8,128)(2,1)S(1)} %get-tuple-element.18), channel_id=1, source_target_pairs={{0,4},{1,5},{4,8},{5,9},{8,12},{9,13},{12,14},{13,15},{14,10},{15,... | collective-permute-start | bytes 344072 | tf_op jit(solution)/shard_map/ppermute | solution.py:134
  69.8 6.3 %collective-permute-start.9 = (bf16[160,3584]{1,0:T(8,128)(2,1)S(1)}, bf16[160,3584]{1,0:T(8,128)(2,1)S(1)}, u32[]{:S(2)}, u32[]{:S(2)}) collective-permute-start(bf16[160,3584]{1,0:T(8,128)(2,1)S(1)} %get-tuple-element.10), channel_id=1, source_target_pairs={{0,1},{1,0},{2,3},{3,2},{4,5},{5,4},{6,7},{7,6},{8,9},{9,8},{10,11... | collective-permute-start | bytes 3440648 | tf_op jit(solution)/shard_map/ppermute | solution.py:136
  70.0 5.5 %collective-permute-start.22 = (bf16[16,3584]{1,0:T(8,128)(2,1)S(1)}, bf16[16,3584]{1,0:T(8,128)(2,1)S(1)}, u32[]{:S(2)}, u32[]{:S(2)}) collective-permute-start(bf16[16,3584]{1,0:T(8,128)(2,1)S(1)} %get-tuple-element.19), channel_id=1, source_target_pairs={{4,0},{5,1},{8,4},{9,5},{12,8},{13,9},{14,12},{15,13},{10,14},{11,... | collective-permute-start | bytes 344072 | tf_op jit(solution)/shard_map/ppermute | solution.py:135
  70.5 7.7 %collective-permute-start.19 = (bf16[32,3584]{1,0:T(8,128)(2,1)S(1)}, bf16[32,3584]{1,0:T(8,128)(2,1)S(1)}, u32[]{:S(2)}, u32[]{:S(2)}) collective-permute-start(bf16[32,3584]{1,0:T(8,128)(2,1)S(1)} %pad_maximum_fusion), channel_id=1, source_target_pairs={{0,4},{1,5},{4,8},{5,9},{8,12},{9,13},{12,14},{13,15},{14,10},{15,... | collective-permute-start | bytes 688136 | tf_op jit(solution)/shard_map/ppermute | solution.py:134
  75.6 7.2 %collective-permute-start.23 = (bf16[32,3584]{1,0:T(8,128)(2,1)S(1)}, bf16[32,3584]{1,0:T(8,128)(2,1)S(1)}, u32[]{:S(2)}, u32[]{:S(2)}) collective-permute-start(bf16[32,3584]{1,0:T(8,128)(2,1)S(1)} %pad_maximum_fusion.1), channel_id=1, source_target_pairs={{4,0},{5,1},{8,4},{9,5},{12,8},{13,9},{14,12},{15,13},{10,14},{11,... | collective-permute-start | bytes 688136 | tf_op jit(solution)/shard_map/ppermute | solution.py:135
  78.3 6.9 %collective-permute-start.20 = (bf16[32,3584]{1,0:T(8,128)(2,1)S(1)}, bf16[32,3584]{1,0:T(8,128)(2,1)S(1)}, u32[]{:S(2)}, u32[]{:S(2)}) collective-permute-start(bf16[32,3584]{1,0:T(8,128)(2,1)S(1)} %add_convert_fusion.4), channel_id=1, source_target_pairs={{0,4},{1,5},{4,8},{5,9},{8,12},{9,13},{12,14},{13,15},{14,10},{15,... | collective-permute-start | bytes 688136 | tf_op jit(solution)/shard_map/ppermute | solution.py:134
  85.4 6.1 %collective-permute-start.24 = (bf16[32,3584]{1,0:T(8,128)(2,1)S(1)}, bf16[32,3584]{1,0:T(8,128)(2,1)S(1)}, u32[]{:S(2)}, u32[]{:S(2)}) collective-permute-start(bf16[32,3584]{1,0:T(8,128)(2,1)S(1)} %get-tuple-element.14), channel_id=1, source_target_pairs={{4,0},{5,1},{8,4},{9,5},{12,8},{13,9},{14,12},{15,13},{10,14},{11,... | collective-permute-start | bytes 688136 | tf_op jit(solution)/shard_map/ppermute | solution.py:135
  86.7 6.2 %collective-permute-start.21 = (bf16[32,3584]{1,0:T(8,128)(2,1)S(1)}, bf16[32,3584]{1,0:T(8,128)(2,1)S(1)}, u32[]{:S(2)}, u32[]{:S(2)}) collective-permute-start(bf16[32,3584]{1,0:T(8,128)(2,1)S(1)} %get-tuple-element.13), channel_id=1, source_target_pairs={{0,4},{1,5},{4,8},{5,9},{8,12},{9,13},{12,14},{13,15},{14,10},{15,... | collective-permute-start | bytes 688136 | tf_op jit(solution)/shard_map/ppermute | solution.py:134
  91.5 6.1 %collective-permute-start.25 = (bf16[32,3584]{1,0:T(8,128)(2,1)S(1)}, bf16[32,3584]{1,0:T(8,128)(2,1)S(1)}, u32[]{:S(2)}, u32[]{:S(2)}) collective-permute-start(bf16[32,3584]{1,0:T(8,128)(2,1)S(1)} %add_convert_fusion.1), channel_id=1, source_target_pairs={{4,0},{5,1},{8,4},{9,5},{12,8},{13,9},{14,12},{15,13},{10,14},{11,... | collective-permute-start | bytes 688136 | tf_op jit(solution)/shard_map/ppermute | solution.py:135

commit v2 on v1

--- a/solution.py
+++ b/solution.py
@@ -8,6 +8,7 @@
 from jax.sharding import PartitionSpec as P
 
 F32, BF16 = jnp.float32, jnp.bfloat16
+SCRATCH = 16 * 2**20
 
 
 def chip_layout(mesh):
@@ -28,63 +29,74 @@
     return cores, order
 
 
-def pack_kernel(experts, tok_ref, routes_ref, gates_ref, out_ref):
-    rows, width = tok_ref.shape
+def pack_kernel(experts, tok_hbm, routes_hbm, gates_hbm, out_ref, routes_ref, gates_ref, sems):
+    rows, width = tok_hbm.shape
     extra = out_ref.shape[1] - width
-    lane = lax.broadcasted_iota(jnp.int32, (rows, extra), 1)
+    moves = [
+        pltpu.make_async_copy(routes_hbm, routes_ref, sems.at[0]),
+        pltpu.make_async_copy(gates_hbm, gates_ref, sems.at[1]),
+        pltpu.make_async_copy(tok_hbm, out_ref.at[:, :width], sems.at[2]),
+    ]
+    for move in moves:
+        move.start()
+    for move in moves[:2]:
+        move.wait()
+    lane = lax.broadcasted_iota(jnp.int32, (extra, rows), 0)
     expert, piece = lax.rem(lane, experts), lax.div(lane, experts)
-    weight = jnp.zeros((rows, extra), F32)
-    for k in range(routes_ref.shape[1]):
-        weight += jnp.where(routes_ref[:, k : k + 1] == expert, gates_ref[:, k : k + 1], 0.0)
+    weight = jnp.zeros((extra, rows), F32)
+    for k in range(routes_ref.shape[0]):
+        weight += jnp.where(routes_ref[k : k + 1] == expert, gates_ref[k : k + 1], 0.0)
     high = weight.astype(BF16).astype(F32)
     middle = (weight - high).astype(BF16).astype(F32)
     low = weight - high - middle
     table = jnp.where(piece == 0, high, jnp.where(piece == 1, middle, jnp.where(piece == 2, low, 0.0)))
-    out_ref[:, :width] = tok_ref[...]
-    out_ref[:, width:] = table.astype(BF16)
+    out_ref[:, width:] = table.T.astype(BF16)
+    moves[2].wait()
 
 
 def pack(tokens, routes, gates, experts):
     rows, width = tokens.shape
     extra = pl.cdiv(3 * experts, 128) * 128
+    hbm = pl.BlockSpec(memory_space=pltpu.HBM)
     return pl.pallas_call(
         functools.partial(pack_kernel, experts),
         out_shape=jax.ShapeDtypeStruct((rows, width + extra), BF16),
-    )(tokens, routes, gates)
+        in_specs=[hbm] * 3,
+        out_specs=pl.BlockSpec(memory_space=pltpu.VMEM),
+        scratch_shapes=[
+            pltpu.VMEM(routes.shape[::-1], routes.dtype),
+            pltpu.VMEM(gates.shape[::-1], gates.dtype),
+            pltpu.SemaphoreType.DMA((3,)),
+        ],
+        compiler_params=pltpu.CompilerParams(vmem_limit_bytes=SCRATCH),
+        cost_estimate=pl.CostEstimate(flops=40 * 2**30, bytes_accessed=0, transcendentals=0),
+    )(tokens, routes.T, gates.T)
 
 
-def ffn_kernel(count, rows, experts, n_ff, me_ref, *refs):
+def ffn_kernel(count, rows, experts, tile_ff, tile_d, me_ref, *refs):
     blocks, (gate_ref, up_ref, down_ref, mine_ref, other_ref, x_ref, w_ref, h_ref) = refs[:count], refs[count:]
-    i = pl.program_id(0)
     width = x_ref.shape[1]
     half = mine_ref.shape[0]
+    for at, ref in enumerate(blocks):
+        x_ref[at * rows : (at + 1) * rows, :] = ref[:, :width]
+        table = ref[:, width:].astype(F32)
+        lane = lax.broadcasted_iota(jnp.int32, table.shape, 1)
+        own = lax.rem(lane, experts) == me_ref[0]
+        w_ref[at * rows : (at + 1) * rows, :] = jnp.sum(jnp.where(own, table, 0.0), axis=1, keepdims=True)
 
-    @pl.when(i == 0)
-    def _():
-        for at, ref in enumerate(blocks):
-            x_ref[at * rows : (at + 1) * rows, :] = ref[:, :width]
-            table = ref[:, width:].astype(F32)
-            lane = lax.broadcasted_iota(jnp.int32, table.shape, 1)
-            own = lax.rem(lane, experts) == me_ref[0]
-            w_ref[at * rows : (at + 1) * rows, :] = jnp.sum(jnp.where(own, table, 0.0), axis=1, keepdims=True)
+    @pl.loop(0, h_ref.shape[1] // tile_ff)
+    def _(j):
+        at = pl.ds(pl.multiple_of(j * tile_ff, tile_ff), tile_ff)
+        gate = jnp.dot(x_ref[...], gate_ref[0, :, at], preferred_element_type=F32)
+        upper = jnp.dot(x_ref[...], up_ref[0, :, at], preferred_element_type=F32)
+        h_ref[:, at] = (gate / (1.0 + jnp.exp(-gate)) * upper).astype(BF16)
 
-    @pl.when(i < n_ff)
-    def _():
-        x = x_ref[...]
-        gate = jnp.dot(x, gate_ref[0], preferred_element_type=F32)
-        upper = jnp.dot(x, up_ref[0], preferred_element_type=F32)
-        h_ref[jnp.minimum(i, n_ff - 1)] = (gate / (1.0 + jnp.exp(-gate)) * upper).astype(BF16)
-
-    @pl.when(i >= n_ff)
-    def _():
-        tile = h_ref.shape[2]
-        out = jnp.dot(h_ref[0], down_ref[0, :tile], preferred_element_type=F32)
-        for j in range(1, n_ff):
-            out += jnp.dot(h_ref[j], down_ref[0, j * tile : (j + 1) * tile], preferred_element_type=F32)
-        out = out * w_ref[...]
-        mine_ref[...] = out[:half]
-        if count * rows > half:
-            other_ref[...] = out[half:].astype(BF16)
+    @pl.loop(0, width // tile_d)
+    def _(j):
+        at = pl.ds(pl.multiple_of(j * tile_d, tile_d), tile_d)
+        out = jnp.dot(h_ref[...], down_ref[0, :, at], preferred_element_type=F32) * w_ref[...]
+        mine_ref[:, at] = out[:half]
+        other_ref[:, at] = out[half:].astype(BF16)
 
 
 def ffn(blocks, mine, me, experts, w_gate, w_up, w_down):
@@ -92,33 +104,24 @@
     _, width, ff = w_gate.shape
     tile_ff = 256 if ff % 256 == 0 else ff
     tile_d = next(t for t in (512, 256, 128, width) if width % t == 0)
-    n_ff, n_d = ff // tile_ff, width // tile_d
     total, half = count * rows, mine * rows
-    first = lambda i: (0, 0, jnp.minimum(i, n_ff - 1))
-    second = lambda i: (0, jnp.maximum(i - n_ff, 0))
+    vmem = pl.BlockSpec(memory_space=pltpu.VMEM)
     return pl.pallas_call(
-        functools.partial(ffn_kernel, count, rows, experts, n_ff),
-        grid=(n_ff + n_d,),
+        functools.partial(ffn_kernel, count, rows, experts, tile_ff, tile_d),
         out_shape=[
             jax.ShapeDtypeStruct((half, width), F32),
             jax.ShapeDtypeStruct((total - half, width), BF16),
         ],
-        in_specs=[pl.BlockSpec(memory_space=pltpu.SMEM)]
-        + [pl.BlockSpec(b.shape, lambda i: (0, 0)) for b in blocks]
-        + [
-            pl.BlockSpec((1, width, tile_ff), first),
-            pl.BlockSpec((1, width, tile_ff), first),
-            pl.BlockSpec((1, ff, tile_d), lambda i: (0, 0, jnp.maximum(i - n_ff, 0))),
-        ],
-        out_specs=[pl.BlockSpec((half, tile_d), second), pl.BlockSpec((total - half, tile_d), second)],
+        in_specs=[pl.BlockSpec(memory_space=pltpu.SMEM)] + [vmem] * (count + 3),
+        out_specs=[vmem, vmem],
         scratch_shapes=[
             pltpu.VMEM((total, width), BF16),
             pltpu.VMEM((total, 1), F32),
-            pltpu.VMEM((n_ff, total, tile_ff), BF16),
+            pltpu.VMEM((total, ff), BF16),
         ],
-        compiler_params=pltpu.CompilerParams(vmem_limit_bytes=40 * 2**20),
+        compiler_params=pltpu.CompilerParams(vmem_limit_bytes=SCRATCH),
         cost_estimate=pl.CostEstimate(
-            flops=6 * total * width * ff, bytes_accessed=6 * width * ff, transcendentals=total * ff
+            flops=6 * max(total, 256) * width * ff, bytes_accessed=0, transcendentals=total * ff
         ),
     )(me, *blocks, w_gate, w_up, w_down)
 
@@ -148,9 +151,10 @@
 
     run = lambda at: ffn([got[d] for d in at] + [twin[d] for d in at], len(at), me, experts, w_gate, w_up, w_down)
     late = [far] + [s * (far - 1) for s in (1, -1)]
-    early = [d for d in sorted(got, key=abs) if d not in late]
+    near = [0, 1, -1]
+    middle = [d for d in sorted(got, key=abs) if d not in late + near]
     mine, theirs = {}, {}
-    for at in (early, late):
+    for at in (late, middle, near):
         kept, sent = run(at)
         sent = sibling(sent)
         for j, d in enumerate(at):

time: 98.9 us -> 91.6 us (0.926)
  Pallas kernels: 29.3 us -> 18.7 us
  local copies, waits for them, and re-layouts: 5.9 us -> 11.7 us
  waiting for transfers between devices: 41.1 us -> 39.8 us
  starting transfers between devices: 20.6 us -> 19.6 us
    ppermute x8, waiting for transfers between devices: 16.7 us -> 4.51 us  [local(): left = lambda a: lax.ppermute(a, 'node', back)]
    ppermute x8, waiting for transfers between devices: 21.9 us -> 31.7 us  [local(): right = lambda a: lax.ppermute(a, 'node', forth)]
    pallas_call x2 -> x3, Pallas kernels: 27.5 us -> 18.5 us  [ffn(): pl.pallas_call(functools.partial(ffn_kernel, count, rows, experts, tile_f...]
    unnamed x9 -> x19, local copies, waits for them, and re-layouts: 5.82 us -> 11.6 us
    pallas_call x1, Pallas kernels: 1.8 us -> 0.19 us  [pack(): pl.pallas_call(functools.partial(pack_kernel, experts), out_shape=jax.Sha...]
    ppermute x10 -> x11, waiting for transfers between devices: 2.5 us -> 3.6 us  [local(): sibling = lambda a: lax.ppermute(a, 'node', swap)]
    ppermute x10 -> x11, starting transfers between devices: 2.1 us -> 2.22 us  [local(): sibling = lambda a: lax.ppermute(a, 'node', swap)]
  transfers between devices with their start and end apart: 26 -> 27, of which waited for: 13 -> 14; matrix products, arithmetic and copies ran while one was open for 0% -> 1% of each run, Pallas kernels for 15% -> 13%
where the time goes in v2:
time: 91.6 us; the launch traced here: 91.3 us
  waiting for transfers between devices  39.8 us (43%)
  starting transfers between devices  19.6 us (21%)
  Pallas kernels  18.7 us (20%)
  local copies, waits for them, and re-layouts  11.7 us (13%)
  other arithmetic  1.36 us (1%)
    ppermute x8, waiting for transfers between devices, local(): right = lambda a: lax.ppermute(a, 'node', forth)  31.7 us
    pallas_call x3, Pallas kernels, ffn(): pl.pallas_call(functools.partial(ffn_kernel, count, rows, experts, tile_f...  18.5 us
    ppermute x8, starting transfers between devices, local(): right = lambda a: lax.ppermute(a, 'node', forth)  13.5 us
    unnamed x19, local copies, waits for them, and re-layouts  11.6 us
    ppermute x8, waiting for transfers between devices, local(): left = lambda a: lax.ppermute(a, 'node', back)  4.51 us
    ppermute x8, starting transfers between devices, local(): left = lambda a: lax.ppermute(a, 'node', back)  3.88 us
    ppermute x11, waiting for transfers between devices, local(): sibling = lambda a: lax.ppermute(a, 'node', swap)  3.6 us
    ppermute x11, starting transfers between devices, local(): sibling = lambda a: lax.ppermute(a, 'node', swap)  2.22 us
  transfers between devices with their start and end apart: 27, of which 14 were waited for; matrix products, arithmetic and copies ran while one was open for 1% of the time, Pallas kernels for 13%

profile of v2, /device:TPU:0, one launch (start us, length us, event | category | flops | bytes accessed | tf_op | source)
XLA Modules:
  0.0 91.3 jit_solution(13742008326151858791)
XLA Ops:
  0.0 0.9 %copy-done.6 = bf16[32,3584]{1,0:T(8,128)(2,1)S(1)} copy-done((bf16[32,3584]{1,0:T(8,128)(2,1)S(1)}, bf16[32,3584]{1,0:T(8,128)(2,1)}, u32[]{:S(2)}) %copy-start.6) | copy-done | bytes 229400
  0.9 0.7 copy-done.7
  1.6 0.7 copy-done.8
  2.3 0.2 shard_map.64.refs_0_
  2.5 3.1 %collective-permute-start.1 = (bf16[32,3712]{1,0:T(8,128)(2,1)S(1)}, bf16[32,3712]{1,0:T(8,128)(2,1)S(1)}, u32[]{:S(2)}, u32[]{:S(2)}) collective-permute-start(bf16[32,3712]{1,0:T(8,128)(2,1)S(1)} %shard_map.64.refs_0_), channel_id=1, source_target_pairs={{0,4},{1,5},{4,8},{5,9},{8,12},{9,13},{12,14},{13,15},{14,10},{15,... | collective-permute-start | bytes 712712 | tf_op jit(solution)/shard_map/ppermute | solution.py:137
  5.6 5.7 %collective-permute-done.1.refs_2_ = bf16[32,3712]{1,0:T(8,128)(2,1)S(1)} collective-permute-done((bf16[32,3712]{1,0:T(8,128)(2,1)S(1)}, bf16[32,3712]{1,0:T(8,128)(2,1)S(1)}, u32[]{:S(2)}, u32[]{:S(2)}) %collective-permute-start.1) | collective-permute-done | bytes 237600 | tf_op jit(solution)/shard_map/ppermute | solution.py:137
  11.3 1.8 %collective-permute-start.6 = (bf16[32,3712]{1,0:T(8,128)(2,1)S(1)}, bf16[32,3712]{1,0:T(8,128)(2,1)S(1)}, u32[]{:S(2)}, u32[]{:S(2)}) collective-permute-start(bf16[32,3712]{1,0:T(8,128)(2,1)S(1)} %collective-permute-done.1.refs_2_), channel_id=1, source_target_pairs={{0,4},{1,5},{4,8},{5,9},{8,12},{9,13},{12,14},{13,15},{14,10},{15,... | collective-permute-start | bytes 712712 | tf_op jit(solution)/shard_map/ppermute | solution.py:137
  13.1 0.2 collective-permute-start.7
  13.3 4.9 %collective-permute-done.6.refs_0_ = bf16[32,3712]{1,0:T(8,128)(2,1)S(1)} collective-permute-done((bf16[32,3712]{1,0:T(8,128)(2,1)S(1)}, bf16[32,3712]{1,0:T(8,128)(2,1)S(1)}, u32[]{:S(2)}, u32[]{:S(2)}) %collective-permute-start.6) | collective-permute-done | bytes 237600 | tf_op jit(solution)/shard_map/ppermute | solution.py:137
  18.3 1.5 %collective-permute-start.11 = (bf16[32,3712]{1,0:T(8,128)(2,1)S(1)}, bf16[32,3712]{1,0:T(8,128)(2,1)S(1)}, u32[]{:S(2)}, u32[]{:S(2)}) collective-permute-start(bf16[32,3712]{1,0:T(8,128)(2,1)S(1)} %collective-permute-done.6.refs_0_), channel_id=1, source_target_pairs={{0,4},{1,5},{4,8},{5,9},{8,12},{9,13},{12,14},{13,15},{14,10},{15,... | collective-permute-start | bytes 712712 | tf_op jit(solution)/shard_map/ppermute | solution.py:137
  19.8 0.5 collective-permute-start.13
  20.3 4.1 %collective-permute-done.11.refs_2_ = bf16[32,3712]{1,0:T(8,128)(2,1)S(1)} collective-permute-done((bf16[32,3712]{1,0:T(8,128)(2,1)S(1)}, bf16[32,3712]{1,0:T(8,128)(2,1)S(1)}, u32[]{:S(2)}, u32[]{:S(2)}) %collective-permute-start.11) | collective-permute-done | bytes 237600 | tf_op jit(solution)/shard_map/ppermute | solution.py:137
  24.5 1.8 %collective-permute-start.12 = (bf16[16,3712]{1,0:T(8,128)(2,1)S(1)}, bf16[16,3712]{1,0:T(8,128)(2,1)S(1)}, u32[]{:S(2)}, u32[]{:S(2)}) collective-permute-start(bf16[16,3712]{1,0:T(8,128)(2,1)S(1)} %slice.101), channel_id=1, source_target_pairs={{0,4},{1,5},{4,8},{5,9},{8,12},{9,13},{12,14},{13,15},{14,10},{15,... | collective-permute-start | bytes 356360 | tf_op jit(solution)/shard_map/ppermute | solution.py:137
  26.3 0.3 collective-permute-start.14
  26.6 0.5 collective-permute-start.17
  27.1 2.2 %collective-permute-done.12 = bf16[16,3712]{1,0:T(8,128)(2,1)S(1)} collective-permute-done((bf16[16,3712]{1,0:T(8,128)(2,1)S(1)}, bf16[16,3712]{1,0:T(8,128)(2,1)S(1)}, u32[]{:S(2)}, u32[]{:S(2)}) %collective-permute-start.12) | collective-permute-done | bytes 118816 | tf_op jit(solution)/shard_map/ppermute | solution.py:137
  29.4 1.9 %collective-permute-done.14 = bf16[16,3712]{1,0:T(8,128)(2,1)S(1)} collective-permute-done((bf16[16,3712]{1,0:T(8,128)(2,1)S(1)}, bf16[16,3712]{1,0:T(8,128)(2,1)S(1)}, u32[]{:S(2)}, u32[]{:S(2)}) %collective-permute-start.14) | collective-permute-done | bytes 118816 | tf_op jit(solution)/shard_map/ppermute | solution.py:138
  31.3 1.5 %collective-permute-done.15.refs_3_ = bf16[32,3712]{1,0:T(8,128)(2,1)S(1)} collective-permute-done((bf16[32,3712]{1,0:T(8,128)(2,1)S(1)}, bf16[32,3712]{1,0:T(8,128)(2,1)S(1)}, u32[]{:S(2)}, u32[]{:S(2)}) %collective-permute-start.15) | collective-permute-done | bytes 237600 | tf_op jit(solution)/shard_map/ppermute | solution.py:139
  32.8 3.1 %copy-done = bf16[1,3584,1024]{2,1,0:T(8,128)(2,1)S(1)} copy-done((bf16[1,3584,1024]{2,1,0:T(8,128)(2,1)S(1)}, bf16[1,3584,1024]{2,1,0:T(8,128)(2,1)}, u32[]{:S(2)}) %copy-start) | copy-done | bytes 7340056
  35.9 3.1 %copy-done.2 = bf16[1,3584,1024]{2,1,0:T(8,128)(2,1)S(1)} copy-done((bf16[1,3584,1024]{2,1,0:T(8,128)(2,1)S(1)}, bf16[1,3584,1024]{2,1,0:T(8,128)(2,1)}, u32[]{:S(2)}) %copy-start.2) | copy-done | bytes 7340056
  39.0 3.1 %copy-done.4 = bf16[1,1024,3584]{2,1,0:T(8,128)(2,1)S(1)} copy-done((bf16[1,1024,3584]{2,1,0:T(8,128)(2,1)S(1)}, bf16[1,1024,3584]{2,1,0:T(8,128)(2,1)}, u32[]{:S(2)}) %copy-start.4) | copy-done | bytes 7340056
  42.1 6.6 %shard_map.67 = (f32[96,3584]{1,0:T(8,128)S(1)}, bf16[96,3584]{1,0:T(8,128)(2,1)S(1)}) custom-call(s32[1]{0:T(128)} %bitcast.me_ref, bf16[32,3712]{1,0:T(8,128)(2,1)S(1)} %constant_dynamic-update-slice_fusion.refs_0_, bf16[32,3712]{1,0:T(8,128)(2,1)S(1)} %collective-permute-done.13.refs_1_, bf16[32,3712]{1,0:T(8,128)(2,1)S(1)} %collective-permute-done.11.refs_2_, ...), custom_call_target="tpu_custom_call" | custom-call | flops 5637144576 | tf_op jit(solution)/shard_map/pallas_call | solution.py:109
  48.7 0.2 collective-permute-start.18
  48.9 0.4 collective-permute-start.2
  49.2 0.1 collective-permute-start.3
  49.4 0.4 collective-permute-start.4
  49.9 1.0 %collective-permute-done.18 = bf16[96,3584]{1,0:T(8,128)(2,1)S(1)} collective-permute-done((bf16[96,3584]{1,0:T(8,128)(2,1)S(1)}, bf16[96,3584]{1,0:T(8,128)(2,1)S(1)}, u32[]{:S(2)}, u32[]{:S(2)}) %collective-permute-start.18) | collective-permute-done | bytes 688160 | tf_op jit(solution)/shard_map/ppermute | solution.py:139
  51.0 0.1 convert_add_fusion.1
  51.2 1.0 %collective-permute-done.8.refs_2_ = bf16[32,3712]{1,0:T(8,128)(2,1)S(1)} collective-permute-done((bf16[32,3712]{1,0:T(8,128)(2,1)S(1)}, bf16[32,3712]{1,0:T(8,128)(2,1)S(1)}, u32[]{:S(2)}, u32[]{:S(2)}) %collective-permute-start.8) | collective-permute-done | bytes 237600 | tf_op jit(solution)/shard_map/ppermute | solution.py:139
  52.2 0.2 collective-permute-start.23
  52.6 5.3 %shard_map.66 = (f32[64,3584]{1,0:T(8,128)S(1)}, bf16[64,3584]{1,0:T(8,128)(2,1)S(1)}) custom-call(s32[1]{0:T(128)} %bitcast.me_ref, bf16[32,3712]{1,0:T(8,128)(2,1)S(1)} %collective-permute-done.6.refs_0_, bf16[32,3712]{1,0:T(8,128)(2,1)S(1)} %collective-permute-done.7.refs_1_, bf16[32,3712]{1,0:T(8,128)(2,1)S(1)} %collective-permute-done.8.refs_2_, ...), custom_call_target="tpu_custom_call" | custom-call | flops 5637144576 | tf_op jit(solution)/shard_map/pallas_call | solution.py:109
  57.9 0.2 collective-permute-start.10
  58.1 1.6 %collective-permute-start.19 = (bf16[16,3584]{1,0:T(8,128)(2,1)S(1)}, bf16[16,3584]{1,0:T(8,128)(2,1)S(1)}, u32[]{:S(2)}, u32[]{:S(2)}) collective-permute-start(bf16[16,3584]{1,0:T(8,128)(2,1)S(1)} %get-tuple-element.24), channel_id=1, source_target_pairs={{0,4},{1,5},{4,8},{5,9},{8,12},{9,13},{12,14},{13,15},{14,10},{15,... | collective-permute-start | bytes 344072 | tf_op jit(solution)/shard_map/ppermute | solution.py:137
  59.8 3.9 %collective-permute-done.19 = bf16[16,3584]{1,0:T(8,128)(2,1)S(1)} collective-permute-done((bf16[16,3584]{1,0:T(8,128)(2,1)S(1)}, bf16[16,3584]{1,0:T(8,128)(2,1)S(1)}, u32[]{:S(2)}, u32[]{:S(2)}) %collective-permute-start.19) | collective-permute-done | bytes 114720 | tf_op jit(solution)/shard_map/ppermute | solution.py:137
  63.7 1.7 %collective-permute-start.24 = (bf16[32,3584]{1,0:T(8,128)(2,1)S(1)}, bf16[32,3584]{1,0:T(8,128)(2,1)S(1)}, u32[]{:S(2)}, u32[]{:S(2)}) collective-permute-start(bf16[32,3584]{1,0:T(8,128)(2,1)S(1)} %pad_maximum_fusion.1), channel_id=1, source_target_pairs={{4,0},{5,1},{8,4},{9,5},{12,8},{13,9},{14,12},{15,13},{10,14},{11,... | collective-permute-start | bytes 688136 | tf_op jit(solution)/shard_map/ppermute | solution.py:138
  65.5 0.3 collective-permute-start.20
  65.8 6.6 %shard_map.65 = (f32[96,3584]{1,0:T(8,128)S(1)}, bf16[96,3584]{1,0:T(8,128)(2,1)S(1)}) custom-call(s32[1]{0:T(128)} %bitcast.me_ref, bf16[32,3712]{1,0:T(8,128)(2,1)S(1)} %shard_map.64.refs_0_, bf16[32,3712]{1,0:T(8,128)(2,1)S(1)} %collective-permute-done.refs_1_, bf16[32,3712]{1,0:T(8,128)(2,1)S(1)} %collective-permute-done.1.refs_2_, ...), custom_call_target="tpu_custom_call" | custom-call | flops 5637144576 | tf_op jit(solution)/shard_map/pallas_call | solution.py:109
  72.5 0.1 add_convert_fusion.4
  72.7 1.7 %collective-permute-start.21 = (bf16[32,3584]{1,0:T(8,128)(2,1)S(1)}, bf16[32,3584]{1,0:T(8,128)(2,1)S(1)}, u32[]{:S(2)}, u32[]{:S(2)}) collective-permute-start(bf16[32,3584]{1,0:T(8,128)(2,1)S(1)} %get-tuple-element.22), channel_id=1, source_target_pairs={{0,4},{1,5},{4,8},{5,9},{8,12},{9,13},{12,14},{13,15},{14,10},{15,... | collective-permute-start | bytes 688136 | tf_op jit(solution)/shard_map/ppermute | solution.py:137
  74.4 0.4 collective-permute-start.25
  74.8 6.0 %collective-permute-done.21 = bf16[32,3584]{1,0:T(8,128)(2,1)S(1)} collective-permute-done((bf16[32,3584]{1,0:T(8,128)(2,1)S(1)}, bf16[32,3584]{1,0:T(8,128)(2,1)S(1)}, u32[]{:S(2)}, u32[]{:S(2)}) %collective-permute-start.21) | collective-permute-done | bytes 229408 | tf_op jit(solution)/shard_map/ppermute | solution.py:137
  80.7 1.3 %collective-permute-done.25 = bf16[32,3584]{1,0:T(8,128)(2,1)S(1)} collective-permute-done((bf16[32,3584]{1,0:T(8,128)(2,1)S(1)}, bf16[32,3584]{1,0:T(8,128)(2,1)S(1)}, u32[]{:S(2)}, u32[]{:S(2)}) %collective-permute-start.25) | collective-permute-done | bytes 229408 | tf_op jit(solution)/shard_map/ppermute | solution.py:138
  82.1 0.2 add_convert_fusion.3
  82.3 1.6 %collective-permute-start.22 = (bf16[32,3584]{1,0:T(8,128)(2,1)S(1)}, bf16[32,3584]{1,0:T(8,128)(2,1)S(1)}, u32[]{:S(2)}, u32[]{:S(2)}) collective-permute-start(bf16[32,3584]{1,0:T(8,128)(2,1)S(1)} %get-tuple-element.17), channel_id=1, source_target_pairs={{0,4},{1,5},{4,8},{5,9},{8,12},{9,13},{12,14},{13,15},{14,10},{15,... | collective-permute-start | bytes 688136 | tf_op jit(solution)/shard_map/ppermute | solution.py:137
  83.9 0.4 collective-permute-start.26
  84.3 4.9 %collective-permute-done.22 = bf16[32,3584]{1,0:T(8,128)(2,1)S(1)} collective-permute-done((bf16[32,3584]{1,0:T(8,128)(2,1)S(1)}, bf16[32,3584]{1,0:T(8,128)(2,1)S(1)}, u32[]{:S(2)}, u32[]{:S(2)}) %collective-permute-start.22) | collective-permute-done | bytes 229408 | tf_op jit(solution)/shard_map/ppermute | solution.py:137
  89.2 1.3 %collective-permute-done.26 = bf16[32,3584]{1,0:T(8,128)(2,1)S(1)} collective-permute-done((bf16[32,3584]{1,0:T(8,128)(2,1)S(1)}, bf16[32,3584]{1,0:T(8,128)(2,1)S(1)}, u32[]{:S(2)}, u32[]{:S(2)}) %collective-permute-start.26) | collective-permute-done | bytes 229408 | tf_op jit(solution)/shard_map/ppermute | solution.py:138
  90.5 0.8 add_convert_fusion
  (43 shorter events, 0.8 us)
Async XLA Ops:
  0.0 0.9 %copy-start.6 = (bf16[32,3584]{1,0:T(8,128)(2,1)S(1)}, bf16[32,3584]{1,0:T(8,128)(2,1)}, u32[]{:S(2)}) copy-start(bf16[32,3584]{1,0:T(8,128)(2,1)} %tok_hbm.1) | copy-start | bytes 688132
  0.9 0.7 copy-start.7
  1.6 0.7 copy-start.8
  2.5 8.8 %collective-permute-start.1 = (bf16[32,3712]{1,0:T(8,128)(2,1)S(1)}, bf16[32,3712]{1,0:T(8,128)(2,1)S(1)}, u32[]{:S(2)}, u32[]{:S(2)}) collective-permute-start(bf16[32,3712]{1,0:T(8,128)(2,1)S(1)} %shard_map.64.refs_0_), channel_id=1, source_target_pairs={{0,4},{1,5},{4,8},{5,9},{8,12},{9,13},{12,14},{13,15},{14,10},{15,... | collective-permute-start | bytes 712712 | tf_op jit(solution)/shard_map/ppermute | solution.py:137
  5.6 7.5 %collective-permute-start = (bf16[32,3712]{1,0:T(8,128)(2,1)S(1)}, bf16[32,3712]{1,0:T(8,128)(2,1)S(1)}, u32[]{:S(2)}, u32[]{:S(2)}) collective-permute-start(bf16[32,3712]{1,0:T(8,128)(2,1)S(1)} %shard_map.64.refs_0_), channel_id=1, source_target_pairs={{4,0},{5,1},{8,4},{9,5},{12,8},{13,9},{14,12},{15,13},{10,14},{11,... | collective-permute-start | bytes 712712 | tf_op jit(solution)/shard_map/ppermute | solution.py:138
  11.3 7.0 %collective-permute-start.6 = (bf16[32,3712]{1,0:T(8,128)(2,1)S(1)}, bf16[32,3712]{1,0:T(8,128)(2,1)S(1)}, u32[]{:S(2)}, u32[]{:S(2)}) collective-permute-start(bf16[32,3712]{1,0:T(8,128)(2,1)S(1)} %collective-permute-done.1.refs_2_), channel_id=1, source_target_pairs={{0,4},{1,5},{4,8},{5,9},{8,12},{9,13},{12,14},{13,15},{14,10},{15,... | collective-permute-start | bytes 712712 | tf_op jit(solution)/shard_map/ppermute | solution.py:137
  13.1 6.6 %collective-permute-start.7 = (bf16[32,3712]{1,0:T(8,128)(2,1)S(1)}, bf16[32,3712]{1,0:T(8,128)(2,1)S(1)}, u32[]{:S(2)}, u32[]{:S(2)}) collective-permute-start(bf16[32,3712]{1,0:T(8,128)(2,1)S(1)} %collective-permute-done.refs_1_), channel_id=1, source_target_pairs={{4,0},{5,1},{8,4},{9,5},{12,8},{13,9},{14,12},{15,13},{10,14},{11,... | collective-permute-start | bytes 712712 | tf_op jit(solution)/shard_map/ppermute | solution.py:138
  18.3 6.2 %collective-permute-start.11 = (bf16[32,3712]{1,0:T(8,128)(2,1)S(1)}, bf16[32,3712]{1,0:T(8,128)(2,1)S(1)}, u32[]{:S(2)}, u32[]{:S(2)}) collective-permute-start(bf16[32,3712]{1,0:T(8,128)(2,1)S(1)} %collective-permute-done.6.refs_0_), channel_id=1, source_target_pairs={{0,4},{1,5},{4,8},{5,9},{8,12},{9,13},{12,14},{13,15},{14,10},{15,... | collective-permute-start | bytes 712712 | tf_op jit(solution)/shard_map/ppermute | solution.py:137
  19.8 6.6 %collective-permute-start.13 = (bf16[32,3712]{1,0:T(8,128)(2,1)S(1)}, bf16[32,3712]{1,0:T(8,128)(2,1)S(1)}, u32[]{:S(2)}, u32[]{:S(2)}) collective-permute-start(bf16[32,3712]{1,0:T(8,128)(2,1)S(1)} %collective-permute-done.7.refs_1_), channel_id=1, source_target_pairs={{4,0},{5,1},{8,4},{9,5},{12,8},{13,9},{14,12},{15,13},{10,14},{11,... | collective-permute-start | bytes 712712 | tf_op jit(solution)/shard_map/ppermute | solution.py:138
  24.5 4.9 %collective-permute-start.12 = (bf16[16,3712]{1,0:T(8,128)(2,1)S(1)}, bf16[16,3712]{1,0:T(8,128)(2,1)S(1)}, u32[]{:S(2)}, u32[]{:S(2)}) collective-permute-start(bf16[16,3712]{1,0:T(8,128)(2,1)S(1)} %slice.101), channel_id=1, source_target_pairs={{0,4},{1,5},{4,8},{5,9},{8,12},{9,13},{12,14},{13,15},{14,10},{15,... | collective-permute-start | bytes 356360 | tf_op jit(solution)/shard_map/ppermute | solution.py:137
  26.3 4.9 %collective-permute-start.14 = (bf16[16,3712]{1,0:T(8,128)(2,1)S(1)}, bf16[16,3712]{1,0:T(8,128)(2,1)S(1)}, u32[]{:S(2)}, u32[]{:S(2)}) collective-permute-start(bf16[16,3712]{1,0:T(8,128)(2,1)S(1)} %slice.102), channel_id=1, source_target_pairs={{4,0},{5,1},{8,4},{9,5},{12,8},{13,9},{14,12},{15,13},{10,14},{11,... | collective-permute-start | bytes 356360 | tf_op jit(solution)/shard_map/ppermute | solution.py:138
  26.6 4.7 %collective-permute-start.16 = (bf16[32,3712]{1,0:T(8,128)(2,1)S(1)}, bf16[32,3712]{1,0:T(8,128)(2,1)S(1)}, u32[]{:S(2)}, u32[]{:S(2)}) collective-permute-start(bf16[32,3712]{1,0:T(8,128)(2,1)S(1)} %collective-permute-done.13.refs_1_), channel_id=1, source_target_pairs={{0,1},{1,0},{2,3},{3,2},{4,5},{5,4},{6,7},{7,6},{8,9},{9,8},{10,11... | collective-permute-start | bytes 712712 | tf_op jit(solution)/shard_map/ppermute | solution.py:139
  26.6 4.7 %collective-permute-start.17 = (bf16[32,3712]{1,0:T(8,128)(2,1)S(1)}, bf16[32,3712]{1,0:T(8,128)(2,1)S(1)}, u32[]{:S(2)}, u32[]{:S(2)}) collective-permute-start(bf16[32,3712]{1,0:T(8,128)(2,1)S(1)} %collective-permute-done.11.refs_2_), channel_id=1, source_target_pairs={{0,1},{1,0},{2,3},{3,2},{4,5},{5,4},{6,7},{7,6},{8,9},{9,8},{10,11... | collective-permute-start | bytes 712712 | tf_op jit(solution)/shard_map/ppermute | solution.py:139
  31.2 1.6 %collective-permute-start.15 = (bf16[32,3712]{1,0:T(8,128)(2,1)S(1)}, bf16[32,3712]{1,0:T(8,128)(2,1)S(1)}, u32[]{:S(2)}, u32[]{:S(2)}) collective-permute-start(bf16[32,3712]{1,0:T(8,128)(2,1)S(1)} %constant_dynamic-update-slice_fusion.refs_0_), channel_id=1, source_target_pairs={{0,1},{1,0},{2,3},{3,2},{4,5},{5,4},{6,7},{7,6},{8,9},{9,8},{10,11... | collective-permute-start | bytes 712712 | tf_op jit(solution)/shard_map/ppermute | solution.py:139
  32.8 3.1 %copy-start = (bf16[1,3584,1024]{2,1,0:T(8,128)(2,1)S(1)}, bf16[1,3584,1024]{2,1,0:T(8,128)(2,1)}, u32[]{:S(2)}) copy-start(bf16[1,3584,1024]{2,1,0:T(8,128)(2,1)} %refs_6_.5) | copy-start | bytes 22020100
  35.9 3.1 %copy-start.2 = (bf16[1,3584,1024]{2,1,0:T(8,128)(2,1)S(1)}, bf16[1,3584,1024]{2,1,0:T(8,128)(2,1)}, u32[]{:S(2)}) copy-start(bf16[1,3584,1024]{2,1,0:T(8,128)(2,1)} %refs_7_.3) | copy-start | bytes 22020100
  39.0 3.1 %copy-start.4 = (bf16[1,1024,3584]{2,1,0:T(8,128)(2,1)S(1)}, bf16[1,1024,3584]{2,1,0:T(8,128)(2,1)}, u32[]{:S(2)}) copy-start(bf16[1,1024,3584]{2,1,0:T(8,128)(2,1)} %refs_8_.3) | copy-start | bytes 22020100
  42.0 10.5 %copy-start.1 = (bf16[1,3584,1024]{2,1,0:T(8,128)(2,1)S(1)}, bf16[1,3584,1024]{2,1,0:T(8,128)(2,1)}, u32[]{:S(2)}) copy-start(bf16[1,3584,1024]{2,1,0:T(8,128)(2,1)} %refs_6_.5) | copy-start | bytes 22020100
  42.1 10.5 %copy-start.3 = (bf16[1,3584,1024]{2,1,0:T(8,128)(2,1)S(1)}, bf16[1,3584,1024]{2,1,0:T(8,128)(2,1)}, u32[]{:S(2)}) copy-start(bf16[1,3584,1024]{2,1,0:T(8,128)(2,1)} %refs_7_.3) | copy-start | bytes 22020100
  42.1 10.5 %copy-start.5 = (bf16[1,1024,3584]{2,1,0:T(8,128)(2,1)S(1)}, bf16[1,1024,3584]{2,1,0:T(8,128)(2,1)}, u32[]{:S(2)}) copy-start(bf16[1,1024,3584]{2,1,0:T(8,128)(2,1)} %refs_8_.3) | copy-start | bytes 22020100
  48.7 2.2 %collective-permute-start.18 = (bf16[96,3584]{1,0:T(8,128)(2,1)S(1)}, bf16[96,3584]{1,0:T(8,128)(2,1)S(1)}, u32[]{:S(2)}, u32[]{:S(2)}) collective-permute-start(bf16[96,3584]{1,0:T(8,128)(2,1)S(1)} %get-tuple-element.16), channel_id=1, source_target_pairs={{0,1},{1,0},{2,3},{3,2},{4,5},{5,4},{6,7},{7,6},{8,9},{9,8},{10,11... | collective-permute-start | bytes 2064392 | tf_op jit(solution)/shard_map/ppermute | solution.py:139
  48.9 16.6 %collective-permute-start.2 = (bf16[32,3712]{1,0:T(8,128)(2,1)S(1)}, bf16[32,3712]{1,0:T(8,128)(2,1)S(1)}, u32[]{:S(2)}, u32[]{:S(2)}) collective-permute-start(bf16[32,3712]{1,0:T(8,128)(2,1)S(1)} %shard_map.64.refs_0_), channel_id=1, source_target_pairs={{0,1},{1,0},{2,3},{3,2},{4,5},{5,4},{6,7},{7,6},{8,9},{9,8},{10,11... | collective-permute-start | bytes 712712 | tf_op jit(solution)/shard_map/ppermute | solution.py:139
  49.2 16.6 %collective-permute-start.3 = (bf16[32,3712]{1,0:T(8,128)(2,1)S(1)}, bf16[32,3712]{1,0:T(8,128)(2,1)S(1)}, u32[]{:S(2)}, u32[]{:S(2)}) collective-permute-start(bf16[32,3712]{1,0:T(8,128)(2,1)S(1)} %collective-permute-done.refs_1_), channel_id=1, source_target_pairs={{0,1},{1,0},{2,3},{3,2},{4,5},{5,4},{6,7},{7,6},{8,9},{9,8},{10,11... | collective-permute-start | bytes 712712 | tf_op jit(solution)/shard_map/ppermute | solution.py:139
  49.4 16.4 %collective-permute-start.4 = (bf16[32,3712]{1,0:T(8,128)(2,1)S(1)}, bf16[32,3712]{1,0:T(8,128)(2,1)S(1)}, u32[]{:S(2)}, u32[]{:S(2)}) collective-permute-start(bf16[32,3712]{1,0:T(8,128)(2,1)S(1)} %collective-permute-done.1.refs_2_), channel_id=1, source_target_pairs={{0,1},{1,0},{2,3},{3,2},{4,5},{5,4},{6,7},{7,6},{8,9},{9,8},{10,11... | collective-permute-start | bytes 712712 | tf_op jit(solution)/shard_map/ppermute | solution.py:139
  49.8 2.5 %collective-permute-start.8 = (bf16[32,3712]{1,0:T(8,128)(2,1)S(1)}, bf16[32,3712]{1,0:T(8,128)(2,1)S(1)}, u32[]{:S(2)}, u32[]{:S(2)}) collective-permute-start(bf16[32,3712]{1,0:T(8,128)(2,1)S(1)} %collective-permute-done.6.refs_0_), channel_id=1, source_target_pairs={{0,1},{1,0},{2,3},{3,2},{4,5},{5,4},{6,7},{7,6},{8,9},{9,8},{10,11... | collective-permute-start | bytes 712712 | tf_op jit(solution)/shard_map/ppermute | solution.py:139
  50.9 1.7 %collective-permute-start.9 = (bf16[32,3712]{1,0:T(8,128)(2,1)S(1)}, bf16[32,3712]{1,0:T(8,128)(2,1)S(1)}, u32[]{:S(2)}, u32[]{:S(2)}) collective-permute-start(bf16[32,3712]{1,0:T(8,128)(2,1)S(1)} %collective-permute-done.7.refs_1_), channel_id=1, source_target_pairs={{0,1},{1,0},{2,3},{3,2},{4,5},{5,4},{6,7},{7,6},{8,9},{9,8},{10,11... | collective-permute-start | bytes 712712 | tf_op jit(solution)/shard_map/ppermute | solution.py:139
  52.2 5.9 %collective-permute-start.23 = (bf16[16,3584]{1,0:T(8,128)(2,1)S(1)}, bf16[16,3584]{1,0:T(8,128)(2,1)S(1)}, u32[]{:S(2)}, u32[]{:S(2)}) collective-permute-start(bf16[16,3584]{1,0:T(8,128)(2,1)S(1)} %get-tuple-element.25), channel_id=1, source_target_pairs={{4,0},{5,1},{8,4},{9,5},{12,8},{13,9},{14,12},{15,13},{10,14},{11,... | collective-permute-start | bytes 344072 | tf_op jit(solution)/shard_map/ppermute | solution.py:138
  57.9 14.6 %collective-permute-start.10 = (bf16[64,3584]{1,0:T(8,128)(2,1)S(1)}, bf16[64,3584]{1,0:T(8,128)(2,1)S(1)}, u32[]{:S(2)}, u32[]{:S(2)}) collective-permute-start(bf16[64,3584]{1,0:T(8,128)(2,1)S(1)} %get-tuple-element.14), channel_id=1, source_target_pairs={{0,1},{1,0},{2,3},{3,2},{4,5},{5,4},{6,7},{7,6},{8,9},{9,8},{10,11... | collective-permute-start | bytes 1376264 | tf_op jit(solution)/shard_map/ppermute | solution.py:139
  58.1 5.6 %collective-permute-start.19 = (bf16[16,3584]{1,0:T(8,128)(2,1)S(1)}, bf16[16,3584]{1,0:T(8,128)(2,1)S(1)}, u32[]{:S(2)}, u32[]{:S(2)}) collective-permute-start(bf16[16,3584]{1,0:T(8,128)(2,1)S(1)} %get-tuple-element.24), channel_id=1, source_target_pairs={{0,4},{1,5},{4,8},{5,9},{8,12},{9,13},{12,14},{13,15},{14,10},{15,... | collective-permute-start | bytes 344072 | tf_op jit(solution)/shard_map/ppermute | solution.py:137
  63.7 8.8 %collective-permute-start.24 = (bf16[32,3584]{1,0:T(8,128)(2,1)S(1)}, bf16[32,3584]{1,0:T(8,128)(2,1)S(1)}, u32[]{:S(2)}, u32[]{:S(2)}) collective-permute-start(bf16[32,3584]{1,0:T(8,128)(2,1)S(1)} %pad_maximum_fusion.1), channel_id=1, source_target_pairs={{4,0},{5,1},{8,4},{9,5},{12,8},{13,9},{14,12},{15,13},{10,14},{11,... | collective-permute-start | bytes 688136 | tf_op jit(solution)/shard_map/ppermute | solution.py:138
  65.5 7.1 %collective-permute-start.20 = (bf16[32,3584]{1,0:T(8,128)(2,1)S(1)}, bf16[32,3584]{1,0:T(8,128)(2,1)S(1)}, u32[]{:S(2)}, u32[]{:S(2)}) collective-permute-start(bf16[32,3584]{1,0:T(8,128)(2,1)S(1)} %pad_maximum_fusion), channel_id=1, source_target_pairs={{0,4},{1,5},{4,8},{5,9},{8,12},{9,13},{12,14},{13,15},{14,10},{15,... | collective-permute-start | bytes 688136 | tf_op jit(solution)/shard_map/ppermute | solution.py:137
  72.4 2.3 %collective-permute-start.5 = (bf16[96,3584]{1,0:T(8,128)(2,1)S(1)}, bf16[96,3584]{1,0:T(8,128)(2,1)S(1)}, u32[]{:S(2)}, u32[]{:S(2)}) collective-permute-start(bf16[96,3584]{1,0:T(8,128)(2,1)S(1)} %get-tuple-element.12), channel_id=1, source_target_pairs={{0,1},{1,0},{2,3},{3,2},{4,5},{5,4},{6,7},{7,6},{8,9},{9,8},{10,11... | collective-permute-start | bytes 2064392 | tf_op jit(solution)/shard_map/ppermute | solution.py:139
  72.7 8.1 %collective-permute-start.21 = (bf16[32,3584]{1,0:T(8,128)(2,1)S(1)}, bf16[32,3584]{1,0:T(8,128)(2,1)S(1)}, u32[]{:S(2)}, u32[]{:S(2)}) collective-permute-start(bf16[32,3584]{1,0:T(8,128)(2,1)S(1)} %get-tuple-element.22), channel_id=1, source_target_pairs={{0,4},{1,5},{4,8},{5,9},{8,12},{9,13},{12,14},{13,15},{14,10},{15,... | collective-permute-start | bytes 688136 | tf_op jit(solution)/shard_map/ppermute | solution.py:137
  74.4 7.7 %collective-permute-start.25 = (bf16[32,3584]{1,0:T(8,128)(2,1)S(1)}, bf16[32,3584]{1,0:T(8,128)(2,1)S(1)}, u32[]{:S(2)}, u32[]{:S(2)}) collective-permute-start(bf16[32,3584]{1,0:T(8,128)(2,1)S(1)} %get-tuple-element.23), channel_id=1, source_target_pairs={{4,0},{5,1},{8,4},{9,5},{12,8},{13,9},{14,12},{15,13},{10,14},{11,... | collective-permute-start | bytes 688136 | tf_op jit(solution)/shard_map/ppermute | solution.py:138
  82.3 6.9 %collective-permute-start.22 = (bf16[32,3584]{1,0:T(8,128)(2,1)S(1)}, bf16[32,3584]{1,0:T(8,128)(2,1)S(1)}, u32[]{:S(2)}, u32[]{:S(2)}) collective-permute-start(bf16[32,3584]{1,0:T(8,128)(2,1)S(1)} %get-tuple-element.17), channel_id=1, source_target_pairs={{0,4},{1,5},{4,8},{5,9},{8,12},{9,13},{12,14},{13,15},{14,10},{15,... | collective-permute-start | bytes 688136 | tf_op jit(solution)/shard_map/ppermute | solution.py:137
  83.9 6.6 %collective-permute-start.26 = (bf16[32,3584]{1,0:T(8,128)(2,1)S(1)}, bf16[32,3584]{1,0:T(8,128)(2,1)S(1)}, u32[]{:S(2)}, u32[]{:S(2)}) collective-permute-start(bf16[32,3584]{1,0:T(8,128)(2,1)S(1)} %get-tuple-element.18), channel_id=1, source_target_pairs={{4,0},{5,1},{8,4},{9,5},{12,8},{13,9},{14,12},{15,13},{10,14},{11,... | collective-permute-start | bytes 688136 | tf_op jit(solution)/shard_map/ppermute | solution.py:138

commit v3 on v2

--- a/solution.py
+++ b/solution.py
@@ -69,8 +69,8 @@
             pltpu.SemaphoreType.DMA((3,)),
         ],
         compiler_params=pltpu.CompilerParams(vmem_limit_bytes=SCRATCH),
-        cost_estimate=pl.CostEstimate(flops=40 * 2**30, bytes_accessed=0, transcendentals=0),
-    )(tokens, routes.T, gates.T)
+        cost_estimate=pl.CostEstimate(flops=10 * 2**30, bytes_accessed=0, transcendentals=0),
+    )(*(pltpu.with_memory_space_constraint(a, pltpu.HBM) for a in (tokens, routes.T, gates.T)))
 
 
 def ffn_kernel(count, rows, experts, tile_ff, tile_d, me_ref, *refs):

time: 91.6 us -> 90 us (0.983)
  local copies, waits for them, and re-layouts: 11.7 us -> 9.35 us
    unnamed x19 -> x13, local copies, waits for them, and re-layouts: 11.6 us -> 9.27 us
where the time goes in v3:
time: 90 us; the launch traced here: 89.8 us
  waiting for transfers between devices  39.8 us (44%)
  starting transfers between devices  19.6 us (22%)
  Pallas kernels  19.5 us (22%)
  local copies, waits for them, and re-layouts  9.35 us (10%)
  other arithmetic  1.36 us (2%)
    ppermute x8, waiting for transfers between devices, local(): right = lambda a: lax.ppermute(a, 'node', forth)  31.7 us
    pallas_call x3, Pallas kernels, ffn(): pl.pallas_call(functools.partial(ffn_kernel, count, rows, experts, tile_f...  18.5 us
    ppermute x8, starting transfers between devices, local(): right = lambda a: lax.ppermute(a, 'node', forth)  13.5 us
    unnamed x13, local copies, waits for them, and re-layouts  9.27 us
    ppermute x8, waiting for transfers between devices, local(): left = lambda a: lax.ppermute(a, 'node', back)  4.55 us
    ppermute x8, starting transfers between devices, local(): left = lambda a: lax.ppermute(a, 'node', back)  3.85 us
    ppermute x11, waiting for transfers between devices, local(): sibling = lambda a: lax.ppermute(a, 'node', swap)  3.63 us
    ppermute x11, starting transfers between devices, local(): sibling = lambda a: lax.ppermute(a, 'node', swap)  2.19 us
  transfers between devices with their start and end apart: 27, of which 14 were waited for; matrix products, arithmetic and copies ran while one was open for 1% of the time, Pallas kernels for 13%

profile of v3, /device:TPU:0, one launch (start us, length us, event | category | flops | bytes accessed | tf_op | source)
XLA Modules:
  0.0 89.8 jit_solution(5963045942915216559)
XLA Ops:
  0.0 1.0 %shard_map.64.refs_0_ = bf16[32,3712]{1,0:T(8,128)(2,1)S(1)} custom-call(bf16[32,3584]{1,0:T(8,128)(2,1)} %tok_hbm.1, s32[8,32]{1,0:T(8,128)} %bitcast.3, f32[8,32]{1,0:T(8,128)} %bitcast.4), custom_call_target="tpu_custom_call" | custom-call | flops 10737418240 | tf_op jit(solution)/shard_map/pallas_call | solution.py:61
  1.0 3.1 %collective-permute-start.1 = (bf16[32,3712]{1,0:T(8,128)(2,1)S(1)}, bf16[32,3712]{1,0:T(8,128)(2,1)S(1)}, u32[]{:S(2)}, u32[]{:S(2)}) collective-permute-start(bf16[32,3712]{1,0:T(8,128)(2,1)S(1)} %shard_map.64.refs_0_), channel_id=1, source_target_pairs={{0,4},{1,5},{4,8},{5,9},{8,12},{9,13},{12,14},{13,15},{14,10},{15,... | collective-permute-start | bytes 712712 | tf_op jit(solution)/shard_map/ppermute | solution.py:137
  4.1 5.7 %collective-permute-done.1.refs_2_ = bf16[32,3712]{1,0:T(8,128)(2,1)S(1)} collective-permute-done((bf16[32,3712]{1,0:T(8,128)(2,1)S(1)}, bf16[32,3712]{1,0:T(8,128)(2,1)S(1)}, u32[]{:S(2)}, u32[]{:S(2)}) %collective-permute-start.1) | collective-permute-done | bytes 237600 | tf_op jit(solution)/shard_map/ppermute | solution.py:137
  9.8 1.8 %collective-permute-start.6 = (bf16[32,3712]{1,0:T(8,128)(2,1)S(1)}, bf16[32,3712]{1,0:T(8,128)(2,1)S(1)}, u32[]{:S(2)}, u32[]{:S(2)}) collective-permute-start(bf16[32,3712]{1,0:T(8,128)(2,1)S(1)} %collective-permute-done.1.refs_2_), channel_id=1, source_target_pairs={{0,4},{1,5},{4,8},{5,9},{8,12},{9,13},{12,14},{13,15},{14,10},{15,... | collective-permute-start | bytes 712712 | tf_op jit(solution)/shard_map/ppermute | solution.py:137
  11.6 0.2 collective-permute-start.7
  11.8 4.9 %collective-permute-done.6.refs_0_ = bf16[32,3712]{1,0:T(8,128)(2,1)S(1)} collective-permute-done((bf16[32,3712]{1,0:T(8,128)(2,1)S(1)}, bf16[32,3712]{1,0:T(8,128)(2,1)S(1)}, u32[]{:S(2)}, u32[]{:S(2)}) %collective-permute-start.6) | collective-permute-done | bytes 237600 | tf_op jit(solution)/shard_map/ppermute | solution.py:137
  16.8 1.5 %collective-permute-start.11 = (bf16[32,3712]{1,0:T(8,128)(2,1)S(1)}, bf16[32,3712]{1,0:T(8,128)(2,1)S(1)}, u32[]{:S(2)}, u32[]{:S(2)}) collective-permute-start(bf16[32,3712]{1,0:T(8,128)(2,1)S(1)} %collective-permute-done.6.refs_0_), channel_id=1, source_target_pairs={{0,4},{1,5},{4,8},{5,9},{8,12},{9,13},{12,14},{13,15},{14,10},{15,... | collective-permute-start | bytes 712712 | tf_op jit(solution)/shard_map/ppermute | solution.py:137
  18.3 0.5 collective-permute-start.13
  18.8 4.1 %collective-permute-done.11.refs_2_ = bf16[32,3712]{1,0:T(8,128)(2,1)S(1)} collective-permute-done((bf16[32,3712]{1,0:T(8,128)(2,1)S(1)}, bf16[32,3712]{1,0:T(8,128)(2,1)S(1)}, u32[]{:S(2)}, u32[]{:S(2)}) %collective-permute-start.11) | collective-permute-done | bytes 237600 | tf_op jit(solution)/shard_map/ppermute | solution.py:137
  23.0 1.8 %collective-permute-start.12 = (bf16[16,3712]{1,0:T(8,128)(2,1)S(1)}, bf16[16,3712]{1,0:T(8,128)(2,1)S(1)}, u32[]{:S(2)}, u32[]{:S(2)}) collective-permute-start(bf16[16,3712]{1,0:T(8,128)(2,1)S(1)} %slice.101), channel_id=1, source_target_pairs={{0,4},{1,5},{4,8},{5,9},{8,12},{9,13},{12,14},{13,15},{14,10},{15,... | collective-permute-start | bytes 356360 | tf_op jit(solution)/shard_map/ppermute | solution.py:137
  24.8 0.3 collective-permute-start.14
  25.1 0.5 collective-permute-start.17
  25.6 2.2 %collective-permute-done.12 = bf16[16,3712]{1,0:T(8,128)(2,1)S(1)} collective-permute-done((bf16[16,3712]{1,0:T(8,128)(2,1)S(1)}, bf16[16,3712]{1,0:T(8,128)(2,1)S(1)}, u32[]{:S(2)}, u32[]{:S(2)}) %collective-permute-start.12) | collective-permute-done | bytes 118816 | tf_op jit(solution)/shard_map/ppermute | solution.py:137
  27.9 1.9 %collective-permute-done.14 = bf16[16,3712]{1,0:T(8,128)(2,1)S(1)} collective-permute-done((bf16[16,3712]{1,0:T(8,128)(2,1)S(1)}, bf16[16,3712]{1,0:T(8,128)(2,1)S(1)}, u32[]{:S(2)}, u32[]{:S(2)}) %collective-permute-start.14) | collective-permute-done | bytes 118816 | tf_op jit(solution)/shard_map/ppermute | solution.py:138
  29.8 1.5 %collective-permute-done.15.refs_3_ = bf16[32,3712]{1,0:T(8,128)(2,1)S(1)} collective-permute-done((bf16[32,3712]{1,0:T(8,128)(2,1)S(1)}, bf16[32,3712]{1,0:T(8,128)(2,1)S(1)}, u32[]{:S(2)}, u32[]{:S(2)}) %collective-permute-start.15) | collective-permute-done | bytes 237600 | tf_op jit(solution)/shard_map/ppermute | solution.py:139
  31.3 3.1 %copy-done = bf16[1,3584,1024]{2,1,0:T(8,128)(2,1)S(1)} copy-done((bf16[1,3584,1024]{2,1,0:T(8,128)(2,1)S(1)}, bf16[1,3584,1024]{2,1,0:T(8,128)(2,1)}, u32[]{:S(2)}) %copy-start) | copy-done | bytes 7340056
  34.4 3.1 %copy-done.2 = bf16[1,3584,1024]{2,1,0:T(8,128)(2,1)S(1)} copy-done((bf16[1,3584,1024]{2,1,0:T(8,128)(2,1)S(1)}, bf16[1,3584,1024]{2,1,0:T(8,128)(2,1)}, u32[]{:S(2)}) %copy-start.2) | copy-done | bytes 7340056
  37.5 3.1 %copy-done.4 = bf16[1,1024,3584]{2,1,0:T(8,128)(2,1)S(1)} copy-done((bf16[1,1024,3584]{2,1,0:T(8,128)(2,1)S(1)}, bf16[1,1024,3584]{2,1,0:T(8,128)(2,1)}, u32[]{:S(2)}) %copy-start.4) | copy-done | bytes 7340056
  40.5 6.6 %shard_map.67 = (f32[96,3584]{1,0:T(8,128)S(1)}, bf16[96,3584]{1,0:T(8,128)(2,1)S(1)}) custom-call(s32[1]{0:T(128)} %bitcast.me_ref, bf16[32,3712]{1,0:T(8,128)(2,1)S(1)} %constant_dynamic-update-slice_fusion.refs_0_, bf16[32,3712]{1,0:T(8,128)(2,1)S(1)} %collective-permute-done.13.refs_1_, bf16[32,3712]{1,0:T(8,128)(2,1)S(1)} %collective-permute-done.11.refs_2_, ...), custom_call_target="tpu_custom_call" | custom-call | flops 5637144576 | tf_op jit(solution)/shard_map/pallas_call | solution.py:109
  47.2 0.2 collective-permute-start.18
  47.4 0.4 collective-permute-start.2
  47.8 0.1 collective-permute-start.3
  47.9 0.4 collective-permute-start.4
  48.3 0.1 collective-permute-start.8
  48.4 1.0 %collective-permute-done.18 = bf16[96,3584]{1,0:T(8,128)(2,1)S(1)} collective-permute-done((bf16[96,3584]{1,0:T(8,128)(2,1)S(1)}, bf16[96,3584]{1,0:T(8,128)(2,1)S(1)}, u32[]{:S(2)}, u32[]{:S(2)}) %collective-permute-start.18) | collective-permute-done | bytes 688160 | tf_op jit(solution)/shard_map/ppermute | solution.py:139
  49.4 0.1 collective-permute-start.9
  49.5 0.1 convert_add_fusion.1
  49.7 1.0 %collective-permute-done.8.refs_2_ = bf16[32,3712]{1,0:T(8,128)(2,1)S(1)} collective-permute-done((bf16[32,3712]{1,0:T(8,128)(2,1)S(1)}, bf16[32,3712]{1,0:T(8,128)(2,1)S(1)}, u32[]{:S(2)}, u32[]{:S(2)}) %collective-permute-start.8) | collective-permute-done | bytes 237600 | tf_op jit(solution)/shard_map/ppermute | solution.py:139
  50.7 0.2 collective-permute-start.23
  51.0 0.1 collective-permute-done.9.refs_3_
  51.1 5.3 %shard_map.66 = (f32[64,3584]{1,0:T(8,128)S(1)}, bf16[64,3584]{1,0:T(8,128)(2,1)S(1)}) custom-call(s32[1]{0:T(128)} %bitcast.me_ref, bf16[32,3712]{1,0:T(8,128)(2,1)S(1)} %collective-permute-done.6.refs_0_, bf16[32,3712]{1,0:T(8,128)(2,1)S(1)} %collective-permute-done.7.refs_1_, bf16[32,3712]{1,0:T(8,128)(2,1)S(1)} %collective-permute-done.8.refs_2_, ...), custom_call_target="tpu_custom_call" | custom-call | flops 5637144576 | tf_op jit(solution)/shard_map/pallas_call | solution.py:109
  56.4 0.2 collective-permute-start.10
  56.6 1.6 %collective-permute-start.19 = (bf16[16,3584]{1,0:T(8,128)(2,1)S(1)}, bf16[16,3584]{1,0:T(8,128)(2,1)S(1)}, u32[]{:S(2)}, u32[]{:S(2)}) collective-permute-start(bf16[16,3584]{1,0:T(8,128)(2,1)S(1)} %get-tuple-element.24), channel_id=1, source_target_pairs={{0,4},{1,5},{4,8},{5,9},{8,12},{9,13},{12,14},{13,15},{14,10},{15,... | collective-permute-start | bytes 344072 | tf_op jit(solution)/shard_map/ppermute | solution.py:137
  58.3 3.8 %collective-permute-done.19 = bf16[16,3584]{1,0:T(8,128)(2,1)S(1)} collective-permute-done((bf16[16,3584]{1,0:T(8,128)(2,1)S(1)}, bf16[16,3584]{1,0:T(8,128)(2,1)S(1)}, u32[]{:S(2)}, u32[]{:S(2)}) %collective-permute-start.19) | collective-permute-done | bytes 114720 | tf_op jit(solution)/shard_map/ppermute | solution.py:137
  62.1 1.7 %collective-permute-start.24 = (bf16[32,3584]{1,0:T(8,128)(2,1)S(1)}, bf16[32,3584]{1,0:T(8,128)(2,1)S(1)}, u32[]{:S(2)}, u32[]{:S(2)}) collective-permute-start(bf16[32,3584]{1,0:T(8,128)(2,1)S(1)} %pad_maximum_fusion.1), channel_id=1, source_target_pairs={{4,0},{5,1},{8,4},{9,5},{12,8},{13,9},{14,12},{15,13},{10,14},{11,... | collective-permute-start | bytes 688136 | tf_op jit(solution)/shard_map/ppermute | solution.py:138
  63.9 0.3 collective-permute-start.20
  64.3 6.6 %shard_map.65 = (f32[96,3584]{1,0:T(8,128)S(1)}, bf16[96,3584]{1,0:T(8,128)(2,1)S(1)}) custom-call(s32[1]{0:T(128)} %bitcast.me_ref, bf16[32,3712]{1,0:T(8,128)(2,1)S(1)} %shard_map.64.refs_0_, bf16[32,3712]{1,0:T(8,128)(2,1)S(1)} %collective-permute-done.refs_1_, bf16[32,3712]{1,0:T(8,128)(2,1)S(1)} %collective-permute-done.1.refs_2_, ...), custom_call_target="tpu_custom_call" | custom-call | flops 5637144576 | tf_op jit(solution)/shard_map/pallas_call | solution.py:109
  71.0 0.1 add_convert_fusion.4
  71.2 1.7 %collective-permute-start.21 = (bf16[32,3584]{1,0:T(8,128)(2,1)S(1)}, bf16[32,3584]{1,0:T(8,128)(2,1)S(1)}, u32[]{:S(2)}, u32[]{:S(2)}) collective-permute-start(bf16[32,3584]{1,0:T(8,128)(2,1)S(1)} %get-tuple-element.22), channel_id=1, source_target_pairs={{0,4},{1,5},{4,8},{5,9},{8,12},{9,13},{12,14},{13,15},{14,10},{15,... | collective-permute-start | bytes 688136 | tf_op jit(solution)/shard_map/ppermute | solution.py:137
  72.9 0.4 collective-permute-start.25
  73.2 6.0 %collective-permute-done.21 = bf16[32,3584]{1,0:T(8,128)(2,1)S(1)} collective-permute-done((bf16[32,3584]{1,0:T(8,128)(2,1)S(1)}, bf16[32,3584]{1,0:T(8,128)(2,1)S(1)}, u32[]{:S(2)}, u32[]{:S(2)}) %collective-permute-start.21) | collective-permute-done | bytes 229408 | tf_op jit(solution)/shard_map/ppermute | solution.py:137
  79.2 1.4 %collective-permute-done.25 = bf16[32,3584]{1,0:T(8,128)(2,1)S(1)} collective-permute-done((bf16[32,3584]{1,0:T(8,128)(2,1)S(1)}, bf16[32,3584]{1,0:T(8,128)(2,1)S(1)}, u32[]{:S(2)}, u32[]{:S(2)}) %collective-permute-start.25) | collective-permute-done | bytes 229408 | tf_op jit(solution)/shard_map/ppermute | solution.py:138
  80.6 0.2 add_convert_fusion.3
  80.7 1.6 %collective-permute-start.22 = (bf16[32,3584]{1,0:T(8,128)(2,1)S(1)}, bf16[32,3584]{1,0:T(8,128)(2,1)S(1)}, u32[]{:S(2)}, u32[]{:S(2)}) collective-permute-start(bf16[32,3584]{1,0:T(8,128)(2,1)S(1)} %get-tuple-element.17), channel_id=1, source_target_pairs={{0,4},{1,5},{4,8},{5,9},{8,12},{9,13},{12,14},{13,15},{14,10},{15,... | collective-permute-start | bytes 688136 | tf_op jit(solution)/shard_map/ppermute | solution.py:137
  82.4 0.4 collective-permute-start.26
  82.8 4.9 %collective-permute-done.22 = bf16[32,3584]{1,0:T(8,128)(2,1)S(1)} collective-permute-done((bf16[32,3584]{1,0:T(8,128)(2,1)S(1)}, bf16[32,3584]{1,0:T(8,128)(2,1)S(1)}, u32[]{:S(2)}, u32[]{:S(2)}) %collective-permute-start.22) | collective-permute-done | bytes 229408 | tf_op jit(solution)/shard_map/ppermute | solution.py:137
  87.7 1.3 %collective-permute-done.26 = bf16[32,3584]{1,0:T(8,128)(2,1)S(1)} collective-permute-done((bf16[32,3584]{1,0:T(8,128)(2,1)S(1)}, bf16[32,3584]{1,0:T(8,128)(2,1)S(1)}, u32[]{:S(2)}, u32[]{:S(2)}) %collective-permute-start.26) | collective-permute-done | bytes 229408 | tf_op jit(solution)/shard_map/ppermute | solution.py:138
  89.0 0.8 add_convert_fusion
  (37 shorter events, 0.4 us)
Async XLA Ops:
  1.0 8.8 %collective-permute-start.1 = (bf16[32,3712]{1,0:T(8,128)(2,1)S(1)}, bf16[32,3712]{1,0:T(8,128)(2,1)S(1)}, u32[]{:S(2)}, u32[]{:S(2)}) collective-permute-start(bf16[32,3712]{1,0:T(8,128)(2,1)S(1)} %shard_map.64.refs_0_), channel_id=1, source_target_pairs={{0,4},{1,5},{4,8},{5,9},{8,12},{9,13},{12,14},{13,15},{14,10},{15,... | collective-permute-start | bytes 712712 | tf_op jit(solution)/shard_map/ppermute | solution.py:137
  4.1 7.5 %collective-permute-start = (bf16[32,3712]{1,0:T(8,128)(2,1)S(1)}, bf16[32,3712]{1,0:T(8,128)(2,1)S(1)}, u32[]{:S(2)}, u32[]{:S(2)}) collective-permute-start(bf16[32,3712]{1,0:T(8,128)(2,1)S(1)} %shard_map.64.refs_0_), channel_id=1, source_target_pairs={{4,0},{5,1},{8,4},{9,5},{12,8},{13,9},{14,12},{15,13},{10,14},{11,... | collective-permute-start | bytes 712712 | tf_op jit(solution)/shard_map/ppermute | solution.py:138
  9.8 7.0 %collective-permute-start.6 = (bf16[32,3712]{1,0:T(8,128)(2,1)S(1)}, bf16[32,3712]{1,0:T(8,128)(2,1)S(1)}, u32[]{:S(2)}, u32[]{:S(2)}) collective-permute-start(bf16[32,3712]{1,0:T(8,128)(2,1)S(1)} %collective-permute-done.1.refs_2_), channel_id=1, source_target_pairs={{0,4},{1,5},{4,8},{5,9},{8,12},{9,13},{12,14},{13,15},{14,10},{15,... | collective-permute-start | bytes 712712 | tf_op jit(solution)/shard_map/ppermute | solution.py:137
  11.6 6.6 %collective-permute-start.7 = (bf16[32,3712]{1,0:T(8,128)(2,1)S(1)}, bf16[32,3712]{1,0:T(8,128)(2,1)S(1)}, u32[]{:S(2)}, u32[]{:S(2)}) collective-permute-start(bf16[32,3712]{1,0:T(8,128)(2,1)S(1)} %collective-permute-done.refs_1_), channel_id=1, source_target_pairs={{4,0},{5,1},{8,4},{9,5},{12,8},{13,9},{14,12},{15,13},{10,14},{11,... | collective-permute-start | bytes 712712 | tf_op jit(solution)/shard_map/ppermute | solution.py:138
  16.8 6.2 %collective-permute-start.11 = (bf16[32,3712]{1,0:T(8,128)(2,1)S(1)}, bf16[32,3712]{1,0:T(8,128)(2,1)S(1)}, u32[]{:S(2)}, u32[]{:S(2)}) collective-permute-start(bf16[32,3712]{1,0:T(8,128)(2,1)S(1)} %collective-permute-done.6.refs_0_), channel_id=1, source_target_pairs={{0,4},{1,5},{4,8},{5,9},{8,12},{9,13},{12,14},{13,15},{14,10},{15,... | collective-permute-start | bytes 712712 | tf_op jit(solution)/shard_map/ppermute | solution.py:137
  18.3 6.6 %collective-permute-start.13 = (bf16[32,3712]{1,0:T(8,128)(2,1)S(1)}, bf16[32,3712]{1,0:T(8,128)(2,1)S(1)}, u32[]{:S(2)}, u32[]{:S(2)}) collective-permute-start(bf16[32,3712]{1,0:T(8,128)(2,1)S(1)} %collective-permute-done.7.refs_1_), channel_id=1, source_target_pairs={{4,0},{5,1},{8,4},{9,5},{12,8},{13,9},{14,12},{15,13},{10,14},{11,... | collective-permute-start | bytes 712712 | tf_op jit(solution)/shard_map/ppermute | solution.py:138
  23.0 4.9 %collective-permute-start.12 = (bf16[16,3712]{1,0:T(8,128)(2,1)S(1)}, bf16[16,3712]{1,0:T(8,128)(2,1)S(1)}, u32[]{:S(2)}, u32[]{:S(2)}) collective-permute-start(bf16[16,3712]{1,0:T(8,128)(2,1)S(1)} %slice.101), channel_id=1, source_target_pairs={{0,4},{1,5},{4,8},{5,9},{8,12},{9,13},{12,14},{13,15},{14,10},{15,... | collective-permute-start | bytes 356360 | tf_op jit(solution)/shard_map/ppermute | solution.py:137
  24.8 4.9 %collective-permute-start.14 = (bf16[16,3712]{1,0:T(8,128)(2,1)S(1)}, bf16[16,3712]{1,0:T(8,128)(2,1)S(1)}, u32[]{:S(2)}, u32[]{:S(2)}) collective-permute-start(bf16[16,3712]{1,0:T(8,128)(2,1)S(1)} %slice.102), channel_id=1, source_target_pairs={{4,0},{5,1},{8,4},{9,5},{12,8},{13,9},{14,12},{15,13},{10,14},{11,... | collective-permute-start | bytes 356360 | tf_op jit(solution)/shard_map/ppermute | solution.py:138
  25.1 4.7 %collective-permute-start.16 = (bf16[32,3712]{1,0:T(8,128)(2,1)S(1)}, bf16[32,3712]{1,0:T(8,128)(2,1)S(1)}, u32[]{:S(2)}, u32[]{:S(2)}) collective-permute-start(bf16[32,3712]{1,0:T(8,128)(2,1)S(1)} %collective-permute-done.13.refs_1_), channel_id=1, source_target_pairs={{0,1},{1,0},{2,3},{3,2},{4,5},{5,4},{6,7},{7,6},{8,9},{9,8},{10,11... | collective-permute-start | bytes 712712 | tf_op jit(solution)/shard_map/ppermute | solution.py:139
  25.1 4.7 %collective-permute-start.17 = (bf16[32,3712]{1,0:T(8,128)(2,1)S(1)}, bf16[32,3712]{1,0:T(8,128)(2,1)S(1)}, u32[]{:S(2)}, u32[]{:S(2)}) collective-permute-start(bf16[32,3712]{1,0:T(8,128)(2,1)S(1)} %collective-permute-done.11.refs_2_), channel_id=1, source_target_pairs={{0,1},{1,0},{2,3},{3,2},{4,5},{5,4},{6,7},{7,6},{8,9},{9,8},{10,11... | collective-permute-start | bytes 712712 | tf_op jit(solution)/shard_map/ppermute | solution.py:139
  29.7 1.6 %collective-permute-start.15 = (bf16[32,3712]{1,0:T(8,128)(2,1)S(1)}, bf16[32,3712]{1,0:T(8,128)(2,1)S(1)}, u32[]{:S(2)}, u32[]{:S(2)}) collective-permute-start(bf16[32,3712]{1,0:T(8,128)(2,1)S(1)} %constant_dynamic-update-slice_fusion.refs_0_), channel_id=1, source_target_pairs={{0,1},{1,0},{2,3},{3,2},{4,5},{5,4},{6,7},{7,6},{8,9},{9,8},{10,11... | collective-permute-start | bytes 712712 | tf_op jit(solution)/shard_map/ppermute | solution.py:139
  31.3 3.1 %copy-start = (bf16[1,3584,1024]{2,1,0:T(8,128)(2,1)S(1)}, bf16[1,3584,1024]{2,1,0:T(8,128)(2,1)}, u32[]{:S(2)}) copy-start(bf16[1,3584,1024]{2,1,0:T(8,128)(2,1)} %refs_6_.5) | copy-start | bytes 22020100
  34.4 3.1 %copy-start.2 = (bf16[1,3584,1024]{2,1,0:T(8,128)(2,1)S(1)}, bf16[1,3584,1024]{2,1,0:T(8,128)(2,1)}, u32[]{:S(2)}) copy-start(bf16[1,3584,1024]{2,1,0:T(8,128)(2,1)} %refs_7_.3) | copy-start | bytes 22020100
  37.5 3.1 %copy-start.4 = (bf16[1,1024,3584]{2,1,0:T(8,128)(2,1)S(1)}, bf16[1,1024,3584]{2,1,0:T(8,128)(2,1)}, u32[]{:S(2)}) copy-start(bf16[1,1024,3584]{2,1,0:T(8,128)(2,1)} %refs_8_.3) | copy-start | bytes 22020100
  40.5 10.6 %copy-start.1 = (bf16[1,3584,1024]{2,1,0:T(8,128)(2,1)S(1)}, bf16[1,3584,1024]{2,1,0:T(8,128)(2,1)}, u32[]{:S(2)}) copy-start(bf16[1,3584,1024]{2,1,0:T(8,128)(2,1)} %refs_6_.5) | copy-start | bytes 22020100
  40.5 10.6 %copy-start.3 = (bf16[1,3584,1024]{2,1,0:T(8,128)(2,1)S(1)}, bf16[1,3584,1024]{2,1,0:T(8,128)(2,1)}, u32[]{:S(2)}) copy-start(bf16[1,3584,1024]{2,1,0:T(8,128)(2,1)} %refs_7_.3) | copy-start | bytes 22020100
  40.5 10.6 %copy-start.5 = (bf16[1,1024,3584]{2,1,0:T(8,128)(2,1)S(1)}, bf16[1,1024,3584]{2,1,0:T(8,128)(2,1)}, u32[]{:S(2)}) copy-start(bf16[1,1024,3584]{2,1,0:T(8,128)(2,1)} %refs_8_.3) | copy-start | bytes 22020100
  47.2 2.2 %collective-permute-start.18 = (bf16[96,3584]{1,0:T(8,128)(2,1)S(1)}, bf16[96,3584]{1,0:T(8,128)(2,1)S(1)}, u32[]{:S(2)}, u32[]{:S(2)}) collective-permute-start(bf16[96,3584]{1,0:T(8,128)(2,1)S(1)} %get-tuple-element.16), channel_id=1, source_target_pairs={{0,1},{1,0},{2,3},{3,2},{4,5},{5,4},{6,7},{7,6},{8,9},{9,8},{10,11... | collective-permute-start | bytes 2064392 | tf_op jit(solution)/shard_map/ppermute | solution.py:139
  47.4 16.6 %collective-permute-start.2 = (bf16[32,3712]{1,0:T(8,128)(2,1)S(1)}, bf16[32,3712]{1,0:T(8,128)(2,1)S(1)}, u32[]{:S(2)}, u32[]{:S(2)}) collective-permute-start(bf16[32,3712]{1,0:T(8,128)(2,1)S(1)} %shard_map.64.refs_0_), channel_id=1, source_target_pairs={{0,1},{1,0},{2,3},{3,2},{4,5},{5,4},{6,7},{7,6},{8,9},{9,8},{10,11... | collective-permute-start | bytes 712712 | tf_op jit(solution)/shard_map/ppermute | solution.py:139
  47.8 16.5 %collective-permute-start.3 = (bf16[32,3712]{1,0:T(8,128)(2,1)S(1)}, bf16[32,3712]{1,0:T(8,128)(2,1)S(1)}, u32[]{:S(2)}, u32[]{:S(2)}) collective-permute-start(bf16[32,3712]{1,0:T(8,128)(2,1)S(1)} %collective-permute-done.refs_1_), channel_id=1, source_target_pairs={{0,1},{1,0},{2,3},{3,2},{4,5},{5,4},{6,7},{7,6},{8,9},{9,8},{10,11... | collective-permute-start | bytes 712712 | tf_op jit(solution)/shard_map/ppermute | solution.py:139
  47.9 16.4 %collective-permute-start.4 = (bf16[32,3712]{1,0:T(8,128)(2,1)S(1)}, bf16[32,3712]{1,0:T(8,128)(2,1)S(1)}, u32[]{:S(2)}, u32[]{:S(2)}) collective-permute-start(bf16[32,3712]{1,0:T(8,128)(2,1)S(1)} %collective-permute-done.1.refs_2_), channel_id=1, source_target_pairs={{0,1},{1,0},{2,3},{3,2},{4,5},{5,4},{6,7},{7,6},{8,9},{9,8},{10,11... | collective-permute-start | bytes 712712 | tf_op jit(solution)/shard_map/ppermute | solution.py:139
  48.3 2.5 %collective-permute-start.8 = (bf16[32,3712]{1,0:T(8,128)(2,1)S(1)}, bf16[32,3712]{1,0:T(8,128)(2,1)S(1)}, u32[]{:S(2)}, u32[]{:S(2)}) collective-permute-start(bf16[32,3712]{1,0:T(8,128)(2,1)S(1)} %collective-permute-done.6.refs_0_), channel_id=1, source_target_pairs={{0,1},{1,0},{2,3},{3,2},{4,5},{5,4},{6,7},{7,6},{8,9},{9,8},{10,11... | collective-permute-start | bytes 712712 | tf_op jit(solution)/shard_map/ppermute | solution.py:139
  49.4 1.7 %collective-permute-start.9 = (bf16[32,3712]{1,0:T(8,128)(2,1)S(1)}, bf16[32,3712]{1,0:T(8,128)(2,1)S(1)}, u32[]{:S(2)}, u32[]{:S(2)}) collective-permute-start(bf16[32,3712]{1,0:T(8,128)(2,1)S(1)} %collective-permute-done.7.refs_1_), channel_id=1, source_target_pairs={{0,1},{1,0},{2,3},{3,2},{4,5},{5,4},{6,7},{7,6},{8,9},{9,8},{10,11... | collective-permute-start | bytes 712712 | tf_op jit(solution)/shard_map/ppermute | solution.py:139
  50.7 5.9 %collective-permute-start.23 = (bf16[16,3584]{1,0:T(8,128)(2,1)S(1)}, bf16[16,3584]{1,0:T(8,128)(2,1)S(1)}, u32[]{:S(2)}, u32[]{:S(2)}) collective-permute-start(bf16[16,3584]{1,0:T(8,128)(2,1)S(1)} %get-tuple-element.25), channel_id=1, source_target_pairs={{4,0},{5,1},{8,4},{9,5},{12,8},{13,9},{14,12},{15,13},{10,14},{11,... | collective-permute-start | bytes 344072 | tf_op jit(solution)/shard_map/ppermute | solution.py:138
  56.4 14.6 %collective-permute-start.10 = (bf16[64,3584]{1,0:T(8,128)(2,1)S(1)}, bf16[64,3584]{1,0:T(8,128)(2,1)S(1)}, u32[]{:S(2)}, u32[]{:S(2)}) collective-permute-start(bf16[64,3584]{1,0:T(8,128)(2,1)S(1)} %get-tuple-element.14), channel_id=1, source_target_pairs={{0,1},{1,0},{2,3},{3,2},{4,5},{5,4},{6,7},{7,6},{8,9},{9,8},{10,11... | collective-permute-start | bytes 1376264 | tf_op jit(solution)/shard_map/ppermute | solution.py:139
  56.6 5.5 %collective-permute-start.19 = (bf16[16,3584]{1,0:T(8,128)(2,1)S(1)}, bf16[16,3584]{1,0:T(8,128)(2,1)S(1)}, u32[]{:S(2)}, u32[]{:S(2)}) collective-permute-start(bf16[16,3584]{1,0:T(8,128)(2,1)S(1)} %get-tuple-element.24), channel_id=1, source_target_pairs={{0,4},{1,5},{4,8},{5,9},{8,12},{9,13},{12,14},{13,15},{14,10},{15,... | collective-permute-start | bytes 344072 | tf_op jit(solution)/shard_map/ppermute | solution.py:137
  62.1 8.8 %collective-permute-start.24 = (bf16[32,3584]{1,0:T(8,128)(2,1)S(1)}, bf16[32,3584]{1,0:T(8,128)(2,1)S(1)}, u32[]{:S(2)}, u32[]{:S(2)}) collective-permute-start(bf16[32,3584]{1,0:T(8,128)(2,1)S(1)} %pad_maximum_fusion.1), channel_id=1, source_target_pairs={{4,0},{5,1},{8,4},{9,5},{12,8},{13,9},{14,12},{15,13},{10,14},{11,... | collective-permute-start | bytes 688136 | tf_op jit(solution)/shard_map/ppermute | solution.py:138
  63.9 7.1 %collective-permute-start.20 = (bf16[32,3584]{1,0:T(8,128)(2,1)S(1)}, bf16[32,3584]{1,0:T(8,128)(2,1)S(1)}, u32[]{:S(2)}, u32[]{:S(2)}) collective-permute-start(bf16[32,3584]{1,0:T(8,128)(2,1)S(1)} %pad_maximum_fusion), channel_id=1, source_target_pairs={{0,4},{1,5},{4,8},{5,9},{8,12},{9,13},{12,14},{13,15},{14,10},{15,... | collective-permute-start | bytes 688136 | tf_op jit(solution)/shard_map/ppermute | solution.py:137
  70.9 2.3 %collective-permute-start.5 = (bf16[96,3584]{1,0:T(8,128)(2,1)S(1)}, bf16[96,3584]{1,0:T(8,128)(2,1)S(1)}, u32[]{:S(2)}, u32[]{:S(2)}) collective-permute-start(bf16[96,3584]{1,0:T(8,128)(2,1)S(1)} %get-tuple-element.12), channel_id=1, source_target_pairs={{0,1},{1,0},{2,3},{3,2},{4,5},{5,4},{6,7},{7,6},{8,9},{9,8},{10,11... | collective-permute-start | bytes 2064392 | tf_op jit(solution)/shard_map/ppermute | solution.py:139
  71.2 8.0 %collective-permute-start.21 = (bf16[32,3584]{1,0:T(8,128)(2,1)S(1)}, bf16[32,3584]{1,0:T(8,128)(2,1)S(1)}, u32[]{:S(2)}, u32[]{:S(2)}) collective-permute-start(bf16[32,3584]{1,0:T(8,128)(2,1)S(1)} %get-tuple-element.22), channel_id=1, source_target_pairs={{0,4},{1,5},{4,8},{5,9},{8,12},{9,13},{12,14},{13,15},{14,10},{15,... | collective-permute-start | bytes 688136 | tf_op jit(solution)/shard_map/ppermute | solution.py:137
  72.9 7.7 %collective-permute-start.25 = (bf16[32,3584]{1,0:T(8,128)(2,1)S(1)}, bf16[32,3584]{1,0:T(8,128)(2,1)S(1)}, u32[]{:S(2)}, u32[]{:S(2)}) collective-permute-start(bf16[32,3584]{1,0:T(8,128)(2,1)S(1)} %get-tuple-element.23), channel_id=1, source_target_pairs={{4,0},{5,1},{8,4},{9,5},{12,8},{13,9},{14,12},{15,13},{10,14},{11,... | collective-permute-start | bytes 688136 | tf_op jit(solution)/shard_map/ppermute | solution.py:138
  80.7 6.9 %collective-permute-start.22 = (bf16[32,3584]{1,0:T(8,128)(2,1)S(1)}, bf16[32,3584]{1,0:T(8,128)(2,1)S(1)}, u32[]{:S(2)}, u32[]{:S(2)}) collective-permute-start(bf16[32,3584]{1,0:T(8,128)(2,1)S(1)} %get-tuple-element.17), channel_id=1, source_target_pairs={{0,4},{1,5},{4,8},{5,9},{8,12},{9,13},{12,14},{13,15},{14,10},{15,... | collective-permute-start | bytes 688136 | tf_op jit(solution)/shard_map/ppermute | solution.py:137
  82.4 6.6 %collective-permute-start.26 = (bf16[32,3584]{1,0:T(8,128)(2,1)S(1)}, bf16[32,3584]{1,0:T(8,128)(2,1)S(1)}, u32[]{:S(2)}, u32[]{:S(2)}) collective-permute-start(bf16[32,3584]{1,0:T(8,128)(2,1)S(1)} %get-tuple-element.18), channel_id=1, source_target_pairs={{4,0},{5,1},{8,4},{9,5},{12,8},{13,9},{14,12},{15,13},{10,14},{11,... | collective-permute-start | bytes 688136 | tf_op jit(solution)/shard_map/ppermute | solution.py:138

commit v4 on v3

v4 whole, which is shorter than its diff:
```python
import functools

import jax
import jax.numpy as jnp
from jax import lax
from jax.experimental import pallas as pl
from jax.experimental.pallas import tpu as pltpu
from jax.sharding import PartitionSpec as P

F32, BF16 = jnp.float32, jnp.bfloat16
SCRATCH = 16 * 2**20


def chip_layout(mesh):
    names = list(mesh.axis_names)
    count = mesh.shape["node"]
    row = mesh.devices.transpose([names.index(n) for n in names if n != "node"] + [names.index("node")])
    row = list(row.reshape(-1, count)[0])
    where = [tuple(getattr(d, "coords", None) or (i // 2,)) for i, d in enumerate(row)]
    cores = 2 if count % 2 == 0 and all(where[i] == where[i + 1] for i in range(0, count, 2)) else 1
    chips = where[::cores]
    order = list(range(len(chips)))
    axes = [a for a in range(len(chips[0])) if len({c[a] for c in chips}) > 1]
    if len(axes) == 2:
        short, long = sorted(axes, key=lambda a: len({c[a] for c in chips}))
        low = min(c[short] for c in chips)
        if len({c[short] for c in chips}) == 2:
            order.sort(key=lambda i: (chips[i][short], chips[i][long] if chips[i][short] == low else -chips[i][long]))
    return cores, order


def pack_kernel(experts, tok_hbm, routes_hbm, gates_hbm, out_ref, routes_ref, gates_ref, sems):
    rows, width = tok_hbm.shape
    extra = out_ref.shape[1] - width
    moves = [
        pltpu.make_async_copy(routes_hbm, routes_ref, sems.at[0]),
        pltpu.make_async_copy(gates_hbm, gates_ref, sems.at[1]),
        pltpu.make_async_copy(tok_hbm, out_ref.at[:, :width], sems.at[2]),
    ]
    for move in moves:
        move.start()
    for move in moves[:2]:
        move.wait()
    lane = lax.broadcasted_iota(jnp.int32, (extra, rows), 0)
    expert, piece = lax.rem(lane, experts), lax.div(lane, experts)
    weight = jnp.zeros((extra, rows), F32)
    for k in range(routes_ref.shape[0]):
        weight += jnp.where(routes_ref[k : k + 1] == expert, gates_ref[k : k + 1], 0.0)
    high = weight.astype(BF16).astype(F32)
    middle = (weight - high).astype(BF16).astype(F32)
    low = weight - high - middle
    table = jnp.where(piece == 0, high, jnp.where(piece == 1, middle, jnp.where(piece == 2, low, 0.0)))
    out_ref[:, width:] = table.T.astype(BF16)
    moves[2].wait()


def pack(tokens, routes, gates, experts):
    rows, width = tokens.shape
    extra = pl.cdiv(3 * experts, 128) * 128
    there = pl.BlockSpec(memory_space=pltpu.HBM)
    return pl.pallas_call(
        functools.partial(pack_kernel, experts),
        out_shape=pltpu.VMEM((rows, width + extra), BF16),
        in_specs=[there] * 3,
        out_specs=pl.BlockSpec(memory_space=pltpu.VMEM),
        scratch_shapes=[
            pltpu.VMEM(routes.shape[::-1], routes.dtype),
            pltpu.VMEM(gates.shape[::-1], gates.dtype),
            pltpu.SemaphoreType.DMA((3,)),
        ],
        compiler_params=pltpu.CompilerParams(vmem_limit_bytes=SCRATCH),
    )(hbm(tokens), hbm(routes.T), hbm(gates.T))


def hbm(a):
    return pltpu.with_memory_space_constraint(a, pltpu.HBM)


def vmem(a):
    return pltpu.with_memory_space_constraint(a, pltpu.VMEM)


def fetches(parts, source, target, sems):
    step = target.shape[2] // parts
    moves = []
    for i in range(parts):
        at = (slice(None), slice(None), slice(i * step, (i + 1) * step))
        moves.append(pltpu.make_async_copy(source.at[at], target.at[at], sems.at[i]))
        moves[-1].start()
    return moves


def load_kernel(parts, source, after, target, sems):
    step = target.shape[1] // parts
    moves = [
        pltpu.make_async_copy(
            source.at[:, i * step : (i + 1) * step], target.at[:, i * step : (i + 1) * step], sems.at[i]
        )
        for i in range(parts)
    ]
    for move in moves:
        move.start()
    for move in moves:
        move.wait()


def load(weight, after):
    parts = 8 if weight.shape[1] % 128 == 0 else 1
    return pl.pallas_call(
        functools.partial(load_kernel, parts),
        out_shape=pltpu.VMEM(weight.shape, weight.dtype),
        in_specs=[pl.BlockSpec(memory_space=pltpu.HBM), pl.BlockSpec(memory_space=pl.ANY)],
        out_specs=pl.BlockSpec(memory_space=pltpu.VMEM),
        scratch_shapes=[pltpu.SemaphoreType.DMA((parts,))],
        compiler_params=pltpu.CompilerParams(vmem_limit_bytes=SCRATCH),
        cost_estimate=pl.CostEstimate(flops=0, bytes_accessed=2 * weight.size, transcendentals=0),
    )(hbm(weight), after)


def gather_rows(blocks, x_ref):
    rows, width = blocks[0].shape[0], x_ref.shape[1]
    for at, ref in enumerate(blocks):
        x_ref[at * rows : (at + 1) * rows, :] = ref[:, :width]


def gather_weights(experts, me_ref, blocks, width, w_ref):
    rows = blocks[0].shape[0]
    for at, ref in enumerate(blocks):
        table = ref[:, width:].astype(F32)
        lane = lax.broadcasted_iota(jnp.int32, table.shape, 1)
        own = lax.rem(lane, experts) == me_ref[0]
        w_ref[at * rows : (at + 1) * rows, :] = jnp.sum(jnp.where(own, table, 0.0), axis=1, keepdims=True)


def first_half(x_ref, gate_ref, up_ref, h_ref, tile, begin, end):
    @pl.loop(begin // tile, end // tile)
    def _(j):
        at = pl.ds(pl.multiple_of(j * tile, tile), tile)
        gate = jnp.dot(x_ref[...], gate_ref[0, :, at], preferred_element_type=F32)
        upper = jnp.dot(x_ref[...], up_ref[0, :, at], preferred_element_type=F32)
        h_ref[:, at] = (gate / (1.0 + jnp.exp(-gate)) * upper).astype(BF16)


def second_half(h_ref, down_ref, w_ref, mine_ref, other_ref, tile, begin, end):
    half = mine_ref.shape[0]

    @pl.loop(begin // tile, end // tile)
    def _(j):
        at = pl.ds(pl.multiple_of(j * tile, tile), tile)
        out = jnp.dot(h_ref[...], down_ref[0, :, at], preferred_element_type=F32) * w_ref[...]
        mine_ref[:, at] = out[:half]
        other_ref[:, at] = out[half:].astype(BF16)


def tiles(width, ff):
    return (256 if ff % 256 == 0 else ff), next(t for t in (512, 256, 128, width) if width % t == 0)


def hidden_kernel(count, tile, parts, *refs):
    blocks, (gate_ref, source, h_ref, *rest) = refs[:count], refs[count:]
    if parts:
        up_ref, x_ref, sems = rest
        moves = fetches(parts, source, up_ref, sems)
    else:
        up_ref, (x_ref,), moves = source, rest, []
    gather_rows(blocks, x_ref)
    ff = h_ref.shape[1]
    for i in range(max(parts, 1)):
        if parts:
            moves[i].wait()
        first_half(x_ref, gate_ref, up_ref, h_ref, tile, i * ff // max(parts, 1), (i + 1) * ff // max(parts, 1))


def hidden(blocks, w_gate, w_up, fetch):
    count, rows = len(blocks), blocks[0].shape[0]
    _, width, ff = w_gate.shape
    tile, _ = tiles(width, ff)
    parts = (2 if ff % (2 * tile) == 0 else 1) if fetch else 0
    here = pl.BlockSpec(memory_space=pltpu.VMEM)
    return pl.pallas_call(
        functools.partial(hidden_kernel, count, tile, parts),
        out_shape=[pltpu.VMEM((count * rows, ff), BF16)] + [pltpu.VMEM(w_up.shape, BF16)] * fetch,
        in_specs=[here] * (count + 1) + [pl.BlockSpec(memory_space=pltpu.HBM if fetch else pltpu.VMEM)],
        out_specs=[here] * (1 + fetch),
        scratch_shapes=[pltpu.VMEM((count * rows, width), BF16)] + [pltpu.SemaphoreType.DMA((parts,))] * fetch,
        compiler_params=pltpu.CompilerParams(vmem_limit_bytes=SCRATCH),
        cost_estimate=pl.CostEstimate(
            flops=4 * max(count * rows, 256) * width * ff, bytes_accessed=0, transcendentals=count * rows * ff
        ),
    )(*blocks, vmem(w_gate), hbm(w_up) if fetch else vmem(w_up))


def output_kernel(count, experts, tile, parts, me_ref, *refs):
    blocks, (h_ref, source, mine_ref, other_ref, *rest) = refs[:count], refs[count:]
    if parts:
        down_ref, w_ref, sems = rest
        moves = fetches(parts, source, down_ref, sems)
    else:
        down_ref, (w_ref,), moves = source, rest, []
    width = mine_ref.shape[1]
    gather_weights(experts, me_ref, blocks, width, w_ref)
    for i in range(max(parts, 1)):
        if parts:
            moves[i].wait()
        begin, end = i * width // max(parts, 1), (i + 1) * width // max(parts, 1)
        second_half(h_ref, down_ref, w_ref, mine_ref, other_ref, tile, begin, end)


def output(blocks, mine, me, experts, h, w_down, fetch):
    count, rows = len(blocks), blocks[0].shape[0]
    _, ff, width = w_down.shape
    _, tile = tiles(width, ff)
    parts = width // tile if fetch else 0
    here = pl.BlockSpec(memory_space=pltpu.VMEM)
    return pl.pallas_call(
        functools.partial(output_kernel, count, experts, tile, parts),
        out_shape=[pltpu.VMEM((mine * rows, width), F32), pltpu.VMEM(((count - mine) * rows, width), BF16)]
        + [pltpu.VMEM(w_down.shape, BF16)] * fetch,
        in_specs=[pl.BlockSpec(memory_space=pltpu.SMEM)]
        + [here] * (count + 1)
        + [pl.BlockSpec(memory_space=pltpu.HBM if fetch else pltpu.VMEM)],
        out_specs=[here] * (2 + fetch),
        scratch_shapes=[pltpu.VMEM((count * rows, 1), F32)] + [pltpu.SemaphoreType.DMA((parts,))] * fetch,
        compiler_params=pltpu.CompilerParams(vmem_limit_bytes=SCRATCH),
        cost_estimate=pl.CostEstimate(
            flops=2 * max(count * rows, 256) * width * ff, bytes_accessed=0, transcendentals=0
        ),
    )(me, *blocks, h, hbm(w_down) if fetch else vmem(w_down))


def expert_kernel(count, experts, tile_ff, tile_d, me_ref, *refs):
    blocks, (gate_ref, up_ref, down_ref, mine_ref, other_ref, x_ref, w_ref, h_ref) = refs[:count], refs[count:]
    gather_rows(blocks, x_ref)
    gather_weights(experts, me_ref, blocks, x_ref.shape[1], w_ref)
    first_half(x_ref, gate_ref, up_ref, h_ref, tile_ff, 0, h_ref.shape[1])
    second_half(h_ref, down_ref, w_ref, mine_ref, other_ref, tile_d, 0, x_ref.shape[1])


def expert(blocks, mine, me, experts, w_gate, w_up, w_down):
    count, rows = len(blocks), blocks[0].shape[0]
    _, width, ff = w_gate.shape
    total = count * rows
    here = pl.BlockSpec(memory_space=pltpu.VMEM)
    return pl.pallas_call(
        functools.partial(expert_kernel, count, experts, *tiles(width, ff)),
        out_shape=[pltpu.VMEM((mine * rows, width), F32), pltpu.VMEM((total - mine * rows, width), BF16)],
        in_specs=[pl.BlockSpec(memory_space=pltpu.SMEM)] + [here] * (count + 3),
        out_specs=[here] * 2,
        scratch_shapes=[pltpu.VMEM((total, width), BF16), pltpu.VMEM((total, 1), F32), pltpu.VMEM((total, ff), BF16)],
        compiler_params=pltpu.CompilerParams(vmem_limit_bytes=SCRATCH),
        cost_estimate=pl.CostEstimate(
            flops=6 * max(total, 256) * width * ff, bytes_accessed=0, transcendentals=total * ff
        ),
    )(me, *blocks, vmem(w_gate), vmem(w_up), vmem(w_down))


def local(cores, order, tokens, routes, gates, w_gate, w_up, w_down):
    chips = len(order)
    experts = chips * cores
    rows, width = tokens.shape
    me = lax.axis_index("node").astype(jnp.int32).reshape(1)
    forth = [(order[i] * cores + c, order[(i + 1) % chips] * cores + c) for i in range(chips) for c in range(cores)]
    back = [(b, a) for a, b in forth]
    swap = [(chip * cores + c, chip * cores + 1 - c) for chip in range(chips) for c in range(cores)]
    right = lambda a: lax.ppermute(a, "node", forth)
    left = lambda a: lax.ppermute(a, "node", back)
    sibling = lambda a: lax.ppermute(a, "node", swap)
    together = lax.optimization_barrier

    far, cut = chips // 2, rows // 2
    own = pack(tokens, routes, gates, experts)
    got, twin = {0: own}, {}
    middle = [s * d for d in range(2, far - 1) for s in (1, -1)]
    late = [far, far - 1, 1 - far]
    for d in range(1, far):
        a, b = left(got[d - 1]), right(got[1 - d])
        new = {e: sibling(got[e]) for e in {d - 1, 1 - d}}
        if d == 1:
            w_gate, new, a, b = together((load(w_gate, own), new, a, b))
        elif d == 2:
            near = [got[0], got[1], got[-1], twin[0]]
            (h_near, w_up), new, a, b = together((hidden(near, w_gate, w_up, True), new, a, b))
        elif d == 3:
            (*near_out, w_down), new, a, b = together((output(near, 3, me, experts, h_near, w_down, True), new, a, b))
        else:
            new, a, b = together((new, a, b))
        got[d], got[-d] = a, b
        twin.update(new)
    ends = right(got[1 - far][:cut]), left(got[far - 1][cut:])
    new = {e: sibling(got[e]) for e in (far - 1, 1 - far)}
    rest = [got[d] for d in middle] + [twin[1], twin[-1]] + [twin[d] for d in middle]
    (h_rest,), ends, new, near_sent = together((hidden(rest, w_gate, w_up, False), ends, new, sibling(near_out[1])))
    twin.update(new)
    got[far] = jnp.concatenate(ends, axis=0)
    rest_out, twin[far] = together((output(rest, len(middle), me, experts, h_rest, w_down, False), sibling(got[far])))
    late_out = expert([got[d] for d in late] + [twin[d] for d in late], len(late), me, experts, w_gate, w_up, w_down)

    block = lambda a, j: a[j * rows : (j + 1) * rows]
    mine, theirs = {}, {0: near_sent}
    for j, d in enumerate((0, 1, -1)):
        mine[d] = block(near_out[0], j)
    rest_sent, late_sent = sibling(rest_out[1]), sibling(late_out[1])
    for j, d in enumerate(middle):
        mine[d] = block(rest_out[0], j)
    for j, d in enumerate([1, -1] + middle):
        theirs[d] = block(rest_sent, j)
    for j, d in enumerate(late):
        mine[d], theirs[d] = block(late_out[0], j), block(late_sent, j)

    split = width // 256 * 128
    spans = [slice(0, split), slice(split, width)] if split else [slice(0, width)]
    both = lambda d, s: mine[d][:, s] + theirs[d][:, s].astype(F32)
    ends = [both(far, s).astype(BF16) for s in spans]
    flow = [(right(end[:cut]), left(end[cut:])) for end in ends]
    added = None
    for d in range(far - 1, 0, -1):
        for i, s in enumerate(spans):
            a, b = flow[i]
            if added is not None:
                a, b, _ = together((a, b, added))
            up, down = both(d, s), both(-d, s)
            if d == far - 1:
                up = jnp.concatenate([up[:cut] + a.astype(F32), up[cut:]], axis=0)
                down = jnp.concatenate([down[:cut], down[cut:] + b.astype(F32)], axis=0)
            else:
                up, down = up + a.astype(F32), down + b.astype(F32)
            added = up.astype(BF16), down.astype(BF16)
            flow[i] = right(added[0]), left(added[1])
    out = [both(0, s) + flow[i][0].astype(F32) + flow[i][1].astype(F32) for i, s in enumerate(spans)]
    return jnp.concatenate([o.astype(BF16) for o in out], axis=1)


def solution(mesh):
    cores, order = chip_layout(mesh)
    in_specs = (
        P(("groups", "node"), None),
        P(("groups", "node"), None),
        P(("groups", "node"), None),
        P("node", None, None),
        P("node", None, None),
        P("node", None, None),
    )
    out_specs = P(("groups", "node"), None)
    body = functools.partial(local, cores, order)
    return jax.shard_map(body, mesh=mesh, in_specs=in_specs, out_specs=out_specs, check_vma=False)
```

time: 90 us -> 86.8 us (0.964)
  waiting for transfers between devices: 39.8 us -> 20.9 us
  starting transfers between devices: 19.6 us -> 28.1 us
  Pallas kernels: 19.5 us -> 27 us
    ppermute x8 -> x12, waiting for transfers between devices: 31.7 us -> 6.23 us  [local(): right = lambda a: lax.ppermute(a, 'node', forth)]
    ppermute x8 -> x12, waiting for transfers between devices: 4.55 us -> 13 us  [local(): left = lambda a: lax.ppermute(a, 'node', back)]
    ppermute x8 -> x12, starting transfers between devices: 13.5 us -> 21.1 us  [local(): right = lambda a: lax.ppermute(a, 'node', forth)]
    pallas_call x4 -> x7, Pallas kernels: 19.5 us -> 27 us  [the longest x2 8.74 us: hidden(): pl.pallas_call(functools.partial(hidden_kernel, count, tile, parts), out_...]
    ppermute x11, waiting for transfers between devices: 3.63 us -> 1.66 us  [local(): sibling = lambda a: lax.ppermute(a, 'node', swap)]
    unnamed x13 -> x15, local copies, waits for them, and re-layouts: 9.27 us -> 7.93 us
    ppermute x8 -> x12, starting transfers between devices: 3.85 us -> 4.77 us  [local(): left = lambda a: lax.ppermute(a, 'node', back)]
    slice x2, local copies, waits for them, and re-layouts: 0.02 us -> 0.92 us  [local(): ends = (right(got[1 - far][:cut]), left(got[far - 1][cut:]))]
  transfers between devices with their start and end apart: 27 -> 35, of which waited for: 14 -> 15; matrix products, arithmetic and copies ran while one was open for 1% -> 2% of each run, Pallas kernels for 13% -> 21%
where the time goes in v4:
time: 86.8 us; the launch traced here: 86.6 us
  starting transfers between devices  28.1 us (32%)
  Pallas kernels  27 us (31%)
  waiting for transfers between devices  20.9 us (24%)
  local copies, waits for them, and re-layouts  8.92 us (10%)
  other arithmetic  1.3 us (1%)
    ppermute x12, starting transfers between devices, local(): right = lambda a: lax.ppermute(a, 'node', forth)  21.1 us
    ppermute x12, waiting for transfers between devices, local(): left = lambda a: lax.ppermute(a, 'node', back)  13 us
    pallas_call x2, Pallas kernels, hidden(): pl.pallas_call(functools.partial(hidden_kernel, count, tile, parts), out_...  8.74 us
    unnamed x15, local copies, waits for them, and re-layouts  7.93 us
    pallas_call x1, Pallas kernels, expert(): pl.pallas_call(functools.partial(expert_kernel, count, experts, *tiles(wi...  7.55 us
    pallas_call x2, Pallas kernels, output(): pl.pallas_call(functools.partial(output_kernel, count, experts, tile, par...  6.57 us
    ppermute x12, waiting for transfers between devices, local(): right = lambda a: lax.ppermute(a, 'node', forth)  6.23 us
    ppermute x12, starting transfers between devices, local(): left = lambda a: lax.ppermute(a, 'node', back)  4.77 us
  transfers between devices with their start and end apart: 35, of which 15 were waited for; matrix products, arithmetic and copies ran while one was open for 2% of the time, Pallas kernels for 21%

profile of v4, /device:TPU:0, one launch (start us, length us, event | category | flops | bytes accessed | tf_op | source)
XLA Modules:
  0.0 86.6 jit_solution(11455376092536858675)
XLA Ops:
  0.0 1.0 %shard_map.64.after.refs_0_ = bf16[32,3712]{1,0:T(8,128)(2,1)S(1)} custom-call(bf16[32,3584]{1,0:T(8,128)(2,1)} %tok_hbm.1, s32[8,32]{1,0:T(8,128)} %bitcast.3, f32[8,32]{1,0:T(8,128)} %bitcast.4), custom_call_target="tpu_custom_call" | custom-call | tf_op jit(solution)/shard_map/pallas_call | solution.py:61
  1.0 3.1 %collective-permute-start.2 = (bf16[32,3712]{1,0:T(8,128)(2,1)S(1)}, bf16[32,3712]{1,0:T(8,128)(2,1)S(1)}, u32[]{:S(2)}, u32[]{:S(2)}) collective-permute-start(bf16[32,3712]{1,0:T(8,128)(2,1)S(1)} %shard_map.64.after.refs_0_), channel_id=1, source_target_pairs={{0,4},{1,5},{4,8},{5,9},{8,12},{9,13},{12,14},{13,15},{14,10},{15,... | collective-permute-start | bytes 712712 | tf_op jit(solution)/shard_map/ppermute | solution.py:265
  4.1 3.2 %shard_map.65.refs_4_.refs_6_ = bf16[1,3584,1024]{2,1,0:T(8,128)(2,1)S(1)} custom-call(bf16[1,3584,1024]{2,1,0:T(8,128)(2,1)} %source.1, bf16[32,3712]{1,0:T(8,128)(2,1)S(1)} %shard_map.64.after.refs_0_), custom_call_target="tpu_custom_call" | custom-call | bytes 7340032 | tf_op jit(solution)/shard_map/pallas_call | solution.py:109
  7.3 2.5 %collective-permute-done.2.refs_2_ = bf16[32,3712]{1,0:T(8,128)(2,1)S(1)} collective-permute-done((bf16[32,3712]{1,0:T(8,128)(2,1)S(1)}, bf16[32,3712]{1,0:T(8,128)(2,1)S(1)}, u32[]{:S(2)}, u32[]{:S(2)}) %collective-permute-start.2) | collective-permute-done | bytes 237600 | tf_op jit(solution)/shard_map/ppermute | solution.py:265
  9.8 1.5 %collective-permute-done.1.refs_1_ = bf16[32,3712]{1,0:T(8,128)(2,1)S(1)} collective-permute-done((bf16[32,3712]{1,0:T(8,128)(2,1)S(1)}, bf16[32,3712]{1,0:T(8,128)(2,1)S(1)}, u32[]{:S(2)}, u32[]{:S(2)}) %collective-permute-start.1) | collective-permute-done | bytes 237600 | tf_op jit(solution)/shard_map/ppermute | solution.py:266
  11.6 1.7 %collective-permute-start.6 = (bf16[32,3712]{1,0:T(8,128)(2,1)S(1)}, bf16[32,3712]{1,0:T(8,128)(2,1)S(1)}, u32[]{:S(2)}, u32[]{:S(2)}) collective-permute-start(bf16[32,3712]{1,0:T(8,128)(2,1)S(1)} %collective-permute-done.2.refs_2_), channel_id=1, source_target_pairs={{0,4},{1,5},{4,8},{5,9},{8,12},{9,13},{12,14},{13,15},{14,10},{15,... | collective-permute-start | bytes 712712 | tf_op jit(solution)/shard_map/ppermute | solution.py:265
  13.6 4.9 %shard_map.66 = (bf16[128,1024]{1,0:T(8,128)(2,1)S(1)}, bf16[1,3584,1024]{2,1,0:T(8,128)(2,1)S(1)}) custom-call(bf16[32,3712]{1,0:T(8,128)(2,1)S(1)} %shard_map.64.after.refs_0_, bf16[32,3712]{1,0:T(8,128)(2,1)S(1)} %collective-permute-done.1.refs_1_, bf16[32,3712]{1,0:T(8,128)(2,1)S(1)} %collective-permute-done.2.refs_2_, ...), custom_call_target="tpu_custom_call" | custom-call | flops 3758096384 | tf_op jit(solution)/shard_map/pallas_call | solution.py:180
  18.6 3.0 %copy-done.2 = bf16[1,3584,1024]{2,1,0:T(8,128)(2,1)} copy-done((bf16[1,3584,1024]{2,1,0:T(8,128)(2,1)}, bf16[1,3584,1024]{2,1,0:T(8,128)(2,1)S(1)}, u32[]{:S(2)}) %copy-start.2) | copy-done | bytes 7340056
  21.6 0.7 copy-done.5
  22.3 1.6 %collective-permute-start.10 = (bf16[32,3712]{1,0:T(8,128)(2,1)S(1)}, bf16[32,3712]{1,0:T(8,128)(2,1)S(1)}, u32[]{:S(2)}, u32[]{:S(2)}) collective-permute-start(bf16[32,3712]{1,0:T(8,128)(2,1)S(1)} %collective-permute-done.6.refs_1_), channel_id=1, source_target_pairs={{0,4},{1,5},{4,8},{5,9},{8,12},{9,13},{12,14},{13,15},{14,10},{15,... | collective-permute-start | bytes 712712 | tf_op jit(solution)/shard_map/ppermute | solution.py:265
  23.9 0.4 collective-permute-start.9
  24.6 1.1 %copy-done.6 = bf16[128,1024]{1,0:T(8,128)(2,1)S(1)} copy-done((bf16[128,1024]{1,0:T(8,128)(2,1)S(1)}, bf16[128,1024]{1,0:T(8,128)(2,1)}, u32[]{:S(2)}) %copy-start.6) | copy-done | bytes 262168
  25.7 3.8 %shard_map.67 = (f32[96,3584]{1,0:T(8,128)S(1)}, bf16[32,3584]{1,0:T(8,128)(2,1)S(1)}, bf16[1,1024,3584]{2,1,0:T(8,128)(2,1)S(1)}) custom-call(s32[1]{0:T(128)} %bitcast.me_ref, bf16[32,3712]{1,0:T(8,128)(2,1)S(1)} %shard_map.64.after.refs_0_, bf16[32,3712]{1,0:T(8,128)(2,1)S(1)} %collective-permute-done.1.refs_1_, ...), custom_call_target="tpu_custom_call" | custom-call | flops 1879048192 | tf_op jit(solution)/shard_map/pallas_call | solution.py:215
  29.5 0.8 collective-permute-done.10.refs_2_
  30.3 1.9 %collective-permute-done.9.refs_1_ = bf16[32,3712]{1,0:T(8,128)(2,1)} collective-permute-done((bf16[32,3712]{1,0:T(8,128)(2,1)S(1)}, bf16[32,3712]{1,0:T(8,128)(2,1)}, u32[]{:S(2)}, u32[]{:S(2)}) %collective-permute-start.9) | collective-permute-done | bytes 237600 | tf_op jit(solution)/shard_map/ppermute | solution.py:266
  32.3 0.9 %slice.189 = bf16[16,3712]{1,0:T(8,128)(2,1)S(1)} slice(bf16[32,3712]{1,0:T(8,128)(2,1)} %collective-permute-done.9.refs_1_), slice={[16:32], [0:3712]} | slice | bytes 237568 | tf_op jit(solution)/shard_map/slice | solution.py:289
  33.3 0.6 collective-permute-start.14
  33.8 0.4 collective-permute-start.12
  34.2 1.6 %collective-permute-start.11 = (bf16[16,3712]{1,0:T(8,128)(2,1)S(1)}, bf16[16,3712]{1,0:T(8,128)(2,1)S(1)}, u32[]{:S(2)}, u32[]{:S(2)}) collective-permute-start(bf16[16,3712]{1,0:T(8,128)(2,1)S(1)} %slice.188), channel_id=1, source_target_pairs={{0,4},{1,5},{4,8},{5,9},{8,12},{9,13},{12,14},{13,15},{14,10},{15,... | collective-permute-start | bytes 356360 | tf_op jit(solution)/shard_map/ppermute | solution.py:265
  35.8 3.1 %copy-done.3 = bf16[1,3584,1024]{2,1,0:T(8,128)(2,1)S(1)} copy-done((bf16[1,3584,1024]{2,1,0:T(8,128)(2,1)S(1)}, bf16[1,3584,1024]{2,1,0:T(8,128)(2,1)}, u32[]{:S(2)}) %copy-start.3) | copy-done | bytes 7340056
  38.9 3.8 %shard_map.68.refs_6_ = bf16[192,1024]{1,0:T(8,128)(2,1)S(1)} custom-call(bf16[32,3712]{1,0:T(8,128)(2,1)S(1)} %collective-permute-done.5.refs_0_, bf16[32,3712]{1,0:T(8,128)(2,1)S(1)} %collective-permute-done.6.refs_1_, bf16[32,3712]{1,0:T(8,128)(2,1)S(1)} %collective-permute-done.4.refs_2_, bf16[32,3712]{1,0:T(8,128)(2,1)S(1)} %collective-permute-done.3.refs_3_, ...), custom_call_target="tpu_custom_call" | custom-call | flops 3758096384 | tf_op jit(solution)/shard_map/pallas_call | solution.py:180
  42.8 0.6 collective-permute-start.16
  43.4 2.8 %shard_map.69 = (f32[64,3584]{1,0:T(8,128)S(1)}, bf16[128,3584]{1,0:T(8,128)(2,1)S(1)}) custom-call(s32[1]{0:T(128)} %bitcast.me_ref, bf16[32,3712]{1,0:T(8,128)(2,1)S(1)} %collective-permute-done.5.refs_0_, bf16[32,3712]{1,0:T(8,128)(2,1)S(1)} %collective-permute-done.6.refs_1_, bf16[32,3712]{1,0:T(8,128)(2,1)S(1)} %collective-permute-done.4.refs_2_, ...), custom_call_target="tpu_custom_call" | custom-call | flops 1879048192 | tf_op jit(solution)/shard_map/pallas_call | solution.py:215
  46.3 7.6 %shard_map.70 = (f32[96,3584]{1,0:T(8,128)S(1)}, bf16[96,3584]{1,0:T(8,128)(2,1)S(1)}) custom-call(s32[1]{0:T(128)} %bitcast.me_ref, bf16[32,3712]{1,0:T(8,128)(2,1)S(1)} %constant_dynamic-update-slice_fusion.refs_0_, bf16[32,3712]{1,0:T(8,128)(2,1)} %collective-permute-done.9.refs_1_, bf16[32,3712]{1,0:T(8,128)(2,1)S(1)} %collective-permute-done.10.refs_2_, ...), custom_call_target="tpu_custom_call" | custom-call | flops 5637144576 | tf_op jit(solution)/shard_map/pallas_call | solution.py:244
  54.4 1.6 %collective-permute-done.18 = bf16[96,3584]{1,0:T(8,128)(2,1)S(1)} collective-permute-done((bf16[96,3584]{1,0:T(8,128)(2,1)S(1)}, bf16[96,3584]{1,0:T(8,128)(2,1)S(1)}, u32[]{:S(2)}, u32[]{:S(2)}) %collective-permute-start.18) | collective-permute-done | bytes 688160 | tf_op jit(solution)/shard_map/ppermute | solution.py:267
  56.2 1.6 %collective-permute-start.19 = (bf16[16,1792]{1,0:T(8,128)(2,1)S(1)}, bf16[16,1792]{1,0:T(8,128)(2,1)S(1)}, u32[]{:S(2)}, u32[]{:S(2)}) collective-permute-start(bf16[16,1792]{1,0:T(8,128)(2,1)S(1)} %get-tuple-element.112), channel_id=1, source_target_pairs={{0,4},{1,5},{4,8},{5,9},{8,12},{9,13},{12,14},{13,15},{14,10},{15,... | collective-permute-start | bytes 172040 | tf_op jit(solution)/shard_map/ppermute | solution.py:265
  57.9 0.5 collective-permute-start.24
  58.4 1.6 %collective-permute-start.23 = (bf16[16,1792]{1,0:T(8,128)(2,1)S(1)}, bf16[16,1792]{1,0:T(8,128)(2,1)S(1)}, u32[]{:S(2)}, u32[]{:S(2)}) collective-permute-start(bf16[16,1792]{1,0:T(8,128)(2,1)S(1)} %get-tuple-element.114), channel_id=1, source_target_pairs={{0,4},{1,5},{4,8},{5,9},{8,12},{9,13},{12,14},{13,15},{14,10},{15,... | collective-permute-start | bytes 172040 | tf_op jit(solution)/shard_map/ppermute | solution.py:265
  59.9 0.4 collective-permute-start.21
  60.4 1.6 %collective-permute-start.20 = (bf16[32,1792]{1,0:T(8,128)(2,1)S(1)}, bf16[32,1792]{1,0:T(8,128)(2,1)S(1)}, u32[]{:S(2)}, u32[]{:S(2)}) collective-permute-start(bf16[32,1792]{1,0:T(8,128)(2,1)S(1)} %pad_maximum_fusion.1), channel_id=1, source_target_pairs={{0,4},{1,5},{4,8},{5,9},{8,12},{9,13},{12,14},{13,15},{14,10},{15,... | collective-permute-start | bytes 344072 | tf_op jit(solution)/shard_map/ppermute | solution.py:265
  62.1 2.1 %collective-permute-done.21 = bf16[16,1792]{1,0:T(8,128)(2,1)S(1)} collective-permute-done((bf16[16,1792]{1,0:T(8,128)(2,1)S(1)}, bf16[16,1792]{1,0:T(8,128)(2,1)S(1)}, u32[]{:S(2)}, u32[]{:S(2)}) %collective-permute-start.21) | collective-permute-done | bytes 57376 | tf_op jit(solution)/shard_map/ppermute | solution.py:266
  64.2 0.5 collective-permute-start.22
  64.7 0.5 collective-permute-start.28
  65.2 1.6 %collective-permute-start.27 = (bf16[32,1792]{1,0:T(8,128)(2,1)S(1)}, bf16[32,1792]{1,0:T(8,128)(2,1)S(1)}, u32[]{:S(2)}, u32[]{:S(2)}) collective-permute-start(bf16[32,1792]{1,0:T(8,128)(2,1)S(1)} %pad_maximum_fusion.3), channel_id=1, source_target_pairs={{0,4},{1,5},{4,8},{5,9},{8,12},{9,13},{12,14},{13,15},{14,10},{15,... | collective-permute-start | bytes 344072 | tf_op jit(solution)/shard_map/ppermute | solution.py:265
  66.9 2.3 %collective-permute-done.22 = bf16[32,1792]{1,0:T(8,128)(2,1)S(1)} collective-permute-done((bf16[32,1792]{1,0:T(8,128)(2,1)S(1)}, bf16[32,1792]{1,0:T(8,128)(2,1)S(1)}, u32[]{:S(2)}, u32[]{:S(2)}) %collective-permute-start.22) | collective-permute-done | bytes 114720 | tf_op jit(solution)/shard_map/ppermute | solution.py:266
  69.3 0.5 collective-permute-start.26
  69.8 1.6 %collective-permute-start.25 = (bf16[32,1792]{1,0:T(8,128)(2,1)S(1)}, bf16[32,1792]{1,0:T(8,128)(2,1)S(1)}, u32[]{:S(2)}, u32[]{:S(2)}) collective-permute-start(bf16[32,1792]{1,0:T(8,128)(2,1)S(1)} %get-tuple-element.108), channel_id=1, source_target_pairs={{0,4},{1,5},{4,8},{5,9},{8,12},{9,13},{12,14},{13,15},{14,10},{15,... | collective-permute-start | bytes 344072 | tf_op jit(solution)/shard_map/ppermute | solution.py:265
  71.6 0.5 collective-permute-start.32
  72.1 1.6 %collective-permute-start.31 = (bf16[32,1792]{1,0:T(8,128)(2,1)S(1)}, bf16[32,1792]{1,0:T(8,128)(2,1)S(1)}, u32[]{:S(2)}, u32[]{:S(2)}) collective-permute-start(bf16[32,1792]{1,0:T(8,128)(2,1)S(1)} %get-tuple-element.106), channel_id=1, source_target_pairs={{0,4},{1,5},{4,8},{5,9},{8,12},{9,13},{12,14},{13,15},{14,10},{15,... | collective-permute-start | bytes 344072 | tf_op jit(solution)/shard_map/ppermute | solution.py:265
  73.7 0.5 collective-permute-done.26
  74.6 1.8 %collective-permute-done.32 = bf16[32,1792]{1,0:T(8,128)(2,1)S(1)} collective-permute-done((bf16[32,1792]{1,0:T(8,128)(2,1)S(1)}, bf16[32,1792]{1,0:T(8,128)(2,1)S(1)}, u32[]{:S(2)}, u32[]{:S(2)}) %collective-permute-start.32) | collective-permute-done | bytes 114720 | tf_op jit(solution)/shard_map/ppermute | solution.py:266
  76.4 1.7 %collective-permute-done.31 = bf16[32,1792]{1,0:T(8,128)(2,1)S(1)} collective-permute-done((bf16[32,1792]{1,0:T(8,128)(2,1)S(1)}, bf16[32,1792]{1,0:T(8,128)(2,1)S(1)}, u32[]{:S(2)}, u32[]{:S(2)}) %collective-permute-start.31) | collective-permute-done | bytes 114720 | tf_op jit(solution)/shard_map/ppermute | solution.py:265
  78.2 1.6 %collective-permute-start.33 = (bf16[32,1792]{1,0:T(8,128)(2,1)S(1)}, bf16[32,1792]{1,0:T(8,128)(2,1)S(1)}, u32[]{:S(2)}, u32[]{:S(2)}) collective-permute-start(bf16[32,1792]{1,0:T(8,128)(2,1)S(1)} %get-tuple-element.95), channel_id=1, source_target_pairs={{0,4},{1,5},{4,8},{5,9},{8,12},{9,13},{12,14},{13,15},{14,10},{15,... | collective-permute-start | bytes 344072 | tf_op jit(solution)/shard_map/ppermute | solution.py:265
  80.5 1.8 %collective-permute-start.29 = (bf16[32,1792]{1,0:T(8,128)(2,1)S(1)}, bf16[32,1792]{1,0:T(8,128)(2,1)S(1)}, u32[]{:S(2)}, u32[]{:S(2)}) collective-permute-start(bf16[32,1792]{1,0:T(8,128)(2,1)S(1)} %get-tuple-element.98), channel_id=1, source_target_pairs={{0,4},{1,5},{4,8},{5,9},{8,12},{9,13},{12,14},{13,15},{14,10},{15,... | collective-permute-start | bytes 344072 | tf_op jit(solution)/shard_map/ppermute | solution.py:265
  82.3 0.7 collective-permute-done.33
  83.0 1.6 %collective-permute-done.34 = bf16[32,1792]{1,0:T(8,128)(2,1)S(1)} collective-permute-done((bf16[32,1792]{1,0:T(8,128)(2,1)S(1)}, bf16[32,1792]{1,0:T(8,128)(2,1)S(1)}, u32[]{:S(2)}, u32[]{:S(2)}) %collective-permute-start.34) | collective-permute-done | bytes 114720 | tf_op jit(solution)/shard_map/ppermute | solution.py:266
  84.6 1.2 %collective-permute-done.30 = bf16[32,1792]{1,0:T(8,128)(2,1)S(1)} collective-permute-done((bf16[32,1792]{1,0:T(8,128)(2,1)S(1)}, bf16[32,1792]{1,0:T(8,128)(2,1)S(1)}, u32[]{:S(2)}, u32[]{:S(2)}) %collective-permute-start.30) | collective-permute-done | bytes 114720 | tf_op jit(solution)/shard_map/ppermute | solution.py:266
  85.9 0.7 pad_maximum_fusion
  (68 shorter events, 3.4 us)
Async XLA Ops:
  1.0 8.8 %collective-permute-start.2 = (bf16[32,3712]{1,0:T(8,128)(2,1)S(1)}, bf16[32,3712]{1,0:T(8,128)(2,1)S(1)}, u32[]{:S(2)}, u32[]{:S(2)}) collective-permute-start(bf16[32,3712]{1,0:T(8,128)(2,1)S(1)} %shard_map.64.after.refs_0_), channel_id=1, source_target_pairs={{0,4},{1,5},{4,8},{5,9},{8,12},{9,13},{12,14},{13,15},{14,10},{15,... | collective-permute-start | bytes 712712 | tf_op jit(solution)/shard_map/ppermute | solution.py:265
  4.1 7.2 %collective-permute-start.1 = (bf16[32,3712]{1,0:T(8,128)(2,1)S(1)}, bf16[32,3712]{1,0:T(8,128)(2,1)S(1)}, u32[]{:S(2)}, u32[]{:S(2)}) collective-permute-start(bf16[32,3712]{1,0:T(8,128)(2,1)S(1)} %shard_map.64.after.refs_0_), channel_id=1, source_target_pairs={{4,0},{5,1},{8,4},{9,5},{12,8},{13,9},{14,12},{15,13},{10,14},{11,... | collective-permute-start | bytes 712712 | tf_op jit(solution)/shard_map/ppermute | solution.py:266
  4.1 7.2 %collective-permute-start = (bf16[32,3712]{1,0:T(8,128)(2,1)S(1)}, bf16[32,3712]{1,0:T(8,128)(2,1)S(1)}, u32[]{:S(2)}, u32[]{:S(2)}) collective-permute-start(bf16[32,3712]{1,0:T(8,128)(2,1)S(1)} %shard_map.64.after.refs_0_), channel_id=1, source_target_pairs={{0,1},{1,0},{2,3},{3,2},{4,5},{5,4},{6,7},{7,6},{8,9},{9,8},{10,11... | collective-permute-start | bytes 712712 | tf_op jit(solution)/shard_map/ppermute | solution.py:267
  7.3 11.3 %copy-start = (bf16[1,3584,1024]{2,1,0:T(8,128)(2,1)}, bf16[1,3584,1024]{2,1,0:T(8,128)(2,1)S(1)}, u32[]{:S(2)}) copy-start(bf16[1,3584,1024]{2,1,0:T(8,128)(2,1)S(1)} %shard_map.65.refs_4_.refs_6_) | copy-start | bytes 22020100
  11.3 11.0 %collective-permute-start.5 = (bf16[32,3712]{1,0:T(8,128)(2,1)S(1)}, bf16[32,3712]{1,0:T(8,128)(2,1)S(1)}, u32[]{:S(2)}, u32[]{:S(2)}) collective-permute-start(bf16[32,3712]{1,0:T(8,128)(2,1)S(1)} %collective-permute-done.1.refs_1_), channel_id=1, source_target_pairs={{4,0},{5,1},{8,4},{9,5},{12,8},{13,9},{14,12},{15,13},{10,14},{11,... | collective-permute-start | bytes 712712 | tf_op jit(solution)/shard_map/ppermute | solution.py:266
  11.6 10.7 %collective-permute-start.4 = (bf16[32,3712]{1,0:T(8,128)(2,1)S(1)}, bf16[32,3712]{1,0:T(8,128)(2,1)S(1)}, u32[]{:S(2)}, u32[]{:S(2)}) collective-permute-start(bf16[32,3712]{1,0:T(8,128)(2,1)S(1)} %collective-permute-done.1.refs_1_), channel_id=1, source_target_pairs={{0,1},{1,0},{2,3},{3,2},{4,5},{5,4},{6,7},{7,6},{8,9},{9,8},{10,11... | collective-permute-start | bytes 712712 | tf_op jit(solution)/shard_map/ppermute | solution.py:267
  11.6 10.7 %collective-permute-start.6 = (bf16[32,3712]{1,0:T(8,128)(2,1)S(1)}, bf16[32,3712]{1,0:T(8,128)(2,1)S(1)}, u32[]{:S(2)}, u32[]{:S(2)}) collective-permute-start(bf16[32,3712]{1,0:T(8,128)(2,1)S(1)} %collective-permute-done.2.refs_2_), channel_id=1, source_target_pairs={{0,4},{1,5},{4,8},{5,9},{8,12},{9,13},{12,14},{13,15},{14,10},{15,... | collective-permute-start | bytes 712712 | tf_op jit(solution)/shard_map/ppermute | solution.py:265
  13.4 8.9 %collective-permute-start.3 = (bf16[32,3712]{1,0:T(8,128)(2,1)S(1)}, bf16[32,3712]{1,0:T(8,128)(2,1)S(1)}, u32[]{:S(2)}, u32[]{:S(2)}) collective-permute-start(bf16[32,3712]{1,0:T(8,128)(2,1)S(1)} %collective-permute-done.2.refs_2_), channel_id=1, source_target_pairs={{0,1},{1,0},{2,3},{3,2},{4,5},{5,4},{6,7},{7,6},{8,9},{9,8},{10,11... | collective-permute-start | bytes 712712 | tf_op jit(solution)/shard_map/ppermute | solution.py:267
  18.5 3.0 %copy-start.2 = (bf16[1,3584,1024]{2,1,0:T(8,128)(2,1)}, bf16[1,3584,1024]{2,1,0:T(8,128)(2,1)S(1)}, u32[]{:S(2)}) copy-start(bf16[1,3584,1024]{2,1,0:T(8,128)(2,1)S(1)} %get-tuple-element.67.refs_7_) | copy-start | bytes 22020100
  21.6 0.7 copy-start.5
  22.3 8.0 %collective-permute-start.10 = (bf16[32,3712]{1,0:T(8,128)(2,1)S(1)}, bf16[32,3712]{1,0:T(8,128)(2,1)S(1)}, u32[]{:S(2)}, u32[]{:S(2)}) collective-permute-start(bf16[32,3712]{1,0:T(8,128)(2,1)S(1)} %collective-permute-done.6.refs_1_), channel_id=1, source_target_pairs={{0,4},{1,5},{4,8},{5,9},{8,12},{9,13},{12,14},{13,15},{14,10},{15,... | collective-permute-start | bytes 712712 | tf_op jit(solution)/shard_map/ppermute | solution.py:265
  23.9 6.4 %collective-permute-start.7 = (bf16[32,3712]{1,0:T(8,128)(2,1)S(1)}, bf16[32,3712]{1,0:T(8,128)(2,1)S(1)}, u32[]{:S(2)}, u32[]{:S(2)}) collective-permute-start(bf16[32,3712]{1,0:T(8,128)(2,1)S(1)} %collective-permute-done.6.refs_1_), channel_id=1, source_target_pairs={{0,1},{1,0},{2,3},{3,2},{4,5},{5,4},{6,7},{7,6},{8,9},{9,8},{10,11... | collective-permute-start | bytes 712712 | tf_op jit(solution)/shard_map/ppermute | solution.py:267
  23.9 8.3 %collective-permute-start.9 = (bf16[32,3712]{1,0:T(8,128)(2,1)S(1)}, bf16[32,3712]{1,0:T(8,128)(2,1)}, u32[]{:S(2)}, u32[]{:S(2)}) collective-permute-start(bf16[32,3712]{1,0:T(8,128)(2,1)S(1)} %collective-permute-done.5.refs_0_), channel_id=1, source_target_pairs={{4,0},{5,1},{8,4},{9,5},{12,8},{13,9},{14,12},{15,13},{10,14},{11,... | collective-permute-start | bytes 712712 | tf_op jit(solution)/shard_map/ppermute | solution.py:266
  24.4 7.9 %collective-permute-start.8 = (bf16[32,3712]{1,0:T(8,128)(2,1)S(1)}, bf16[32,3712]{1,0:T(8,128)(2,1)S(1)}, u32[]{:S(2)}, u32[]{:S(2)}) collective-permute-start(bf16[32,3712]{1,0:T(8,128)(2,1)S(1)} %collective-permute-done.5.refs_0_), channel_id=1, source_target_pairs={{0,1},{1,0},{2,3},{3,2},{4,5},{5,4},{6,7},{7,6},{8,9},{9,8},{10,11... | collective-permute-start | bytes 712712 | tf_op jit(solution)/shard_map/ppermute | solution.py:267
  24.6 11.2 %copy-start.1 = (bf16[1,3584,1024]{2,1,0:T(8,128)(2,1)S(1)}, bf16[1,3584,1024]{2,1,0:T(8,128)(2,1)}, u32[]{:S(2)}) copy-start(bf16[1,3584,1024]{2,1,0:T(8,128)(2,1)} %copy-done) | copy-start | bytes 22020100
  24.6 1.1 %copy-start.6 = (bf16[128,1024]{1,0:T(8,128)(2,1)S(1)}, bf16[128,1024]{1,0:T(8,128)(2,1)}, u32[]{:S(2)}) copy-start(bf16[128,1024]{1,0:T(8,128)(2,1)} %copy-done.5) | copy-start | bytes 786436
  32.3 10.5 %collective-permute-start.13 = (bf16[32,3712]{1,0:T(8,128)(2,1)S(1)}, bf16[32,3712]{1,0:T(8,128)(2,1)S(1)}, u32[]{:S(2)}, u32[]{:S(2)}) collective-permute-start(bf16[32,3712]{1,0:T(8,128)(2,1)S(1)} %collective-permute-done.10.refs_2_), channel_id=1, source_target_pairs={{0,1},{1,0},{2,3},{3,2},{4,5},{5,4},{6,7},{7,6},{8,9},{9,8},{10,11... | collective-permute-start | bytes 712712 | tf_op jit(solution)/shard_map/ppermute | solution.py:267
  33.3 9.5 %collective-permute-start.14 = (bf16[32,3712]{1,0:T(8,128)(2,1)}, bf16[32,3712]{1,0:T(8,128)(2,1)S(1)}, u32[]{:S(2)}, u32[]{:S(2)}) collective-permute-start(bf16[32,3712]{1,0:T(8,128)(2,1)} %collective-permute-done.9.refs_1_), channel_id=1, source_target_pairs={{0,1},{1,0},{2,3},{3,2},{4,5},{5,4},{6,7},{7,6},{8,9},{9,8},{10,11... | collective-permute-start | bytes 712712 | tf_op jit(solution)/shard_map/ppermute | solution.py:267
  33.8 8.9 %collective-permute-start.12 = (bf16[16,3712]{1,0:T(8,128)(2,1)S(1)}, bf16[16,3712]{1,0:T(8,128)(2,1)S(1)}, u32[]{:S(2)}, u32[]{:S(2)}) collective-permute-start(bf16[16,3712]{1,0:T(8,128)(2,1)S(1)} %slice.189), channel_id=1, source_target_pairs={{4,0},{5,1},{8,4},{9,5},{12,8},{13,9},{14,12},{15,13},{10,14},{11,... | collective-permute-start | bytes 356360 | tf_op jit(solution)/shard_map/ppermute | solution.py:266
  34.2 8.5 %collective-permute-start.11 = (bf16[16,3712]{1,0:T(8,128)(2,1)S(1)}, bf16[16,3712]{1,0:T(8,128)(2,1)S(1)}, u32[]{:S(2)}, u32[]{:S(2)}) collective-permute-start(bf16[16,3712]{1,0:T(8,128)(2,1)S(1)} %slice.188), channel_id=1, source_target_pairs={{0,4},{1,5},{4,8},{5,9},{8,12},{9,13},{12,14},{13,15},{14,10},{15,... | collective-permute-start | bytes 356360 | tf_op jit(solution)/shard_map/ppermute | solution.py:265
  35.8 6.9 %collective-permute-start.15 = (bf16[32,3584]{1,0:T(8,128)(2,1)S(1)}, bf16[32,3584]{1,0:T(8,128)(2,1)S(1)}, u32[]{:S(2)}, u32[]{:S(2)}) collective-permute-start(bf16[32,3584]{1,0:T(8,128)(2,1)S(1)} %get-tuple-element.70), channel_id=1, source_target_pairs={{0,1},{1,0},{2,3},{3,2},{4,5},{5,4},{6,7},{7,6},{8,9},{9,8},{10,11... | collective-permute-start | bytes 688136 | tf_op jit(solution)/shard_map/ppermute | solution.py:267
  35.8 3.1 %copy-start.3 = (bf16[1,3584,1024]{2,1,0:T(8,128)(2,1)S(1)}, bf16[1,3584,1024]{2,1,0:T(8,128)(2,1)}, u32[]{:S(2)}) copy-start(bf16[1,3584,1024]{2,1,0:T(8,128)(2,1)} %copy-done.2) | copy-start | bytes 22020100
  42.7 3.5 %copy-start.4 = (bf16[1,3584,1024]{2,1,0:T(8,128)(2,1)S(1)}, bf16[1,3584,1024]{2,1,0:T(8,128)(2,1)}, u32[]{:S(2)}) copy-start(bf16[1,3584,1024]{2,1,0:T(8,128)(2,1)} %copy-done.2) | copy-start | bytes 22020100
  42.8 3.4 %collective-permute-start.16 = (bf16[32,3712]{1,0:T(8,128)(2,1)S(1)}, bf16[32,3712]{1,0:T(8,128)(2,1)S(1)}, u32[]{:S(2)}, u32[]{:S(2)}) collective-permute-start(bf16[32,3712]{1,0:T(8,128)(2,1)S(1)} %constant_dynamic-update-slice_fusion.refs_0_), channel_id=1, source_target_pairs={{0,1},{1,0},{2,3},{3,2},{4,5},{5,4},{6,7},{7,6},{8,9},{9,8},{10,11... | collective-permute-start | bytes 712712 | tf_op jit(solution)/shard_map/ppermute | solution.py:267
  53.8 2.2 %collective-permute-start.18 = (bf16[96,3584]{1,0:T(8,128)(2,1)S(1)}, bf16[96,3584]{1,0:T(8,128)(2,1)S(1)}, u32[]{:S(2)}, u32[]{:S(2)}) collective-permute-start(bf16[96,3584]{1,0:T(8,128)(2,1)S(1)} %get-tuple-element.84), channel_id=1, source_target_pairs={{0,1},{1,0},{2,3},{3,2},{4,5},{5,4},{6,7},{7,6},{8,9},{9,8},{10,11... | collective-permute-start | bytes 2064392 | tf_op jit(solution)/shard_map/ppermute | solution.py:267
  54.0 15.2 %collective-permute-start.17 = (bf16[128,3584]{1,0:T(8,128)(2,1)S(1)}, bf16[128,3584]{1,0:T(8,128)(2,1)S(1)}, u32[]{:S(2)}, u32[]{:S(2)}) collective-permute-start(bf16[128,3584]{1,0:T(8,128)(2,1)S(1)} %get-tuple-element.78), channel_id=1, source_target_pairs={{0,1},{1,0},{2,3},{3,2},{4,5},{5,4},{6,7},{7,6},{8,9},{9,8},{10,11... | collective-permute-start | bytes 2752520 | tf_op jit(solution)/shard_map/ppermute | solution.py:267
  56.2 4.2 %collective-permute-start.19 = (bf16[16,1792]{1,0:T(8,128)(2,1)S(1)}, bf16[16,1792]{1,0:T(8,128)(2,1)S(1)}, u32[]{:S(2)}, u32[]{:S(2)}) collective-permute-start(bf16[16,1792]{1,0:T(8,128)(2,1)S(1)} %get-tuple-element.112), channel_id=1, source_target_pairs={{0,4},{1,5},{4,8},{5,9},{8,12},{9,13},{12,14},{13,15},{14,10},{15,... | collective-permute-start | bytes 172040 | tf_op jit(solution)/shard_map/ppermute | solution.py:265
  57.9 6.8 %collective-permute-start.24 = (bf16[16,1792]{1,0:T(8,128)(2,1)S(1)}, bf16[16,1792]{1,0:T(8,128)(2,1)S(1)}, u32[]{:S(2)}, u32[]{:S(2)}) collective-permute-start(bf16[16,1792]{1,0:T(8,128)(2,1)S(1)} %get-tuple-element.113), channel_id=1, source_target_pairs={{4,0},{5,1},{8,4},{9,5},{12,8},{13,9},{14,12},{15,13},{10,14},{11,... | collective-permute-start | bytes 172040 | tf_op jit(solution)/shard_map/ppermute | solution.py:266
  58.4 6.3 %collective-permute-start.23 = (bf16[16,1792]{1,0:T(8,128)(2,1)S(1)}, bf16[16,1792]{1,0:T(8,128)(2,1)S(1)}, u32[]{:S(2)}, u32[]{:S(2)}) collective-permute-start(bf16[16,1792]{1,0:T(8,128)(2,1)S(1)} %get-tuple-element.114), channel_id=1, source_target_pairs={{0,4},{1,5},{4,8},{5,9},{8,12},{9,13},{12,14},{13,15},{14,10},{15,... | collective-permute-start | bytes 172040 | tf_op jit(solution)/shard_map/ppermute | solution.py:265
  59.9 4.2 %collective-permute-start.21 = (bf16[16,1792]{1,0:T(8,128)(2,1)S(1)}, bf16[16,1792]{1,0:T(8,128)(2,1)S(1)}, u32[]{:S(2)}, u32[]{:S(2)}) collective-permute-start(bf16[16,1792]{1,0:T(8,128)(2,1)S(1)} %get-tuple-element.111), channel_id=1, source_target_pairs={{4,0},{5,1},{8,4},{9,5},{12,8},{13,9},{14,12},{15,13},{10,14},{11,... | collective-permute-start | bytes 172040 | tf_op jit(solution)/shard_map/ppermute | solution.py:266
  60.4 6.4 %collective-permute-start.20 = (bf16[32,1792]{1,0:T(8,128)(2,1)S(1)}, bf16[32,1792]{1,0:T(8,128)(2,1)S(1)}, u32[]{:S(2)}, u32[]{:S(2)}) collective-permute-start(bf16[32,1792]{1,0:T(8,128)(2,1)S(1)} %pad_maximum_fusion.1), channel_id=1, source_target_pairs={{0,4},{1,5},{4,8},{5,9},{8,12},{9,13},{12,14},{13,15},{14,10},{15,... | collective-permute-start | bytes 344072 | tf_op jit(solution)/shard_map/ppermute | solution.py:265
  64.2 5.0 %collective-permute-start.22 = (bf16[32,1792]{1,0:T(8,128)(2,1)S(1)}, bf16[32,1792]{1,0:T(8,128)(2,1)S(1)}, u32[]{:S(2)}, u32[]{:S(2)}) collective-permute-start(bf16[32,1792]{1,0:T(8,128)(2,1)S(1)} %pad_maximum_fusion.2), channel_id=1, source_target_pairs={{4,0},{5,1},{8,4},{9,5},{12,8},{13,9},{14,12},{15,13},{10,14},{11,... | collective-permute-start | bytes 344072 | tf_op jit(solution)/shard_map/ppermute | solution.py:266
  64.7 6.8 %collective-permute-start.28 = (bf16[32,1792]{1,0:T(8,128)(2,1)S(1)}, bf16[32,1792]{1,0:T(8,128)(2,1)S(1)}, u32[]{:S(2)}, u32[]{:S(2)}) collective-permute-start(bf16[32,1792]{1,0:T(8,128)(2,1)S(1)} %pad_maximum_fusion.4), channel_id=1, source_target_pairs={{4,0},{5,1},{8,4},{9,5},{12,8},{13,9},{14,12},{15,13},{10,14},{11,... | collective-permute-start | bytes 344072 | tf_op jit(solution)/shard_map/ppermute | solution.py:266
  65.2 6.3 %collective-permute-start.27 = (bf16[32,1792]{1,0:T(8,128)(2,1)S(1)}, bf16[32,1792]{1,0:T(8,128)(2,1)S(1)}, u32[]{:S(2)}, u32[]{:S(2)}) collective-permute-start(bf16[32,1792]{1,0:T(8,128)(2,1)S(1)} %pad_maximum_fusion.3), channel_id=1, source_target_pairs={{0,4},{1,5},{4,8},{5,9},{8,12},{9,13},{12,14},{13,15},{14,10},{15,... | collective-permute-start | bytes 344072 | tf_op jit(solution)/shard_map/ppermute | solution.py:265
  69.3 4.8 %collective-permute-start.26 = (bf16[32,1792]{1,0:T(8,128)(2,1)S(1)}, bf16[32,1792]{1,0:T(8,128)(2,1)S(1)}, u32[]{:S(2)}, u32[]{:S(2)}) collective-permute-start(bf16[32,1792]{1,0:T(8,128)(2,1)S(1)} %get-tuple-element.107), channel_id=1, source_target_pairs={{4,0},{5,1},{8,4},{9,5},{12,8},{13,9},{14,12},{15,13},{10,14},{11,... | collective-permute-start | bytes 344072 | tf_op jit(solution)/shard_map/ppermute | solution.py:266
  69.8 4.8 %collective-permute-start.25 = (bf16[32,1792]{1,0:T(8,128)(2,1)S(1)}, bf16[32,1792]{1,0:T(8,128)(2,1)S(1)}, u32[]{:S(2)}, u32[]{:S(2)}) collective-permute-start(bf16[32,1792]{1,0:T(8,128)(2,1)S(1)} %get-tuple-element.108), channel_id=1, source_target_pairs={{0,4},{1,5},{4,8},{5,9},{8,12},{9,13},{12,14},{13,15},{14,10},{15,... | collective-permute-start | bytes 344072 | tf_op jit(solution)/shard_map/ppermute | solution.py:265
  71.6 4.8 %collective-permute-start.32 = (bf16[32,1792]{1,0:T(8,128)(2,1)S(1)}, bf16[32,1792]{1,0:T(8,128)(2,1)S(1)}, u32[]{:S(2)}, u32[]{:S(2)}) collective-permute-start(bf16[32,1792]{1,0:T(8,128)(2,1)S(1)} %get-tuple-element.105), channel_id=1, source_target_pairs={{4,0},{5,1},{8,4},{9,5},{12,8},{13,9},{14,12},{15,13},{10,14},{11,... | collective-permute-start | bytes 344072 | tf_op jit(solution)/shard_map/ppermute | solution.py:266
  72.1 6.0 %collective-permute-start.31 = (bf16[32,1792]{1,0:T(8,128)(2,1)S(1)}, bf16[32,1792]{1,0:T(8,128)(2,1)S(1)}, u32[]{:S(2)}, u32[]{:S(2)}) collective-permute-start(bf16[32,1792]{1,0:T(8,128)(2,1)S(1)} %get-tuple-element.106), channel_id=1, source_target_pairs={{0,4},{1,5},{4,8},{5,9},{8,12},{9,13},{12,14},{13,15},{14,10},{15,... | collective-permute-start | bytes 344072 | tf_op jit(solution)/shard_map/ppermute | solution.py:265
  78.2 4.8 %collective-permute-start.33 = (bf16[32,1792]{1,0:T(8,128)(2,1)S(1)}, bf16[32,1792]{1,0:T(8,128)(2,1)S(1)}, u32[]{:S(2)}, u32[]{:S(2)}) collective-permute-start(bf16[32,1792]{1,0:T(8,128)(2,1)S(1)} %get-tuple-element.95), channel_id=1, source_target_pairs={{0,4},{1,5},{4,8},{5,9},{8,12},{9,13},{12,14},{13,15},{14,10},{15,... | collective-permute-start | bytes 344072 | tf_op jit(solution)/shard_map/ppermute | solution.py:265
  79.8 4.8 %collective-permute-start.34 = (bf16[32,1792]{1,0:T(8,128)(2,1)S(1)}, bf16[32,1792]{1,0:T(8,128)(2,1)S(1)}, u32[]{:S(2)}, u32[]{:S(2)}) collective-permute-start(bf16[32,1792]{1,0:T(8,128)(2,1)S(1)} %get-tuple-element.96), channel_id=1, source_target_pairs={{4,0},{5,1},{8,4},{9,5},{12,8},{13,9},{14,12},{15,13},{10,14},{11,... | collective-permute-start | bytes 344072 | tf_op jit(solution)/shard_map/ppermute | solution.py:266
  80.2 5.6 %collective-permute-start.30 = (bf16[32,1792]{1,0:T(8,128)(2,1)S(1)}, bf16[32,1792]{1,0:T(8,128)(2,1)S(1)}, u32[]{:S(2)}, u32[]{:S(2)}) collective-permute-start(bf16[32,1792]{1,0:T(8,128)(2,1)S(1)} %get-tuple-element.97), channel_id=1, source_target_pairs={{4,0},{5,1},{8,4},{9,5},{12,8},{13,9},{14,12},{15,13},{10,14},{11,... | collective-permute-start | bytes 344072 | tf_op jit(solution)/shard_map/ppermute | solution.py:266
  80.5 5.3 %collective-permute-start.29 = (bf16[32,1792]{1,0:T(8,128)(2,1)S(1)}, bf16[32,1792]{1,0:T(8,128)(2,1)S(1)}, u32[]{:S(2)}, u32[]{:S(2)}) collective-permute-start(bf16[32,1792]{1,0:T(8,128)(2,1)S(1)} %get-tuple-element.98), channel_id=1, source_target_pairs={{0,4},{1,5},{4,8},{5,9},{8,12},{9,13},{12,14},{13,15},{14,10},{15,... | collective-permute-start | bytes 344072 | tf_op jit(solution)/shard_map/ppermute | solution.py:265

commit v5 on v4

--- a/solution.py
+++ b/solution.py
@@ -123,12 +123,13 @@
         x_ref[at * rows : (at + 1) * rows, :] = ref[:, :width]
 
 
-def gather_weights(experts, me_ref, blocks, width, w_ref):
+def gather_weights(experts, blocks, width, w_ref):
+    me = lax.axis_index("node")
     rows = blocks[0].shape[0]
     for at, ref in enumerate(blocks):
         table = ref[:, width:].astype(F32)
         lane = lax.broadcasted_iota(jnp.int32, table.shape, 1)
-        own = lax.rem(lane, experts) == me_ref[0]
+        own = lax.rem(lane, experts) == me
         w_ref[at * rows : (at + 1) * rows, :] = jnp.sum(jnp.where(own, table, 0.0), axis=1, keepdims=True)
 
 
@@ -190,7 +191,7 @@
     )(*blocks, vmem(w_gate), hbm(w_up) if fetch else vmem(w_up))
 
 
-def output_kernel(count, experts, tile, parts, me_ref, *refs):
+def output_kernel(count, experts, tile, parts, *refs):
     blocks, (h_ref, source, mine_ref, other_ref, *rest) = refs[:count], refs[count:]
     if parts:
         down_ref, w_ref, sems = rest
@@ -198,7 +199,7 @@
     else:
         down_ref, (w_ref,), moves = source, rest, []
     width = mine_ref.shape[1]
-    gather_weights(experts, me_ref, blocks, width, w_ref)
+    gather_weights(experts, blocks, width, w_ref)
     for i in range(max(parts, 1)):
         if parts:
             moves[i].wait()
@@ -206,7 +207,7 @@
         second_half(h_ref, down_ref, w_ref, mine_ref, other_ref, tile, begin, end)
 
 
-def output(blocks, mine, me, experts, h, w_down, fetch):
+def output(blocks, mine, experts, h, w_down, fetch):
     count, rows = len(blocks), blocks[0].shape[0]
     _, ff, width = w_down.shape
     _, tile = tiles(width, ff)
@@ -216,8 +217,7 @@
         functools.partial(output_kernel, count, experts, tile, parts),
         out_shape=[pltpu.VMEM((mine * rows, width), F32), pltpu.VMEM(((count - mine) * rows, width), BF16)]
         + [pltpu.VMEM(w_down.shape, BF16)] * fetch,
-        in_specs=[pl.BlockSpec(memory_space=pltpu.SMEM)]
-        + [here] * (count + 1)
+        in_specs=[here] * (count + 1)
         + [pl.BlockSpec(memory_space=pltpu.HBM if fetch else pltpu.VMEM)],
         out_specs=[here] * (2 + fetch),
         scratch_shapes=[pltpu.VMEM((count * rows, 1), F32)] + [pltpu.SemaphoreType.DMA((parts,))] * fetch,
@@ -225,18 +225,18 @@
         cost_estimate=pl.CostEstimate(
             flops=2 * max(count * rows, 256) * width * ff, bytes_accessed=0, transcendentals=0
         ),
-    )(me, *blocks, h, hbm(w_down) if fetch else vmem(w_down))
-
-
-def expert_kernel(count, experts, tile_ff, tile_d, me_ref, *refs):
+    )(*blocks, h, hbm(w_down) if fetch else vmem(w_down))
+
+
+def expert_kernel(count, experts, tile_ff, tile_d, *refs):
     blocks, (gate_ref, up_ref, down_ref, mine_ref, other_ref, x_ref, w_ref, h_ref) = refs[:count], refs[count:]
     gather_rows(blocks, x_ref)
-    gather_weights(experts, me_ref, blocks, x_ref.shape[1], w_ref)
+    gather_weights(experts, blocks, x_ref.shape[1], w_ref)
     first_half(x_ref, gate_ref, up_ref, h_ref, tile_ff, 0, h_ref.shape[1])
     second_half(h_ref, down_ref, w_ref, mine_ref, other_ref, tile_d, 0, x_ref.shape[1])
 
 
-def expert(blocks, mine, me, experts, w_gate, w_up, w_down):
+def expert(blocks, mine, experts, w_gate, w_up, w_down):
     count, rows = len(blocks), blocks[0].shape[0]
     _, width, ff = w_gate.shape
     total = count * rows
@@ -244,21 +244,20 @@
     return pl.pallas_call(
         functools.partial(expert_kernel, count, experts, *tiles(width, ff)),
         out_shape=[pltpu.VMEM((mine * rows, width), F32), pltpu.VMEM((total - mine * rows, width), BF16)],
-        in_specs=[pl.BlockSpec(memory_space=pltpu.SMEM)] + [here] * (count + 3),
+        in_specs=[here] * (count + 3),
         out_specs=[here] * 2,
         scratch_shapes=[pltpu.VMEM((total, width), BF16), pltpu.VMEM((total, 1), F32), pltpu.VMEM((total, ff), BF16)],
         compiler_params=pltpu.CompilerParams(vmem_limit_bytes=SCRATCH),
         cost_estimate=pl.CostEstimate(
             flops=6 * max(total, 256) * width * ff, bytes_accessed=0, transcendentals=total * ff
         ),
-    )(me, *blocks, vmem(w_gate), vmem(w_up), vmem(w_down))
+    )(*blocks, vmem(w_gate), vmem(w_up), vmem(w_down))
 
 
 def local(cores, order, tokens, routes, gates, w_gate, w_up, w_down):
     chips = len(order)
     experts = chips * cores
     rows, width = tokens.shape
-    me = lax.axis_index("node").astype(jnp.int32).reshape(1)
     forth = [(order[i] * cores + c, order[(i + 1) % chips] * cores + c) for i in range(chips) for c in range(cores)]
     back = [(b, a) for a, b in forth]
     swap = [(chip * cores + c, chip * cores + 1 - c) for chip in range(chips) for c in range(cores)]
@@ -281,7 +280,7 @@
             near = [got[0], got[1], got[-1], twin[0]]
             (h_near, w_up), new, a, b = together((hidden(near, w_gate, w_up, True), new, a, b))
         elif d == 3:
-            (*near_out, w_down), new, a, b = together((output(near, 3, me, experts, h_near, w_down, True), new, a, b))
+            (*near_out, w_down), new, a, b = together((output(near, 3, experts, h_near, w_down, True), new, a, b))
         else:
             new, a, b = together((new, a, b))
         got[d], got[-d] = a, b
@@ -292,8 +291,8 @@
     (h_rest,), ends, new, near_sent = together((hidden(rest, w_gate, w_up, False), ends, new, sibling(near_out[1])))
     twin.update(new)
     got[far] = jnp.concatenate(ends, axis=0)
-    rest_out, twin[far] = together((output(rest, len(middle), me, experts, h_rest, w_down, False), sibling(got[far])))
-    late_out = expert([got[d] for d in late] + [twin[d] for d in late], len(late), me, experts, w_gate, w_up, w_down)
+    rest_out, twin[far] = together((output(rest, len(middle), experts, h_rest, w_down, False), sibling(got[far])))
+    late_out = expert([got[d] for d in late] + [twin[d] for d in late], len(late), experts, w_gate, w_up, w_down)
 
     block = lambda a, j: a[j * rows : (j + 1) * rows]
     mine, theirs = {}, {0: near_sent}

time: 86.8 us -> 79.8 us (0.919)
  local copies, waits for them, and re-layouts: 8.92 us -> 0.1 us
  waiting for transfers between devices: 20.9 us -> 23.9 us
  Pallas kernels: 27 us -> 25.9 us
    unnamed x15 -> x1, local copies, waits for them, and re-layouts: 7.93 us -> 0.01 us
    ppermute x12, waiting for transfers between devices: 6.23 us -> 8.53 us  [local(): right = lambda a: lax.ppermute(a, 'node', forth)]
    ppermute x12, starting transfers between devices: 21.1 us -> 19.4 us  [local(): right = lambda a: lax.ppermute(a, 'node', forth)]
    ppermute x12, starting transfers between devices: 4.77 us -> 6.39 us  [local(): left = lambda a: lax.ppermute(a, 'node', back)]
    pallas_call x1, Pallas kernels: 7.55 us -> 6.57 us  [expert(): pl.pallas_call(functools.partial(expert_kernel, count, experts, *tiles(wi...]
    slice x2, local copies, waits for them, and re-layouts: 0.92 us -> 0.02 us  [local(): ends = (right(got[1 - far][:cut]), left(got[far - 1][cut:]))]
  transfers between devices with their start and end apart: 35 -> 35, of which waited for: 15 -> 17; matrix products, arithmetic and copies ran while one was open for 2% -> 1% of each run, Pallas kernels for 21% -> 23%
where the time goes in v5:
time: 79.8 us; the launch traced here: 79.6 us
  starting transfers between devices  28.1 us (35%)
  Pallas kernels  25.9 us (32%)
  waiting for transfers between devices  23.9 us (30%)
  other arithmetic  1.34 us (2%)
    ppermute x12, starting transfers between devices, local(): right = lambda a: lax.ppermute(a, 'node', forth)  19.4 us
    ppermute x12, waiting for transfers between devices, local(): left = lambda a: lax.ppermute(a, 'node', back)  13.7 us
    pallas_call x2, Pallas kernels, hidden(): pl.pallas_call(functools.partial(hidden_kernel, count, tile, parts), out_...  8.77 us
    ppermute x12, waiting for transfers between devices, local(): right = lambda a: lax.ppermute(a, 'node', forth)  8.53 us
    pallas_call x1, Pallas kernels, expert(): pl.pallas_call(functools.partial(expert_kernel, count, experts, *tiles(wi...  6.57 us
    pallas_call x2, Pallas kernels, output(): pl.pallas_call(functools.partial(output_kernel, count, experts, tile, par...  6.4 us
    ppermute x12, starting transfers between devices, local(): left = lambda a: lax.ppermute(a, 'node', back)  6.39 us
    pallas_call x1, Pallas kernels, load(): pl.pallas_call(functools.partial(load_kernel, parts), out_shape=pltpu.VME...  3.17 us
  transfers between devices with their start and end apart: 35, of which 17 were waited for; matrix products, arithmetic and copies ran while one was open for 1% of the time, Pallas kernels for 23%

profile of v5, /device:TPU:0, one launch (start us, length us, event | category | flops | bytes accessed | tf_op | source)
XLA Modules:
  0.0 79.6 jit_solution(12511749740343552455)
XLA Ops:
  0.0 1.0 %shard_map.64.after.refs_0_ = bf16[32,3712]{1,0:T(8,128)(2,1)S(1)} custom-call(bf16[32,3584]{1,0:T(8,128)(2,1)} %tok_hbm.1, s32[8,32]{1,0:T(8,128)} %bitcast.2, f32[8,32]{1,0:T(8,128)} %bitcast.3), custom_call_target="tpu_custom_call" | custom-call | tf_op jit(solution)/shard_map/pallas_call | solution.py:61
  1.0 3.1 %collective-permute-start.2 = (bf16[32,3712]{1,0:T(8,128)(2,1)S(1)}, bf16[32,3712]{1,0:T(8,128)(2,1)S(1)}, u32[]{:S(2)}, u32[]{:S(2)}) collective-permute-start(bf16[32,3712]{1,0:T(8,128)(2,1)S(1)} %shard_map.64.after.refs_0_), channel_id=1, source_target_pairs={{0,4},{1,5},{4,8},{5,9},{8,12},{9,13},{12,14},{13,15},{14,10},{15,... | collective-permute-start | bytes 712712 | tf_op jit(solution)/shard_map/ppermute | solution.py:264
  4.1 3.2 %shard_map.65.refs_4_.refs_6_ = bf16[1,3584,1024]{2,1,0:T(8,128)(2,1)S(1)} custom-call(bf16[1,3584,1024]{2,1,0:T(8,128)(2,1)} %source.1, bf16[32,3712]{1,0:T(8,128)(2,1)S(1)} %shard_map.64.after.refs_0_), custom_call_target="tpu_custom_call" | custom-call | bytes 7340032 | tf_op jit(solution)/shard_map/pallas_call | solution.py:109
  7.3 2.5 %collective-permute-done.2.refs_2_ = bf16[32,3712]{1,0:T(8,128)(2,1)S(1)} collective-permute-done((bf16[32,3712]{1,0:T(8,128)(2,1)S(1)}, bf16[32,3712]{1,0:T(8,128)(2,1)S(1)}, u32[]{:S(2)}, u32[]{:S(2)}) %collective-permute-start.2) | collective-permute-done | bytes 237600 | tf_op jit(solution)/shard_map/ppermute | solution.py:264
  9.8 1.5 %collective-permute-done.1.refs_1_ = bf16[32,3712]{1,0:T(8,128)(2,1)S(1)} collective-permute-done((bf16[32,3712]{1,0:T(8,128)(2,1)S(1)}, bf16[32,3712]{1,0:T(8,128)(2,1)S(1)}, u32[]{:S(2)}, u32[]{:S(2)}) %collective-permute-start.1) | collective-permute-done | bytes 237600 | tf_op jit(solution)/shard_map/ppermute | solution.py:265
  11.3 0.3 collective-permute-start.5
  11.6 1.7 %collective-permute-start.6 = (bf16[32,3712]{1,0:T(8,128)(2,1)S(1)}, bf16[32,3712]{1,0:T(8,128)(2,1)S(1)}, u32[]{:S(2)}, u32[]{:S(2)}) collective-permute-start(bf16[32,3712]{1,0:T(8,128)(2,1)S(1)} %collective-permute-done.2.refs_2_), channel_id=1, source_target_pairs={{0,4},{1,5},{4,8},{5,9},{8,12},{9,13},{12,14},{13,15},{14,10},{15,... | collective-permute-start | bytes 712712 | tf_op jit(solution)/shard_map/ppermute | solution.py:264
  13.6 5.0 %shard_map.66 = (bf16[128,1024]{1,0:T(8,128)(2,1)S(1)}, bf16[1,3584,1024]{2,1,0:T(8,128)(2,1)S(1)}) custom-call(bf16[32,3712]{1,0:T(8,128)(2,1)S(1)} %shard_map.64.after.refs_0_, bf16[32,3712]{1,0:T(8,128)(2,1)S(1)} %collective-permute-done.1.refs_1_, bf16[32,3712]{1,0:T(8,128)(2,1)S(1)} %collective-permute-done.2.refs_2_, ...), custom_call_target="tpu_custom_call" | custom-call | flops 3758096384 | tf_op jit(solution)/shard_map/pallas_call | solution.py:181
  18.6 1.2 %collective-permute-done.6.refs_1_ = bf16[32,3712]{1,0:T(8,128)(2,1)S(1)} collective-permute-done((bf16[32,3712]{1,0:T(8,128)(2,1)S(1)}, bf16[32,3712]{1,0:T(8,128)(2,1)S(1)}, u32[]{:S(2)}, u32[]{:S(2)}) %collective-permute-start.6) | collective-permute-done | bytes 237600 | tf_op jit(solution)/shard_map/ppermute | solution.py:264
  19.8 1.7 %collective-permute-start.10 = (bf16[32,3712]{1,0:T(8,128)(2,1)S(1)}, bf16[32,3712]{1,0:T(8,128)(2,1)S(1)}, u32[]{:S(2)}, u32[]{:S(2)}) collective-permute-start(bf16[32,3712]{1,0:T(8,128)(2,1)S(1)} %collective-permute-done.6.refs_1_), channel_id=1, source_target_pairs={{0,4},{1,5},{4,8},{5,9},{8,12},{9,13},{12,14},{13,15},{14,10},{15,... | collective-permute-start | bytes 712712 | tf_op jit(solution)/shard_map/ppermute | solution.py:264
  21.6 0.3 collective-permute-start.9
  22.1 3.5 %shard_map.67 = (f32[96,3584]{1,0:T(8,128)S(1)}, bf16[32,3584]{1,0:T(8,128)(2,1)S(1)}, bf16[1,1024,3584]{2,1,0:T(8,128)(2,1)S(1)}) custom-call(bf16[32,3712]{1,0:T(8,128)(2,1)S(1)} %shard_map.64.after.refs_0_, bf16[32,3712]{1,0:T(8,128)(2,1)S(1)} %collective-permute-done.1.refs_1_, bf16[32,3712]{1,0:T(8,128)(2,1)S(1)} %collective-permute-done.2.refs_2_, ...), custom_call_target="tpu_custom_call" | custom-call | flops 1879048192 | tf_op jit(solution)/shard_map/pallas_call | solution.py:216
  25.6 1.6 %collective-permute-done.10.refs_2_ = bf16[32,3712]{1,0:T(8,128)(2,1)S(1)} collective-permute-done((bf16[32,3712]{1,0:T(8,128)(2,1)S(1)}, bf16[32,3712]{1,0:T(8,128)(2,1)S(1)}, u32[]{:S(2)}, u32[]{:S(2)}) %collective-permute-start.10) | collective-permute-done | bytes 237600 | tf_op jit(solution)/shard_map/ppermute | solution.py:264
  27.2 2.5 %collective-permute-done.9.refs_1_ = bf16[32,3712]{1,0:T(8,128)(2,1)S(1)} collective-permute-done((bf16[32,3712]{1,0:T(8,128)(2,1)S(1)}, bf16[32,3712]{1,0:T(8,128)(2,1)S(1)}, u32[]{:S(2)}, u32[]{:S(2)}) %collective-permute-start.9) | collective-permute-done | bytes 237600 | tf_op jit(solution)/shard_map/ppermute | solution.py:265
  29.9 0.6 collective-permute-start.14
  30.7 1.7 %collective-permute-start.11 = (bf16[16,3712]{1,0:T(8,128)(2,1)S(1)}, bf16[16,3712]{1,0:T(8,128)(2,1)S(1)}, u32[]{:S(2)}, u32[]{:S(2)}) collective-permute-start(bf16[16,3712]{1,0:T(8,128)(2,1)S(1)} %slice.188), channel_id=1, source_target_pairs={{0,4},{1,5},{4,8},{5,9},{8,12},{9,13},{12,14},{13,15},{14,10},{15,... | collective-permute-start | bytes 356360 | tf_op jit(solution)/shard_map/ppermute | solution.py:264
  32.4 3.8 %shard_map.68.refs_6_ = bf16[192,1024]{1,0:T(8,128)(2,1)S(1)} custom-call(bf16[32,3712]{1,0:T(8,128)(2,1)S(1)} %collective-permute-done.5.refs_0_, bf16[32,3712]{1,0:T(8,128)(2,1)S(1)} %collective-permute-done.6.refs_1_, bf16[32,3712]{1,0:T(8,128)(2,1)S(1)} %collective-permute-done.4.refs_2_, bf16[32,3712]{1,0:T(8,128)(2,1)S(1)} %collective-permute-done.3.refs_3_, ...), custom_call_target="tpu_custom_call" | custom-call | flops 3758096384 | tf_op jit(solution)/shard_map/pallas_call | solution.py:181
  36.4 0.6 collective-permute-start.16
  36.9 2.9 %shard_map.69 = (f32[64,3584]{1,0:T(8,128)S(1)}, bf16[128,3584]{1,0:T(8,128)(2,1)S(1)}) custom-call(bf16[32,3712]{1,0:T(8,128)(2,1)S(1)} %collective-permute-done.5.refs_0_, bf16[32,3712]{1,0:T(8,128)(2,1)S(1)} %collective-permute-done.6.refs_1_, bf16[32,3712]{1,0:T(8,128)(2,1)S(1)} %collective-permute-done.4.refs_2_, ...), custom_call_target="tpu_custom_call" | custom-call | flops 1879048192 | tf_op jit(solution)/shard_map/pallas_call | solution.py:216
  39.8 6.6 %shard_map.70 = (f32[96,3584]{1,0:T(8,128)S(1)}, bf16[96,3584]{1,0:T(8,128)(2,1)S(1)}) custom-call(bf16[32,3712]{1,0:T(8,128)(2,1)S(1)} %constant_dynamic-update-slice_fusion.refs_0_, bf16[32,3712]{1,0:T(8,128)(2,1)S(1)} %collective-permute-done.9.refs_1_, bf16[32,3712]{1,0:T(8,128)(2,1)S(1)} %collective-permute-done.10.refs_2_, ...), custom_call_target="tpu_custom_call" | custom-call | flops 5637144576 | tf_op jit(solution)/shard_map/pallas_call | solution.py:244
  46.5 0.5 collective-permute-start.17
  47.0 1.6 %collective-permute-done.18 = bf16[96,3584]{1,0:T(8,128)(2,1)S(1)} collective-permute-done((bf16[96,3584]{1,0:T(8,128)(2,1)S(1)}, bf16[96,3584]{1,0:T(8,128)(2,1)S(1)}, u32[]{:S(2)}, u32[]{:S(2)}) %collective-permute-start.18) | collective-permute-done | bytes 688160 | tf_op jit(solution)/shard_map/ppermute | solution.py:266
  48.7 1.6 %collective-permute-start.19 = (bf16[16,1792]{1,0:T(8,128)(2,1)S(1)}, bf16[16,1792]{1,0:T(8,128)(2,1)S(1)}, u32[]{:S(2)}, u32[]{:S(2)}) collective-permute-start(bf16[16,1792]{1,0:T(8,128)(2,1)S(1)} %get-tuple-element.112), channel_id=1, source_target_pairs={{0,4},{1,5},{4,8},{5,9},{8,12},{9,13},{12,14},{13,15},{14,10},{15,... | collective-permute-start | bytes 172040 | tf_op jit(solution)/shard_map/ppermute | solution.py:264
  50.4 0.5 collective-permute-start.24
  50.9 1.5 %collective-permute-start.23 = (bf16[16,1792]{1,0:T(8,128)(2,1)S(1)}, bf16[16,1792]{1,0:T(8,128)(2,1)S(1)}, u32[]{:S(2)}, u32[]{:S(2)}) collective-permute-start(bf16[16,1792]{1,0:T(8,128)(2,1)S(1)} %get-tuple-element.114), channel_id=1, source_target_pairs={{0,4},{1,5},{4,8},{5,9},{8,12},{9,13},{12,14},{13,15},{14,10},{15,... | collective-permute-start | bytes 172040 | tf_op jit(solution)/shard_map/ppermute | solution.py:264
  52.5 0.5 collective-permute-start.21
  53.0 1.6 %collective-permute-start.20 = (bf16[32,1792]{1,0:T(8,128)(2,1)S(1)}, bf16[32,1792]{1,0:T(8,128)(2,1)S(1)}, u32[]{:S(2)}, u32[]{:S(2)}) collective-permute-start(bf16[32,1792]{1,0:T(8,128)(2,1)S(1)} %pad_maximum_fusion.1), channel_id=1, source_target_pairs={{0,4},{1,5},{4,8},{5,9},{8,12},{9,13},{12,14},{13,15},{14,10},{15,... | collective-permute-start | bytes 344072 | tf_op jit(solution)/shard_map/ppermute | solution.py:264
  54.6 2.1 %collective-permute-done.21 = bf16[16,1792]{1,0:T(8,128)(2,1)S(1)} collective-permute-done((bf16[16,1792]{1,0:T(8,128)(2,1)S(1)}, bf16[16,1792]{1,0:T(8,128)(2,1)S(1)}, u32[]{:S(2)}, u32[]{:S(2)}) %collective-permute-start.21) | collective-permute-done | bytes 57376 | tf_op jit(solution)/shard_map/ppermute | solution.py:265
  56.7 0.5 collective-permute-start.22
  57.3 0.6 collective-permute-start.28
  57.9 1.5 %collective-permute-start.27 = (bf16[32,1792]{1,0:T(8,128)(2,1)S(1)}, bf16[32,1792]{1,0:T(8,128)(2,1)S(1)}, u32[]{:S(2)}, u32[]{:S(2)}) collective-permute-start(bf16[32,1792]{1,0:T(8,128)(2,1)S(1)} %pad_maximum_fusion.3), channel_id=1, source_target_pairs={{0,4},{1,5},{4,8},{5,9},{8,12},{9,13},{12,14},{13,15},{14,10},{15,... | collective-permute-start | bytes 344072 | tf_op jit(solution)/shard_map/ppermute | solution.py:264
  59.4 2.3 %collective-permute-done.22 = bf16[32,1792]{1,0:T(8,128)(2,1)S(1)} collective-permute-done((bf16[32,1792]{1,0:T(8,128)(2,1)S(1)}, bf16[32,1792]{1,0:T(8,128)(2,1)S(1)}, u32[]{:S(2)}, u32[]{:S(2)}) %collective-permute-start.22) | collective-permute-done | bytes 114720 | tf_op jit(solution)/shard_map/ppermute | solution.py:265
  61.8 0.5 collective-permute-start.26
  62.4 1.5 %collective-permute-start.25 = (bf16[32,1792]{1,0:T(8,128)(2,1)S(1)}, bf16[32,1792]{1,0:T(8,128)(2,1)S(1)}, u32[]{:S(2)}, u32[]{:S(2)}) collective-permute-start(bf16[32,1792]{1,0:T(8,128)(2,1)S(1)} %get-tuple-element.108), channel_id=1, source_target_pairs={{0,4},{1,5},{4,8},{5,9},{8,12},{9,13},{12,14},{13,15},{14,10},{15,... | collective-permute-start | bytes 344072 | tf_op jit(solution)/shard_map/ppermute | solution.py:264
  64.1 1.1 %collective-permute-start.32 = (bf16[32,1792]{1,0:T(8,128)(2,1)S(1)}, bf16[32,1792]{1,0:T(8,128)(2,1)S(1)}, u32[]{:S(2)}, u32[]{:S(2)}) collective-permute-start(bf16[32,1792]{1,0:T(8,128)(2,1)S(1)} %get-tuple-element.105), channel_id=1, source_target_pairs={{4,0},{5,1},{8,4},{9,5},{12,8},{13,9},{14,12},{15,13},{10,14},{11,... | collective-permute-start | bytes 344072 | tf_op jit(solution)/shard_map/ppermute | solution.py:265
  65.2 1.0 %collective-permute-start.31 = (bf16[32,1792]{1,0:T(8,128)(2,1)S(1)}, bf16[32,1792]{1,0:T(8,128)(2,1)S(1)}, u32[]{:S(2)}, u32[]{:S(2)}) collective-permute-start(bf16[32,1792]{1,0:T(8,128)(2,1)S(1)} %get-tuple-element.106), channel_id=1, source_target_pairs={{0,4},{1,5},{4,8},{5,9},{8,12},{9,13},{12,14},{13,15},{14,10},{15,... | collective-permute-start | bytes 344072 | tf_op jit(solution)/shard_map/ppermute | solution.py:264
  66.2 0.5 collective-permute-done.26
  66.7 0.5 collective-permute-done.25
  67.2 1.7 %collective-permute-done.32 = bf16[32,1792]{1,0:T(8,128)(2,1)S(1)} collective-permute-done((bf16[32,1792]{1,0:T(8,128)(2,1)S(1)}, bf16[32,1792]{1,0:T(8,128)(2,1)S(1)}, u32[]{:S(2)}, u32[]{:S(2)}) %collective-permute-start.32) | collective-permute-done | bytes 114720 | tf_op jit(solution)/shard_map/ppermute | solution.py:265
  68.9 1.5 %collective-permute-done.31 = bf16[32,1792]{1,0:T(8,128)(2,1)S(1)} collective-permute-done((bf16[32,1792]{1,0:T(8,128)(2,1)S(1)}, bf16[32,1792]{1,0:T(8,128)(2,1)S(1)}, u32[]{:S(2)}, u32[]{:S(2)}) %collective-permute-start.31) | collective-permute-done | bytes 114720 | tf_op jit(solution)/shard_map/ppermute | solution.py:264
  70.5 1.8 %collective-permute-start.33 = (bf16[32,1792]{1,0:T(8,128)(2,1)S(1)}, bf16[32,1792]{1,0:T(8,128)(2,1)S(1)}, u32[]{:S(2)}, u32[]{:S(2)}) collective-permute-start(bf16[32,1792]{1,0:T(8,128)(2,1)S(1)} %get-tuple-element.95), channel_id=1, source_target_pairs={{0,4},{1,5},{4,8},{5,9},{8,12},{9,13},{12,14},{13,15},{14,10},{15,... | collective-permute-start | bytes 344072 | tf_op jit(solution)/shard_map/ppermute | solution.py:264
  72.6 1.4 %collective-permute-start.30 = (bf16[32,1792]{1,0:T(8,128)(2,1)S(1)}, bf16[32,1792]{1,0:T(8,128)(2,1)S(1)}, u32[]{:S(2)}, u32[]{:S(2)}) collective-permute-start(bf16[32,1792]{1,0:T(8,128)(2,1)S(1)} %get-tuple-element.97), channel_id=1, source_target_pairs={{4,0},{5,1},{8,4},{9,5},{12,8},{13,9},{14,12},{15,13},{10,14},{11,... | collective-permute-start | bytes 344072 | tf_op jit(solution)/shard_map/ppermute | solution.py:265
  74.0 0.6 collective-permute-start.29
  74.6 0.7 collective-permute-done.33
  75.3 1.8 %collective-permute-done.34 = bf16[32,1792]{1,0:T(8,128)(2,1)S(1)} collective-permute-done((bf16[32,1792]{1,0:T(8,128)(2,1)S(1)}, bf16[32,1792]{1,0:T(8,128)(2,1)S(1)}, u32[]{:S(2)}, u32[]{:S(2)}) %collective-permute-start.34) | collective-permute-done | bytes 114720 | tf_op jit(solution)/shard_map/ppermute | solution.py:265
  77.1 1.2 %collective-permute-done.30 = bf16[32,1792]{1,0:T(8,128)(2,1)S(1)} collective-permute-done((bf16[32,1792]{1,0:T(8,128)(2,1)S(1)}, bf16[32,1792]{1,0:T(8,128)(2,1)S(1)}, u32[]{:S(2)}, u32[]{:S(2)}) %collective-permute-start.30) | collective-permute-done | bytes 114720 | tf_op jit(solution)/shard_map/ppermute | solution.py:265
  78.4 0.4 collective-permute-done.29
  78.9 0.7 pad_maximum_fusion
  (54 shorter events, 2.1 us)
Async XLA Ops:
  1.0 8.8 %collective-permute-start.2 = (bf16[32,3712]{1,0:T(8,128)(2,1)S(1)}, bf16[32,3712]{1,0:T(8,128)(2,1)S(1)}, u32[]{:S(2)}, u32[]{:S(2)}) collective-permute-start(bf16[32,3712]{1,0:T(8,128)(2,1)S(1)} %shard_map.64.after.refs_0_), channel_id=1, source_target_pairs={{0,4},{1,5},{4,8},{5,9},{8,12},{9,13},{12,14},{13,15},{14,10},{15,... | collective-permute-start | bytes 712712 | tf_op jit(solution)/shard_map/ppermute | solution.py:264
  4.1 7.2 %collective-permute-start.1 = (bf16[32,3712]{1,0:T(8,128)(2,1)S(1)}, bf16[32,3712]{1,0:T(8,128)(2,1)S(1)}, u32[]{:S(2)}, u32[]{:S(2)}) collective-permute-start(bf16[32,3712]{1,0:T(8,128)(2,1)S(1)} %shard_map.64.after.refs_0_), channel_id=1, source_target_pairs={{4,0},{5,1},{8,4},{9,5},{12,8},{13,9},{14,12},{15,13},{10,14},{11,... | collective-permute-start | bytes 712712 | tf_op jit(solution)/shard_map/ppermute | solution.py:265
  4.1 7.2 %collective-permute-start = (bf16[32,3712]{1,0:T(8,128)(2,1)S(1)}, bf16[32,3712]{1,0:T(8,128)(2,1)S(1)}, u32[]{:S(2)}, u32[]{:S(2)}) collective-permute-start(bf16[32,3712]{1,0:T(8,128)(2,1)S(1)} %shard_map.64.after.refs_0_), channel_id=1, source_target_pairs={{0,1},{1,0},{2,3},{3,2},{4,5},{5,4},{6,7},{7,6},{8,9},{9,8},{10,11... | collective-permute-start | bytes 712712 | tf_op jit(solution)/shard_map/ppermute | solution.py:266
  11.3 7.2 %collective-permute-start.5 = (bf16[32,3712]{1,0:T(8,128)(2,1)S(1)}, bf16[32,3712]{1,0:T(8,128)(2,1)S(1)}, u32[]{:S(2)}, u32[]{:S(2)}) collective-permute-start(bf16[32,3712]{1,0:T(8,128)(2,1)S(1)} %collective-permute-done.1.refs_1_), channel_id=1, source_target_pairs={{4,0},{5,1},{8,4},{9,5},{12,8},{13,9},{14,12},{15,13},{10,14},{11,... | collective-permute-start | bytes 712712 | tf_op jit(solution)/shard_map/ppermute | solution.py:265
  11.6 7.0 %collective-permute-start.4 = (bf16[32,3712]{1,0:T(8,128)(2,1)S(1)}, bf16[32,3712]{1,0:T(8,128)(2,1)S(1)}, u32[]{:S(2)}, u32[]{:S(2)}) collective-permute-start(bf16[32,3712]{1,0:T(8,128)(2,1)S(1)} %collective-permute-done.1.refs_1_), channel_id=1, source_target_pairs={{0,1},{1,0},{2,3},{3,2},{4,5},{5,4},{6,7},{7,6},{8,9},{9,8},{10,11... | collective-permute-start | bytes 712712 | tf_op jit(solution)/shard_map/ppermute | solution.py:266
  11.6 8.2 %collective-permute-start.6 = (bf16[32,3712]{1,0:T(8,128)(2,1)S(1)}, bf16[32,3712]{1,0:T(8,128)(2,1)S(1)}, u32[]{:S(2)}, u32[]{:S(2)}) collective-permute-start(bf16[32,3712]{1,0:T(8,128)(2,1)S(1)} %collective-permute-done.2.refs_2_), channel_id=1, source_target_pairs={{0,4},{1,5},{4,8},{5,9},{8,12},{9,13},{12,14},{13,15},{14,10},{15,... | collective-permute-start | bytes 712712 | tf_op jit(solution)/shard_map/ppermute | solution.py:264
  13.4 6.5 %collective-permute-start.3 = (bf16[32,3712]{1,0:T(8,128)(2,1)S(1)}, bf16[32,3712]{1,0:T(8,128)(2,1)S(1)}, u32[]{:S(2)}, u32[]{:S(2)}) collective-permute-start(bf16[32,3712]{1,0:T(8,128)(2,1)S(1)} %collective-permute-done.2.refs_2_), channel_id=1, source_target_pairs={{0,1},{1,0},{2,3},{3,2},{4,5},{5,4},{6,7},{7,6},{8,9},{9,8},{10,11... | collective-permute-start | bytes 712712 | tf_op jit(solution)/shard_map/ppermute | solution.py:266
  19.8 7.4 %collective-permute-start.10 = (bf16[32,3712]{1,0:T(8,128)(2,1)S(1)}, bf16[32,3712]{1,0:T(8,128)(2,1)S(1)}, u32[]{:S(2)}, u32[]{:S(2)}) collective-permute-start(bf16[32,3712]{1,0:T(8,128)(2,1)S(1)} %collective-permute-done.6.refs_1_), channel_id=1, source_target_pairs={{0,4},{1,5},{4,8},{5,9},{8,12},{9,13},{12,14},{13,15},{14,10},{15,... | collective-permute-start | bytes 712712 | tf_op jit(solution)/shard_map/ppermute | solution.py:264
  21.6 5.7 %collective-permute-start.7 = (bf16[32,3712]{1,0:T(8,128)(2,1)S(1)}, bf16[32,3712]{1,0:T(8,128)(2,1)S(1)}, u32[]{:S(2)}, u32[]{:S(2)}) collective-permute-start(bf16[32,3712]{1,0:T(8,128)(2,1)S(1)} %collective-permute-done.6.refs_1_), channel_id=1, source_target_pairs={{0,1},{1,0},{2,3},{3,2},{4,5},{5,4},{6,7},{7,6},{8,9},{9,8},{10,11... | collective-permute-start | bytes 712712 | tf_op jit(solution)/shard_map/ppermute | solution.py:266
  21.6 8.2 %collective-permute-start.9 = (bf16[32,3712]{1,0:T(8,128)(2,1)S(1)}, bf16[32,3712]{1,0:T(8,128)(2,1)S(1)}, u32[]{:S(2)}, u32[]{:S(2)}) collective-permute-start(bf16[32,3712]{1,0:T(8,128)(2,1)S(1)} %collective-permute-done.5.refs_0_), channel_id=1, source_target_pairs={{4,0},{5,1},{8,4},{9,5},{12,8},{13,9},{14,12},{15,13},{10,14},{11,... | collective-permute-start | bytes 712712 | tf_op jit(solution)/shard_map/ppermute | solution.py:265
  21.8 7.9 %collective-permute-start.8 = (bf16[32,3712]{1,0:T(8,128)(2,1)S(1)}, bf16[32,3712]{1,0:T(8,128)(2,1)S(1)}, u32[]{:S(2)}, u32[]{:S(2)}) collective-permute-start(bf16[32,3712]{1,0:T(8,128)(2,1)S(1)} %collective-permute-done.5.refs_0_), channel_id=1, source_target_pairs={{0,1},{1,0},{2,3},{3,2},{4,5},{5,4},{6,7},{7,6},{8,9},{9,8},{10,11... | collective-permute-start | bytes 712712 | tf_op jit(solution)/shard_map/ppermute | solution.py:266
  29.8 6.5 %collective-permute-start.13 = (bf16[32,3712]{1,0:T(8,128)(2,1)S(1)}, bf16[32,3712]{1,0:T(8,128)(2,1)S(1)}, u32[]{:S(2)}, u32[]{:S(2)}) collective-permute-start(bf16[32,3712]{1,0:T(8,128)(2,1)S(1)} %collective-permute-done.10.refs_2_), channel_id=1, source_target_pairs={{0,1},{1,0},{2,3},{3,2},{4,5},{5,4},{6,7},{7,6},{8,9},{9,8},{10,11... | collective-permute-start | bytes 712712 | tf_op jit(solution)/shard_map/ppermute | solution.py:266
  29.9 6.4 %collective-permute-start.14 = (bf16[32,3712]{1,0:T(8,128)(2,1)S(1)}, bf16[32,3712]{1,0:T(8,128)(2,1)S(1)}, u32[]{:S(2)}, u32[]{:S(2)}) collective-permute-start(bf16[32,3712]{1,0:T(8,128)(2,1)S(1)} %collective-permute-done.9.refs_1_), channel_id=1, source_target_pairs={{0,1},{1,0},{2,3},{3,2},{4,5},{5,4},{6,7},{7,6},{8,9},{9,8},{10,11... | collective-permute-start | bytes 712712 | tf_op jit(solution)/shard_map/ppermute | solution.py:266
  30.4 5.8 %collective-permute-start.12 = (bf16[16,3712]{1,0:T(8,128)(2,1)S(1)}, bf16[16,3712]{1,0:T(8,128)(2,1)S(1)}, u32[]{:S(2)}, u32[]{:S(2)}) collective-permute-start(bf16[16,3712]{1,0:T(8,128)(2,1)S(1)} %slice.189), channel_id=1, source_target_pairs={{4,0},{5,1},{8,4},{9,5},{12,8},{13,9},{14,12},{15,13},{10,14},{11,... | collective-permute-start | bytes 356360 | tf_op jit(solution)/shard_map/ppermute | solution.py:265
  30.7 5.6 %collective-permute-start.11 = (bf16[16,3712]{1,0:T(8,128)(2,1)S(1)}, bf16[16,3712]{1,0:T(8,128)(2,1)S(1)}, u32[]{:S(2)}, u32[]{:S(2)}) collective-permute-start(bf16[16,3712]{1,0:T(8,128)(2,1)S(1)} %slice.188), channel_id=1, source_target_pairs={{0,4},{1,5},{4,8},{5,9},{8,12},{9,13},{12,14},{13,15},{14,10},{15,... | collective-permute-start | bytes 356360 | tf_op jit(solution)/shard_map/ppermute | solution.py:264
  32.4 3.8 %collective-permute-start.15 = (bf16[32,3584]{1,0:T(8,128)(2,1)S(1)}, bf16[32,3584]{1,0:T(8,128)(2,1)S(1)}, u32[]{:S(2)}, u32[]{:S(2)}) collective-permute-start(bf16[32,3584]{1,0:T(8,128)(2,1)S(1)} %get-tuple-element.70), channel_id=1, source_target_pairs={{0,1},{1,0},{2,3},{3,2},{4,5},{5,4},{6,7},{7,6},{8,9},{9,8},{10,11... | collective-permute-start | bytes 688136 | tf_op jit(solution)/shard_map/ppermute | solution.py:266
  36.4 3.5 %collective-permute-start.16 = (bf16[32,3712]{1,0:T(8,128)(2,1)S(1)}, bf16[32,3712]{1,0:T(8,128)(2,1)S(1)}, u32[]{:S(2)}, u32[]{:S(2)}) collective-permute-start(bf16[32,3712]{1,0:T(8,128)(2,1)S(1)} %constant_dynamic-update-slice_fusion.refs_0_), channel_id=1, source_target_pairs={{0,1},{1,0},{2,3},{3,2},{4,5},{5,4},{6,7},{7,6},{8,9},{9,8},{10,11... | collective-permute-start | bytes 712712 | tf_op jit(solution)/shard_map/ppermute | solution.py:266
  46.4 2.2 %collective-permute-start.18 = (bf16[96,3584]{1,0:T(8,128)(2,1)S(1)}, bf16[96,3584]{1,0:T(8,128)(2,1)S(1)}, u32[]{:S(2)}, u32[]{:S(2)}) collective-permute-start(bf16[96,3584]{1,0:T(8,128)(2,1)S(1)} %get-tuple-element.84), channel_id=1, source_target_pairs={{0,1},{1,0},{2,3},{3,2},{4,5},{5,4},{6,7},{7,6},{8,9},{9,8},{10,11... | collective-permute-start | bytes 2064392 | tf_op jit(solution)/shard_map/ppermute | solution.py:266
  46.5 15.3 %collective-permute-start.17 = (bf16[128,3584]{1,0:T(8,128)(2,1)S(1)}, bf16[128,3584]{1,0:T(8,128)(2,1)S(1)}, u32[]{:S(2)}, u32[]{:S(2)}) collective-permute-start(bf16[128,3584]{1,0:T(8,128)(2,1)S(1)} %get-tuple-element.78), channel_id=1, source_target_pairs={{0,1},{1,0},{2,3},{3,2},{4,5},{5,4},{6,7},{7,6},{8,9},{9,8},{10,11... | collective-permute-start | bytes 2752520 | tf_op jit(solution)/shard_map/ppermute | solution.py:266
  48.7 4.2 %collective-permute-start.19 = (bf16[16,1792]{1,0:T(8,128)(2,1)S(1)}, bf16[16,1792]{1,0:T(8,128)(2,1)S(1)}, u32[]{:S(2)}, u32[]{:S(2)}) collective-permute-start(bf16[16,1792]{1,0:T(8,128)(2,1)S(1)} %get-tuple-element.112), channel_id=1, source_target_pairs={{0,4},{1,5},{4,8},{5,9},{8,12},{9,13},{12,14},{13,15},{14,10},{15,... | collective-permute-start | bytes 172040 | tf_op jit(solution)/shard_map/ppermute | solution.py:264
  50.4 6.8 %collective-permute-start.24 = (bf16[16,1792]{1,0:T(8,128)(2,1)S(1)}, bf16[16,1792]{1,0:T(8,128)(2,1)S(1)}, u32[]{:S(2)}, u32[]{:S(2)}) collective-permute-start(bf16[16,1792]{1,0:T(8,128)(2,1)S(1)} %get-tuple-element.113), channel_id=1, source_target_pairs={{4,0},{5,1},{8,4},{9,5},{12,8},{13,9},{14,12},{15,13},{10,14},{11,... | collective-permute-start | bytes 172040 | tf_op jit(solution)/shard_map/ppermute | solution.py:265
  50.9 6.3 %collective-permute-start.23 = (bf16[16,1792]{1,0:T(8,128)(2,1)S(1)}, bf16[16,1792]{1,0:T(8,128)(2,1)S(1)}, u32[]{:S(2)}, u32[]{:S(2)}) collective-permute-start(bf16[16,1792]{1,0:T(8,128)(2,1)S(1)} %get-tuple-element.114), channel_id=1, source_target_pairs={{0,4},{1,5},{4,8},{5,9},{8,12},{9,13},{12,14},{13,15},{14,10},{15,... | collective-permute-start | bytes 172040 | tf_op jit(solution)/shard_map/ppermute | solution.py:264
  52.5 4.2 %collective-permute-start.21 = (bf16[16,1792]{1,0:T(8,128)(2,1)S(1)}, bf16[16,1792]{1,0:T(8,128)(2,1)S(1)}, u32[]{:S(2)}, u32[]{:S(2)}) collective-permute-start(bf16[16,1792]{1,0:T(8,128)(2,1)S(1)} %get-tuple-element.111), channel_id=1, source_target_pairs={{4,0},{5,1},{8,4},{9,5},{12,8},{13,9},{14,12},{15,13},{10,14},{11,... | collective-permute-start | bytes 172040 | tf_op jit(solution)/shard_map/ppermute | solution.py:265
  53.0 6.4 %collective-permute-start.20 = (bf16[32,1792]{1,0:T(8,128)(2,1)S(1)}, bf16[32,1792]{1,0:T(8,128)(2,1)S(1)}, u32[]{:S(2)}, u32[]{:S(2)}) collective-permute-start(bf16[32,1792]{1,0:T(8,128)(2,1)S(1)} %pad_maximum_fusion.1), channel_id=1, source_target_pairs={{0,4},{1,5},{4,8},{5,9},{8,12},{9,13},{12,14},{13,15},{14,10},{15,... | collective-permute-start | bytes 344072 | tf_op jit(solution)/shard_map/ppermute | solution.py:264
  56.7 5.0 %collective-permute-start.22 = (bf16[32,1792]{1,0:T(8,128)(2,1)S(1)}, bf16[32,1792]{1,0:T(8,128)(2,1)S(1)}, u32[]{:S(2)}, u32[]{:S(2)}) collective-permute-start(bf16[32,1792]{1,0:T(8,128)(2,1)S(1)} %pad_maximum_fusion.2), channel_id=1, source_target_pairs={{4,0},{5,1},{8,4},{9,5},{12,8},{13,9},{14,12},{15,13},{10,14},{11,... | collective-permute-start | bytes 344072 | tf_op jit(solution)/shard_map/ppermute | solution.py:265
  57.3 6.7 %collective-permute-start.28 = (bf16[32,1792]{1,0:T(8,128)(2,1)S(1)}, bf16[32,1792]{1,0:T(8,128)(2,1)S(1)}, u32[]{:S(2)}, u32[]{:S(2)}) collective-permute-start(bf16[32,1792]{1,0:T(8,128)(2,1)S(1)} %pad_maximum_fusion.4), channel_id=1, source_target_pairs={{4,0},{5,1},{8,4},{9,5},{12,8},{13,9},{14,12},{15,13},{10,14},{11,... | collective-permute-start | bytes 344072 | tf_op jit(solution)/shard_map/ppermute | solution.py:265
  57.9 6.1 %collective-permute-start.27 = (bf16[32,1792]{1,0:T(8,128)(2,1)S(1)}, bf16[32,1792]{1,0:T(8,128)(2,1)S(1)}, u32[]{:S(2)}, u32[]{:S(2)}) collective-permute-start(bf16[32,1792]{1,0:T(8,128)(2,1)S(1)} %pad_maximum_fusion.3), channel_id=1, source_target_pairs={{0,4},{1,5},{4,8},{5,9},{8,12},{9,13},{12,14},{13,15},{14,10},{15,... | collective-permute-start | bytes 344072 | tf_op jit(solution)/shard_map/ppermute | solution.py:264
  61.8 4.8 %collective-permute-start.26 = (bf16[32,1792]{1,0:T(8,128)(2,1)S(1)}, bf16[32,1792]{1,0:T(8,128)(2,1)S(1)}, u32[]{:S(2)}, u32[]{:S(2)}) collective-permute-start(bf16[32,1792]{1,0:T(8,128)(2,1)S(1)} %get-tuple-element.107), channel_id=1, source_target_pairs={{4,0},{5,1},{8,4},{9,5},{12,8},{13,9},{14,12},{15,13},{10,14},{11,... | collective-permute-start | bytes 344072 | tf_op jit(solution)/shard_map/ppermute | solution.py:265
  62.4 4.8 %collective-permute-start.25 = (bf16[32,1792]{1,0:T(8,128)(2,1)S(1)}, bf16[32,1792]{1,0:T(8,128)(2,1)S(1)}, u32[]{:S(2)}, u32[]{:S(2)}) collective-permute-start(bf16[32,1792]{1,0:T(8,128)(2,1)S(1)} %get-tuple-element.108), channel_id=1, source_target_pairs={{0,4},{1,5},{4,8},{5,9},{8,12},{9,13},{12,14},{13,15},{14,10},{15,... | collective-permute-start | bytes 344072 | tf_op jit(solution)/shard_map/ppermute | solution.py:264
  64.1 4.8 %collective-permute-start.32 = (bf16[32,1792]{1,0:T(8,128)(2,1)S(1)}, bf16[32,1792]{1,0:T(8,128)(2,1)S(1)}, u32[]{:S(2)}, u32[]{:S(2)}) collective-permute-start(bf16[32,1792]{1,0:T(8,128)(2,1)S(1)} %get-tuple-element.105), channel_id=1, source_target_pairs={{4,0},{5,1},{8,4},{9,5},{12,8},{13,9},{14,12},{15,13},{10,14},{11,... | collective-permute-start | bytes 344072 | tf_op jit(solution)/shard_map/ppermute | solution.py:265
  65.2 5.2 %collective-permute-start.31 = (bf16[32,1792]{1,0:T(8,128)(2,1)S(1)}, bf16[32,1792]{1,0:T(8,128)(2,1)S(1)}, u32[]{:S(2)}, u32[]{:S(2)}) collective-permute-start(bf16[32,1792]{1,0:T(8,128)(2,1)S(1)} %get-tuple-element.106), channel_id=1, source_target_pairs={{0,4},{1,5},{4,8},{5,9},{8,12},{9,13},{12,14},{13,15},{14,10},{15,... | collective-permute-start | bytes 344072 | tf_op jit(solution)/shard_map/ppermute | solution.py:264
  70.5 4.8 %collective-permute-start.33 = (bf16[32,1792]{1,0:T(8,128)(2,1)S(1)}, bf16[32,1792]{1,0:T(8,128)(2,1)S(1)}, u32[]{:S(2)}, u32[]{:S(2)}) collective-permute-start(bf16[32,1792]{1,0:T(8,128)(2,1)S(1)} %get-tuple-element.95), channel_id=1, source_target_pairs={{0,4},{1,5},{4,8},{5,9},{8,12},{9,13},{12,14},{13,15},{14,10},{15,... | collective-permute-start | bytes 344072 | tf_op jit(solution)/shard_map/ppermute | solution.py:264
  72.3 4.8 %collective-permute-start.34 = (bf16[32,1792]{1,0:T(8,128)(2,1)S(1)}, bf16[32,1792]{1,0:T(8,128)(2,1)S(1)}, u32[]{:S(2)}, u32[]{:S(2)}) collective-permute-start(bf16[32,1792]{1,0:T(8,128)(2,1)S(1)} %get-tuple-element.96), channel_id=1, source_target_pairs={{4,0},{5,1},{8,4},{9,5},{12,8},{13,9},{14,12},{15,13},{10,14},{11,... | collective-permute-start | bytes 344072 | tf_op jit(solution)/shard_map/ppermute | solution.py:265
  72.6 5.8 %collective-permute-start.30 = (bf16[32,1792]{1,0:T(8,128)(2,1)S(1)}, bf16[32,1792]{1,0:T(8,128)(2,1)S(1)}, u32[]{:S(2)}, u32[]{:S(2)}) collective-permute-start(bf16[32,1792]{1,0:T(8,128)(2,1)S(1)} %get-tuple-element.97), channel_id=1, source_target_pairs={{4,0},{5,1},{8,4},{9,5},{12,8},{13,9},{14,12},{15,13},{10,14},{11,... | collective-permute-start | bytes 344072 | tf_op jit(solution)/shard_map/ppermute | solution.py:265
  74.0 4.8 %collective-permute-start.29 = (bf16[32,1792]{1,0:T(8,128)(2,1)S(1)}, bf16[32,1792]{1,0:T(8,128)(2,1)S(1)}, u32[]{:S(2)}, u32[]{:S(2)}) collective-permute-start(bf16[32,1792]{1,0:T(8,128)(2,1)S(1)} %get-tuple-element.98), channel_id=1, source_target_pairs={{0,4},{1,5},{4,8},{5,9},{8,12},{9,13},{12,14},{13,15},{14,10},{15,... | collective-permute-start | bytes 344072 | tf_op jit(solution)/shard_map/ppermute | solution.py:264

commit v6 on v5

--- a/solution.py
+++ b/solution.py
@@ -134,23 +134,21 @@
 
 
 def first_half(x_ref, gate_ref, up_ref, h_ref, tile, begin, end):
-    @pl.loop(begin // tile, end // tile)
-    def _(j):
-        at = pl.ds(pl.multiple_of(j * tile, tile), tile)
+    for j in range(begin // tile, end // tile):
+        at = slice(j * tile, (j + 1) * tile)
         gate = jnp.dot(x_ref[...], gate_ref[0, :, at], preferred_element_type=F32)
         upper = jnp.dot(x_ref[...], up_ref[0, :, at], preferred_element_type=F32)
         h_ref[:, at] = (gate / (1.0 + jnp.exp(-gate)) * upper).astype(BF16)
 
 
-def second_half(h_ref, down_ref, w_ref, mine_ref, other_ref, tile, begin, end):
-    half = mine_ref.shape[0]
-
-    @pl.loop(begin // tile, end // tile)
-    def _(j):
-        at = pl.ds(pl.multiple_of(j * tile, tile), tile)
+def second_half(h_ref, down_ref, w_ref, out_refs, tile, begin, end):
+    for j in range(begin // tile, end // tile):
+        at = slice(j * tile, (j + 1) * tile)
         out = jnp.dot(h_ref[...], down_ref[0, :, at], preferred_element_type=F32) * w_ref[...]
-        mine_ref[:, at] = out[:half]
-        other_ref[:, at] = out[half:].astype(BF16)
+        row = 0
+        for ref in out_refs:
+            ref[:, at] = out[row : row + ref.shape[0]].astype(ref.dtype)
+            row += ref.shape[0]
 
 
 def tiles(width, ff):
@@ -204,7 +202,7 @@
         if parts:
             moves[i].wait()
         begin, end = i * width // max(parts, 1), (i + 1) * width // max(parts, 1)
-        second_half(h_ref, down_ref, w_ref, mine_ref, other_ref, tile, begin, end)
+        second_half(h_ref, down_ref, w_ref, [mine_ref, other_ref], tile, begin, end)
 
 
 def output(blocks, mine, experts, h, w_down, fetch):
@@ -229,11 +227,11 @@
 
 
 def expert_kernel(count, experts, tile_ff, tile_d, *refs):
-    blocks, (gate_ref, up_ref, down_ref, mine_ref, other_ref, x_ref, w_ref, h_ref) = refs[:count], refs[count:]
+    blocks, (gate_ref, up_ref, down_ref, mine_ref, first_ref, other_ref, x_ref, w_ref, h_ref) = refs[:count], refs[count:]
     gather_rows(blocks, x_ref)
     gather_weights(experts, blocks, x_ref.shape[1], w_ref)
     first_half(x_ref, gate_ref, up_ref, h_ref, tile_ff, 0, h_ref.shape[1])
-    second_half(h_ref, down_ref, w_ref, mine_ref, other_ref, tile_d, 0, x_ref.shape[1])
+    second_half(h_ref, down_ref, w_ref, [mine_ref, first_ref, other_ref], tile_d, 0, x_ref.shape[1])
 
 
 def expert(blocks, mine, experts, w_gate, w_up, w_down):
@@ -243,9 +241,13 @@
     here = pl.BlockSpec(memory_space=pltpu.VMEM)
     return pl.pallas_call(
         functools.partial(expert_kernel, count, experts, *tiles(width, ff)),
-        out_shape=[pltpu.VMEM((mine * rows, width), F32), pltpu.VMEM((total - mine * rows, width), BF16)],
+        out_shape=[
+            pltpu.VMEM((mine * rows, width), F32),
+            pltpu.VMEM((rows, width), BF16),
+            pltpu.VMEM((total - (mine + 1) * rows, width), BF16),
+        ],
         in_specs=[here] * (count + 3),
-        out_specs=[here] * 2,
+        out_specs=[here] * 3,
         scratch_shapes=[pltpu.VMEM((total, width), BF16), pltpu.VMEM((total, 1), F32), pltpu.VMEM((total, ff), BF16)],
         compiler_params=pltpu.CompilerParams(vmem_limit_bytes=SCRATCH),
         cost_estimate=pl.CostEstimate(
@@ -298,35 +300,29 @@
     mine, theirs = {}, {0: near_sent}
     for j, d in enumerate((0, 1, -1)):
         mine[d] = block(near_out[0], j)
-    rest_sent, late_sent = sibling(rest_out[1]), sibling(late_out[1])
+    mine[far], theirs[far] = block(late_out[0], 0), sibling(late_out[1])
+    end = (mine[far] + theirs[far].astype(F32)).astype(BF16)
+    late_sent, rest_sent, _ = together((sibling(late_out[2]), sibling(rest_out[1]), end))
     for j, d in enumerate(middle):
         mine[d] = block(rest_out[0], j)
     for j, d in enumerate([1, -1] + middle):
         theirs[d] = block(rest_sent, j)
-    for j, d in enumerate(late):
-        mine[d], theirs[d] = block(late_out[0], j), block(late_sent, j)
-
-    split = width // 256 * 128
-    spans = [slice(0, split), slice(split, width)] if split else [slice(0, width)]
-    both = lambda d, s: mine[d][:, s] + theirs[d][:, s].astype(F32)
-    ends = [both(far, s).astype(BF16) for s in spans]
-    flow = [(right(end[:cut]), left(end[cut:])) for end in ends]
-    added = None
+    for j, d in enumerate(late[1:]):
+        mine[d], theirs[d] = block(late_out[0], j + 1), block(late_sent, j)
+
+    both = lambda d: mine[d] + theirs[d].astype(F32)
+    a, b = right(end[:cut]), left(end[cut:])
     for d in range(far - 1, 0, -1):
-        for i, s in enumerate(spans):
-            a, b = flow[i]
-            if added is not None:
-                a, b, _ = together((a, b, added))
-            up, down = both(d, s), both(-d, s)
-            if d == far - 1:
-                up = jnp.concatenate([up[:cut] + a.astype(F32), up[cut:]], axis=0)
-                down = jnp.concatenate([down[:cut], down[cut:] + b.astype(F32)], axis=0)
-            else:
-                up, down = up + a.astype(F32), down + b.astype(F32)
-            added = up.astype(BF16), down.astype(BF16)
-            flow[i] = right(added[0]), left(added[1])
-    out = [both(0, s) + flow[i][0].astype(F32) + flow[i][1].astype(F32) for i, s in enumerate(spans)]
-    return jnp.concatenate([o.astype(BF16) for o in out], axis=1)
+        up = both(d)
+        up = jnp.concatenate([up[:cut] + a.astype(F32), up[cut:]], axis=0) if d == far - 1 else up + a.astype(F32)
+        up = up.astype(BF16)
+        b, _ = together((b, up))
+        down = both(-d)
+        down = jnp.concatenate([down[:cut], down[cut:] + b.astype(F32)], axis=0) if d == far - 1 else down + b.astype(F32)
+        down = down.astype(BF16)
+        a, _ = together((right(up), down))
+        b = left(down)
+    return (both(0) + a.astype(F32) + b.astype(F32)).astype(BF16)
 
 
 def solution(mesh):

time: 79.8 us -> 71.5 us (0.90)
  starting transfers between devices: 28.1 us -> 19.9 us
  waiting for transfers between devices: 23.9 us -> 28.4 us
  Pallas kernels: 25.9 us -> 21.5 us
    ppermute x12 -> x8, waiting for transfers between devices: 8.53 us -> 21.8 us  [local(): right = lambda a: lax.ppermute(a, 'node', forth)]
    ppermute x12 -> x8, waiting for transfers between devices: 13.7 us -> 5.79 us  [local(): left = lambda a: lax.ppermute(a, 'node', back)]
    ppermute x12 -> x8, starting transfers between devices: 19.4 us -> 14.8 us  [local(): right = lambda a: lax.ppermute(a, 'node', forth)]
    ppermute x12 -> x8, starting transfers between devices: 6.39 us -> 2.83 us  [local(): left = lambda a: lax.ppermute(a, 'node', back)]
    pallas_call x1, Pallas kernels: 6.57 us -> 4.59 us  [expert(): pl.pallas_call(functools.partial(expert_kernel, count, experts, *tiles(wi...]
    pallas_call x2, Pallas kernels: 6.4 us -> 5.16 us  [output(): pl.pallas_call(functools.partial(output_kernel, count, experts, tile, par...]
    pallas_call x2, Pallas kernels: 8.77 us -> 7.59 us  [hidden(): pl.pallas_call(functools.partial(hidden_kernel, count, tile, parts), out_...]
    ppermute x11 -> x12, waiting for transfers between devices: 1.66 us -> 0.76 us  [local(): sibling = lambda a: lax.ppermute(a, 'node', swap)]
  transfers between devices with their start and end apart: 35 -> 28, of which waited for: 17 -> 12; matrix products, arithmetic and copies ran while one was open for 1% -> 1% of each run, Pallas kernels for 23% -> 22%
where the time goes in v6:
time: 71.5 us; the launch traced here: 71.3 us
  waiting for transfers between devices  28.4 us (40%)
  Pallas kernels  21.5 us (30%)
  starting transfers between devices  19.9 us (28%)
  other arithmetic  1.28 us (2%)
    ppermute x8, waiting for transfers between devices, local(): right = lambda a: lax.ppermute(a, 'node', forth)  21.8 us
    ppermute x8, starting transfers between devices, local(): right = lambda a: lax.ppermute(a, 'node', forth)  14.8 us
    pallas_call x2, Pallas kernels, hidden(): pl.pallas_call(functools.partial(hidden_kernel, count, tile, parts), out_...  7.59 us
    ppermute x8, waiting for transfers between devices, local(): left = lambda a: lax.ppermute(a, 'node', back)  5.79 us
    pallas_call x2, Pallas kernels, output(): pl.pallas_call(functools.partial(output_kernel, count, experts, tile, par...  5.16 us
    pallas_call x1, Pallas kernels, expert(): pl.pallas_call(functools.partial(expert_kernel, count, experts, *tiles(wi...  4.59 us
    pallas_call x1, Pallas kernels, load(): pl.pallas_call(functools.partial(load_kernel, parts), out_shape=pltpu.VME...  3.17 us
    ppermute x8, starting transfers between devices, local(): left = lambda a: lax.ppermute(a, 'node', back)  2.83 us
  transfers between devices with their start and end apart: 28, of which 12 were waited for; matrix products, arithmetic and copies ran while one was open for 1% of the time, Pallas kernels for 22%

profile of v6, /device:TPU:0, one launch (start us, length us, event | category | flops | bytes accessed | tf_op | source)
XLA Modules:
  0.0 71.3 jit_solution(9616605465183273604)
XLA Ops:
  0.0 1.0 %shard_map.64.after.refs_0_ = bf16[32,3712]{1,0:T(8,128)(2,1)S(1)} custom-call(bf16[32,3584]{1,0:T(8,128)(2,1)} %tok_hbm.1, s32[8,32]{1,0:T(8,128)} %bitcast.2, f32[8,32]{1,0:T(8,128)} %bitcast.3), custom_call_target="tpu_custom_call" | custom-call | tf_op jit(solution)/shard_map/pallas_call | solution.py:61
  1.0 3.1 %collective-permute-start.2 = (bf16[32,3712]{1,0:T(8,128)(2,1)S(1)}, bf16[32,3712]{1,0:T(8,128)(2,1)S(1)}, u32[]{:S(2)}, u32[]{:S(2)}) collective-permute-start(bf16[32,3712]{1,0:T(8,128)(2,1)S(1)} %shard_map.64.after.refs_0_), channel_id=1, source_target_pairs={{0,4},{1,5},{4,8},{5,9},{8,12},{9,13},{12,14},{13,15},{14,10},{15,... | collective-permute-start | bytes 712712 | tf_op jit(solution)/shard_map/ppermute | solution.py:266
  4.1 3.2 %shard_map.65.refs_4_.refs_6_ = bf16[1,3584,1024]{2,1,0:T(8,128)(2,1)S(1)} custom-call(bf16[1,3584,1024]{2,1,0:T(8,128)(2,1)} %source.1, bf16[32,3712]{1,0:T(8,128)(2,1)S(1)} %shard_map.64.after.refs_0_), custom_call_target="tpu_custom_call" | custom-call | bytes 7340032 | tf_op jit(solution)/shard_map/pallas_call | solution.py:109
  7.3 2.5 %collective-permute-done.2.refs_2_ = bf16[32,3712]{1,0:T(8,128)(2,1)S(1)} collective-permute-done((bf16[32,3712]{1,0:T(8,128)(2,1)S(1)}, bf16[32,3712]{1,0:T(8,128)(2,1)S(1)}, u32[]{:S(2)}, u32[]{:S(2)}) %collective-permute-start.2) | collective-permute-done | bytes 237600 | tf_op jit(solution)/shard_map/ppermute | solution.py:266
  9.8 1.5 %collective-permute-done.1.refs_1_ = bf16[32,3712]{1,0:T(8,128)(2,1)S(1)} collective-permute-done((bf16[32,3712]{1,0:T(8,128)(2,1)S(1)}, bf16[32,3712]{1,0:T(8,128)(2,1)S(1)}, u32[]{:S(2)}, u32[]{:S(2)}) %collective-permute-start.1) | collective-permute-done | bytes 237600 | tf_op jit(solution)/shard_map/ppermute | solution.py:267
  11.3 0.3 collective-permute-start.5
  11.6 1.7 %collective-permute-start.6 = (bf16[32,3712]{1,0:T(8,128)(2,1)S(1)}, bf16[32,3712]{1,0:T(8,128)(2,1)S(1)}, u32[]{:S(2)}, u32[]{:S(2)}) collective-permute-start(bf16[32,3712]{1,0:T(8,128)(2,1)S(1)} %collective-permute-done.2.refs_2_), channel_id=1, source_target_pairs={{0,4},{1,5},{4,8},{5,9},{8,12},{9,13},{12,14},{13,15},{14,10},{15,... | collective-permute-start | bytes 712712 | tf_op jit(solution)/shard_map/ppermute | solution.py:266
  13.4 0.2 collective-permute-start.3
  13.6 4.5 %shard_map.66 = (bf16[128,1024]{1,0:T(8,128)(2,1)S(1)}, bf16[1,3584,1024]{2,1,0:T(8,128)(2,1)S(1)}) custom-call(bf16[32,3712]{1,0:T(8,128)(2,1)S(1)} %shard_map.64.after.refs_0_, bf16[32,3712]{1,0:T(8,128)(2,1)S(1)} %collective-permute-done.1.refs_1_, bf16[32,3712]{1,0:T(8,128)(2,1)S(1)} %collective-permute-done.2.refs_2_, ...), custom_call_target="tpu_custom_call" | custom-call | flops 3758096384 | tf_op jit(solution)/shard_map/pallas_call | solution.py:179
  18.1 1.7 %collective-permute-done.6.refs_1_ = bf16[32,3712]{1,0:T(8,128)(2,1)S(1)} collective-permute-done((bf16[32,3712]{1,0:T(8,128)(2,1)S(1)}, bf16[32,3712]{1,0:T(8,128)(2,1)S(1)}, u32[]{:S(2)}, u32[]{:S(2)}) %collective-permute-start.6) | collective-permute-done | bytes 237600 | tf_op jit(solution)/shard_map/ppermute | solution.py:266
  19.8 1.7 %collective-permute-start.10 = (bf16[32,3712]{1,0:T(8,128)(2,1)S(1)}, bf16[32,3712]{1,0:T(8,128)(2,1)S(1)}, u32[]{:S(2)}, u32[]{:S(2)}) collective-permute-start(bf16[32,3712]{1,0:T(8,128)(2,1)S(1)} %collective-permute-done.6.refs_1_), channel_id=1, source_target_pairs={{0,4},{1,5},{4,8},{5,9},{8,12},{9,13},{12,14},{13,15},{14,10},{15,... | collective-permute-start | bytes 712712 | tf_op jit(solution)/shard_map/ppermute | solution.py:266
  21.6 0.3 collective-permute-start.9
  21.8 0.2 collective-permute-start.8
  22.1 3.5 %shard_map.67 = (f32[96,3584]{1,0:T(8,128)S(1)}, bf16[32,3584]{1,0:T(8,128)(2,1)S(1)}, bf16[1,1024,3584]{2,1,0:T(8,128)(2,1)S(1)}) custom-call(bf16[32,3712]{1,0:T(8,128)(2,1)S(1)} %shard_map.64.after.refs_0_, bf16[32,3712]{1,0:T(8,128)(2,1)S(1)} %collective-permute-done.1.refs_1_, bf16[32,3712]{1,0:T(8,128)(2,1)S(1)} %collective-permute-done.2.refs_2_, ...), custom_call_target="tpu_custom_call" | custom-call | flops 1879048192 | tf_op jit(solution)/shard_map/pallas_call | solution.py:214
  25.6 1.6 %collective-permute-done.10.refs_2_ = bf16[32,3712]{1,0:T(8,128)(2,1)S(1)} collective-permute-done((bf16[32,3712]{1,0:T(8,128)(2,1)S(1)}, bf16[32,3712]{1,0:T(8,128)(2,1)S(1)}, u32[]{:S(2)}, u32[]{:S(2)}) %collective-permute-start.10) | collective-permute-done | bytes 237600 | tf_op jit(solution)/shard_map/ppermute | solution.py:266
  27.2 2.5 %collective-permute-done.9.refs_1_ = bf16[32,3712]{1,0:T(8,128)(2,1)S(1)} collective-permute-done((bf16[32,3712]{1,0:T(8,128)(2,1)S(1)}, bf16[32,3712]{1,0:T(8,128)(2,1)S(1)}, u32[]{:S(2)}, u32[]{:S(2)}) %collective-permute-start.9) | collective-permute-done | bytes 237600 | tf_op jit(solution)/shard_map/ppermute | solution.py:267
  29.8 0.1 collective-permute-start.13
  29.9 0.6 collective-permute-start.14
  30.4 0.3 collective-permute-start.12
  30.7 1.7 %collective-permute-start.11 = (bf16[16,3712]{1,0:T(8,128)(2,1)S(1)}, bf16[16,3712]{1,0:T(8,128)(2,1)S(1)}, u32[]{:S(2)}, u32[]{:S(2)}) collective-permute-start(bf16[16,3712]{1,0:T(8,128)(2,1)S(1)} %slice.69), channel_id=1, source_target_pairs={{0,4},{1,5},{4,8},{5,9},{8,12},{9,13},{12,14},{13,15},{14,10},{15,... | collective-permute-start | bytes 356360 | tf_op jit(solution)/shard_map/ppermute | solution.py:266
  32.4 3.1 %shard_map.68.refs_6_ = bf16[192,1024]{1,0:T(8,128)(2,1)S(1)} custom-call(bf16[32,3712]{1,0:T(8,128)(2,1)S(1)} %collective-permute-done.5.refs_0_, bf16[32,3712]{1,0:T(8,128)(2,1)S(1)} %collective-permute-done.6.refs_1_, bf16[32,3712]{1,0:T(8,128)(2,1)S(1)} %collective-permute-done.4.refs_2_, bf16[32,3712]{1,0:T(8,128)(2,1)S(1)} %collective-permute-done.3.refs_3_, ...), custom_call_target="tpu_custom_call" | custom-call | flops 3758096384 | tf_op jit(solution)/shard_map/pallas_call | solution.py:179
  35.6 0.2 collective-permute-done.11
  35.9 0.3 collective-permute-start.16
  36.2 1.6 %shard_map.69 = (f32[64,3584]{1,0:T(8,128)S(1)}, bf16[128,3584]{1,0:T(8,128)(2,1)S(1)}) custom-call(bf16[32,3712]{1,0:T(8,128)(2,1)S(1)} %collective-permute-done.5.refs_0_, bf16[32,3712]{1,0:T(8,128)(2,1)S(1)} %collective-permute-done.6.refs_1_, bf16[32,3712]{1,0:T(8,128)(2,1)S(1)} %collective-permute-done.4.refs_2_, ...), custom_call_target="tpu_custom_call" | custom-call | flops 1879048192 | tf_op jit(solution)/shard_map/pallas_call | solution.py:214
  37.9 4.6 %shard_map.70 = (f32[96,3584]{1,0:T(8,128)S(1)}, bf16[32,3584]{1,0:T(8,128)(2,1)S(1)}, bf16[64,3584]{1,0:T(8,128)(2,1)S(1)}) custom-call(bf16[32,3712]{1,0:T(8,128)(2,1)S(1)} %constant_dynamic-update-slice_fusion.refs_0_, bf16[32,3712]{1,0:T(8,128)(2,1)S(1)} %collective-permute-done.9.refs_1_, bf16[32,3712]{1,0:T(8,128)(2,1)S(1)} %collective-permute-done.10.refs_2_, ...), custom_call_target="tpu_custom_call" | custom-call | flops 5637144576 | tf_op jit(solution)/shard_map/pallas_call | solution.py:242
  42.5 0.3 collective-permute-start.19
  42.8 0.3 collective-permute-start.17
  43.1 0.2 collective-permute-start.18
  43.3 0.7 %collective-permute-done.19 = bf16[32,3584]{1,0:T(8,128)(2,1)S(1)} collective-permute-done((bf16[32,3584]{1,0:T(8,128)(2,1)S(1)}, bf16[32,3584]{1,0:T(8,128)(2,1)S(1)}, u32[]{:S(2)}, u32[]{:S(2)}) %collective-permute-start.19) | collective-permute-done | bytes 229408 | tf_op jit(solution)/shard_map/ppermute | solution.py:268
  44.1 1.6 %collective-permute-start.20 = (bf16[16,3584]{1,0:T(8,128)(2,1)S(1)}, bf16[16,3584]{1,0:T(8,128)(2,1)S(1)}, u32[]{:S(2)}, u32[]{:S(2)}) collective-permute-start(bf16[16,3584]{1,0:T(8,128)(2,1)S(1)} %get-tuple-element.95), channel_id=1, source_target_pairs={{0,4},{1,5},{4,8},{5,9},{8,12},{9,13},{12,14},{13,15},{14,10},{15,... | collective-permute-start | bytes 344072 | tf_op jit(solution)/shard_map/ppermute | solution.py:266
  45.7 0.4 collective-permute-start.22
  46.2 0.1 convert_add_fusion.1
  46.3 3.2 %collective-permute-done.20 = bf16[16,3584]{1,0:T(8,128)(2,1)S(1)} collective-permute-done((bf16[16,3584]{1,0:T(8,128)(2,1)S(1)}, bf16[16,3584]{1,0:T(8,128)(2,1)S(1)}, u32[]{:S(2)}, u32[]{:S(2)}) %collective-permute-start.20) | collective-permute-done | bytes 114720 | tf_op jit(solution)/shard_map/ppermute | solution.py:266
  49.5 1.6 %collective-permute-start.21 = (bf16[32,3584]{1,0:T(8,128)(2,1)S(1)}, bf16[32,3584]{1,0:T(8,128)(2,1)S(1)}, u32[]{:S(2)}, u32[]{:S(2)}) collective-permute-start(bf16[32,3584]{1,0:T(8,128)(2,1)S(1)} %pad_maximum_fusion), channel_id=1, source_target_pairs={{0,4},{1,5},{4,8},{5,9},{8,12},{9,13},{12,14},{13,15},{14,10},{15,... | collective-permute-start | bytes 688136 | tf_op jit(solution)/shard_map/ppermute | solution.py:266
  51.2 0.5 collective-permute-start.24
  51.7 4.8 %collective-permute-done.21 = bf16[32,3584]{1,0:T(8,128)(2,1)S(1)} collective-permute-done((bf16[32,3584]{1,0:T(8,128)(2,1)S(1)}, bf16[32,3584]{1,0:T(8,128)(2,1)S(1)}, u32[]{:S(2)}, u32[]{:S(2)}) %collective-permute-start.21) | collective-permute-done | bytes 229408 | tf_op jit(solution)/shard_map/ppermute | solution.py:266
  56.5 0.1 add_convert_fusion.4
  56.6 1.6 %collective-permute-start.23 = (bf16[32,3584]{1,0:T(8,128)(2,1)S(1)}, bf16[32,3584]{1,0:T(8,128)(2,1)S(1)}, u32[]{:S(2)}, u32[]{:S(2)}) collective-permute-start(bf16[32,3584]{1,0:T(8,128)(2,1)S(1)} %add_convert_fusion.4), channel_id=1, source_target_pairs={{0,4},{1,5},{4,8},{5,9},{8,12},{9,13},{12,14},{13,15},{14,10},{15,... | collective-permute-start | bytes 688136 | tf_op jit(solution)/shard_map/ppermute | solution.py:266
  58.2 0.1 add_convert_fusion.3
  58.3 0.5 collective-permute-start.26
  58.8 3.9 %collective-permute-done.23 = bf16[32,3584]{1,0:T(8,128)(2,1)S(1)} collective-permute-done((bf16[32,3584]{1,0:T(8,128)(2,1)S(1)}, bf16[32,3584]{1,0:T(8,128)(2,1)S(1)}, u32[]{:S(2)}, u32[]{:S(2)}) %collective-permute-start.23) | collective-permute-done | bytes 229408 | tf_op jit(solution)/shard_map/ppermute | solution.py:266
  62.7 0.1 add_convert_fusion.2
  62.7 1.6 %collective-permute-start.25 = (bf16[32,3584]{1,0:T(8,128)(2,1)S(1)}, bf16[32,3584]{1,0:T(8,128)(2,1)S(1)}, u32[]{:S(2)}, u32[]{:S(2)}) collective-permute-start(bf16[32,3584]{1,0:T(8,128)(2,1)S(1)} %add_convert_fusion.2), channel_id=1, source_target_pairs={{0,4},{1,5},{4,8},{5,9},{8,12},{9,13},{12,14},{13,15},{14,10},{15,... | collective-permute-start | bytes 688136 | tf_op jit(solution)/shard_map/ppermute | solution.py:266
  64.4 0.1 add_convert_fusion.1
  64.4 0.5 collective-permute-start.27
  64.9 3.9 %collective-permute-done.25 = bf16[32,3584]{1,0:T(8,128)(2,1)S(1)} collective-permute-done((bf16[32,3584]{1,0:T(8,128)(2,1)S(1)}, bf16[32,3584]{1,0:T(8,128)(2,1)S(1)}, u32[]{:S(2)}, u32[]{:S(2)}) %collective-permute-start.25) | collective-permute-done | bytes 229408 | tf_op jit(solution)/shard_map/ppermute | solution.py:266
  68.8 1.7 %collective-permute-done.27 = bf16[32,3584]{1,0:T(8,128)(2,1)S(1)} collective-permute-done((bf16[32,3584]{1,0:T(8,128)(2,1)S(1)}, bf16[32,3584]{1,0:T(8,128)(2,1)S(1)}, u32[]{:S(2)}, u32[]{:S(2)}) %collective-permute-start.27) | collective-permute-done | bytes 229408 | tf_op jit(solution)/shard_map/ppermute | solution.py:267
  70.5 0.8 %add_convert_fusion = bf16[32,3584]{1,0:T(8,128)(2,1)} fusion(bf16[32,3584]{1,0:T(8,128)(2,1)S(1)} %collective-permute-done.27, bf16[32,3584]{1,0:T(8,128)(2,1)S(1)} %collective-permute-done.25, bf16[32,3584]{1,0:T(8,128)(2,1)S(1)} %collective-permute-done.15, f32[96,3584]{1,0:T(8,128)S(1)} %get-tuple-element.61), kind=kLoop, calls=%fused_computation | loop fusion | flops 802816 | bytes 1376256 | tf_op jit(solution)/shard_map/convert_element_type | solution.py:325
  (33 shorter events, 0.3 us)
Async XLA Ops:
  1.0 8.8 %collective-permute-start.2 = (bf16[32,3712]{1,0:T(8,128)(2,1)S(1)}, bf16[32,3712]{1,0:T(8,128)(2,1)S(1)}, u32[]{:S(2)}, u32[]{:S(2)}) collective-permute-start(bf16[32,3712]{1,0:T(8,128)(2,1)S(1)} %shard_map.64.after.refs_0_), channel_id=1, source_target_pairs={{0,4},{1,5},{4,8},{5,9},{8,12},{9,13},{12,14},{13,15},{14,10},{15,... | collective-permute-start | bytes 712712 | tf_op jit(solution)/shard_map/ppermute | solution.py:266
  4.1 7.2 %collective-permute-start.1 = (bf16[32,3712]{1,0:T(8,128)(2,1)S(1)}, bf16[32,3712]{1,0:T(8,128)(2,1)S(1)}, u32[]{:S(2)}, u32[]{:S(2)}) collective-permute-start(bf16[32,3712]{1,0:T(8,128)(2,1)S(1)} %shard_map.64.after.refs_0_), channel_id=1, source_target_pairs={{4,0},{5,1},{8,4},{9,5},{12,8},{13,9},{14,12},{15,13},{10,14},{11,... | collective-permute-start | bytes 712712 | tf_op jit(solution)/shard_map/ppermute | solution.py:267
  4.1 7.2 %collective-permute-start = (bf16[32,3712]{1,0:T(8,128)(2,1)S(1)}, bf16[32,3712]{1,0:T(8,128)(2,1)S(1)}, u32[]{:S(2)}, u32[]{:S(2)}) collective-permute-start(bf16[32,3712]{1,0:T(8,128)(2,1)S(1)} %shard_map.64.after.refs_0_), channel_id=1, source_target_pairs={{0,1},{1,0},{2,3},{3,2},{4,5},{5,4},{6,7},{7,6},{8,9},{9,8},{10,11... | collective-permute-start | bytes 712712 | tf_op jit(solution)/shard_map/ppermute | solution.py:268
  11.3 6.7 %collective-permute-start.5 = (bf16[32,3712]{1,0:T(8,128)(2,1)S(1)}, bf16[32,3712]{1,0:T(8,128)(2,1)S(1)}, u32[]{:S(2)}, u32[]{:S(2)}) collective-permute-start(bf16[32,3712]{1,0:T(8,128)(2,1)S(1)} %collective-permute-done.1.refs_1_), channel_id=1, source_target_pairs={{4,0},{5,1},{8,4},{9,5},{12,8},{13,9},{14,12},{15,13},{10,14},{11,... | collective-permute-start | bytes 712712 | tf_op jit(solution)/shard_map/ppermute | solution.py:267
  11.6 6.5 %collective-permute-start.4 = (bf16[32,3712]{1,0:T(8,128)(2,1)S(1)}, bf16[32,3712]{1,0:T(8,128)(2,1)S(1)}, u32[]{:S(2)}, u32[]{:S(2)}) collective-permute-start(bf16[32,3712]{1,0:T(8,128)(2,1)S(1)} %collective-permute-done.1.refs_1_), channel_id=1, source_target_pairs={{0,1},{1,0},{2,3},{3,2},{4,5},{5,4},{6,7},{7,6},{8,9},{9,8},{10,11... | collective-permute-start | bytes 712712 | tf_op jit(solution)/shard_map/ppermute | solution.py:268
  11.6 8.2 %collective-permute-start.6 = (bf16[32,3712]{1,0:T(8,128)(2,1)S(1)}, bf16[32,3712]{1,0:T(8,128)(2,1)S(1)}, u32[]{:S(2)}, u32[]{:S(2)}) collective-permute-start(bf16[32,3712]{1,0:T(8,128)(2,1)S(1)} %collective-permute-done.2.refs_2_), channel_id=1, source_target_pairs={{0,4},{1,5},{4,8},{5,9},{8,12},{9,13},{12,14},{13,15},{14,10},{15,... | collective-permute-start | bytes 712712 | tf_op jit(solution)/shard_map/ppermute | solution.py:266
  13.4 6.5 %collective-permute-start.3 = (bf16[32,3712]{1,0:T(8,128)(2,1)S(1)}, bf16[32,3712]{1,0:T(8,128)(2,1)S(1)}, u32[]{:S(2)}, u32[]{:S(2)}) collective-permute-start(bf16[32,3712]{1,0:T(8,128)(2,1)S(1)} %collective-permute-done.2.refs_2_), channel_id=1, source_target_pairs={{0,1},{1,0},{2,3},{3,2},{4,5},{5,4},{6,7},{7,6},{8,9},{9,8},{10,11... | collective-permute-start | bytes 712712 | tf_op jit(solution)/shard_map/ppermute | solution.py:268
  19.8 7.4 %collective-permute-start.10 = (bf16[32,3712]{1,0:T(8,128)(2,1)S(1)}, bf16[32,3712]{1,0:T(8,128)(2,1)S(1)}, u32[]{:S(2)}, u32[]{:S(2)}) collective-permute-start(bf16[32,3712]{1,0:T(8,128)(2,1)S(1)} %collective-permute-done.6.refs_1_), channel_id=1, source_target_pairs={{0,4},{1,5},{4,8},{5,9},{8,12},{9,13},{12,14},{13,15},{14,10},{15,... | collective-permute-start | bytes 712712 | tf_op jit(solution)/shard_map/ppermute | solution.py:266
  21.6 5.7 %collective-permute-start.7 = (bf16[32,3712]{1,0:T(8,128)(2,1)S(1)}, bf16[32,3712]{1,0:T(8,128)(2,1)S(1)}, u32[]{:S(2)}, u32[]{:S(2)}) collective-permute-start(bf16[32,3712]{1,0:T(8,128)(2,1)S(1)} %collective-permute-done.6.refs_1_), channel_id=1, source_target_pairs={{0,1},{1,0},{2,3},{3,2},{4,5},{5,4},{6,7},{7,6},{8,9},{9,8},{10,11... | collective-permute-start | bytes 712712 | tf_op jit(solution)/shard_map/ppermute | solution.py:268
  21.6 8.2 %collective-permute-start.9 = (bf16[32,3712]{1,0:T(8,128)(2,1)S(1)}, bf16[32,3712]{1,0:T(8,128)(2,1)S(1)}, u32[]{:S(2)}, u32[]{:S(2)}) collective-permute-start(bf16[32,3712]{1,0:T(8,128)(2,1)S(1)} %collective-permute-done.5.refs_0_), channel_id=1, source_target_pairs={{4,0},{5,1},{8,4},{9,5},{12,8},{13,9},{14,12},{15,13},{10,14},{11,... | collective-permute-start | bytes 712712 | tf_op jit(solution)/shard_map/ppermute | solution.py:267
  21.8 7.9 %collective-permute-start.8 = (bf16[32,3712]{1,0:T(8,128)(2,1)S(1)}, bf16[32,3712]{1,0:T(8,128)(2,1)S(1)}, u32[]{:S(2)}, u32[]{:S(2)}) collective-permute-start(bf16[32,3712]{1,0:T(8,128)(2,1)S(1)} %collective-permute-done.5.refs_0_), channel_id=1, source_target_pairs={{0,1},{1,0},{2,3},{3,2},{4,5},{5,4},{6,7},{7,6},{8,9},{9,8},{10,11... | collective-permute-start | bytes 712712 | tf_op jit(solution)/shard_map/ppermute | solution.py:268
  29.8 6.1 %collective-permute-start.13 = (bf16[32,3712]{1,0:T(8,128)(2,1)S(1)}, bf16[32,3712]{1,0:T(8,128)(2,1)S(1)}, u32[]{:S(2)}, u32[]{:S(2)}) collective-permute-start(bf16[32,3712]{1,0:T(8,128)(2,1)S(1)} %collective-permute-done.10.refs_2_), channel_id=1, source_target_pairs={{0,1},{1,0},{2,3},{3,2},{4,5},{5,4},{6,7},{7,6},{8,9},{9,8},{10,11... | collective-permute-start | bytes 712712 | tf_op jit(solution)/shard_map/ppermute | solution.py:268
  29.9 6.0 %collective-permute-start.14 = (bf16[32,3712]{1,0:T(8,128)(2,1)S(1)}, bf16[32,3712]{1,0:T(8,128)(2,1)S(1)}, u32[]{:S(2)}, u32[]{:S(2)}) collective-permute-start(bf16[32,3712]{1,0:T(8,128)(2,1)S(1)} %collective-permute-done.9.refs_1_), channel_id=1, source_target_pairs={{0,1},{1,0},{2,3},{3,2},{4,5},{5,4},{6,7},{7,6},{8,9},{9,8},{10,11... | collective-permute-start | bytes 712712 | tf_op jit(solution)/shard_map/ppermute | solution.py:268
  30.4 5.2 %collective-permute-start.12 = (bf16[16,3712]{1,0:T(8,128)(2,1)S(1)}, bf16[16,3712]{1,0:T(8,128)(2,1)S(1)}, u32[]{:S(2)}, u32[]{:S(2)}) collective-permute-start(bf16[16,3712]{1,0:T(8,128)(2,1)S(1)} %slice.70), channel_id=1, source_target_pairs={{4,0},{5,1},{8,4},{9,5},{12,8},{13,9},{14,12},{15,13},{10,14},{11,... | collective-permute-start | bytes 356360 | tf_op jit(solution)/shard_map/ppermute | solution.py:267
  30.7 5.2 %collective-permute-start.11 = (bf16[16,3712]{1,0:T(8,128)(2,1)S(1)}, bf16[16,3712]{1,0:T(8,128)(2,1)S(1)}, u32[]{:S(2)}, u32[]{:S(2)}) collective-permute-start(bf16[16,3712]{1,0:T(8,128)(2,1)S(1)} %slice.69), channel_id=1, source_target_pairs={{0,4},{1,5},{4,8},{5,9},{8,12},{9,13},{12,14},{13,15},{14,10},{15,... | collective-permute-start | bytes 356360 | tf_op jit(solution)/shard_map/ppermute | solution.py:266
  32.4 3.4 %collective-permute-start.15 = (bf16[32,3584]{1,0:T(8,128)(2,1)S(1)}, bf16[32,3584]{1,0:T(8,128)(2,1)S(1)}, u32[]{:S(2)}, u32[]{:S(2)}) collective-permute-start(bf16[32,3584]{1,0:T(8,128)(2,1)S(1)} %get-tuple-element.69), channel_id=1, source_target_pairs={{0,1},{1,0},{2,3},{3,2},{4,5},{5,4},{6,7},{7,6},{8,9},{9,8},{10,11... | collective-permute-start | bytes 688136 | tf_op jit(solution)/shard_map/ppermute | solution.py:268
  35.9 2.0 %collective-permute-start.16 = (bf16[32,3712]{1,0:T(8,128)(2,1)S(1)}, bf16[32,3712]{1,0:T(8,128)(2,1)S(1)}, u32[]{:S(2)}, u32[]{:S(2)}) collective-permute-start(bf16[32,3712]{1,0:T(8,128)(2,1)S(1)} %constant_dynamic-update-slice_fusion.refs_0_), channel_id=1, source_target_pairs={{0,1},{1,0},{2,3},{3,2},{4,5},{5,4},{6,7},{7,6},{8,9},{9,8},{10,11... | collective-permute-start | bytes 712712 | tf_op jit(solution)/shard_map/ppermute | solution.py:268
  42.5 1.6 %collective-permute-start.19 = (bf16[32,3584]{1,0:T(8,128)(2,1)S(1)}, bf16[32,3584]{1,0:T(8,128)(2,1)S(1)}, u32[]{:S(2)}, u32[]{:S(2)}) collective-permute-start(bf16[32,3584]{1,0:T(8,128)(2,1)S(1)} %get-tuple-element.83), channel_id=1, source_target_pairs={{0,1},{1,0},{2,3},{3,2},{4,5},{5,4},{6,7},{7,6},{8,9},{9,8},{10,11... | collective-permute-start | bytes 688136 | tf_op jit(solution)/shard_map/ppermute | solution.py:268
  42.8 3.4 %collective-permute-start.17 = (bf16[64,3584]{1,0:T(8,128)(2,1)S(1)}, bf16[64,3584]{1,0:T(8,128)(2,1)S(1)}, u32[]{:S(2)}, u32[]{:S(2)}) collective-permute-start(bf16[64,3584]{1,0:T(8,128)(2,1)S(1)} %get-tuple-element.80), channel_id=1, source_target_pairs={{0,1},{1,0},{2,3},{3,2},{4,5},{5,4},{6,7},{7,6},{8,9},{9,8},{10,11... | collective-permute-start | bytes 1376264 | tf_op jit(solution)/shard_map/ppermute | solution.py:268
  43.1 3.1 %collective-permute-start.18 = (bf16[128,3584]{1,0:T(8,128)(2,1)S(1)}, bf16[128,3584]{1,0:T(8,128)(2,1)S(1)}, u32[]{:S(2)}, u32[]{:S(2)}) collective-permute-start(bf16[128,3584]{1,0:T(8,128)(2,1)S(1)} %get-tuple-element.81), channel_id=1, source_target_pairs={{0,1},{1,0},{2,3},{3,2},{4,5},{5,4},{6,7},{7,6},{8,9},{9,8},{10,11... | collective-permute-start | bytes 2752520 | tf_op jit(solution)/shard_map/ppermute | solution.py:268
  44.1 5.4 %collective-permute-start.20 = (bf16[16,3584]{1,0:T(8,128)(2,1)S(1)}, bf16[16,3584]{1,0:T(8,128)(2,1)S(1)}, u32[]{:S(2)}, u32[]{:S(2)}) collective-permute-start(bf16[16,3584]{1,0:T(8,128)(2,1)S(1)} %get-tuple-element.95), channel_id=1, source_target_pairs={{0,4},{1,5},{4,8},{5,9},{8,12},{9,13},{12,14},{13,15},{14,10},{15,... | collective-permute-start | bytes 344072 | tf_op jit(solution)/shard_map/ppermute | solution.py:266
  45.7 5.4 %collective-permute-start.22 = (bf16[16,3584]{1,0:T(8,128)(2,1)S(1)}, bf16[16,3584]{1,0:T(8,128)(2,1)S(1)}, u32[]{:S(2)}, u32[]{:S(2)}) collective-permute-start(bf16[16,3584]{1,0:T(8,128)(2,1)S(1)} %get-tuple-element.96), channel_id=1, source_target_pairs={{4,0},{5,1},{8,4},{9,5},{12,8},{13,9},{14,12},{15,13},{10,14},{11,... | collective-permute-start | bytes 344072 | tf_op jit(solution)/shard_map/ppermute | solution.py:267
  49.5 7.0 %collective-permute-start.21 = (bf16[32,3584]{1,0:T(8,128)(2,1)S(1)}, bf16[32,3584]{1,0:T(8,128)(2,1)S(1)}, u32[]{:S(2)}, u32[]{:S(2)}) collective-permute-start(bf16[32,3584]{1,0:T(8,128)(2,1)S(1)} %pad_maximum_fusion), channel_id=1, source_target_pairs={{0,4},{1,5},{4,8},{5,9},{8,12},{9,13},{12,14},{13,15},{14,10},{15,... | collective-permute-start | bytes 688136 | tf_op jit(solution)/shard_map/ppermute | solution.py:266
  51.2 7.0 %collective-permute-start.24 = (bf16[32,3584]{1,0:T(8,128)(2,1)S(1)}, bf16[32,3584]{1,0:T(8,128)(2,1)S(1)}, u32[]{:S(2)}, u32[]{:S(2)}) collective-permute-start(bf16[32,3584]{1,0:T(8,128)(2,1)S(1)} %pad_maximum_fusion.1), channel_id=1, source_target_pairs={{4,0},{5,1},{8,4},{9,5},{12,8},{13,9},{14,12},{15,13},{10,14},{11,... | collective-permute-start | bytes 688136 | tf_op jit(solution)/shard_map/ppermute | solution.py:267
  56.6 6.1 %collective-permute-start.23 = (bf16[32,3584]{1,0:T(8,128)(2,1)S(1)}, bf16[32,3584]{1,0:T(8,128)(2,1)S(1)}, u32[]{:S(2)}, u32[]{:S(2)}) collective-permute-start(bf16[32,3584]{1,0:T(8,128)(2,1)S(1)} %add_convert_fusion.4), channel_id=1, source_target_pairs={{0,4},{1,5},{4,8},{5,9},{8,12},{9,13},{12,14},{13,15},{14,10},{15,... | collective-permute-start | bytes 688136 | tf_op jit(solution)/shard_map/ppermute | solution.py:266
  58.3 6.1 %collective-permute-start.26 = (bf16[32,3584]{1,0:T(8,128)(2,1)S(1)}, bf16[32,3584]{1,0:T(8,128)(2,1)S(1)}, u32[]{:S(2)}, u32[]{:S(2)}) collective-permute-start(bf16[32,3584]{1,0:T(8,128)(2,1)S(1)} %add_convert_fusion.3), channel_id=1, source_target_pairs={{4,0},{5,1},{8,4},{9,5},{12,8},{13,9},{14,12},{15,13},{10,14},{11,... | collective-permute-start | bytes 688136 | tf_op jit(solution)/shard_map/ppermute | solution.py:267
  62.7 6.1 %collective-permute-start.25 = (bf16[32,3584]{1,0:T(8,128)(2,1)S(1)}, bf16[32,3584]{1,0:T(8,128)(2,1)S(1)}, u32[]{:S(2)}, u32[]{:S(2)}) collective-permute-start(bf16[32,3584]{1,0:T(8,128)(2,1)S(1)} %add_convert_fusion.2), channel_id=1, source_target_pairs={{0,4},{1,5},{4,8},{5,9},{8,12},{9,13},{12,14},{13,15},{14,10},{15,... | collective-permute-start | bytes 688136 | tf_op jit(solution)/shard_map/ppermute | solution.py:266
  64.4 6.1 %collective-permute-start.27 = (bf16[32,3584]{1,0:T(8,128)(2,1)S(1)}, bf16[32,3584]{1,0:T(8,128)(2,1)S(1)}, u32[]{:S(2)}, u32[]{:S(2)}) collective-permute-start(bf16[32,3584]{1,0:T(8,128)(2,1)S(1)} %add_convert_fusion.1), channel_id=1, source_target_pairs={{4,0},{5,1},{8,4},{9,5},{12,8},{13,9},{14,12},{15,13},{10,14},{11,... | collective-permute-start | bytes 688136 | tf_op jit(solution)/shard_map/ppermute | solution.py:267

commit v7 on v6

--- a/solution.py
+++ b/solution.py
@@ -273,27 +273,51 @@
     got, twin = {0: own}, {}
     middle = [s * d for d in range(2, far - 1) for s in (1, -1)]
     late = [far, far - 1, 1 - far]
+    exchanged = {}
     for d in range(1, far):
         a, b = left(got[d - 1]), right(got[1 - d])
-        new = {e: sibling(got[e]) for e in {d - 1, 1 - d}}
         if d == 1:
-            w_gate, new, a, b = together((load(w_gate, own), new, a, b))
+            done = (load(w_gate, own),)
         elif d == 2:
             near = [got[0], got[1], got[-1], twin[0]]
-            (h_near, w_up), new, a, b = together((hidden(near, w_gate, w_up, True), new, a, b))
+            done = hidden(near, w_gate, w_up, True)
         elif d == 3:
-            (*near_out, w_down), new, a, b = together((output(near, 3, experts, h_near, w_down, True), new, a, b))
+            done = output(near, 3, experts, h_near, w_down, True)
         else:
-            new, a, b = together((new, a, b))
+            done = None
+        ready, done = together(({e: got[e] for e in {d - 1, 1 - d}}, done))
+        started = {e: sibling(ready[e]) for e in ready}
+        if d == 1:
+            a, b, (w_gate,), started = together((a, b, done, started))
+            twin.update(started)
+            started = {}
+        else:
+            a, b, done, exchanged = together((a, b, done, exchanged))
+        if d == 2:
+            h_near, w_up = done
+        if d == 3:
+            *near_out, w_down = done
+        twin.update(exchanged)
+        exchanged = started
         got[d], got[-d] = a, b
-        twin.update(new)
     ends = right(got[1 - far][:cut]), left(got[far - 1][cut:])
-    new = {e: sibling(got[e]) for e in (far - 1, 1 - far)}
+    exchanged = together(exchanged)
+    twin.update(exchanged)
     rest = [got[d] for d in middle] + [twin[1], twin[-1]] + [twin[d] for d in middle]
-    (h_rest,), ends, new, near_sent = together((hidden(rest, w_gate, w_up, False), ends, new, sibling(near_out[1])))
-    twin.update(new)
+    (h_rest,) = hidden(rest, w_gate, w_up, False)
+    ready, h_rest = together(({e: got[e] for e in (far - 1, 1 - far)}, h_rest))
+    exchanged = {e: sibling(ready[e]) for e in ready}
+    ends, h_rest = together((ends, h_rest))
     got[far] = jnp.concatenate(ends, axis=0)
-    rest_out, twin[far] = together((output(rest, len(middle), experts, h_rest, w_down, False), sibling(got[far])))
+    rest_out, twin[far], exchanged, near_sent = together(
+        (
+            output(rest, len(middle), experts, h_rest, w_down, False),
+            sibling(got[far]),
+            exchanged,
+            sibling(near_out[1]),
+        )
+    )
+    twin.update(exchanged)
     late_out = expert([got[d] for d in late] + [twin[d] for d in late], len(late), experts, w_gate, w_up, w_down)
 
     block = lambda a, j: a[j * rows : (j + 1) * rows]

time: 71.5 us -> 67.8 us (0.948)
  waiting for transfers between devices: 28.4 us -> 23.8 us
  starting transfers between devices: 19.9 us -> 20.7 us
    ppermute x8, starting transfers between devices: 2.83 us -> 7.8 us  [local(): left = lambda a: lax.ppermute(a, 'node', back)]
    ppermute x8, starting transfers between devices: 14.8 us -> 9.89 us  [local(): right = lambda a: lax.ppermute(a, 'node', forth)]
    ppermute x8, waiting for transfers between devices: 21.8 us -> 18.7 us  [local(): right = lambda a: lax.ppermute(a, 'node', forth)]
    ppermute x8, waiting for transfers between devices: 5.79 us -> 4.26 us  [local(): left = lambda a: lax.ppermute(a, 'node', back)]
    ppermute x12, starting transfers between devices: 2.24 us -> 2.99 us  [local(): sibling = lambda a: lax.ppermute(a, 'node', swap)]
  transfers between devices with their start and end apart: 28 -> 28, of which waited for: 12 -> 11; matrix products, arithmetic and copies ran while one was open for 1% -> 1% of each run, Pallas kernels for 22% -> 24%
where the time goes in v7:
time: 67.8 us; the launch traced here: 67.7 us
  waiting for transfers between devices  23.8 us (35%)
  Pallas kernels  21.5 us (32%)
  starting transfers between devices  20.7 us (31%)
  other arithmetic  1.28 us (2%)
    ppermute x8, waiting for transfers between devices, local(): right = lambda a: lax.ppermute(a, 'node', forth)  18.7 us
    ppermute x8, starting transfers between devices, local(): right = lambda a: lax.ppermute(a, 'node', forth)  9.89 us
    ppermute x8, starting transfers between devices, local(): left = lambda a: lax.ppermute(a, 'node', back)  7.8 us
    pallas_call x2, Pallas kernels, hidden(): pl.pallas_call(functools.partial(hidden_kernel, count, tile, parts), out_...  7.61 us
    pallas_call x2, Pallas kernels, output(): pl.pallas_call(functools.partial(output_kernel, count, experts, tile, par...  5.16 us
    pallas_call x1, Pallas kernels, expert(): pl.pallas_call(functools.partial(expert_kernel, count, experts, *tiles(wi...  4.58 us
    ppermute x8, waiting for transfers between devices, local(): left = lambda a: lax.ppermute(a, 'node', back)  4.26 us
    pallas_call x1, Pallas kernels, load(): pl.pallas_call(functools.partial(load_kernel, parts), out_shape=pltpu.VME...  3.17 us
  transfers between devices with their start and end apart: 28, of which 11 were waited for; matrix products, arithmetic and copies ran while one was open for 1% of the time, Pallas kernels for 24%

profile of v7, /device:TPU:0, one launch (start us, length us, event | category | flops | bytes accessed | tf_op | source)
XLA Modules:
  0.0 67.7 jit_solution(4115648434426870852)
XLA Ops:
  0.0 1.0 %shard_map.64.after.refs_0_ = bf16[32,3712]{1,0:T(8,128)(2,1)S(1)} custom-call(bf16[32,3584]{1,0:T(8,128)(2,1)} %tok_hbm.1, s32[8,32]{1,0:T(8,128)} %bitcast.2, f32[8,32]{1,0:T(8,128)} %bitcast.3), custom_call_target="tpu_custom_call" | custom-call | tf_op jit(solution)/shard_map/pallas_call | solution.py:61
  1.0 3.1 %collective-permute-start.1 = (bf16[32,3712]{1,0:T(8,128)(2,1)S(1)}, bf16[32,3712]{1,0:T(8,128)(2,1)S(1)}, u32[]{:S(2)}, u32[]{:S(2)}) collective-permute-start(bf16[32,3712]{1,0:T(8,128)(2,1)S(1)} %shard_map.64.after.refs_0_), channel_id=1, source_target_pairs={{0,4},{1,5},{4,8},{5,9},{8,12},{9,13},{12,14},{13,15},{14,10},{15,... | collective-permute-start | bytes 712712 | tf_op jit(solution)/shard_map/ppermute | solution.py:266
  4.1 3.2 %shard_map.65.refs_4_.refs_6_ = bf16[1,3584,1024]{2,1,0:T(8,128)(2,1)S(1)} custom-call(bf16[1,3584,1024]{2,1,0:T(8,128)(2,1)} %source.1, bf16[32,3712]{1,0:T(8,128)(2,1)S(1)} %shard_map.64.after.refs_0_), custom_call_target="tpu_custom_call" | custom-call | bytes 7340032 | tf_op jit(solution)/shard_map/pallas_call | solution.py:109
  7.3 0.1 collective-permute-start.2
  7.3 2.5 %collective-permute-done.1.refs_2_ = bf16[32,3712]{1,0:T(8,128)(2,1)S(1)} collective-permute-done((bf16[32,3712]{1,0:T(8,128)(2,1)S(1)}, bf16[32,3712]{1,0:T(8,128)(2,1)S(1)}, u32[]{:S(2)}, u32[]{:S(2)}) %collective-permute-start.1) | collective-permute-done | bytes 237600 | tf_op jit(solution)/shard_map/ppermute | solution.py:266
  9.8 1.5 %collective-permute-done.refs_1_ = bf16[32,3712]{1,0:T(8,128)(2,1)S(1)} collective-permute-done((bf16[32,3712]{1,0:T(8,128)(2,1)S(1)}, bf16[32,3712]{1,0:T(8,128)(2,1)S(1)}, u32[]{:S(2)}, u32[]{:S(2)}) %collective-permute-start) | collective-permute-done | bytes 237600 | tf_op jit(solution)/shard_map/ppermute | solution.py:267
  11.3 0.3 collective-permute-start.3
  11.6 1.7 %collective-permute-start.4 = (bf16[32,3712]{1,0:T(8,128)(2,1)S(1)}, bf16[32,3712]{1,0:T(8,128)(2,1)S(1)}, u32[]{:S(2)}, u32[]{:S(2)}) collective-permute-start(bf16[32,3712]{1,0:T(8,128)(2,1)S(1)} %collective-permute-done.1.refs_2_), channel_id=1, source_target_pairs={{0,4},{1,5},{4,8},{5,9},{8,12},{9,13},{12,14},{13,15},{14,10},{15,... | collective-permute-start | bytes 712712 | tf_op jit(solution)/shard_map/ppermute | solution.py:266
  13.4 4.5 %shard_map.66 = (bf16[128,1024]{1,0:T(8,128)(2,1)S(1)}, bf16[1,3584,1024]{2,1,0:T(8,128)(2,1)S(1)}) custom-call(bf16[32,3712]{1,0:T(8,128)(2,1)S(1)} %shard_map.64.after.refs_0_, bf16[32,3712]{1,0:T(8,128)(2,1)S(1)} %collective-permute-done.refs_1_, bf16[32,3712]{1,0:T(8,128)(2,1)S(1)} %collective-permute-done.1.refs_2_, ...), custom_call_target="tpu_custom_call" | custom-call | flops 3758096384 | tf_op jit(solution)/shard_map/pallas_call | solution.py:179
  17.8 0.1 collective-permute-start.7
  17.9 0.5 collective-permute-start.8
  18.4 1.5 %collective-permute-start.5 = (bf16[32,3712]{1,0:T(8,128)(2,1)S(1)}, bf16[32,3712]{1,0:T(8,128)(2,1)S(1)}, u32[]{:S(2)}, u32[]{:S(2)}) collective-permute-start(bf16[32,3712]{1,0:T(8,128)(2,1)S(1)} %collective-permute-done.3.refs_0_), channel_id=1, source_target_pairs={{4,0},{5,1},{8,4},{9,5},{12,8},{13,9},{14,12},{15,13},{10,14},{11,... | collective-permute-start | bytes 712712 | tf_op jit(solution)/shard_map/ppermute | solution.py:267
  19.9 0.5 collective-permute-start.6
  20.4 3.5 %shard_map.67 = (f32[96,3584]{1,0:T(8,128)S(1)}, bf16[32,3584]{1,0:T(8,128)(2,1)S(1)}, bf16[1,1024,3584]{2,1,0:T(8,128)(2,1)S(1)}) custom-call(bf16[32,3712]{1,0:T(8,128)(2,1)S(1)} %shard_map.64.after.refs_0_, bf16[32,3712]{1,0:T(8,128)(2,1)S(1)} %collective-permute-done.refs_1_, bf16[32,3712]{1,0:T(8,128)(2,1)S(1)} %collective-permute-done.1.refs_2_, ...), custom_call_target="tpu_custom_call" | custom-call | flops 1879048192 | tf_op jit(solution)/shard_map/pallas_call | solution.py:214
  24.0 0.1 collective-permute-start.9
  24.1 0.5 collective-permute-start.10
  24.6 1.6 %collective-permute-done.5.refs_1_ = bf16[32,3712]{1,0:T(8,128)(2,1)S(1)} collective-permute-done((bf16[32,3712]{1,0:T(8,128)(2,1)S(1)}, bf16[32,3712]{1,0:T(8,128)(2,1)S(1)}, u32[]{:S(2)}, u32[]{:S(2)}) %collective-permute-start.5) | collective-permute-done | bytes 237600 | tf_op jit(solution)/shard_map/ppermute | solution.py:267
  26.3 1.7 %collective-permute-start.12 = (bf16[16,3712]{1,0:T(8,128)(2,1)S(1)}, bf16[16,3712]{1,0:T(8,128)(2,1)S(1)}, u32[]{:S(2)}, u32[]{:S(2)}) collective-permute-start(bf16[16,3712]{1,0:T(8,128)(2,1)S(1)} %slice.70), channel_id=1, source_target_pairs={{4,0},{5,1},{8,4},{9,5},{12,8},{13,9},{14,12},{15,13},{10,14},{11,... | collective-permute-start | bytes 356360 | tf_op jit(solution)/shard_map/ppermute | solution.py:267
  27.9 0.4 collective-permute-start.11
  28.3 3.1 %shard_map.68.refs_6_ = bf16[192,1024]{1,0:T(8,128)(2,1)S(1)} custom-call(bf16[32,3712]{1,0:T(8,128)(2,1)S(1)} %collective-permute-done.3.refs_0_, bf16[32,3712]{1,0:T(8,128)(2,1)S(1)} %collective-permute-done.4.refs_1_, bf16[32,3712]{1,0:T(8,128)(2,1)S(1)} %collective-permute-done.8.refs_2_, bf16[32,3712]{1,0:T(8,128)(2,1)S(1)} %collective-permute-done.7.refs_3_, ...), custom_call_target="tpu_custom_call" | custom-call | flops 3758096384 | tf_op jit(solution)/shard_map/pallas_call | solution.py:179
  31.5 0.1 collective-permute-start.14
  31.6 0.5 collective-permute-start.15
  32.1 0.7 %collective-permute-done.11 = bf16[16,3712]{1,0:T(8,128)(2,1)S(1)} collective-permute-done((bf16[16,3712]{1,0:T(8,128)(2,1)S(1)}, bf16[16,3712]{1,0:T(8,128)(2,1)S(1)}, u32[]{:S(2)}, u32[]{:S(2)}) %collective-permute-start.11) | collective-permute-done | bytes 118816 | tf_op jit(solution)/shard_map/ppermute | solution.py:266
  32.8 0.1 collective-permute-start.13
  32.9 0.5 collective-permute-start.16
  33.4 1.6 %shard_map.69 = (f32[64,3584]{1,0:T(8,128)S(1)}, bf16[128,3584]{1,0:T(8,128)(2,1)S(1)}) custom-call(bf16[32,3712]{1,0:T(8,128)(2,1)S(1)} %collective-permute-done.3.refs_0_, bf16[32,3712]{1,0:T(8,128)(2,1)S(1)} %collective-permute-done.4.refs_1_, bf16[32,3712]{1,0:T(8,128)(2,1)S(1)} %collective-permute-done.8.refs_2_, ...), custom_call_target="tpu_custom_call" | custom-call | flops 1879048192 | tf_op jit(solution)/shard_map/pallas_call | solution.py:214
  35.1 4.6 %shard_map.70 = (f32[96,3584]{1,0:T(8,128)S(1)}, bf16[32,3584]{1,0:T(8,128)(2,1)S(1)}, bf16[64,3584]{1,0:T(8,128)(2,1)S(1)}) custom-call(bf16[32,3712]{1,0:T(8,128)(2,1)S(1)} %constant_dynamic-update-slice_fusion.refs_0_, bf16[32,3712]{1,0:T(8,128)(2,1)S(1)} %collective-permute-done.5.refs_1_, bf16[32,3712]{1,0:T(8,128)(2,1)S(1)} %collective-permute-done.6.refs_2_, ...), custom_call_target="tpu_custom_call" | custom-call | flops 5637144576 | tf_op jit(solution)/shard_map/pallas_call | solution.py:242
  39.7 0.1 collective-permute-start.19
  39.8 0.4 collective-permute-start.17
  40.2 0.1 collective-permute-start.18
  40.3 0.9 %collective-permute-done.19 = bf16[32,3584]{1,0:T(8,128)(2,1)S(1)} collective-permute-done((bf16[32,3584]{1,0:T(8,128)(2,1)S(1)}, bf16[32,3584]{1,0:T(8,128)(2,1)S(1)}, u32[]{:S(2)}, u32[]{:S(2)}) %collective-permute-start.19) | collective-permute-done | bytes 229408 | tf_op jit(solution)/shard_map/ppermute | solution.py:268
  41.3 1.0 %collective-permute-start.20 = (bf16[16,3584]{1,0:T(8,128)(2,1)S(1)}, bf16[16,3584]{1,0:T(8,128)(2,1)S(1)}, u32[]{:S(2)}, u32[]{:S(2)}) collective-permute-start(bf16[16,3584]{1,0:T(8,128)(2,1)S(1)} %get-tuple-element.123), channel_id=1, source_target_pairs={{0,4},{1,5},{4,8},{5,9},{8,12},{9,13},{12,14},{13,15},{14,10},{15,... | collective-permute-start | bytes 344072 | tf_op jit(solution)/shard_map/ppermute | solution.py:266
  42.3 1.0 %collective-permute-start.22 = (bf16[16,3584]{1,0:T(8,128)(2,1)S(1)}, bf16[16,3584]{1,0:T(8,128)(2,1)S(1)}, u32[]{:S(2)}, u32[]{:S(2)}) collective-permute-start(bf16[16,3584]{1,0:T(8,128)(2,1)S(1)} %get-tuple-element.124), channel_id=1, source_target_pairs={{4,0},{5,1},{8,4},{9,5},{12,8},{13,9},{14,12},{15,13},{10,14},{11,... | collective-permute-start | bytes 344072 | tf_op jit(solution)/shard_map/ppermute | solution.py:267
  43.4 0.1 convert_add_fusion.1
  43.5 3.0 %collective-permute-done.20 = bf16[16,3584]{1,0:T(8,128)(2,1)S(1)} collective-permute-done((bf16[16,3584]{1,0:T(8,128)(2,1)S(1)}, bf16[16,3584]{1,0:T(8,128)(2,1)S(1)}, u32[]{:S(2)}, u32[]{:S(2)}) %collective-permute-start.20) | collective-permute-done | bytes 114720 | tf_op jit(solution)/shard_map/ppermute | solution.py:266
  46.6 1.0 %collective-permute-start.21 = (bf16[32,3584]{1,0:T(8,128)(2,1)S(1)}, bf16[32,3584]{1,0:T(8,128)(2,1)S(1)}, u32[]{:S(2)}, u32[]{:S(2)}) collective-permute-start(bf16[32,3584]{1,0:T(8,128)(2,1)S(1)} %pad_maximum_fusion), channel_id=1, source_target_pairs={{0,4},{1,5},{4,8},{5,9},{8,12},{9,13},{12,14},{13,15},{14,10},{15,... | collective-permute-start | bytes 688136 | tf_op jit(solution)/shard_map/ppermute | solution.py:266
  47.7 1.1 %collective-permute-start.24 = (bf16[32,3584]{1,0:T(8,128)(2,1)S(1)}, bf16[32,3584]{1,0:T(8,128)(2,1)S(1)}, u32[]{:S(2)}, u32[]{:S(2)}) collective-permute-start(bf16[32,3584]{1,0:T(8,128)(2,1)S(1)} %pad_maximum_fusion.1), channel_id=1, source_target_pairs={{4,0},{5,1},{8,4},{9,5},{12,8},{13,9},{14,12},{15,13},{10,14},{11,... | collective-permute-start | bytes 688136 | tf_op jit(solution)/shard_map/ppermute | solution.py:267
  48.8 4.7 %collective-permute-done.21 = bf16[32,3584]{1,0:T(8,128)(2,1)S(1)} collective-permute-done((bf16[32,3584]{1,0:T(8,128)(2,1)S(1)}, bf16[32,3584]{1,0:T(8,128)(2,1)S(1)}, u32[]{:S(2)}, u32[]{:S(2)}) %collective-permute-start.21) | collective-permute-done | bytes 229408 | tf_op jit(solution)/shard_map/ppermute | solution.py:266
  53.4 0.1 add_convert_fusion.4
  53.5 1.0 %collective-permute-start.23 = (bf16[32,3584]{1,0:T(8,128)(2,1)S(1)}, bf16[32,3584]{1,0:T(8,128)(2,1)S(1)}, u32[]{:S(2)}, u32[]{:S(2)}) collective-permute-start(bf16[32,3584]{1,0:T(8,128)(2,1)S(1)} %add_convert_fusion.4), channel_id=1, source_target_pairs={{0,4},{1,5},{4,8},{5,9},{8,12},{9,13},{12,14},{13,15},{14,10},{15,... | collective-permute-start | bytes 688136 | tf_op jit(solution)/shard_map/ppermute | solution.py:266
  54.6 1.1 %collective-permute-start.26 = (bf16[32,3584]{1,0:T(8,128)(2,1)S(1)}, bf16[32,3584]{1,0:T(8,128)(2,1)S(1)}, u32[]{:S(2)}, u32[]{:S(2)}) collective-permute-start(bf16[32,3584]{1,0:T(8,128)(2,1)S(1)} %add_convert_fusion.3), channel_id=1, source_target_pairs={{4,0},{5,1},{8,4},{9,5},{12,8},{13,9},{14,12},{15,13},{10,14},{11,... | collective-permute-start | bytes 688136 | tf_op jit(solution)/shard_map/ppermute | solution.py:267
  55.7 3.9 %collective-permute-done.23 = bf16[32,3584]{1,0:T(8,128)(2,1)S(1)} collective-permute-done((bf16[32,3584]{1,0:T(8,128)(2,1)S(1)}, bf16[32,3584]{1,0:T(8,128)(2,1)S(1)}, u32[]{:S(2)}, u32[]{:S(2)}) %collective-permute-start.23) | collective-permute-done | bytes 229408 | tf_op jit(solution)/shard_map/ppermute | solution.py:266
  59.6 0.1 add_convert_fusion.2
  59.7 1.0 %collective-permute-start.25 = (bf16[32,3584]{1,0:T(8,128)(2,1)S(1)}, bf16[32,3584]{1,0:T(8,128)(2,1)S(1)}, u32[]{:S(2)}, u32[]{:S(2)}) collective-permute-start(bf16[32,3584]{1,0:T(8,128)(2,1)S(1)} %add_convert_fusion.2), channel_id=1, source_target_pairs={{0,4},{1,5},{4,8},{5,9},{8,12},{9,13},{12,14},{13,15},{14,10},{15,... | collective-permute-start | bytes 688136 | tf_op jit(solution)/shard_map/ppermute | solution.py:266
  60.8 1.1 %collective-permute-start.27 = (bf16[32,3584]{1,0:T(8,128)(2,1)S(1)}, bf16[32,3584]{1,0:T(8,128)(2,1)S(1)}, u32[]{:S(2)}, u32[]{:S(2)}) collective-permute-start(bf16[32,3584]{1,0:T(8,128)(2,1)S(1)} %add_convert_fusion.1), channel_id=1, source_target_pairs={{4,0},{5,1},{8,4},{9,5},{12,8},{13,9},{14,12},{15,13},{10,14},{11,... | collective-permute-start | bytes 688136 | tf_op jit(solution)/shard_map/ppermute | solution.py:267
  61.9 3.9 %collective-permute-done.25 = bf16[32,3584]{1,0:T(8,128)(2,1)S(1)} collective-permute-done((bf16[32,3584]{1,0:T(8,128)(2,1)S(1)}, bf16[32,3584]{1,0:T(8,128)(2,1)S(1)}, u32[]{:S(2)}, u32[]{:S(2)}) %collective-permute-start.25) | collective-permute-done | bytes 229408 | tf_op jit(solution)/shard_map/ppermute | solution.py:266
  65.7 1.1 %collective-permute-done.27 = bf16[32,3584]{1,0:T(8,128)(2,1)S(1)} collective-permute-done((bf16[32,3584]{1,0:T(8,128)(2,1)S(1)}, bf16[32,3584]{1,0:T(8,128)(2,1)S(1)}, u32[]{:S(2)}, u32[]{:S(2)}) %collective-permute-start.27) | collective-permute-done | bytes 229408 | tf_op jit(solution)/shard_map/ppermute | solution.py:267
  66.9 0.8 %add_convert_fusion = bf16[32,3584]{1,0:T(8,128)(2,1)} fusion(bf16[32,3584]{1,0:T(8,128)(2,1)S(1)} %collective-permute-done.27, bf16[32,3584]{1,0:T(8,128)(2,1)S(1)} %collective-permute-done.25, bf16[32,3584]{1,0:T(8,128)(2,1)S(1)} %collective-permute-done.16, f32[96,3584]{1,0:T(8,128)S(1)} %get-tuple-element.84), kind=kLoop, calls=%fused_computation | loop fusion | flops 802816 | bytes 1376256 | tf_op jit(solution)/shard_map/convert_element_type | solution.py:349
  (33 shorter events, 0.5 us)
Async XLA Ops:
  1.0 8.8 %collective-permute-start.1 = (bf16[32,3712]{1,0:T(8,128)(2,1)S(1)}, bf16[32,3712]{1,0:T(8,128)(2,1)S(1)}, u32[]{:S(2)}, u32[]{:S(2)}) collective-permute-start(bf16[32,3712]{1,0:T(8,128)(2,1)S(1)} %shard_map.64.after.refs_0_), channel_id=1, source_target_pairs={{0,4},{1,5},{4,8},{5,9},{8,12},{9,13},{12,14},{13,15},{14,10},{15,... | collective-permute-start | bytes 712712 | tf_op jit(solution)/shard_map/ppermute | solution.py:266
  4.1 7.2 %collective-permute-start = (bf16[32,3712]{1,0:T(8,128)(2,1)S(1)}, bf16[32,3712]{1,0:T(8,128)(2,1)S(1)}, u32[]{:S(2)}, u32[]{:S(2)}) collective-permute-start(bf16[32,3712]{1,0:T(8,128)(2,1)S(1)} %shard_map.64.after.refs_0_), channel_id=1, source_target_pairs={{4,0},{5,1},{8,4},{9,5},{12,8},{13,9},{14,12},{15,13},{10,14},{11,... | collective-permute-start | bytes 712712 | tf_op jit(solution)/shard_map/ppermute | solution.py:267
  7.3 4.1 %collective-permute-start.2 = (bf16[32,3712]{1,0:T(8,128)(2,1)S(1)}, bf16[32,3712]{1,0:T(8,128)(2,1)S(1)}, u32[]{:S(2)}, u32[]{:S(2)}) collective-permute-start(bf16[32,3712]{1,0:T(8,128)(2,1)S(1)} %shard_map.64.after.refs_0_), channel_id=1, source_target_pairs={{0,1},{1,0},{2,3},{3,2},{4,5},{5,4},{6,7},{7,6},{8,9},{9,8},{10,11... | collective-permute-start | bytes 712712 | tf_op jit(solution)/shard_map/ppermute | solution.py:268
  11.3 7.1 %collective-permute-start.3 = (bf16[32,3712]{1,0:T(8,128)(2,1)S(1)}, bf16[32,3712]{1,0:T(8,128)(2,1)S(1)}, u32[]{:S(2)}, u32[]{:S(2)}) collective-permute-start(bf16[32,3712]{1,0:T(8,128)(2,1)S(1)} %collective-permute-done.refs_1_), channel_id=1, source_target_pairs={{4,0},{5,1},{8,4},{9,5},{12,8},{13,9},{14,12},{15,13},{10,14},{11,... | collective-permute-start | bytes 712712 | tf_op jit(solution)/shard_map/ppermute | solution.py:267
  11.6 6.8 %collective-permute-start.4 = (bf16[32,3712]{1,0:T(8,128)(2,1)S(1)}, bf16[32,3712]{1,0:T(8,128)(2,1)S(1)}, u32[]{:S(2)}, u32[]{:S(2)}) collective-permute-start(bf16[32,3712]{1,0:T(8,128)(2,1)S(1)} %collective-permute-done.1.refs_2_), channel_id=1, source_target_pairs={{0,4},{1,5},{4,8},{5,9},{8,12},{9,13},{12,14},{13,15},{14,10},{15,... | collective-permute-start | bytes 712712 | tf_op jit(solution)/shard_map/ppermute | solution.py:266
  17.8 6.2 %collective-permute-start.7 = (bf16[32,3712]{1,0:T(8,128)(2,1)S(1)}, bf16[32,3712]{1,0:T(8,128)(2,1)S(1)}, u32[]{:S(2)}, u32[]{:S(2)}) collective-permute-start(bf16[32,3712]{1,0:T(8,128)(2,1)S(1)} %collective-permute-done.1.refs_2_), channel_id=1, source_target_pairs={{0,1},{1,0},{2,3},{3,2},{4,5},{5,4},{6,7},{7,6},{8,9},{9,8},{10,11... | collective-permute-start | bytes 712712 | tf_op jit(solution)/shard_map/ppermute | solution.py:268
  17.9 6.7 %collective-permute-start.8 = (bf16[32,3712]{1,0:T(8,128)(2,1)S(1)}, bf16[32,3712]{1,0:T(8,128)(2,1)S(1)}, u32[]{:S(2)}, u32[]{:S(2)}) collective-permute-start(bf16[32,3712]{1,0:T(8,128)(2,1)S(1)} %collective-permute-done.refs_1_), channel_id=1, source_target_pairs={{0,1},{1,0},{2,3},{3,2},{4,5},{5,4},{6,7},{7,6},{8,9},{9,8},{10,11... | collective-permute-start | bytes 712712 | tf_op jit(solution)/shard_map/ppermute | solution.py:268
  18.4 7.8 %collective-permute-start.5 = (bf16[32,3712]{1,0:T(8,128)(2,1)S(1)}, bf16[32,3712]{1,0:T(8,128)(2,1)S(1)}, u32[]{:S(2)}, u32[]{:S(2)}) collective-permute-start(bf16[32,3712]{1,0:T(8,128)(2,1)S(1)} %collective-permute-done.3.refs_0_), channel_id=1, source_target_pairs={{4,0},{5,1},{8,4},{9,5},{12,8},{13,9},{14,12},{15,13},{10,14},{11,... | collective-permute-start | bytes 712712 | tf_op jit(solution)/shard_map/ppermute | solution.py:267
  19.9 6.3 %collective-permute-start.6 = (bf16[32,3712]{1,0:T(8,128)(2,1)S(1)}, bf16[32,3712]{1,0:T(8,128)(2,1)S(1)}, u32[]{:S(2)}, u32[]{:S(2)}) collective-permute-start(bf16[32,3712]{1,0:T(8,128)(2,1)S(1)} %collective-permute-done.4.refs_1_), channel_id=1, source_target_pairs={{0,4},{1,5},{4,8},{5,9},{8,12},{9,13},{12,14},{13,15},{14,10},{15,... | collective-permute-start | bytes 712712 | tf_op jit(solution)/shard_map/ppermute | solution.py:266
  24.0 4.4 %collective-permute-start.9 = (bf16[32,3712]{1,0:T(8,128)(2,1)S(1)}, bf16[32,3712]{1,0:T(8,128)(2,1)S(1)}, u32[]{:S(2)}, u32[]{:S(2)}) collective-permute-start(bf16[32,3712]{1,0:T(8,128)(2,1)S(1)} %collective-permute-done.4.refs_1_), channel_id=1, source_target_pairs={{0,1},{1,0},{2,3},{3,2},{4,5},{5,4},{6,7},{7,6},{8,9},{9,8},{10,11... | collective-permute-start | bytes 712712 | tf_op jit(solution)/shard_map/ppermute | solution.py:268
  24.1 4.3 %collective-permute-start.10 = (bf16[32,3712]{1,0:T(8,128)(2,1)S(1)}, bf16[32,3712]{1,0:T(8,128)(2,1)S(1)}, u32[]{:S(2)}, u32[]{:S(2)}) collective-permute-start(bf16[32,3712]{1,0:T(8,128)(2,1)S(1)} %collective-permute-done.3.refs_0_), channel_id=1, source_target_pairs={{0,1},{1,0},{2,3},{3,2},{4,5},{5,4},{6,7},{7,6},{8,9},{9,8},{10,11... | collective-permute-start | bytes 712712 | tf_op jit(solution)/shard_map/ppermute | solution.py:268
  26.3 5.8 %collective-permute-start.12 = (bf16[16,3712]{1,0:T(8,128)(2,1)S(1)}, bf16[16,3712]{1,0:T(8,128)(2,1)S(1)}, u32[]{:S(2)}, u32[]{:S(2)}) collective-permute-start(bf16[16,3712]{1,0:T(8,128)(2,1)S(1)} %slice.70), channel_id=1, source_target_pairs={{4,0},{5,1},{8,4},{9,5},{12,8},{13,9},{14,12},{15,13},{10,14},{11,... | collective-permute-start | bytes 356360 | tf_op jit(solution)/shard_map/ppermute | solution.py:267
  27.9 4.8 %collective-permute-start.11 = (bf16[16,3712]{1,0:T(8,128)(2,1)S(1)}, bf16[16,3712]{1,0:T(8,128)(2,1)S(1)}, u32[]{:S(2)}, u32[]{:S(2)}) collective-permute-start(bf16[16,3712]{1,0:T(8,128)(2,1)S(1)} %slice.69), channel_id=1, source_target_pairs={{0,4},{1,5},{4,8},{5,9},{8,12},{9,13},{12,14},{13,15},{14,10},{15,... | collective-permute-start | bytes 356360 | tf_op jit(solution)/shard_map/ppermute | solution.py:266
  31.5 3.5 %collective-permute-start.14 = (bf16[32,3712]{1,0:T(8,128)(2,1)S(1)}, bf16[32,3712]{1,0:T(8,128)(2,1)S(1)}, u32[]{:S(2)}, u32[]{:S(2)}) collective-permute-start(bf16[32,3712]{1,0:T(8,128)(2,1)S(1)} %collective-permute-done.6.refs_2_), channel_id=1, source_target_pairs={{0,1},{1,0},{2,3},{3,2},{4,5},{5,4},{6,7},{7,6},{8,9},{9,8},{10,11... | collective-permute-start | bytes 712712 | tf_op jit(solution)/shard_map/ppermute | solution.py:268
  31.6 3.5 %collective-permute-start.15 = (bf16[32,3712]{1,0:T(8,128)(2,1)S(1)}, bf16[32,3712]{1,0:T(8,128)(2,1)S(1)}, u32[]{:S(2)}, u32[]{:S(2)}) collective-permute-start(bf16[32,3712]{1,0:T(8,128)(2,1)S(1)} %collective-permute-done.5.refs_1_), channel_id=1, source_target_pairs={{0,1},{1,0},{2,3},{3,2},{4,5},{5,4},{6,7},{7,6},{8,9},{9,8},{10,11... | collective-permute-start | bytes 712712 | tf_op jit(solution)/shard_map/ppermute | solution.py:268
  32.8 2.2 %collective-permute-start.13 = (bf16[32,3712]{1,0:T(8,128)(2,1)S(1)}, bf16[32,3712]{1,0:T(8,128)(2,1)S(1)}, u32[]{:S(2)}, u32[]{:S(2)}) collective-permute-start(bf16[32,3712]{1,0:T(8,128)(2,1)S(1)} %constant_dynamic-update-slice_fusion.refs_0_), channel_id=1, source_target_pairs={{0,1},{1,0},{2,3},{3,2},{4,5},{5,4},{6,7},{7,6},{8,9},{9,8},{10,11... | collective-permute-start | bytes 712712 | tf_op jit(solution)/shard_map/ppermute | solution.py:268
  32.9 2.1 %collective-permute-start.16 = (bf16[32,3584]{1,0:T(8,128)(2,1)S(1)}, bf16[32,3584]{1,0:T(8,128)(2,1)S(1)}, u32[]{:S(2)}, u32[]{:S(2)}) collective-permute-start(bf16[32,3584]{1,0:T(8,128)(2,1)S(1)} %get-tuple-element.103), channel_id=1, source_target_pairs={{0,1},{1,0},{2,3},{3,2},{4,5},{5,4},{6,7},{7,6},{8,9},{9,8},{10,11... | collective-permute-start | bytes 688136 | tf_op jit(solution)/shard_map/ppermute | solution.py:268
  39.7 1.6 %collective-permute-start.19 = (bf16[32,3584]{1,0:T(8,128)(2,1)S(1)}, bf16[32,3584]{1,0:T(8,128)(2,1)S(1)}, u32[]{:S(2)}, u32[]{:S(2)}) collective-permute-start(bf16[32,3584]{1,0:T(8,128)(2,1)S(1)} %get-tuple-element.111), channel_id=1, source_target_pairs={{0,1},{1,0},{2,3},{3,2},{4,5},{5,4},{6,7},{7,6},{8,9},{9,8},{10,11... | collective-permute-start | bytes 688136 | tf_op jit(solution)/shard_map/ppermute | solution.py:268
  39.8 3.6 %collective-permute-start.17 = (bf16[64,3584]{1,0:T(8,128)(2,1)S(1)}, bf16[64,3584]{1,0:T(8,128)(2,1)S(1)}, u32[]{:S(2)}, u32[]{:S(2)}) collective-permute-start(bf16[64,3584]{1,0:T(8,128)(2,1)S(1)} %get-tuple-element.108), channel_id=1, source_target_pairs={{0,1},{1,0},{2,3},{3,2},{4,5},{5,4},{6,7},{7,6},{8,9},{9,8},{10,11... | collective-permute-start | bytes 1376264 | tf_op jit(solution)/shard_map/ppermute | solution.py:268
  40.2 3.1 %collective-permute-start.18 = (bf16[128,3584]{1,0:T(8,128)(2,1)S(1)}, bf16[128,3584]{1,0:T(8,128)(2,1)S(1)}, u32[]{:S(2)}, u32[]{:S(2)}) collective-permute-start(bf16[128,3584]{1,0:T(8,128)(2,1)S(1)} %get-tuple-element.109), channel_id=1, source_target_pairs={{0,1},{1,0},{2,3},{3,2},{4,5},{5,4},{6,7},{7,6},{8,9},{9,8},{10,11... | collective-permute-start | bytes 2752520 | tf_op jit(solution)/shard_map/ppermute | solution.py:268
  41.3 5.2 %collective-permute-start.20 = (bf16[16,3584]{1,0:T(8,128)(2,1)S(1)}, bf16[16,3584]{1,0:T(8,128)(2,1)S(1)}, u32[]{:S(2)}, u32[]{:S(2)}) collective-permute-start(bf16[16,3584]{1,0:T(8,128)(2,1)S(1)} %get-tuple-element.123), channel_id=1, source_target_pairs={{0,4},{1,5},{4,8},{5,9},{8,12},{9,13},{12,14},{13,15},{14,10},{15,... | collective-permute-start | bytes 344072 | tf_op jit(solution)/shard_map/ppermute | solution.py:266
  42.3 5.3 %collective-permute-start.22 = (bf16[16,3584]{1,0:T(8,128)(2,1)S(1)}, bf16[16,3584]{1,0:T(8,128)(2,1)S(1)}, u32[]{:S(2)}, u32[]{:S(2)}) collective-permute-start(bf16[16,3584]{1,0:T(8,128)(2,1)S(1)} %get-tuple-element.124), channel_id=1, source_target_pairs={{4,0},{5,1},{8,4},{9,5},{12,8},{13,9},{14,12},{15,13},{10,14},{11,... | collective-permute-start | bytes 344072 | tf_op jit(solution)/shard_map/ppermute | solution.py:267
  46.6 6.9 %collective-permute-start.21 = (bf16[32,3584]{1,0:T(8,128)(2,1)S(1)}, bf16[32,3584]{1,0:T(8,128)(2,1)S(1)}, u32[]{:S(2)}, u32[]{:S(2)}) collective-permute-start(bf16[32,3584]{1,0:T(8,128)(2,1)S(1)} %pad_maximum_fusion), channel_id=1, source_target_pairs={{0,4},{1,5},{4,8},{5,9},{8,12},{9,13},{12,14},{13,15},{14,10},{15,... | collective-permute-start | bytes 688136 | tf_op jit(solution)/shard_map/ppermute | solution.py:266
  47.7 6.9 %collective-permute-start.24 = (bf16[32,3584]{1,0:T(8,128)(2,1)S(1)}, bf16[32,3584]{1,0:T(8,128)(2,1)S(1)}, u32[]{:S(2)}, u32[]{:S(2)}) collective-permute-start(bf16[32,3584]{1,0:T(8,128)(2,1)S(1)} %pad_maximum_fusion.1), channel_id=1, source_target_pairs={{4,0},{5,1},{8,4},{9,5},{12,8},{13,9},{14,12},{15,13},{10,14},{11,... | collective-permute-start | bytes 688136 | tf_op jit(solution)/shard_map/ppermute | solution.py:267
  53.5 6.1 %collective-permute-start.23 = (bf16[32,3584]{1,0:T(8,128)(2,1)S(1)}, bf16[32,3584]{1,0:T(8,128)(2,1)S(1)}, u32[]{:S(2)}, u32[]{:S(2)}) collective-permute-start(bf16[32,3584]{1,0:T(8,128)(2,1)S(1)} %add_convert_fusion.4), channel_id=1, source_target_pairs={{0,4},{1,5},{4,8},{5,9},{8,12},{9,13},{12,14},{13,15},{14,10},{15,... | collective-permute-start | bytes 688136 | tf_op jit(solution)/shard_map/ppermute | solution.py:266
  54.6 6.1 %collective-permute-start.26 = (bf16[32,3584]{1,0:T(8,128)(2,1)S(1)}, bf16[32,3584]{1,0:T(8,128)(2,1)S(1)}, u32[]{:S(2)}, u32[]{:S(2)}) collective-permute-start(bf16[32,3584]{1,0:T(8,128)(2,1)S(1)} %add_convert_fusion.3), channel_id=1, source_target_pairs={{4,0},{5,1},{8,4},{9,5},{12,8},{13,9},{14,12},{15,13},{10,14},{11,... | collective-permute-start | bytes 688136 | tf_op jit(solution)/shard_map/ppermute | solution.py:267
  59.7 6.1 %collective-permute-start.25 = (bf16[32,3584]{1,0:T(8,128)(2,1)S(1)}, bf16[32,3584]{1,0:T(8,128)(2,1)S(1)}, u32[]{:S(2)}, u32[]{:S(2)}) collective-permute-start(bf16[32,3584]{1,0:T(8,128)(2,1)S(1)} %add_convert_fusion.2), channel_id=1, source_target_pairs={{0,4},{1,5},{4,8},{5,9},{8,12},{9,13},{12,14},{13,15},{14,10},{15,... | collective-permute-start | bytes 688136 | tf_op jit(solution)/shard_map/ppermute | solution.py:266
  60.8 6.1 %collective-permute-start.27 = (bf16[32,3584]{1,0:T(8,128)(2,1)S(1)}, bf16[32,3584]{1,0:T(8,128)(2,1)S(1)}, u32[]{:S(2)}, u32[]{:S(2)}) collective-permute-start(bf16[32,3584]{1,0:T(8,128)(2,1)S(1)} %add_convert_fusion.1), channel_id=1, source_target_pairs={{4,0},{5,1},{8,4},{9,5},{12,8},{13,9},{14,12},{15,13},{10,14},{11,... | collective-permute-start | bytes 688136 | tf_op jit(solution)/shard_map/ppermute | solution.py:267

commit v8 on v7

--- a/solution.py
+++ b/solution.py
@@ -69,52 +69,12 @@
             pltpu.SemaphoreType.DMA((3,)),
         ],
         compiler_params=pltpu.CompilerParams(vmem_limit_bytes=SCRATCH),
+        cost_estimate=pl.CostEstimate(flops=10 * 2**30, bytes_accessed=0, transcendentals=0),
     )(hbm(tokens), hbm(routes.T), hbm(gates.T))
 
 
 def hbm(a):
     return pltpu.with_memory_space_constraint(a, pltpu.HBM)
-
-
-def vmem(a):
-    return pltpu.with_memory_space_constraint(a, pltpu.VMEM)
-
-
-def fetches(parts, source, target, sems):
-    step = target.shape[2] // parts
-    moves = []
-    for i in range(parts):
-        at = (slice(None), slice(None), slice(i * step, (i + 1) * step))
-        moves.append(pltpu.make_async_copy(source.at[at], target.at[at], sems.at[i]))
-        moves[-1].start()
-    return moves
-
-
-def load_kernel(parts, source, after, target, sems):
-    step = target.shape[1] // parts
-    moves = [
-        pltpu.make_async_copy(
-            source.at[:, i * step : (i + 1) * step], target.at[:, i * step : (i + 1) * step], sems.at[i]
-        )
-        for i in range(parts)
-    ]
-    for move in moves:
-        move.start()
-    for move in moves:
-        move.wait()
-
-
-def load(weight, after):
-    parts = 8 if weight.shape[1] % 128 == 0 else 1
-    return pl.pallas_call(
-        functools.partial(load_kernel, parts),
-        out_shape=pltpu.VMEM(weight.shape, weight.dtype),
-        in_specs=[pl.BlockSpec(memory_space=pltpu.HBM), pl.BlockSpec(memory_space=pl.ANY)],
-        out_specs=pl.BlockSpec(memory_space=pltpu.VMEM),
-        scratch_shapes=[pltpu.SemaphoreType.DMA((parts,))],
-        compiler_params=pltpu.CompilerParams(vmem_limit_bytes=SCRATCH),
-        cost_estimate=pl.CostEstimate(flops=0, bytes_accessed=2 * weight.size, transcendentals=0),
-    )(hbm(weight), after)
 
 
 def gather_rows(blocks, x_ref):
@@ -155,75 +115,51 @@
     return (256 if ff % 256 == 0 else ff), next(t for t in (512, 256, 128, width) if width % t == 0)
 
 
-def hidden_kernel(count, tile, parts, *refs):
-    blocks, (gate_ref, source, h_ref, *rest) = refs[:count], refs[count:]
-    if parts:
-        up_ref, x_ref, sems = rest
-        moves = fetches(parts, source, up_ref, sems)
-    else:
-        up_ref, (x_ref,), moves = source, rest, []
+def hidden_kernel(count, tile, *refs):
+    blocks, (gate_ref, up_ref, h_ref, x_ref) = refs[:count], refs[count:]
     gather_rows(blocks, x_ref)
-    ff = h_ref.shape[1]
-    for i in range(max(parts, 1)):
-        if parts:
-            moves[i].wait()
-        first_half(x_ref, gate_ref, up_ref, h_ref, tile, i * ff // max(parts, 1), (i + 1) * ff // max(parts, 1))
-
-
-def hidden(blocks, w_gate, w_up, fetch):
+    first_half(x_ref, gate_ref, up_ref, h_ref, tile, 0, h_ref.shape[1])
+
+
+def hidden(blocks, w_gate, w_up):
     count, rows = len(blocks), blocks[0].shape[0]
     _, width, ff = w_gate.shape
-    tile, _ = tiles(width, ff)
-    parts = (2 if ff % (2 * tile) == 0 else 1) if fetch else 0
     here = pl.BlockSpec(memory_space=pltpu.VMEM)
     return pl.pallas_call(
-        functools.partial(hidden_kernel, count, tile, parts),
-        out_shape=[pltpu.VMEM((count * rows, ff), BF16)] + [pltpu.VMEM(w_up.shape, BF16)] * fetch,
-        in_specs=[here] * (count + 1) + [pl.BlockSpec(memory_space=pltpu.HBM if fetch else pltpu.VMEM)],
-        out_specs=[here] * (1 + fetch),
-        scratch_shapes=[pltpu.VMEM((count * rows, width), BF16)] + [pltpu.SemaphoreType.DMA((parts,))] * fetch,
+        functools.partial(hidden_kernel, count, tiles(width, ff)[0]),
+        out_shape=pltpu.VMEM((count * rows, ff), BF16),
+        in_specs=[here] * (count + 2),
+        out_specs=here,
+        scratch_shapes=[pltpu.VMEM((count * rows, width), BF16)],
         compiler_params=pltpu.CompilerParams(vmem_limit_bytes=SCRATCH),
         cost_estimate=pl.CostEstimate(
             flops=4 * max(count * rows, 256) * width * ff, bytes_accessed=0, transcendentals=count * rows * ff
         ),
-    )(*blocks, vmem(w_gate), hbm(w_up) if fetch else vmem(w_up))
-
-
-def output_kernel(count, experts, tile, parts, *refs):
-    blocks, (h_ref, source, mine_ref, other_ref, *rest) = refs[:count], refs[count:]
-    if parts:
-        down_ref, w_ref, sems = rest
-        moves = fetches(parts, source, down_ref, sems)
-    else:
-        down_ref, (w_ref,), moves = source, rest, []
+    )(*blocks, w_gate, w_up)
+
+
+def output_kernel(count, experts, tile, *refs):
+    blocks, (h_ref, down_ref, mine_ref, other_ref, w_ref) = refs[:count], refs[count:]
     width = mine_ref.shape[1]
     gather_weights(experts, blocks, width, w_ref)
-    for i in range(max(parts, 1)):
-        if parts:
-            moves[i].wait()
-        begin, end = i * width // max(parts, 1), (i + 1) * width // max(parts, 1)
-        second_half(h_ref, down_ref, w_ref, [mine_ref, other_ref], tile, begin, end)
-
-
-def output(blocks, mine, experts, h, w_down, fetch):
+    second_half(h_ref, down_ref, w_ref, [mine_ref, other_ref], tile, 0, width)
+
+
+def output(blocks, mine, experts, h, w_down):
     count, rows = len(blocks), blocks[0].shape[0]
     _, ff, width = w_down.shape
-    _, tile = tiles(width, ff)
-    parts = width // tile if fetch else 0
     here = pl.BlockSpec(memory_space=pltpu.VMEM)
     return pl.pallas_call(
-        functools.partial(output_kernel, count, experts, tile, parts),
-        out_shape=[pltpu.VMEM((mine * rows, width), F32), pltpu.VMEM(((count - mine) * rows, width), BF16)]
-        + [pltpu.VMEM(w_down.shape, BF16)] * fetch,
-        in_specs=[here] * (count + 1)
-        + [pl.BlockSpec(memory_space=pltpu.HBM if fetch else pltpu.VMEM)],
-        out_specs=[here] * (2 + fetch),
-        scratch_shapes=[pltpu.VMEM((count * rows, 1), F32)] + [pltpu.SemaphoreType.DMA((parts,))] * fetch,
+        functools.partial(output_kernel, count, experts, tiles(width, ff)[1]),
+        out_shape=[pltpu.VMEM((mine * rows, width), F32), pltpu.VMEM(((count - mine) * rows, width), BF16)],
+        in_specs=[here] * (count + 2),
+        out_specs=[here] * 2,
+        scratch_shapes=[pltpu.VMEM((count * rows, 1), F32)],
         compiler_params=pltpu.CompilerParams(vmem_limit_bytes=SCRATCH),
         cost_estimate=pl.CostEstimate(
             flops=2 * max(count * rows, 256) * width * ff, bytes_accessed=0, transcendentals=0
         ),
-    )(*blocks, h, hbm(w_down) if fetch else vmem(w_down))
+    )(*blocks, h, w_down)
 
 
 def expert_kernel(count, experts, tile_ff, tile_d, *refs):
@@ -253,7 +189,7 @@
         cost_estimate=pl.CostEstimate(
             flops=6 * max(total, 256) * width * ff, bytes_accessed=0, transcendentals=total * ff
         ),
-    )(*blocks, vmem(w_gate), vmem(w_up), vmem(w_down))
+    )(*blocks, w_gate, w_up, w_down)
 
 
 def local(cores, order, tokens, routes, gates, w_gate, w_up, w_down):
@@ -277,26 +213,26 @@
     for d in range(1, far):
         a, b = left(got[d - 1]), right(got[1 - d])
         if d == 1:
-            done = (load(w_gate, own),)
+            done = None
         elif d == 2:
             near = [got[0], got[1], got[-1], twin[0]]
-            done = hidden(near, w_gate, w_up, True)
+            done = hidden(near, w_gate, w_up)
         elif d == 3:
-            done = output(near, 3, experts, h_near, w_down, True)
+            done = output(near, 3, experts, h_near, w_down)
         else:
             done = None
         ready, done = together(({e: got[e] for e in {d - 1, 1 - d}}, done))
         started = {e: sibling(ready[e]) for e in ready}
         if d == 1:
-            a, b, (w_gate,), started = together((a, b, done, started))
+            a, b, started = together((a, b, started))
             twin.update(started)
             started = {}
         else:
             a, b, done, exchanged = together((a, b, done, exchanged))
         if d == 2:
-            h_near, w_up = done
+            h_near = done
         if d == 3:
-            *near_out, w_down = done
+            near_out = done
         twin.update(exchanged)
         exchanged = started
         got[d], got[-d] = a, b
@@ -304,14 +240,14 @@
     exchanged = together(exchanged)
     twin.update(exchanged)
     rest = [got[d] for d in middle] + [twin[1], twin[-1]] + [twin[d] for d in middle]
-    (h_rest,) = hidden(rest, w_gate, w_up, False)
+    h_rest = hidden(rest, w_gate, w_up)
     ready, h_rest = together(({e: got[e] for e in (far - 1, 1 - far)}, h_rest))
     exchanged = {e: sibling(ready[e]) for e in ready}
     ends, h_rest = together((ends, h_rest))
     got[far] = jnp.concatenate(ends, axis=0)
     rest_out, twin[far], exchanged, near_sent = together(
         (
-            output(rest, len(middle), experts, h_rest, w_down, False),
+            output(rest, len(middle), experts, h_rest, w_down),
             sibling(got[far]),
             exchanged,
             sibling(near_out[1]),
@@ -334,19 +270,29 @@
     for j, d in enumerate(late[1:]):
         mine[d], theirs[d] = block(late_out[0], j + 1), block(late_sent, j)
 
-    both = lambda d: mine[d] + theirs[d].astype(F32)
-    a, b = right(end[:cut]), left(end[cut:])
+    split = width // 256 * 128
+    spans = [slice(0, split), slice(split, width)] if split else [slice(0, width)]
+    both = lambda d, s: mine[d][:, s] + theirs[d][:, s].astype(F32)
+    flow = [(right(end[:cut, s]), left(end[cut:, s])) for s in spans]
+    last = end
     for d in range(far - 1, 0, -1):
-        up = both(d)
-        up = jnp.concatenate([up[:cut] + a.astype(F32), up[cut:]], axis=0) if d == far - 1 else up + a.astype(F32)
-        up = up.astype(BF16)
-        b, _ = together((b, up))
-        down = both(-d)
-        down = jnp.concatenate([down[:cut], down[cut:] + b.astype(F32)], axis=0) if d == far - 1 else down + b.astype(F32)
-        down = down.astype(BF16)
-        a, _ = together((right(up), down))
-        b = left(down)
-    return (both(0) + a.astype(F32) + b.astype(F32)).astype(BF16)
+        for i, s in enumerate(spans):
+            up, down = both(d, s), both(-d, s)
+            a, _ = together((flow[i][0], last))
+            up = jnp.concatenate([up[:cut] + a.astype(F32), up[cut:]], axis=0) if d == far - 1 else up + a.astype(F32)
+            up = up.astype(BF16)
+            b, _ = together((flow[i][1], up))
+            down = jnp.concatenate([down[:cut], down[cut:] + b.astype(F32)], axis=0) if d == far - 1 else down + b.astype(F32)
+            last = down.astype(BF16)
+            flow[i] = right(up), left(last)
+    out = []
+    for (a, b), s in zip(flow, spans):
+        a, _ = together((a, last))
+        total = both(0, s) + a.astype(F32)
+        b, total = together((b, total))
+        last = (total + b.astype(F32)).astype(BF16)
+        out.append(last)
+    return jnp.concatenate(out, axis=1)
 
 
 def solution(mesh):

time: 67.8 us -> 70.7 us (1.043)
  starting transfers between devices: 20.7 us -> 29.1 us
  Pallas kernels: 21.5 us -> 14 us
  waiting for transfers between devices: 23.8 us -> 25.5 us
    ppermute x8 -> x12, starting transfers between devices: 7.8 us -> 16 us  [local(): left = lambda a: lax.ppermute(a, 'node', back)]
    ppermute x8 -> x12, waiting for transfers between devices: 4.26 us -> 11.9 us  [local(): left = lambda a: lax.ppermute(a, 'node', back)]
    pallas_call x5 -> x4, Pallas kernels: 15.9 us -> 8.33 us  [the longest x2 5.53 us: hidden(): pl.pallas_call(functools.partial(hidden_kernel, count, tiles(width, ff)[0...]
    ppermute x8 -> x12, waiting for transfers between devices: 18.7 us -> 12.7 us  [local(): right = lambda a: lax.ppermute(a, 'node', forth)]
    convert_element_type x3 -> x6, other arithmetic: 0.94 us -> 0.2 us  [the longest x4 0.15 us: local(): last = down.astype(BF16)]
    ppermute x8 -> x12, starting transfers between devices: 9.89 us -> 9.64 us  [local(): right = lambda a: lax.ppermute(a, 'node', forth)]
  transfers between devices with their start and end apart: 28 -> 36, of which waited for: 11 -> 18; matrix products, arithmetic and copies ran while one was open for 1% -> 1% of each run, Pallas kernels for 24% -> 12%
where the time goes in v8:
time: 70.7 us; the launch traced here: 70.6 us
  starting transfers between devices  29.1 us (41%)
  waiting for transfers between devices  25.5 us (36%)
  Pallas kernels  14 us (20%)
  other arithmetic  1.41 us (2%)
    ppermute x12, starting transfers between devices, local(): left = lambda a: lax.ppermute(a, 'node', back)  16 us
    ppermute x12, waiting for transfers between devices, local(): right = lambda a: lax.ppermute(a, 'node', forth)  12.7 us
    ppermute x12, waiting for transfers between devices, local(): left = lambda a: lax.ppermute(a, 'node', back)  11.9 us
    ppermute x12, starting transfers between devices, local(): right = lambda a: lax.ppermute(a, 'node', forth)  9.64 us
    pallas_call x2, Pallas kernels, hidden(): pl.pallas_call(functools.partial(hidden_kernel, count, tiles(width, ff)[0...  5.53 us
    pallas_call x1, Pallas kernels, expert(): pl.pallas_call(functools.partial(expert_kernel, count, experts, *tiles(wi...  4.56 us
    ppermute x12, starting transfers between devices, local(): sibling = lambda a: lax.ppermute(a, 'node', swap)  3.46 us
    pallas_call x2, Pallas kernels, output(): pl.pallas_call(functools.partial(output_kernel, count, experts, tiles(wid...  2.8 us
  transfers between devices with their start and end apart: 36, of which 18 were waited for; matrix products, arithmetic and copies ran while one was open for 1% of the time, Pallas kernels for 12%

profile of v8, /device:TPU:0, one launch (start us, length us, event | category | flops | bytes accessed | tf_op | source)
XLA Modules:
  0.0 70.6 jit_solution(9489695792508096411)
XLA Ops:
  0.0 1.1 %shard_map.64.refs_0_ = bf16[32,3712]{1,0:T(8,128)(2,1)S(1)} custom-call(bf16[32,3584]{1,0:T(8,128)(2,1)} %tok_hbm.1, s32[8,32]{1,0:T(8,128)} %bitcast.6, f32[8,32]{1,0:T(8,128)} %bitcast.7), custom_call_target="tpu_custom_call" | custom-call | flops 10737418240 | tf_op jit(solution)/shard_map/pallas_call | solution.py:61
  1.2 0.5 collective-permute-start.2
  1.7 2.6 %collective-permute-start.1 = (bf16[32,3712]{1,0:T(8,128)(2,1)S(1)}, bf16[32,3712]{1,0:T(8,128)(2,1)S(1)}, u32[]{:S(2)}, u32[]{:S(2)}) collective-permute-start(bf16[32,3712]{1,0:T(8,128)(2,1)S(1)} %shard_map.64.refs_0_), channel_id=1, source_target_pairs={{0,4},{1,5},{4,8},{5,9},{8,12},{9,13},{12,14},{13,15},{14,10},{15,... | collective-permute-start | bytes 712712 | tf_op jit(solution)/shard_map/ppermute | solution.py:202
  4.4 6.3 %collective-permute-done.1.refs_2_ = bf16[32,3712]{1,0:T(8,128)(2,1)S(1)} collective-permute-done((bf16[32,3712]{1,0:T(8,128)(2,1)S(1)}, bf16[32,3712]{1,0:T(8,128)(2,1)S(1)}, u32[]{:S(2)}, u32[]{:S(2)}) %collective-permute-start.1) | collective-permute-done | bytes 237600 | tf_op jit(solution)/shard_map/ppermute | solution.py:202
  10.7 1.5 %collective-permute-done.refs_1_ = bf16[32,3712]{1,0:T(8,128)(2,1)S(1)} collective-permute-done((bf16[32,3712]{1,0:T(8,128)(2,1)S(1)}, bf16[32,3712]{1,0:T(8,128)(2,1)S(1)}, u32[]{:S(2)}, u32[]{:S(2)}) %collective-permute-start) | collective-permute-done | bytes 237600 | tf_op jit(solution)/shard_map/ppermute | solution.py:203
  12.5 1.7 %collective-permute-start.4 = (bf16[32,3712]{1,0:T(8,128)(2,1)S(1)}, bf16[32,3712]{1,0:T(8,128)(2,1)S(1)}, u32[]{:S(2)}, u32[]{:S(2)}) collective-permute-start(bf16[32,3712]{1,0:T(8,128)(2,1)S(1)} %collective-permute-done.1.refs_2_), channel_id=1, source_target_pairs={{0,4},{1,5},{4,8},{5,9},{8,12},{9,13},{12,14},{13,15},{14,10},{15,... | collective-permute-start | bytes 712712 | tf_op jit(solution)/shard_map/ppermute | solution.py:202
  14.2 2.4 %shard_map.65.refs_4_ = bf16[128,1024]{1,0:T(8,128)(2,1)S(1)} custom-call(bf16[32,3712]{1,0:T(8,128)(2,1)S(1)} %shard_map.64.refs_0_, bf16[32,3712]{1,0:T(8,128)(2,1)S(1)} %collective-permute-done.refs_1_, bf16[32,3712]{1,0:T(8,128)(2,1)S(1)} %collective-permute-done.1.refs_2_, bf16[32,3712]{1,0:T(8,128)(2,1)S(1)} %collective-permute-done.2.refs_3_, ...), custom_call_target="tpu_custom_call" | custom-call | flops 3758096384 | tf_op jit(solution)/shard_map/pallas_call | solution.py:128
  16.7 0.5 collective-permute-start.8
  17.2 2.0 %collective-permute-done.3.refs_0_ = bf16[32,3712]{1,0:T(8,128)(2,1)S(1)} collective-permute-done((bf16[32,3712]{1,0:T(8,128)(2,1)S(1)}, bf16[32,3712]{1,0:T(8,128)(2,1)S(1)}, u32[]{:S(2)}, u32[]{:S(2)}) %collective-permute-start.3) | collective-permute-done | bytes 237600 | tf_op jit(solution)/shard_map/ppermute | solution.py:203
  19.5 1.6 %collective-permute-start.5 = (bf16[32,3712]{1,0:T(8,128)(2,1)S(1)}, bf16[32,3712]{1,0:T(8,128)(2,1)S(1)}, u32[]{:S(2)}, u32[]{:S(2)}) collective-permute-start(bf16[32,3712]{1,0:T(8,128)(2,1)S(1)} %collective-permute-done.3.refs_0_), channel_id=1, source_target_pairs={{4,0},{5,1},{8,4},{9,5},{12,8},{13,9},{14,12},{15,13},{10,14},{11,... | collective-permute-start | bytes 712712 | tf_op jit(solution)/shard_map/ppermute | solution.py:203
  21.0 0.5 collective-permute-start.6
  21.5 1.2 %shard_map.66 = (f32[96,3584]{1,0:T(8,128)S(1)}, bf16[32,3584]{1,0:T(8,128)(2,1)S(1)}) custom-call(bf16[32,3712]{1,0:T(8,128)(2,1)S(1)} %shard_map.64.refs_0_, bf16[32,3712]{1,0:T(8,128)(2,1)S(1)} %collective-permute-done.refs_1_, bf16[32,3712]{1,0:T(8,128)(2,1)S(1)} %collective-permute-done.1.refs_2_, bf16[32,3712]{1,0:T(8,128)(2,1)S(1)} %collective-permute-done.2.refs_3_, ...), custom_call_target="tpu_custom_call" | custom-call | flops 1879048192 | tf_op jit(solution)/shard_map/pallas_call | solution.py:152
  22.8 0.5 collective-permute-start.12
  23.3 2.3 %collective-permute-done.5.refs_1_ = bf16[32,3712]{1,0:T(8,128)(2,1)S(1)} collective-permute-done((bf16[32,3712]{1,0:T(8,128)(2,1)S(1)}, bf16[32,3712]{1,0:T(8,128)(2,1)S(1)}, u32[]{:S(2)}, u32[]{:S(2)}) %collective-permute-start.5) | collective-permute-done | bytes 237600 | tf_op jit(solution)/shard_map/ppermute | solution.py:203
  25.6 1.6 %collective-permute-done.6.refs_2_ = bf16[32,3712]{1,0:T(8,128)(2,1)S(1)} collective-permute-done((bf16[32,3712]{1,0:T(8,128)(2,1)S(1)}, bf16[32,3712]{1,0:T(8,128)(2,1)S(1)}, u32[]{:S(2)}, u32[]{:S(2)}) %collective-permute-start.6) | collective-permute-done | bytes 237600 | tf_op jit(solution)/shard_map/ppermute | solution.py:202
  27.2 1.6 %collective-permute-start.10 = (bf16[16,3712]{1,0:T(8,128)(2,1)S(1)}, bf16[16,3712]{1,0:T(8,128)(2,1)S(1)}, u32[]{:S(2)}, u32[]{:S(2)}) collective-permute-start(bf16[16,3712]{1,0:T(8,128)(2,1)S(1)} %slice.174), channel_id=1, source_target_pairs={{4,0},{5,1},{8,4},{9,5},{12,8},{13,9},{14,12},{15,13},{10,14},{11,... | collective-permute-start | bytes 356360 | tf_op jit(solution)/shard_map/ppermute | solution.py:203
  28.8 0.5 collective-permute-start.9
  29.3 3.2 %shard_map.67.refs_6_ = bf16[192,1024]{1,0:T(8,128)(2,1)S(1)} custom-call(bf16[32,3712]{1,0:T(8,128)(2,1)S(1)} %collective-permute-done.3.refs_0_, bf16[32,3712]{1,0:T(8,128)(2,1)S(1)} %collective-permute-done.4.refs_1_, bf16[32,3712]{1,0:T(8,128)(2,1)S(1)} %collective-permute-done.8.refs_2_, bf16[32,3712]{1,0:T(8,128)(2,1)S(1)} %collective-permute-done.7.refs_3_, ...), custom_call_target="tpu_custom_call" | custom-call | flops 3758096384 | tf_op jit(solution)/shard_map/pallas_call | solution.py:128
  32.5 0.5 collective-permute-start.15
  33.0 0.6 collective-permute-done.9
  33.8 0.5 collective-permute-start.16
  34.3 1.6 %shard_map.68 = (f32[64,3584]{1,0:T(8,128)S(1)}, bf16[128,3584]{1,0:T(8,128)(2,1)S(1)}) custom-call(bf16[32,3712]{1,0:T(8,128)(2,1)S(1)} %collective-permute-done.3.refs_0_, bf16[32,3712]{1,0:T(8,128)(2,1)S(1)} %collective-permute-done.4.refs_1_, bf16[32,3712]{1,0:T(8,128)(2,1)S(1)} %collective-permute-done.8.refs_2_, ...), custom_call_target="tpu_custom_call" | custom-call | flops 1879048192 | tf_op jit(solution)/shard_map/pallas_call | solution.py:152
  35.9 4.6 %shard_map.69 = (f32[96,3584]{1,0:T(8,128)S(1)}, bf16[32,3584]{1,0:T(8,128)(2,1)S(1)}, bf16[64,3584]{1,0:T(8,128)(2,1)S(1)}) custom-call(bf16[32,3712]{1,0:T(8,128)(2,1)S(1)} %constant_dynamic-update-slice_fusion.refs_0_, bf16[32,3712]{1,0:T(8,128)(2,1)S(1)} %collective-permute-done.5.refs_1_, bf16[32,3712]{1,0:T(8,128)(2,1)S(1)} %collective-permute-done.6.refs_2_, ...), custom_call_target="tpu_custom_call" | custom-call | flops 5637144576 | tf_op jit(solution)/shard_map/pallas_call | solution.py:178
  41.2 0.9 %collective-permute-done.19 = bf16[32,3584]{1,0:T(8,128)(2,1)S(1)} collective-permute-done((bf16[32,3584]{1,0:T(8,128)(2,1)S(1)}, bf16[32,3584]{1,0:T(8,128)(2,1)S(1)}, u32[]{:S(2)}, u32[]{:S(2)}) %collective-permute-start.19) | collective-permute-done | bytes 229408 | tf_op jit(solution)/shard_map/ppermute | solution.py:204
  42.1 0.5 collective-permute-start.21
  42.6 0.9 %collective-permute-start.25 = (bf16[16,1792]{1,0:T(8,128)(2,1)S(1)}, bf16[16,1792]{1,0:T(8,128)(2,1)S(1)}, u32[]{:S(2)}, u32[]{:S(2)}) collective-permute-start(bf16[16,1792]{1,0:T(8,128)(2,1)S(1)} %get-tuple-element.130), channel_id=1, source_target_pairs={{0,4},{1,5},{4,8},{5,9},{8,12},{9,13},{12,14},{13,15},{14,10},{15,... | collective-permute-start | bytes 172040 | tf_op jit(solution)/shard_map/ppermute | solution.py:202
  43.5 1.2 %collective-permute-start.24 = (bf16[16,1792]{1,0:T(8,128)(2,1)S(1)}, bf16[16,1792]{1,0:T(8,128)(2,1)S(1)}, u32[]{:S(2)}, u32[]{:S(2)}) collective-permute-start(bf16[16,1792]{1,0:T(8,128)(2,1)S(1)} %get-tuple-element.131), channel_id=1, source_target_pairs={{4,0},{5,1},{8,4},{9,5},{12,8},{13,9},{14,12},{15,13},{10,14},{11,... | collective-permute-start | bytes 172040 | tf_op jit(solution)/shard_map/ppermute | solution.py:203
  44.7 2.1 %collective-permute-done.21 = bf16[16,1792]{1,0:T(8,128)(2,1)S(1)} collective-permute-done((bf16[16,1792]{1,0:T(8,128)(2,1)S(1)}, bf16[16,1792]{1,0:T(8,128)(2,1)S(1)}, u32[]{:S(2)}, u32[]{:S(2)}) %collective-permute-start.21) | collective-permute-done | bytes 57376 | tf_op jit(solution)/shard_map/ppermute | solution.py:202
  46.8 1.6 %collective-permute-start.20 = (bf16[16,1792]{1,0:T(8,128)(2,1)S(1)}, bf16[16,1792]{1,0:T(8,128)(2,1)S(1)}, u32[]{:S(2)}, u32[]{:S(2)}) collective-permute-start(bf16[16,1792]{1,0:T(8,128)(2,1)S(1)} %get-tuple-element.132), channel_id=1, source_target_pairs={{4,0},{5,1},{8,4},{9,5},{12,8},{13,9},{14,12},{15,13},{10,14},{11,... | collective-permute-start | bytes 172040 | tf_op jit(solution)/shard_map/ppermute | solution.py:203
  48.5 0.5 collective-permute-start.23
  49.0 1.9 %collective-permute-done.20 = bf16[16,1792]{1,0:T(8,128)(2,1)S(1)} collective-permute-done((bf16[16,1792]{1,0:T(8,128)(2,1)S(1)}, bf16[16,1792]{1,0:T(8,128)(2,1)S(1)}, u32[]{:S(2)}, u32[]{:S(2)}) %collective-permute-start.20) | collective-permute-done | bytes 57376 | tf_op jit(solution)/shard_map/ppermute | solution.py:203
  51.0 1.6 %collective-permute-start.22 = (bf16[32,1792]{1,0:T(8,128)(2,1)S(1)}, bf16[32,1792]{1,0:T(8,128)(2,1)S(1)}, u32[]{:S(2)}, u32[]{:S(2)}) collective-permute-start(bf16[32,1792]{1,0:T(8,128)(2,1)S(1)} %pad_maximum_fusion.2), channel_id=1, source_target_pairs={{4,0},{5,1},{8,4},{9,5},{12,8},{13,9},{14,12},{15,13},{10,14},{11,... | collective-permute-start | bytes 344072 | tf_op jit(solution)/shard_map/ppermute | solution.py:203
  52.7 0.5 collective-permute-start.29
  53.2 1.6 %collective-permute-start.28 = (bf16[32,1792]{1,0:T(8,128)(2,1)S(1)}, bf16[32,1792]{1,0:T(8,128)(2,1)S(1)}, u32[]{:S(2)}, u32[]{:S(2)}) collective-permute-start(bf16[32,1792]{1,0:T(8,128)(2,1)S(1)} %pad_maximum_fusion.4), channel_id=1, source_target_pairs={{4,0},{5,1},{8,4},{9,5},{12,8},{13,9},{14,12},{15,13},{10,14},{11,... | collective-permute-start | bytes 344072 | tf_op jit(solution)/shard_map/ppermute | solution.py:203
  54.9 0.5 collective-permute-start.27
  55.4 1.2 %collective-permute-done.22 = bf16[32,1792]{1,0:T(8,128)(2,1)S(1)} collective-permute-done((bf16[32,1792]{1,0:T(8,128)(2,1)S(1)}, bf16[32,1792]{1,0:T(8,128)(2,1)S(1)}, u32[]{:S(2)}, u32[]{:S(2)}) %collective-permute-start.22) | collective-permute-done | bytes 114720 | tf_op jit(solution)/shard_map/ppermute | solution.py:203
  56.7 1.6 %collective-permute-start.26 = (bf16[32,1792]{1,0:T(8,128)(2,1)S(1)}, bf16[32,1792]{1,0:T(8,128)(2,1)S(1)}, u32[]{:S(2)}, u32[]{:S(2)}) collective-permute-start(bf16[32,1792]{1,0:T(8,128)(2,1)S(1)} %add_convert_fusion.9), channel_id=1, source_target_pairs={{4,0},{5,1},{8,4},{9,5},{12,8},{13,9},{14,12},{15,13},{10,14},{11,... | collective-permute-start | bytes 344072 | tf_op jit(solution)/shard_map/ppermute | solution.py:203
  58.4 0.5 collective-permute-start.33
  59.3 1.6 %collective-permute-start.32 = (bf16[32,1792]{1,0:T(8,128)(2,1)S(1)}, bf16[32,1792]{1,0:T(8,128)(2,1)S(1)}, u32[]{:S(2)}, u32[]{:S(2)}) collective-permute-start(bf16[32,1792]{1,0:T(8,128)(2,1)S(1)} %add_convert_fusion.7), channel_id=1, source_target_pairs={{4,0},{5,1},{8,4},{9,5},{12,8},{13,9},{14,12},{15,13},{10,14},{11,... | collective-permute-start | bytes 344072 | tf_op jit(solution)/shard_map/ppermute | solution.py:203
  61.1 0.5 collective-permute-start.31
  61.6 1.0 %collective-permute-done.26 = bf16[32,1792]{1,0:T(8,128)(2,1)S(1)} collective-permute-done((bf16[32,1792]{1,0:T(8,128)(2,1)S(1)}, bf16[32,1792]{1,0:T(8,128)(2,1)S(1)}, u32[]{:S(2)}, u32[]{:S(2)}) %collective-permute-start.26) | collective-permute-done | bytes 114720 | tf_op jit(solution)/shard_map/ppermute | solution.py:203
  62.6 1.6 %collective-permute-start.30 = (bf16[32,1792]{1,0:T(8,128)(2,1)S(1)}, bf16[32,1792]{1,0:T(8,128)(2,1)S(1)}, u32[]{:S(2)}, u32[]{:S(2)}) collective-permute-start(bf16[32,1792]{1,0:T(8,128)(2,1)S(1)} %add_convert_fusion.5), channel_id=1, source_target_pairs={{4,0},{5,1},{8,4},{9,5},{12,8},{13,9},{14,12},{15,13},{10,14},{11,... | collective-permute-start | bytes 344072 | tf_op jit(solution)/shard_map/ppermute | solution.py:203
  64.3 0.5 collective-permute-start.35
  65.0 1.6 %collective-permute-start.34 = (bf16[32,1792]{1,0:T(8,128)(2,1)S(1)}, bf16[32,1792]{1,0:T(8,128)(2,1)S(1)}, u32[]{:S(2)}, u32[]{:S(2)}) collective-permute-start(bf16[32,1792]{1,0:T(8,128)(2,1)S(1)} %add_convert_fusion.3), channel_id=1, source_target_pairs={{4,0},{5,1},{8,4},{9,5},{12,8},{13,9},{14,12},{15,13},{10,14},{11,... | collective-permute-start | bytes 344072 | tf_op jit(solution)/shard_map/ppermute | solution.py:203
  66.7 0.8 %collective-permute-done.30 = bf16[32,1792]{1,0:T(8,128)(2,1)S(1)} collective-permute-done((bf16[32,1792]{1,0:T(8,128)(2,1)S(1)}, bf16[32,1792]{1,0:T(8,128)(2,1)S(1)}, u32[]{:S(2)}, u32[]{:S(2)}) %collective-permute-start.30) | collective-permute-done | bytes 114720 | tf_op jit(solution)/shard_map/ppermute | solution.py:203
  67.5 1.6 %collective-permute-done.35 = bf16[32,1792]{1,0:T(8,128)(2,1)S(1)} collective-permute-done((bf16[32,1792]{1,0:T(8,128)(2,1)S(1)}, bf16[32,1792]{1,0:T(8,128)(2,1)S(1)}, u32[]{:S(2)}, u32[]{:S(2)}) %collective-permute-start.35) | collective-permute-done | bytes 114720 | tf_op jit(solution)/shard_map/ppermute | solution.py:202
  69.1 0.7 collective-permute-done.34
  69.9 0.7 pad_maximum_fusion
  (74 shorter events, 3.1 us)
Async XLA Ops:
  0.0 14.2 %slice-start = ((s8[7340032]{0:T(1024)(128)(4,1)}), s8[4194304]{0:T(1024)(128)(4,1)S(1)}, s32[]{:S(2)}) async-start(s8[7340032]{0:T(1024)(128)(4,1)} %bitcast.2), calls=%async_computation | async-start | bytes 8388608
  0.0 14.2 %slice-start.2 = ((s8[7340032]{0:T(1024)(128)(4,1)}), s8[4194304]{0:T(1024)(128)(4,1)S(1)}, s32[]{:S(2)}) async-start(s8[7340032]{0:T(1024)(128)(4,1)} %bitcast.4), calls=%async_computation.2 | async-start | bytes 8388608
  0.0 14.2 %slice-start.1 = ((s8[7340032]{0:T(1024)(128)(4,1)}), s8[3145728]{0:T(1024)(128)(4,1)S(1)}, s32[]{:S(2)}) async-start(s8[7340032]{0:T(1024)(128)(4,1)} %bitcast.2), calls=%async_computation.1 | async-start | bytes 6291456
  0.0 14.2 %slice-start.3 = ((s8[7340032]{0:T(1024)(128)(4,1)}), s8[3145728]{0:T(1024)(128)(4,1)S(1)}, s32[]{:S(2)}) async-start(s8[7340032]{0:T(1024)(128)(4,1)} %bitcast.4), calls=%async_computation.3 | async-start | bytes 6291456
  1.2 3.2 %collective-permute-start.2 = (bf16[32,3712]{1,0:T(8,128)(2,1)S(1)}, bf16[32,3712]{1,0:T(8,128)(2,1)S(1)}, u32[]{:S(2)}, u32[]{:S(2)}) collective-permute-start(bf16[32,3712]{1,0:T(8,128)(2,1)S(1)} %shard_map.64.refs_0_), channel_id=1, source_target_pairs={{0,1},{1,0},{2,3},{3,2},{4,5},{5,4},{6,7},{7,6},{8,9},{9,8},{10,11... | collective-permute-start | bytes 712712 | tf_op jit(solution)/shard_map/ppermute | solution.py:204
  1.7 9.0 %collective-permute-start.1 = (bf16[32,3712]{1,0:T(8,128)(2,1)S(1)}, bf16[32,3712]{1,0:T(8,128)(2,1)S(1)}, u32[]{:S(2)}, u32[]{:S(2)}) collective-permute-start(bf16[32,3712]{1,0:T(8,128)(2,1)S(1)} %shard_map.64.refs_0_), channel_id=1, source_target_pairs={{0,4},{1,5},{4,8},{5,9},{8,12},{9,13},{12,14},{13,15},{14,10},{15,... | collective-permute-start | bytes 712712 | tf_op jit(solution)/shard_map/ppermute | solution.py:202
  4.3 7.8 %collective-permute-start = (bf16[32,3712]{1,0:T(8,128)(2,1)S(1)}, bf16[32,3712]{1,0:T(8,128)(2,1)S(1)}, u32[]{:S(2)}, u32[]{:S(2)}) collective-permute-start(bf16[32,3712]{1,0:T(8,128)(2,1)S(1)} %shard_map.64.refs_0_), channel_id=1, source_target_pairs={{4,0},{5,1},{8,4},{9,5},{12,8},{13,9},{14,12},{15,13},{10,14},{11,... | collective-permute-start | bytes 712712 | tf_op jit(solution)/shard_map/ppermute | solution.py:203
  12.2 7.0 %collective-permute-start.3 = (bf16[32,3712]{1,0:T(8,128)(2,1)S(1)}, bf16[32,3712]{1,0:T(8,128)(2,1)S(1)}, u32[]{:S(2)}, u32[]{:S(2)}) collective-permute-start(bf16[32,3712]{1,0:T(8,128)(2,1)S(1)} %collective-permute-done.refs_1_), channel_id=1, source_target_pairs={{4,0},{5,1},{8,4},{9,5},{12,8},{13,9},{14,12},{15,13},{10,14},{11,... | collective-permute-start | bytes 712712 | tf_op jit(solution)/shard_map/ppermute | solution.py:203
  12.5 7.0 %collective-permute-start.4 = (bf16[32,3712]{1,0:T(8,128)(2,1)S(1)}, bf16[32,3712]{1,0:T(8,128)(2,1)S(1)}, u32[]{:S(2)}, u32[]{:S(2)}) collective-permute-start(bf16[32,3712]{1,0:T(8,128)(2,1)S(1)} %collective-permute-done.1.refs_2_), channel_id=1, source_target_pairs={{0,4},{1,5},{4,8},{5,9},{8,12},{9,13},{12,14},{13,15},{14,10},{15,... | collective-permute-start | bytes 712712 | tf_op jit(solution)/shard_map/ppermute | solution.py:202
  14.2 7.3 %copy-start = (bf16[1,1024,3584]{2,1,0:T(8,128)(2,1)S(1)}, bf16[1,1024,3584]{2,1,0:T(8,128)(2,1)}, u32[]{:S(2)}) copy-start(bf16[1,1024,3584]{2,1,0:T(8,128)(2,1)} %refs_8_.1) | copy-start | bytes 22020100
  16.6 6.2 %collective-permute-start.7 = (bf16[32,3712]{1,0:T(8,128)(2,1)S(1)}, bf16[32,3712]{1,0:T(8,128)(2,1)S(1)}, u32[]{:S(2)}, u32[]{:S(2)}) collective-permute-start(bf16[32,3712]{1,0:T(8,128)(2,1)S(1)} %collective-permute-done.1.refs_2_), channel_id=1, source_target_pairs={{0,1},{1,0},{2,3},{3,2},{4,5},{5,4},{6,7},{7,6},{8,9},{9,8},{10,11... | collective-permute-start | bytes 712712 | tf_op jit(solution)/shard_map/ppermute | solution.py:204
  16.7 6.6 %collective-permute-start.8 = (bf16[32,3712]{1,0:T(8,128)(2,1)S(1)}, bf16[32,3712]{1,0:T(8,128)(2,1)S(1)}, u32[]{:S(2)}, u32[]{:S(2)}) collective-permute-start(bf16[32,3712]{1,0:T(8,128)(2,1)S(1)} %collective-permute-done.refs_1_), channel_id=1, source_target_pairs={{0,1},{1,0},{2,3},{3,2},{4,5},{5,4},{6,7},{7,6},{8,9},{9,8},{10,11... | collective-permute-start | bytes 712712 | tf_op jit(solution)/shard_map/ppermute | solution.py:204
  19.5 6.1 %collective-permute-start.5 = (bf16[32,3712]{1,0:T(8,128)(2,1)S(1)}, bf16[32,3712]{1,0:T(8,128)(2,1)S(1)}, u32[]{:S(2)}, u32[]{:S(2)}) collective-permute-start(bf16[32,3712]{1,0:T(8,128)(2,1)S(1)} %collective-permute-done.3.refs_0_), channel_id=1, source_target_pairs={{4,0},{5,1},{8,4},{9,5},{12,8},{13,9},{14,12},{15,13},{10,14},{11,... | collective-permute-start | bytes 712712 | tf_op jit(solution)/shard_map/ppermute | solution.py:203
  21.0 6.1 %collective-permute-start.6 = (bf16[32,3712]{1,0:T(8,128)(2,1)S(1)}, bf16[32,3712]{1,0:T(8,128)(2,1)S(1)}, u32[]{:S(2)}, u32[]{:S(2)}) collective-permute-start(bf16[32,3712]{1,0:T(8,128)(2,1)S(1)} %collective-permute-done.4.refs_1_), channel_id=1, source_target_pairs={{0,4},{1,5},{4,8},{5,9},{8,12},{9,13},{12,14},{13,15},{14,10},{15,... | collective-permute-start | bytes 712712 | tf_op jit(solution)/shard_map/ppermute | solution.py:202
  22.7 6.6 %collective-permute-start.11 = (bf16[32,3712]{1,0:T(8,128)(2,1)S(1)}, bf16[32,3712]{1,0:T(8,128)(2,1)S(1)}, u32[]{:S(2)}, u32[]{:S(2)}) collective-permute-start(bf16[32,3712]{1,0:T(8,128)(2,1)S(1)} %collective-permute-done.4.refs_1_), channel_id=1, source_target_pairs={{0,1},{1,0},{2,3},{3,2},{4,5},{5,4},{6,7},{7,6},{8,9},{9,8},{10,11... | collective-permute-start | bytes 712712 | tf_op jit(solution)/shard_map/ppermute | solution.py:204
  22.8 6.5 %collective-permute-start.12 = (bf16[32,3712]{1,0:T(8,128)(2,1)S(1)}, bf16[32,3712]{1,0:T(8,128)(2,1)S(1)}, u32[]{:S(2)}, u32[]{:S(2)}) collective-permute-start(bf16[32,3712]{1,0:T(8,128)(2,1)S(1)} %collective-permute-done.3.refs_0_), channel_id=1, source_target_pairs={{0,1},{1,0},{2,3},{3,2},{4,5},{5,4},{6,7},{7,6},{8,9},{9,8},{10,11... | collective-permute-start | bytes 712712 | tf_op jit(solution)/shard_map/ppermute | solution.py:204
  27.2 5.8 %collective-permute-start.10 = (bf16[16,3712]{1,0:T(8,128)(2,1)S(1)}, bf16[16,3712]{1,0:T(8,128)(2,1)S(1)}, u32[]{:S(2)}, u32[]{:S(2)}) collective-permute-start(bf16[16,3712]{1,0:T(8,128)(2,1)S(1)} %slice.174), channel_id=1, source_target_pairs={{4,0},{5,1},{8,4},{9,5},{12,8},{13,9},{14,12},{15,13},{10,14},{11,... | collective-permute-start | bytes 356360 | tf_op jit(solution)/shard_map/ppermute | solution.py:203
  28.8 4.8 %collective-permute-start.9 = (bf16[16,3712]{1,0:T(8,128)(2,1)S(1)}, bf16[16,3712]{1,0:T(8,128)(2,1)S(1)}, u32[]{:S(2)}, u32[]{:S(2)}) collective-permute-start(bf16[16,3712]{1,0:T(8,128)(2,1)S(1)} %slice.173), channel_id=1, source_target_pairs={{0,4},{1,5},{4,8},{5,9},{8,12},{9,13},{12,14},{13,15},{14,10},{15,... | collective-permute-start | bytes 356360 | tf_op jit(solution)/shard_map/ppermute | solution.py:202
  32.4 3.5 %collective-permute-start.14 = (bf16[32,3712]{1,0:T(8,128)(2,1)S(1)}, bf16[32,3712]{1,0:T(8,128)(2,1)S(1)}, u32[]{:S(2)}, u32[]{:S(2)}) collective-permute-start(bf16[32,3712]{1,0:T(8,128)(2,1)S(1)} %collective-permute-done.6.refs_2_), channel_id=1, source_target_pairs={{0,1},{1,0},{2,3},{3,2},{4,5},{5,4},{6,7},{7,6},{8,9},{9,8},{10,11... | collective-permute-start | bytes 712712 | tf_op jit(solution)/shard_map/ppermute | solution.py:204
  32.5 3.4 %collective-permute-start.15 = (bf16[32,3712]{1,0:T(8,128)(2,1)S(1)}, bf16[32,3712]{1,0:T(8,128)(2,1)S(1)}, u32[]{:S(2)}, u32[]{:S(2)}) collective-permute-start(bf16[32,3712]{1,0:T(8,128)(2,1)S(1)} %collective-permute-done.5.refs_1_), channel_id=1, source_target_pairs={{0,1},{1,0},{2,3},{3,2},{4,5},{5,4},{6,7},{7,6},{8,9},{9,8},{10,11... | collective-permute-start | bytes 712712 | tf_op jit(solution)/shard_map/ppermute | solution.py:204
  33.7 2.2 %collective-permute-start.13 = (bf16[32,3712]{1,0:T(8,128)(2,1)S(1)}, bf16[32,3712]{1,0:T(8,128)(2,1)S(1)}, u32[]{:S(2)}, u32[]{:S(2)}) collective-permute-start(bf16[32,3712]{1,0:T(8,128)(2,1)S(1)} %constant_dynamic-update-slice_fusion.refs_0_), channel_id=1, source_target_pairs={{0,1},{1,0},{2,3},{3,2},{4,5},{5,4},{6,7},{7,6},{8,9},{9,8},{10,11... | collective-permute-start | bytes 712712 | tf_op jit(solution)/shard_map/ppermute | solution.py:204
  33.8 2.1 %collective-permute-start.16 = (bf16[32,3584]{1,0:T(8,128)(2,1)S(1)}, bf16[32,3584]{1,0:T(8,128)(2,1)S(1)}, u32[]{:S(2)}, u32[]{:S(2)}) collective-permute-start(bf16[32,3584]{1,0:T(8,128)(2,1)S(1)} %get-tuple-element.95), channel_id=1, source_target_pairs={{0,1},{1,0},{2,3},{3,2},{4,5},{5,4},{6,7},{7,6},{8,9},{9,8},{10,11... | collective-permute-start | bytes 688136 | tf_op jit(solution)/shard_map/ppermute | solution.py:204
  40.5 1.6 %collective-permute-start.19 = (bf16[32,3584]{1,0:T(8,128)(2,1)S(1)}, bf16[32,3584]{1,0:T(8,128)(2,1)S(1)}, u32[]{:S(2)}, u32[]{:S(2)}) collective-permute-start(bf16[32,3584]{1,0:T(8,128)(2,1)S(1)} %get-tuple-element.102), channel_id=1, source_target_pairs={{0,1},{1,0},{2,3},{3,2},{4,5},{5,4},{6,7},{7,6},{8,9},{9,8},{10,11... | collective-permute-start | bytes 688136 | tf_op jit(solution)/shard_map/ppermute | solution.py:204
  40.7 7.7 %collective-permute-start.17 = (bf16[64,3584]{1,0:T(8,128)(2,1)S(1)}, bf16[64,3584]{1,0:T(8,128)(2,1)S(1)}, u32[]{:S(2)}, u32[]{:S(2)}) collective-permute-start(bf16[64,3584]{1,0:T(8,128)(2,1)S(1)} %get-tuple-element.99), channel_id=1, source_target_pairs={{0,1},{1,0},{2,3},{3,2},{4,5},{5,4},{6,7},{7,6},{8,9},{9,8},{10,11... | collective-permute-start | bytes 1376264 | tf_op jit(solution)/shard_map/ppermute | solution.py:204
  41.1 7.3 %collective-permute-start.18 = (bf16[128,3584]{1,0:T(8,128)(2,1)S(1)}, bf16[128,3584]{1,0:T(8,128)(2,1)S(1)}, u32[]{:S(2)}, u32[]{:S(2)}) collective-permute-start(bf16[128,3584]{1,0:T(8,128)(2,1)S(1)} %get-tuple-element.100), channel_id=1, source_target_pairs={{0,1},{1,0},{2,3},{3,2},{4,5},{5,4},{6,7},{7,6},{8,9},{9,8},{10,11... | collective-permute-start | bytes 2752520 | tf_op jit(solution)/shard_map/ppermute | solution.py:204
  42.1 4.6 %collective-permute-start.21 = (bf16[16,1792]{1,0:T(8,128)(2,1)S(1)}, bf16[16,1792]{1,0:T(8,128)(2,1)S(1)}, u32[]{:S(2)}, u32[]{:S(2)}) collective-permute-start(bf16[16,1792]{1,0:T(8,128)(2,1)S(1)} %get-tuple-element.129), channel_id=1, source_target_pairs={{0,4},{1,5},{4,8},{5,9},{8,12},{9,13},{12,14},{13,15},{14,10},{15,... | collective-permute-start | bytes 172040 | tf_op jit(solution)/shard_map/ppermute | solution.py:202
  42.6 10.0 %collective-permute-start.25 = (bf16[16,1792]{1,0:T(8,128)(2,1)S(1)}, bf16[16,1792]{1,0:T(8,128)(2,1)S(1)}, u32[]{:S(2)}, u32[]{:S(2)}) collective-permute-start(bf16[16,1792]{1,0:T(8,128)(2,1)S(1)} %get-tuple-element.130), channel_id=1, source_target_pairs={{0,4},{1,5},{4,8},{5,9},{8,12},{9,13},{12,14},{13,15},{14,10},{15,... | collective-permute-start | bytes 172040 | tf_op jit(solution)/shard_map/ppermute | solution.py:202
  43.5 9.7 %collective-permute-start.24 = (bf16[16,1792]{1,0:T(8,128)(2,1)S(1)}, bf16[16,1792]{1,0:T(8,128)(2,1)S(1)}, u32[]{:S(2)}, u32[]{:S(2)}) collective-permute-start(bf16[16,1792]{1,0:T(8,128)(2,1)S(1)} %get-tuple-element.131), channel_id=1, source_target_pairs={{4,0},{5,1},{8,4},{9,5},{12,8},{13,9},{14,12},{15,13},{10,14},{11,... | collective-permute-start | bytes 172040 | tf_op jit(solution)/shard_map/ppermute | solution.py:203
  46.8 4.2 %collective-permute-start.20 = (bf16[16,1792]{1,0:T(8,128)(2,1)S(1)}, bf16[16,1792]{1,0:T(8,128)(2,1)S(1)}, u32[]{:S(2)}, u32[]{:S(2)}) collective-permute-start(bf16[16,1792]{1,0:T(8,128)(2,1)S(1)} %get-tuple-element.132), channel_id=1, source_target_pairs={{4,0},{5,1},{8,4},{9,5},{12,8},{13,9},{14,12},{15,13},{10,14},{11,... | collective-permute-start | bytes 172040 | tf_op jit(solution)/shard_map/ppermute | solution.py:203
  48.5 6.4 %collective-permute-start.23 = (bf16[32,1792]{1,0:T(8,128)(2,1)S(1)}, bf16[32,1792]{1,0:T(8,128)(2,1)S(1)}, u32[]{:S(2)}, u32[]{:S(2)}) collective-permute-start(bf16[32,1792]{1,0:T(8,128)(2,1)S(1)} %pad_maximum_fusion.1), channel_id=1, source_target_pairs={{0,4},{1,5},{4,8},{5,9},{8,12},{9,13},{12,14},{13,15},{14,10},{15,... | collective-permute-start | bytes 344072 | tf_op jit(solution)/shard_map/ppermute | solution.py:202
  51.0 5.6 %collective-permute-start.22 = (bf16[32,1792]{1,0:T(8,128)(2,1)S(1)}, bf16[32,1792]{1,0:T(8,128)(2,1)S(1)}, u32[]{:S(2)}, u32[]{:S(2)}) collective-permute-start(bf16[32,1792]{1,0:T(8,128)(2,1)S(1)} %pad_maximum_fusion.2), channel_id=1, source_target_pairs={{4,0},{5,1},{8,4},{9,5},{12,8},{13,9},{14,12},{15,13},{10,14},{11,... | collective-permute-start | bytes 344072 | tf_op jit(solution)/shard_map/ppermute | solution.py:203
  52.7 5.6 %collective-permute-start.29 = (bf16[32,1792]{1,0:T(8,128)(2,1)S(1)}, bf16[32,1792]{1,0:T(8,128)(2,1)S(1)}, u32[]{:S(2)}, u32[]{:S(2)}) collective-permute-start(bf16[32,1792]{1,0:T(8,128)(2,1)S(1)} %pad_maximum_fusion.3), channel_id=1, source_target_pairs={{0,4},{1,5},{4,8},{5,9},{8,12},{9,13},{12,14},{13,15},{14,10},{15,... | collective-permute-start | bytes 344072 | tf_op jit(solution)/shard_map/ppermute | solution.py:202
  53.2 6.0 %collective-permute-start.28 = (bf16[32,1792]{1,0:T(8,128)(2,1)S(1)}, bf16[32,1792]{1,0:T(8,128)(2,1)S(1)}, u32[]{:S(2)}, u32[]{:S(2)}) collective-permute-start(bf16[32,1792]{1,0:T(8,128)(2,1)S(1)} %pad_maximum_fusion.4), channel_id=1, source_target_pairs={{4,0},{5,1},{8,4},{9,5},{12,8},{13,9},{14,12},{15,13},{10,14},{11,... | collective-permute-start | bytes 344072 | tf_op jit(solution)/shard_map/ppermute | solution.py:203
  54.9 6.1 %collective-permute-start.27 = (bf16[32,1792]{1,0:T(8,128)(2,1)S(1)}, bf16[32,1792]{1,0:T(8,128)(2,1)S(1)}, u32[]{:S(2)}, u32[]{:S(2)}) collective-permute-start(bf16[32,1792]{1,0:T(8,128)(2,1)S(1)} %add_convert_fusion.10), channel_id=1, source_target_pairs={{0,4},{1,5},{4,8},{5,9},{8,12},{9,13},{12,14},{13,15},{14,10},{15,... | collective-permute-start | bytes 344072 | tf_op jit(solution)/shard_map/ppermute | solution.py:202
  56.7 5.9 %collective-permute-start.26 = (bf16[32,1792]{1,0:T(8,128)(2,1)S(1)}, bf16[32,1792]{1,0:T(8,128)(2,1)S(1)}, u32[]{:S(2)}, u32[]{:S(2)}) collective-permute-start(bf16[32,1792]{1,0:T(8,128)(2,1)S(1)} %add_convert_fusion.9), channel_id=1, source_target_pairs={{4,0},{5,1},{8,4},{9,5},{12,8},{13,9},{14,12},{15,13},{10,14},{11,... | collective-permute-start | bytes 344072 | tf_op jit(solution)/shard_map/ppermute | solution.py:203
  58.4 5.9 %collective-permute-start.33 = (bf16[32,1792]{1,0:T(8,128)(2,1)S(1)}, bf16[32,1792]{1,0:T(8,128)(2,1)S(1)}, u32[]{:S(2)}, u32[]{:S(2)}) collective-permute-start(bf16[32,1792]{1,0:T(8,128)(2,1)S(1)} %add_convert_fusion.8), channel_id=1, source_target_pairs={{0,4},{1,5},{4,8},{5,9},{8,12},{9,13},{12,14},{13,15},{14,10},{15,... | collective-permute-start | bytes 344072 | tf_op jit(solution)/shard_map/ppermute | solution.py:202
  59.3 5.7 %collective-permute-start.32 = (bf16[32,1792]{1,0:T(8,128)(2,1)S(1)}, bf16[32,1792]{1,0:T(8,128)(2,1)S(1)}, u32[]{:S(2)}, u32[]{:S(2)}) collective-permute-start(bf16[32,1792]{1,0:T(8,128)(2,1)S(1)} %add_convert_fusion.7), channel_id=1, source_target_pairs={{4,0},{5,1},{8,4},{9,5},{12,8},{13,9},{14,12},{15,13},{10,14},{11,... | collective-permute-start | bytes 344072 | tf_op jit(solution)/shard_map/ppermute | solution.py:203
  61.1 5.5 %collective-permute-start.31 = (bf16[32,1792]{1,0:T(8,128)(2,1)S(1)}, bf16[32,1792]{1,0:T(8,128)(2,1)S(1)}, u32[]{:S(2)}, u32[]{:S(2)}) collective-permute-start(bf16[32,1792]{1,0:T(8,128)(2,1)S(1)} %add_convert_fusion.6), channel_id=1, source_target_pairs={{0,4},{1,5},{4,8},{5,9},{8,12},{9,13},{12,14},{13,15},{14,10},{15,... | collective-permute-start | bytes 344072 | tf_op jit(solution)/shard_map/ppermute | solution.py:202
  62.6 4.8 %collective-permute-start.30 = (bf16[32,1792]{1,0:T(8,128)(2,1)S(1)}, bf16[32,1792]{1,0:T(8,128)(2,1)S(1)}, u32[]{:S(2)}, u32[]{:S(2)}) collective-permute-start(bf16[32,1792]{1,0:T(8,128)(2,1)S(1)} %add_convert_fusion.5), channel_id=1, source_target_pairs={{4,0},{5,1},{8,4},{9,5},{12,8},{13,9},{14,12},{15,13},{10,14},{11,... | collective-permute-start | bytes 344072 | tf_op jit(solution)/shard_map/ppermute | solution.py:203
  64.3 4.8 %collective-permute-start.35 = (bf16[32,1792]{1,0:T(8,128)(2,1)S(1)}, bf16[32,1792]{1,0:T(8,128)(2,1)S(1)}, u32[]{:S(2)}, u32[]{:S(2)}) collective-permute-start(bf16[32,1792]{1,0:T(8,128)(2,1)S(1)} %add_convert_fusion.4), channel_id=1, source_target_pairs={{0,4},{1,5},{4,8},{5,9},{8,12},{9,13},{12,14},{13,15},{14,10},{15,... | collective-permute-start | bytes 344072 | tf_op jit(solution)/shard_map/ppermute | solution.py:202
  65.0 4.8 %collective-permute-start.34 = (bf16[32,1792]{1,0:T(8,128)(2,1)S(1)}, bf16[32,1792]{1,0:T(8,128)(2,1)S(1)}, u32[]{:S(2)}, u32[]{:S(2)}) collective-permute-start(bf16[32,1792]{1,0:T(8,128)(2,1)S(1)} %add_convert_fusion.3), channel_id=1, source_target_pairs={{4,0},{5,1},{8,4},{9,5},{12,8},{13,9},{14,12},{15,13},{10,14},{11,... | collective-permute-start | bytes 344072 | tf_op jit(solution)/shard_map/ppermute | solution.py:203

commit v9 on v3

v9 whole, which is shorter than its diff:
```python
import functools

import jax
import jax.numpy as jnp
from jax import lax
from jax.experimental import pallas as pl
from jax.experimental.pallas import tpu as pltpu
from jax.sharding import PartitionSpec as P

F32, BF16 = jnp.float32, jnp.bfloat16
SCRATCH = 20 * 2**20
GROUP = 8


def chip_order(mesh):
    names = list(mesh.axis_names)
    count = mesh.shape["node"]
    row = mesh.devices.transpose([names.index(n) for n in names if n != "node"] + [names.index("node")])
    row = list(row.reshape(-1, count)[0])
    chips = [tuple(getattr(d, "coords", None) or (i // 2,)) for i, d in enumerate(row)][::2]
    order = list(range(len(chips)))
    axes = [a for a in range(len(chips[0])) if len({c[a] for c in chips}) > 1]
    if len(axes) == 2:
        short, long = sorted(axes, key=lambda a: len({c[a] for c in chips}))
        low = min(c[short] for c in chips)
        if len({c[short] for c in chips}) == 2:
            order.sort(key=lambda i: (chips[i][short], chips[i][long] if chips[i][short] == low else -chips[i][long]))
    return order


def pack_kernel(experts, tok_hbm, routes_hbm, gates_hbm, out_ref, routes_ref, gates_ref, sems):
    rows, width = tok_hbm.shape
    extra = out_ref.shape[1] - width
    moves = [
        pltpu.make_async_copy(routes_hbm, routes_ref, sems.at[0]),
        pltpu.make_async_copy(gates_hbm, gates_ref, sems.at[1]),
        pltpu.make_async_copy(tok_hbm, out_ref.at[:, :width], sems.at[2]),
    ]
    for move in moves:
        move.start()
    for move in moves[:2]:
        move.wait()
    lane = lax.broadcasted_iota(jnp.int32, (extra, rows), 0)
    expert, piece = lax.rem(lane, experts), lax.div(lane, experts)
    weight = jnp.zeros((extra, rows), F32)
    for k in range(routes_ref.shape[0]):
        weight += jnp.where(routes_ref[k : k + 1] == expert, gates_ref[k : k + 1], 0.0)
    high = weight.astype(BF16).astype(F32)
    middle = (weight - high).astype(BF16).astype(F32)
    low = weight - high - middle
    table = jnp.where(piece == 0, high, jnp.where(piece == 1, middle, jnp.where(piece == 2, low, 0.0)))
    out_ref[:, width:] = table.T.astype(BF16)
    moves[2].wait()


def pack(tokens, routes, gates, experts):
    rows, width = tokens.shape
    extra = pl.cdiv(3 * experts, 128) * 128
    there = pl.BlockSpec(memory_space=pltpu.HBM)
    return pl.pallas_call(
        functools.partial(pack_kernel, experts),
        out_shape=pltpu.VMEM((rows, width + extra), BF16),
        in_specs=[there] * 3,
        out_specs=pl.BlockSpec(memory_space=pltpu.VMEM),
        scratch_shapes=[
            pltpu.VMEM(routes.shape[::-1], routes.dtype),
            pltpu.VMEM(gates.shape[::-1], gates.dtype),
            pltpu.SemaphoreType.DMA((3,)),
        ],
        compiler_params=pltpu.CompilerParams(vmem_limit_bytes=SCRATCH),
        cost_estimate=pl.CostEstimate(flops=10 * 2**30, bytes_accessed=0, transcendentals=0),
    )(hbm(tokens), hbm(routes.T), hbm(gates.T))


def hbm(a):
    return pltpu.with_memory_space_constraint(a, pltpu.HBM)


def gather_rows(blocks, x_ref):
    rows, width = blocks[0].shape[0], x_ref.shape[1]
    for at, ref in enumerate(blocks):
        x_ref[at * rows : (at + 1) * rows, :] = ref[:, :width]


def gather_weights(experts, blocks, width, w_ref):
    me = lax.axis_index("node")
    rows = blocks[0].shape[0]
    for at, ref in enumerate(blocks):
        table = ref[:, width:].astype(F32)
        lane = lax.broadcasted_iota(jnp.int32, table.shape, 1)
        own = lax.rem(lane, experts) == me
        w_ref[at * rows : (at + 1) * rows, :] = jnp.sum(jnp.where(own, table, 0.0), axis=1, keepdims=True)


def first_half(x_ref, gate_ref, up_ref, h_ref, tile, begin, end):
    for j in range(begin // tile, end // tile):
        at = slice(j * tile, (j + 1) * tile)
        gate = jnp.dot(x_ref[...], gate_ref[0, :, at], preferred_element_type=F32)
        upper = jnp.dot(x_ref[...], up_ref[0, :, at], preferred_element_type=F32)
        h_ref[:, at] = (gate / (1.0 + jnp.exp(-gate)) * upper).astype(BF16)


def second_half(h_ref, down_ref, w_ref, out_refs, tile, begin, end):
    for j in range(begin // tile, end // tile):
        at = slice(j * tile, (j + 1) * tile)
        out = jnp.dot(h_ref[...], down_ref[0, :, at], preferred_element_type=F32) * w_ref[...]
        row = 0
        for ref in out_refs:
            ref[:, at] = out[row : row + ref.shape[0]].astype(ref.dtype)
            row += ref.shape[0]


def tiles(width, ff):
    return (256 if ff % 256 == 0 else ff), next(t for t in (512, 256, 128, width) if width % t == 0)


def expert_kernel(count, experts, tile_ff, tile_d, *refs):
    blocks, (gate_ref, up_ref, down_ref, *out_refs) = refs[:count], refs[count:]
    out_refs, (x_ref, w_ref, h_ref) = out_refs[:-3], out_refs[-3:]
    gather_rows(blocks, x_ref)
    gather_weights(experts, blocks, x_ref.shape[1], w_ref)
    first_half(x_ref, gate_ref, up_ref, h_ref, tile_ff, 0, h_ref.shape[1])
    second_half(h_ref, down_ref, w_ref, out_refs, tile_d, 0, x_ref.shape[1])


def expert(blocks, pieces, experts, w_gate, w_up, w_down):
    count, rows = len(blocks), blocks[0].shape[0]
    _, width, ff = w_gate.shape
    total = count * rows
    here = pl.BlockSpec(memory_space=pltpu.VMEM)
    return pl.pallas_call(
        functools.partial(expert_kernel, count, experts, *tiles(width, ff)),
        out_shape=[pltpu.VMEM((n * rows, width), kind) for n, kind in pieces],
        in_specs=[here] * (count + 3),
        out_specs=[here] * len(pieces),
        scratch_shapes=[pltpu.VMEM((total, width), BF16), pltpu.VMEM((total, 1), F32), pltpu.VMEM((total, ff), BF16)],
        compiler_params=pltpu.CompilerParams(vmem_limit_bytes=SCRATCH),
        cost_estimate=pl.CostEstimate(
            flops=6 * max(total, 256) * width * ff, bytes_accessed=0, transcendentals=total * ff
        ),
    )(*blocks, w_gate, w_up, w_down)


def local(order, tokens, routes, gates, w_gate, w_up, w_down):
    chips = len(order)
    experts = 2 * chips
    rows, width = tokens.shape
    forth = [(2 * order[i], 2 * order[(i + 1) % chips]) for i in range(chips)]
    spin = forth + [(b + 1, a + 1) for a, b in forth]
    swap = [(i, i ^ 1) for i in range(experts)]
    send = lambda a: lax.ppermute(a, "node", spin)
    sibling = lambda a: lax.ppermute(a, "node", swap)
    together = lax.optimization_barrier
    block = lambda a, j: a[j * rows : (j + 1) * rows]

    far = chips // 2
    own = pack(tokens, routes, gates, experts)
    up, up_twin, down, down_twin = {0: own}, {0: sibling(own)}, {}, {}
    for k in range(1, far):
        up[k] = send(up[k - 1])
        up_twin[k] = send(up_twin[k - 1])
        down_twin[k], down[k] = sibling(up[k]), sibling(up_twin[k])
    up[far] = send(up[far - 1])
    far_twin = sibling(up[far])

    kept, given = [up[far]], [far_twin]
    for k in range(far - 1, 0, -1):
        kept += [down_twin[k], down[k]]
        given += [up[k], up_twin[k]]
    kept, given = kept + [own], given + [up_twin[0]]
    mine, theirs = [], []
    for at in range(0, len(kept), GROUP):
        some = slice(at, at + GROUP)
        n = len(kept[some])
        sizes = [m for m in (min(n, 2), min(n - 2, 2), n - 4) if m > 0]
        out = expert(kept[some] + given[some], [(n, F32)] + [(m, BF16) for m in sizes], experts, w_gate, w_up, w_down)
        mine += [block(out[0], j) for j in range(n)]
        for m, piece in zip(sizes, out[1:]):
            piece = sibling(piece)
            theirs += [(piece, j) for j in range(m)]

    def add(j, *arrived):
        nonlocal last
        piece, at = theirs[j]
        (piece, *arrived), _ = together(((piece, *arrived), last))
        total = mine[j] + block(piece, at).astype(F32)
        for a in arrived:
            total = total + a.astype(F32)
        last = total.astype(BF16)
        return last

    last = mine[0]
    sums = send(add(0))
    sums_twin = []
    for j in range(1, len(mine) - 1, 2):
        sums_twin = [send(add(j, *sums_twin))]
        sums = send(add(j + 1, sums))
    end = len(mine) - 1
    piece, sums = together((theirs[end][0], sums))
    total = mine[end] + block(piece, theirs[end][1]).astype(F32) + sums.astype(F32)
    for a in sums_twin:
        a, total = together((sibling(a), total))
        total = total + a.astype(F32)
    return total.astype(BF16)


def solution(mesh):
    order = chip_order(mesh)
    in_specs = (
        P(("groups", "node"), None),
        P(("groups", "node"), None),
        P(("groups", "node"), None),
        P("node", None, None),
        P("node", None, None),
        P("node", None, None),
    )
    out_specs = P(("groups", "node"), None)
    body = functools.partial(local, order)
    return jax.shard_map(body, mesh=mesh, in_specs=in_specs, out_specs=out_specs, check_vma=False)
```

time: 90 us -> 67.5 us (0.75)
  waiting for transfers between devices: 39.8 us -> 21.3 us
  starting transfers between devices: 19.6 us -> 31.7 us
  local copies, waits for them, and re-layouts: 9.35 us -> 0.01 us
  Pallas kernels: 19.5 us -> 12.9 us
    ppermute x16 -> x14, waiting for transfers between devices: 36.2 us -> 18.6 us  [local(): send = lambda a: lax.ppermute(a, 'node', spin)]
    ppermute x16 -> x14, starting transfers between devices: 17.4 us -> 28.9 us  [local(): send = lambda a: lax.ppermute(a, 'node', spin)]
    unnamed x13 -> x6, local copies, waits for them, and re-layouts: 9.27 us -> 0.01 us
    pallas_call x4 -> x2, Pallas kernels: 19.5 us -> 12.9 us  [the longest x1 11.8 us: expert(): pl.pallas_call(functools.partial(expert_kernel, count, experts, *tiles(wi...]
    ppermute x11 -> x12, waiting for transfers between devices: 3.63 us -> 2.66 us  [local(): sibling = lambda a: lax.ppermute(a, 'node', swap)]
    ppermute x11 -> x12, starting transfers between devices: 2.19 us -> 2.77 us  [local(): sibling = lambda a: lax.ppermute(a, 'node', swap)]
  transfers between devices with their start and end apart: 27 -> 26, of which waited for: 14 -> 14; matrix products, arithmetic and copies ran while one was open for 1% -> 1% of each run, Pallas kernels for 13% -> 0%
where the time goes in v9:
time: 67.5 us; the launch traced here: 67.4 us
  starting transfers between devices  31.7 us (47%)
  waiting for transfers between devices  21.3 us (32%)
  Pallas kernels  12.9 us (19%)
  other arithmetic  1.36 us (2%)
    ppermute x14, starting transfers between devices, local(): send = lambda a: lax.ppermute(a, 'node', spin)  28.9 us
    ppermute x14, waiting for transfers between devices, local(): send = lambda a: lax.ppermute(a, 'node', spin)  18.6 us
    pallas_call x1, Pallas kernels, expert(): pl.pallas_call(functools.partial(expert_kernel, count, experts, *tiles(wi...  11.8 us
    ppermute x12, starting transfers between devices, local(): sibling = lambda a: lax.ppermute(a, 'node', swap)  2.77 us
    ppermute x12, waiting for transfers between devices, local(): sibling = lambda a: lax.ppermute(a, 'node', swap)  2.66 us
  transfers between devices with their start and end apart: 26, of which 14 were waited for; matrix products, arithmetic and copies ran while one was open for 1% of the time, Pallas kernels for 0%

profile of v9, /device:TPU:0, one launch (start us, length us, event | category | flops | bytes accessed | tf_op | source)
XLA Modules:
  0.0 67.4 jit_solution(9870243304716528270)
XLA Ops:
  0.0 1.1 %shard_map.64.refs_7_ = bf16[32,3712]{1,0:T(8,128)(2,1)S(1)} custom-call(bf16[32,3584]{1,0:T(8,128)(2,1)} %tok_hbm.1, s32[8,32]{1,0:T(8,128)} %bitcast.2, f32[8,32]{1,0:T(8,128)} %bitcast.3), custom_call_target="tpu_custom_call" | custom-call | flops 10737418240 | tf_op jit(solution)/shard_map/pallas_call | solution.py:60
  1.2 0.5 collective-permute-start.5
  1.7 2.6 %collective-permute-start = (bf16[32,3712]{1,0:T(8,128)(2,1)S(1)}, bf16[32,3712]{1,0:T(8,128)(2,1)S(1)}, u32[]{:S(2)}, u32[]{:S(2)}) collective-permute-start(bf16[32,3712]{1,0:T(8,128)(2,1)S(1)} %shard_map.64.refs_7_), channel_id=1, source_target_pairs={{0,4},{4,8},{8,12},{12,14},{14,10},{10,6},{6,2},{2,0},{5,1},{9,5},... | collective-permute-start | bytes 712712 | tf_op jit(solution)/shard_map/ppermute | solution.py:151
  4.3 1.6 %collective-permute-start.6 = (bf16[32,3712]{1,0:T(8,128)(2,1)S(1)}, bf16[32,3712]{1,0:T(8,128)(2,1)S(1)}, u32[]{:S(2)}, u32[]{:S(2)}) collective-permute-start(bf16[32,3712]{1,0:T(8,128)(2,1)S(1)} %collective-permute-done.5.refs_15_), channel_id=1, source_target_pairs={{0,4},{4,8},{8,12},{12,14},{14,10},{10,6},{6,2},{2,0},{5,1},{9,5},... | collective-permute-start | bytes 712712 | tf_op jit(solution)/shard_map/ppermute | solution.py:151
  5.9 2.5 %collective-permute-done.refs_13_ = bf16[32,3712]{1,0:T(8,128)(2,1)S(1)} collective-permute-done((bf16[32,3712]{1,0:T(8,128)(2,1)S(1)}, bf16[32,3712]{1,0:T(8,128)(2,1)S(1)}, u32[]{:S(2)}, u32[]{:S(2)}) %collective-permute-start) | collective-permute-done | bytes 237600 | tf_op jit(solution)/shard_map/ppermute | solution.py:151
  8.4 2.1 %collective-permute-start.1 = (bf16[32,3712]{1,0:T(8,128)(2,1)S(1)}, bf16[32,3712]{1,0:T(8,128)(2,1)S(1)}, u32[]{:S(2)}, u32[]{:S(2)}) collective-permute-start(bf16[32,3712]{1,0:T(8,128)(2,1)S(1)} %collective-permute-done.refs_13_), channel_id=1, source_target_pairs={{0,4},{4,8},{8,12},{12,14},{14,10},{10,6},{6,2},{2,0},{5,1},{9,5},... | collective-permute-start | bytes 712712 | tf_op jit(solution)/shard_map/ppermute | solution.py:151
  10.4 0.5 collective-permute-done.6.refs_14_
  10.9 2.1 %collective-permute-start.7 = (bf16[32,3712]{1,0:T(8,128)(2,1)S(1)}, bf16[32,3712]{1,0:T(8,128)(2,1)S(1)}, u32[]{:S(2)}, u32[]{:S(2)}) collective-permute-start(bf16[32,3712]{1,0:T(8,128)(2,1)S(1)} %collective-permute-done.6.refs_14_), channel_id=1, source_target_pairs={{0,4},{4,8},{8,12},{12,14},{14,10},{10,6},{6,2},{2,0},{5,1},{9,5},... | collective-permute-start | bytes 712712 | tf_op jit(solution)/shard_map/ppermute | solution.py:151
  13.0 1.5 %collective-permute-done.1.refs_11_ = bf16[32,3712]{1,0:T(8,128)(2,1)S(1)} collective-permute-done((bf16[32,3712]{1,0:T(8,128)(2,1)S(1)}, bf16[32,3712]{1,0:T(8,128)(2,1)S(1)}, u32[]{:S(2)}, u32[]{:S(2)}) %collective-permute-start.1) | collective-permute-done | bytes 237600 | tf_op jit(solution)/shard_map/ppermute | solution.py:151
  14.5 2.1 %collective-permute-start.2 = (bf16[32,3712]{1,0:T(8,128)(2,1)S(1)}, bf16[32,3712]{1,0:T(8,128)(2,1)S(1)}, u32[]{:S(2)}, u32[]{:S(2)}) collective-permute-start(bf16[32,3712]{1,0:T(8,128)(2,1)S(1)} %collective-permute-done.1.refs_11_), channel_id=1, source_target_pairs={{0,4},{4,8},{8,12},{12,14},{14,10},{10,6},{6,2},{2,0},{5,1},{9,5},... | collective-permute-start | bytes 712712 | tf_op jit(solution)/shard_map/ppermute | solution.py:151
  16.5 0.0 collective-permute-start.12
  16.5 0.5 collective-permute-start.13
  17.1 2.0 %collective-permute-start.8 = (bf16[32,3712]{1,0:T(8,128)(2,1)S(1)}, bf16[32,3712]{1,0:T(8,128)(2,1)S(1)}, u32[]{:S(2)}, u32[]{:S(2)}) collective-permute-start(bf16[32,3712]{1,0:T(8,128)(2,1)S(1)} %collective-permute-done.7.refs_12_), channel_id=1, source_target_pairs={{0,4},{4,8},{8,12},{12,14},{14,10},{10,6},{6,2},{2,0},{5,1},{9,5},... | collective-permute-start | bytes 712712 | tf_op jit(solution)/shard_map/ppermute | solution.py:151
  19.1 1.5 %collective-permute-done.2.refs_9_ = bf16[32,3712]{1,0:T(8,128)(2,1)S(1)} collective-permute-done((bf16[32,3712]{1,0:T(8,128)(2,1)S(1)}, bf16[32,3712]{1,0:T(8,128)(2,1)S(1)}, u32[]{:S(2)}, u32[]{:S(2)}) %collective-permute-start.2) | collective-permute-done | bytes 237600 | tf_op jit(solution)/shard_map/ppermute | solution.py:151
  20.6 2.1 %collective-permute-start.3 = (bf16[32,3712]{1,0:T(8,128)(2,1)S(1)}, bf16[32,3712]{1,0:T(8,128)(2,1)S(1)}, u32[]{:S(2)}, u32[]{:S(2)}) collective-permute-start(bf16[32,3712]{1,0:T(8,128)(2,1)S(1)} %collective-permute-done.2.refs_9_), channel_id=1, source_target_pairs={{0,4},{4,8},{8,12},{12,14},{14,10},{10,6},{6,2},{2,0},{5,1},{9,5},... | collective-permute-start | bytes 712712 | tf_op jit(solution)/shard_map/ppermute | solution.py:151
  22.7 0.5 collective-permute-start.11
  23.2 0.1 collective-permute-start.4
  23.2 0.4 collective-permute-start.9
  23.7 3.0 %collective-permute-done.3.refs_0_ = bf16[32,3712]{1,0:T(8,128)(2,1)S(1)} collective-permute-done((bf16[32,3712]{1,0:T(8,128)(2,1)S(1)}, bf16[32,3712]{1,0:T(8,128)(2,1)S(1)}, u32[]{:S(2)}, u32[]{:S(2)}) %collective-permute-start.3) | collective-permute-done | bytes 237600 | tf_op jit(solution)/shard_map/ppermute | solution.py:151
  26.7 1.5 %collective-permute-done.14.refs_8_ = bf16[32,3712]{1,0:T(8,128)(2,1)S(1)} collective-permute-done((bf16[32,3712]{1,0:T(8,128)(2,1)S(1)}, bf16[32,3712]{1,0:T(8,128)(2,1)S(1)}, u32[]{:S(2)}, u32[]{:S(2)}) %collective-permute-start.14) | collective-permute-done | bytes 237600 | tf_op jit(solution)/shard_map/ppermute | solution.py:152
  28.2 11.8 %shard_map.65 = (f32[256,3584]{1,0:T(8,128)S(1)}, bf16[64,3584]{1,0:T(8,128)(2,1)S(1)}, bf16[64,3584]{1,0:T(8,128)(2,1)S(1)}, bf16[128,3584]{1,0:T(8,128)(2,1)S(1)}) custom-call(bf16[32,3712]{1,0:T(8,128)(2,1)S(1)} %collective-permute-done.3.refs_0_, bf16[32,3712]{1,0:T(8,128)(2,1)S(1)} %collective-permute-done.4.refs_1_, ...), custom_call_target="tpu_custom_call" | custom-call | flops 11274289152 | tf_op jit(solution)/shard_map/pallas_call | solution.py:131
  40.0 0.2 collective-permute-start.17
  40.2 0.4 collective-permute-start.16
  40.6 0.1 collective-permute-start.15
  40.7 1.2 %collective-permute-done.17 = bf16[64,3584]{1,0:T(8,128)(2,1)S(1)} collective-permute-done((bf16[64,3584]{1,0:T(8,128)(2,1)S(1)}, bf16[64,3584]{1,0:T(8,128)(2,1)S(1)}, u32[]{:S(2)}, u32[]{:S(2)}) %collective-permute-start.17) | collective-permute-done | bytes 458784 | tf_op jit(solution)/shard_map/ppermute | solution.py:152
  41.9 0.1 add_convert_fusion.7
  41.9 2.1 %collective-permute-start.19 = (bf16[32,3584]{1,0:T(8,128)(2,1)S(1)}, bf16[32,3584]{1,0:T(8,128)(2,1)S(1)}, u32[]{:S(2)}, u32[]{:S(2)}) collective-permute-start(bf16[32,3584]{1,0:T(8,128)(2,1)S(1)} %add_convert_fusion.7), channel_id=1, source_target_pairs={{0,4},{4,8},{8,12},{12,14},{14,10},{10,6},{6,2},{2,0},{5,1},{9,5},... | collective-permute-start | bytes 688136 | tf_op jit(solution)/shard_map/ppermute | solution.py:151
  44.1 0.1 add_convert_fusion.6
  44.1 1.6 %collective-permute-start.18 = (bf16[32,3584]{1,0:T(8,128)(2,1)S(1)}, bf16[32,3584]{1,0:T(8,128)(2,1)S(1)}, u32[]{:S(2)}, u32[]{:S(2)}) collective-permute-start(bf16[32,3584]{1,0:T(8,128)(2,1)S(1)} %add_convert_fusion.6), channel_id=1, source_target_pairs={{0,4},{4,8},{8,12},{12,14},{14,10},{10,6},{6,2},{2,0},{5,1},{9,5},... | collective-permute-start | bytes 688136 | tf_op jit(solution)/shard_map/ppermute | solution.py:151
  45.8 2.3 %collective-permute-done.19 = bf16[32,3584]{1,0:T(8,128)(2,1)S(1)} collective-permute-done((bf16[32,3584]{1,0:T(8,128)(2,1)S(1)}, bf16[32,3584]{1,0:T(8,128)(2,1)S(1)}, u32[]{:S(2)}, u32[]{:S(2)}) %collective-permute-start.19) | collective-permute-done | bytes 229408 | tf_op jit(solution)/shard_map/ppermute | solution.py:151
  48.0 0.1 add_convert_fusion.5
  48.1 2.1 %collective-permute-start.21 = (bf16[32,3584]{1,0:T(8,128)(2,1)S(1)}, bf16[32,3584]{1,0:T(8,128)(2,1)S(1)}, u32[]{:S(2)}, u32[]{:S(2)}) collective-permute-start(bf16[32,3584]{1,0:T(8,128)(2,1)S(1)} %add_convert_fusion.5), channel_id=1, source_target_pairs={{0,4},{4,8},{8,12},{12,14},{14,10},{10,6},{6,2},{2,0},{5,1},{9,5},... | collective-permute-start | bytes 688136 | tf_op jit(solution)/shard_map/ppermute | solution.py:151
  50.2 0.2 collective-permute-done.18
  50.5 0.1 add_convert_fusion.4
  50.6 2.1 %collective-permute-start.20 = (bf16[32,3584]{1,0:T(8,128)(2,1)S(1)}, bf16[32,3584]{1,0:T(8,128)(2,1)S(1)}, u32[]{:S(2)}, u32[]{:S(2)}) collective-permute-start(bf16[32,3584]{1,0:T(8,128)(2,1)S(1)} %add_convert_fusion.4), channel_id=1, source_target_pairs={{0,4},{4,8},{8,12},{12,14},{14,10},{10,6},{6,2},{2,0},{5,1},{9,5},... | collective-permute-start | bytes 688136 | tf_op jit(solution)/shard_map/ppermute | solution.py:151
  52.7 1.5 %collective-permute-done.21 = bf16[32,3584]{1,0:T(8,128)(2,1)S(1)} collective-permute-done((bf16[32,3584]{1,0:T(8,128)(2,1)S(1)}, bf16[32,3584]{1,0:T(8,128)(2,1)S(1)}, u32[]{:S(2)}, u32[]{:S(2)}) %collective-permute-start.21) | collective-permute-done | bytes 229408 | tf_op jit(solution)/shard_map/ppermute | solution.py:151
  54.2 0.1 add_convert_fusion.3
  54.3 2.1 %collective-permute-start.24 = (bf16[32,3584]{1,0:T(8,128)(2,1)S(1)}, bf16[32,3584]{1,0:T(8,128)(2,1)S(1)}, u32[]{:S(2)}, u32[]{:S(2)}) collective-permute-start(bf16[32,3584]{1,0:T(8,128)(2,1)S(1)} %add_convert_fusion.3), channel_id=1, source_target_pairs={{0,4},{4,8},{8,12},{12,14},{14,10},{10,6},{6,2},{2,0},{5,1},{9,5},... | collective-permute-start | bytes 688136 | tf_op jit(solution)/shard_map/ppermute | solution.py:151
  56.4 0.2 collective-permute-done.20
  56.7 0.1 add_convert_fusion.2
  56.8 2.1 %collective-permute-start.22 = (bf16[32,3584]{1,0:T(8,128)(2,1)S(1)}, bf16[32,3584]{1,0:T(8,128)(2,1)S(1)}, u32[]{:S(2)}, u32[]{:S(2)}) collective-permute-start(bf16[32,3584]{1,0:T(8,128)(2,1)S(1)} %add_convert_fusion.2), channel_id=1, source_target_pairs={{0,4},{4,8},{8,12},{12,14},{14,10},{10,6},{6,2},{2,0},{5,1},{9,5},... | collective-permute-start | bytes 688136 | tf_op jit(solution)/shard_map/ppermute | solution.py:151
  58.9 1.5 %collective-permute-done.24 = bf16[32,3584]{1,0:T(8,128)(2,1)S(1)} collective-permute-done((bf16[32,3584]{1,0:T(8,128)(2,1)S(1)}, bf16[32,3584]{1,0:T(8,128)(2,1)S(1)}, u32[]{:S(2)}, u32[]{:S(2)}) %collective-permute-start.24) | collective-permute-done | bytes 229408 | tf_op jit(solution)/shard_map/ppermute | solution.py:151
  60.4 0.1 add_convert_fusion.1
  60.5 2.1 %collective-permute-start.25 = (bf16[32,3584]{1,0:T(8,128)(2,1)S(1)}, bf16[32,3584]{1,0:T(8,128)(2,1)S(1)}, u32[]{:S(2)}, u32[]{:S(2)}) collective-permute-start(bf16[32,3584]{1,0:T(8,128)(2,1)S(1)} %add_convert_fusion.1), channel_id=1, source_target_pairs={{0,4},{4,8},{8,12},{12,14},{14,10},{10,6},{6,2},{2,0},{5,1},{9,5},... | collective-permute-start | bytes 688136 | tf_op jit(solution)/shard_map/ppermute | solution.py:151
  62.6 0.2 collective-permute-done.22
  62.8 3.7 %collective-permute-done.25 = bf16[32,3584]{1,0:T(8,128)(2,1)S(1)} collective-permute-done((bf16[32,3584]{1,0:T(8,128)(2,1)S(1)}, bf16[32,3584]{1,0:T(8,128)(2,1)S(1)}, u32[]{:S(2)}, u32[]{:S(2)}) %collective-permute-start.25) | collective-permute-done | bytes 229408 | tf_op jit(solution)/shard_map/ppermute | solution.py:151
  66.5 0.1 convert_add_fusion
  66.6 0.7 %add_convert_fusion = bf16[32,3584]{1,0:T(8,128)(2,1)} fusion(f32[32,3584]{1,0:T(8,128)S(1)} %convert_add_fusion, bf16[32,3584]{1,0:T(8,128)(2,1)S(1)} %collective-permute-done.23), kind=kLoop, calls=%fused_computation | loop fusion | flops 344064 | bytes 917504 | tf_op jit(solution)/shard_map/convert_element_type | solution.py:204
  (21 shorter events, 0.1 us)
Async XLA Ops:
  0.0 28.2 %copy-start = (bf16[1,3584,1024]{2,1,0:T(8,128)(2,1)S(1)}, bf16[1,3584,1024]{2,1,0:T(8,128)(2,1)}, u32[]{:S(2)}) copy-start(bf16[1,3584,1024]{2,1,0:T(8,128)(2,1)} %refs_16_.1) | copy-start | bytes 22020100
  0.0 28.2 %copy-start.1 = (bf16[1,3584,1024]{2,1,0:T(8,128)(2,1)S(1)}, bf16[1,3584,1024]{2,1,0:T(8,128)(2,1)}, u32[]{:S(2)}) copy-start(bf16[1,3584,1024]{2,1,0:T(8,128)(2,1)} %refs_17_.1) | copy-start | bytes 22020100
  0.0 28.2 %copy-start.2 = (bf16[1,1024,3584]{2,1,0:T(8,128)(2,1)S(1)}, bf16[1,1024,3584]{2,1,0:T(8,128)(2,1)}, u32[]{:S(2)}) copy-start(bf16[1,1024,3584]{2,1,0:T(8,128)(2,1)} %refs_18_.1) | copy-start | bytes 22020100
  1.2 3.2 %collective-permute-start.5 = (bf16[32,3712]{1,0:T(8,128)(2,1)S(1)}, bf16[32,3712]{1,0:T(8,128)(2,1)S(1)}, u32[]{:S(2)}, u32[]{:S(2)}) collective-permute-start(bf16[32,3712]{1,0:T(8,128)(2,1)S(1)} %shard_map.64.refs_7_), channel_id=1, source_target_pairs={{0,1},{1,0},{2,3},{3,2},{4,5},{5,4},{6,7},{7,6},{8,9},{9,8},{10,11... | collective-permute-start | bytes 712712 | tf_op jit(solution)/shard_map/ppermute | solution.py:152
  1.7 6.7 %collective-permute-start = (bf16[32,3712]{1,0:T(8,128)(2,1)S(1)}, bf16[32,3712]{1,0:T(8,128)(2,1)S(1)}, u32[]{:S(2)}, u32[]{:S(2)}) collective-permute-start(bf16[32,3712]{1,0:T(8,128)(2,1)S(1)} %shard_map.64.refs_7_), channel_id=1, source_target_pairs={{0,4},{4,8},{8,12},{12,14},{14,10},{10,6},{6,2},{2,0},{5,1},{9,5},... | collective-permute-start | bytes 712712 | tf_op jit(solution)/shard_map/ppermute | solution.py:151
  4.3 6.6 %collective-permute-start.6 = (bf16[32,3712]{1,0:T(8,128)(2,1)S(1)}, bf16[32,3712]{1,0:T(8,128)(2,1)S(1)}, u32[]{:S(2)}, u32[]{:S(2)}) collective-permute-start(bf16[32,3712]{1,0:T(8,128)(2,1)S(1)} %collective-permute-done.5.refs_15_), channel_id=1, source_target_pairs={{0,4},{4,8},{8,12},{12,14},{14,10},{10,6},{6,2},{2,0},{5,1},{9,5},... | collective-permute-start | bytes 712712 | tf_op jit(solution)/shard_map/ppermute | solution.py:151
  8.4 6.1 %collective-permute-start.1 = (bf16[32,3712]{1,0:T(8,128)(2,1)S(1)}, bf16[32,3712]{1,0:T(8,128)(2,1)S(1)}, u32[]{:S(2)}, u32[]{:S(2)}) collective-permute-start(bf16[32,3712]{1,0:T(8,128)(2,1)S(1)} %collective-permute-done.refs_13_), channel_id=1, source_target_pairs={{0,4},{4,8},{8,12},{12,14},{14,10},{10,6},{6,2},{2,0},{5,1},{9,5},... | collective-permute-start | bytes 712712 | tf_op jit(solution)/shard_map/ppermute | solution.py:151
  10.9 6.2 %collective-permute-start.7 = (bf16[32,3712]{1,0:T(8,128)(2,1)S(1)}, bf16[32,3712]{1,0:T(8,128)(2,1)S(1)}, u32[]{:S(2)}, u32[]{:S(2)}) collective-permute-start(bf16[32,3712]{1,0:T(8,128)(2,1)S(1)} %collective-permute-done.6.refs_14_), channel_id=1, source_target_pairs={{0,4},{4,8},{8,12},{12,14},{14,10},{10,6},{6,2},{2,0},{5,1},{9,5},... | collective-permute-start | bytes 712712 | tf_op jit(solution)/shard_map/ppermute | solution.py:151
  14.5 6.1 %collective-permute-start.2 = (bf16[32,3712]{1,0:T(8,128)(2,1)S(1)}, bf16[32,3712]{1,0:T(8,128)(2,1)S(1)}, u32[]{:S(2)}, u32[]{:S(2)}) collective-permute-start(bf16[32,3712]{1,0:T(8,128)(2,1)S(1)} %collective-permute-done.1.refs_11_), channel_id=1, source_target_pairs={{0,4},{4,8},{8,12},{12,14},{14,10},{10,6},{6,2},{2,0},{5,1},{9,5},... | collective-permute-start | bytes 712712 | tf_op jit(solution)/shard_map/ppermute | solution.py:151
  16.5 6.1 %collective-permute-start.12 = (bf16[32,3712]{1,0:T(8,128)(2,1)S(1)}, bf16[32,3712]{1,0:T(8,128)(2,1)S(1)}, u32[]{:S(2)}, u32[]{:S(2)}) collective-permute-start(bf16[32,3712]{1,0:T(8,128)(2,1)S(1)} %collective-permute-done.refs_13_), channel_id=1, source_target_pairs={{0,1},{1,0},{2,3},{3,2},{4,5},{5,4},{6,7},{7,6},{8,9},{9,8},{10,11... | collective-permute-start | bytes 712712 | tf_op jit(solution)/shard_map/ppermute | solution.py:152
  16.5 6.6 %collective-permute-start.13 = (bf16[32,3712]{1,0:T(8,128)(2,1)S(1)}, bf16[32,3712]{1,0:T(8,128)(2,1)S(1)}, u32[]{:S(2)}, u32[]{:S(2)}) collective-permute-start(bf16[32,3712]{1,0:T(8,128)(2,1)S(1)} %collective-permute-done.6.refs_14_), channel_id=1, source_target_pairs={{0,1},{1,0},{2,3},{3,2},{4,5},{5,4},{6,7},{7,6},{8,9},{9,8},{10,11... | collective-permute-start | bytes 712712 | tf_op jit(solution)/shard_map/ppermute | solution.py:152
  17.1 6.2 %collective-permute-start.8 = (bf16[32,3712]{1,0:T(8,128)(2,1)S(1)}, bf16[32,3712]{1,0:T(8,128)(2,1)S(1)}, u32[]{:S(2)}, u32[]{:S(2)}) collective-permute-start(bf16[32,3712]{1,0:T(8,128)(2,1)S(1)} %collective-permute-done.7.refs_12_), channel_id=1, source_target_pairs={{0,4},{4,8},{8,12},{12,14},{14,10},{10,6},{6,2},{2,0},{5,1},{9,5},... | collective-permute-start | bytes 712712 | tf_op jit(solution)/shard_map/ppermute | solution.py:151
  20.6 6.1 %collective-permute-start.3 = (bf16[32,3712]{1,0:T(8,128)(2,1)S(1)}, bf16[32,3712]{1,0:T(8,128)(2,1)S(1)}, u32[]{:S(2)}, u32[]{:S(2)}) collective-permute-start(bf16[32,3712]{1,0:T(8,128)(2,1)S(1)} %collective-permute-done.2.refs_9_), channel_id=1, source_target_pairs={{0,4},{4,8},{8,12},{12,14},{14,10},{10,6},{6,2},{2,0},{5,1},{9,5},... | collective-permute-start | bytes 712712 | tf_op jit(solution)/shard_map/ppermute | solution.py:151
  22.6 4.0 %collective-permute-start.10 = (bf16[32,3712]{1,0:T(8,128)(2,1)S(1)}, bf16[32,3712]{1,0:T(8,128)(2,1)S(1)}, u32[]{:S(2)}, u32[]{:S(2)}) collective-permute-start(bf16[32,3712]{1,0:T(8,128)(2,1)S(1)} %collective-permute-done.1.refs_11_), channel_id=1, source_target_pairs={{0,1},{1,0},{2,3},{3,2},{4,5},{5,4},{6,7},{7,6},{8,9},{9,8},{10,11... | collective-permute-start | bytes 712712 | tf_op jit(solution)/shard_map/ppermute | solution.py:152
  22.7 4.0 %collective-permute-start.11 = (bf16[32,3712]{1,0:T(8,128)(2,1)S(1)}, bf16[32,3712]{1,0:T(8,128)(2,1)S(1)}, u32[]{:S(2)}, u32[]{:S(2)}) collective-permute-start(bf16[32,3712]{1,0:T(8,128)(2,1)S(1)} %collective-permute-done.7.refs_12_), channel_id=1, source_target_pairs={{0,1},{1,0},{2,3},{3,2},{4,5},{5,4},{6,7},{7,6},{8,9},{9,8},{10,11... | collective-permute-start | bytes 712712 | tf_op jit(solution)/shard_map/ppermute | solution.py:152
  23.2 3.5 %collective-permute-start.4 = (bf16[32,3712]{1,0:T(8,128)(2,1)S(1)}, bf16[32,3712]{1,0:T(8,128)(2,1)S(1)}, u32[]{:S(2)}, u32[]{:S(2)}) collective-permute-start(bf16[32,3712]{1,0:T(8,128)(2,1)S(1)} %collective-permute-done.2.refs_9_), channel_id=1, source_target_pairs={{0,1},{1,0},{2,3},{3,2},{4,5},{5,4},{6,7},{7,6},{8,9},{9,8},{10,11... | collective-permute-start | bytes 712712 | tf_op jit(solution)/shard_map/ppermute | solution.py:152
  23.2 3.5 %collective-permute-start.9 = (bf16[32,3712]{1,0:T(8,128)(2,1)S(1)}, bf16[32,3712]{1,0:T(8,128)(2,1)S(1)}, u32[]{:S(2)}, u32[]{:S(2)}) collective-permute-start(bf16[32,3712]{1,0:T(8,128)(2,1)S(1)} %collective-permute-done.8.refs_10_), channel_id=1, source_target_pairs={{0,1},{1,0},{2,3},{3,2},{4,5},{5,4},{6,7},{7,6},{8,9},{9,8},{10,11... | collective-permute-start | bytes 712712 | tf_op jit(solution)/shard_map/ppermute | solution.py:152
  26.7 1.5 %collective-permute-start.14 = (bf16[32,3712]{1,0:T(8,128)(2,1)S(1)}, bf16[32,3712]{1,0:T(8,128)(2,1)S(1)}, u32[]{:S(2)}, u32[]{:S(2)}) collective-permute-start(bf16[32,3712]{1,0:T(8,128)(2,1)S(1)} %collective-permute-done.3.refs_0_), channel_id=1, source_target_pairs={{0,1},{1,0},{2,3},{3,2},{4,5},{5,4},{6,7},{7,6},{8,9},{9,8},{10,11... | collective-permute-start | bytes 712712 | tf_op jit(solution)/shard_map/ppermute | solution.py:152
  40.0 1.9 %collective-permute-start.17 = (bf16[64,3584]{1,0:T(8,128)(2,1)S(1)}, bf16[64,3584]{1,0:T(8,128)(2,1)S(1)}, u32[]{:S(2)}, u32[]{:S(2)}) collective-permute-start(bf16[64,3584]{1,0:T(8,128)(2,1)S(1)} %get-tuple-element.28), channel_id=1, source_target_pairs={{0,1},{1,0},{2,3},{3,2},{4,5},{5,4},{6,7},{7,6},{8,9},{9,8},{10,11... | collective-permute-start | bytes 1376264 | tf_op jit(solution)/shard_map/ppermute | solution.py:152
  40.2 5.6 %collective-permute-start.16 = (bf16[64,3584]{1,0:T(8,128)(2,1)S(1)}, bf16[64,3584]{1,0:T(8,128)(2,1)S(1)}, u32[]{:S(2)}, u32[]{:S(2)}) collective-permute-start(bf16[64,3584]{1,0:T(8,128)(2,1)S(1)} %get-tuple-element.27), channel_id=1, source_target_pairs={{0,1},{1,0},{2,3},{3,2},{4,5},{5,4},{6,7},{7,6},{8,9},{9,8},{10,11... | collective-permute-start | bytes 1376264 | tf_op jit(solution)/shard_map/ppermute | solution.py:152
  40.6 13.6 %collective-permute-start.15 = (bf16[128,3584]{1,0:T(8,128)(2,1)S(1)}, bf16[128,3584]{1,0:T(8,128)(2,1)S(1)}, u32[]{:S(2)}, u32[]{:S(2)}) collective-permute-start(bf16[128,3584]{1,0:T(8,128)(2,1)S(1)} %get-tuple-element.26), channel_id=1, source_target_pairs={{0,1},{1,0},{2,3},{3,2},{4,5},{5,4},{6,7},{7,6},{8,9},{9,8},{10,11... | collective-permute-start | bytes 2752520 | tf_op jit(solution)/shard_map/ppermute | solution.py:152
  41.9 6.1 %collective-permute-start.19 = (bf16[32,3584]{1,0:T(8,128)(2,1)S(1)}, bf16[32,3584]{1,0:T(8,128)(2,1)S(1)}, u32[]{:S(2)}, u32[]{:S(2)}) collective-permute-start(bf16[32,3584]{1,0:T(8,128)(2,1)S(1)} %add_convert_fusion.7), channel_id=1, source_target_pairs={{0,4},{4,8},{8,12},{12,14},{14,10},{10,6},{6,2},{2,0},{5,1},{9,5},... | collective-permute-start | bytes 688136 | tf_op jit(solution)/shard_map/ppermute | solution.py:151
  44.1 6.4 %collective-permute-start.18 = (bf16[32,3584]{1,0:T(8,128)(2,1)S(1)}, bf16[32,3584]{1,0:T(8,128)(2,1)S(1)}, u32[]{:S(2)}, u32[]{:S(2)}) collective-permute-start(bf16[32,3584]{1,0:T(8,128)(2,1)S(1)} %add_convert_fusion.6), channel_id=1, source_target_pairs={{0,4},{4,8},{8,12},{12,14},{14,10},{10,6},{6,2},{2,0},{5,1},{9,5},... | collective-permute-start | bytes 688136 | tf_op jit(solution)/shard_map/ppermute | solution.py:151
  48.1 6.1 %collective-permute-start.21 = (bf16[32,3584]{1,0:T(8,128)(2,1)S(1)}, bf16[32,3584]{1,0:T(8,128)(2,1)S(1)}, u32[]{:S(2)}, u32[]{:S(2)}) collective-permute-start(bf16[32,3584]{1,0:T(8,128)(2,1)S(1)} %add_convert_fusion.5), channel_id=1, source_target_pairs={{0,4},{4,8},{8,12},{12,14},{14,10},{10,6},{6,2},{2,0},{5,1},{9,5},... | collective-permute-start | bytes 688136 | tf_op jit(solution)/shard_map/ppermute | solution.py:151
  50.6 6.1 %collective-permute-start.20 = (bf16[32,3584]{1,0:T(8,128)(2,1)S(1)}, bf16[32,3584]{1,0:T(8,128)(2,1)S(1)}, u32[]{:S(2)}, u32[]{:S(2)}) collective-permute-start(bf16[32,3584]{1,0:T(8,128)(2,1)S(1)} %add_convert_fusion.4), channel_id=1, source_target_pairs={{0,4},{4,8},{8,12},{12,14},{14,10},{10,6},{6,2},{2,0},{5,1},{9,5},... | collective-permute-start | bytes 688136 | tf_op jit(solution)/shard_map/ppermute | solution.py:151
  54.3 6.1 %collective-permute-start.24 = (bf16[32,3584]{1,0:T(8,128)(2,1)S(1)}, bf16[32,3584]{1,0:T(8,128)(2,1)S(1)}, u32[]{:S(2)}, u32[]{:S(2)}) collective-permute-start(bf16[32,3584]{1,0:T(8,128)(2,1)S(1)} %add_convert_fusion.3), channel_id=1, source_target_pairs={{0,4},{4,8},{8,12},{12,14},{14,10},{10,6},{6,2},{2,0},{5,1},{9,5},... | collective-permute-start | bytes 688136 | tf_op jit(solution)/shard_map/ppermute | solution.py:151
  56.8 6.1 %collective-permute-start.22 = (bf16[32,3584]{1,0:T(8,128)(2,1)S(1)}, bf16[32,3584]{1,0:T(8,128)(2,1)S(1)}, u32[]{:S(2)}, u32[]{:S(2)}) collective-permute-start(bf16[32,3584]{1,0:T(8,128)(2,1)S(1)} %add_convert_fusion.2), channel_id=1, source_target_pairs={{0,4},{4,8},{8,12},{12,14},{14,10},{10,6},{6,2},{2,0},{5,1},{9,5},... | collective-permute-start | bytes 688136 | tf_op jit(solution)/shard_map/ppermute | solution.py:151
  60.5 6.1 %collective-permute-start.25 = (bf16[32,3584]{1,0:T(8,128)(2,1)S(1)}, bf16[32,3584]{1,0:T(8,128)(2,1)S(1)}, u32[]{:S(2)}, u32[]{:S(2)}) collective-permute-start(bf16[32,3584]{1,0:T(8,128)(2,1)S(1)} %add_convert_fusion.1), channel_id=1, source_target_pairs={{0,4},{4,8},{8,12},{12,14},{14,10},{10,6},{6,2},{2,0},{5,1},{9,5},... | collective-permute-start | bytes 688136 | tf_op jit(solution)/shard_map/ppermute | solution.py:151
  62.8 3.8 %collective-permute-start.23 = (bf16[32,3584]{1,0:T(8,128)(2,1)S(1)}, bf16[32,3584]{1,0:T(8,128)(2,1)S(1)}, u32[]{:S(2)}, u32[]{:S(2)}) collective-permute-start(bf16[32,3584]{1,0:T(8,128)(2,1)S(1)} %collective-permute-done.22), channel_id=1, source_target_pairs={{0,1},{1,0},{2,3},{3,2},{4,5},{5,4},{6,7},{7,6},{8,9},{9,8},{10,11... | collective-permute-start | bytes 688136 | tf_op jit(solution)/shard_map/ppermute | solution.py:152

commit v10 on v9

--- a/solution.py
+++ b/solution.py
@@ -8,8 +8,7 @@
 from jax.sharding import PartitionSpec as P
 
 F32, BF16 = jnp.float32, jnp.bfloat16
-SCRATCH = 20 * 2**20
-GROUP = 8
+SCRATCH = 16 * 2**20
 
 
 def chip_order(mesh):
@@ -163,45 +162,74 @@
     up[far] = send(up[far - 1])
     far_twin = sibling(up[far])
 
-    kept, given = [up[far]], [far_twin]
-    for k in range(far - 1, 0, -1):
-        kept += [down_twin[k], down[k]]
-        given += [up[k], up_twin[k]]
-    kept, given = kept + [own], given + [up_twin[0]]
-    mine, theirs = [], []
-    for at in range(0, len(kept), GROUP):
-        some = slice(at, at + GROUP)
-        n = len(kept[some])
-        sizes = [m for m in (min(n, 2), min(n - 2, 2), n - 4) if m > 0]
-        out = expert(kept[some] + given[some], [(n, F32)] + [(m, BF16) for m in sizes], experts, w_gate, w_up, w_down)
-        mine += [block(out[0], j) for j in range(n)]
-        for m, piece in zip(sizes, out[1:]):
-            piece = sibling(piece)
-            theirs += [(piece, j) for j in range(m)]
-
-    def add(j, *arrived):
-        nonlocal last
-        piece, at = theirs[j]
+    mine, theirs = {}, {}
+    weights = w_gate, w_up, w_down
+
+    def compute(places, heads):
+        kept = [up[k] if k >= 0 else down[-k] for k in places]
+        given = [far_twin if k == far else (down_twin[k] if k > 0 else up_twin[-k]) for k in places]
+        sizes = [n for n in (heads, len(places) - heads) if n]
+        return expert(kept + given, [(len(kept), F32)] + [(n, BF16) for n in sizes], experts, *weights)
+
+    def note(places, out, pieces):
+        at = [(piece, j) for piece in pieces for j in range(piece.shape[0] // rows)]
+        for j, k in enumerate(places):
+            mine[k], theirs[k] = (out, j), at[j]
+
+    def add(k, last, *arrived):
+        piece, at = theirs[k]
         (piece, *arrived), _ = together(((piece, *arrived), last))
-        total = mine[j] + block(piece, at).astype(F32)
+        total = block(mine[k][0], mine[k][1]) + block(piece, at).astype(F32)
         for a in arrived:
             total = total + a.astype(F32)
-        last = total.astype(BF16)
-        return last
-
-    last = mine[0]
-    sums = send(add(0))
-    sums_twin = []
-    for j in range(1, len(mine) - 1, 2):
-        sums_twin = [send(add(j, *sums_twin))]
-        sums = send(add(j + 1, sums))
-    end = len(mine) - 1
-    piece, sums = together((theirs[end][0], sums))
-    total = mine[end] + block(piece, theirs[end][1]).astype(F32) + sums.astype(F32)
-    for a in sums_twin:
-        a, total = together((sibling(a), total))
-        total = total + a.astype(F32)
-    return total.astype(BF16)
+        return total
+
+    up, up_twin, down, down_twin, far_twin = together((up, up_twin, down, down_twin, far_twin))
+    late = [far, far - 1, 1 - far]
+    out, first, other = compute(late, 1)
+    first = sibling(first)
+    note(late[:1], out, [first])
+    last = add(far, first).astype(BF16)
+    other, _ = together((sibling(other), last))
+    note(late[1:], None, [other])
+    for j, k in enumerate(late):
+        mine[k] = out, j
+
+    cut = rows // 2
+    return_send = lambda a: lax.ppermute(a, "node", [(b, a) for a, b in spin])
+    ahead, astern = send(last[:cut]), return_send(last[cut:])
+    tasks = [[s * k for k in range(2, far - 1) for s in (1, -1)], [1, -1], [0]]
+    computed = None
+    for d in range(far - 1, -1, -1):
+        exchanged, computed = computed, None
+        if exchanged is not None:
+            places, out, piece = exchanged
+            piece, _ = together((piece, last))
+            exchanged = places, out, sibling(piece)
+        if tasks:
+            places = tasks.pop(0)
+            saved = up, down, up_twin, down_twin
+            up, down, up_twin, down_twin, _ = together((*saved, last))
+            out, piece = compute(places, 0)
+            out, piece, ahead = together((out, piece, ahead))
+            up, down, up_twin, down_twin = saved
+            computed = places, out, piece
+        if exchanged is not None:
+            places, out, piece = exchanged
+            piece, ahead = together((piece, ahead))
+            note(places, out, [piece])
+        if d == far - 1:
+            pad = jnp.zeros_like(ahead)
+            ahead = jnp.concatenate([ahead, pad], axis=0)
+            astern = jnp.concatenate([pad, astern], axis=0)
+        if d:
+            last = add(-d, last, ahead).astype(BF16)
+            ahead = send(last)
+            last = add(d, last, astern).astype(BF16)
+            astern = return_send(last)
+    total = add(0, last, ahead)
+    astern, total = together((astern, total))
+    return (total + astern.astype(F32)).astype(BF16)
 
 
 def solution(mesh):

time: 67.5 us -> 66.6 us (0.987)
  starting transfers between devices: 31.7 us -> 25.6 us
  Pallas kernels: 12.9 us -> 16.5 us
  waiting for transfers between devices: 21.3 us -> 22.7 us
    ppermute x14 -> x11, starting transfers between devices: 28.9 us -> 20.2 us  [local(): send = lambda a: lax.ppermute(a, 'node', spin)]
    pallas_call x1 -> x4, Pallas kernels: 11.8 us -> 15.3 us  [expert(): pl.pallas_call(functools.partial(expert_kernel, count, experts, *tiles(wi...]
    ppermute x0 -> x4, starting transfers between devices: none -> 2.74 us  [local(): return_send = lambda a: lax.ppermute(a, 'node', [(b, a) for a, b in spin])]
    ppermute x0 -> x4, waiting for transfers between devices: none -> 2.44 us  [local(): return_send = lambda a: lax.ppermute(a, 'node', [(b, a) for a, b in spin])]
    ppermute x14 -> x11, waiting for transfers between devices: 18.6 us -> 17.8 us  [local(): send = lambda a: lax.ppermute(a, 'node', spin)]
    ppermute x12 -> x13, waiting for transfers between devices: 2.66 us -> 2.47 us  [local(): sibling = lambda a: lax.ppermute(a, 'node', swap)]
    ppermute x12 -> x13, starting transfers between devices: 2.77 us -> 2.72 us  [local(): sibling = lambda a: lax.ppermute(a, 'node', swap)]
  transfers between devices with their start and end apart: 26 -> 28, of which waited for: 14 -> 13; matrix products, arithmetic and copies ran while one was open for 1% -> 1% of each run, Pallas kernels for 0% -> 16%
where the time goes in v10:
time: 66.6 us; the launch traced here: 66.5 us
  starting transfers between devices  25.6 us (38%)
  waiting for transfers between devices  22.7 us (34%)
  Pallas kernels  16.5 us (25%)
  other arithmetic  1.35 us (2%)
    ppermute x11, starting transfers between devices, local(): send = lambda a: lax.ppermute(a, 'node', spin)  20.2 us
    ppermute x11, waiting for transfers between devices, local(): send = lambda a: lax.ppermute(a, 'node', spin)  17.8 us
    pallas_call x4, Pallas kernels, expert(): pl.pallas_call(functools.partial(expert_kernel, count, experts, *tiles(wi...  15.3 us
    ppermute x4, starting transfers between devices, local(): return_send = lambda a: lax.ppermute(a, 'node', [(b, a) for a, b in spin])  2.74 us
    ppermute x13, starting transfers between devices, local(): sibling = lambda a: lax.ppermute(a, 'node', swap)  2.72 us
    ppermute x13, waiting for transfers between devices, local(): sibling = lambda a: lax.ppermute(a, 'node', swap)  2.47 us
    ppermute x4, waiting for transfers between devices, local(): return_send = lambda a: lax.ppermute(a, 'node', [(b, a) for a, b in spin])  2.44 us
  transfers between devices with their start and end apart: 28, of which 13 were waited for; matrix products, arithmetic and copies ran while one was open for 1% of the time, Pallas kernels for 16%

profile of v10, /device:TPU:0, one launch (start us, length us, event | category | flops | bytes accessed | tf_op | source)
XLA Modules:
  0.0 66.5 jit_solution(14912261097312532717)
XLA Ops:
  0.0 1.1 %shard_map.64.refs_0_ = bf16[32,3712]{1,0:T(8,128)(2,1)S(1)} custom-call(bf16[32,3584]{1,0:T(8,128)(2,1)} %tok_hbm.1, s32[8,32]{1,0:T(8,128)} %bitcast.8, f32[8,32]{1,0:T(8,128)} %bitcast.9), custom_call_target="tpu_custom_call" | custom-call | flops 10737418240 | tf_op jit(solution)/shard_map/pallas_call | solution.py:59
  1.2 0.5 collective-permute-start.4
  1.7 2.6 %collective-permute-start = (bf16[32,3712]{1,0:T(8,128)(2,1)S(1)}, bf16[32,3712]{1,0:T(8,128)(2,1)S(1)}, u32[]{:S(2)}, u32[]{:S(2)}) collective-permute-start(bf16[32,3712]{1,0:T(8,128)(2,1)S(1)} %shard_map.64.refs_0_), channel_id=1, source_target_pairs={{0,4},{4,8},{8,12},{12,14},{14,10},{10,6},{6,2},{2,0},{5,1},{9,5},... | collective-permute-start | bytes 712712 | tf_op jit(solution)/shard_map/ppermute | solution.py:150
  4.4 1.6 %collective-permute-start.5 = (bf16[32,3712]{1,0:T(8,128)(2,1)S(1)}, bf16[32,3712]{1,0:T(8,128)(2,1)S(1)}, u32[]{:S(2)}, u32[]{:S(2)}) collective-permute-start(bf16[32,3712]{1,0:T(8,128)(2,1)S(1)} %collective-permute-done.4.refs_1_), channel_id=1, source_target_pairs={{0,4},{4,8},{8,12},{12,14},{14,10},{10,6},{6,2},{2,0},{5,1},{9,5},... | collective-permute-start | bytes 712712 | tf_op jit(solution)/shard_map/ppermute | solution.py:150
  5.9 2.5 %collective-permute-done.refs_0_ = bf16[32,3712]{1,0:T(8,128)(2,1)S(1)} collective-permute-done((bf16[32,3712]{1,0:T(8,128)(2,1)S(1)}, bf16[32,3712]{1,0:T(8,128)(2,1)S(1)}, u32[]{:S(2)}, u32[]{:S(2)}) %collective-permute-start) | collective-permute-done | bytes 237600 | tf_op jit(solution)/shard_map/ppermute | solution.py:150
  8.4 2.1 %collective-permute-start.1 = (bf16[32,3712]{1,0:T(8,128)(2,1)S(1)}, bf16[32,3712]{1,0:T(8,128)(2,1)S(1)}, u32[]{:S(2)}, u32[]{:S(2)}) collective-permute-start(bf16[32,3712]{1,0:T(8,128)(2,1)S(1)} %collective-permute-done.refs_0_), channel_id=1, source_target_pairs={{0,4},{4,8},{8,12},{12,14},{14,10},{10,6},{6,2},{2,0},{5,1},{9,5},... | collective-permute-start | bytes 712712 | tf_op jit(solution)/shard_map/ppermute | solution.py:150
  10.5 0.5 collective-permute-done.5.refs_3_
  10.9 2.1 %collective-permute-start.6 = (bf16[32,3712]{1,0:T(8,128)(2,1)S(1)}, bf16[32,3712]{1,0:T(8,128)(2,1)S(1)}, u32[]{:S(2)}, u32[]{:S(2)}) collective-permute-start(bf16[32,3712]{1,0:T(8,128)(2,1)S(1)} %collective-permute-done.5.refs_3_), channel_id=1, source_target_pairs={{0,4},{4,8},{8,12},{12,14},{14,10},{10,6},{6,2},{2,0},{5,1},{9,5},... | collective-permute-start | bytes 712712 | tf_op jit(solution)/shard_map/ppermute | solution.py:150
  13.0 1.5 %collective-permute-done.1.refs_0_ = bf16[32,3712]{1,0:T(8,128)(2,1)S(1)} collective-permute-done((bf16[32,3712]{1,0:T(8,128)(2,1)S(1)}, bf16[32,3712]{1,0:T(8,128)(2,1)S(1)}, u32[]{:S(2)}, u32[]{:S(2)}) %collective-permute-start.1) | collective-permute-done | bytes 237600 | tf_op jit(solution)/shard_map/ppermute | solution.py:150
  14.5 2.1 %collective-permute-start.2 = (bf16[32,3712]{1,0:T(8,128)(2,1)S(1)}, bf16[32,3712]{1,0:T(8,128)(2,1)S(1)}, u32[]{:S(2)}, u32[]{:S(2)}) collective-permute-start(bf16[32,3712]{1,0:T(8,128)(2,1)S(1)} %collective-permute-done.1.refs_0_), channel_id=1, source_target_pairs={{0,4},{4,8},{8,12},{12,14},{14,10},{10,6},{6,2},{2,0},{5,1},{9,5},... | collective-permute-start | bytes 712712 | tf_op jit(solution)/shard_map/ppermute | solution.py:150
  16.6 0.5 collective-permute-start.8
  17.1 2.0 %collective-permute-start.7 = (bf16[32,3712]{1,0:T(8,128)(2,1)S(1)}, bf16[32,3712]{1,0:T(8,128)(2,1)S(1)}, u32[]{:S(2)}, u32[]{:S(2)}) collective-permute-start(bf16[32,3712]{1,0:T(8,128)(2,1)S(1)} %collective-permute-done.6.refs_3_), channel_id=1, source_target_pairs={{0,4},{4,8},{8,12},{12,14},{14,10},{10,6},{6,2},{2,0},{5,1},{9,5},... | collective-permute-start | bytes 712712 | tf_op jit(solution)/shard_map/ppermute | solution.py:150
  19.1 1.5 %collective-permute-done.2.refs_1_ = bf16[32,3712]{1,0:T(8,128)(2,1)S(1)} collective-permute-done((bf16[32,3712]{1,0:T(8,128)(2,1)S(1)}, bf16[32,3712]{1,0:T(8,128)(2,1)S(1)}, u32[]{:S(2)}, u32[]{:S(2)}) %collective-permute-start.2) | collective-permute-done | bytes 237600 | tf_op jit(solution)/shard_map/ppermute | solution.py:150
  20.6 2.1 %collective-permute-start.3 = (bf16[32,3712]{1,0:T(8,128)(2,1)S(1)}, bf16[32,3712]{1,0:T(8,128)(2,1)S(1)}, u32[]{:S(2)}, u32[]{:S(2)}) collective-permute-start(bf16[32,3712]{1,0:T(8,128)(2,1)S(1)} %collective-permute-done.2.refs_1_), channel_id=1, source_target_pairs={{0,4},{4,8},{8,12},{12,14},{14,10},{10,6},{6,2},{2,0},{5,1},{9,5},... | collective-permute-start | bytes 712712 | tf_op jit(solution)/shard_map/ppermute | solution.py:150
  22.7 0.5 collective-permute-start.9
  23.2 0.1 collective-permute-start.13
  23.3 0.4 collective-permute-start.10
  23.7 3.0 %collective-permute-done.3.refs_0_ = bf16[32,3712]{1,0:T(8,128)(2,1)S(1)} collective-permute-done((bf16[32,3712]{1,0:T(8,128)(2,1)S(1)}, bf16[32,3712]{1,0:T(8,128)(2,1)S(1)}, u32[]{:S(2)}, u32[]{:S(2)}) %collective-permute-start.3) | collective-permute-done | bytes 237600 | tf_op jit(solution)/shard_map/ppermute | solution.py:150
  26.7 1.5 %collective-permute-done.14.refs_3_ = bf16[32,3712]{1,0:T(8,128)(2,1)S(1)} collective-permute-done((bf16[32,3712]{1,0:T(8,128)(2,1)S(1)}, bf16[32,3712]{1,0:T(8,128)(2,1)S(1)}, u32[]{:S(2)}, u32[]{:S(2)}) %collective-permute-start.14) | collective-permute-done | bytes 237600 | tf_op jit(solution)/shard_map/ppermute | solution.py:151
  28.3 4.6 %shard_map.65 = (f32[96,3584]{1,0:T(8,128)S(1)}, bf16[32,3584]{1,0:T(8,128)(2,1)S(1)}, bf16[64,3584]{1,0:T(8,128)(2,1)S(1)}) custom-call(bf16[32,3712]{1,0:T(8,128)(2,1)S(1)} %collective-permute-done.3.refs_0_, bf16[32,3712]{1,0:T(8,128)(2,1)S(1)} %collective-permute-done.2.refs_1_, bf16[32,3712]{1,0:T(8,128)(2,1)S(1)} %collective-permute-done.10.refs_2_, ...), custom_call_target="tpu_custom_call" | custom-call | flops 5637144576 | tf_op jit(solution)/shard_map/pallas_call | solution.py:130
  32.9 0.2 collective-permute-start.16
  33.1 0.4 collective-permute-start.15
  33.4 1.0 %collective-permute-done.16 = bf16[32,3584]{1,0:T(8,128)(2,1)S(1)} collective-permute-done((bf16[32,3584]{1,0:T(8,128)(2,1)S(1)}, bf16[32,3584]{1,0:T(8,128)(2,1)S(1)}, u32[]{:S(2)}, u32[]{:S(2)}) %collective-permute-start.16) | collective-permute-done | bytes 229408 | tf_op jit(solution)/shard_map/ppermute | solution.py:151
  34.5 2.1 %collective-permute-start.18 = (bf16[16,3584]{1,0:T(8,128)(2,1)S(1)}, bf16[16,3584]{1,0:T(8,128)(2,1)S(1)}, u32[]{:S(2)}, u32[]{:S(2)}) collective-permute-start(bf16[16,3584]{1,0:T(8,128)(2,1)S(1)} %get-tuple-element.145), channel_id=1, source_target_pairs={{0,4},{4,8},{8,12},{12,14},{14,10},{10,6},{6,2},{2,0},{5,1},{9,5},... | collective-permute-start | bytes 344072 | tf_op jit(solution)/shard_map/ppermute | solution.py:150
  36.6 3.3 %shard_map.66 = (f32[64,3584]{1,0:T(8,128)S(1)}, bf16[64,3584]{1,0:T(8,128)(2,1)S(1)}) custom-call(bf16[32,3712]{1,0:T(8,128)(2,1)S(1)} %collective-permute-done.1.refs_0_, bf16[32,3712]{1,0:T(8,128)(2,1)S(1)} %collective-permute-done.9.refs_1_, bf16[32,3712]{1,0:T(8,128)(2,1)S(1)} %collective-permute-done.12.refs_2_, ...), custom_call_target="tpu_custom_call" | custom-call | flops 5637144576 | tf_op jit(solution)/shard_map/pallas_call | solution.py:130
  40.0 1.4 %collective-permute-done.17 = bf16[16,3584]{1,0:T(8,128)(2,1)S(1)} collective-permute-done((bf16[16,3584]{1,0:T(8,128)(2,1)S(1)}, bf16[16,3584]{1,0:T(8,128)(2,1)S(1)}, u32[]{:S(2)}, u32[]{:S(2)}) %collective-permute-start.17) | collective-permute-done | bytes 114720 | tf_op jit(solution)/shard_map/ppermute | solution.py:199
  41.4 0.1 add_convert_fusion.6
  41.5 0.1 add_convert_fusion.5
  41.6 0.9 %collective-permute-start.21 = (bf16[32,3584]{1,0:T(8,128)(2,1)S(1)}, bf16[32,3584]{1,0:T(8,128)(2,1)S(1)}, u32[]{:S(2)}, u32[]{:S(2)}) collective-permute-start(bf16[32,3584]{1,0:T(8,128)(2,1)S(1)} %add_convert_fusion.5), channel_id=1, source_target_pairs={{4,0},{8,4},{12,8},{14,12},{10,14},{6,10},{2,6},{0,2},{1,5},{5,9},... | collective-permute-start | bytes 688136 | tf_op jit(solution)/shard_map/ppermute | solution.py:199
  42.5 1.2 %collective-permute-start.19 = (bf16[32,3584]{1,0:T(8,128)(2,1)S(1)}, bf16[32,3584]{1,0:T(8,128)(2,1)S(1)}, u32[]{:S(2)}, u32[]{:S(2)}) collective-permute-start(bf16[32,3584]{1,0:T(8,128)(2,1)S(1)} %add_convert_fusion.6), channel_id=1, source_target_pairs={{0,4},{4,8},{8,12},{12,14},{14,10},{10,6},{6,2},{2,0},{5,1},{9,5},... | collective-permute-start | bytes 688136 | tf_op jit(solution)/shard_map/ppermute | solution.py:150
  43.7 3.4 %shard_map.67 = (f32[64,3584]{1,0:T(8,128)S(1)}, bf16[64,3584]{1,0:T(8,128)(2,1)S(1)}) custom-call(bf16[32,3712]{1,0:T(8,128)(2,1)S(1)} %collective-permute-done.refs_0_, bf16[32,3712]{1,0:T(8,128)(2,1)S(1)} %collective-permute-done.8.refs_1_, bf16[32,3712]{1,0:T(8,128)(2,1)S(1)} %collective-permute-done.11.refs_2_, ...), custom_call_target="tpu_custom_call" | custom-call | flops 5637144576 | tf_op jit(solution)/shard_map/pallas_call | solution.py:130
  47.1 1.4 %collective-permute-done.19 = bf16[32,3584]{1,0:T(8,128)(2,1)S(1)} collective-permute-done((bf16[32,3584]{1,0:T(8,128)(2,1)S(1)}, bf16[32,3584]{1,0:T(8,128)(2,1)S(1)}, u32[]{:S(2)}, u32[]{:S(2)}) %collective-permute-start.19) | collective-permute-done | bytes 229408 | tf_op jit(solution)/shard_map/ppermute | solution.py:150
  48.5 0.1 add_convert_fusion.4
  48.6 0.5 collective-permute-done.21
  49.1 0.1 add_convert_fusion.3
  49.2 1.4 %collective-permute-start.24 = (bf16[32,3584]{1,0:T(8,128)(2,1)S(1)}, bf16[32,3584]{1,0:T(8,128)(2,1)S(1)}, u32[]{:S(2)}, u32[]{:S(2)}) collective-permute-start(bf16[32,3584]{1,0:T(8,128)(2,1)S(1)} %add_convert_fusion.3), channel_id=1, source_target_pairs={{4,0},{8,4},{12,8},{14,12},{10,14},{6,10},{2,6},{0,2},{1,5},{5,9},... | collective-permute-start | bytes 688136 | tf_op jit(solution)/shard_map/ppermute | solution.py:199
  50.6 0.7 %collective-permute-start.23 = (bf16[32,3584]{1,0:T(8,128)(2,1)S(1)}, bf16[32,3584]{1,0:T(8,128)(2,1)S(1)}, u32[]{:S(2)}, u32[]{:S(2)}) collective-permute-start(bf16[32,3584]{1,0:T(8,128)(2,1)S(1)} %add_convert_fusion.4), channel_id=1, source_target_pairs={{0,4},{4,8},{8,12},{12,14},{14,10},{10,6},{6,2},{2,0},{5,1},{9,5},... | collective-permute-start | bytes 688136 | tf_op jit(solution)/shard_map/ppermute | solution.py:150
  51.2 4.1 %shard_map.68 = (f32[32,3584]{1,0:T(8,128)S(1)}, bf16[32,3584]{1,0:T(8,128)(2,1)S(1)}) custom-call(bf16[32,3712]{1,0:T(8,128)(2,1)S(1)} %shard_map.64.refs_0_, bf16[32,3712]{1,0:T(8,128)(2,1)S(1)} %collective-permute-done.4.refs_1_, bf16[1,3584,1024]{2,1,0:T(8,128)(2,1)S(1)} %bitcast.3, bf16[1,3584,1024]{2,1,0:T(8,128)(2,1)S(1)} %bitcast.5, ...), custom_call_target="tpu_custom_call" | custom-call | flops 5637144576 | tf_op jit(solution)/shard_map/pallas_call | solution.py:130
  55.3 1.3 %collective-permute-done.23 = bf16[32,3584]{1,0:T(8,128)(2,1)S(1)} collective-permute-done((bf16[32,3584]{1,0:T(8,128)(2,1)S(1)}, bf16[32,3584]{1,0:T(8,128)(2,1)S(1)}, u32[]{:S(2)}, u32[]{:S(2)}) %collective-permute-start.23) | collective-permute-done | bytes 229408 | tf_op jit(solution)/shard_map/ppermute | solution.py:150
  56.6 0.1 add_convert_fusion.2
  56.7 0.5 collective-permute-done.24
  57.2 0.1 add_convert_fusion.1
  57.3 0.1 collective-permute-start.26
  57.4 1.6 %collective-permute-start.27 = (bf16[32,3584]{1,0:T(8,128)(2,1)S(1)}, bf16[32,3584]{1,0:T(8,128)(2,1)S(1)}, u32[]{:S(2)}, u32[]{:S(2)}) collective-permute-start(bf16[32,3584]{1,0:T(8,128)(2,1)S(1)} %add_convert_fusion.2), channel_id=1, source_target_pairs={{0,4},{4,8},{8,12},{12,14},{14,10},{10,6},{6,2},{2,0},{5,1},{9,5},... | collective-permute-start | bytes 688136 | tf_op jit(solution)/shard_map/ppermute | solution.py:150
  59.0 0.5 collective-permute-start.25
  59.5 6.2 %collective-permute-done.27 = bf16[32,3584]{1,0:T(8,128)(2,1)S(1)} collective-permute-done((bf16[32,3584]{1,0:T(8,128)(2,1)S(1)}, bf16[32,3584]{1,0:T(8,128)(2,1)S(1)}, u32[]{:S(2)}, u32[]{:S(2)}) %collective-permute-start.27) | collective-permute-done | bytes 229408 | tf_op jit(solution)/shard_map/ppermute | solution.py:150
  65.7 0.1 convert_add_fusion
  65.8 0.7 %add_convert_fusion = bf16[32,3584]{1,0:T(8,128)(2,1)} fusion(f32[32,3584]{1,0:T(8,128)S(1)} %convert_add_fusion, bf16[32,3584]{1,0:T(8,128)(2,1)S(1)} %collective-permute-done.25), kind=kLoop, calls=%fused_computation | loop fusion | flops 344064 | bytes 917504 | tf_op jit(solution)/shard_map/convert_element_type | solution.py:232
  (40 shorter events, 0.2 us)
Async XLA Ops:
  0.0 28.2 %slice-start = ((s8[7340032]{0:T(1024)(128)(4,1)}), s8[4194304]{0:T(1024)(128)(4,1)S(1)}, s32[]{:S(2)}) async-start(s8[7340032]{0:T(1024)(128)(4,1)} %bitcast.2), calls=%async_computation | async-start | bytes 8388608
  0.0 28.2 %slice-start.2 = ((s8[7340032]{0:T(1024)(128)(4,1)}), s8[4194304]{0:T(1024)(128)(4,1)S(1)}, s32[]{:S(2)}) async-start(s8[7340032]{0:T(1024)(128)(4,1)} %bitcast.4), calls=%async_computation.2 | async-start | bytes 8388608
  0.0 28.2 %slice-start.4 = ((s8[7340032]{0:T(1024)(128)(4,1)}), s8[4194304]{0:T(1024)(128)(4,1)S(1)}, s32[]{:S(2)}) async-start(s8[7340032]{0:T(1024)(128)(4,1)} %bitcast.6), calls=%async_computation.4 | async-start | bytes 8388608
  0.0 28.2 %slice-start.1 = ((s8[7340032]{0:T(1024)(128)(4,1)}), s8[3145728]{0:T(1024)(128)(4,1)S(1)}, s32[]{:S(2)}) async-start(s8[7340032]{0:T(1024)(128)(4,1)} %bitcast.2), calls=%async_computation.1 | async-start | bytes 6291456
  0.0 28.2 %slice-start.3 = ((s8[7340032]{0:T(1024)(128)(4,1)}), s8[3145728]{0:T(1024)(128)(4,1)S(1)}, s32[]{:S(2)}) async-start(s8[7340032]{0:T(1024)(128)(4,1)} %bitcast.4), calls=%async_computation.3 | async-start | bytes 6291456
  0.0 28.2 %slice-start.5 = ((s8[7340032]{0:T(1024)(128)(4,1)}), s8[3145728]{0:T(1024)(128)(4,1)S(1)}, s32[]{:S(2)}) async-start(s8[7340032]{0:T(1024)(128)(4,1)} %bitcast.6), calls=%async_computation.5 | async-start | bytes 6291456
  1.2 3.2 %collective-permute-start.4 = (bf16[32,3712]{1,0:T(8,128)(2,1)S(1)}, bf16[32,3712]{1,0:T(8,128)(2,1)S(1)}, u32[]{:S(2)}, u32[]{:S(2)}) collective-permute-start(bf16[32,3712]{1,0:T(8,128)(2,1)S(1)} %shard_map.64.refs_0_), channel_id=1, source_target_pairs={{0,1},{1,0},{2,3},{3,2},{4,5},{5,4},{6,7},{7,6},{8,9},{9,8},{10,11... | collective-permute-start | bytes 712712 | tf_op jit(solution)/shard_map/ppermute | solution.py:151
  1.7 6.7 %collective-permute-start = (bf16[32,3712]{1,0:T(8,128)(2,1)S(1)}, bf16[32,3712]{1,0:T(8,128)(2,1)S(1)}, u32[]{:S(2)}, u32[]{:S(2)}) collective-permute-start(bf16[32,3712]{1,0:T(8,128)(2,1)S(1)} %shard_map.64.refs_0_), channel_id=1, source_target_pairs={{0,4},{4,8},{8,12},{12,14},{14,10},{10,6},{6,2},{2,0},{5,1},{9,5},... | collective-permute-start | bytes 712712 | tf_op jit(solution)/shard_map/ppermute | solution.py:150
  4.4 6.6 %collective-permute-start.5 = (bf16[32,3712]{1,0:T(8,128)(2,1)S(1)}, bf16[32,3712]{1,0:T(8,128)(2,1)S(1)}, u32[]{:S(2)}, u32[]{:S(2)}) collective-permute-start(bf16[32,3712]{1,0:T(8,128)(2,1)S(1)} %collective-permute-done.4.refs_1_), channel_id=1, source_target_pairs={{0,4},{4,8},{8,12},{12,14},{14,10},{10,6},{6,2},{2,0},{5,1},{9,5},... | collective-permute-start | bytes 712712 | tf_op jit(solution)/shard_map/ppermute | solution.py:150
  8.4 6.1 %collective-permute-start.1 = (bf16[32,3712]{1,0:T(8,128)(2,1)S(1)}, bf16[32,3712]{1,0:T(8,128)(2,1)S(1)}, u32[]{:S(2)}, u32[]{:S(2)}) collective-permute-start(bf16[32,3712]{1,0:T(8,128)(2,1)S(1)} %collective-permute-done.refs_0_), channel_id=1, source_target_pairs={{0,4},{4,8},{8,12},{12,14},{14,10},{10,6},{6,2},{2,0},{5,1},{9,5},... | collective-permute-start | bytes 712712 | tf_op jit(solution)/shard_map/ppermute | solution.py:150
  10.9 6.2 %collective-permute-start.6 = (bf16[32,3712]{1,0:T(8,128)(2,1)S(1)}, bf16[32,3712]{1,0:T(8,128)(2,1)S(1)}, u32[]{:S(2)}, u32[]{:S(2)}) collective-permute-start(bf16[32,3712]{1,0:T(8,128)(2,1)S(1)} %collective-permute-done.5.refs_3_), channel_id=1, source_target_pairs={{0,4},{4,8},{8,12},{12,14},{14,10},{10,6},{6,2},{2,0},{5,1},{9,5},... | collective-permute-start | bytes 712712 | tf_op jit(solution)/shard_map/ppermute | solution.py:150
  14.5 6.1 %collective-permute-start.2 = (bf16[32,3712]{1,0:T(8,128)(2,1)S(1)}, bf16[32,3712]{1,0:T(8,128)(2,1)S(1)}, u32[]{:S(2)}, u32[]{:S(2)}) collective-permute-start(bf16[32,3712]{1,0:T(8,128)(2,1)S(1)} %collective-permute-done.1.refs_0_), channel_id=1, source_target_pairs={{0,4},{4,8},{8,12},{12,14},{14,10},{10,6},{6,2},{2,0},{5,1},{9,5},... | collective-permute-start | bytes 712712 | tf_op jit(solution)/shard_map/ppermute | solution.py:150
  16.6 6.1 %collective-permute-start.11 = (bf16[32,3712]{1,0:T(8,128)(2,1)S(1)}, bf16[32,3712]{1,0:T(8,128)(2,1)S(1)}, u32[]{:S(2)}, u32[]{:S(2)}) collective-permute-start(bf16[32,3712]{1,0:T(8,128)(2,1)S(1)} %collective-permute-done.refs_0_), channel_id=1, source_target_pairs={{0,1},{1,0},{2,3},{3,2},{4,5},{5,4},{6,7},{7,6},{8,9},{9,8},{10,11... | collective-permute-start | bytes 712712 | tf_op jit(solution)/shard_map/ppermute | solution.py:151
  16.6 6.6 %collective-permute-start.8 = (bf16[32,3712]{1,0:T(8,128)(2,1)S(1)}, bf16[32,3712]{1,0:T(8,128)(2,1)S(1)}, u32[]{:S(2)}, u32[]{:S(2)}) collective-permute-start(bf16[32,3712]{1,0:T(8,128)(2,1)S(1)} %collective-permute-done.5.refs_3_), channel_id=1, source_target_pairs={{0,1},{1,0},{2,3},{3,2},{4,5},{5,4},{6,7},{7,6},{8,9},{9,8},{10,11... | collective-permute-start | bytes 712712 | tf_op jit(solution)/shard_map/ppermute | solution.py:151
  17.1 6.2 %collective-permute-start.7 = (bf16[32,3712]{1,0:T(8,128)(2,1)S(1)}, bf16[32,3712]{1,0:T(8,128)(2,1)S(1)}, u32[]{:S(2)}, u32[]{:S(2)}) collective-permute-start(bf16[32,3712]{1,0:T(8,128)(2,1)S(1)} %collective-permute-done.6.refs_3_), channel_id=1, source_target_pairs={{0,4},{4,8},{8,12},{12,14},{14,10},{10,6},{6,2},{2,0},{5,1},{9,5},... | collective-permute-start | bytes 712712 | tf_op jit(solution)/shard_map/ppermute | solution.py:150
  20.6 6.1 %collective-permute-start.3 = (bf16[32,3712]{1,0:T(8,128)(2,1)S(1)}, bf16[32,3712]{1,0:T(8,128)(2,1)S(1)}, u32[]{:S(2)}, u32[]{:S(2)}) collective-permute-start(bf16[32,3712]{1,0:T(8,128)(2,1)S(1)} %collective-permute-done.2.refs_1_), channel_id=1, source_target_pairs={{0,4},{4,8},{8,12},{12,14},{14,10},{10,6},{6,2},{2,0},{5,1},{9,5},... | collective-permute-start | bytes 712712 | tf_op jit(solution)/shard_map/ppermute | solution.py:150
  22.7 4.0 %collective-permute-start.12 = (bf16[32,3712]{1,0:T(8,128)(2,1)S(1)}, bf16[32,3712]{1,0:T(8,128)(2,1)S(1)}, u32[]{:S(2)}, u32[]{:S(2)}) collective-permute-start(bf16[32,3712]{1,0:T(8,128)(2,1)S(1)} %collective-permute-done.1.refs_0_), channel_id=1, source_target_pairs={{0,1},{1,0},{2,3},{3,2},{4,5},{5,4},{6,7},{7,6},{8,9},{9,8},{10,11... | collective-permute-start | bytes 712712 | tf_op jit(solution)/shard_map/ppermute | solution.py:151
  22.7 4.0 %collective-permute-start.9 = (bf16[32,3712]{1,0:T(8,128)(2,1)S(1)}, bf16[32,3712]{1,0:T(8,128)(2,1)S(1)}, u32[]{:S(2)}, u32[]{:S(2)}) collective-permute-start(bf16[32,3712]{1,0:T(8,128)(2,1)S(1)} %collective-permute-done.6.refs_3_), channel_id=1, source_target_pairs={{0,1},{1,0},{2,3},{3,2},{4,5},{5,4},{6,7},{7,6},{8,9},{9,8},{10,11... | collective-permute-start | bytes 712712 | tf_op jit(solution)/shard_map/ppermute | solution.py:151
  23.2 3.5 %collective-permute-start.13 = (bf16[32,3712]{1,0:T(8,128)(2,1)S(1)}, bf16[32,3712]{1,0:T(8,128)(2,1)S(1)}, u32[]{:S(2)}, u32[]{:S(2)}) collective-permute-start(bf16[32,3712]{1,0:T(8,128)(2,1)S(1)} %collective-permute-done.2.refs_1_), channel_id=1, source_target_pairs={{0,1},{1,0},{2,3},{3,2},{4,5},{5,4},{6,7},{7,6},{8,9},{9,8},{10,11... | collective-permute-start | bytes 712712 | tf_op jit(solution)/shard_map/ppermute | solution.py:151
  23.3 3.5 %collective-permute-start.10 = (bf16[32,3712]{1,0:T(8,128)(2,1)S(1)}, bf16[32,3712]{1,0:T(8,128)(2,1)S(1)}, u32[]{:S(2)}, u32[]{:S(2)}) collective-permute-start(bf16[32,3712]{1,0:T(8,128)(2,1)S(1)} %collective-permute-done.7.refs_5_), channel_id=1, source_target_pairs={{0,1},{1,0},{2,3},{3,2},{4,5},{5,4},{6,7},{7,6},{8,9},{9,8},{10,11... | collective-permute-start | bytes 712712 | tf_op jit(solution)/shard_map/ppermute | solution.py:151
  26.7 1.5 %collective-permute-start.14 = (bf16[32,3712]{1,0:T(8,128)(2,1)S(1)}, bf16[32,3712]{1,0:T(8,128)(2,1)S(1)}, u32[]{:S(2)}, u32[]{:S(2)}) collective-permute-start(bf16[32,3712]{1,0:T(8,128)(2,1)S(1)} %collective-permute-done.3.refs_0_), channel_id=1, source_target_pairs={{0,1},{1,0},{2,3},{3,2},{4,5},{5,4},{6,7},{7,6},{8,9},{9,8},{10,11... | collective-permute-start | bytes 712712 | tf_op jit(solution)/shard_map/ppermute | solution.py:151
  32.9 1.6 %collective-permute-start.16 = (bf16[32,3584]{1,0:T(8,128)(2,1)S(1)}, bf16[32,3584]{1,0:T(8,128)(2,1)S(1)}, u32[]{:S(2)}, u32[]{:S(2)}) collective-permute-start(bf16[32,3584]{1,0:T(8,128)(2,1)S(1)} %get-tuple-element.93), channel_id=1, source_target_pairs={{0,1},{1,0},{2,3},{3,2},{4,5},{5,4},{6,7},{7,6},{8,9},{9,8},{10,11... | collective-permute-start | bytes 688136 | tf_op jit(solution)/shard_map/ppermute | solution.py:151
  33.1 8.4 %collective-permute-start.15 = (bf16[64,3584]{1,0:T(8,128)(2,1)S(1)}, bf16[64,3584]{1,0:T(8,128)(2,1)S(1)}, u32[]{:S(2)}, u32[]{:S(2)}) collective-permute-start(bf16[64,3584]{1,0:T(8,128)(2,1)S(1)} %get-tuple-element.92), channel_id=1, source_target_pairs={{0,1},{1,0},{2,3},{3,2},{4,5},{5,4},{6,7},{7,6},{8,9},{9,8},{10,11... | collective-permute-start | bytes 1376264 | tf_op jit(solution)/shard_map/ppermute | solution.py:151
  34.5 5.5 %collective-permute-start.18 = (bf16[16,3584]{1,0:T(8,128)(2,1)S(1)}, bf16[16,3584]{1,0:T(8,128)(2,1)S(1)}, u32[]{:S(2)}, u32[]{:S(2)}) collective-permute-start(bf16[16,3584]{1,0:T(8,128)(2,1)S(1)} %get-tuple-element.145), channel_id=1, source_target_pairs={{0,4},{4,8},{8,12},{12,14},{14,10},{10,6},{6,2},{2,0},{5,1},{9,5},... | collective-permute-start | bytes 344072 | tf_op jit(solution)/shard_map/ppermute | solution.py:150
  36.6 4.8 %collective-permute-start.17 = (bf16[16,3584]{1,0:T(8,128)(2,1)S(1)}, bf16[16,3584]{1,0:T(8,128)(2,1)S(1)}, u32[]{:S(2)}, u32[]{:S(2)}) collective-permute-start(bf16[16,3584]{1,0:T(8,128)(2,1)S(1)} %get-tuple-element.146), channel_id=1, source_target_pairs={{4,0},{8,4},{12,8},{14,12},{10,14},{6,10},{2,6},{0,2},{1,5},{5,9},... | collective-permute-start | bytes 344072 | tf_op jit(solution)/shard_map/ppermute | solution.py:199
  41.6 7.5 %collective-permute-start.21 = (bf16[32,3584]{1,0:T(8,128)(2,1)S(1)}, bf16[32,3584]{1,0:T(8,128)(2,1)S(1)}, u32[]{:S(2)}, u32[]{:S(2)}) collective-permute-start(bf16[32,3584]{1,0:T(8,128)(2,1)S(1)} %add_convert_fusion.5), channel_id=1, source_target_pairs={{4,0},{8,4},{12,8},{14,12},{10,14},{6,10},{2,6},{0,2},{1,5},{5,9},... | collective-permute-start | bytes 688136 | tf_op jit(solution)/shard_map/ppermute | solution.py:199
  42.5 6.0 %collective-permute-start.19 = (bf16[32,3584]{1,0:T(8,128)(2,1)S(1)}, bf16[32,3584]{1,0:T(8,128)(2,1)S(1)}, u32[]{:S(2)}, u32[]{:S(2)}) collective-permute-start(bf16[32,3584]{1,0:T(8,128)(2,1)S(1)} %add_convert_fusion.6), channel_id=1, source_target_pairs={{0,4},{4,8},{8,12},{12,14},{14,10},{10,6},{6,2},{2,0},{5,1},{9,5},... | collective-permute-start | bytes 688136 | tf_op jit(solution)/shard_map/ppermute | solution.py:150
  43.7 4.8 %collective-permute-start.20 = (bf16[64,3584]{1,0:T(8,128)(2,1)S(1)}, bf16[64,3584]{1,0:T(8,128)(2,1)S(1)}, u32[]{:S(2)}, u32[]{:S(2)}) collective-permute-start(bf16[64,3584]{1,0:T(8,128)(2,1)S(1)} %get-tuple-element.116), channel_id=1, source_target_pairs={{0,1},{1,0},{2,3},{3,2},{4,5},{5,4},{6,7},{7,6},{8,9},{9,8},{10,11... | collective-permute-start | bytes 1376264 | tf_op jit(solution)/shard_map/ppermute | solution.py:151
  49.2 8.0 %collective-permute-start.24 = (bf16[32,3584]{1,0:T(8,128)(2,1)S(1)}, bf16[32,3584]{1,0:T(8,128)(2,1)S(1)}, u32[]{:S(2)}, u32[]{:S(2)}) collective-permute-start(bf16[32,3584]{1,0:T(8,128)(2,1)S(1)} %add_convert_fusion.3), channel_id=1, source_target_pairs={{4,0},{8,4},{12,8},{14,12},{10,14},{6,10},{2,6},{0,2},{1,5},{5,9},... | collective-permute-start | bytes 688136 | tf_op jit(solution)/shard_map/ppermute | solution.py:199
  50.6 6.0 %collective-permute-start.23 = (bf16[32,3584]{1,0:T(8,128)(2,1)S(1)}, bf16[32,3584]{1,0:T(8,128)(2,1)S(1)}, u32[]{:S(2)}, u32[]{:S(2)}) collective-permute-start(bf16[32,3584]{1,0:T(8,128)(2,1)S(1)} %add_convert_fusion.4), channel_id=1, source_target_pairs={{0,4},{4,8},{8,12},{12,14},{14,10},{10,6},{6,2},{2,0},{5,1},{9,5},... | collective-permute-start | bytes 688136 | tf_op jit(solution)/shard_map/ppermute | solution.py:150
  51.2 5.3 %collective-permute-start.22 = (bf16[64,3584]{1,0:T(8,128)(2,1)S(1)}, bf16[64,3584]{1,0:T(8,128)(2,1)S(1)}, u32[]{:S(2)}, u32[]{:S(2)}) collective-permute-start(bf16[64,3584]{1,0:T(8,128)(2,1)S(1)} %get-tuple-element.124), channel_id=1, source_target_pairs={{0,1},{1,0},{2,3},{3,2},{4,5},{5,4},{6,7},{7,6},{8,9},{9,8},{10,11... | collective-permute-start | bytes 1376264 | tf_op jit(solution)/shard_map/ppermute | solution.py:151
  57.3 2.2 %collective-permute-start.26 = (bf16[32,3584]{1,0:T(8,128)(2,1)S(1)}, bf16[32,3584]{1,0:T(8,128)(2,1)S(1)}, u32[]{:S(2)}, u32[]{:S(2)}) collective-permute-start(bf16[32,3584]{1,0:T(8,128)(2,1)S(1)} %get-tuple-element.138), channel_id=1, source_target_pairs={{0,1},{1,0},{2,3},{3,2},{4,5},{5,4},{6,7},{7,6},{8,9},{9,8},{10,11... | collective-permute-start | bytes 688136 | tf_op jit(solution)/shard_map/ppermute | solution.py:151
  57.4 8.3 %collective-permute-start.27 = (bf16[32,3584]{1,0:T(8,128)(2,1)S(1)}, bf16[32,3584]{1,0:T(8,128)(2,1)S(1)}, u32[]{:S(2)}, u32[]{:S(2)}) collective-permute-start(bf16[32,3584]{1,0:T(8,128)(2,1)S(1)} %add_convert_fusion.2), channel_id=1, source_target_pairs={{0,4},{4,8},{8,12},{12,14},{14,10},{10,6},{6,2},{2,0},{5,1},{9,5},... | collective-permute-start | bytes 688136 | tf_op jit(solution)/shard_map/ppermute | solution.py:150
  59.0 6.8 %collective-permute-start.25 = (bf16[32,3584]{1,0:T(8,128)(2,1)S(1)}, bf16[32,3584]{1,0:T(8,128)(2,1)S(1)}, u32[]{:S(2)}, u32[]{:S(2)}) collective-permute-start(bf16[32,3584]{1,0:T(8,128)(2,1)S(1)} %add_convert_fusion.1), channel_id=1, source_target_pairs={{4,0},{8,4},{12,8},{14,12},{10,14},{6,10},{2,6},{0,2},{1,5},{5,9},... | collective-permute-start | bytes 688136 | tf_op jit(solution)/shard_map/ppermute | solution.py:199

commit v11 on v10

--- a/solution.py
+++ b/solution.py
@@ -147,7 +147,13 @@
     forth = [(2 * order[i], 2 * order[(i + 1) % chips]) for i in range(chips)]
     spin = forth + [(b + 1, a + 1) for a, b in forth]
     swap = [(i, i ^ 1) for i in range(experts)]
+    turn = dict(spin)
+    spin_two = [(a, turn[b]) for a, b in spin]
+    reverse = lambda pairs: [(b, a) for a, b in pairs]
     send = lambda a: lax.ppermute(a, "node", spin)
+    send_two = lambda a: lax.ppermute(a, "node", spin_two)
+    return_send = lambda a: lax.ppermute(a, "node", reverse(spin))
+    return_two = lambda a: lax.ppermute(a, "node", reverse(spin_two))
     sibling = lambda a: lax.ppermute(a, "node", swap)
     together = lax.optimization_barrier
     block = lambda a, j: a[j * rows : (j + 1) * rows]
@@ -159,7 +165,7 @@
         up[k] = send(up[k - 1])
         up_twin[k] = send(up_twin[k - 1])
         down_twin[k], down[k] = sibling(up[k]), sibling(up_twin[k])
-    up[far] = send(up[far - 1])
+    up[far] = send_two(up[far - 2])
     far_twin = sibling(up[far])
 
     mine, theirs = {}, {}
@@ -185,22 +191,21 @@
         return total
 
     up, up_twin, down, down_twin, far_twin = together((up, up_twin, down, down_twin, far_twin))
-    late = [far, far - 1, 1 - far]
-    out, first, other = compute(late, 1)
-    first = sibling(first)
-    note(late[:1], out, [first])
-    last = add(far, first).astype(BF16)
-    other, _ = together((sibling(other), last))
-    note(late[1:], None, [other])
-    for j, k in enumerate(late):
-        mine[k] = out, j
+    late = [far] + [s * k for k in (far - 1, far - 2) for s in (1, -1)]
+    out, first, other = compute(late, 3)
+    note(late, out, [sibling(first), sibling(other)])
 
     cut = rows // 2
-    return_send = lambda a: lax.ppermute(a, "node", [(b, a) for a, b in spin])
-    ahead, astern = send(last[:cut]), return_send(last[cut:])
-    tasks = [[s * k for k in range(2, far - 1) for s in (1, -1)], [1, -1], [0]]
+    last = add(far, out).astype(BF16)
+    ahead_two, astern_two = send_two(last[:cut]), return_two(last[cut:])
+    last = add(1 - far, last).astype(BF16)
+    ahead = send(last)
+    last = add(far - 1, last).astype(BF16)
+    astern = return_send(last)
+    tasks = [[s * k for k in range(2, far - 2) for s in (1, -1)], [0, 1, -1]]
+    tasks = [places for places in tasks if places]
     computed = None
-    for d in range(far - 1, -1, -1):
+    for d in range(far - 2, -1, -1):
         exchanged, computed = computed, None
         if exchanged is not None:
             places, out, piece = exchanged
@@ -218,14 +223,15 @@
             places, out, piece = exchanged
             piece, ahead = together((piece, ahead))
             note(places, out, [piece])
-        if d == far - 1:
-            pad = jnp.zeros_like(ahead)
-            ahead = jnp.concatenate([ahead, pad], axis=0)
-            astern = jnp.concatenate([pad, astern], axis=0)
         if d:
-            last = add(-d, last, ahead).astype(BF16)
+            ahead_all, astern_all = [ahead], [astern]
+            if d == far - 2:
+                pad = jnp.zeros_like(ahead_two)
+                ahead_all.append(jnp.concatenate([ahead_two, pad], axis=0))
+                astern_all.append(jnp.concatenate([pad, astern_two], axis=0))
+            last = add(-d, last, *ahead_all).astype(BF16)
             ahead = send(last)
-            last = add(d, last, astern).astype(BF16)
+            last = add(d, last, *astern_all).astype(BF16)
             astern = return_send(last)
     total = add(0, last, ahead)
     astern, total = together((astern, total))

time: 66.6 us -> 71.9 us (1.080)
  waiting for transfers between devices: 22.7 us -> 27.6 us
  starting transfers between devices: 25.6 us -> 29.4 us
  Pallas kernels: 16.5 us -> 13.3 us
    ppermute x4 -> x6, starting transfers between devices: 2.74 us -> 7.14 us  [the longest x2 7.02 us: local(): send_two = lambda a: lax.ppermute(a, 'node', spin_two)]
    ppermute x4 -> x6, waiting for transfers between devices: 2.44 us -> 6.24 us  [the longest x2 3.11 us: local(): send_two = lambda a: lax.ppermute(a, 'node', spin_two)]
    pallas_call x4 -> x2, Pallas kernels: 15.3 us -> 12.1 us  [expert(): pl.pallas_call(functools.partial(expert_kernel, count, experts, *tiles(wi...]
    ppermute x11 -> x9, starting transfers between devices: 20.2 us -> 19.3 us  [local(): send = lambda a: lax.ppermute(a, 'node', spin)]
    ppermute x13 -> x11, waiting for transfers between devices: 2.47 us -> 3.02 us  [local(): sibling = lambda a: lax.ppermute(a, 'node', swap)]
    ppermute x11 -> x9, waiting for transfers between devices: 17.8 us -> 18.3 us  [local(): send = lambda a: lax.ppermute(a, 'node', spin)]
    ppermute x13 -> x11, starting transfers between devices: 2.72 us -> 2.98 us  [local(): sibling = lambda a: lax.ppermute(a, 'node', swap)]
  transfers between devices with their start and end apart: 28 -> 26, of which waited for: 13 -> 13; matrix products, arithmetic and copies ran while one was open for 1% -> 1% of each run, Pallas kernels for 16% -> 6%
where the time goes in v11:
time: 71.9 us; the launch traced here: 71.7 us
  starting transfers between devices  29.4 us (41%)
  waiting for transfers between devices  27.6 us (38%)
  Pallas kernels  13.3 us (18%)
  other arithmetic  1.34 us (2%)
    ppermute x9, starting transfers between devices, local(): send = lambda a: lax.ppermute(a, 'node', spin)  19.3 us
    ppermute x9, waiting for transfers between devices, local(): send = lambda a: lax.ppermute(a, 'node', spin)  18.3 us
    pallas_call x2, Pallas kernels, expert(): pl.pallas_call(functools.partial(expert_kernel, count, experts, *tiles(wi...  12.1 us
    ppermute x2, starting transfers between devices, local(): send_two = lambda a: lax.ppermute(a, 'node', spin_two)  7.02 us
    ppermute x2, waiting for transfers between devices, local(): send_two = lambda a: lax.ppermute(a, 'node', spin_two)  3.11 us
    ppermute x11, waiting for transfers between devices, local(): sibling = lambda a: lax.ppermute(a, 'node', swap)  3.02 us
    ppermute x11, starting transfers between devices, local(): sibling = lambda a: lax.ppermute(a, 'node', swap)  2.98 us
    ppermute x1, waiting for transfers between devices, local(): return_two = lambda a: lax.ppermute(a, 'node', reverse(spin_two))  2.56 us
  transfers between devices with their start and end apart: 26, of which 13 were waited for; matrix products, arithmetic and copies ran while one was open for 1% of the time, Pallas kernels for 6%

profile of v11, /device:TPU:0, one launch (start us, length us, event | category | flops | bytes accessed | tf_op | source)
XLA Modules:
  0.0 71.7 jit_solution(15080809784063021084)
XLA Ops:
  0.0 1.1 %shard_map.64.refs_0_ = bf16[32,3712]{1,0:T(8,128)(2,1)S(1)} custom-call(bf16[32,3584]{1,0:T(8,128)(2,1)} %tok_hbm.1, s32[8,32]{1,0:T(8,128)} %bitcast.2, f32[8,32]{1,0:T(8,128)} %bitcast.3), custom_call_target="tpu_custom_call" | custom-call | flops 10737418240 | tf_op jit(solution)/shard_map/pallas_call | solution.py:59
  1.2 0.5 collective-permute-start.4
  1.7 2.6 %collective-permute-start = (bf16[32,3712]{1,0:T(8,128)(2,1)S(1)}, bf16[32,3712]{1,0:T(8,128)(2,1)S(1)}, u32[]{:S(2)}, u32[]{:S(2)}) collective-permute-start(bf16[32,3712]{1,0:T(8,128)(2,1)S(1)} %shard_map.64.refs_0_), channel_id=1, source_target_pairs={{0,4},{4,8},{8,12},{12,14},{14,10},{10,6},{6,2},{2,0},{5,1},{9,5},... | collective-permute-start | bytes 712712 | tf_op jit(solution)/shard_map/ppermute | solution.py:153
  4.3 1.6 %collective-permute-start.5 = (bf16[32,3712]{1,0:T(8,128)(2,1)S(1)}, bf16[32,3712]{1,0:T(8,128)(2,1)S(1)}, u32[]{:S(2)}, u32[]{:S(2)}) collective-permute-start(bf16[32,3712]{1,0:T(8,128)(2,1)S(1)} %collective-permute-done.4.refs_3_), channel_id=1, source_target_pairs={{0,4},{4,8},{8,12},{12,14},{14,10},{10,6},{6,2},{2,0},{5,1},{9,5},... | collective-permute-start | bytes 712712 | tf_op jit(solution)/shard_map/ppermute | solution.py:153
  5.9 2.5 %collective-permute-done.refs_1_ = bf16[32,3712]{1,0:T(8,128)(2,1)S(1)} collective-permute-done((bf16[32,3712]{1,0:T(8,128)(2,1)S(1)}, bf16[32,3712]{1,0:T(8,128)(2,1)S(1)}, u32[]{:S(2)}, u32[]{:S(2)}) %collective-permute-start) | collective-permute-done | bytes 237600 | tf_op jit(solution)/shard_map/ppermute | solution.py:153
  8.4 2.1 %collective-permute-start.1 = (bf16[32,3712]{1,0:T(8,128)(2,1)S(1)}, bf16[32,3712]{1,0:T(8,128)(2,1)S(1)}, u32[]{:S(2)}, u32[]{:S(2)}) collective-permute-start(bf16[32,3712]{1,0:T(8,128)(2,1)S(1)} %collective-permute-done.refs_1_), channel_id=1, source_target_pairs={{0,4},{4,8},{8,12},{12,14},{14,10},{10,6},{6,2},{2,0},{5,1},{9,5},... | collective-permute-start | bytes 712712 | tf_op jit(solution)/shard_map/ppermute | solution.py:153
  10.4 0.5 collective-permute-done.5.refs_5_
  10.9 2.1 %collective-permute-start.6 = (bf16[32,3712]{1,0:T(8,128)(2,1)S(1)}, bf16[32,3712]{1,0:T(8,128)(2,1)S(1)}, u32[]{:S(2)}, u32[]{:S(2)}) collective-permute-start(bf16[32,3712]{1,0:T(8,128)(2,1)S(1)} %collective-permute-done.5.refs_5_), channel_id=1, source_target_pairs={{0,4},{4,8},{8,12},{12,14},{14,10},{10,6},{6,2},{2,0},{5,1},{9,5},... | collective-permute-start | bytes 712712 | tf_op jit(solution)/shard_map/ppermute | solution.py:153
  13.0 0.5 collective-permute-start.8
  13.5 1.0 %collective-permute-done.1.refs_3_ = bf16[32,3712]{1,0:T(8,128)(2,1)S(1)} collective-permute-done((bf16[32,3712]{1,0:T(8,128)(2,1)S(1)}, bf16[32,3712]{1,0:T(8,128)(2,1)S(1)}, u32[]{:S(2)}, u32[]{:S(2)}) %collective-permute-start.1) | collective-permute-done | bytes 237600 | tf_op jit(solution)/shard_map/ppermute | solution.py:153
  14.5 3.1 %collective-permute-start.3 = (bf16[32,3712]{1,0:T(8,128)(2,1)S(1)}, bf16[32,3712]{1,0:T(8,128)(2,1)S(1)}, u32[]{:S(2)}, u32[]{:S(2)}) collective-permute-start(bf16[32,3712]{1,0:T(8,128)(2,1)S(1)} %collective-permute-done.1.refs_3_), channel_id=1, source_target_pairs={{0,8},{4,12},{8,14},{12,10},{14,6},{10,2},{6,0},{2,4},{5,3},{9,1},... | collective-permute-start | bytes 712712 | tf_op jit(solution)/shard_map/ppermute | solution.py:154
  17.6 1.6 %collective-permute-start.2 = (bf16[32,3712]{1,0:T(8,128)(2,1)S(1)}, bf16[32,3712]{1,0:T(8,128)(2,1)S(1)}, u32[]{:S(2)}, u32[]{:S(2)}) collective-permute-start(bf16[32,3712]{1,0:T(8,128)(2,1)S(1)} %collective-permute-done.1.refs_3_), channel_id=1, source_target_pairs={{0,4},{4,8},{8,12},{12,14},{14,10},{10,6},{6,2},{2,0},{5,1},{9,5},... | collective-permute-start | bytes 712712 | tf_op jit(solution)/shard_map/ppermute | solution.py:153
  19.1 0.0 collective-permute-done.6.refs_9_
  19.1 1.5 %collective-permute-start.7 = (bf16[32,3712]{1,0:T(8,128)(2,1)S(1)}, bf16[32,3712]{1,0:T(8,128)(2,1)S(1)}, u32[]{:S(2)}, u32[]{:S(2)}) collective-permute-start(bf16[32,3712]{1,0:T(8,128)(2,1)S(1)} %collective-permute-done.6.refs_9_), channel_id=1, source_target_pairs={{0,4},{4,8},{8,12},{12,14},{14,10},{10,6},{6,2},{2,0},{5,1},{9,5},... | collective-permute-start | bytes 712712 | tf_op jit(solution)/shard_map/ppermute | solution.py:153
  20.7 0.0 collective-permute-done.11.refs_4_
  20.7 0.0 collective-permute-start.12
  20.7 0.0 collective-permute-done.8.refs_2_
  20.7 0.5 collective-permute-start.9
  21.2 2.8 %collective-permute-done.3.refs_0_ = bf16[32,3712]{1,0:T(8,128)(2,1)S(1)} collective-permute-done((bf16[32,3712]{1,0:T(8,128)(2,1)S(1)}, bf16[32,3712]{1,0:T(8,128)(2,1)S(1)}, u32[]{:S(2)}, u32[]{:S(2)}) %collective-permute-start.3) | collective-permute-done | bytes 237600 | tf_op jit(solution)/shard_map/ppermute | solution.py:154
  24.0 0.0 collective-permute-start.14
  24.0 0.7 %collective-permute-done.2.refs_1_ = bf16[32,3712]{1,0:T(8,128)(2,1)S(1)} collective-permute-done((bf16[32,3712]{1,0:T(8,128)(2,1)S(1)}, bf16[32,3712]{1,0:T(8,128)(2,1)S(1)}, u32[]{:S(2)}, u32[]{:S(2)}) %collective-permute-start.2) | collective-permute-done | bytes 237600 | tf_op jit(solution)/shard_map/ppermute | solution.py:153
  24.8 0.2 collective-permute-start.13
  24.9 2.4 %collective-permute-done.7.refs_7_ = bf16[32,3712]{1,0:T(8,128)(2,1)S(1)} collective-permute-done((bf16[32,3712]{1,0:T(8,128)(2,1)S(1)}, bf16[32,3712]{1,0:T(8,128)(2,1)S(1)}, u32[]{:S(2)}, u32[]{:S(2)}) %collective-permute-start.7) | collective-permute-done | bytes 237600 | tf_op jit(solution)/shard_map/ppermute | solution.py:153
  27.3 0.1 collective-permute-start.10
  27.4 1.4 %collective-permute-done.10.refs_2_ = bf16[32,3712]{1,0:T(8,128)(2,1)S(1)} collective-permute-done((bf16[32,3712]{1,0:T(8,128)(2,1)S(1)}, bf16[32,3712]{1,0:T(8,128)(2,1)S(1)}, u32[]{:S(2)}, u32[]{:S(2)}) %collective-permute-start.10) | collective-permute-done | bytes 237600 | tf_op jit(solution)/shard_map/ppermute | solution.py:157
  28.8 7.5 %shard_map.65 = (f32[160,3584]{1,0:T(8,128)S(1)}, bf16[96,3584]{1,0:T(8,128)(2,1)S(1)}, bf16[64,3584]{1,0:T(8,128)(2,1)S(1)}) custom-call(bf16[32,3712]{1,0:T(8,128)(2,1)S(1)} %collective-permute-done.3.refs_0_, bf16[32,3712]{1,0:T(8,128)(2,1)S(1)} %collective-permute-done.2.refs_1_, bf16[32,3712]{1,0:T(8,128)(2,1)S(1)} %collective-permute-done.10.refs_2_, ...), custom_call_target="tpu_custom_call" | custom-call | flops 7046430720 | tf_op jit(solution)/shard_map/pallas_call | solution.py:130
  36.3 0.2 collective-permute-start.15
  36.5 0.4 collective-permute-start.17
  36.9 1.6 %collective-permute-done.15 = bf16[96,3584]{1,0:T(8,128)(2,1)S(1)} collective-permute-done((bf16[96,3584]{1,0:T(8,128)(2,1)S(1)}, bf16[96,3584]{1,0:T(8,128)(2,1)S(1)}, u32[]{:S(2)}, u32[]{:S(2)}) %collective-permute-start.15) | collective-permute-done | bytes 688160 | tf_op jit(solution)/shard_map/ppermute | solution.py:157
  38.7 3.2 %collective-permute-start.16 = (bf16[32,3584]{1,0:T(8,128)(2,1)S(1)}, bf16[32,3584]{1,0:T(8,128)(2,1)S(1)}, u32[]{:S(2)}, u32[]{:S(2)}) collective-permute-start(bf16[32,3584]{1,0:T(8,128)(2,1)S(1)} %add_convert_fusion.6), channel_id=1, source_target_pairs={{0,4},{4,8},{8,12},{12,14},{14,10},{10,6},{6,2},{2,0},{5,1},{9,5},... | collective-permute-start | bytes 688136 | tf_op jit(solution)/shard_map/ppermute | solution.py:153
  41.9 0.1 collective-permute-start.18
  42.0 3.9 %collective-permute-start.20 = (bf16[16,3584]{1,0:T(8,128)(2,1)S(1)}, bf16[16,3584]{1,0:T(8,128)(2,1)S(1)}, u32[]{:S(2)}, u32[]{:S(2)}) collective-permute-start(bf16[16,3584]{1,0:T(8,128)(2,1)S(1)} %get-tuple-element.105), channel_id=1, source_target_pairs={{0,8},{4,12},{8,14},{12,10},{14,6},{10,2},{6,0},{2,4},{5,3},{9,1},... | collective-permute-start | bytes 344072 | tf_op jit(solution)/shard_map/ppermute | solution.py:154
  45.9 4.6 %shard_map.66 = (f32[96,3584]{1,0:T(8,128)S(1)}, bf16[96,3584]{1,0:T(8,128)(2,1)S(1)}) custom-call(bf16[32,3712]{1,0:T(8,128)(2,1)S(1)} %shard_map.64.refs_0_, bf16[32,3712]{1,0:T(8,128)(2,1)S(1)} %collective-permute-done.refs_1_, bf16[32,3712]{1,0:T(8,128)(2,1)S(1)} %collective-permute-done.8.refs_2_, bf16[32,3712]{1,0:T(8,128)(2,1)S(1)} %collective-permute-done.4.refs_3_, ...), custom_call_target="tpu_custom_call" | custom-call | flops 5637144576 | tf_op jit(solution)/shard_map/pallas_call | solution.py:130
  50.5 0.3 collective-permute-done.20
  50.8 2.6 %collective-permute-done.19 = bf16[16,3584]{1,0:T(8,128)(2,1)S(1)} collective-permute-done((bf16[16,3584]{1,0:T(8,128)(2,1)S(1)}, bf16[16,3584]{1,0:T(8,128)(2,1)S(1)}, u32[]{:S(2)}, u32[]{:S(2)}) %collective-permute-start.19) | collective-permute-done | bytes 114720 | tf_op jit(solution)/shard_map/ppermute | solution.py:156
  53.4 0.1 add_convert_fusion.4
  53.5 0.1 add_convert_fusion.3
  53.7 0.6 collective-permute-start.21
  54.2 2.5 %collective-permute-start.22 = (bf16[32,3584]{1,0:T(8,128)(2,1)S(1)}, bf16[32,3584]{1,0:T(8,128)(2,1)S(1)}, u32[]{:S(2)}, u32[]{:S(2)}) collective-permute-start(bf16[32,3584]{1,0:T(8,128)(2,1)S(1)} %add_convert_fusion.4), channel_id=1, source_target_pairs={{0,4},{4,8},{8,12},{12,14},{14,10},{10,6},{6,2},{2,0},{5,1},{9,5},... | collective-permute-start | bytes 688136 | tf_op jit(solution)/shard_map/ppermute | solution.py:153
  56.8 5.9 %collective-permute-done.22 = bf16[32,3584]{1,0:T(8,128)(2,1)S(1)} collective-permute-done((bf16[32,3584]{1,0:T(8,128)(2,1)S(1)}, bf16[32,3584]{1,0:T(8,128)(2,1)S(1)}, u32[]{:S(2)}, u32[]{:S(2)}) %collective-permute-start.22) | collective-permute-done | bytes 229408 | tf_op jit(solution)/shard_map/ppermute | solution.py:153
  62.7 0.1 add_convert_fusion.2
  62.8 2.1 %collective-permute-start.25 = (bf16[32,3584]{1,0:T(8,128)(2,1)S(1)}, bf16[32,3584]{1,0:T(8,128)(2,1)S(1)}, u32[]{:S(2)}, u32[]{:S(2)}) collective-permute-start(bf16[32,3584]{1,0:T(8,128)(2,1)S(1)} %add_convert_fusion.2), channel_id=1, source_target_pairs={{0,4},{4,8},{8,12},{12,14},{14,10},{10,6},{6,2},{2,0},{5,1},{9,5},... | collective-permute-start | bytes 688136 | tf_op jit(solution)/shard_map/ppermute | solution.py:153
  64.9 0.1 add_convert_fusion.1
  64.9 0.1 collective-permute-start.24
  65.0 5.4 %collective-permute-done.25 = bf16[32,3584]{1,0:T(8,128)(2,1)S(1)} collective-permute-done((bf16[32,3584]{1,0:T(8,128)(2,1)S(1)}, bf16[32,3584]{1,0:T(8,128)(2,1)S(1)}, u32[]{:S(2)}, u32[]{:S(2)}) %collective-permute-start.25) | collective-permute-done | bytes 229408 | tf_op jit(solution)/shard_map/ppermute | solution.py:153
  70.4 0.1 convert_add_fusion
  70.5 0.6 collective-permute-done.24
  71.0 0.7 %add_convert_fusion = bf16[32,3584]{1,0:T(8,128)(2,1)} fusion(f32[32,3584]{1,0:T(8,128)S(1)} %convert_add_fusion, bf16[32,3584]{1,0:T(8,128)(2,1)S(1)} %collective-permute-done.24), kind=kLoop, calls=%fused_computation | loop fusion | flops 344064 | bytes 917504 | tf_op jit(solution)/shard_map/convert_element_type | solution.py:238
  (25 shorter events, 0.2 us)
Async XLA Ops:
  0.0 28.8 %copy-start = (bf16[1,3584,1024]{2,1,0:T(8,128)(2,1)S(1)}, bf16[1,3584,1024]{2,1,0:T(8,128)(2,1)}, u32[]{:S(2)}) copy-start(bf16[1,3584,1024]{2,1,0:T(8,128)(2,1)} %refs_6_.1) | copy-start | bytes 22020100
  0.0 28.8 %copy-start.1 = (bf16[1,3584,1024]{2,1,0:T(8,128)(2,1)S(1)}, bf16[1,3584,1024]{2,1,0:T(8,128)(2,1)}, u32[]{:S(2)}) copy-start(bf16[1,3584,1024]{2,1,0:T(8,128)(2,1)} %refs_7_.1) | copy-start | bytes 22020100
  0.0 28.8 %copy-start.2 = (bf16[1,1024,3584]{2,1,0:T(8,128)(2,1)S(1)}, bf16[1,1024,3584]{2,1,0:T(8,128)(2,1)}, u32[]{:S(2)}) copy-start(bf16[1,1024,3584]{2,1,0:T(8,128)(2,1)} %refs_8_.1) | copy-start | bytes 22020100
  1.2 3.2 %collective-permute-start.4 = (bf16[32,3712]{1,0:T(8,128)(2,1)S(1)}, bf16[32,3712]{1,0:T(8,128)(2,1)S(1)}, u32[]{:S(2)}, u32[]{:S(2)}) collective-permute-start(bf16[32,3712]{1,0:T(8,128)(2,1)S(1)} %shard_map.64.refs_0_), channel_id=1, source_target_pairs={{0,1},{1,0},{2,3},{3,2},{4,5},{5,4},{6,7},{7,6},{8,9},{9,8},{10,11... | collective-permute-start | bytes 712712 | tf_op jit(solution)/shard_map/ppermute | solution.py:157
  1.7 6.7 %collective-permute-start = (bf16[32,3712]{1,0:T(8,128)(2,1)S(1)}, bf16[32,3712]{1,0:T(8,128)(2,1)S(1)}, u32[]{:S(2)}, u32[]{:S(2)}) collective-permute-start(bf16[32,3712]{1,0:T(8,128)(2,1)S(1)} %shard_map.64.refs_0_), channel_id=1, source_target_pairs={{0,4},{4,8},{8,12},{12,14},{14,10},{10,6},{6,2},{2,0},{5,1},{9,5},... | collective-permute-start | bytes 712712 | tf_op jit(solution)/shard_map/ppermute | solution.py:153
  4.3 6.6 %collective-permute-start.5 = (bf16[32,3712]{1,0:T(8,128)(2,1)S(1)}, bf16[32,3712]{1,0:T(8,128)(2,1)S(1)}, u32[]{:S(2)}, u32[]{:S(2)}) collective-permute-start(bf16[32,3712]{1,0:T(8,128)(2,1)S(1)} %collective-permute-done.4.refs_3_), channel_id=1, source_target_pairs={{0,4},{4,8},{8,12},{12,14},{14,10},{10,6},{6,2},{2,0},{5,1},{9,5},... | collective-permute-start | bytes 712712 | tf_op jit(solution)/shard_map/ppermute | solution.py:153
  8.4 6.1 %collective-permute-start.1 = (bf16[32,3712]{1,0:T(8,128)(2,1)S(1)}, bf16[32,3712]{1,0:T(8,128)(2,1)S(1)}, u32[]{:S(2)}, u32[]{:S(2)}) collective-permute-start(bf16[32,3712]{1,0:T(8,128)(2,1)S(1)} %collective-permute-done.refs_1_), channel_id=1, source_target_pairs={{0,4},{4,8},{8,12},{12,14},{14,10},{10,6},{6,2},{2,0},{5,1},{9,5},... | collective-permute-start | bytes 712712 | tf_op jit(solution)/shard_map/ppermute | solution.py:153
  10.9 8.2 %collective-permute-start.6 = (bf16[32,3712]{1,0:T(8,128)(2,1)S(1)}, bf16[32,3712]{1,0:T(8,128)(2,1)S(1)}, u32[]{:S(2)}, u32[]{:S(2)}) collective-permute-start(bf16[32,3712]{1,0:T(8,128)(2,1)S(1)} %collective-permute-done.5.refs_5_), channel_id=1, source_target_pairs={{0,4},{4,8},{8,12},{12,14},{14,10},{10,6},{6,2},{2,0},{5,1},{9,5},... | collective-permute-start | bytes 712712 | tf_op jit(solution)/shard_map/ppermute | solution.py:153
  13.0 7.7 %collective-permute-start.11 = (bf16[32,3712]{1,0:T(8,128)(2,1)S(1)}, bf16[32,3712]{1,0:T(8,128)(2,1)S(1)}, u32[]{:S(2)}, u32[]{:S(2)}) collective-permute-start(bf16[32,3712]{1,0:T(8,128)(2,1)S(1)} %collective-permute-done.refs_1_), channel_id=1, source_target_pairs={{0,1},{1,0},{2,3},{3,2},{4,5},{5,4},{6,7},{7,6},{8,9},{9,8},{10,11... | collective-permute-start | bytes 712712 | tf_op jit(solution)/shard_map/ppermute | solution.py:157
  13.0 7.7 %collective-permute-start.8 = (bf16[32,3712]{1,0:T(8,128)(2,1)S(1)}, bf16[32,3712]{1,0:T(8,128)(2,1)S(1)}, u32[]{:S(2)}, u32[]{:S(2)}) collective-permute-start(bf16[32,3712]{1,0:T(8,128)(2,1)S(1)} %collective-permute-done.5.refs_5_), channel_id=1, source_target_pairs={{0,1},{1,0},{2,3},{3,2},{4,5},{5,4},{6,7},{7,6},{8,9},{9,8},{10,11... | collective-permute-start | bytes 712712 | tf_op jit(solution)/shard_map/ppermute | solution.py:157
  14.5 9.5 %collective-permute-start.3 = (bf16[32,3712]{1,0:T(8,128)(2,1)S(1)}, bf16[32,3712]{1,0:T(8,128)(2,1)S(1)}, u32[]{:S(2)}, u32[]{:S(2)}) collective-permute-start(bf16[32,3712]{1,0:T(8,128)(2,1)S(1)} %collective-permute-done.1.refs_3_), channel_id=1, source_target_pairs={{0,8},{4,12},{8,14},{12,10},{14,6},{10,2},{6,0},{2,4},{5,3},{9,1},... | collective-permute-start | bytes 712712 | tf_op jit(solution)/shard_map/ppermute | solution.py:154
  17.6 7.2 %collective-permute-start.2 = (bf16[32,3712]{1,0:T(8,128)(2,1)S(1)}, bf16[32,3712]{1,0:T(8,128)(2,1)S(1)}, u32[]{:S(2)}, u32[]{:S(2)}) collective-permute-start(bf16[32,3712]{1,0:T(8,128)(2,1)S(1)} %collective-permute-done.1.refs_3_), channel_id=1, source_target_pairs={{0,4},{4,8},{8,12},{12,14},{14,10},{10,6},{6,2},{2,0},{5,1},{9,5},... | collective-permute-start | bytes 712712 | tf_op jit(solution)/shard_map/ppermute | solution.py:153
  19.1 8.2 %collective-permute-start.7 = (bf16[32,3712]{1,0:T(8,128)(2,1)S(1)}, bf16[32,3712]{1,0:T(8,128)(2,1)S(1)}, u32[]{:S(2)}, u32[]{:S(2)}) collective-permute-start(bf16[32,3712]{1,0:T(8,128)(2,1)S(1)} %collective-permute-done.6.refs_9_), channel_id=1, source_target_pairs={{0,4},{4,8},{8,12},{12,14},{14,10},{10,6},{6,2},{2,0},{5,1},{9,5},... | collective-permute-start | bytes 712712 | tf_op jit(solution)/shard_map/ppermute | solution.py:153
  20.7 6.8 %collective-permute-start.12 = (bf16[32,3712]{1,0:T(8,128)(2,1)S(1)}, bf16[32,3712]{1,0:T(8,128)(2,1)S(1)}, u32[]{:S(2)}, u32[]{:S(2)}) collective-permute-start(bf16[32,3712]{1,0:T(8,128)(2,1)S(1)} %collective-permute-done.1.refs_3_), channel_id=1, source_target_pairs={{0,1},{1,0},{2,3},{3,2},{4,5},{5,4},{6,7},{7,6},{8,9},{9,8},{10,11... | collective-permute-start | bytes 712712 | tf_op jit(solution)/shard_map/ppermute | solution.py:157
  20.7 6.8 %collective-permute-start.9 = (bf16[32,3712]{1,0:T(8,128)(2,1)S(1)}, bf16[32,3712]{1,0:T(8,128)(2,1)S(1)}, u32[]{:S(2)}, u32[]{:S(2)}) collective-permute-start(bf16[32,3712]{1,0:T(8,128)(2,1)S(1)} %collective-permute-done.6.refs_9_), channel_id=1, source_target_pairs={{0,1},{1,0},{2,3},{3,2},{4,5},{5,4},{6,7},{7,6},{8,9},{9,8},{10,11... | collective-permute-start | bytes 712712 | tf_op jit(solution)/shard_map/ppermute | solution.py:157
  24.0 3.4 %collective-permute-start.14 = (bf16[32,3712]{1,0:T(8,128)(2,1)S(1)}, bf16[32,3712]{1,0:T(8,128)(2,1)S(1)}, u32[]{:S(2)}, u32[]{:S(2)}) collective-permute-start(bf16[32,3712]{1,0:T(8,128)(2,1)S(1)} %collective-permute-done.3.refs_0_), channel_id=1, source_target_pairs={{0,1},{1,0},{2,3},{3,2},{4,5},{5,4},{6,7},{7,6},{8,9},{9,8},{10,11... | collective-permute-start | bytes 712712 | tf_op jit(solution)/shard_map/ppermute | solution.py:157
  24.8 2.7 %collective-permute-start.13 = (bf16[32,3712]{1,0:T(8,128)(2,1)S(1)}, bf16[32,3712]{1,0:T(8,128)(2,1)S(1)}, u32[]{:S(2)}, u32[]{:S(2)}) collective-permute-start(bf16[32,3712]{1,0:T(8,128)(2,1)S(1)} %collective-permute-done.2.refs_1_), channel_id=1, source_target_pairs={{0,1},{1,0},{2,3},{3,2},{4,5},{5,4},{6,7},{7,6},{8,9},{9,8},{10,11... | collective-permute-start | bytes 712712 | tf_op jit(solution)/shard_map/ppermute | solution.py:157
  27.3 1.5 %collective-permute-start.10 = (bf16[32,3712]{1,0:T(8,128)(2,1)S(1)}, bf16[32,3712]{1,0:T(8,128)(2,1)S(1)}, u32[]{:S(2)}, u32[]{:S(2)}) collective-permute-start(bf16[32,3712]{1,0:T(8,128)(2,1)S(1)} %collective-permute-done.7.refs_7_), channel_id=1, source_target_pairs={{0,1},{1,0},{2,3},{3,2},{4,5},{5,4},{6,7},{7,6},{8,9},{9,8},{10,11... | collective-permute-start | bytes 712712 | tf_op jit(solution)/shard_map/ppermute | solution.py:157
  36.3 2.2 %collective-permute-start.15 = (bf16[96,3584]{1,0:T(8,128)(2,1)S(1)}, bf16[96,3584]{1,0:T(8,128)(2,1)S(1)}, u32[]{:S(2)}, u32[]{:S(2)}) collective-permute-start(bf16[96,3584]{1,0:T(8,128)(2,1)S(1)} %get-tuple-element.72), channel_id=1, source_target_pairs={{0,1},{1,0},{2,3},{3,2},{4,5},{5,4},{6,7},{7,6},{8,9},{9,8},{10,11... | collective-permute-start | bytes 2064392 | tf_op jit(solution)/shard_map/ppermute | solution.py:157
  36.5 16.8 %collective-permute-start.17 = (bf16[64,3584]{1,0:T(8,128)(2,1)S(1)}, bf16[64,3584]{1,0:T(8,128)(2,1)S(1)}, u32[]{:S(2)}, u32[]{:S(2)}) collective-permute-start(bf16[64,3584]{1,0:T(8,128)(2,1)S(1)} %get-tuple-element.86), channel_id=1, source_target_pairs={{0,1},{1,0},{2,3},{3,2},{4,5},{5,4},{6,7},{7,6},{8,9},{9,8},{10,11... | collective-permute-start | bytes 1376264 | tf_op jit(solution)/shard_map/ppermute | solution.py:157
  38.7 14.7 %collective-permute-start.16 = (bf16[32,3584]{1,0:T(8,128)(2,1)S(1)}, bf16[32,3584]{1,0:T(8,128)(2,1)S(1)}, u32[]{:S(2)}, u32[]{:S(2)}) collective-permute-start(bf16[32,3584]{1,0:T(8,128)(2,1)S(1)} %add_convert_fusion.6), channel_id=1, source_target_pairs={{0,4},{4,8},{8,12},{12,14},{14,10},{10,6},{6,2},{2,0},{5,1},{9,5},... | collective-permute-start | bytes 688136 | tf_op jit(solution)/shard_map/ppermute | solution.py:153
  41.9 11.6 %collective-permute-start.18 = (bf16[32,3584]{1,0:T(8,128)(2,1)S(1)}, bf16[32,3584]{1,0:T(8,128)(2,1)S(1)}, u32[]{:S(2)}, u32[]{:S(2)}) collective-permute-start(bf16[32,3584]{1,0:T(8,128)(2,1)S(1)} %add_convert_fusion.5), channel_id=1, source_target_pairs={{4,0},{8,4},{12,8},{14,12},{10,14},{6,10},{2,6},{0,2},{1,5},{5,9},... | collective-permute-start | bytes 688136 | tf_op jit(solution)/shard_map/ppermute | solution.py:155
  42.0 8.8 %collective-permute-start.20 = (bf16[16,3584]{1,0:T(8,128)(2,1)S(1)}, bf16[16,3584]{1,0:T(8,128)(2,1)S(1)}, u32[]{:S(2)}, u32[]{:S(2)}) collective-permute-start(bf16[16,3584]{1,0:T(8,128)(2,1)S(1)} %get-tuple-element.105), channel_id=1, source_target_pairs={{0,8},{4,12},{8,14},{12,10},{14,6},{10,2},{6,0},{2,4},{5,3},{9,1},... | collective-permute-start | bytes 344072 | tf_op jit(solution)/shard_map/ppermute | solution.py:154
  45.9 7.5 %collective-permute-start.19 = (bf16[16,3584]{1,0:T(8,128)(2,1)S(1)}, bf16[16,3584]{1,0:T(8,128)(2,1)S(1)}, u32[]{:S(2)}, u32[]{:S(2)}) collective-permute-start(bf16[16,3584]{1,0:T(8,128)(2,1)S(1)} %get-tuple-element.106), channel_id=1, source_target_pairs={{8,0},{12,4},{14,8},{10,12},{6,14},{2,10},{0,6},{4,2},{3,5},{1,9},... | collective-permute-start | bytes 344072 | tf_op jit(solution)/shard_map/ppermute | solution.py:156
  53.7 9.0 %collective-permute-start.21 = (bf16[96,3584]{1,0:T(8,128)(2,1)S(1)}, bf16[96,3584]{1,0:T(8,128)(2,1)S(1)}, u32[]{:S(2)}, u32[]{:S(2)}) collective-permute-start(bf16[96,3584]{1,0:T(8,128)(2,1)S(1)} %get-tuple-element.94), channel_id=1, source_target_pairs={{0,1},{1,0},{2,3},{3,2},{4,5},{5,4},{6,7},{7,6},{8,9},{9,8},{10,11... | collective-permute-start | bytes 2064392 | tf_op jit(solution)/shard_map/ppermute | solution.py:157
  54.2 8.4 %collective-permute-start.22 = (bf16[32,3584]{1,0:T(8,128)(2,1)S(1)}, bf16[32,3584]{1,0:T(8,128)(2,1)S(1)}, u32[]{:S(2)}, u32[]{:S(2)}) collective-permute-start(bf16[32,3584]{1,0:T(8,128)(2,1)S(1)} %add_convert_fusion.4), channel_id=1, source_target_pairs={{0,4},{4,8},{8,12},{12,14},{14,10},{10,6},{6,2},{2,0},{5,1},{9,5},... | collective-permute-start | bytes 688136 | tf_op jit(solution)/shard_map/ppermute | solution.py:153
  56.8 8.1 %collective-permute-start.23 = (bf16[32,3584]{1,0:T(8,128)(2,1)S(1)}, bf16[32,3584]{1,0:T(8,128)(2,1)S(1)}, u32[]{:S(2)}, u32[]{:S(2)}) collective-permute-start(bf16[32,3584]{1,0:T(8,128)(2,1)S(1)} %add_convert_fusion.3), channel_id=1, source_target_pairs={{4,0},{8,4},{12,8},{14,12},{10,14},{6,10},{2,6},{0,2},{1,5},{5,9},... | collective-permute-start | bytes 688136 | tf_op jit(solution)/shard_map/ppermute | solution.py:155
  62.8 7.6 %collective-permute-start.25 = (bf16[32,3584]{1,0:T(8,128)(2,1)S(1)}, bf16[32,3584]{1,0:T(8,128)(2,1)S(1)}, u32[]{:S(2)}, u32[]{:S(2)}) collective-permute-start(bf16[32,3584]{1,0:T(8,128)(2,1)S(1)} %add_convert_fusion.2), channel_id=1, source_target_pairs={{0,4},{4,8},{8,12},{12,14},{14,10},{10,6},{6,2},{2,0},{5,1},{9,5},... | collective-permute-start | bytes 688136 | tf_op jit(solution)/shard_map/ppermute | solution.py:153
  64.9 6.1 %collective-permute-start.24 = (bf16[32,3584]{1,0:T(8,128)(2,1)S(1)}, bf16[32,3584]{1,0:T(8,128)(2,1)S(1)}, u32[]{:S(2)}, u32[]{:S(2)}) collective-permute-start(bf16[32,3584]{1,0:T(8,128)(2,1)S(1)} %add_convert_fusion.1), channel_id=1, source_target_pairs={{4,0},{8,4},{12,8},{14,12},{10,14},{6,10},{2,6},{0,2},{1,5},{5,9},... | collective-permute-start | bytes 688136 | tf_op jit(solution)/shard_map/ppermute | solution.py:155

commit v12 on v10

--- a/solution.py
+++ b/solution.py
@@ -165,16 +165,11 @@
     mine, theirs = {}, {}
     weights = w_gate, w_up, w_down
 
-    def compute(places, heads):
-        kept = [up[k] if k >= 0 else down[-k] for k in places]
-        given = [far_twin if k == far else (down_twin[k] if k > 0 else up_twin[-k]) for k in places]
-        sizes = [n for n in (heads, len(places) - heads) if n]
+    def compute(keep, give, sizes):
+        kept = [up[k] if k >= 0 else down[-k] for k in keep]
+        given = [far_twin if k == far else (down_twin[k] if k > 0 else up_twin[-k]) for k in give]
+        sizes = [n for n in sizes if n]
         return expert(kept + given, [(len(kept), F32)] + [(n, BF16) for n in sizes], experts, *weights)
-
-    def note(places, out, pieces):
-        at = [(piece, j) for piece in pieces for j in range(piece.shape[0] // rows)]
-        for j, k in enumerate(places):
-            mine[k], theirs[k] = (out, j), at[j]
 
     def add(k, last, *arrived):
         piece, at = theirs[k]
@@ -185,48 +180,30 @@
         return total
 
     up, up_twin, down, down_twin, far_twin = together((up, up_twin, down, down_twin, far_twin))
-    late = [far, far - 1, 1 - far]
-    out, first, other = compute(late, 1)
-    first = sibling(first)
-    note(late[:1], out, [first])
-    last = add(far, first).astype(BF16)
-    other, _ = together((sibling(other), last))
-    note(late[1:], None, [other])
-    for j, k in enumerate(late):
-        mine[k] = out, j
+    places = [far] + [s * k for k in range(far - 1, 0, -1) for s in (1, -1)] + [0]
+    out, *given = compute(places[:3], places, (1, 2, len(places) - 3))
+    mine.update({k: (out, j) for j, k in enumerate(places[:3])})
+    theirs[far] = sibling(given[0]), 0
+    given[1] = sibling(given[1])
+    theirs.update({k: (given[1], j) for j, k in enumerate(places[1:3])})
+    last = add(far, out).astype(BF16)
 
     cut = rows // 2
     return_send = lambda a: lax.ppermute(a, "node", [(b, a) for a, b in spin])
     ahead, astern = send(last[:cut]), return_send(last[cut:])
-    tasks = [[s * k for k in range(2, far - 1) for s in (1, -1)], [1, -1], [0]]
-    computed = None
-    for d in range(far - 1, -1, -1):
-        exchanged, computed = computed, None
-        if exchanged is not None:
-            places, out, piece = exchanged
-            piece, _ = together((piece, last))
-            exchanged = places, out, sibling(piece)
-        if tasks:
-            places = tasks.pop(0)
-            saved = up, down, up_twin, down_twin
-            up, down, up_twin, down_twin, _ = together((*saved, last))
-            out, piece = compute(places, 0)
-            out, piece, ahead = together((out, piece, ahead))
-            up, down, up_twin, down_twin = saved
-            computed = places, out, piece
-        if exchanged is not None:
-            places, out, piece = exchanged
-            piece, ahead = together((piece, ahead))
-            note(places, out, [piece])
-        if d == far - 1:
-            pad = jnp.zeros_like(ahead)
-            ahead = jnp.concatenate([ahead, pad], axis=0)
-            astern = jnp.concatenate([pad, astern], axis=0)
-        if d:
-            last = add(-d, last, ahead).astype(BF16)
-            ahead = send(last)
-            last = add(d, last, astern).astype(BF16)
-            astern = return_send(last)
+    up, down, rest, _ = together((up, down, given[2], last))
+    rest = sibling(rest)
+    (out,) = compute(places[3:], [], ())
+    out, ahead = together((out, ahead))
+    mine.update({k: (out, j) for j, k in enumerate(places[3:])})
+    theirs.update({k: (rest, j) for j, k in enumerate(places[3:])})
+    pad = jnp.zeros_like(ahead)
+    ahead, astern = jnp.concatenate([ahead, pad], axis=0), jnp.concatenate([pad, astern], axis=0)
+    for d in range(far - 1, 0, -1):
+        last = add(-d, last, ahead).astype(BF16)
+        ahead = send(last)
+        last = add(d, last, astern).astype(BF16)
+        astern = return_send(last)
     total = add(0, last, ahead)
     astern, total = together((astern, total))
     return (total + astern.astype(F32)).astype(BF16)

time: 66.6 us -> 72.8 us (1.093)
  waiting for transfers between devices: 22.7 us -> 34.1 us
  Pallas kernels: 16.5 us -> 13.3 us
  starting transfers between devices: 25.6 us -> 23.7 us
    ppermute x11, waiting for transfers between devices: 17.8 us -> 28.3 us  [local(): send = lambda a: lax.ppermute(a, 'node', spin)]
    pallas_call x4 -> x2, Pallas kernels: 15.3 us -> 12.1 us  [expert(): pl.pallas_call(functools.partial(expert_kernel, count, experts, *tiles(wi...]
    ppermute x4, starting transfers between devices: 2.74 us -> 1.45 us  [local(): return_send = lambda a: lax.ppermute(a, 'node', [(b, a) for a, b in spin])]
    ppermute x13 -> x11, starting transfers between devices: 2.72 us -> 1.68 us  [local(): sibling = lambda a: lax.ppermute(a, 'node', swap)]
    ppermute x4, waiting for transfers between devices: 2.44 us -> 3.36 us  [local(): return_send = lambda a: lax.ppermute(a, 'node', [(b, a) for a, b in spin])]
    ppermute x13 -> x11, waiting for transfers between devices: 2.47 us -> 2.47 us  [local(): sibling = lambda a: lax.ppermute(a, 'node', swap)]
  transfers between devices with their start and end apart: 28 -> 26, of which waited for: 13 -> 15; matrix products, arithmetic and copies ran while one was open for 1% -> 1% of each run, Pallas kernels for 16% -> 5%
where the time goes in v12:
time: 72.8 us; the launch traced here: 72.6 us
  waiting for transfers between devices  34.1 us (47%)
  starting transfers between devices  23.7 us (33%)
  Pallas kernels  13.3 us (18%)
  other arithmetic  1.38 us (2%)
    ppermute x11, waiting for transfers between devices, local(): send = lambda a: lax.ppermute(a, 'node', spin)  28.3 us
    ppermute x11, starting transfers between devices, local(): send = lambda a: lax.ppermute(a, 'node', spin)  20.6 us
    pallas_call x2, Pallas kernels, expert(): pl.pallas_call(functools.partial(expert_kernel, count, experts, *tiles(wi...  12.1 us
    ppermute x4, waiting for transfers between devices, local(): return_send = lambda a: lax.ppermute(a, 'node', [(b, a) for a, b in spin])  3.36 us
    ppermute x11, waiting for transfers between devices, local(): sibling = lambda a: lax.ppermute(a, 'node', swap)  2.47 us
    ppermute x11, starting transfers between devices, local(): sibling = lambda a: lax.ppermute(a, 'node', swap)  1.68 us
  transfers between devices with their start and end apart: 26, of which 15 were waited for; matrix products, arithmetic and copies ran while one was open for 1% of the time, Pallas kernels for 5%

profile of v12, /device:TPU:0, one launch (start us, length us, event | category | flops | bytes accessed | tf_op | source)
XLA Modules:
  0.0 72.6 jit_solution(9749707256343872328)
XLA Ops:
  0.0 1.1 %shard_map.64.refs_4_ = bf16[32,3712]{1,0:T(8,128)(2,1)S(1)} custom-call(bf16[32,3584]{1,0:T(8,128)(2,1)} %tok_hbm.1, s32[8,32]{1,0:T(8,128)} %bitcast.2, f32[8,32]{1,0:T(8,128)} %bitcast.3), custom_call_target="tpu_custom_call" | custom-call | flops 10737418240 | tf_op jit(solution)/shard_map/pallas_call | solution.py:59
  1.2 3.1 %collective-permute-start = (bf16[32,3712]{1,0:T(8,128)(2,1)S(1)}, bf16[32,3712]{1,0:T(8,128)(2,1)S(1)}, u32[]{:S(2)}, u32[]{:S(2)}) collective-permute-start(bf16[32,3712]{1,0:T(8,128)(2,1)S(1)} %shard_map.64.refs_4_), channel_id=1, source_target_pairs={{0,4},{4,8},{8,12},{12,14},{14,10},{10,6},{6,2},{2,0},{5,1},{9,5},... | collective-permute-start | bytes 712712 | tf_op jit(solution)/shard_map/ppermute | solution.py:150
  4.2 4.0 %collective-permute-done.refs_2_ = bf16[32,3712]{1,0:T(8,128)(2,1)S(1)} collective-permute-done((bf16[32,3712]{1,0:T(8,128)(2,1)S(1)}, bf16[32,3712]{1,0:T(8,128)(2,1)S(1)}, u32[]{:S(2)}, u32[]{:S(2)}) %collective-permute-start) | collective-permute-done | bytes 237600 | tf_op jit(solution)/shard_map/ppermute | solution.py:150
  8.3 2.1 %collective-permute-start.1 = (bf16[32,3712]{1,0:T(8,128)(2,1)S(1)}, bf16[32,3712]{1,0:T(8,128)(2,1)S(1)}, u32[]{:S(2)}, u32[]{:S(2)}) collective-permute-start(bf16[32,3712]{1,0:T(8,128)(2,1)S(1)} %collective-permute-done.refs_2_), channel_id=1, source_target_pairs={{0,4},{4,8},{8,12},{12,14},{14,10},{10,6},{6,2},{2,0},{5,1},{9,5},... | collective-permute-start | bytes 712712 | tf_op jit(solution)/shard_map/ppermute | solution.py:150
  10.4 0.0 collective-permute-done.4.refs_10_
  10.4 1.6 %collective-permute-start.5 = (bf16[32,3712]{1,0:T(8,128)(2,1)S(1)}, bf16[32,3712]{1,0:T(8,128)(2,1)S(1)}, u32[]{:S(2)}, u32[]{:S(2)}) collective-permute-start(bf16[32,3712]{1,0:T(8,128)(2,1)S(1)} %collective-permute-done.4.refs_10_), channel_id=1, source_target_pairs={{0,4},{4,8},{8,12},{12,14},{14,10},{10,6},{6,2},{2,0},{5,1},{9,5},... | collective-permute-start | bytes 712712 | tf_op jit(solution)/shard_map/ppermute | solution.py:150
  11.9 2.5 %collective-permute-done.1.refs_0_ = bf16[32,3712]{1,0:T(8,128)(2,1)S(1)} collective-permute-done((bf16[32,3712]{1,0:T(8,128)(2,1)S(1)}, bf16[32,3712]{1,0:T(8,128)(2,1)S(1)}, u32[]{:S(2)}, u32[]{:S(2)}) %collective-permute-start.1) | collective-permute-done | bytes 237600 | tf_op jit(solution)/shard_map/ppermute | solution.py:150
  14.4 2.1 %collective-permute-start.2 = (bf16[32,3712]{1,0:T(8,128)(2,1)S(1)}, bf16[32,3712]{1,0:T(8,128)(2,1)S(1)}, u32[]{:S(2)}, u32[]{:S(2)}) collective-permute-start(bf16[32,3712]{1,0:T(8,128)(2,1)S(1)} %collective-permute-done.1.refs_0_), channel_id=1, source_target_pairs={{0,4},{4,8},{8,12},{12,14},{14,10},{10,6},{6,2},{2,0},{5,1},{9,5},... | collective-permute-start | bytes 712712 | tf_op jit(solution)/shard_map/ppermute | solution.py:150
  16.5 0.5 collective-permute-done.5.refs_9_
  16.9 2.1 %collective-permute-start.6 = (bf16[32,3712]{1,0:T(8,128)(2,1)S(1)}, bf16[32,3712]{1,0:T(8,128)(2,1)S(1)}, u32[]{:S(2)}, u32[]{:S(2)}) collective-permute-start(bf16[32,3712]{1,0:T(8,128)(2,1)S(1)} %collective-permute-done.5.refs_9_), channel_id=1, source_target_pairs={{0,4},{4,8},{8,12},{12,14},{14,10},{10,6},{6,2},{2,0},{5,1},{9,5},... | collective-permute-start | bytes 712712 | tf_op jit(solution)/shard_map/ppermute | solution.py:150
  19.0 0.0 collective-permute-start.11
  19.0 0.5 collective-permute-start.12
  19.5 1.0 %collective-permute-done.2.refs_1_ = bf16[32,3712]{1,0:T(8,128)(2,1)S(1)} collective-permute-done((bf16[32,3712]{1,0:T(8,128)(2,1)S(1)}, bf16[32,3712]{1,0:T(8,128)(2,1)S(1)}, u32[]{:S(2)}, u32[]{:S(2)}) %collective-permute-start.2) | collective-permute-done | bytes 237600 | tf_op jit(solution)/shard_map/ppermute | solution.py:150
  20.5 2.1 %collective-permute-start.3 = (bf16[32,3712]{1,0:T(8,128)(2,1)S(1)}, bf16[32,3712]{1,0:T(8,128)(2,1)S(1)}, u32[]{:S(2)}, u32[]{:S(2)}) collective-permute-start(bf16[32,3712]{1,0:T(8,128)(2,1)S(1)} %collective-permute-done.2.refs_1_), channel_id=1, source_target_pairs={{0,4},{4,8},{8,12},{12,14},{14,10},{10,6},{6,2},{2,0},{5,1},{9,5},... | collective-permute-start | bytes 712712 | tf_op jit(solution)/shard_map/ppermute | solution.py:150
  22.6 0.5 collective-permute-done.6.refs_7_
  23.0 2.1 %collective-permute-start.7 = (bf16[32,3712]{1,0:T(8,128)(2,1)S(1)}, bf16[32,3712]{1,0:T(8,128)(2,1)S(1)}, u32[]{:S(2)}, u32[]{:S(2)}) collective-permute-start(bf16[32,3712]{1,0:T(8,128)(2,1)S(1)} %collective-permute-done.6.refs_7_), channel_id=1, source_target_pairs={{0,4},{4,8},{8,12},{12,14},{14,10},{10,6},{6,2},{2,0},{5,1},{9,5},... | collective-permute-start | bytes 712712 | tf_op jit(solution)/shard_map/ppermute | solution.py:150
  25.1 0.5 collective-permute-start.13
  25.6 0.1 collective-permute-start.9
  25.7 0.9 %collective-permute-done.3.refs_0_ = bf16[32,3712]{1,0:T(8,128)(2,1)S(1)} collective-permute-done((bf16[32,3712]{1,0:T(8,128)(2,1)S(1)}, bf16[32,3712]{1,0:T(8,128)(2,1)S(1)}, u32[]{:S(2)}, u32[]{:S(2)}) %collective-permute-start.3) | collective-permute-done | bytes 237600 | tf_op jit(solution)/shard_map/ppermute | solution.py:150
  26.6 2.5 %collective-permute-done.7.refs_5_ = bf16[32,3712]{1,0:T(8,128)(2,1)S(1)} collective-permute-done((bf16[32,3712]{1,0:T(8,128)(2,1)S(1)}, bf16[32,3712]{1,0:T(8,128)(2,1)S(1)}, u32[]{:S(2)}, u32[]{:S(2)}) %collective-permute-start.7) | collective-permute-done | bytes 237600 | tf_op jit(solution)/shard_map/ppermute | solution.py:150
  29.2 1.5 %collective-permute-done.10.refs_2_ = bf16[32,3712]{1,0:T(8,128)(2,1)S(1)} collective-permute-done((bf16[32,3712]{1,0:T(8,128)(2,1)S(1)}, bf16[32,3712]{1,0:T(8,128)(2,1)S(1)}, u32[]{:S(2)}, u32[]{:S(2)}) %collective-permute-start.10) | collective-permute-done | bytes 237600 | tf_op jit(solution)/shard_map/ppermute | solution.py:151
  30.7 8.3 %shard_map.65 = (f32[96,3584]{1,0:T(8,128)S(1)}, bf16[32,3584]{1,0:T(8,128)(2,1)S(1)}, bf16[64,3584]{1,0:T(8,128)(2,1)S(1)}, bf16[160,3584]{1,0:T(8,128)(2,1)S(1)}) custom-call(bf16[32,3712]{1,0:T(8,128)(2,1)S(1)} %collective-permute-done.3.refs_0_, bf16[32,3712]{1,0:T(8,128)(2,1)S(1)} %collective-permute-done.2.refs_1_, ...), custom_call_target="tpu_custom_call" | custom-call | flops 7751073792 | tf_op jit(solution)/shard_map/pallas_call | solution.py:130
  38.9 0.2 collective-permute-start.15
  39.1 0.4 collective-permute-start.18
  39.5 1.0 %collective-permute-done.15 = bf16[32,3584]{1,0:T(8,128)(2,1)S(1)} collective-permute-done((bf16[32,3584]{1,0:T(8,128)(2,1)S(1)}, bf16[32,3584]{1,0:T(8,128)(2,1)S(1)}, u32[]{:S(2)}, u32[]{:S(2)}) %collective-permute-start.15) | collective-permute-done | bytes 229408 | tf_op jit(solution)/shard_map/ppermute | solution.py:151
  40.6 2.1 %collective-permute-start.16 = (bf16[16,3584]{1,0:T(8,128)(2,1)S(1)}, bf16[16,3584]{1,0:T(8,128)(2,1)S(1)}, u32[]{:S(2)}, u32[]{:S(2)}) collective-permute-start(bf16[16,3584]{1,0:T(8,128)(2,1)S(1)} %get-tuple-element.95), channel_id=1, source_target_pairs={{0,4},{4,8},{8,12},{12,14},{14,10},{10,6},{6,2},{2,0},{5,1},{9,5},... | collective-permute-start | bytes 344072 | tf_op jit(solution)/shard_map/ppermute | solution.py:150
  42.7 0.0 collective-permute-start.19
  42.7 3.8 %shard_map.66 = f32[160,3584]{1,0:T(8,128)S(1)} custom-call(bf16[32,3712]{1,0:T(8,128)(2,1)S(1)} %collective-permute-done.1.refs_0_, bf16[32,3712]{1,0:T(8,128)(2,1)S(1)} %collective-permute-done.9.refs_1_, bf16[32,3712]{1,0:T(8,128)(2,1)S(1)} %collective-permute-done.refs_2_, bf16[32,3712]{1,0:T(8,128)(2,1)S(1)} %collective-permute-done.8.refs_3_, ...), custom_call_target="tpu_custom_call" | custom-call | flops 5637144576 | tf_op jit(solution)/shard_map/pallas_call | solution.py:130
  46.6 0.9 %collective-permute-done.19 = bf16[16,3584]{1,0:T(8,128)(2,1)S(1)} collective-permute-done((bf16[16,3584]{1,0:T(8,128)(2,1)S(1)}, bf16[16,3584]{1,0:T(8,128)(2,1)S(1)}, u32[]{:S(2)}, u32[]{:S(2)}) %collective-permute-start.19) | collective-permute-done | bytes 114720 | tf_op jit(solution)/shard_map/ppermute | solution.py:192
  47.5 0.1 add_convert_fusion.6
  47.6 1.6 %collective-permute-start.21 = (bf16[32,3584]{1,0:T(8,128)(2,1)S(1)}, bf16[32,3584]{1,0:T(8,128)(2,1)S(1)}, u32[]{:S(2)}, u32[]{:S(2)}) collective-permute-start(bf16[32,3584]{1,0:T(8,128)(2,1)S(1)} %add_convert_fusion.6), channel_id=1, source_target_pairs={{0,4},{4,8},{8,12},{12,14},{14,10},{10,6},{6,2},{2,0},{5,1},{9,5},... | collective-permute-start | bytes 688136 | tf_op jit(solution)/shard_map/ppermute | solution.py:150
  49.2 0.1 add_convert_fusion.5
  49.3 0.5 collective-permute-start.20
  49.8 5.9 %collective-permute-done.21 = bf16[32,3584]{1,0:T(8,128)(2,1)S(1)} collective-permute-done((bf16[32,3584]{1,0:T(8,128)(2,1)S(1)}, bf16[32,3584]{1,0:T(8,128)(2,1)S(1)}, u32[]{:S(2)}, u32[]{:S(2)}) %collective-permute-start.21) | collective-permute-done | bytes 229408 | tf_op jit(solution)/shard_map/ppermute | solution.py:150
  55.7 0.1 add_convert_fusion.4
  55.8 1.3 %collective-permute-start.23 = (bf16[32,3584]{1,0:T(8,128)(2,1)S(1)}, bf16[32,3584]{1,0:T(8,128)(2,1)S(1)}, u32[]{:S(2)}, u32[]{:S(2)}) collective-permute-start(bf16[32,3584]{1,0:T(8,128)(2,1)S(1)} %add_convert_fusion.4), channel_id=1, source_target_pairs={{0,4},{4,8},{8,12},{12,14},{14,10},{10,6},{6,2},{2,0},{5,1},{9,5},... | collective-permute-start | bytes 688136 | tf_op jit(solution)/shard_map/ppermute | solution.py:150
  57.1 0.1 add_convert_fusion.3
  57.2 0.8 %collective-permute-start.22 = (bf16[32,3584]{1,0:T(8,128)(2,1)S(1)}, bf16[32,3584]{1,0:T(8,128)(2,1)S(1)}, u32[]{:S(2)}, u32[]{:S(2)}) collective-permute-start(bf16[32,3584]{1,0:T(8,128)(2,1)S(1)} %add_convert_fusion.3), channel_id=1, source_target_pairs={{4,0},{8,4},{12,8},{14,12},{10,14},{6,10},{2,6},{0,2},{1,5},{5,9},... | collective-permute-start | bytes 688136 | tf_op jit(solution)/shard_map/ppermute | solution.py:192
  58.1 5.6 %collective-permute-done.23 = bf16[32,3584]{1,0:T(8,128)(2,1)S(1)} collective-permute-done((bf16[32,3584]{1,0:T(8,128)(2,1)S(1)}, bf16[32,3584]{1,0:T(8,128)(2,1)S(1)}, u32[]{:S(2)}, u32[]{:S(2)}) %collective-permute-start.23) | collective-permute-done | bytes 229408 | tf_op jit(solution)/shard_map/ppermute | solution.py:150
  63.6 0.1 add_convert_fusion.2
  63.7 0.5 collective-permute-start.25
  64.2 1.6 %collective-permute-done.22 = bf16[32,3584]{1,0:T(8,128)(2,1)S(1)} collective-permute-done((bf16[32,3584]{1,0:T(8,128)(2,1)S(1)}, bf16[32,3584]{1,0:T(8,128)(2,1)S(1)}, u32[]{:S(2)}, u32[]{:S(2)}) %collective-permute-start.22) | collective-permute-done | bytes 229408 | tf_op jit(solution)/shard_map/ppermute | solution.py:192
  65.7 0.1 add_convert_fusion.1
  65.8 0.1 collective-permute-start.24
  65.9 5.0 %collective-permute-done.25 = bf16[32,3584]{1,0:T(8,128)(2,1)S(1)} collective-permute-done((bf16[32,3584]{1,0:T(8,128)(2,1)S(1)}, bf16[32,3584]{1,0:T(8,128)(2,1)S(1)}, u32[]{:S(2)}, u32[]{:S(2)}) %collective-permute-start.25) | collective-permute-done | bytes 229408 | tf_op jit(solution)/shard_map/ppermute | solution.py:150
  70.9 0.1 convert_add_fusion
  71.0 0.9 %collective-permute-done.24 = bf16[32,3584]{1,0:T(8,128)(2,1)S(1)} collective-permute-done((bf16[32,3584]{1,0:T(8,128)(2,1)S(1)}, bf16[32,3584]{1,0:T(8,128)(2,1)S(1)}, u32[]{:S(2)}, u32[]{:S(2)}) %collective-permute-start.24) | collective-permute-done | bytes 229408 | tf_op jit(solution)/shard_map/ppermute | solution.py:192
  71.9 0.7 %add_convert_fusion = bf16[32,3584]{1,0:T(8,128)(2,1)} fusion(f32[32,3584]{1,0:T(8,128)S(1)} %convert_add_fusion, bf16[32,3584]{1,0:T(8,128)(2,1)S(1)} %collective-permute-done.24), kind=kLoop, calls=%fused_computation | loop fusion | flops 344064 | bytes 917504 | tf_op jit(solution)/shard_map/convert_element_type | solution.py:209
  (25 shorter events, 0.1 us)
Async XLA Ops:
  0.0 30.6 %copy-start = (bf16[1,3584,1024]{2,1,0:T(8,128)(2,1)S(1)}, bf16[1,3584,1024]{2,1,0:T(8,128)(2,1)}, u32[]{:S(2)}) copy-start(bf16[1,3584,1024]{2,1,0:T(8,128)(2,1)} %refs_5_.1) | copy-start | bytes 22020100
  0.0 30.6 %copy-start.1 = (bf16[1,3584,1024]{2,1,0:T(8,128)(2,1)S(1)}, bf16[1,3584,1024]{2,1,0:T(8,128)(2,1)}, u32[]{:S(2)}) copy-start(bf16[1,3584,1024]{2,1,0:T(8,128)(2,1)} %refs_6_.1) | copy-start | bytes 22020100
  0.0 30.7 %copy-start.2 = (bf16[1,1024,3584]{2,1,0:T(8,128)(2,1)S(1)}, bf16[1,1024,3584]{2,1,0:T(8,128)(2,1)}, u32[]{:S(2)}) copy-start(bf16[1,1024,3584]{2,1,0:T(8,128)(2,1)} %refs_7_.1) | copy-start | bytes 22020100
  1.2 7.1 %collective-permute-start = (bf16[32,3712]{1,0:T(8,128)(2,1)S(1)}, bf16[32,3712]{1,0:T(8,128)(2,1)S(1)}, u32[]{:S(2)}, u32[]{:S(2)}) collective-permute-start(bf16[32,3712]{1,0:T(8,128)(2,1)S(1)} %shard_map.64.refs_4_), channel_id=1, source_target_pairs={{0,4},{4,8},{8,12},{12,14},{14,10},{10,6},{6,2},{2,0},{5,1},{9,5},... | collective-permute-start | bytes 712712 | tf_op jit(solution)/shard_map/ppermute | solution.py:150
  4.2 6.1 %collective-permute-start.4 = (bf16[32,3712]{1,0:T(8,128)(2,1)S(1)}, bf16[32,3712]{1,0:T(8,128)(2,1)S(1)}, u32[]{:S(2)}, u32[]{:S(2)}) collective-permute-start(bf16[32,3712]{1,0:T(8,128)(2,1)S(1)} %shard_map.64.refs_4_), channel_id=1, source_target_pairs={{0,1},{1,0},{2,3},{3,2},{4,5},{5,4},{6,7},{7,6},{8,9},{9,8},{10,11... | collective-permute-start | bytes 712712 | tf_op jit(solution)/shard_map/ppermute | solution.py:151
  8.3 6.1 %collective-permute-start.1 = (bf16[32,3712]{1,0:T(8,128)(2,1)S(1)}, bf16[32,3712]{1,0:T(8,128)(2,1)S(1)}, u32[]{:S(2)}, u32[]{:S(2)}) collective-permute-start(bf16[32,3712]{1,0:T(8,128)(2,1)S(1)} %collective-permute-done.refs_2_), channel_id=1, source_target_pairs={{0,4},{4,8},{8,12},{12,14},{14,10},{10,6},{6,2},{2,0},{5,1},{9,5},... | collective-permute-start | bytes 712712 | tf_op jit(solution)/shard_map/ppermute | solution.py:150
  10.4 6.6 %collective-permute-start.5 = (bf16[32,3712]{1,0:T(8,128)(2,1)S(1)}, bf16[32,3712]{1,0:T(8,128)(2,1)S(1)}, u32[]{:S(2)}, u32[]{:S(2)}) collective-permute-start(bf16[32,3712]{1,0:T(8,128)(2,1)S(1)} %collective-permute-done.4.refs_10_), channel_id=1, source_target_pairs={{0,4},{4,8},{8,12},{12,14},{14,10},{10,6},{6,2},{2,0},{5,1},{9,5},... | collective-permute-start | bytes 712712 | tf_op jit(solution)/shard_map/ppermute | solution.py:150
  14.4 6.1 %collective-permute-start.2 = (bf16[32,3712]{1,0:T(8,128)(2,1)S(1)}, bf16[32,3712]{1,0:T(8,128)(2,1)S(1)}, u32[]{:S(2)}, u32[]{:S(2)}) collective-permute-start(bf16[32,3712]{1,0:T(8,128)(2,1)S(1)} %collective-permute-done.1.refs_0_), channel_id=1, source_target_pairs={{0,4},{4,8},{8,12},{12,14},{14,10},{10,6},{6,2},{2,0},{5,1},{9,5},... | collective-permute-start | bytes 712712 | tf_op jit(solution)/shard_map/ppermute | solution.py:150
  16.9 6.1 %collective-permute-start.6 = (bf16[32,3712]{1,0:T(8,128)(2,1)S(1)}, bf16[32,3712]{1,0:T(8,128)(2,1)S(1)}, u32[]{:S(2)}, u32[]{:S(2)}) collective-permute-start(bf16[32,3712]{1,0:T(8,128)(2,1)S(1)} %collective-permute-done.5.refs_9_), channel_id=1, source_target_pairs={{0,4},{4,8},{8,12},{12,14},{14,10},{10,6},{6,2},{2,0},{5,1},{9,5},... | collective-permute-start | bytes 712712 | tf_op jit(solution)/shard_map/ppermute | solution.py:150
  19.0 6.1 %collective-permute-start.11 = (bf16[32,3712]{1,0:T(8,128)(2,1)S(1)}, bf16[32,3712]{1,0:T(8,128)(2,1)S(1)}, u32[]{:S(2)}, u32[]{:S(2)}) collective-permute-start(bf16[32,3712]{1,0:T(8,128)(2,1)S(1)} %collective-permute-done.refs_2_), channel_id=1, source_target_pairs={{0,1},{1,0},{2,3},{3,2},{4,5},{5,4},{6,7},{7,6},{8,9},{9,8},{10,11... | collective-permute-start | bytes 712712 | tf_op jit(solution)/shard_map/ppermute | solution.py:151
  19.0 6.6 %collective-permute-start.12 = (bf16[32,3712]{1,0:T(8,128)(2,1)S(1)}, bf16[32,3712]{1,0:T(8,128)(2,1)S(1)}, u32[]{:S(2)}, u32[]{:S(2)}) collective-permute-start(bf16[32,3712]{1,0:T(8,128)(2,1)S(1)} %collective-permute-done.1.refs_0_), channel_id=1, source_target_pairs={{0,1},{1,0},{2,3},{3,2},{4,5},{5,4},{6,7},{7,6},{8,9},{9,8},{10,11... | collective-permute-start | bytes 712712 | tf_op jit(solution)/shard_map/ppermute | solution.py:151
  20.5 6.1 %collective-permute-start.3 = (bf16[32,3712]{1,0:T(8,128)(2,1)S(1)}, bf16[32,3712]{1,0:T(8,128)(2,1)S(1)}, u32[]{:S(2)}, u32[]{:S(2)}) collective-permute-start(bf16[32,3712]{1,0:T(8,128)(2,1)S(1)} %collective-permute-done.2.refs_1_), channel_id=1, source_target_pairs={{0,4},{4,8},{8,12},{12,14},{14,10},{10,6},{6,2},{2,0},{5,1},{9,5},... | collective-permute-start | bytes 712712 | tf_op jit(solution)/shard_map/ppermute | solution.py:150
  23.0 6.1 %collective-permute-start.7 = (bf16[32,3712]{1,0:T(8,128)(2,1)S(1)}, bf16[32,3712]{1,0:T(8,128)(2,1)S(1)}, u32[]{:S(2)}, u32[]{:S(2)}) collective-permute-start(bf16[32,3712]{1,0:T(8,128)(2,1)S(1)} %collective-permute-done.6.refs_7_), channel_id=1, source_target_pairs={{0,4},{4,8},{8,12},{12,14},{14,10},{10,6},{6,2},{2,0},{5,1},{9,5},... | collective-permute-start | bytes 712712 | tf_op jit(solution)/shard_map/ppermute | solution.py:150
  25.1 4.0 %collective-permute-start.8 = (bf16[32,3712]{1,0:T(8,128)(2,1)S(1)}, bf16[32,3712]{1,0:T(8,128)(2,1)S(1)}, u32[]{:S(2)}, u32[]{:S(2)}) collective-permute-start(bf16[32,3712]{1,0:T(8,128)(2,1)S(1)} %collective-permute-done.5.refs_9_), channel_id=1, source_target_pairs={{0,1},{1,0},{2,3},{3,2},{4,5},{5,4},{6,7},{7,6},{8,9},{9,8},{10,11... | collective-permute-start | bytes 712712 | tf_op jit(solution)/shard_map/ppermute | solution.py:151
  25.1 4.0 %collective-permute-start.13 = (bf16[32,3712]{1,0:T(8,128)(2,1)S(1)}, bf16[32,3712]{1,0:T(8,128)(2,1)S(1)}, u32[]{:S(2)}, u32[]{:S(2)}) collective-permute-start(bf16[32,3712]{1,0:T(8,128)(2,1)S(1)} %collective-permute-done.2.refs_1_), channel_id=1, source_target_pairs={{0,1},{1,0},{2,3},{3,2},{4,5},{5,4},{6,7},{7,6},{8,9},{9,8},{10,11... | collective-permute-start | bytes 712712 | tf_op jit(solution)/shard_map/ppermute | solution.py:151
  25.6 3.5 %collective-permute-start.9 = (bf16[32,3712]{1,0:T(8,128)(2,1)S(1)}, bf16[32,3712]{1,0:T(8,128)(2,1)S(1)}, u32[]{:S(2)}, u32[]{:S(2)}) collective-permute-start(bf16[32,3712]{1,0:T(8,128)(2,1)S(1)} %collective-permute-done.6.refs_7_), channel_id=1, source_target_pairs={{0,1},{1,0},{2,3},{3,2},{4,5},{5,4},{6,7},{7,6},{8,9},{9,8},{10,11... | collective-permute-start | bytes 712712 | tf_op jit(solution)/shard_map/ppermute | solution.py:151
  26.6 2.6 %collective-permute-start.14 = (bf16[32,3712]{1,0:T(8,128)(2,1)S(1)}, bf16[32,3712]{1,0:T(8,128)(2,1)S(1)}, u32[]{:S(2)}, u32[]{:S(2)}) collective-permute-start(bf16[32,3712]{1,0:T(8,128)(2,1)S(1)} %collective-permute-done.3.refs_0_), channel_id=1, source_target_pairs={{0,1},{1,0},{2,3},{3,2},{4,5},{5,4},{6,7},{7,6},{8,9},{9,8},{10,11... | collective-permute-start | bytes 712712 | tf_op jit(solution)/shard_map/ppermute | solution.py:151
  29.1 1.5 %collective-permute-start.10 = (bf16[32,3712]{1,0:T(8,128)(2,1)S(1)}, bf16[32,3712]{1,0:T(8,128)(2,1)S(1)}, u32[]{:S(2)}, u32[]{:S(2)}) collective-permute-start(bf16[32,3712]{1,0:T(8,128)(2,1)S(1)} %collective-permute-done.7.refs_5_), channel_id=1, source_target_pairs={{0,1},{1,0},{2,3},{3,2},{4,5},{5,4},{6,7},{7,6},{8,9},{9,8},{10,11... | collective-permute-start | bytes 712712 | tf_op jit(solution)/shard_map/ppermute | solution.py:151
  38.9 1.6 %collective-permute-start.15 = (bf16[32,3584]{1,0:T(8,128)(2,1)S(1)}, bf16[32,3584]{1,0:T(8,128)(2,1)S(1)}, u32[]{:S(2)}, u32[]{:S(2)}) collective-permute-start(bf16[32,3584]{1,0:T(8,128)(2,1)S(1)} %get-tuple-element.68), channel_id=1, source_target_pairs={{0,1},{1,0},{2,3},{3,2},{4,5},{5,4},{6,7},{7,6},{8,9},{9,8},{10,11... | collective-permute-start | bytes 688136 | tf_op jit(solution)/shard_map/ppermute | solution.py:151
  39.1 8.4 %collective-permute-start.18 = (bf16[64,3584]{1,0:T(8,128)(2,1)S(1)}, bf16[64,3584]{1,0:T(8,128)(2,1)S(1)}, u32[]{:S(2)}, u32[]{:S(2)}) collective-permute-start(bf16[64,3584]{1,0:T(8,128)(2,1)S(1)} %get-tuple-element.77), channel_id=1, source_target_pairs={{0,1},{1,0},{2,3},{3,2},{4,5},{5,4},{6,7},{7,6},{8,9},{9,8},{10,11... | collective-permute-start | bytes 1376264 | tf_op jit(solution)/shard_map/ppermute | solution.py:151
  40.6 6.0 %collective-permute-start.16 = (bf16[16,3584]{1,0:T(8,128)(2,1)S(1)}, bf16[16,3584]{1,0:T(8,128)(2,1)S(1)}, u32[]{:S(2)}, u32[]{:S(2)}) collective-permute-start(bf16[16,3584]{1,0:T(8,128)(2,1)S(1)} %get-tuple-element.95), channel_id=1, source_target_pairs={{0,4},{4,8},{8,12},{12,14},{14,10},{10,6},{6,2},{2,0},{5,1},{9,5},... | collective-permute-start | bytes 344072 | tf_op jit(solution)/shard_map/ppermute | solution.py:150
  42.7 4.8 %collective-permute-start.19 = (bf16[16,3584]{1,0:T(8,128)(2,1)S(1)}, bf16[16,3584]{1,0:T(8,128)(2,1)S(1)}, u32[]{:S(2)}, u32[]{:S(2)}) collective-permute-start(bf16[16,3584]{1,0:T(8,128)(2,1)S(1)} %get-tuple-element.96), channel_id=1, source_target_pairs={{4,0},{8,4},{12,8},{14,12},{10,14},{6,10},{2,6},{0,2},{1,5},{5,9},... | collective-permute-start | bytes 344072 | tf_op jit(solution)/shard_map/ppermute | solution.py:192
  42.7 13.0 %collective-permute-start.17 = (bf16[160,3584]{1,0:T(8,128)(2,1)S(1)}, bf16[160,3584]{1,0:T(8,128)(2,1)S(1)}, u32[]{:S(2)}, u32[]{:S(2)}) collective-permute-start(bf16[160,3584]{1,0:T(8,128)(2,1)S(1)} %get-tuple-element.76), channel_id=1, source_target_pairs={{0,1},{1,0},{2,3},{3,2},{4,5},{5,4},{6,7},{7,6},{8,9},{9,8},{10,11... | collective-permute-start | bytes 3440648 | tf_op jit(solution)/shard_map/ppermute | solution.py:151
  47.6 8.1 %collective-permute-start.21 = (bf16[32,3584]{1,0:T(8,128)(2,1)S(1)}, bf16[32,3584]{1,0:T(8,128)(2,1)S(1)}, u32[]{:S(2)}, u32[]{:S(2)}) collective-permute-start(bf16[32,3584]{1,0:T(8,128)(2,1)S(1)} %add_convert_fusion.6), channel_id=1, source_target_pairs={{0,4},{4,8},{8,12},{12,14},{14,10},{10,6},{6,2},{2,0},{5,1},{9,5},... | collective-permute-start | bytes 688136 | tf_op jit(solution)/shard_map/ppermute | solution.py:150
  49.3 7.8 %collective-permute-start.20 = (bf16[32,3584]{1,0:T(8,128)(2,1)S(1)}, bf16[32,3584]{1,0:T(8,128)(2,1)S(1)}, u32[]{:S(2)}, u32[]{:S(2)}) collective-permute-start(bf16[32,3584]{1,0:T(8,128)(2,1)S(1)} %add_convert_fusion.5), channel_id=1, source_target_pairs={{4,0},{8,4},{12,8},{14,12},{10,14},{6,10},{2,6},{0,2},{1,5},{5,9},... | collective-permute-start | bytes 688136 | tf_op jit(solution)/shard_map/ppermute | solution.py:192
  55.8 7.8 %collective-permute-start.23 = (bf16[32,3584]{1,0:T(8,128)(2,1)S(1)}, bf16[32,3584]{1,0:T(8,128)(2,1)S(1)}, u32[]{:S(2)}, u32[]{:S(2)}) collective-permute-start(bf16[32,3584]{1,0:T(8,128)(2,1)S(1)} %add_convert_fusion.4), channel_id=1, source_target_pairs={{0,4},{4,8},{8,12},{12,14},{14,10},{10,6},{6,2},{2,0},{5,1},{9,5},... | collective-permute-start | bytes 688136 | tf_op jit(solution)/shard_map/ppermute | solution.py:150
  57.2 8.5 %collective-permute-start.22 = (bf16[32,3584]{1,0:T(8,128)(2,1)S(1)}, bf16[32,3584]{1,0:T(8,128)(2,1)S(1)}, u32[]{:S(2)}, u32[]{:S(2)}) collective-permute-start(bf16[32,3584]{1,0:T(8,128)(2,1)S(1)} %add_convert_fusion.3), channel_id=1, source_target_pairs={{4,0},{8,4},{12,8},{14,12},{10,14},{6,10},{2,6},{0,2},{1,5},{5,9},... | collective-permute-start | bytes 688136 | tf_op jit(solution)/shard_map/ppermute | solution.py:192
  63.7 7.2 %collective-permute-start.25 = (bf16[32,3584]{1,0:T(8,128)(2,1)S(1)}, bf16[32,3584]{1,0:T(8,128)(2,1)S(1)}, u32[]{:S(2)}, u32[]{:S(2)}) collective-permute-start(bf16[32,3584]{1,0:T(8,128)(2,1)S(1)} %add_convert_fusion.2), channel_id=1, source_target_pairs={{0,4},{4,8},{8,12},{12,14},{14,10},{10,6},{6,2},{2,0},{5,1},{9,5},... | collective-permute-start | bytes 688136 | tf_op jit(solution)/shard_map/ppermute | solution.py:150
  65.8 6.1 %collective-permute-start.24 = (bf16[32,3584]{1,0:T(8,128)(2,1)S(1)}, bf16[32,3584]{1,0:T(8,128)(2,1)S(1)}, u32[]{:S(2)}, u32[]{:S(2)}) collective-permute-start(bf16[32,3584]{1,0:T(8,128)(2,1)S(1)} %add_convert_fusion.1), channel_id=1, source_target_pairs={{4,0},{8,4},{12,8},{14,12},{10,14},{6,10},{2,6},{0,2},{1,5},{5,9},... | collective-permute-start | bytes 688136 | tf_op jit(solution)/shard_map/ppermute | solution.py:192

commit v13 on v9

--- a/solution.py
+++ b/solution.py
@@ -9,7 +9,6 @@
 
 F32, BF16 = jnp.float32, jnp.bfloat16
 SCRATCH = 20 * 2**20
-GROUP = 8
 
 
 def chip_order(mesh):
@@ -168,36 +167,59 @@
         kept += [down_twin[k], down[k]]
         given += [up[k], up_twin[k]]
     kept, given = kept + [own], given + [up_twin[0]]
-    mine, theirs = [], []
-    for at in range(0, len(kept), GROUP):
-        some = slice(at, at + GROUP)
-        n = len(kept[some])
-        sizes = [m for m in (min(n, 2), min(n - 2, 2), n - 4) if m > 0]
-        out = expert(kept[some] + given[some], [(n, F32)] + [(m, BF16) for m in sizes], experts, w_gate, w_up, w_down)
-        mine += [block(out[0], j) for j in range(n)]
-        for m, piece in zip(sizes, out[1:]):
-            piece = sibling(piece)
-            theirs += [(piece, j) for j in range(m)]
+    end = len(kept) - 1
+    mine, theirs = {}, {}
+
+    def compute(keep, give, sizes):
+        sizes = [n for n in sizes if n]
+        blocks = [kept[j] for j in keep] + [given[j] for j in give]
+        out, *pieces = expert(blocks, [(len(keep), F32)] + [(n, BF16) for n in sizes], experts, w_gate, w_up, w_down)
+        return out, pieces
+
+    def note(keep, out, give, pieces):
+        mine.update({j: (out, at) for at, j in enumerate(keep)})
+        theirs.update(zip(give, [(piece, at) for piece in pieces for at in range(piece.shape[0] // rows)]))
+
+    keep, give = [end], [end - 2, end - 1, end]
+    kept[end], given[end - 2 :], _ = together((kept[end], given[end - 2 :], up[far - 1]))
+    out, pieces = compute(keep, give, (3,))
+    out, pieces, kept[0], given[2] = together((out, pieces, kept[0], given[2]))
+    given[0] = sibling(kept[0])
+    kept[2] = sibling(given[2])
+    pieces = [sibling(p) for p in pieces]
+    note(keep, out, give, pieces)
+
+    keep, give = [end - 2, end - 1], [end - 4, end - 3]
+    kept[end - 2 : end], given[end - 4 : end - 2], _ = together((kept[end - 2 : end], given[end - 4 : end - 2], kept[0]))
+    out_too, given_too = compute(keep, give, (2,))
+    out_too, given_too, given[0], kept[2], pieces = together((out_too, given_too, given[0], kept[2], pieces))
+    note([end], out, [end - 2, end - 1, end], pieces)
+    sent_too = [sibling(p) for p in given_too]
+
+    keep_last, give_last = list(range(end - 2)), list(range(end - 4))
+    out, pieces = compute(keep_last, give_last, (2, len(give_last) - 2))
+    out, pieces, sent_too = together((out, pieces, sent_too))
+    note(keep, out_too, give, sent_too)
+    note(keep_last, out, give_last, [sibling(p) for p in pieces])
 
     def add(j, *arrived):
         nonlocal last
         piece, at = theirs[j]
         (piece, *arrived), _ = together(((piece, *arrived), last))
-        total = mine[j] + block(piece, at).astype(F32)
+        total = block(*mine[j]) + block(piece, at).astype(F32)
         for a in arrived:
             total = total + a.astype(F32)
         last = total.astype(BF16)
         return last
 
-    last = mine[0]
+    last = mine[0][0]
     sums = send(add(0))
     sums_twin = []
-    for j in range(1, len(mine) - 1, 2):
+    for j in range(1, end, 2):
         sums_twin = [send(add(j, *sums_twin))]
         sums = send(add(j + 1, sums))
-    end = len(mine) - 1
     piece, sums = together((theirs[end][0], sums))
-    total = mine[end] + block(piece, theirs[end][1]).astype(F32) + sums.astype(F32)
+    total = block(*mine[end]) + block(piece, theirs[end][1]).astype(F32) + sums.astype(F32)
     for a in sums_twin:
         a, total = together((sibling(a), total))
         total = total + a.astype(F32)

time: 67.5 us -> 68.1 us (level)
  Pallas kernels: 12.9 us -> 13.8 us
  waiting for transfers between devices: 21.3 us -> 20.6 us
    ppermute x12 -> x13, waiting for transfers between devices: 2.66 us -> 1.74 us  [local(): sibling = lambda a: lax.ppermute(a, 'node', swap)]
    pallas_call x1 -> x3, Pallas kernels: 11.8 us -> 12.6 us  [expert(): pl.pallas_call(functools.partial(expert_kernel, count, experts, *tiles(wi...]
    ppermute x12 -> x13, starting transfers between devices: 2.77 us -> 2.76 us  [local(): sibling = lambda a: lax.ppermute(a, 'node', swap)]
  transfers between devices with their start and end apart: 26 -> 27, of which waited for: 14 -> 15; matrix products, arithmetic and copies ran while one was open for 1% -> 1% of each run, Pallas kernels for 0% -> 19%
where the time goes in v13:
time: 68.1 us; the launch traced here: 67.9 us
  starting transfers between devices  32.2 us (47%)
  waiting for transfers between devices  20.6 us (30%)
  Pallas kernels  13.8 us (20%)
  other arithmetic  1.32 us (2%)
    ppermute x14, starting transfers between devices, local(): send = lambda a: lax.ppermute(a, 'node', spin)  29.4 us
    ppermute x14, waiting for transfers between devices, local(): send = lambda a: lax.ppermute(a, 'node', spin)  18.8 us
    pallas_call x3, Pallas kernels, expert(): pl.pallas_call(functools.partial(expert_kernel, count, experts, *tiles(wi...  12.6 us
    ppermute x13, starting transfers between devices, local(): sibling = lambda a: lax.ppermute(a, 'node', swap)  2.76 us
    ppermute x13, waiting for transfers between devices, local(): sibling = lambda a: lax.ppermute(a, 'node', swap)  1.74 us
  transfers between devices with their start and end apart: 27, of which 15 were waited for; matrix products, arithmetic and copies ran while one was open for 1% of the time, Pallas kernels for 19%

profile of v13, /device:TPU:0, one launch (start us, length us, event | category | flops | bytes accessed | tf_op | source)
XLA Modules:
  0.0 67.9 jit_solution(3763386978588741192)
XLA Ops:
  0.0 1.1 %shard_map.64.refs_0_ = bf16[32,3712]{1,0:T(8,128)(2,1)S(1)} custom-call(bf16[32,3584]{1,0:T(8,128)(2,1)} %tok_hbm.1, s32[8,32]{1,0:T(8,128)} %bitcast.2, f32[8,32]{1,0:T(8,128)} %bitcast.3), custom_call_target="tpu_custom_call" | custom-call | flops 10737418240 | tf_op jit(solution)/shard_map/pallas_call | solution.py:59
  1.2 3.1 %collective-permute-start = (bf16[32,3712]{1,0:T(8,128)(2,1)S(1)}, bf16[32,3712]{1,0:T(8,128)(2,1)S(1)}, u32[]{:S(2)}, u32[]{:S(2)}) collective-permute-start(bf16[32,3712]{1,0:T(8,128)(2,1)S(1)} %shard_map.64.refs_0_), channel_id=1, source_target_pairs={{0,4},{4,8},{8,12},{12,14},{14,10},{10,6},{6,2},{2,0},{5,1},{9,5},... | collective-permute-start | bytes 712712 | tf_op jit(solution)/shard_map/ppermute | solution.py:150
  4.2 4.0 %collective-permute-done.refs_1_ = bf16[32,3712]{1,0:T(8,128)(2,1)S(1)} collective-permute-done((bf16[32,3712]{1,0:T(8,128)(2,1)S(1)}, bf16[32,3712]{1,0:T(8,128)(2,1)S(1)}, u32[]{:S(2)}, u32[]{:S(2)}) %collective-permute-start) | collective-permute-done | bytes 237600 | tf_op jit(solution)/shard_map/ppermute | solution.py:150
  8.3 2.1 %collective-permute-start.5 = (bf16[32,3712]{1,0:T(8,128)(2,1)S(1)}, bf16[32,3712]{1,0:T(8,128)(2,1)S(1)}, u32[]{:S(2)}, u32[]{:S(2)}) collective-permute-start(bf16[32,3712]{1,0:T(8,128)(2,1)S(1)} %collective-permute-done.refs_1_), channel_id=1, source_target_pairs={{0,4},{4,8},{8,12},{12,14},{14,10},{10,6},{6,2},{2,0},{5,1},{9,5},... | collective-permute-start | bytes 712712 | tf_op jit(solution)/shard_map/ppermute | solution.py:150
  10.4 1.6 %collective-permute-start.3 = (bf16[32,3712]{1,0:T(8,128)(2,1)S(1)}, bf16[32,3712]{1,0:T(8,128)(2,1)S(1)}, u32[]{:S(2)}, u32[]{:S(2)}) collective-permute-start(bf16[32,3712]{1,0:T(8,128)(2,1)S(1)} %collective-permute-done.2.refs_3_), channel_id=1, source_target_pairs={{0,4},{4,8},{8,12},{12,14},{14,10},{10,6},{6,2},{2,0},{5,1},{9,5},... | collective-permute-start | bytes 712712 | tf_op jit(solution)/shard_map/ppermute | solution.py:150
  11.9 2.5 %collective-permute-done.5.refs_2_ = bf16[32,3712]{1,0:T(8,128)(2,1)S(1)} collective-permute-done((bf16[32,3712]{1,0:T(8,128)(2,1)S(1)}, bf16[32,3712]{1,0:T(8,128)(2,1)S(1)}, u32[]{:S(2)}, u32[]{:S(2)}) %collective-permute-start.5) | collective-permute-done | bytes 237600 | tf_op jit(solution)/shard_map/ppermute | solution.py:150
  14.4 2.1 %collective-permute-start.7 = (bf16[32,3712]{1,0:T(8,128)(2,1)S(1)}, bf16[32,3712]{1,0:T(8,128)(2,1)S(1)}, u32[]{:S(2)}, u32[]{:S(2)}) collective-permute-start(bf16[32,3712]{1,0:T(8,128)(2,1)S(1)} %collective-permute-done.5.refs_2_), channel_id=1, source_target_pairs={{0,4},{4,8},{8,12},{12,14},{14,10},{10,6},{6,2},{2,0},{5,1},{9,5},... | collective-permute-start | bytes 712712 | tf_op jit(solution)/shard_map/ppermute | solution.py:150
  16.5 0.5 collective-permute-done.3.refs_2_
  16.9 2.1 %collective-permute-start.6 = (bf16[32,3712]{1,0:T(8,128)(2,1)S(1)}, bf16[32,3712]{1,0:T(8,128)(2,1)S(1)}, u32[]{:S(2)}, u32[]{:S(2)}) collective-permute-start(bf16[32,3712]{1,0:T(8,128)(2,1)S(1)} %collective-permute-done.3.refs_2_), channel_id=1, source_target_pairs={{0,4},{4,8},{8,12},{12,14},{14,10},{10,6},{6,2},{2,0},{5,1},{9,5},... | collective-permute-start | bytes 712712 | tf_op jit(solution)/shard_map/ppermute | solution.py:150
  19.0 0.5 collective-permute-start.4
  19.5 1.0 %collective-permute-done.7.refs_6_ = bf16[32,3712]{1,0:T(8,128)(2,1)S(1)} collective-permute-done((bf16[32,3712]{1,0:T(8,128)(2,1)S(1)}, bf16[32,3712]{1,0:T(8,128)(2,1)S(1)}, u32[]{:S(2)}, u32[]{:S(2)}) %collective-permute-start.7) | collective-permute-done | bytes 237600 | tf_op jit(solution)/shard_map/ppermute | solution.py:150
  20.5 2.1 %collective-permute-start.8 = (bf16[32,3712]{1,0:T(8,128)(2,1)S(1)}, bf16[32,3712]{1,0:T(8,128)(2,1)S(1)}, u32[]{:S(2)}, u32[]{:S(2)}) collective-permute-start(bf16[32,3712]{1,0:T(8,128)(2,1)S(1)} %collective-permute-done.7.refs_6_), channel_id=1, source_target_pairs={{0,4},{4,8},{8,12},{12,14},{14,10},{10,6},{6,2},{2,0},{5,1},{9,5},... | collective-permute-start | bytes 712712 | tf_op jit(solution)/shard_map/ppermute | solution.py:150
  22.6 0.5 collective-permute-done.6.refs_3_
  23.0 2.1 %collective-permute-start.9 = (bf16[32,3712]{1,0:T(8,128)(2,1)S(1)}, bf16[32,3712]{1,0:T(8,128)(2,1)S(1)}, u32[]{:S(2)}, u32[]{:S(2)}) collective-permute-start(bf16[32,3712]{1,0:T(8,128)(2,1)S(1)} %collective-permute-done.6.refs_3_), channel_id=1, source_target_pairs={{0,4},{4,8},{8,12},{12,14},{14,10},{10,6},{6,2},{2,0},{5,1},{9,5},... | collective-permute-start | bytes 712712 | tf_op jit(solution)/shard_map/ppermute | solution.py:150
  25.1 3.3 %shard_map.65 = (f32[32,3584]{1,0:T(8,128)S(1)}, bf16[96,3584]{1,0:T(8,128)(2,1)S(1)}) custom-call(bf16[32,3712]{1,0:T(8,128)(2,1)S(1)} %shard_map.64.refs_0_, bf16[32,3712]{1,0:T(8,128)(2,1)S(1)} %collective-permute-done.refs_1_, bf16[32,3712]{1,0:T(8,128)(2,1)S(1)} %collective-permute-done.3.refs_2_, bf16[32,3712]{1,0:T(8,128)(2,1)S(1)} %collective-permute-done.2.refs_3_, ...), custom_call_target="tpu_custom_call" | custom-call | flops 5637144576 | tf_op jit(solution)/shard_map/pallas_call | solution.py:130
  28.4 0.7 %collective-permute-done.9.refs_7_ = bf16[32,3712]{1,0:T(8,128)(2,1)S(1)} collective-permute-done((bf16[32,3712]{1,0:T(8,128)(2,1)S(1)}, bf16[32,3712]{1,0:T(8,128)(2,1)S(1)}, u32[]{:S(2)}, u32[]{:S(2)}) %collective-permute-start.9) | collective-permute-done | bytes 237600 | tf_op jit(solution)/shard_map/ppermute | solution.py:150
  29.2 0.5 collective-permute-start.12
  29.7 0.5 collective-permute-start.15
  30.2 0.1 collective-permute-start.13
  30.3 0.4 collective-permute-done.11.refs_2_
  30.7 0.1 collective-permute-start.10
  30.8 3.3 %shard_map.66 = (f32[64,3584]{1,0:T(8,128)S(1)}, bf16[64,3584]{1,0:T(8,128)(2,1)S(1)}) custom-call(bf16[32,3712]{1,0:T(8,128)(2,1)S(1)} %collective-permute-done.1.refs_0_, bf16[32,3712]{1,0:T(8,128)(2,1)S(1)} %collective-permute-done.4.refs_1_, bf16[32,3712]{1,0:T(8,128)(2,1)S(1)} %collective-permute-done.5.refs_2_, ...), custom_call_target="tpu_custom_call" | custom-call | flops 5637144576 | tf_op jit(solution)/shard_map/pallas_call | solution.py:130
  34.1 0.4 collective-permute-start.16
  34.6 6.0 %shard_map.67 = (f32[160,3584]{1,0:T(8,128)S(1)}, bf16[64,3584]{1,0:T(8,128)(2,1)S(1)}, bf16[32,3584]{1,0:T(8,128)(2,1)S(1)}) custom-call(bf16[32,3712]{1,0:T(8,128)(2,1)S(1)} %collective-permute-done.8.refs_0_, bf16[32,3712]{1,0:T(8,128)(2,1)S(1)} %collective-permute-done.13.refs_1_, bf16[32,3712]{1,0:T(8,128)(2,1)S(1)} %collective-permute-done.11.refs_2_, ...), custom_call_target="tpu_custom_call" | custom-call | flops 5637144576 | tf_op jit(solution)/shard_map/pallas_call | solution.py:130
  40.6 0.2 collective-permute-start.17
  40.8 0.4 collective-permute-start.19
  41.2 1.3 %collective-permute-done.17 = bf16[64,3584]{1,0:T(8,128)(2,1)S(1)} collective-permute-done((bf16[64,3584]{1,0:T(8,128)(2,1)S(1)}, bf16[64,3584]{1,0:T(8,128)(2,1)S(1)}, u32[]{:S(2)}, u32[]{:S(2)}) %collective-permute-start.17) | collective-permute-done | bytes 458784 | tf_op jit(solution)/shard_map/ppermute | solution.py:151
  42.5 2.1 %collective-permute-start.20 = (bf16[32,3584]{1,0:T(8,128)(2,1)S(1)}, bf16[32,3584]{1,0:T(8,128)(2,1)S(1)}, u32[]{:S(2)}, u32[]{:S(2)}) collective-permute-start(bf16[32,3584]{1,0:T(8,128)(2,1)S(1)} %add_convert_fusion.7), channel_id=1, source_target_pairs={{0,4},{4,8},{8,12},{12,14},{14,10},{10,6},{6,2},{2,0},{5,1},{9,5},... | collective-permute-start | bytes 688136 | tf_op jit(solution)/shard_map/ppermute | solution.py:150
  44.7 1.6 %collective-permute-start.18 = (bf16[32,3584]{1,0:T(8,128)(2,1)S(1)}, bf16[32,3584]{1,0:T(8,128)(2,1)S(1)}, u32[]{:S(2)}, u32[]{:S(2)}) collective-permute-start(bf16[32,3584]{1,0:T(8,128)(2,1)S(1)} %add_convert_fusion.6), channel_id=1, source_target_pairs={{0,4},{4,8},{8,12},{12,14},{14,10},{10,6},{6,2},{2,0},{5,1},{9,5},... | collective-permute-start | bytes 688136 | tf_op jit(solution)/shard_map/ppermute | solution.py:150
  46.4 2.3 %collective-permute-done.20 = bf16[32,3584]{1,0:T(8,128)(2,1)S(1)} collective-permute-done((bf16[32,3584]{1,0:T(8,128)(2,1)S(1)}, bf16[32,3584]{1,0:T(8,128)(2,1)S(1)}, u32[]{:S(2)}, u32[]{:S(2)}) %collective-permute-start.20) | collective-permute-done | bytes 229408 | tf_op jit(solution)/shard_map/ppermute | solution.py:150
  48.6 0.1 add_convert_fusion.5
  48.7 2.1 %collective-permute-start.22 = (bf16[32,3584]{1,0:T(8,128)(2,1)S(1)}, bf16[32,3584]{1,0:T(8,128)(2,1)S(1)}, u32[]{:S(2)}, u32[]{:S(2)}) collective-permute-start(bf16[32,3584]{1,0:T(8,128)(2,1)S(1)} %add_convert_fusion.5), channel_id=1, source_target_pairs={{0,4},{4,8},{8,12},{12,14},{14,10},{10,6},{6,2},{2,0},{5,1},{9,5},... | collective-permute-start | bytes 688136 | tf_op jit(solution)/shard_map/ppermute | solution.py:150
  50.8 0.3 collective-permute-done.18
  51.1 0.1 add_convert_fusion.4
  51.2 2.1 %collective-permute-start.21 = (bf16[32,3584]{1,0:T(8,128)(2,1)S(1)}, bf16[32,3584]{1,0:T(8,128)(2,1)S(1)}, u32[]{:S(2)}, u32[]{:S(2)}) collective-permute-start(bf16[32,3584]{1,0:T(8,128)(2,1)S(1)} %add_convert_fusion.4), channel_id=1, source_target_pairs={{0,4},{4,8},{8,12},{12,14},{14,10},{10,6},{6,2},{2,0},{5,1},{9,5},... | collective-permute-start | bytes 688136 | tf_op jit(solution)/shard_map/ppermute | solution.py:150
  53.3 1.5 %collective-permute-done.22 = bf16[32,3584]{1,0:T(8,128)(2,1)S(1)} collective-permute-done((bf16[32,3584]{1,0:T(8,128)(2,1)S(1)}, bf16[32,3584]{1,0:T(8,128)(2,1)S(1)}, u32[]{:S(2)}, u32[]{:S(2)}) %collective-permute-start.22) | collective-permute-done | bytes 229408 | tf_op jit(solution)/shard_map/ppermute | solution.py:150
  54.8 0.1 add_convert_fusion.3
  54.9 2.1 %collective-permute-start.25 = (bf16[32,3584]{1,0:T(8,128)(2,1)S(1)}, bf16[32,3584]{1,0:T(8,128)(2,1)S(1)}, u32[]{:S(2)}, u32[]{:S(2)}) collective-permute-start(bf16[32,3584]{1,0:T(8,128)(2,1)S(1)} %add_convert_fusion.3), channel_id=1, source_target_pairs={{0,4},{4,8},{8,12},{12,14},{14,10},{10,6},{6,2},{2,0},{5,1},{9,5},... | collective-permute-start | bytes 688136 | tf_op jit(solution)/shard_map/ppermute | solution.py:150
  57.0 0.3 collective-permute-done.21
  57.3 0.1 add_convert_fusion.2
  57.3 2.1 %collective-permute-start.23 = (bf16[32,3584]{1,0:T(8,128)(2,1)S(1)}, bf16[32,3584]{1,0:T(8,128)(2,1)S(1)}, u32[]{:S(2)}, u32[]{:S(2)}) collective-permute-start(bf16[32,3584]{1,0:T(8,128)(2,1)S(1)} %add_convert_fusion.2), channel_id=1, source_target_pairs={{0,4},{4,8},{8,12},{12,14},{14,10},{10,6},{6,2},{2,0},{5,1},{9,5},... | collective-permute-start | bytes 688136 | tf_op jit(solution)/shard_map/ppermute | solution.py:150
  59.5 1.5 %collective-permute-done.25 = bf16[32,3584]{1,0:T(8,128)(2,1)S(1)} collective-permute-done((bf16[32,3584]{1,0:T(8,128)(2,1)S(1)}, bf16[32,3584]{1,0:T(8,128)(2,1)S(1)}, u32[]{:S(2)}, u32[]{:S(2)}) %collective-permute-start.25) | collective-permute-done | bytes 229408 | tf_op jit(solution)/shard_map/ppermute | solution.py:150
  61.0 0.1 add_convert_fusion.1
  61.0 2.1 %collective-permute-start.26 = (bf16[32,3584]{1,0:T(8,128)(2,1)S(1)}, bf16[32,3584]{1,0:T(8,128)(2,1)S(1)}, u32[]{:S(2)}, u32[]{:S(2)}) collective-permute-start(bf16[32,3584]{1,0:T(8,128)(2,1)S(1)} %add_convert_fusion.1), channel_id=1, source_target_pairs={{0,4},{4,8},{8,12},{12,14},{14,10},{10,6},{6,2},{2,0},{5,1},{9,5},... | collective-permute-start | bytes 688136 | tf_op jit(solution)/shard_map/ppermute | solution.py:150
  63.2 0.2 collective-permute-done.23
  63.4 3.7 %collective-permute-done.26 = bf16[32,3584]{1,0:T(8,128)(2,1)S(1)} collective-permute-done((bf16[32,3584]{1,0:T(8,128)(2,1)S(1)}, bf16[32,3584]{1,0:T(8,128)(2,1)S(1)}, u32[]{:S(2)}, u32[]{:S(2)}) %collective-permute-start.26) | collective-permute-done | bytes 229408 | tf_op jit(solution)/shard_map/ppermute | solution.py:150
  67.1 0.1 convert_add_fusion
  67.2 0.7 %add_convert_fusion = bf16[32,3584]{1,0:T(8,128)(2,1)} fusion(f32[32,3584]{1,0:T(8,128)S(1)} %convert_add_fusion, bf16[32,3584]{1,0:T(8,128)(2,1)S(1)} %collective-permute-done.24), kind=kLoop, calls=%fused_computation | loop fusion | flops 344064 | bytes 917504 | tf_op jit(solution)/shard_map/convert_element_type | solution.py:226
  (25 shorter events, 0.1 us)
Async XLA Ops:
  0.0 25.1 %copy-start = (bf16[1,3584,1024]{2,1,0:T(8,128)(2,1)S(1)}, bf16[1,3584,1024]{2,1,0:T(8,128)(2,1)}, u32[]{:S(2)}) copy-start(bf16[1,3584,1024]{2,1,0:T(8,128)(2,1)} %refs_8_.1) | copy-start | bytes 22020100
  0.0 25.1 %copy-start.1 = (bf16[1,3584,1024]{2,1,0:T(8,128)(2,1)S(1)}, bf16[1,3584,1024]{2,1,0:T(8,128)(2,1)}, u32[]{:S(2)}) copy-start(bf16[1,3584,1024]{2,1,0:T(8,128)(2,1)} %refs_9_.1) | copy-start | bytes 22020100
  0.0 25.1 %copy-start.2 = (bf16[1,1024,3584]{2,1,0:T(8,128)(2,1)S(1)}, bf16[1,1024,3584]{2,1,0:T(8,128)(2,1)}, u32[]{:S(2)}) copy-start(bf16[1,1024,3584]{2,1,0:T(8,128)(2,1)} %refs_10_.1) | copy-start | bytes 22020100
  1.2 7.1 %collective-permute-start = (bf16[32,3712]{1,0:T(8,128)(2,1)S(1)}, bf16[32,3712]{1,0:T(8,128)(2,1)S(1)}, u32[]{:S(2)}, u32[]{:S(2)}) collective-permute-start(bf16[32,3712]{1,0:T(8,128)(2,1)S(1)} %shard_map.64.refs_0_), channel_id=1, source_target_pairs={{0,4},{4,8},{8,12},{12,14},{14,10},{10,6},{6,2},{2,0},{5,1},{9,5},... | collective-permute-start | bytes 712712 | tf_op jit(solution)/shard_map/ppermute | solution.py:150
  4.2 6.1 %collective-permute-start.2 = (bf16[32,3712]{1,0:T(8,128)(2,1)S(1)}, bf16[32,3712]{1,0:T(8,128)(2,1)S(1)}, u32[]{:S(2)}, u32[]{:S(2)}) collective-permute-start(bf16[32,3712]{1,0:T(8,128)(2,1)S(1)} %shard_map.64.refs_0_), channel_id=1, source_target_pairs={{0,1},{1,0},{2,3},{3,2},{4,5},{5,4},{6,7},{7,6},{8,9},{9,8},{10,11... | collective-permute-start | bytes 712712 | tf_op jit(solution)/shard_map/ppermute | solution.py:151
  8.3 6.1 %collective-permute-start.5 = (bf16[32,3712]{1,0:T(8,128)(2,1)S(1)}, bf16[32,3712]{1,0:T(8,128)(2,1)S(1)}, u32[]{:S(2)}, u32[]{:S(2)}) collective-permute-start(bf16[32,3712]{1,0:T(8,128)(2,1)S(1)} %collective-permute-done.refs_1_), channel_id=1, source_target_pairs={{0,4},{4,8},{8,12},{12,14},{14,10},{10,6},{6,2},{2,0},{5,1},{9,5},... | collective-permute-start | bytes 712712 | tf_op jit(solution)/shard_map/ppermute | solution.py:150
  10.4 6.6 %collective-permute-start.3 = (bf16[32,3712]{1,0:T(8,128)(2,1)S(1)}, bf16[32,3712]{1,0:T(8,128)(2,1)S(1)}, u32[]{:S(2)}, u32[]{:S(2)}) collective-permute-start(bf16[32,3712]{1,0:T(8,128)(2,1)S(1)} %collective-permute-done.2.refs_3_), channel_id=1, source_target_pairs={{0,4},{4,8},{8,12},{12,14},{14,10},{10,6},{6,2},{2,0},{5,1},{9,5},... | collective-permute-start | bytes 712712 | tf_op jit(solution)/shard_map/ppermute | solution.py:150
  14.4 6.1 %collective-permute-start.7 = (bf16[32,3712]{1,0:T(8,128)(2,1)S(1)}, bf16[32,3712]{1,0:T(8,128)(2,1)S(1)}, u32[]{:S(2)}, u32[]{:S(2)}) collective-permute-start(bf16[32,3712]{1,0:T(8,128)(2,1)S(1)} %collective-permute-done.5.refs_2_), channel_id=1, source_target_pairs={{0,4},{4,8},{8,12},{12,14},{14,10},{10,6},{6,2},{2,0},{5,1},{9,5},... | collective-permute-start | bytes 712712 | tf_op jit(solution)/shard_map/ppermute | solution.py:150
  16.9 6.1 %collective-permute-start.6 = (bf16[32,3712]{1,0:T(8,128)(2,1)S(1)}, bf16[32,3712]{1,0:T(8,128)(2,1)S(1)}, u32[]{:S(2)}, u32[]{:S(2)}) collective-permute-start(bf16[32,3712]{1,0:T(8,128)(2,1)S(1)} %collective-permute-done.3.refs_2_), channel_id=1, source_target_pairs={{0,4},{4,8},{8,12},{12,14},{14,10},{10,6},{6,2},{2,0},{5,1},{9,5},... | collective-permute-start | bytes 712712 | tf_op jit(solution)/shard_map/ppermute | solution.py:150
  19.0 10.7 %collective-permute-start.1 = (bf16[32,3712]{1,0:T(8,128)(2,1)S(1)}, bf16[32,3712]{1,0:T(8,128)(2,1)S(1)}, u32[]{:S(2)}, u32[]{:S(2)}) collective-permute-start(bf16[32,3712]{1,0:T(8,128)(2,1)S(1)} %collective-permute-done.refs_1_), channel_id=1, source_target_pairs={{0,1},{1,0},{2,3},{3,2},{4,5},{5,4},{6,7},{7,6},{8,9},{9,8},{10,11... | collective-permute-start | bytes 712712 | tf_op jit(solution)/shard_map/ppermute | solution.py:151
  19.0 11.2 %collective-permute-start.4 = (bf16[32,3712]{1,0:T(8,128)(2,1)S(1)}, bf16[32,3712]{1,0:T(8,128)(2,1)S(1)}, u32[]{:S(2)}, u32[]{:S(2)}) collective-permute-start(bf16[32,3712]{1,0:T(8,128)(2,1)S(1)} %collective-permute-done.3.refs_2_), channel_id=1, source_target_pairs={{0,1},{1,0},{2,3},{3,2},{4,5},{5,4},{6,7},{7,6},{8,9},{9,8},{10,11... | collective-permute-start | bytes 712712 | tf_op jit(solution)/shard_map/ppermute | solution.py:151
  20.5 8.7 %collective-permute-start.8 = (bf16[32,3712]{1,0:T(8,128)(2,1)S(1)}, bf16[32,3712]{1,0:T(8,128)(2,1)S(1)}, u32[]{:S(2)}, u32[]{:S(2)}) collective-permute-start(bf16[32,3712]{1,0:T(8,128)(2,1)S(1)} %collective-permute-done.7.refs_6_), channel_id=1, source_target_pairs={{0,4},{4,8},{8,12},{12,14},{14,10},{10,6},{6,2},{2,0},{5,1},{9,5},... | collective-permute-start | bytes 712712 | tf_op jit(solution)/shard_map/ppermute | solution.py:150
  23.0 6.1 %collective-permute-start.9 = (bf16[32,3712]{1,0:T(8,128)(2,1)S(1)}, bf16[32,3712]{1,0:T(8,128)(2,1)S(1)}, u32[]{:S(2)}, u32[]{:S(2)}) collective-permute-start(bf16[32,3712]{1,0:T(8,128)(2,1)S(1)} %collective-permute-done.6.refs_3_), channel_id=1, source_target_pairs={{0,4},{4,8},{8,12},{12,14},{14,10},{10,6},{6,2},{2,0},{5,1},{9,5},... | collective-permute-start | bytes 712712 | tf_op jit(solution)/shard_map/ppermute | solution.py:150
  29.1 1.5 %collective-permute-start.11 = (bf16[32,3712]{1,0:T(8,128)(2,1)S(1)}, bf16[32,3712]{1,0:T(8,128)(2,1)S(1)}, u32[]{:S(2)}, u32[]{:S(2)}) collective-permute-start(bf16[32,3712]{1,0:T(8,128)(2,1)S(1)} %collective-permute-done.9.refs_7_), channel_id=1, source_target_pairs={{0,1},{1,0},{2,3},{3,2},{4,5},{5,4},{6,7},{7,6},{8,9},{9,8},{10,11... | collective-permute-start | bytes 712712 | tf_op jit(solution)/shard_map/ppermute | solution.py:151
  29.2 5.0 %collective-permute-start.12 = (bf16[96,3584]{1,0:T(8,128)(2,1)S(1)}, bf16[96,3584]{1,0:T(8,128)(2,1)S(1)}, u32[]{:S(2)}, u32[]{:S(2)}) collective-permute-start(bf16[96,3584]{1,0:T(8,128)(2,1)S(1)} %get-tuple-element.63), channel_id=1, source_target_pairs={{0,1},{1,0},{2,3},{3,2},{4,5},{5,4},{6,7},{7,6},{8,9},{9,8},{10,11... | collective-permute-start | bytes 2064392 | tf_op jit(solution)/shard_map/ppermute | solution.py:151
  29.7 4.9 %collective-permute-start.14 = (bf16[32,3712]{1,0:T(8,128)(2,1)S(1)}, bf16[32,3712]{1,0:T(8,128)(2,1)S(1)}, u32[]{:S(2)}, u32[]{:S(2)}) collective-permute-start(bf16[32,3712]{1,0:T(8,128)(2,1)S(1)} %collective-permute-done.5.refs_2_), channel_id=1, source_target_pairs={{0,1},{1,0},{2,3},{3,2},{4,5},{5,4},{6,7},{7,6},{8,9},{9,8},{10,11... | collective-permute-start | bytes 712712 | tf_op jit(solution)/shard_map/ppermute | solution.py:151
  29.7 4.9 %collective-permute-start.15 = (bf16[32,3712]{1,0:T(8,128)(2,1)S(1)}, bf16[32,3712]{1,0:T(8,128)(2,1)S(1)}, u32[]{:S(2)}, u32[]{:S(2)}) collective-permute-start(bf16[32,3712]{1,0:T(8,128)(2,1)S(1)} %collective-permute-done.6.refs_3_), channel_id=1, source_target_pairs={{0,1},{1,0},{2,3},{3,2},{4,5},{5,4},{6,7},{7,6},{8,9},{9,8},{10,11... | collective-permute-start | bytes 712712 | tf_op jit(solution)/shard_map/ppermute | solution.py:151
  30.2 4.4 %collective-permute-start.13 = (bf16[32,3712]{1,0:T(8,128)(2,1)S(1)}, bf16[32,3712]{1,0:T(8,128)(2,1)S(1)}, u32[]{:S(2)}, u32[]{:S(2)}) collective-permute-start(bf16[32,3712]{1,0:T(8,128)(2,1)S(1)} %collective-permute-done.7.refs_6_), channel_id=1, source_target_pairs={{0,1},{1,0},{2,3},{3,2},{4,5},{5,4},{6,7},{7,6},{8,9},{9,8},{10,11... | collective-permute-start | bytes 712712 | tf_op jit(solution)/shard_map/ppermute | solution.py:151
  30.7 3.4 %collective-permute-start.10 = (bf16[32,3712]{1,0:T(8,128)(2,1)S(1)}, bf16[32,3712]{1,0:T(8,128)(2,1)S(1)}, u32[]{:S(2)}, u32[]{:S(2)}) collective-permute-start(bf16[32,3712]{1,0:T(8,128)(2,1)S(1)} %collective-permute-done.8.refs_0_), channel_id=1, source_target_pairs={{0,1},{1,0},{2,3},{3,2},{4,5},{5,4},{6,7},{7,6},{8,9},{9,8},{10,11... | collective-permute-start | bytes 712712 | tf_op jit(solution)/shard_map/ppermute | solution.py:151
  34.1 6.5 %collective-permute-start.16 = (bf16[64,3584]{1,0:T(8,128)(2,1)S(1)}, bf16[64,3584]{1,0:T(8,128)(2,1)S(1)}, u32[]{:S(2)}, u32[]{:S(2)}) collective-permute-start(bf16[64,3584]{1,0:T(8,128)(2,1)S(1)} %get-tuple-element.71), channel_id=1, source_target_pairs={{0,1},{1,0},{2,3},{3,2},{4,5},{5,4},{6,7},{7,6},{8,9},{9,8},{10,11... | collective-permute-start | bytes 1376264 | tf_op jit(solution)/shard_map/ppermute | solution.py:151
  40.6 1.9 %collective-permute-start.17 = (bf16[64,3584]{1,0:T(8,128)(2,1)S(1)}, bf16[64,3584]{1,0:T(8,128)(2,1)S(1)}, u32[]{:S(2)}, u32[]{:S(2)}) collective-permute-start(bf16[64,3584]{1,0:T(8,128)(2,1)S(1)} %get-tuple-element.74), channel_id=1, source_target_pairs={{0,1},{1,0},{2,3},{3,2},{4,5},{5,4},{6,7},{7,6},{8,9},{9,8},{10,11... | collective-permute-start | bytes 1376264 | tf_op jit(solution)/shard_map/ppermute | solution.py:151
  40.8 5.5 %collective-permute-start.19 = (bf16[32,3584]{1,0:T(8,128)(2,1)S(1)}, bf16[32,3584]{1,0:T(8,128)(2,1)S(1)}, u32[]{:S(2)}, u32[]{:S(2)}) collective-permute-start(bf16[32,3584]{1,0:T(8,128)(2,1)S(1)} %get-tuple-element.77), channel_id=1, source_target_pairs={{0,1},{1,0},{2,3},{3,2},{4,5},{5,4},{6,7},{7,6},{8,9},{9,8},{10,11... | collective-permute-start | bytes 688136 | tf_op jit(solution)/shard_map/ppermute | solution.py:151
  42.5 6.1 %collective-permute-start.20 = (bf16[32,3584]{1,0:T(8,128)(2,1)S(1)}, bf16[32,3584]{1,0:T(8,128)(2,1)S(1)}, u32[]{:S(2)}, u32[]{:S(2)}) collective-permute-start(bf16[32,3584]{1,0:T(8,128)(2,1)S(1)} %add_convert_fusion.7), channel_id=1, source_target_pairs={{0,4},{4,8},{8,12},{12,14},{14,10},{10,6},{6,2},{2,0},{5,1},{9,5},... | collective-permute-start | bytes 688136 | tf_op jit(solution)/shard_map/ppermute | solution.py:150
  44.7 6.4 %collective-permute-start.18 = (bf16[32,3584]{1,0:T(8,128)(2,1)S(1)}, bf16[32,3584]{1,0:T(8,128)(2,1)S(1)}, u32[]{:S(2)}, u32[]{:S(2)}) collective-permute-start(bf16[32,3584]{1,0:T(8,128)(2,1)S(1)} %add_convert_fusion.6), channel_id=1, source_target_pairs={{0,4},{4,8},{8,12},{12,14},{14,10},{10,6},{6,2},{2,0},{5,1},{9,5},... | collective-permute-start | bytes 688136 | tf_op jit(solution)/shard_map/ppermute | solution.py:150
  48.7 6.1 %collective-permute-start.22 = (bf16[32,3584]{1,0:T(8,128)(2,1)S(1)}, bf16[32,3584]{1,0:T(8,128)(2,1)S(1)}, u32[]{:S(2)}, u32[]{:S(2)}) collective-permute-start(bf16[32,3584]{1,0:T(8,128)(2,1)S(1)} %add_convert_fusion.5), channel_id=1, source_target_pairs={{0,4},{4,8},{8,12},{12,14},{14,10},{10,6},{6,2},{2,0},{5,1},{9,5},... | collective-permute-start | bytes 688136 | tf_op jit(solution)/shard_map/ppermute | solution.py:150
  51.2 6.1 %collective-permute-start.21 = (bf16[32,3584]{1,0:T(8,128)(2,1)S(1)}, bf16[32,3584]{1,0:T(8,128)(2,1)S(1)}, u32[]{:S(2)}, u32[]{:S(2)}) collective-permute-start(bf16[32,3584]{1,0:T(8,128)(2,1)S(1)} %add_convert_fusion.4), channel_id=1, source_target_pairs={{0,4},{4,8},{8,12},{12,14},{14,10},{10,6},{6,2},{2,0},{5,1},{9,5},... | collective-permute-start | bytes 688136 | tf_op jit(solution)/shard_map/ppermute | solution.py:150
  54.9 6.1 %collective-permute-start.25 = (bf16[32,3584]{1,0:T(8,128)(2,1)S(1)}, bf16[32,3584]{1,0:T(8,128)(2,1)S(1)}, u32[]{:S(2)}, u32[]{:S(2)}) collective-permute-start(bf16[32,3584]{1,0:T(8,128)(2,1)S(1)} %add_convert_fusion.3), channel_id=1, source_target_pairs={{0,4},{4,8},{8,12},{12,14},{14,10},{10,6},{6,2},{2,0},{5,1},{9,5},... | collective-permute-start | bytes 688136 | tf_op jit(solution)/shard_map/ppermute | solution.py:150
  57.3 6.1 %collective-permute-start.23 = (bf16[32,3584]{1,0:T(8,128)(2,1)S(1)}, bf16[32,3584]{1,0:T(8,128)(2,1)S(1)}, u32[]{:S(2)}, u32[]{:S(2)}) collective-permute-start(bf16[32,3584]{1,0:T(8,128)(2,1)S(1)} %add_convert_fusion.2), channel_id=1, source_target_pairs={{0,4},{4,8},{8,12},{12,14},{14,10},{10,6},{6,2},{2,0},{5,1},{9,5},... | collective-permute-start | bytes 688136 | tf_op jit(solution)/shard_map/ppermute | solution.py:150
  61.0 6.1 %collective-permute-start.26 = (bf16[32,3584]{1,0:T(8,128)(2,1)S(1)}, bf16[32,3584]{1,0:T(8,128)(2,1)S(1)}, u32[]{:S(2)}, u32[]{:S(2)}) collective-permute-start(bf16[32,3584]{1,0:T(8,128)(2,1)S(1)} %add_convert_fusion.1), channel_id=1, source_target_pairs={{0,4},{4,8},{8,12},{12,14},{14,10},{10,6},{6,2},{2,0},{5,1},{9,5},... | collective-permute-start | bytes 688136 | tf_op jit(solution)/shard_map/ppermute | solution.py:150
  63.4 3.8 %collective-permute-start.24 = (bf16[32,3584]{1,0:T(8,128)(2,1)S(1)}, bf16[32,3584]{1,0:T(8,128)(2,1)S(1)}, u32[]{:S(2)}, u32[]{:S(2)}) collective-permute-start(bf16[32,3584]{1,0:T(8,128)(2,1)S(1)} %collective-permute-done.23), channel_id=1, source_target_pairs={{0,1},{1,0},{2,3},{3,2},{4,5},{5,4},{6,7},{7,6},{8,9},{9,8},{10,11... | collective-permute-start | bytes 688136 | tf_op jit(solution)/shard_map/ppermute | solution.py:151

commit v14 on v13

--- a/solution.py
+++ b/solution.py
@@ -181,7 +181,6 @@
         theirs.update(zip(give, [(piece, at) for piece in pieces for at in range(piece.shape[0] // rows)]))
 
     keep, give = [end], [end - 2, end - 1, end]
-    kept[end], given[end - 2 :], _ = together((kept[end], given[end - 2 :], up[far - 1]))
     out, pieces = compute(keep, give, (3,))
     out, pieces, kept[0], given[2] = together((out, pieces, kept[0], given[2]))
     given[0] = sibling(kept[0])

time: 68.1 us -> 65.6 us (0.963)
  waiting for transfers between devices: 20.6 us -> 18.1 us
    ppermute x14, waiting for transfers between devices: 18.8 us -> 16.3 us  [local(): send = lambda a: lax.ppermute(a, 'node', spin)]
  transfers between devices with their start and end apart: 27 -> 27, of which waited for: 15 -> 14; matrix products, arithmetic and copies ran while one was open for 1% -> 1% of each run, Pallas kernels for 19% -> 19%
where the time goes in v14:
time: 65.6 us; the launch traced here: 65.4 us
  starting transfers between devices  32.2 us (49%)
  waiting for transfers between devices  18.1 us (28%)
  Pallas kernels  13.8 us (21%)
  other arithmetic  1.24 us (2%)
    ppermute x14, starting transfers between devices, local(): send = lambda a: lax.ppermute(a, 'node', spin)  29 us
    ppermute x14, waiting for transfers between devices, local(): send = lambda a: lax.ppermute(a, 'node', spin)  16.3 us
    pallas_call x3, Pallas kernels, expert(): pl.pallas_call(functools.partial(expert_kernel, count, experts, *tiles(wi...  12.6 us
    ppermute x13, starting transfers between devices, local(): sibling = lambda a: lax.ppermute(a, 'node', swap)  3.28 us
    ppermute x13, waiting for transfers between devices, local(): sibling = lambda a: lax.ppermute(a, 'node', swap)  1.74 us
  transfers between devices with their start and end apart: 27, of which 14 were waited for; matrix products, arithmetic and copies ran while one was open for 1% of the time, Pallas kernels for 19%

profile of v14, /device:TPU:0, one launch (start us, length us, event | category | flops | bytes accessed | tf_op | source)
XLA Modules:
  0.0 65.4 jit_solution(14715814579920758654)
XLA Ops:
  0.0 1.1 %shard_map.64.refs_0_ = bf16[32,3712]{1,0:T(8,128)(2,1)S(1)} custom-call(bf16[32,3584]{1,0:T(8,128)(2,1)} %tok_hbm.1, s32[8,32]{1,0:T(8,128)} %bitcast.2, f32[8,32]{1,0:T(8,128)} %bitcast.3), custom_call_target="tpu_custom_call" | custom-call | flops 10737418240 | tf_op jit(solution)/shard_map/pallas_call | solution.py:59
  1.2 0.5 collective-permute-start.2
  1.7 2.6 %collective-permute-start = (bf16[32,3712]{1,0:T(8,128)(2,1)S(1)}, bf16[32,3712]{1,0:T(8,128)(2,1)S(1)}, u32[]{:S(2)}, u32[]{:S(2)}) collective-permute-start(bf16[32,3712]{1,0:T(8,128)(2,1)S(1)} %shard_map.64.refs_0_), channel_id=1, source_target_pairs={{0,4},{4,8},{8,12},{12,14},{14,10},{10,6},{6,2},{2,0},{5,1},{9,5},... | collective-permute-start | bytes 712712 | tf_op jit(solution)/shard_map/ppermute | solution.py:150
  4.3 1.6 %collective-permute-start.3 = (bf16[32,3712]{1,0:T(8,128)(2,1)S(1)}, bf16[32,3712]{1,0:T(8,128)(2,1)S(1)}, u32[]{:S(2)}, u32[]{:S(2)}) collective-permute-start(bf16[32,3712]{1,0:T(8,128)(2,1)S(1)} %collective-permute-done.2.refs_3_), channel_id=1, source_target_pairs={{0,4},{4,8},{8,12},{12,14},{14,10},{10,6},{6,2},{2,0},{5,1},{9,5},... | collective-permute-start | bytes 712712 | tf_op jit(solution)/shard_map/ppermute | solution.py:150
  5.9 2.5 %collective-permute-done.refs_1_ = bf16[32,3712]{1,0:T(8,128)(2,1)S(1)} collective-permute-done((bf16[32,3712]{1,0:T(8,128)(2,1)S(1)}, bf16[32,3712]{1,0:T(8,128)(2,1)S(1)}, u32[]{:S(2)}, u32[]{:S(2)}) %collective-permute-start) | collective-permute-done | bytes 237600 | tf_op jit(solution)/shard_map/ppermute | solution.py:150
  8.4 2.1 %collective-permute-start.5 = (bf16[32,3712]{1,0:T(8,128)(2,1)S(1)}, bf16[32,3712]{1,0:T(8,128)(2,1)S(1)}, u32[]{:S(2)}, u32[]{:S(2)}) collective-permute-start(bf16[32,3712]{1,0:T(8,128)(2,1)S(1)} %collective-permute-done.refs_1_), channel_id=1, source_target_pairs={{0,4},{4,8},{8,12},{12,14},{14,10},{10,6},{6,2},{2,0},{5,1},{9,5},... | collective-permute-start | bytes 712712 | tf_op jit(solution)/shard_map/ppermute | solution.py:150
  10.4 0.5 collective-permute-done.3.refs_2_
  10.9 2.1 %collective-permute-start.6 = (bf16[32,3712]{1,0:T(8,128)(2,1)S(1)}, bf16[32,3712]{1,0:T(8,128)(2,1)S(1)}, u32[]{:S(2)}, u32[]{:S(2)}) collective-permute-start(bf16[32,3712]{1,0:T(8,128)(2,1)S(1)} %collective-permute-done.3.refs_2_), channel_id=1, source_target_pairs={{0,4},{4,8},{8,12},{12,14},{14,10},{10,6},{6,2},{2,0},{5,1},{9,5},... | collective-permute-start | bytes 712712 | tf_op jit(solution)/shard_map/ppermute | solution.py:150
  13.0 1.5 %collective-permute-done.5.refs_2_ = bf16[32,3712]{1,0:T(8,128)(2,1)S(1)} collective-permute-done((bf16[32,3712]{1,0:T(8,128)(2,1)S(1)}, bf16[32,3712]{1,0:T(8,128)(2,1)S(1)}, u32[]{:S(2)}, u32[]{:S(2)}) %collective-permute-start.5) | collective-permute-done | bytes 237600 | tf_op jit(solution)/shard_map/ppermute | solution.py:150
  14.5 2.1 %collective-permute-start.7 = (bf16[32,3712]{1,0:T(8,128)(2,1)S(1)}, bf16[32,3712]{1,0:T(8,128)(2,1)S(1)}, u32[]{:S(2)}, u32[]{:S(2)}) collective-permute-start(bf16[32,3712]{1,0:T(8,128)(2,1)S(1)} %collective-permute-done.5.refs_2_), channel_id=1, source_target_pairs={{0,4},{4,8},{8,12},{12,14},{14,10},{10,6},{6,2},{2,0},{5,1},{9,5},... | collective-permute-start | bytes 712712 | tf_op jit(solution)/shard_map/ppermute | solution.py:150
  16.5 0.5 collective-permute-start.4
  17.1 2.0 %collective-permute-start.9 = (bf16[32,3712]{1,0:T(8,128)(2,1)S(1)}, bf16[32,3712]{1,0:T(8,128)(2,1)S(1)}, u32[]{:S(2)}, u32[]{:S(2)}) collective-permute-start(bf16[32,3712]{1,0:T(8,128)(2,1)S(1)} %collective-permute-done.6.refs_3_), channel_id=1, source_target_pairs={{0,4},{4,8},{8,12},{12,14},{14,10},{10,6},{6,2},{2,0},{5,1},{9,5},... | collective-permute-start | bytes 712712 | tf_op jit(solution)/shard_map/ppermute | solution.py:150
  19.1 1.5 %collective-permute-done.7.refs_6_ = bf16[32,3712]{1,0:T(8,128)(2,1)S(1)} collective-permute-done((bf16[32,3712]{1,0:T(8,128)(2,1)S(1)}, bf16[32,3712]{1,0:T(8,128)(2,1)S(1)}, u32[]{:S(2)}, u32[]{:S(2)}) %collective-permute-start.7) | collective-permute-done | bytes 237600 | tf_op jit(solution)/shard_map/ppermute | solution.py:150
  20.6 2.1 %collective-permute-start.8 = (bf16[32,3712]{1,0:T(8,128)(2,1)S(1)}, bf16[32,3712]{1,0:T(8,128)(2,1)S(1)}, u32[]{:S(2)}, u32[]{:S(2)}) collective-permute-start(bf16[32,3712]{1,0:T(8,128)(2,1)S(1)} %collective-permute-done.7.refs_6_), channel_id=1, source_target_pairs={{0,4},{4,8},{8,12},{12,14},{14,10},{10,6},{6,2},{2,0},{5,1},{9,5},... | collective-permute-start | bytes 712712 | tf_op jit(solution)/shard_map/ppermute | solution.py:150
  22.7 3.3 %shard_map.65 = (f32[32,3584]{1,0:T(8,128)S(1)}, bf16[96,3584]{1,0:T(8,128)(2,1)S(1)}) custom-call(bf16[32,3712]{1,0:T(8,128)(2,1)S(1)} %shard_map.64.refs_0_, bf16[32,3712]{1,0:T(8,128)(2,1)S(1)} %collective-permute-done.refs_1_, bf16[32,3712]{1,0:T(8,128)(2,1)S(1)} %collective-permute-done.3.refs_2_, bf16[32,3712]{1,0:T(8,128)(2,1)S(1)} %collective-permute-done.2.refs_3_, ...), custom_call_target="tpu_custom_call" | custom-call | flops 5637144576 | tf_op jit(solution)/shard_map/pallas_call | solution.py:130
  25.9 0.7 %collective-permute-done.8.refs_0_ = bf16[32,3712]{1,0:T(8,128)(2,1)S(1)} collective-permute-done((bf16[32,3712]{1,0:T(8,128)(2,1)S(1)}, bf16[32,3712]{1,0:T(8,128)(2,1)S(1)}, u32[]{:S(2)}, u32[]{:S(2)}) %collective-permute-start.8) | collective-permute-done | bytes 237600 | tf_op jit(solution)/shard_map/ppermute | solution.py:150
  26.7 0.5 collective-permute-start.12
  27.2 0.5 collective-permute-start.15
  27.7 0.1 collective-permute-start.13
  27.8 0.4 collective-permute-done.11.refs_2_
  28.2 0.1 collective-permute-start.10
  28.3 3.3 %shard_map.66 = (f32[64,3584]{1,0:T(8,128)S(1)}, bf16[64,3584]{1,0:T(8,128)(2,1)S(1)}) custom-call(bf16[32,3712]{1,0:T(8,128)(2,1)S(1)} %collective-permute-done.1.refs_0_, bf16[32,3712]{1,0:T(8,128)(2,1)S(1)} %collective-permute-done.4.refs_1_, bf16[32,3712]{1,0:T(8,128)(2,1)S(1)} %collective-permute-done.5.refs_2_, ...), custom_call_target="tpu_custom_call" | custom-call | flops 5637144576 | tf_op jit(solution)/shard_map/pallas_call | solution.py:130
  31.7 0.4 collective-permute-start.16
  32.1 6.1 %shard_map.67 = (f32[160,3584]{1,0:T(8,128)S(1)}, bf16[64,3584]{1,0:T(8,128)(2,1)S(1)}, bf16[32,3584]{1,0:T(8,128)(2,1)S(1)}) custom-call(bf16[32,3712]{1,0:T(8,128)(2,1)S(1)} %collective-permute-done.8.refs_0_, bf16[32,3712]{1,0:T(8,128)(2,1)S(1)} %collective-permute-done.13.refs_1_, bf16[32,3712]{1,0:T(8,128)(2,1)S(1)} %collective-permute-done.11.refs_2_, ...), custom_call_target="tpu_custom_call" | custom-call | flops 5637144576 | tf_op jit(solution)/shard_map/pallas_call | solution.py:130
  38.2 0.2 collective-permute-start.17
  38.4 0.4 collective-permute-start.19
  38.8 1.3 %collective-permute-done.17 = bf16[64,3584]{1,0:T(8,128)(2,1)S(1)} collective-permute-done((bf16[64,3584]{1,0:T(8,128)(2,1)S(1)}, bf16[64,3584]{1,0:T(8,128)(2,1)S(1)}, u32[]{:S(2)}, u32[]{:S(2)}) %collective-permute-start.17) | collective-permute-done | bytes 458784 | tf_op jit(solution)/shard_map/ppermute | solution.py:151
  40.1 2.1 %collective-permute-start.20 = (bf16[32,3584]{1,0:T(8,128)(2,1)S(1)}, bf16[32,3584]{1,0:T(8,128)(2,1)S(1)}, u32[]{:S(2)}, u32[]{:S(2)}) collective-permute-start(bf16[32,3584]{1,0:T(8,128)(2,1)S(1)} %add_convert_fusion.7), channel_id=1, source_target_pairs={{0,4},{4,8},{8,12},{12,14},{14,10},{10,6},{6,2},{2,0},{5,1},{9,5},... | collective-permute-start | bytes 688136 | tf_op jit(solution)/shard_map/ppermute | solution.py:150
  42.3 1.6 %collective-permute-start.18 = (bf16[32,3584]{1,0:T(8,128)(2,1)S(1)}, bf16[32,3584]{1,0:T(8,128)(2,1)S(1)}, u32[]{:S(2)}, u32[]{:S(2)}) collective-permute-start(bf16[32,3584]{1,0:T(8,128)(2,1)S(1)} %add_convert_fusion.6), channel_id=1, source_target_pairs={{0,4},{4,8},{8,12},{12,14},{14,10},{10,6},{6,2},{2,0},{5,1},{9,5},... | collective-permute-start | bytes 688136 | tf_op jit(solution)/shard_map/ppermute | solution.py:150
  43.9 2.3 %collective-permute-done.20 = bf16[32,3584]{1,0:T(8,128)(2,1)S(1)} collective-permute-done((bf16[32,3584]{1,0:T(8,128)(2,1)S(1)}, bf16[32,3584]{1,0:T(8,128)(2,1)S(1)}, u32[]{:S(2)}, u32[]{:S(2)}) %collective-permute-start.20) | collective-permute-done | bytes 229408 | tf_op jit(solution)/shard_map/ppermute | solution.py:150
  46.2 0.1 add_convert_fusion.5
  46.3 2.1 %collective-permute-start.22 = (bf16[32,3584]{1,0:T(8,128)(2,1)S(1)}, bf16[32,3584]{1,0:T(8,128)(2,1)S(1)}, u32[]{:S(2)}, u32[]{:S(2)}) collective-permute-start(bf16[32,3584]{1,0:T(8,128)(2,1)S(1)} %add_convert_fusion.5), channel_id=1, source_target_pairs={{0,4},{4,8},{8,12},{12,14},{14,10},{10,6},{6,2},{2,0},{5,1},{9,5},... | collective-permute-start | bytes 688136 | tf_op jit(solution)/shard_map/ppermute | solution.py:150
  48.4 0.3 collective-permute-done.18
  48.6 0.1 add_convert_fusion.4
  48.7 2.1 %collective-permute-start.21 = (bf16[32,3584]{1,0:T(8,128)(2,1)S(1)}, bf16[32,3584]{1,0:T(8,128)(2,1)S(1)}, u32[]{:S(2)}, u32[]{:S(2)}) collective-permute-start(bf16[32,3584]{1,0:T(8,128)(2,1)S(1)} %add_convert_fusion.4), channel_id=1, source_target_pairs={{0,4},{4,8},{8,12},{12,14},{14,10},{10,6},{6,2},{2,0},{5,1},{9,5},... | collective-permute-start | bytes 688136 | tf_op jit(solution)/shard_map/ppermute | solution.py:150
  50.9 1.5 %collective-permute-done.22 = bf16[32,3584]{1,0:T(8,128)(2,1)S(1)} collective-permute-done((bf16[32,3584]{1,0:T(8,128)(2,1)S(1)}, bf16[32,3584]{1,0:T(8,128)(2,1)S(1)}, u32[]{:S(2)}, u32[]{:S(2)}) %collective-permute-start.22) | collective-permute-done | bytes 229408 | tf_op jit(solution)/shard_map/ppermute | solution.py:150
  52.3 0.1 add_convert_fusion.3
  52.4 2.1 %collective-permute-start.25 = (bf16[32,3584]{1,0:T(8,128)(2,1)S(1)}, bf16[32,3584]{1,0:T(8,128)(2,1)S(1)}, u32[]{:S(2)}, u32[]{:S(2)}) collective-permute-start(bf16[32,3584]{1,0:T(8,128)(2,1)S(1)} %add_convert_fusion.3), channel_id=1, source_target_pairs={{0,4},{4,8},{8,12},{12,14},{14,10},{10,6},{6,2},{2,0},{5,1},{9,5},... | collective-permute-start | bytes 688136 | tf_op jit(solution)/shard_map/ppermute | solution.py:150
  54.5 0.3 collective-permute-done.21
  54.8 0.1 add_convert_fusion.2
  54.9 2.1 %collective-permute-start.23 = (bf16[32,3584]{1,0:T(8,128)(2,1)S(1)}, bf16[32,3584]{1,0:T(8,128)(2,1)S(1)}, u32[]{:S(2)}, u32[]{:S(2)}) collective-permute-start(bf16[32,3584]{1,0:T(8,128)(2,1)S(1)} %add_convert_fusion.2), channel_id=1, source_target_pairs={{0,4},{4,8},{8,12},{12,14},{14,10},{10,6},{6,2},{2,0},{5,1},{9,5},... | collective-permute-start | bytes 688136 | tf_op jit(solution)/shard_map/ppermute | solution.py:150
  57.0 1.5 %collective-permute-done.25 = bf16[32,3584]{1,0:T(8,128)(2,1)S(1)} collective-permute-done((bf16[32,3584]{1,0:T(8,128)(2,1)S(1)}, bf16[32,3584]{1,0:T(8,128)(2,1)S(1)}, u32[]{:S(2)}, u32[]{:S(2)}) %collective-permute-start.25) | collective-permute-done | bytes 229408 | tf_op jit(solution)/shard_map/ppermute | solution.py:150
  58.5 0.1 add_convert_fusion.1
  58.6 2.1 %collective-permute-start.26 = (bf16[32,3584]{1,0:T(8,128)(2,1)S(1)}, bf16[32,3584]{1,0:T(8,128)(2,1)S(1)}, u32[]{:S(2)}, u32[]{:S(2)}) collective-permute-start(bf16[32,3584]{1,0:T(8,128)(2,1)S(1)} %add_convert_fusion.1), channel_id=1, source_target_pairs={{0,4},{4,8},{8,12},{12,14},{14,10},{10,6},{6,2},{2,0},{5,1},{9,5},... | collective-permute-start | bytes 688136 | tf_op jit(solution)/shard_map/ppermute | solution.py:150
  60.7 0.3 collective-permute-done.23
  60.9 3.7 %collective-permute-done.26 = bf16[32,3584]{1,0:T(8,128)(2,1)S(1)} collective-permute-done((bf16[32,3584]{1,0:T(8,128)(2,1)S(1)}, bf16[32,3584]{1,0:T(8,128)(2,1)S(1)}, u32[]{:S(2)}, u32[]{:S(2)}) %collective-permute-start.26) | collective-permute-done | bytes 229408 | tf_op jit(solution)/shard_map/ppermute | solution.py:150
  64.6 0.1 convert_add_fusion
  64.7 0.7 %add_convert_fusion = bf16[32,3584]{1,0:T(8,128)(2,1)} fusion(f32[32,3584]{1,0:T(8,128)S(1)} %convert_add_fusion, bf16[32,3584]{1,0:T(8,128)(2,1)S(1)} %collective-permute-done.24), kind=kLoop, calls=%fused_computation | loop fusion | flops 344064 | bytes 917504 | tf_op jit(solution)/shard_map/convert_element_type | solution.py:225
  (25 shorter events, 0.1 us)
Async XLA Ops:
  0.0 22.6 %copy-start = (bf16[1,3584,1024]{2,1,0:T(8,128)(2,1)S(1)}, bf16[1,3584,1024]{2,1,0:T(8,128)(2,1)}, u32[]{:S(2)}) copy-start(bf16[1,3584,1024]{2,1,0:T(8,128)(2,1)} %refs_8_.1) | copy-start | bytes 22020100
  0.0 22.7 %copy-start.1 = (bf16[1,3584,1024]{2,1,0:T(8,128)(2,1)S(1)}, bf16[1,3584,1024]{2,1,0:T(8,128)(2,1)}, u32[]{:S(2)}) copy-start(bf16[1,3584,1024]{2,1,0:T(8,128)(2,1)} %refs_9_.1) | copy-start | bytes 22020100
  0.0 22.7 %copy-start.2 = (bf16[1,1024,3584]{2,1,0:T(8,128)(2,1)S(1)}, bf16[1,1024,3584]{2,1,0:T(8,128)(2,1)}, u32[]{:S(2)}) copy-start(bf16[1,1024,3584]{2,1,0:T(8,128)(2,1)} %refs_10_.1) | copy-start | bytes 22020100
  1.2 3.2 %collective-permute-start.2 = (bf16[32,3712]{1,0:T(8,128)(2,1)S(1)}, bf16[32,3712]{1,0:T(8,128)(2,1)S(1)}, u32[]{:S(2)}, u32[]{:S(2)}) collective-permute-start(bf16[32,3712]{1,0:T(8,128)(2,1)S(1)} %shard_map.64.refs_0_), channel_id=1, source_target_pairs={{0,1},{1,0},{2,3},{3,2},{4,5},{5,4},{6,7},{7,6},{8,9},{9,8},{10,11... | collective-permute-start | bytes 712712 | tf_op jit(solution)/shard_map/ppermute | solution.py:151
  1.7 6.7 %collective-permute-start = (bf16[32,3712]{1,0:T(8,128)(2,1)S(1)}, bf16[32,3712]{1,0:T(8,128)(2,1)S(1)}, u32[]{:S(2)}, u32[]{:S(2)}) collective-permute-start(bf16[32,3712]{1,0:T(8,128)(2,1)S(1)} %shard_map.64.refs_0_), channel_id=1, source_target_pairs={{0,4},{4,8},{8,12},{12,14},{14,10},{10,6},{6,2},{2,0},{5,1},{9,5},... | collective-permute-start | bytes 712712 | tf_op jit(solution)/shard_map/ppermute | solution.py:150
  4.3 6.6 %collective-permute-start.3 = (bf16[32,3712]{1,0:T(8,128)(2,1)S(1)}, bf16[32,3712]{1,0:T(8,128)(2,1)S(1)}, u32[]{:S(2)}, u32[]{:S(2)}) collective-permute-start(bf16[32,3712]{1,0:T(8,128)(2,1)S(1)} %collective-permute-done.2.refs_3_), channel_id=1, source_target_pairs={{0,4},{4,8},{8,12},{12,14},{14,10},{10,6},{6,2},{2,0},{5,1},{9,5},... | collective-permute-start | bytes 712712 | tf_op jit(solution)/shard_map/ppermute | solution.py:150
  8.4 6.1 %collective-permute-start.5 = (bf16[32,3712]{1,0:T(8,128)(2,1)S(1)}, bf16[32,3712]{1,0:T(8,128)(2,1)S(1)}, u32[]{:S(2)}, u32[]{:S(2)}) collective-permute-start(bf16[32,3712]{1,0:T(8,128)(2,1)S(1)} %collective-permute-done.refs_1_), channel_id=1, source_target_pairs={{0,4},{4,8},{8,12},{12,14},{14,10},{10,6},{6,2},{2,0},{5,1},{9,5},... | collective-permute-start | bytes 712712 | tf_op jit(solution)/shard_map/ppermute | solution.py:150
  10.9 6.2 %collective-permute-start.6 = (bf16[32,3712]{1,0:T(8,128)(2,1)S(1)}, bf16[32,3712]{1,0:T(8,128)(2,1)S(1)}, u32[]{:S(2)}, u32[]{:S(2)}) collective-permute-start(bf16[32,3712]{1,0:T(8,128)(2,1)S(1)} %collective-permute-done.3.refs_2_), channel_id=1, source_target_pairs={{0,4},{4,8},{8,12},{12,14},{14,10},{10,6},{6,2},{2,0},{5,1},{9,5},... | collective-permute-start | bytes 712712 | tf_op jit(solution)/shard_map/ppermute | solution.py:150
  14.5 6.1 %collective-permute-start.7 = (bf16[32,3712]{1,0:T(8,128)(2,1)S(1)}, bf16[32,3712]{1,0:T(8,128)(2,1)S(1)}, u32[]{:S(2)}, u32[]{:S(2)}) collective-permute-start(bf16[32,3712]{1,0:T(8,128)(2,1)S(1)} %collective-permute-done.5.refs_2_), channel_id=1, source_target_pairs={{0,4},{4,8},{8,12},{12,14},{14,10},{10,6},{6,2},{2,0},{5,1},{9,5},... | collective-permute-start | bytes 712712 | tf_op jit(solution)/shard_map/ppermute | solution.py:150
  16.5 10.7 %collective-permute-start.1 = (bf16[32,3712]{1,0:T(8,128)(2,1)S(1)}, bf16[32,3712]{1,0:T(8,128)(2,1)S(1)}, u32[]{:S(2)}, u32[]{:S(2)}) collective-permute-start(bf16[32,3712]{1,0:T(8,128)(2,1)S(1)} %collective-permute-done.refs_1_), channel_id=1, source_target_pairs={{0,1},{1,0},{2,3},{3,2},{4,5},{5,4},{6,7},{7,6},{8,9},{9,8},{10,11... | collective-permute-start | bytes 712712 | tf_op jit(solution)/shard_map/ppermute | solution.py:151
  16.5 11.2 %collective-permute-start.4 = (bf16[32,3712]{1,0:T(8,128)(2,1)S(1)}, bf16[32,3712]{1,0:T(8,128)(2,1)S(1)}, u32[]{:S(2)}, u32[]{:S(2)}) collective-permute-start(bf16[32,3712]{1,0:T(8,128)(2,1)S(1)} %collective-permute-done.3.refs_2_), channel_id=1, source_target_pairs={{0,1},{1,0},{2,3},{3,2},{4,5},{5,4},{6,7},{7,6},{8,9},{9,8},{10,11... | collective-permute-start | bytes 712712 | tf_op jit(solution)/shard_map/ppermute | solution.py:151
  17.1 8.9 %collective-permute-start.9 = (bf16[32,3712]{1,0:T(8,128)(2,1)S(1)}, bf16[32,3712]{1,0:T(8,128)(2,1)S(1)}, u32[]{:S(2)}, u32[]{:S(2)}) collective-permute-start(bf16[32,3712]{1,0:T(8,128)(2,1)S(1)} %collective-permute-done.6.refs_3_), channel_id=1, source_target_pairs={{0,4},{4,8},{8,12},{12,14},{14,10},{10,6},{6,2},{2,0},{5,1},{9,5},... | collective-permute-start | bytes 712712 | tf_op jit(solution)/shard_map/ppermute | solution.py:150
  20.6 6.1 %collective-permute-start.8 = (bf16[32,3712]{1,0:T(8,128)(2,1)S(1)}, bf16[32,3712]{1,0:T(8,128)(2,1)S(1)}, u32[]{:S(2)}, u32[]{:S(2)}) collective-permute-start(bf16[32,3712]{1,0:T(8,128)(2,1)S(1)} %collective-permute-done.7.refs_6_), channel_id=1, source_target_pairs={{0,4},{4,8},{8,12},{12,14},{14,10},{10,6},{6,2},{2,0},{5,1},{9,5},... | collective-permute-start | bytes 712712 | tf_op jit(solution)/shard_map/ppermute | solution.py:150
  26.7 1.5 %collective-permute-start.11 = (bf16[32,3712]{1,0:T(8,128)(2,1)S(1)}, bf16[32,3712]{1,0:T(8,128)(2,1)S(1)}, u32[]{:S(2)}, u32[]{:S(2)}) collective-permute-start(bf16[32,3712]{1,0:T(8,128)(2,1)S(1)} %collective-permute-done.9.refs_7_), channel_id=1, source_target_pairs={{0,1},{1,0},{2,3},{3,2},{4,5},{5,4},{6,7},{7,6},{8,9},{9,8},{10,11... | collective-permute-start | bytes 712712 | tf_op jit(solution)/shard_map/ppermute | solution.py:151
  26.7 5.0 %collective-permute-start.12 = (bf16[96,3584]{1,0:T(8,128)(2,1)S(1)}, bf16[96,3584]{1,0:T(8,128)(2,1)S(1)}, u32[]{:S(2)}, u32[]{:S(2)}) collective-permute-start(bf16[96,3584]{1,0:T(8,128)(2,1)S(1)} %get-tuple-element.55), channel_id=1, source_target_pairs={{0,1},{1,0},{2,3},{3,2},{4,5},{5,4},{6,7},{7,6},{8,9},{9,8},{10,11... | collective-permute-start | bytes 2064392 | tf_op jit(solution)/shard_map/ppermute | solution.py:151
  27.2 4.9 %collective-permute-start.14 = (bf16[32,3712]{1,0:T(8,128)(2,1)S(1)}, bf16[32,3712]{1,0:T(8,128)(2,1)S(1)}, u32[]{:S(2)}, u32[]{:S(2)}) collective-permute-start(bf16[32,3712]{1,0:T(8,128)(2,1)S(1)} %collective-permute-done.5.refs_2_), channel_id=1, source_target_pairs={{0,1},{1,0},{2,3},{3,2},{4,5},{5,4},{6,7},{7,6},{8,9},{9,8},{10,11... | collective-permute-start | bytes 712712 | tf_op jit(solution)/shard_map/ppermute | solution.py:151
  27.2 4.9 %collective-permute-start.15 = (bf16[32,3712]{1,0:T(8,128)(2,1)S(1)}, bf16[32,3712]{1,0:T(8,128)(2,1)S(1)}, u32[]{:S(2)}, u32[]{:S(2)}) collective-permute-start(bf16[32,3712]{1,0:T(8,128)(2,1)S(1)} %collective-permute-done.6.refs_3_), channel_id=1, source_target_pairs={{0,1},{1,0},{2,3},{3,2},{4,5},{5,4},{6,7},{7,6},{8,9},{9,8},{10,11... | collective-permute-start | bytes 712712 | tf_op jit(solution)/shard_map/ppermute | solution.py:151
  27.7 4.4 %collective-permute-start.13 = (bf16[32,3712]{1,0:T(8,128)(2,1)S(1)}, bf16[32,3712]{1,0:T(8,128)(2,1)S(1)}, u32[]{:S(2)}, u32[]{:S(2)}) collective-permute-start(bf16[32,3712]{1,0:T(8,128)(2,1)S(1)} %collective-permute-done.7.refs_6_), channel_id=1, source_target_pairs={{0,1},{1,0},{2,3},{3,2},{4,5},{5,4},{6,7},{7,6},{8,9},{9,8},{10,11... | collective-permute-start | bytes 712712 | tf_op jit(solution)/shard_map/ppermute | solution.py:151
  28.2 3.5 %collective-permute-start.10 = (bf16[32,3712]{1,0:T(8,128)(2,1)S(1)}, bf16[32,3712]{1,0:T(8,128)(2,1)S(1)}, u32[]{:S(2)}, u32[]{:S(2)}) collective-permute-start(bf16[32,3712]{1,0:T(8,128)(2,1)S(1)} %collective-permute-done.8.refs_0_), channel_id=1, source_target_pairs={{0,1},{1,0},{2,3},{3,2},{4,5},{5,4},{6,7},{7,6},{8,9},{9,8},{10,11... | collective-permute-start | bytes 712712 | tf_op jit(solution)/shard_map/ppermute | solution.py:151
  31.7 6.5 %collective-permute-start.16 = (bf16[64,3584]{1,0:T(8,128)(2,1)S(1)}, bf16[64,3584]{1,0:T(8,128)(2,1)S(1)}, u32[]{:S(2)}, u32[]{:S(2)}) collective-permute-start(bf16[64,3584]{1,0:T(8,128)(2,1)S(1)} %get-tuple-element.63), channel_id=1, source_target_pairs={{0,1},{1,0},{2,3},{3,2},{4,5},{5,4},{6,7},{7,6},{8,9},{9,8},{10,11... | collective-permute-start | bytes 1376264 | tf_op jit(solution)/shard_map/ppermute | solution.py:151
  38.2 1.9 %collective-permute-start.17 = (bf16[64,3584]{1,0:T(8,128)(2,1)S(1)}, bf16[64,3584]{1,0:T(8,128)(2,1)S(1)}, u32[]{:S(2)}, u32[]{:S(2)}) collective-permute-start(bf16[64,3584]{1,0:T(8,128)(2,1)S(1)} %get-tuple-element.66), channel_id=1, source_target_pairs={{0,1},{1,0},{2,3},{3,2},{4,5},{5,4},{6,7},{7,6},{8,9},{9,8},{10,11... | collective-permute-start | bytes 1376264 | tf_op jit(solution)/shard_map/ppermute | solution.py:151
  38.4 5.5 %collective-permute-start.19 = (bf16[32,3584]{1,0:T(8,128)(2,1)S(1)}, bf16[32,3584]{1,0:T(8,128)(2,1)S(1)}, u32[]{:S(2)}, u32[]{:S(2)}) collective-permute-start(bf16[32,3584]{1,0:T(8,128)(2,1)S(1)} %get-tuple-element.69), channel_id=1, source_target_pairs={{0,1},{1,0},{2,3},{3,2},{4,5},{5,4},{6,7},{7,6},{8,9},{9,8},{10,11... | collective-permute-start | bytes 688136 | tf_op jit(solution)/shard_map/ppermute | solution.py:151
  40.1 6.1 %collective-permute-start.20 = (bf16[32,3584]{1,0:T(8,128)(2,1)S(1)}, bf16[32,3584]{1,0:T(8,128)(2,1)S(1)}, u32[]{:S(2)}, u32[]{:S(2)}) collective-permute-start(bf16[32,3584]{1,0:T(8,128)(2,1)S(1)} %add_convert_fusion.7), channel_id=1, source_target_pairs={{0,4},{4,8},{8,12},{12,14},{14,10},{10,6},{6,2},{2,0},{5,1},{9,5},... | collective-permute-start | bytes 688136 | tf_op jit(solution)/shard_map/ppermute | solution.py:150
  42.3 6.4 %collective-permute-start.18 = (bf16[32,3584]{1,0:T(8,128)(2,1)S(1)}, bf16[32,3584]{1,0:T(8,128)(2,1)S(1)}, u32[]{:S(2)}, u32[]{:S(2)}) collective-permute-start(bf16[32,3584]{1,0:T(8,128)(2,1)S(1)} %add_convert_fusion.6), channel_id=1, source_target_pairs={{0,4},{4,8},{8,12},{12,14},{14,10},{10,6},{6,2},{2,0},{5,1},{9,5},... | collective-permute-start | bytes 688136 | tf_op jit(solution)/shard_map/ppermute | solution.py:150
  46.3 6.1 %collective-permute-start.22 = (bf16[32,3584]{1,0:T(8,128)(2,1)S(1)}, bf16[32,3584]{1,0:T(8,128)(2,1)S(1)}, u32[]{:S(2)}, u32[]{:S(2)}) collective-permute-start(bf16[32,3584]{1,0:T(8,128)(2,1)S(1)} %add_convert_fusion.5), channel_id=1, source_target_pairs={{0,4},{4,8},{8,12},{12,14},{14,10},{10,6},{6,2},{2,0},{5,1},{9,5},... | collective-permute-start | bytes 688136 | tf_op jit(solution)/shard_map/ppermute | solution.py:150
  48.7 6.1 %collective-permute-start.21 = (bf16[32,3584]{1,0:T(8,128)(2,1)S(1)}, bf16[32,3584]{1,0:T(8,128)(2,1)S(1)}, u32[]{:S(2)}, u32[]{:S(2)}) collective-permute-start(bf16[32,3584]{1,0:T(8,128)(2,1)S(1)} %add_convert_fusion.4), channel_id=1, source_target_pairs={{0,4},{4,8},{8,12},{12,14},{14,10},{10,6},{6,2},{2,0},{5,1},{9,5},... | collective-permute-start | bytes 688136 | tf_op jit(solution)/shard_map/ppermute | solution.py:150
  52.4 6.1 %collective-permute-start.25 = (bf16[32,3584]{1,0:T(8,128)(2,1)S(1)}, bf16[32,3584]{1,0:T(8,128)(2,1)S(1)}, u32[]{:S(2)}, u32[]{:S(2)}) collective-permute-start(bf16[32,3584]{1,0:T(8,128)(2,1)S(1)} %add_convert_fusion.3), channel_id=1, source_target_pairs={{0,4},{4,8},{8,12},{12,14},{14,10},{10,6},{6,2},{2,0},{5,1},{9,5},... | collective-permute-start | bytes 688136 | tf_op jit(solution)/shard_map/ppermute | solution.py:150
  54.9 6.1 %collective-permute-start.23 = (bf16[32,3584]{1,0:T(8,128)(2,1)S(1)}, bf16[32,3584]{1,0:T(8,128)(2,1)S(1)}, u32[]{:S(2)}, u32[]{:S(2)}) collective-permute-start(bf16[32,3584]{1,0:T(8,128)(2,1)S(1)} %add_convert_fusion.2), channel_id=1, source_target_pairs={{0,4},{4,8},{8,12},{12,14},{14,10},{10,6},{6,2},{2,0},{5,1},{9,5},... | collective-permute-start | bytes 688136 | tf_op jit(solution)/shard_map/ppermute | solution.py:150
  58.6 6.1 %collective-permute-start.26 = (bf16[32,3584]{1,0:T(8,128)(2,1)S(1)}, bf16[32,3584]{1,0:T(8,128)(2,1)S(1)}, u32[]{:S(2)}, u32[]{:S(2)}) collective-permute-start(bf16[32,3584]{1,0:T(8,128)(2,1)S(1)} %add_convert_fusion.1), channel_id=1, source_target_pairs={{0,4},{4,8},{8,12},{12,14},{14,10},{10,6},{6,2},{2,0},{5,1},{9,5},... | collective-permute-start | bytes 688136 | tf_op jit(solution)/shard_map/ppermute | solution.py:150
  60.9 3.8 %collective-permute-start.24 = (bf16[32,3584]{1,0:T(8,128)(2,1)S(1)}, bf16[32,3584]{1,0:T(8,128)(2,1)S(1)}, u32[]{:S(2)}, u32[]{:S(2)}) collective-permute-start(bf16[32,3584]{1,0:T(8,128)(2,1)S(1)} %collective-permute-done.23), channel_id=1, source_target_pairs={{0,1},{1,0},{2,3},{3,2},{4,5},{5,4},{6,7},{7,6},{8,9},{9,8},{10,11... | collective-permute-start | bytes 688136 | tf_op jit(solution)/shard_map/ppermute | solution.py:151

commit v15 on v14

--- a/solution.py
+++ b/solution.py
@@ -180,25 +180,19 @@
         mine.update({j: (out, at) for at, j in enumerate(keep)})
         theirs.update(zip(give, [(piece, at) for piece in pieces for at in range(piece.shape[0] // rows)]))
 
-    keep, give = [end], [end - 2, end - 1, end]
-    out, pieces = compute(keep, give, (3,))
-    out, pieces, kept[0], given[2] = together((out, pieces, kept[0], given[2]))
-    given[0] = sibling(kept[0])
-    kept[2] = sibling(given[2])
-    pieces = [sibling(p) for p in pieces]
-    note(keep, out, give, pieces)
-
-    keep, give = [end - 2, end - 1], [end - 4, end - 3]
-    kept[end - 2 : end], given[end - 4 : end - 2], _ = together((kept[end - 2 : end], given[end - 4 : end - 2], kept[0]))
-    out_too, given_too = compute(keep, give, (2,))
-    out_too, given_too, given[0], kept[2], pieces = together((out_too, given_too, given[0], kept[2], pieces))
-    note([end], out, [end - 2, end - 1, end], pieces)
-    sent_too = [sibling(p) for p in given_too]
+    keep, give = [end - 2, end - 1, end], list(range(end - 4, end + 1))
+    near, near_given = compute(keep, give, (5,))
+    others = kept[1:2] + kept[3 : end - 2]
+    near, near_given, kept[0], given[2], others = together((near, near_given, kept[0], given[2], others))
+    kept[1], kept[3 : end - 2] = others[0], others[1:]
+    given[0], kept[2] = sibling(kept[0]), sibling(given[2])
+    given[0], kept[2], near_given = together((given[0], kept[2], near_given))
+    near_sent = [sibling(p) for p in near_given]
 
     keep_last, give_last = list(range(end - 2)), list(range(end - 4))
     out, pieces = compute(keep_last, give_last, (2, len(give_last) - 2))
-    out, pieces, sent_too = together((out, pieces, sent_too))
-    note(keep, out_too, give, sent_too)
+    out, pieces, near_sent = together((out, pieces, near_sent))
+    note(keep, near, give, near_sent)
     note(keep_last, out, give_last, [sibling(p) for p in pieces])
 
     def add(j, *arrived):

time: 65.6 us -> 64.4 us (0.982)
  starting transfers between devices: 32.2 us -> 28.2 us
  waiting for transfers between devices: 18.1 us -> 21.3 us
    ppermute x14, starting transfers between devices: 29 us -> 25.9 us  [local(): send = lambda a: lax.ppermute(a, 'node', spin)]
    ppermute x14, waiting for transfers between devices: 16.3 us -> 18.7 us  [local(): send = lambda a: lax.ppermute(a, 'node', spin)]
    ppermute x13 -> x12, waiting for transfers between devices: 1.74 us -> 2.66 us  [local(): sibling = lambda a: lax.ppermute(a, 'node', swap)]
    ppermute x13 -> x12, starting transfers between devices: 3.28 us -> 2.38 us  [local(): sibling = lambda a: lax.ppermute(a, 'node', swap)]
    pallas_call x3 -> x2, Pallas kernels: 12.6 us -> 12.1 us  [expert(): pl.pallas_call(functools.partial(expert_kernel, count, experts, *tiles(wi...]
  transfers between devices with their start and end apart: 27 -> 26, of which waited for: 14 -> 14; matrix products, arithmetic and copies ran while one was open for 1% -> 1% of each run, Pallas kernels for 19% -> 19%
where the time goes in v15:
time: 64.4 us; the launch traced here: 64.3 us
  starting transfers between devices  28.2 us (44%)
  waiting for transfers between devices  21.3 us (33%)
  Pallas kernels  13.2 us (20%)
  other arithmetic  1.24 us (2%)
    ppermute x14, starting transfers between devices, local(): send = lambda a: lax.ppermute(a, 'node', spin)  25.9 us
    ppermute x14, waiting for transfers between devices, local(): send = lambda a: lax.ppermute(a, 'node', spin)  18.7 us
    pallas_call x2, Pallas kernels, expert(): pl.pallas_call(functools.partial(expert_kernel, count, experts, *tiles(wi...  12.1 us
    ppermute x12, waiting for transfers between devices, local(): sibling = lambda a: lax.ppermute(a, 'node', swap)  2.66 us
    ppermute x12, starting transfers between devices, local(): sibling = lambda a: lax.ppermute(a, 'node', swap)  2.38 us
  transfers between devices with their start and end apart: 26, of which 14 were waited for; matrix products, arithmetic and copies ran while one was open for 1% of the time, Pallas kernels for 19%

profile of v15, /device:TPU:0, one launch (start us, length us, event | category | flops | bytes accessed | tf_op | source)
XLA Modules:
  0.0 64.3 jit_solution(5816029637321904755)
XLA Ops:
  0.0 0.0 slice-start.5
  0.0 1.1 %shard_map.64.refs_2_ = bf16[32,3712]{1,0:T(8,128)(2,1)S(1)} custom-call(bf16[32,3584]{1,0:T(8,128)(2,1)} %tok_hbm.1, s32[8,32]{1,0:T(8,128)} %bitcast.8, f32[8,32]{1,0:T(8,128)} %bitcast.9), custom_call_target="tpu_custom_call" | custom-call | flops 10737418240 | tf_op jit(solution)/shard_map/pallas_call | solution.py:59
  1.2 0.5 collective-permute-start.2
  1.7 2.6 %collective-permute-start = (bf16[32,3712]{1,0:T(8,128)(2,1)S(1)}, bf16[32,3712]{1,0:T(8,128)(2,1)S(1)}, u32[]{:S(2)}, u32[]{:S(2)}) collective-permute-start(bf16[32,3712]{1,0:T(8,128)(2,1)S(1)} %shard_map.64.refs_2_), channel_id=1, source_target_pairs={{0,4},{4,8},{8,12},{12,14},{14,10},{10,6},{6,2},{2,0},{5,1},{9,5},... | collective-permute-start | bytes 712712 | tf_op jit(solution)/shard_map/ppermute | solution.py:150
  4.4 0.0 collective-permute-done.2.refs_7_
  4.4 1.6 %collective-permute-start.3 = (bf16[32,3712]{1,0:T(8,128)(2,1)S(1)}, bf16[32,3712]{1,0:T(8,128)(2,1)S(1)}, u32[]{:S(2)}, u32[]{:S(2)}) collective-permute-start(bf16[32,3712]{1,0:T(8,128)(2,1)S(1)} %collective-permute-done.2.refs_7_), channel_id=1, source_target_pairs={{0,4},{4,8},{8,12},{12,14},{14,10},{10,6},{6,2},{2,0},{5,1},{9,5},... | collective-permute-start | bytes 712712 | tf_op jit(solution)/shard_map/ppermute | solution.py:150
  5.9 2.5 %collective-permute-done.refs_5_ = bf16[32,3712]{1,0:T(8,128)(2,1)S(1)} collective-permute-done((bf16[32,3712]{1,0:T(8,128)(2,1)S(1)}, bf16[32,3712]{1,0:T(8,128)(2,1)S(1)}, u32[]{:S(2)}, u32[]{:S(2)}) %collective-permute-start) | collective-permute-done | bytes 237600 | tf_op jit(solution)/shard_map/ppermute | solution.py:150
  8.4 2.1 %collective-permute-start.5 = (bf16[32,3712]{1,0:T(8,128)(2,1)S(1)}, bf16[32,3712]{1,0:T(8,128)(2,1)S(1)}, u32[]{:S(2)}, u32[]{:S(2)}) collective-permute-start(bf16[32,3712]{1,0:T(8,128)(2,1)S(1)} %collective-permute-done.refs_5_), channel_id=1, source_target_pairs={{0,4},{4,8},{8,12},{12,14},{14,10},{10,6},{6,2},{2,0},{5,1},{9,5},... | collective-permute-start | bytes 712712 | tf_op jit(solution)/shard_map/ppermute | solution.py:150
  10.5 0.5 collective-permute-done.3.refs_6_
  10.9 2.1 %collective-permute-start.6 = (bf16[32,3712]{1,0:T(8,128)(2,1)S(1)}, bf16[32,3712]{1,0:T(8,128)(2,1)S(1)}, u32[]{:S(2)}, u32[]{:S(2)}) collective-permute-start(bf16[32,3712]{1,0:T(8,128)(2,1)S(1)} %collective-permute-done.3.refs_6_), channel_id=1, source_target_pairs={{0,4},{4,8},{8,12},{12,14},{14,10},{10,6},{6,2},{2,0},{5,1},{9,5},... | collective-permute-start | bytes 712712 | tf_op jit(solution)/shard_map/ppermute | solution.py:150
  13.0 1.5 %collective-permute-done.5.refs_3_ = bf16[32,3712]{1,0:T(8,128)(2,1)S(1)} collective-permute-done((bf16[32,3712]{1,0:T(8,128)(2,1)S(1)}, bf16[32,3712]{1,0:T(8,128)(2,1)S(1)}, u32[]{:S(2)}, u32[]{:S(2)}) %collective-permute-start.5) | collective-permute-done | bytes 237600 | tf_op jit(solution)/shard_map/ppermute | solution.py:150
  14.5 2.1 %collective-permute-start.7 = (bf16[32,3712]{1,0:T(8,128)(2,1)S(1)}, bf16[32,3712]{1,0:T(8,128)(2,1)S(1)}, u32[]{:S(2)}, u32[]{:S(2)}) collective-permute-start(bf16[32,3712]{1,0:T(8,128)(2,1)S(1)} %collective-permute-done.5.refs_3_), channel_id=1, source_target_pairs={{0,4},{4,8},{8,12},{12,14},{14,10},{10,6},{6,2},{2,0},{5,1},{9,5},... | collective-permute-start | bytes 712712 | tf_op jit(solution)/shard_map/ppermute | solution.py:150
  16.6 0.5 collective-permute-start.11
  17.1 0.0 collective-permute-start.12
  17.1 2.0 %collective-permute-start.9 = (bf16[32,3712]{1,0:T(8,128)(2,1)S(1)}, bf16[32,3712]{1,0:T(8,128)(2,1)S(1)}, u32[]{:S(2)}, u32[]{:S(2)}) collective-permute-start(bf16[32,3712]{1,0:T(8,128)(2,1)S(1)} %collective-permute-done.6.refs_4_), channel_id=1, source_target_pairs={{0,4},{4,8},{8,12},{12,14},{14,10},{10,6},{6,2},{2,0},{5,1},{9,5},... | collective-permute-start | bytes 712712 | tf_op jit(solution)/shard_map/ppermute | solution.py:150
  19.1 1.5 %collective-permute-done.7.refs_6_ = bf16[32,3712]{1,0:T(8,128)(2,1)S(1)} collective-permute-done((bf16[32,3712]{1,0:T(8,128)(2,1)S(1)}, bf16[32,3712]{1,0:T(8,128)(2,1)S(1)}, u32[]{:S(2)}, u32[]{:S(2)}) %collective-permute-start.7) | collective-permute-done | bytes 237600 | tf_op jit(solution)/shard_map/ppermute | solution.py:150
  20.6 2.1 %collective-permute-start.8 = (bf16[32,3712]{1,0:T(8,128)(2,1)S(1)}, bf16[32,3712]{1,0:T(8,128)(2,1)S(1)}, u32[]{:S(2)}, u32[]{:S(2)}) collective-permute-start(bf16[32,3712]{1,0:T(8,128)(2,1)S(1)} %collective-permute-done.7.refs_6_), channel_id=1, source_target_pairs={{0,4},{4,8},{8,12},{12,14},{14,10},{10,6},{6,2},{2,0},{5,1},{9,5},... | collective-permute-start | bytes 712712 | tf_op jit(solution)/shard_map/ppermute | solution.py:150
  22.7 6.0 %shard_map.65 = (f32[96,3584]{1,0:T(8,128)S(1)}, bf16[160,3584]{1,0:T(8,128)(2,1)S(1)}) custom-call(bf16[32,3712]{1,0:T(8,128)(2,1)S(1)} %collective-permute-done.1.refs_0_, bf16[32,3712]{1,0:T(8,128)(2,1)S(1)} %collective-permute-done.4.refs_1_, bf16[32,3712]{1,0:T(8,128)(2,1)S(1)} %shard_map.64.refs_2_, ...), custom_call_target="tpu_custom_call" | custom-call | flops 5637144576 | tf_op jit(solution)/shard_map/pallas_call | solution.py:130
  28.9 0.2 collective-permute-start.13
  29.1 0.3 collective-permute-start.14
  29.4 1.0 %collective-permute-done.13.refs_5_ = bf16[32,3712]{1,0:T(8,128)(2,1)S(1)} collective-permute-done((bf16[32,3712]{1,0:T(8,128)(2,1)S(1)}, bf16[32,3712]{1,0:T(8,128)(2,1)S(1)}, u32[]{:S(2)}, u32[]{:S(2)}) %collective-permute-start.13) | collective-permute-done | bytes 237600 | tf_op jit(solution)/shard_map/ppermute | solution.py:151
  30.4 0.3 collective-permute-done.14.refs_2_
  30.8 0.2 collective-permute-start.15
  30.9 6.0 %shard_map.66 = (f32[160,3584]{1,0:T(8,128)S(1)}, bf16[64,3584]{1,0:T(8,128)(2,1)S(1)}, bf16[32,3584]{1,0:T(8,128)(2,1)S(1)}) custom-call(bf16[32,3712]{1,0:T(8,128)(2,1)S(1)} %collective-permute-done.8.refs_0_, bf16[32,3712]{1,0:T(8,128)(2,1)S(1)} %collective-permute-done.10.refs_1_, bf16[32,3712]{1,0:T(8,128)(2,1)S(1)} %collective-permute-done.14.refs_2_, ...), custom_call_target="tpu_custom_call" | custom-call | flops 5637144576 | tf_op jit(solution)/shard_map/pallas_call | solution.py:130
  37.0 0.4 collective-permute-start.16
  37.4 0.2 collective-permute-start.18
  37.6 1.3 %collective-permute-done.16 = bf16[64,3584]{1,0:T(8,128)(2,1)S(1)} collective-permute-done((bf16[64,3584]{1,0:T(8,128)(2,1)S(1)}, bf16[64,3584]{1,0:T(8,128)(2,1)S(1)}, u32[]{:S(2)}, u32[]{:S(2)}) %collective-permute-start.16) | collective-permute-done | bytes 458784 | tf_op jit(solution)/shard_map/ppermute | solution.py:151
  38.9 1.6 %collective-permute-start.19 = (bf16[32,3584]{1,0:T(8,128)(2,1)S(1)}, bf16[32,3584]{1,0:T(8,128)(2,1)S(1)}, u32[]{:S(2)}, u32[]{:S(2)}) collective-permute-start(bf16[32,3584]{1,0:T(8,128)(2,1)S(1)} %add_convert_fusion.7), channel_id=1, source_target_pairs={{0,4},{4,8},{8,12},{12,14},{14,10},{10,6},{6,2},{2,0},{5,1},{9,5},... | collective-permute-start | bytes 688136 | tf_op jit(solution)/shard_map/ppermute | solution.py:150
  40.6 1.6 %collective-permute-start.17 = (bf16[32,3584]{1,0:T(8,128)(2,1)S(1)}, bf16[32,3584]{1,0:T(8,128)(2,1)S(1)}, u32[]{:S(2)}, u32[]{:S(2)}) collective-permute-start(bf16[32,3584]{1,0:T(8,128)(2,1)S(1)} %add_convert_fusion.6), channel_id=1, source_target_pairs={{0,4},{4,8},{8,12},{12,14},{14,10},{10,6},{6,2},{2,0},{5,1},{9,5},... | collective-permute-start | bytes 688136 | tf_op jit(solution)/shard_map/ppermute | solution.py:150
  42.2 2.8 %collective-permute-done.19 = bf16[32,3584]{1,0:T(8,128)(2,1)S(1)} collective-permute-done((bf16[32,3584]{1,0:T(8,128)(2,1)S(1)}, bf16[32,3584]{1,0:T(8,128)(2,1)S(1)}, u32[]{:S(2)}, u32[]{:S(2)}) %collective-permute-start.19) | collective-permute-done | bytes 229408 | tf_op jit(solution)/shard_map/ppermute | solution.py:150
  45.0 0.1 add_convert_fusion.5
  45.1 1.6 %collective-permute-start.21 = (bf16[32,3584]{1,0:T(8,128)(2,1)S(1)}, bf16[32,3584]{1,0:T(8,128)(2,1)S(1)}, u32[]{:S(2)}, u32[]{:S(2)}) collective-permute-start(bf16[32,3584]{1,0:T(8,128)(2,1)S(1)} %add_convert_fusion.5), channel_id=1, source_target_pairs={{0,4},{4,8},{8,12},{12,14},{14,10},{10,6},{6,2},{2,0},{5,1},{9,5},... | collective-permute-start | bytes 688136 | tf_op jit(solution)/shard_map/ppermute | solution.py:150
  46.7 0.8 %collective-permute-done.17 = bf16[32,3584]{1,0:T(8,128)(2,1)S(1)} collective-permute-done((bf16[32,3584]{1,0:T(8,128)(2,1)S(1)}, bf16[32,3584]{1,0:T(8,128)(2,1)S(1)}, u32[]{:S(2)}, u32[]{:S(2)}) %collective-permute-start.17) | collective-permute-done | bytes 229408 | tf_op jit(solution)/shard_map/ppermute | solution.py:150
  47.4 0.1 add_convert_fusion.4
  47.5 1.6 %collective-permute-start.20 = (bf16[32,3584]{1,0:T(8,128)(2,1)S(1)}, bf16[32,3584]{1,0:T(8,128)(2,1)S(1)}, u32[]{:S(2)}, u32[]{:S(2)}) collective-permute-start(bf16[32,3584]{1,0:T(8,128)(2,1)S(1)} %add_convert_fusion.4), channel_id=1, source_target_pairs={{0,4},{4,8},{8,12},{12,14},{14,10},{10,6},{6,2},{2,0},{5,1},{9,5},... | collective-permute-start | bytes 688136 | tf_op jit(solution)/shard_map/ppermute | solution.py:150
  49.1 2.0 %collective-permute-done.21 = bf16[32,3584]{1,0:T(8,128)(2,1)S(1)} collective-permute-done((bf16[32,3584]{1,0:T(8,128)(2,1)S(1)}, bf16[32,3584]{1,0:T(8,128)(2,1)S(1)}, u32[]{:S(2)}, u32[]{:S(2)}) %collective-permute-start.21) | collective-permute-done | bytes 229408 | tf_op jit(solution)/shard_map/ppermute | solution.py:150
  51.2 0.1 add_convert_fusion.3
  51.2 1.6 %collective-permute-start.24 = (bf16[32,3584]{1,0:T(8,128)(2,1)S(1)}, bf16[32,3584]{1,0:T(8,128)(2,1)S(1)}, u32[]{:S(2)}, u32[]{:S(2)}) collective-permute-start(bf16[32,3584]{1,0:T(8,128)(2,1)S(1)} %add_convert_fusion.3), channel_id=1, source_target_pairs={{0,4},{4,8},{8,12},{12,14},{14,10},{10,6},{6,2},{2,0},{5,1},{9,5},... | collective-permute-start | bytes 688136 | tf_op jit(solution)/shard_map/ppermute | solution.py:150
  52.8 0.8 %collective-permute-done.20 = bf16[32,3584]{1,0:T(8,128)(2,1)S(1)} collective-permute-done((bf16[32,3584]{1,0:T(8,128)(2,1)S(1)}, bf16[32,3584]{1,0:T(8,128)(2,1)S(1)}, u32[]{:S(2)}, u32[]{:S(2)}) %collective-permute-start.20) | collective-permute-done | bytes 229408 | tf_op jit(solution)/shard_map/ppermute | solution.py:150
  53.6 0.1 add_convert_fusion.2
  53.7 1.6 %collective-permute-start.22 = (bf16[32,3584]{1,0:T(8,128)(2,1)S(1)}, bf16[32,3584]{1,0:T(8,128)(2,1)S(1)}, u32[]{:S(2)}, u32[]{:S(2)}) collective-permute-start(bf16[32,3584]{1,0:T(8,128)(2,1)S(1)} %add_convert_fusion.2), channel_id=1, source_target_pairs={{0,4},{4,8},{8,12},{12,14},{14,10},{10,6},{6,2},{2,0},{5,1},{9,5},... | collective-permute-start | bytes 688136 | tf_op jit(solution)/shard_map/ppermute | solution.py:150
  55.3 2.0 %collective-permute-done.24 = bf16[32,3584]{1,0:T(8,128)(2,1)S(1)} collective-permute-done((bf16[32,3584]{1,0:T(8,128)(2,1)S(1)}, bf16[32,3584]{1,0:T(8,128)(2,1)S(1)}, u32[]{:S(2)}, u32[]{:S(2)}) %collective-permute-start.24) | collective-permute-done | bytes 229408 | tf_op jit(solution)/shard_map/ppermute | solution.py:150
  57.3 0.1 add_convert_fusion.1
  57.4 1.6 %collective-permute-start.25 = (bf16[32,3584]{1,0:T(8,128)(2,1)S(1)}, bf16[32,3584]{1,0:T(8,128)(2,1)S(1)}, u32[]{:S(2)}, u32[]{:S(2)}) collective-permute-start(bf16[32,3584]{1,0:T(8,128)(2,1)S(1)} %add_convert_fusion.1), channel_id=1, source_target_pairs={{0,4},{4,8},{8,12},{12,14},{14,10},{10,6},{6,2},{2,0},{5,1},{9,5},... | collective-permute-start | bytes 688136 | tf_op jit(solution)/shard_map/ppermute | solution.py:150
  59.0 0.8 %collective-permute-done.22 = bf16[32,3584]{1,0:T(8,128)(2,1)S(1)} collective-permute-done((bf16[32,3584]{1,0:T(8,128)(2,1)S(1)}, bf16[32,3584]{1,0:T(8,128)(2,1)S(1)}, u32[]{:S(2)}, u32[]{:S(2)}) %collective-permute-start.22) | collective-permute-done | bytes 229408 | tf_op jit(solution)/shard_map/ppermute | solution.py:150
  59.8 3.7 %collective-permute-done.25 = bf16[32,3584]{1,0:T(8,128)(2,1)S(1)} collective-permute-done((bf16[32,3584]{1,0:T(8,128)(2,1)S(1)}, bf16[32,3584]{1,0:T(8,128)(2,1)S(1)}, u32[]{:S(2)}, u32[]{:S(2)}) %collective-permute-start.25) | collective-permute-done | bytes 229408 | tf_op jit(solution)/shard_map/ppermute | solution.py:150
  63.4 0.1 convert_add_fusion
  63.5 0.7 %add_convert_fusion = bf16[32,3584]{1,0:T(8,128)(2,1)} fusion(f32[32,3584]{1,0:T(8,128)S(1)} %convert_add_fusion, bf16[32,3584]{1,0:T(8,128)(2,1)S(1)} %collective-permute-done.23), kind=kLoop, calls=%fused_computation | loop fusion | flops 344064 | bytes 917504 | tf_op jit(solution)/shard_map/convert_element_type | solution.py:219
  (31 shorter events, 0.1 us)
Async XLA Ops:
  0.0 22.7 %slice-start = ((s8[7340032]{0:T(1024)(128)(4,1)}), s8[4194304]{0:T(1024)(128)(4,1)S(1)}, s32[]{:S(2)}) async-start(s8[7340032]{0:T(1024)(128)(4,1)} %bitcast.2), calls=%async_computation | async-start | bytes 8388608
  0.0 22.7 %slice-start.2 = ((s8[7340032]{0:T(1024)(128)(4,1)}), s8[4194304]{0:T(1024)(128)(4,1)S(1)}, s32[]{:S(2)}) async-start(s8[7340032]{0:T(1024)(128)(4,1)} %bitcast.4), calls=%async_computation.2 | async-start | bytes 8388608
  0.0 22.7 %slice-start.4 = ((s8[7340032]{0:T(1024)(128)(4,1)}), s8[4194304]{0:T(1024)(128)(4,1)S(1)}, s32[]{:S(2)}) async-start(s8[7340032]{0:T(1024)(128)(4,1)} %bitcast.6), calls=%async_computation.4 | async-start | bytes 8388608
  0.0 22.7 %slice-start.1 = ((s8[7340032]{0:T(1024)(128)(4,1)}), s8[3145728]{0:T(1024)(128)(4,1)S(1)}, s32[]{:S(2)}) async-start(s8[7340032]{0:T(1024)(128)(4,1)} %bitcast.2), calls=%async_computation.1 | async-start | bytes 6291456
  0.0 22.7 %slice-start.3 = ((s8[7340032]{0:T(1024)(128)(4,1)}), s8[3145728]{0:T(1024)(128)(4,1)S(1)}, s32[]{:S(2)}) async-start(s8[7340032]{0:T(1024)(128)(4,1)} %bitcast.4), calls=%async_computation.3 | async-start | bytes 6291456
  0.0 22.7 %slice-start.5 = ((s8[7340032]{0:T(1024)(128)(4,1)}), s8[3145728]{0:T(1024)(128)(4,1)S(1)}, s32[]{:S(2)}) async-start(s8[7340032]{0:T(1024)(128)(4,1)} %bitcast.6), calls=%async_computation.5 | async-start | bytes 6291456
  1.2 3.2 %collective-permute-start.2 = (bf16[32,3712]{1,0:T(8,128)(2,1)S(1)}, bf16[32,3712]{1,0:T(8,128)(2,1)S(1)}, u32[]{:S(2)}, u32[]{:S(2)}) collective-permute-start(bf16[32,3712]{1,0:T(8,128)(2,1)S(1)} %shard_map.64.refs_2_), channel_id=1, source_target_pairs={{0,1},{1,0},{2,3},{3,2},{4,5},{5,4},{6,7},{7,6},{8,9},{9,8},{10,11... | collective-permute-start | bytes 712712 | tf_op jit(solution)/shard_map/ppermute | solution.py:151
  1.7 6.7 %collective-permute-start = (bf16[32,3712]{1,0:T(8,128)(2,1)S(1)}, bf16[32,3712]{1,0:T(8,128)(2,1)S(1)}, u32[]{:S(2)}, u32[]{:S(2)}) collective-permute-start(bf16[32,3712]{1,0:T(8,128)(2,1)S(1)} %shard_map.64.refs_2_), channel_id=1, source_target_pairs={{0,4},{4,8},{8,12},{12,14},{14,10},{10,6},{6,2},{2,0},{5,1},{9,5},... | collective-permute-start | bytes 712712 | tf_op jit(solution)/shard_map/ppermute | solution.py:150
  4.4 6.6 %collective-permute-start.3 = (bf16[32,3712]{1,0:T(8,128)(2,1)S(1)}, bf16[32,3712]{1,0:T(8,128)(2,1)S(1)}, u32[]{:S(2)}, u32[]{:S(2)}) collective-permute-start(bf16[32,3712]{1,0:T(8,128)(2,1)S(1)} %collective-permute-done.2.refs_7_), channel_id=1, source_target_pairs={{0,4},{4,8},{8,12},{12,14},{14,10},{10,6},{6,2},{2,0},{5,1},{9,5},... | collective-permute-start | bytes 712712 | tf_op jit(solution)/shard_map/ppermute | solution.py:150
  8.4 6.1 %collective-permute-start.5 = (bf16[32,3712]{1,0:T(8,128)(2,1)S(1)}, bf16[32,3712]{1,0:T(8,128)(2,1)S(1)}, u32[]{:S(2)}, u32[]{:S(2)}) collective-permute-start(bf16[32,3712]{1,0:T(8,128)(2,1)S(1)} %collective-permute-done.refs_5_), channel_id=1, source_target_pairs={{0,4},{4,8},{8,12},{12,14},{14,10},{10,6},{6,2},{2,0},{5,1},{9,5},... | collective-permute-start | bytes 712712 | tf_op jit(solution)/shard_map/ppermute | solution.py:150
  10.9 6.2 %collective-permute-start.6 = (bf16[32,3712]{1,0:T(8,128)(2,1)S(1)}, bf16[32,3712]{1,0:T(8,128)(2,1)S(1)}, u32[]{:S(2)}, u32[]{:S(2)}) collective-permute-start(bf16[32,3712]{1,0:T(8,128)(2,1)S(1)} %collective-permute-done.3.refs_6_), channel_id=1, source_target_pairs={{0,4},{4,8},{8,12},{12,14},{14,10},{10,6},{6,2},{2,0},{5,1},{9,5},... | collective-permute-start | bytes 712712 | tf_op jit(solution)/shard_map/ppermute | solution.py:150
  13.0 4.1 %collective-permute-start.1 = (bf16[32,3712]{1,0:T(8,128)(2,1)S(1)}, bf16[32,3712]{1,0:T(8,128)(2,1)S(1)}, u32[]{:S(2)}, u32[]{:S(2)}) collective-permute-start(bf16[32,3712]{1,0:T(8,128)(2,1)S(1)} %collective-permute-done.refs_5_), channel_id=1, source_target_pairs={{0,1},{1,0},{2,3},{3,2},{4,5},{5,4},{6,7},{7,6},{8,9},{9,8},{10,11... | collective-permute-start | bytes 712712 | tf_op jit(solution)/shard_map/ppermute | solution.py:151
  14.5 6.1 %collective-permute-start.7 = (bf16[32,3712]{1,0:T(8,128)(2,1)S(1)}, bf16[32,3712]{1,0:T(8,128)(2,1)S(1)}, u32[]{:S(2)}, u32[]{:S(2)}) collective-permute-start(bf16[32,3712]{1,0:T(8,128)(2,1)S(1)} %collective-permute-done.5.refs_3_), channel_id=1, source_target_pairs={{0,4},{4,8},{8,12},{12,14},{14,10},{10,6},{6,2},{2,0},{5,1},{9,5},... | collective-permute-start | bytes 712712 | tf_op jit(solution)/shard_map/ppermute | solution.py:150
  16.6 4.0 %collective-permute-start.4 = (bf16[32,3712]{1,0:T(8,128)(2,1)S(1)}, bf16[32,3712]{1,0:T(8,128)(2,1)S(1)}, u32[]{:S(2)}, u32[]{:S(2)}) collective-permute-start(bf16[32,3712]{1,0:T(8,128)(2,1)S(1)} %collective-permute-done.3.refs_6_), channel_id=1, source_target_pairs={{0,1},{1,0},{2,3},{3,2},{4,5},{5,4},{6,7},{7,6},{8,9},{9,8},{10,11... | collective-permute-start | bytes 712712 | tf_op jit(solution)/shard_map/ppermute | solution.py:151
  16.6 12.2 %collective-permute-start.11 = (bf16[32,3712]{1,0:T(8,128)(2,1)S(1)}, bf16[32,3712]{1,0:T(8,128)(2,1)S(1)}, u32[]{:S(2)}, u32[]{:S(2)}) collective-permute-start(bf16[32,3712]{1,0:T(8,128)(2,1)S(1)} %collective-permute-done.5.refs_3_), channel_id=1, source_target_pairs={{0,1},{1,0},{2,3},{3,2},{4,5},{5,4},{6,7},{7,6},{8,9},{9,8},{10,11... | collective-permute-start | bytes 712712 | tf_op jit(solution)/shard_map/ppermute | solution.py:151
  17.1 11.7 %collective-permute-start.12 = (bf16[32,3712]{1,0:T(8,128)(2,1)S(1)}, bf16[32,3712]{1,0:T(8,128)(2,1)S(1)}, u32[]{:S(2)}, u32[]{:S(2)}) collective-permute-start(bf16[32,3712]{1,0:T(8,128)(2,1)S(1)} %collective-permute-done.6.refs_4_), channel_id=1, source_target_pairs={{0,1},{1,0},{2,3},{3,2},{4,5},{5,4},{6,7},{7,6},{8,9},{9,8},{10,11... | collective-permute-start | bytes 712712 | tf_op jit(solution)/shard_map/ppermute | solution.py:151
  17.1 11.7 %collective-permute-start.9 = (bf16[32,3712]{1,0:T(8,128)(2,1)S(1)}, bf16[32,3712]{1,0:T(8,128)(2,1)S(1)}, u32[]{:S(2)}, u32[]{:S(2)}) collective-permute-start(bf16[32,3712]{1,0:T(8,128)(2,1)S(1)} %collective-permute-done.6.refs_4_), channel_id=1, source_target_pairs={{0,4},{4,8},{8,12},{12,14},{14,10},{10,6},{6,2},{2,0},{5,1},{9,5},... | collective-permute-start | bytes 712712 | tf_op jit(solution)/shard_map/ppermute | solution.py:150
  20.6 8.2 %collective-permute-start.10 = (bf16[32,3712]{1,0:T(8,128)(2,1)S(1)}, bf16[32,3712]{1,0:T(8,128)(2,1)S(1)}, u32[]{:S(2)}, u32[]{:S(2)}) collective-permute-start(bf16[32,3712]{1,0:T(8,128)(2,1)S(1)} %collective-permute-done.7.refs_6_), channel_id=1, source_target_pairs={{0,1},{1,0},{2,3},{3,2},{4,5},{5,4},{6,7},{7,6},{8,9},{9,8},{10,11... | collective-permute-start | bytes 712712 | tf_op jit(solution)/shard_map/ppermute | solution.py:151
  20.6 8.2 %collective-permute-start.8 = (bf16[32,3712]{1,0:T(8,128)(2,1)S(1)}, bf16[32,3712]{1,0:T(8,128)(2,1)S(1)}, u32[]{:S(2)}, u32[]{:S(2)}) collective-permute-start(bf16[32,3712]{1,0:T(8,128)(2,1)S(1)} %collective-permute-done.7.refs_6_), channel_id=1, source_target_pairs={{0,4},{4,8},{8,12},{12,14},{14,10},{10,6},{6,2},{2,0},{5,1},{9,5},... | collective-permute-start | bytes 712712 | tf_op jit(solution)/shard_map/ppermute | solution.py:150
  28.9 1.6 %collective-permute-start.13 = (bf16[32,3712]{1,0:T(8,128)(2,1)S(1)}, bf16[32,3712]{1,0:T(8,128)(2,1)S(1)}, u32[]{:S(2)}, u32[]{:S(2)}) collective-permute-start(bf16[32,3712]{1,0:T(8,128)(2,1)S(1)} %collective-permute-done.8.refs_0_), channel_id=1, source_target_pairs={{0,1},{1,0},{2,3},{3,2},{4,5},{5,4},{6,7},{7,6},{8,9},{9,8},{10,11... | collective-permute-start | bytes 712712 | tf_op jit(solution)/shard_map/ppermute | solution.py:151
  29.1 1.7 %collective-permute-start.14 = (bf16[32,3712]{1,0:T(8,128)(2,1)S(1)}, bf16[32,3712]{1,0:T(8,128)(2,1)S(1)}, u32[]{:S(2)}, u32[]{:S(2)}) collective-permute-start(bf16[32,3712]{1,0:T(8,128)(2,1)S(1)} %collective-permute-done.9.refs_7_), channel_id=1, source_target_pairs={{0,1},{1,0},{2,3},{3,2},{4,5},{5,4},{6,7},{7,6},{8,9},{9,8},{10,11... | collective-permute-start | bytes 712712 | tf_op jit(solution)/shard_map/ppermute | solution.py:151
  30.8 6.2 %collective-permute-start.15 = (bf16[160,3584]{1,0:T(8,128)(2,1)S(1)}, bf16[160,3584]{1,0:T(8,128)(2,1)S(1)}, u32[]{:S(2)}, u32[]{:S(2)}) collective-permute-start(bf16[160,3584]{1,0:T(8,128)(2,1)S(1)} %get-tuple-element.54), channel_id=1, source_target_pairs={{0,1},{1,0},{2,3},{3,2},{4,5},{5,4},{6,7},{7,6},{8,9},{9,8},{10,11... | collective-permute-start | bytes 3440648 | tf_op jit(solution)/shard_map/ppermute | solution.py:151
  37.0 1.9 %collective-permute-start.16 = (bf16[64,3584]{1,0:T(8,128)(2,1)S(1)}, bf16[64,3584]{1,0:T(8,128)(2,1)S(1)}, u32[]{:S(2)}, u32[]{:S(2)}) collective-permute-start(bf16[64,3584]{1,0:T(8,128)(2,1)S(1)} %get-tuple-element.57), channel_id=1, source_target_pairs={{0,1},{1,0},{2,3},{3,2},{4,5},{5,4},{6,7},{7,6},{8,9},{9,8},{10,11... | collective-permute-start | bytes 1376264 | tf_op jit(solution)/shard_map/ppermute | solution.py:151
  37.4 4.8 %collective-permute-start.18 = (bf16[32,3584]{1,0:T(8,128)(2,1)S(1)}, bf16[32,3584]{1,0:T(8,128)(2,1)S(1)}, u32[]{:S(2)}, u32[]{:S(2)}) collective-permute-start(bf16[32,3584]{1,0:T(8,128)(2,1)S(1)} %get-tuple-element.60), channel_id=1, source_target_pairs={{0,1},{1,0},{2,3},{3,2},{4,5},{5,4},{6,7},{7,6},{8,9},{9,8},{10,11... | collective-permute-start | bytes 688136 | tf_op jit(solution)/shard_map/ppermute | solution.py:151
  38.9 6.1 %collective-permute-start.19 = (bf16[32,3584]{1,0:T(8,128)(2,1)S(1)}, bf16[32,3584]{1,0:T(8,128)(2,1)S(1)}, u32[]{:S(2)}, u32[]{:S(2)}) collective-permute-start(bf16[32,3584]{1,0:T(8,128)(2,1)S(1)} %add_convert_fusion.7), channel_id=1, source_target_pairs={{0,4},{4,8},{8,12},{12,14},{14,10},{10,6},{6,2},{2,0},{5,1},{9,5},... | collective-permute-start | bytes 688136 | tf_op jit(solution)/shard_map/ppermute | solution.py:150
  40.6 6.9 %collective-permute-start.17 = (bf16[32,3584]{1,0:T(8,128)(2,1)S(1)}, bf16[32,3584]{1,0:T(8,128)(2,1)S(1)}, u32[]{:S(2)}, u32[]{:S(2)}) collective-permute-start(bf16[32,3584]{1,0:T(8,128)(2,1)S(1)} %add_convert_fusion.6), channel_id=1, source_target_pairs={{0,4},{4,8},{8,12},{12,14},{14,10},{10,6},{6,2},{2,0},{5,1},{9,5},... | collective-permute-start | bytes 688136 | tf_op jit(solution)/shard_map/ppermute | solution.py:150
  45.1 6.1 %collective-permute-start.21 = (bf16[32,3584]{1,0:T(8,128)(2,1)S(1)}, bf16[32,3584]{1,0:T(8,128)(2,1)S(1)}, u32[]{:S(2)}, u32[]{:S(2)}) collective-permute-start(bf16[32,3584]{1,0:T(8,128)(2,1)S(1)} %add_convert_fusion.5), channel_id=1, source_target_pairs={{0,4},{4,8},{8,12},{12,14},{14,10},{10,6},{6,2},{2,0},{5,1},{9,5},... | collective-permute-start | bytes 688136 | tf_op jit(solution)/shard_map/ppermute | solution.py:150
  47.5 6.1 %collective-permute-start.20 = (bf16[32,3584]{1,0:T(8,128)(2,1)S(1)}, bf16[32,3584]{1,0:T(8,128)(2,1)S(1)}, u32[]{:S(2)}, u32[]{:S(2)}) collective-permute-start(bf16[32,3584]{1,0:T(8,128)(2,1)S(1)} %add_convert_fusion.4), channel_id=1, source_target_pairs={{0,4},{4,8},{8,12},{12,14},{14,10},{10,6},{6,2},{2,0},{5,1},{9,5},... | collective-permute-start | bytes 688136 | tf_op jit(solution)/shard_map/ppermute | solution.py:150
  51.2 6.1 %collective-permute-start.24 = (bf16[32,3584]{1,0:T(8,128)(2,1)S(1)}, bf16[32,3584]{1,0:T(8,128)(2,1)S(1)}, u32[]{:S(2)}, u32[]{:S(2)}) collective-permute-start(bf16[32,3584]{1,0:T(8,128)(2,1)S(1)} %add_convert_fusion.3), channel_id=1, source_target_pairs={{0,4},{4,8},{8,12},{12,14},{14,10},{10,6},{6,2},{2,0},{5,1},{9,5},... | collective-permute-start | bytes 688136 | tf_op jit(solution)/shard_map/ppermute | solution.py:150
  53.7 6.1 %collective-permute-start.22 = (bf16[32,3584]{1,0:T(8,128)(2,1)S(1)}, bf16[32,3584]{1,0:T(8,128)(2,1)S(1)}, u32[]{:S(2)}, u32[]{:S(2)}) collective-permute-start(bf16[32,3584]{1,0:T(8,128)(2,1)S(1)} %add_convert_fusion.2), channel_id=1, source_target_pairs={{0,4},{4,8},{8,12},{12,14},{14,10},{10,6},{6,2},{2,0},{5,1},{9,5},... | collective-permute-start | bytes 688136 | tf_op jit(solution)/shard_map/ppermute | solution.py:150
  57.4 6.1 %collective-permute-start.25 = (bf16[32,3584]{1,0:T(8,128)(2,1)S(1)}, bf16[32,3584]{1,0:T(8,128)(2,1)S(1)}, u32[]{:S(2)}, u32[]{:S(2)}) collective-permute-start(bf16[32,3584]{1,0:T(8,128)(2,1)S(1)} %add_convert_fusion.1), channel_id=1, source_target_pairs={{0,4},{4,8},{8,12},{12,14},{14,10},{10,6},{6,2},{2,0},{5,1},{9,5},... | collective-permute-start | bytes 688136 | tf_op jit(solution)/shard_map/ppermute | solution.py:150
  59.8 3.8 %collective-permute-start.23 = (bf16[32,3584]{1,0:T(8,128)(2,1)S(1)}, bf16[32,3584]{1,0:T(8,128)(2,1)S(1)}, u32[]{:S(2)}, u32[]{:S(2)}) collective-permute-start(bf16[32,3584]{1,0:T(8,128)(2,1)S(1)} %collective-permute-done.22), channel_id=1, source_target_pairs={{0,1},{1,0},{2,3},{3,2},{4,5},{5,4},{6,7},{7,6},{8,9},{9,8},{10,11... | collective-permute-start | bytes 688136 | tf_op jit(solution)/shard_map/ppermute | solution.py:151

commit v16 on v15

--- a/solution.py
+++ b/solution.py
@@ -113,31 +113,51 @@
     return (256 if ff % 256 == 0 else ff), next(t for t in (512, 256, 128, width) if width % t == 0)
 
 
-def expert_kernel(count, experts, tile_ff, tile_d, *refs):
-    blocks, (gate_ref, up_ref, down_ref, *out_refs) = refs[:count], refs[count:]
-    out_refs, (x_ref, w_ref, h_ref) = out_refs[:-3], out_refs[-3:]
+def hidden_kernel(count, tile, *refs):
+    blocks, (gate_ref, up_ref, h_ref, x_ref) = refs[:count], refs[count:]
     gather_rows(blocks, x_ref)
-    gather_weights(experts, blocks, x_ref.shape[1], w_ref)
-    first_half(x_ref, gate_ref, up_ref, h_ref, tile_ff, 0, h_ref.shape[1])
-    second_half(h_ref, down_ref, w_ref, out_refs, tile_d, 0, x_ref.shape[1])
-
-
-def expert(blocks, pieces, experts, w_gate, w_up, w_down):
+    first_half(x_ref, gate_ref, up_ref, h_ref, tile, 0, h_ref.shape[1])
+
+
+def hidden(blocks, w_gate, w_up):
     count, rows = len(blocks), blocks[0].shape[0]
     _, width, ff = w_gate.shape
-    total = count * rows
     here = pl.BlockSpec(memory_space=pltpu.VMEM)
     return pl.pallas_call(
-        functools.partial(expert_kernel, count, experts, *tiles(width, ff)),
-        out_shape=[pltpu.VMEM((n * rows, width), kind) for n, kind in pieces],
-        in_specs=[here] * (count + 3),
-        out_specs=[here] * len(pieces),
-        scratch_shapes=[pltpu.VMEM((total, width), BF16), pltpu.VMEM((total, 1), F32), pltpu.VMEM((total, ff), BF16)],
+        functools.partial(hidden_kernel, count, tiles(width, ff)[0]),
+        out_shape=pltpu.VMEM((count * rows, ff), BF16),
+        in_specs=[here] * (count + 2),
+        out_specs=here,
+        scratch_shapes=[pltpu.VMEM((count * rows, width), BF16)],
         compiler_params=pltpu.CompilerParams(vmem_limit_bytes=SCRATCH),
         cost_estimate=pl.CostEstimate(
-            flops=6 * max(total, 256) * width * ff, bytes_accessed=0, transcendentals=total * ff
+            flops=4 * max(count * rows, 256) * width * ff, bytes_accessed=0, transcendentals=count * rows * ff
         ),
-    )(*blocks, w_gate, w_up, w_down)
+    )(*blocks, w_gate, w_up)
+
+
+def output_kernel(count, experts, tile, begin, *refs):
+    blocks, (h_ref, down_ref, *out_refs), w_ref = refs[:count], refs[count:-1], refs[-1]
+    width = out_refs[0].shape[1]
+    gather_weights(experts, blocks, width, w_ref)
+    second_half(h_ref.at[begin : begin + w_ref.shape[0]], down_ref, w_ref, out_refs, tile, 0, width)
+
+
+def output(blocks, h, first, pieces, experts, w_down):
+    count, rows = len(blocks), blocks[0].shape[0]
+    _, ff, width = w_down.shape
+    here = pl.BlockSpec(memory_space=pltpu.VMEM)
+    return pl.pallas_call(
+        functools.partial(output_kernel, count, experts, tiles(width, ff)[1], first * rows),
+        out_shape=[pltpu.VMEM((n * rows, width), kind) for n, kind in pieces],
+        in_specs=[here] * (count + 2),
+        out_specs=[here] * len(pieces),
+        scratch_shapes=[pltpu.VMEM((count * rows, 1), F32)],
+        compiler_params=pltpu.CompilerParams(vmem_limit_bytes=SCRATCH),
+        cost_estimate=pl.CostEstimate(
+            flops=2 * max(count * rows, 256) * width * ff, bytes_accessed=0, transcendentals=0
+        ),
+    )(*blocks, h, w_down)
 
 
 def local(order, tokens, routes, gates, w_gate, w_up, w_down):
@@ -170,30 +190,31 @@
     end = len(kept) - 1
     mine, theirs = {}, {}
 
-    def compute(keep, give, sizes):
-        sizes = [n for n in sizes if n]
-        blocks = [kept[j] for j in keep] + [given[j] for j in give]
-        out, *pieces = expert(blocks, [(len(keep), F32)] + [(n, BF16) for n in sizes], experts, w_gate, w_up, w_down)
-        return out, pieces
-
     def note(keep, out, give, pieces):
         mine.update({j: (out, at) for at, j in enumerate(keep)})
         theirs.update(zip(give, [(piece, at) for piece in pieces for at in range(piece.shape[0] // rows)]))
 
     keep, give = [end - 2, end - 1, end], list(range(end - 4, end + 1))
-    near, near_given = compute(keep, give, (5,))
+    blocks = [kept[j] for j in keep] + [given[j] for j in give]
+    h = hidden(blocks, w_gate, w_up)
     others = kept[1:2] + kept[3 : end - 2]
-    near, near_given, kept[0], given[2], others = together((near, near_given, kept[0], given[2], others))
+    h, kept[0], given[2], others = together((h, kept[0], given[2], others))
     kept[1], kept[3 : end - 2] = others[0], others[1:]
     given[0], kept[2] = sibling(kept[0]), sibling(given[2])
+    near, near_given = output(blocks, h, 0, [(3, F32), (5, BF16)], experts, w_down)
     given[0], kept[2], near_given = together((given[0], kept[2], near_given))
-    near_sent = [sibling(p) for p in near_given]
+    near_sent = sibling(near_given)
 
     keep_last, give_last = list(range(end - 2)), list(range(end - 4))
-    out, pieces = compute(keep_last, give_last, (2, len(give_last) - 2))
-    out, pieces, near_sent = together((out, pieces, near_sent))
-    note(keep, near, give, near_sent)
-    note(keep_last, out, give_last, [sibling(p) for p in pieces])
+    kept_blocks, given_blocks = [kept[j] for j in keep_last], [given[j] for j in give_last]
+    h = hidden(given_blocks + kept_blocks, w_gate, w_up)
+    pieces = output(given_blocks, h, 0, [(2, BF16), (len(give_last) - 2, BF16)], experts, w_down)
+    h, pieces = together((h, pieces))
+    sent = [sibling(p) for p in pieces]
+    (out,) = output(kept_blocks, h, len(give_last), [(len(keep_last), F32)], experts, w_down)
+    out, near_sent = together((out, near_sent))
+    note(keep, near, give, [near_sent])
+    note(keep_last, out, give_last, sent)
 
     def add(j, *arrived):
         nonlocal last

time: 64.4 us -> 62.8 us (0.975)
  waiting for transfers between devices: 21.3 us -> 17.7 us
  starting transfers between devices: 28.2 us -> 29.3 us
  Pallas kernels: 13.2 us -> 14.2 us
    ppermute x12, waiting for transfers between devices: 2.66 us -> 0.03 us  [local(): sibling = lambda a: lax.ppermute(a, 'node', swap)]
    pallas_call x2 -> x5, Pallas kernels: 12.1 us -> 13.1 us  [the longest x2 8.26 us: hidden(): pl.pallas_call(functools.partial(hidden_kernel, count, tiles(width, ff)[0...]
    ppermute x14, waiting for transfers between devices: 18.7 us -> 17.7 us  [local(): send = lambda a: lax.ppermute(a, 'node', spin)]
    ppermute x14, starting transfers between devices: 25.9 us -> 26.8 us  [local(): send = lambda a: lax.ppermute(a, 'node', spin)]
  transfers between devices with their start and end apart: 26 -> 26, of which waited for: 14 -> 11; matrix products, arithmetic and copies ran while one was open for 1% -> 1% of each run, Pallas kernels for 19% -> 21%
where the time goes in v16:
time: 62.8 us; the launch traced here: 62.7 us
  starting transfers between devices  29.3 us (47%)
  waiting for transfers between devices  17.7 us (28%)
  Pallas kernels  14.2 us (23%)
  other arithmetic  1.29 us (2%)
    ppermute x14, starting transfers between devices, local(): send = lambda a: lax.ppermute(a, 'node', spin)  26.8 us
    ppermute x14, waiting for transfers between devices, local(): send = lambda a: lax.ppermute(a, 'node', spin)  17.7 us
    pallas_call x2, Pallas kernels, hidden(): pl.pallas_call(functools.partial(hidden_kernel, count, tiles(width, ff)[0...  8.26 us
    pallas_call x3, Pallas kernels, output(): pl.pallas_call(functools.partial(output_kernel, count, experts, tiles(wid...  4.81 us
    ppermute x12, starting transfers between devices, local(): sibling = lambda a: lax.ppermute(a, 'node', swap)  2.44 us
  transfers between devices with their start and end apart: 26, of which 11 were waited for; matrix products, arithmetic and copies ran while one was open for 1% of the time, Pallas kernels for 21%

profile of v16, /device:TPU:0, one launch (start us, length us, event | category | flops | bytes accessed | tf_op | source)
XLA Modules:
  0.0 62.7 jit_solution(6006902181734162637)
XLA Ops:
  0.0 1.1 %shard_map.64.refs_2_ = bf16[32,3712]{1,0:T(8,128)(2,1)S(1)} custom-call(bf16[32,3584]{1,0:T(8,128)(2,1)} %tok_hbm.1, s32[8,32]{1,0:T(8,128)} %bitcast.6, f32[8,32]{1,0:T(8,128)} %bitcast.7), custom_call_target="tpu_custom_call" | custom-call | flops 10737418240 | tf_op jit(solution)/shard_map/pallas_call | solution.py:59
  1.2 0.5 collective-permute-start.2
  1.7 2.6 %collective-permute-start = (bf16[32,3712]{1,0:T(8,128)(2,1)S(1)}, bf16[32,3712]{1,0:T(8,128)(2,1)S(1)}, u32[]{:S(2)}, u32[]{:S(2)}) collective-permute-start(bf16[32,3712]{1,0:T(8,128)(2,1)S(1)} %shard_map.64.refs_2_), channel_id=1, source_target_pairs={{0,4},{4,8},{8,12},{12,14},{14,10},{10,6},{6,2},{2,0},{5,1},{9,5},... | collective-permute-start | bytes 712712 | tf_op jit(solution)/shard_map/ppermute | solution.py:170
  4.3 1.6 %collective-permute-start.3 = (bf16[32,3712]{1,0:T(8,128)(2,1)S(1)}, bf16[32,3712]{1,0:T(8,128)(2,1)S(1)}, u32[]{:S(2)}, u32[]{:S(2)}) collective-permute-start(bf16[32,3712]{1,0:T(8,128)(2,1)S(1)} %collective-permute-done.2.refs_7_), channel_id=1, source_target_pairs={{0,4},{4,8},{8,12},{12,14},{14,10},{10,6},{6,2},{2,0},{5,1},{9,5},... | collective-permute-start | bytes 712712 | tf_op jit(solution)/shard_map/ppermute | solution.py:170
  5.9 2.5 %collective-permute-done.refs_5_ = bf16[32,3712]{1,0:T(8,128)(2,1)S(1)} collective-permute-done((bf16[32,3712]{1,0:T(8,128)(2,1)S(1)}, bf16[32,3712]{1,0:T(8,128)(2,1)S(1)}, u32[]{:S(2)}, u32[]{:S(2)}) %collective-permute-start) | collective-permute-done | bytes 237600 | tf_op jit(solution)/shard_map/ppermute | solution.py:170
  8.4 2.1 %collective-permute-start.5 = (bf16[32,3712]{1,0:T(8,128)(2,1)S(1)}, bf16[32,3712]{1,0:T(8,128)(2,1)S(1)}, u32[]{:S(2)}, u32[]{:S(2)}) collective-permute-start(bf16[32,3712]{1,0:T(8,128)(2,1)S(1)} %collective-permute-done.refs_5_), channel_id=1, source_target_pairs={{0,4},{4,8},{8,12},{12,14},{14,10},{10,6},{6,2},{2,0},{5,1},{9,5},... | collective-permute-start | bytes 712712 | tf_op jit(solution)/shard_map/ppermute | solution.py:170
  10.4 0.5 collective-permute-done.3.refs_6_
  10.9 2.1 %collective-permute-start.6 = (bf16[32,3712]{1,0:T(8,128)(2,1)S(1)}, bf16[32,3712]{1,0:T(8,128)(2,1)S(1)}, u32[]{:S(2)}, u32[]{:S(2)}) collective-permute-start(bf16[32,3712]{1,0:T(8,128)(2,1)S(1)} %collective-permute-done.3.refs_6_), channel_id=1, source_target_pairs={{0,4},{4,8},{8,12},{12,14},{14,10},{10,6},{6,2},{2,0},{5,1},{9,5},... | collective-permute-start | bytes 712712 | tf_op jit(solution)/shard_map/ppermute | solution.py:170
  13.0 1.5 %collective-permute-done.5.refs_3_ = bf16[32,3712]{1,0:T(8,128)(2,1)S(1)} collective-permute-done((bf16[32,3712]{1,0:T(8,128)(2,1)S(1)}, bf16[32,3712]{1,0:T(8,128)(2,1)S(1)}, u32[]{:S(2)}, u32[]{:S(2)}) %collective-permute-start.5) | collective-permute-done | bytes 237600 | tf_op jit(solution)/shard_map/ppermute | solution.py:170
  14.5 2.1 %collective-permute-start.7 = (bf16[32,3712]{1,0:T(8,128)(2,1)S(1)}, bf16[32,3712]{1,0:T(8,128)(2,1)S(1)}, u32[]{:S(2)}, u32[]{:S(2)}) collective-permute-start(bf16[32,3712]{1,0:T(8,128)(2,1)S(1)} %collective-permute-done.5.refs_3_), channel_id=1, source_target_pairs={{0,4},{4,8},{8,12},{12,14},{14,10},{10,6},{6,2},{2,0},{5,1},{9,5},... | collective-permute-start | bytes 712712 | tf_op jit(solution)/shard_map/ppermute | solution.py:170
  16.6 0.5 collective-permute-start.11
  17.1 0.0 collective-permute-start.12
  17.1 2.0 %collective-permute-start.9 = (bf16[32,3712]{1,0:T(8,128)(2,1)S(1)}, bf16[32,3712]{1,0:T(8,128)(2,1)S(1)}, u32[]{:S(2)}, u32[]{:S(2)}) collective-permute-start(bf16[32,3712]{1,0:T(8,128)(2,1)S(1)} %collective-permute-done.6.refs_4_), channel_id=1, source_target_pairs={{0,4},{4,8},{8,12},{12,14},{14,10},{10,6},{6,2},{2,0},{5,1},{9,5},... | collective-permute-start | bytes 712712 | tf_op jit(solution)/shard_map/ppermute | solution.py:170
  19.1 1.5 %collective-permute-done.7.refs_1_ = bf16[32,3712]{1,0:T(8,128)(2,1)S(1)} collective-permute-done((bf16[32,3712]{1,0:T(8,128)(2,1)S(1)}, bf16[32,3712]{1,0:T(8,128)(2,1)S(1)}, u32[]{:S(2)}, u32[]{:S(2)}) %collective-permute-start.7) | collective-permute-done | bytes 237600 | tf_op jit(solution)/shard_map/ppermute | solution.py:170
  20.6 2.1 %collective-permute-start.8 = (bf16[32,3712]{1,0:T(8,128)(2,1)S(1)}, bf16[32,3712]{1,0:T(8,128)(2,1)S(1)}, u32[]{:S(2)}, u32[]{:S(2)}) collective-permute-start(bf16[32,3712]{1,0:T(8,128)(2,1)S(1)} %collective-permute-done.7.refs_1_), channel_id=1, source_target_pairs={{0,4},{4,8},{8,12},{12,14},{14,10},{10,6},{6,2},{2,0},{5,1},{9,5},... | collective-permute-start | bytes 712712 | tf_op jit(solution)/shard_map/ppermute | solution.py:170
  22.7 0.0 copy-start
  22.7 4.1 %shard_map.65.refs_8_ = bf16[256,1024]{1,0:T(8,128)(2,1)S(1)} custom-call(bf16[32,3712]{1,0:T(8,128)(2,1)S(1)} %collective-permute-done.1.refs_0_, bf16[32,3712]{1,0:T(8,128)(2,1)S(1)} %collective-permute-done.4.refs_1_, bf16[32,3712]{1,0:T(8,128)(2,1)S(1)} %shard_map.64.refs_2_, bf16[32,3712]{1,0:T(8,128)(2,1)S(1)} %collective-permute-done.5.refs_3_, ...), custom_call_target="tpu_custom_call" | custom-call | flops 3758096384 | tf_op jit(solution)/shard_map/pallas_call | solution.py:126
  26.9 0.2 collective-permute-start.13
  27.1 0.3 collective-permute-start.14
  27.5 2.1 %shard_map.66 = (f32[96,3584]{1,0:T(8,128)S(1)}, bf16[160,3584]{1,0:T(8,128)(2,1)S(1)}) custom-call(bf16[32,3712]{1,0:T(8,128)(2,1)S(1)} %collective-permute-done.1.refs_0_, bf16[32,3712]{1,0:T(8,128)(2,1)S(1)} %collective-permute-done.4.refs_1_, bf16[32,3712]{1,0:T(8,128)(2,1)S(1)} %shard_map.64.refs_2_, ...), custom_call_target="tpu_custom_call" | custom-call | flops 1879048192 | tf_op jit(solution)/shard_map/pallas_call | solution.py:150
  29.6 0.2 collective-permute-start.15
  29.8 4.1 %shard_map.67.refs_3_.refs_5_ = bf16[256,1024]{1,0:T(8,128)(2,1)S(1)} custom-call(bf16[32,3712]{1,0:T(8,128)(2,1)S(1)} %collective-permute-done.13.refs_0_, bf16[32,3712]{1,0:T(8,128)(2,1)S(1)} %collective-permute-done.7.refs_1_, bf16[32,3712]{1,0:T(8,128)(2,1)S(1)} %collective-permute-done.9.refs_2_, ...), custom_call_target="tpu_custom_call" | custom-call | flops 3758096384 | tf_op jit(solution)/shard_map/pallas_call | solution.py:126
  34.0 1.3 %shard_map.68 = (bf16[64,3584]{1,0:T(8,128)(2,1)S(1)}, bf16[32,3584]{1,0:T(8,128)(2,1)S(1)}) custom-call(bf16[32,3712]{1,0:T(8,128)(2,1)S(1)} %collective-permute-done.13.refs_0_, bf16[32,3712]{1,0:T(8,128)(2,1)S(1)} %collective-permute-done.7.refs_1_, bf16[32,3712]{1,0:T(8,128)(2,1)S(1)} %collective-permute-done.9.refs_2_, ...), custom_call_target="tpu_custom_call" | custom-call | flops 1879048192 | tf_op jit(solution)/shard_map/pallas_call | solution.py:150
  35.3 0.4 collective-permute-start.16
  35.7 0.2 collective-permute-start.18
  35.9 1.4 %shard_map.69 = f32[160,3584]{1,0:T(8,128)S(1)} custom-call(bf16[32,3712]{1,0:T(8,128)(2,1)S(1)} %collective-permute-done.8.refs_3_.refs_0_, bf16[32,3712]{1,0:T(8,128)(2,1)S(1)} %collective-permute-done.10.refs_4_.refs_1_, bf16[32,3712]{1,0:T(8,128)(2,1)S(1)} %collective-permute-done.14.refs_5_.refs_2_, ...), custom_call_target="tpu_custom_call" | custom-call | flops 1879048192 | tf_op jit(solution)/shard_map/pallas_call | solution.py:150
  37.3 0.1 add_convert_fusion.7
  37.4 1.8 %collective-permute-start.19 = (bf16[32,3584]{1,0:T(8,128)(2,1)S(1)}, bf16[32,3584]{1,0:T(8,128)(2,1)S(1)}, u32[]{:S(2)}, u32[]{:S(2)}) collective-permute-start(bf16[32,3584]{1,0:T(8,128)(2,1)S(1)} %add_convert_fusion.7), channel_id=1, source_target_pairs={{0,4},{4,8},{8,12},{12,14},{14,10},{10,6},{6,2},{2,0},{5,1},{9,5},... | collective-permute-start | bytes 688136 | tf_op jit(solution)/shard_map/ppermute | solution.py:170
  39.2 1.6 %collective-permute-start.17 = (bf16[32,3584]{1,0:T(8,128)(2,1)S(1)}, bf16[32,3584]{1,0:T(8,128)(2,1)S(1)}, u32[]{:S(2)}, u32[]{:S(2)}) collective-permute-start(bf16[32,3584]{1,0:T(8,128)(2,1)S(1)} %add_convert_fusion.6), channel_id=1, source_target_pairs={{0,4},{4,8},{8,12},{12,14},{14,10},{10,6},{6,2},{2,0},{5,1},{9,5},... | collective-permute-start | bytes 688136 | tf_op jit(solution)/shard_map/ppermute | solution.py:170
  40.8 2.6 %collective-permute-done.19 = bf16[32,3584]{1,0:T(8,128)(2,1)S(1)} collective-permute-done((bf16[32,3584]{1,0:T(8,128)(2,1)S(1)}, bf16[32,3584]{1,0:T(8,128)(2,1)S(1)}, u32[]{:S(2)}, u32[]{:S(2)}) %collective-permute-start.19) | collective-permute-done | bytes 229408 | tf_op jit(solution)/shard_map/ppermute | solution.py:170
  43.4 0.1 add_convert_fusion.5
  43.5 1.8 %collective-permute-start.21 = (bf16[32,3584]{1,0:T(8,128)(2,1)S(1)}, bf16[32,3584]{1,0:T(8,128)(2,1)S(1)}, u32[]{:S(2)}, u32[]{:S(2)}) collective-permute-start(bf16[32,3584]{1,0:T(8,128)(2,1)S(1)} %add_convert_fusion.5), channel_id=1, source_target_pairs={{0,4},{4,8},{8,12},{12,14},{14,10},{10,6},{6,2},{2,0},{5,1},{9,5},... | collective-permute-start | bytes 688136 | tf_op jit(solution)/shard_map/ppermute | solution.py:170
  45.3 0.6 collective-permute-done.17
  45.9 0.1 add_convert_fusion.4
  46.0 1.8 %collective-permute-start.20 = (bf16[32,3584]{1,0:T(8,128)(2,1)S(1)}, bf16[32,3584]{1,0:T(8,128)(2,1)S(1)}, u32[]{:S(2)}, u32[]{:S(2)}) collective-permute-start(bf16[32,3584]{1,0:T(8,128)(2,1)S(1)} %add_convert_fusion.4), channel_id=1, source_target_pairs={{0,4},{4,8},{8,12},{12,14},{14,10},{10,6},{6,2},{2,0},{5,1},{9,5},... | collective-permute-start | bytes 688136 | tf_op jit(solution)/shard_map/ppermute | solution.py:170
  47.7 1.8 %collective-permute-done.21 = bf16[32,3584]{1,0:T(8,128)(2,1)S(1)} collective-permute-done((bf16[32,3584]{1,0:T(8,128)(2,1)S(1)}, bf16[32,3584]{1,0:T(8,128)(2,1)S(1)}, u32[]{:S(2)}, u32[]{:S(2)}) %collective-permute-start.21) | collective-permute-done | bytes 229408 | tf_op jit(solution)/shard_map/ppermute | solution.py:170
  49.6 0.1 add_convert_fusion.3
  49.7 1.8 %collective-permute-start.24 = (bf16[32,3584]{1,0:T(8,128)(2,1)S(1)}, bf16[32,3584]{1,0:T(8,128)(2,1)S(1)}, u32[]{:S(2)}, u32[]{:S(2)}) collective-permute-start(bf16[32,3584]{1,0:T(8,128)(2,1)S(1)} %add_convert_fusion.3), channel_id=1, source_target_pairs={{0,4},{4,8},{8,12},{12,14},{14,10},{10,6},{6,2},{2,0},{5,1},{9,5},... | collective-permute-start | bytes 688136 | tf_op jit(solution)/shard_map/ppermute | solution.py:170
  51.4 0.6 collective-permute-done.20
  52.0 0.1 add_convert_fusion.2
  52.1 1.8 %collective-permute-start.22 = (bf16[32,3584]{1,0:T(8,128)(2,1)S(1)}, bf16[32,3584]{1,0:T(8,128)(2,1)S(1)}, u32[]{:S(2)}, u32[]{:S(2)}) collective-permute-start(bf16[32,3584]{1,0:T(8,128)(2,1)S(1)} %add_convert_fusion.2), channel_id=1, source_target_pairs={{0,4},{4,8},{8,12},{12,14},{14,10},{10,6},{6,2},{2,0},{5,1},{9,5},... | collective-permute-start | bytes 688136 | tf_op jit(solution)/shard_map/ppermute | solution.py:170
  53.9 1.9 %collective-permute-done.24 = bf16[32,3584]{1,0:T(8,128)(2,1)S(1)} collective-permute-done((bf16[32,3584]{1,0:T(8,128)(2,1)S(1)}, bf16[32,3584]{1,0:T(8,128)(2,1)S(1)}, u32[]{:S(2)}, u32[]{:S(2)}) %collective-permute-start.24) | collective-permute-done | bytes 229408 | tf_op jit(solution)/shard_map/ppermute | solution.py:170
  55.7 0.1 add_convert_fusion.1
  55.8 1.8 %collective-permute-start.25 = (bf16[32,3584]{1,0:T(8,128)(2,1)S(1)}, bf16[32,3584]{1,0:T(8,128)(2,1)S(1)}, u32[]{:S(2)}, u32[]{:S(2)}) collective-permute-start(bf16[32,3584]{1,0:T(8,128)(2,1)S(1)} %add_convert_fusion.1), channel_id=1, source_target_pairs={{0,4},{4,8},{8,12},{12,14},{14,10},{10,6},{6,2},{2,0},{5,1},{9,5},... | collective-permute-start | bytes 688136 | tf_op jit(solution)/shard_map/ppermute | solution.py:170
  57.6 0.6 collective-permute-done.22
  58.2 3.7 %collective-permute-done.25 = bf16[32,3584]{1,0:T(8,128)(2,1)S(1)} collective-permute-done((bf16[32,3584]{1,0:T(8,128)(2,1)S(1)}, bf16[32,3584]{1,0:T(8,128)(2,1)S(1)}, u32[]{:S(2)}, u32[]{:S(2)}) %collective-permute-start.25) | collective-permute-done | bytes 229408 | tf_op jit(solution)/shard_map/ppermute | solution.py:170
  61.9 0.1 convert_add_fusion
  62.0 0.7 %add_convert_fusion = bf16[32,3584]{1,0:T(8,128)(2,1)} fusion(f32[32,3584]{1,0:T(8,128)S(1)} %convert_add_fusion, bf16[32,3584]{1,0:T(8,128)(2,1)S(1)} %collective-permute-done.23), kind=kLoop, calls=%fused_computation | loop fusion | flops 344064 | bytes 917504 | tf_op jit(solution)/shard_map/convert_element_type | solution.py:240
  (31 shorter events, 0.1 us)
Async XLA Ops:
  0.0 22.7 %slice-start = ((s8[7340032]{0:T(1024)(128)(4,1)}), s8[4194304]{0:T(1024)(128)(4,1)S(1)}, s32[]{:S(2)}) async-start(s8[7340032]{0:T(1024)(128)(4,1)} %bitcast.2), calls=%async_computation | async-start | bytes 8388608
  0.0 22.7 %slice-start.2 = ((s8[7340032]{0:T(1024)(128)(4,1)}), s8[4194304]{0:T(1024)(128)(4,1)S(1)}, s32[]{:S(2)}) async-start(s8[7340032]{0:T(1024)(128)(4,1)} %bitcast.4), calls=%async_computation.2 | async-start | bytes 8388608
  0.0 22.7 %slice-start.1 = ((s8[7340032]{0:T(1024)(128)(4,1)}), s8[3145728]{0:T(1024)(128)(4,1)S(1)}, s32[]{:S(2)}) async-start(s8[7340032]{0:T(1024)(128)(4,1)} %bitcast.2), calls=%async_computation.1 | async-start | bytes 6291456
  0.0 22.7 %slice-start.3 = ((s8[7340032]{0:T(1024)(128)(4,1)}), s8[3145728]{0:T(1024)(128)(4,1)S(1)}, s32[]{:S(2)}) async-start(s8[7340032]{0:T(1024)(128)(4,1)} %bitcast.4), calls=%async_computation.3 | async-start | bytes 6291456
  1.2 3.2 %collective-permute-start.2 = (bf16[32,3712]{1,0:T(8,128)(2,1)S(1)}, bf16[32,3712]{1,0:T(8,128)(2,1)S(1)}, u32[]{:S(2)}, u32[]{:S(2)}) collective-permute-start(bf16[32,3712]{1,0:T(8,128)(2,1)S(1)} %shard_map.64.refs_2_), channel_id=1, source_target_pairs={{0,1},{1,0},{2,3},{3,2},{4,5},{5,4},{6,7},{7,6},{8,9},{9,8},{10,11... | collective-permute-start | bytes 712712 | tf_op jit(solution)/shard_map/ppermute | solution.py:171
  1.7 6.7 %collective-permute-start = (bf16[32,3712]{1,0:T(8,128)(2,1)S(1)}, bf16[32,3712]{1,0:T(8,128)(2,1)S(1)}, u32[]{:S(2)}, u32[]{:S(2)}) collective-permute-start(bf16[32,3712]{1,0:T(8,128)(2,1)S(1)} %shard_map.64.refs_2_), channel_id=1, source_target_pairs={{0,4},{4,8},{8,12},{12,14},{14,10},{10,6},{6,2},{2,0},{5,1},{9,5},... | collective-permute-start | bytes 712712 | tf_op jit(solution)/shard_map/ppermute | solution.py:170
  4.3 6.6 %collective-permute-start.3 = (bf16[32,3712]{1,0:T(8,128)(2,1)S(1)}, bf16[32,3712]{1,0:T(8,128)(2,1)S(1)}, u32[]{:S(2)}, u32[]{:S(2)}) collective-permute-start(bf16[32,3712]{1,0:T(8,128)(2,1)S(1)} %collective-permute-done.2.refs_7_), channel_id=1, source_target_pairs={{0,4},{4,8},{8,12},{12,14},{14,10},{10,6},{6,2},{2,0},{5,1},{9,5},... | collective-permute-start | bytes 712712 | tf_op jit(solution)/shard_map/ppermute | solution.py:170
  8.4 6.1 %collective-permute-start.5 = (bf16[32,3712]{1,0:T(8,128)(2,1)S(1)}, bf16[32,3712]{1,0:T(8,128)(2,1)S(1)}, u32[]{:S(2)}, u32[]{:S(2)}) collective-permute-start(bf16[32,3712]{1,0:T(8,128)(2,1)S(1)} %collective-permute-done.refs_5_), channel_id=1, source_target_pairs={{0,4},{4,8},{8,12},{12,14},{14,10},{10,6},{6,2},{2,0},{5,1},{9,5},... | collective-permute-start | bytes 712712 | tf_op jit(solution)/shard_map/ppermute | solution.py:170
  10.9 6.2 %collective-permute-start.6 = (bf16[32,3712]{1,0:T(8,128)(2,1)S(1)}, bf16[32,3712]{1,0:T(8,128)(2,1)S(1)}, u32[]{:S(2)}, u32[]{:S(2)}) collective-permute-start(bf16[32,3712]{1,0:T(8,128)(2,1)S(1)} %collective-permute-done.3.refs_6_), channel_id=1, source_target_pairs={{0,4},{4,8},{8,12},{12,14},{14,10},{10,6},{6,2},{2,0},{5,1},{9,5},... | collective-permute-start | bytes 712712 | tf_op jit(solution)/shard_map/ppermute | solution.py:170
  13.0 4.1 %collective-permute-start.1 = (bf16[32,3712]{1,0:T(8,128)(2,1)S(1)}, bf16[32,3712]{1,0:T(8,128)(2,1)S(1)}, u32[]{:S(2)}, u32[]{:S(2)}) collective-permute-start(bf16[32,3712]{1,0:T(8,128)(2,1)S(1)} %collective-permute-done.refs_5_), channel_id=1, source_target_pairs={{0,1},{1,0},{2,3},{3,2},{4,5},{5,4},{6,7},{7,6},{8,9},{9,8},{10,11... | collective-permute-start | bytes 712712 | tf_op jit(solution)/shard_map/ppermute | solution.py:171
  14.5 6.1 %collective-permute-start.7 = (bf16[32,3712]{1,0:T(8,128)(2,1)S(1)}, bf16[32,3712]{1,0:T(8,128)(2,1)S(1)}, u32[]{:S(2)}, u32[]{:S(2)}) collective-permute-start(bf16[32,3712]{1,0:T(8,128)(2,1)S(1)} %collective-permute-done.5.refs_3_), channel_id=1, source_target_pairs={{0,4},{4,8},{8,12},{12,14},{14,10},{10,6},{6,2},{2,0},{5,1},{9,5},... | collective-permute-start | bytes 712712 | tf_op jit(solution)/shard_map/ppermute | solution.py:170
  16.5 4.0 %collective-permute-start.4 = (bf16[32,3712]{1,0:T(8,128)(2,1)S(1)}, bf16[32,3712]{1,0:T(8,128)(2,1)S(1)}, u32[]{:S(2)}, u32[]{:S(2)}) collective-permute-start(bf16[32,3712]{1,0:T(8,128)(2,1)S(1)} %collective-permute-done.3.refs_6_), channel_id=1, source_target_pairs={{0,1},{1,0},{2,3},{3,2},{4,5},{5,4},{6,7},{7,6},{8,9},{9,8},{10,11... | collective-permute-start | bytes 712712 | tf_op jit(solution)/shard_map/ppermute | solution.py:171
  16.6 10.3 %collective-permute-start.11 = (bf16[32,3712]{1,0:T(8,128)(2,1)S(1)}, bf16[32,3712]{1,0:T(8,128)(2,1)S(1)}, u32[]{:S(2)}, u32[]{:S(2)}) collective-permute-start(bf16[32,3712]{1,0:T(8,128)(2,1)S(1)} %collective-permute-done.5.refs_3_), channel_id=1, source_target_pairs={{0,1},{1,0},{2,3},{3,2},{4,5},{5,4},{6,7},{7,6},{8,9},{9,8},{10,11... | collective-permute-start | bytes 712712 | tf_op jit(solution)/shard_map/ppermute | solution.py:171
  17.1 9.8 %collective-permute-start.12 = (bf16[32,3712]{1,0:T(8,128)(2,1)S(1)}, bf16[32,3712]{1,0:T(8,128)(2,1)S(1)}, u32[]{:S(2)}, u32[]{:S(2)}) collective-permute-start(bf16[32,3712]{1,0:T(8,128)(2,1)S(1)} %collective-permute-done.6.refs_4_), channel_id=1, source_target_pairs={{0,1},{1,0},{2,3},{3,2},{4,5},{5,4},{6,7},{7,6},{8,9},{9,8},{10,11... | collective-permute-start | bytes 712712 | tf_op jit(solution)/shard_map/ppermute | solution.py:171
  17.1 9.8 %collective-permute-start.9 = (bf16[32,3712]{1,0:T(8,128)(2,1)S(1)}, bf16[32,3712]{1,0:T(8,128)(2,1)S(1)}, u32[]{:S(2)}, u32[]{:S(2)}) collective-permute-start(bf16[32,3712]{1,0:T(8,128)(2,1)S(1)} %collective-permute-done.6.refs_4_), channel_id=1, source_target_pairs={{0,4},{4,8},{8,12},{12,14},{14,10},{10,6},{6,2},{2,0},{5,1},{9,5},... | collective-permute-start | bytes 712712 | tf_op jit(solution)/shard_map/ppermute | solution.py:170
  20.6 6.3 %collective-permute-start.10 = (bf16[32,3712]{1,0:T(8,128)(2,1)S(1)}, bf16[32,3712]{1,0:T(8,128)(2,1)S(1)}, u32[]{:S(2)}, u32[]{:S(2)}) collective-permute-start(bf16[32,3712]{1,0:T(8,128)(2,1)S(1)} %collective-permute-done.7.refs_1_), channel_id=1, source_target_pairs={{0,1},{1,0},{2,3},{3,2},{4,5},{5,4},{6,7},{7,6},{8,9},{9,8},{10,11... | collective-permute-start | bytes 712712 | tf_op jit(solution)/shard_map/ppermute | solution.py:171
  20.6 6.3 %collective-permute-start.8 = (bf16[32,3712]{1,0:T(8,128)(2,1)S(1)}, bf16[32,3712]{1,0:T(8,128)(2,1)S(1)}, u32[]{:S(2)}, u32[]{:S(2)}) collective-permute-start(bf16[32,3712]{1,0:T(8,128)(2,1)S(1)} %collective-permute-done.7.refs_1_), channel_id=1, source_target_pairs={{0,4},{4,8},{8,12},{12,14},{14,10},{10,6},{6,2},{2,0},{5,1},{9,5},... | collective-permute-start | bytes 712712 | tf_op jit(solution)/shard_map/ppermute | solution.py:170
  22.7 4.8 %copy-start = (bf16[1,1024,3584]{2,1,0:T(8,128)(2,1)S(1)}, bf16[1,1024,3584]{2,1,0:T(8,128)(2,1)}, u32[]{:S(2)}) copy-start(bf16[1,1024,3584]{2,1,0:T(8,128)(2,1)} %refs_6_.1) | copy-start | bytes 22020100
  26.9 2.7 %collective-permute-start.13 = (bf16[32,3712]{1,0:T(8,128)(2,1)S(1)}, bf16[32,3712]{1,0:T(8,128)(2,1)S(1)}, u32[]{:S(2)}, u32[]{:S(2)}) collective-permute-start(bf16[32,3712]{1,0:T(8,128)(2,1)S(1)} %collective-permute-done.8.refs_3_.refs_0_), channel_id=1, source_target_pairs={{0,1},{1,0},{2,3},{3,2},{4,5},{5,4},{6,7},{7,6},{8,9},{9,8},{10,11... | collective-permute-start | bytes 712712 | tf_op jit(solution)/shard_map/ppermute | solution.py:171
  27.1 2.4 %collective-permute-start.14 = (bf16[32,3712]{1,0:T(8,128)(2,1)S(1)}, bf16[32,3712]{1,0:T(8,128)(2,1)S(1)}, u32[]{:S(2)}, u32[]{:S(2)}) collective-permute-start(bf16[32,3712]{1,0:T(8,128)(2,1)S(1)} %collective-permute-done.9.refs_2_), channel_id=1, source_target_pairs={{0,1},{1,0},{2,3},{3,2},{4,5},{5,4},{6,7},{7,6},{8,9},{9,8},{10,11... | collective-permute-start | bytes 712712 | tf_op jit(solution)/shard_map/ppermute | solution.py:171
  29.6 7.7 %collective-permute-start.15 = (bf16[160,3584]{1,0:T(8,128)(2,1)S(1)}, bf16[160,3584]{1,0:T(8,128)(2,1)S(1)}, u32[]{:S(2)}, u32[]{:S(2)}) collective-permute-start(bf16[160,3584]{1,0:T(8,128)(2,1)S(1)} %get-tuple-element.52), channel_id=1, source_target_pairs={{0,1},{1,0},{2,3},{3,2},{4,5},{5,4},{6,7},{7,6},{8,9},{9,8},{10,11... | collective-permute-start | bytes 3440648 | tf_op jit(solution)/shard_map/ppermute | solution.py:171
  35.3 2.0 %collective-permute-start.16 = (bf16[64,3584]{1,0:T(8,128)(2,1)S(1)}, bf16[64,3584]{1,0:T(8,128)(2,1)S(1)}, u32[]{:S(2)}, u32[]{:S(2)}) collective-permute-start(bf16[64,3584]{1,0:T(8,128)(2,1)S(1)} %get-tuple-element.55), channel_id=1, source_target_pairs={{0,1},{1,0},{2,3},{3,2},{4,5},{5,4},{6,7},{7,6},{8,9},{9,8},{10,11... | collective-permute-start | bytes 1376264 | tf_op jit(solution)/shard_map/ppermute | solution.py:171
  35.7 5.1 %collective-permute-start.18 = (bf16[32,3584]{1,0:T(8,128)(2,1)S(1)}, bf16[32,3584]{1,0:T(8,128)(2,1)S(1)}, u32[]{:S(2)}, u32[]{:S(2)}) collective-permute-start(bf16[32,3584]{1,0:T(8,128)(2,1)S(1)} %get-tuple-element.58), channel_id=1, source_target_pairs={{0,1},{1,0},{2,3},{3,2},{4,5},{5,4},{6,7},{7,6},{8,9},{9,8},{10,11... | collective-permute-start | bytes 688136 | tf_op jit(solution)/shard_map/ppermute | solution.py:171
  37.4 6.1 %collective-permute-start.19 = (bf16[32,3584]{1,0:T(8,128)(2,1)S(1)}, bf16[32,3584]{1,0:T(8,128)(2,1)S(1)}, u32[]{:S(2)}, u32[]{:S(2)}) collective-permute-start(bf16[32,3584]{1,0:T(8,128)(2,1)S(1)} %add_convert_fusion.7), channel_id=1, source_target_pairs={{0,4},{4,8},{8,12},{12,14},{14,10},{10,6},{6,2},{2,0},{5,1},{9,5},... | collective-permute-start | bytes 688136 | tf_op jit(solution)/shard_map/ppermute | solution.py:170
  39.2 6.7 %collective-permute-start.17 = (bf16[32,3584]{1,0:T(8,128)(2,1)S(1)}, bf16[32,3584]{1,0:T(8,128)(2,1)S(1)}, u32[]{:S(2)}, u32[]{:S(2)}) collective-permute-start(bf16[32,3584]{1,0:T(8,128)(2,1)S(1)} %add_convert_fusion.6), channel_id=1, source_target_pairs={{0,4},{4,8},{8,12},{12,14},{14,10},{10,6},{6,2},{2,0},{5,1},{9,5},... | collective-permute-start | bytes 688136 | tf_op jit(solution)/shard_map/ppermute | solution.py:170
  43.5 6.1 %collective-permute-start.21 = (bf16[32,3584]{1,0:T(8,128)(2,1)S(1)}, bf16[32,3584]{1,0:T(8,128)(2,1)S(1)}, u32[]{:S(2)}, u32[]{:S(2)}) collective-permute-start(bf16[32,3584]{1,0:T(8,128)(2,1)S(1)} %add_convert_fusion.5), channel_id=1, source_target_pairs={{0,4},{4,8},{8,12},{12,14},{14,10},{10,6},{6,2},{2,0},{5,1},{9,5},... | collective-permute-start | bytes 688136 | tf_op jit(solution)/shard_map/ppermute | solution.py:170
  46.0 6.1 %collective-permute-start.20 = (bf16[32,3584]{1,0:T(8,128)(2,1)S(1)}, bf16[32,3584]{1,0:T(8,128)(2,1)S(1)}, u32[]{:S(2)}, u32[]{:S(2)}) collective-permute-start(bf16[32,3584]{1,0:T(8,128)(2,1)S(1)} %add_convert_fusion.4), channel_id=1, source_target_pairs={{0,4},{4,8},{8,12},{12,14},{14,10},{10,6},{6,2},{2,0},{5,1},{9,5},... | collective-permute-start | bytes 688136 | tf_op jit(solution)/shard_map/ppermute | solution.py:170
  49.7 6.1 %collective-permute-start.24 = (bf16[32,3584]{1,0:T(8,128)(2,1)S(1)}, bf16[32,3584]{1,0:T(8,128)(2,1)S(1)}, u32[]{:S(2)}, u32[]{:S(2)}) collective-permute-start(bf16[32,3584]{1,0:T(8,128)(2,1)S(1)} %add_convert_fusion.3), channel_id=1, source_target_pairs={{0,4},{4,8},{8,12},{12,14},{14,10},{10,6},{6,2},{2,0},{5,1},{9,5},... | collective-permute-start | bytes 688136 | tf_op jit(solution)/shard_map/ppermute | solution.py:170
  52.1 6.1 %collective-permute-start.22 = (bf16[32,3584]{1,0:T(8,128)(2,1)S(1)}, bf16[32,3584]{1,0:T(8,128)(2,1)S(1)}, u32[]{:S(2)}, u32[]{:S(2)}) collective-permute-start(bf16[32,3584]{1,0:T(8,128)(2,1)S(1)} %add_convert_fusion.2), channel_id=1, source_target_pairs={{0,4},{4,8},{8,12},{12,14},{14,10},{10,6},{6,2},{2,0},{5,1},{9,5},... | collective-permute-start | bytes 688136 | tf_op jit(solution)/shard_map/ppermute | solution.py:170
  55.8 6.1 %collective-permute-start.25 = (bf16[32,3584]{1,0:T(8,128)(2,1)S(1)}, bf16[32,3584]{1,0:T(8,128)(2,1)S(1)}, u32[]{:S(2)}, u32[]{:S(2)}) collective-permute-start(bf16[32,3584]{1,0:T(8,128)(2,1)S(1)} %add_convert_fusion.1), channel_id=1, source_target_pairs={{0,4},{4,8},{8,12},{12,14},{14,10},{10,6},{6,2},{2,0},{5,1},{9,5},... | collective-permute-start | bytes 688136 | tf_op jit(solution)/shard_map/ppermute | solution.py:170
  58.2 3.8 %collective-permute-start.23 = (bf16[32,3584]{1,0:T(8,128)(2,1)S(1)}, bf16[32,3584]{1,0:T(8,128)(2,1)S(1)}, u32[]{:S(2)}, u32[]{:S(2)}) collective-permute-start(bf16[32,3584]{1,0:T(8,128)(2,1)S(1)} %collective-permute-done.22), channel_id=1, source_target_pairs={{0,1},{1,0},{2,3},{3,2},{4,5},{5,4},{6,7},{7,6},{8,9},{9,8},{10,11... | collective-permute-start | bytes 688136 | tf_op jit(solution)/shard_map/ppermute | solution.py:171

commit v17 on v16

--- a/solution.py
+++ b/solution.py
@@ -167,7 +167,9 @@
     forth = [(2 * order[i], 2 * order[(i + 1) % chips]) for i in range(chips)]
     spin = forth + [(b + 1, a + 1) for a, b in forth]
     swap = [(i, i ^ 1) for i in range(experts)]
+    turn = dict(spin)
     send = lambda a: lax.ppermute(a, "node", spin)
+    send_two = lambda a: lax.ppermute(a, "node", [(a, turn[b]) for a, b in spin])
     sibling = lambda a: lax.ppermute(a, "node", swap)
     together = lax.optimization_barrier
     block = lambda a, j: a[j * rows : (j + 1) * rows]
@@ -227,14 +229,18 @@
         return last
 
     last = mine[0][0]
-    sums = send(add(0))
-    sums_twin = []
+    sums, sums_twin = [send_two(add(0))], []
     for j in range(1, end, 2):
         sums_twin = [send(add(j, *sums_twin))]
-        sums = send(add(j + 1, sums))
+        if j == 1:
+            sums.append(send(add(2)))
+        else:
+            sums = [send(add(j + 1, *sums))]
+    (sums,) = sums
     piece, sums = together((theirs[end][0], sums))
     total = block(*mine[end]) + block(piece, theirs[end][1]).astype(F32) + sums.astype(F32)
     for a in sums_twin:
+        a, _ = together((a, last))
         a, total = together((sibling(a), total))
         total = total + a.astype(F32)
     return total.astype(BF16)

time: 62.8 us -> 63.9 us (1.018)
  starting transfers between devices: 29.3 us -> 32.8 us
  waiting for transfers between devices: 17.7 us -> 15.3 us
    ppermute x0 -> x1, starting transfers between devices: none -> 2.78 us  [local(): lax.ppermute(a, 'node', [(a, turn[b]) for a, b in spin])]
    ppermute x14 -> x13, waiting for transfers between devices: 17.7 us -> 15.2 us  [local(): send = lambda a: lax.ppermute(a, 'node', spin)]
    ppermute x14 -> x13, starting transfers between devices: 26.8 us -> 27.6 us  [local(): send = lambda a: lax.ppermute(a, 'node', spin)]
  transfers between devices with their start and end apart: 26 -> 26, of which waited for: 11 -> 8; matrix products, arithmetic and copies ran while one was open for 1% -> 1% of each run, Pallas kernels for 21% -> 20%
where the time goes in v17:
time: 63.9 us; the launch traced here: 63.8 us
  starting transfers between devices  32.8 us (51%)
  waiting for transfers between devices  15.3 us (24%)
  Pallas kernels  14.2 us (22%)
  other arithmetic  1.3 us (2%)
    ppermute x13, starting transfers between devices, local(): send = lambda a: lax.ppermute(a, 'node', spin)  27.6 us
    ppermute x13, waiting for transfers between devices, local(): send = lambda a: lax.ppermute(a, 'node', spin)  15.2 us
    pallas_call x2, Pallas kernels, hidden(): pl.pallas_call(functools.partial(hidden_kernel, count, tiles(width, ff)[0...  8.26 us
    pallas_call x3, Pallas kernels, output(): pl.pallas_call(functools.partial(output_kernel, count, experts, tiles(wid...  4.81 us
    ppermute x1, starting transfers between devices, local(): lax.ppermute(a, 'node', [(a, turn[b]) for a, b in spin])  2.78 us
    ppermute x12, starting transfers between devices, local(): sibling = lambda a: lax.ppermute(a, 'node', swap)  2.44 us
  transfers between devices with their start and end apart: 26, of which 8 were waited for; matrix products, arithmetic and copies ran while one was open for 1% of the time, Pallas kernels for 20%

profile of v17, /device:TPU:0, one launch (start us, length us, event | category | flops | bytes accessed | tf_op | source)
XLA Modules:
  0.0 63.8 jit_solution(15565383965011412659)
XLA Ops:
  0.0 1.1 %shard_map.64.refs_2_ = bf16[32,3712]{1,0:T(8,128)(2,1)S(1)} custom-call(bf16[32,3584]{1,0:T(8,128)(2,1)} %tok_hbm.1, s32[8,32]{1,0:T(8,128)} %bitcast.6, f32[8,32]{1,0:T(8,128)} %bitcast.7), custom_call_target="tpu_custom_call" | custom-call | flops 10737418240 | tf_op jit(solution)/shard_map/pallas_call | solution.py:59
  1.2 0.5 collective-permute-start.2
  1.7 2.6 %collective-permute-start = (bf16[32,3712]{1,0:T(8,128)(2,1)S(1)}, bf16[32,3712]{1,0:T(8,128)(2,1)S(1)}, u32[]{:S(2)}, u32[]{:S(2)}) collective-permute-start(bf16[32,3712]{1,0:T(8,128)(2,1)S(1)} %shard_map.64.refs_2_), channel_id=1, source_target_pairs={{0,4},{4,8},{8,12},{12,14},{14,10},{10,6},{6,2},{2,0},{5,1},{9,5},... | collective-permute-start | bytes 712712 | tf_op jit(solution)/shard_map/ppermute | solution.py:171
  4.3 0.0 collective-permute-done.2.refs_7_
  4.3 1.6 %collective-permute-start.3 = (bf16[32,3712]{1,0:T(8,128)(2,1)S(1)}, bf16[32,3712]{1,0:T(8,128)(2,1)S(1)}, u32[]{:S(2)}, u32[]{:S(2)}) collective-permute-start(bf16[32,3712]{1,0:T(8,128)(2,1)S(1)} %collective-permute-done.2.refs_7_), channel_id=1, source_target_pairs={{0,4},{4,8},{8,12},{12,14},{14,10},{10,6},{6,2},{2,0},{5,1},{9,5},... | collective-permute-start | bytes 712712 | tf_op jit(solution)/shard_map/ppermute | solution.py:171
  5.9 2.5 %collective-permute-done.refs_5_ = bf16[32,3712]{1,0:T(8,128)(2,1)S(1)} collective-permute-done((bf16[32,3712]{1,0:T(8,128)(2,1)S(1)}, bf16[32,3712]{1,0:T(8,128)(2,1)S(1)}, u32[]{:S(2)}, u32[]{:S(2)}) %collective-permute-start) | collective-permute-done | bytes 237600 | tf_op jit(solution)/shard_map/ppermute | solution.py:171
  8.4 2.1 %collective-permute-start.5 = (bf16[32,3712]{1,0:T(8,128)(2,1)S(1)}, bf16[32,3712]{1,0:T(8,128)(2,1)S(1)}, u32[]{:S(2)}, u32[]{:S(2)}) collective-permute-start(bf16[32,3712]{1,0:T(8,128)(2,1)S(1)} %collective-permute-done.refs_5_), channel_id=1, source_target_pairs={{0,4},{4,8},{8,12},{12,14},{14,10},{10,6},{6,2},{2,0},{5,1},{9,5},... | collective-permute-start | bytes 712712 | tf_op jit(solution)/shard_map/ppermute | solution.py:171
  10.4 0.5 collective-permute-done.3.refs_6_
  10.9 2.1 %collective-permute-start.6 = (bf16[32,3712]{1,0:T(8,128)(2,1)S(1)}, bf16[32,3712]{1,0:T(8,128)(2,1)S(1)}, u32[]{:S(2)}, u32[]{:S(2)}) collective-permute-start(bf16[32,3712]{1,0:T(8,128)(2,1)S(1)} %collective-permute-done.3.refs_6_), channel_id=1, source_target_pairs={{0,4},{4,8},{8,12},{12,14},{14,10},{10,6},{6,2},{2,0},{5,1},{9,5},... | collective-permute-start | bytes 712712 | tf_op jit(solution)/shard_map/ppermute | solution.py:171
  13.0 0.0 collective-permute-start.1
  13.0 1.5 %collective-permute-done.5.refs_3_ = bf16[32,3712]{1,0:T(8,128)(2,1)S(1)} collective-permute-done((bf16[32,3712]{1,0:T(8,128)(2,1)S(1)}, bf16[32,3712]{1,0:T(8,128)(2,1)S(1)}, u32[]{:S(2)}, u32[]{:S(2)}) %collective-permute-start.5) | collective-permute-done | bytes 237600 | tf_op jit(solution)/shard_map/ppermute | solution.py:171
  14.5 2.1 %collective-permute-start.7 = (bf16[32,3712]{1,0:T(8,128)(2,1)S(1)}, bf16[32,3712]{1,0:T(8,128)(2,1)S(1)}, u32[]{:S(2)}, u32[]{:S(2)}) collective-permute-start(bf16[32,3712]{1,0:T(8,128)(2,1)S(1)} %collective-permute-done.5.refs_3_), channel_id=1, source_target_pairs={{0,4},{4,8},{8,12},{12,14},{14,10},{10,6},{6,2},{2,0},{5,1},{9,5},... | collective-permute-start | bytes 712712 | tf_op jit(solution)/shard_map/ppermute | solution.py:171
  16.6 0.5 collective-permute-start.11
  17.1 0.0 collective-permute-done.6.refs_4_
  17.1 0.0 collective-permute-start.12
  17.1 2.0 %collective-permute-start.9 = (bf16[32,3712]{1,0:T(8,128)(2,1)S(1)}, bf16[32,3712]{1,0:T(8,128)(2,1)S(1)}, u32[]{:S(2)}, u32[]{:S(2)}) collective-permute-start(bf16[32,3712]{1,0:T(8,128)(2,1)S(1)} %collective-permute-done.6.refs_4_), channel_id=1, source_target_pairs={{0,4},{4,8},{8,12},{12,14},{14,10},{10,6},{6,2},{2,0},{5,1},{9,5},... | collective-permute-start | bytes 712712 | tf_op jit(solution)/shard_map/ppermute | solution.py:171
  19.1 1.5 %collective-permute-done.7.refs_1_ = bf16[32,3712]{1,0:T(8,128)(2,1)S(1)} collective-permute-done((bf16[32,3712]{1,0:T(8,128)(2,1)S(1)}, bf16[32,3712]{1,0:T(8,128)(2,1)S(1)}, u32[]{:S(2)}, u32[]{:S(2)}) %collective-permute-start.7) | collective-permute-done | bytes 237600 | tf_op jit(solution)/shard_map/ppermute | solution.py:171
  20.6 2.1 %collective-permute-start.8 = (bf16[32,3712]{1,0:T(8,128)(2,1)S(1)}, bf16[32,3712]{1,0:T(8,128)(2,1)S(1)}, u32[]{:S(2)}, u32[]{:S(2)}) collective-permute-start(bf16[32,3712]{1,0:T(8,128)(2,1)S(1)} %collective-permute-done.7.refs_1_), channel_id=1, source_target_pairs={{0,4},{4,8},{8,12},{12,14},{14,10},{10,6},{6,2},{2,0},{5,1},{9,5},... | collective-permute-start | bytes 712712 | tf_op jit(solution)/shard_map/ppermute | solution.py:171
  22.7 0.0 copy-start
  22.7 4.1 %shard_map.65.refs_8_ = bf16[256,1024]{1,0:T(8,128)(2,1)S(1)} custom-call(bf16[32,3712]{1,0:T(8,128)(2,1)S(1)} %collective-permute-done.1.refs_0_, bf16[32,3712]{1,0:T(8,128)(2,1)S(1)} %collective-permute-done.4.refs_1_, bf16[32,3712]{1,0:T(8,128)(2,1)S(1)} %shard_map.64.refs_2_, bf16[32,3712]{1,0:T(8,128)(2,1)S(1)} %collective-permute-done.5.refs_3_, ...), custom_call_target="tpu_custom_call" | custom-call | flops 3758096384 | tf_op jit(solution)/shard_map/pallas_call | solution.py:126
  26.9 0.2 collective-permute-start.13
  27.1 0.3 collective-permute-start.14
  27.5 2.1 %shard_map.66 = (f32[96,3584]{1,0:T(8,128)S(1)}, bf16[160,3584]{1,0:T(8,128)(2,1)S(1)}) custom-call(bf16[32,3712]{1,0:T(8,128)(2,1)S(1)} %collective-permute-done.1.refs_0_, bf16[32,3712]{1,0:T(8,128)(2,1)S(1)} %collective-permute-done.4.refs_1_, bf16[32,3712]{1,0:T(8,128)(2,1)S(1)} %shard_map.64.refs_2_, ...), custom_call_target="tpu_custom_call" | custom-call | flops 1879048192 | tf_op jit(solution)/shard_map/pallas_call | solution.py:150
  29.6 0.2 collective-permute-start.15
  29.8 4.1 %shard_map.67.refs_3_.refs_5_ = bf16[256,1024]{1,0:T(8,128)(2,1)S(1)} custom-call(bf16[32,3712]{1,0:T(8,128)(2,1)S(1)} %collective-permute-done.13.refs_0_, bf16[32,3712]{1,0:T(8,128)(2,1)S(1)} %collective-permute-done.7.refs_1_, bf16[32,3712]{1,0:T(8,128)(2,1)S(1)} %collective-permute-done.9.refs_2_, ...), custom_call_target="tpu_custom_call" | custom-call | flops 3758096384 | tf_op jit(solution)/shard_map/pallas_call | solution.py:126
  34.0 1.3 %shard_map.68 = (bf16[64,3584]{1,0:T(8,128)(2,1)S(1)}, bf16[32,3584]{1,0:T(8,128)(2,1)S(1)}) custom-call(bf16[32,3712]{1,0:T(8,128)(2,1)S(1)} %collective-permute-done.13.refs_0_, bf16[32,3712]{1,0:T(8,128)(2,1)S(1)} %collective-permute-done.7.refs_1_, bf16[32,3712]{1,0:T(8,128)(2,1)S(1)} %collective-permute-done.9.refs_2_, ...), custom_call_target="tpu_custom_call" | custom-call | flops 1879048192 | tf_op jit(solution)/shard_map/pallas_call | solution.py:150
  35.3 0.4 collective-permute-start.16
  35.7 0.2 collective-permute-start.18
  35.9 1.4 %shard_map.69 = f32[160,3584]{1,0:T(8,128)S(1)} custom-call(bf16[32,3712]{1,0:T(8,128)(2,1)S(1)} %collective-permute-done.8.refs_3_.refs_0_, bf16[32,3712]{1,0:T(8,128)(2,1)S(1)} %collective-permute-done.10.refs_4_.refs_1_, bf16[32,3712]{1,0:T(8,128)(2,1)S(1)} %collective-permute-done.14.refs_5_.refs_2_, ...), custom_call_target="tpu_custom_call" | custom-call | flops 1879048192 | tf_op jit(solution)/shard_map/pallas_call | solution.py:150
  37.3 0.1 add_convert_fusion.7
  37.4 2.8 %collective-permute-start.20 = (bf16[32,3584]{1,0:T(8,128)(2,1)S(1)}, bf16[32,3584]{1,0:T(8,128)(2,1)S(1)}, u32[]{:S(2)}, u32[]{:S(2)}) collective-permute-start(bf16[32,3584]{1,0:T(8,128)(2,1)S(1)} %add_convert_fusion.7), channel_id=1, source_target_pairs={{0,8},{4,12},{8,14},{12,10},{14,6},{10,2},{6,0},{2,4},{5,3},{9,1},... | collective-permute-start | bytes 688136 | tf_op jit(solution)/shard_map/ppermute | solution.py:172
  40.2 1.6 %collective-permute-start.17 = (bf16[32,3584]{1,0:T(8,128)(2,1)S(1)}, bf16[32,3584]{1,0:T(8,128)(2,1)S(1)}, u32[]{:S(2)}, u32[]{:S(2)}) collective-permute-start(bf16[32,3584]{1,0:T(8,128)(2,1)S(1)} %add_convert_fusion.6), channel_id=1, source_target_pairs={{0,4},{4,8},{8,12},{12,14},{14,10},{10,6},{6,2},{2,0},{5,1},{9,5},... | collective-permute-start | bytes 688136 | tf_op jit(solution)/shard_map/ppermute | solution.py:171
  41.9 1.6 %collective-permute-start.21 = (bf16[32,3584]{1,0:T(8,128)(2,1)S(1)}, bf16[32,3584]{1,0:T(8,128)(2,1)S(1)}, u32[]{:S(2)}, u32[]{:S(2)}) collective-permute-start(bf16[32,3584]{1,0:T(8,128)(2,1)S(1)} %add_convert_fusion.5), channel_id=1, source_target_pairs={{0,4},{4,8},{8,12},{12,14},{14,10},{10,6},{6,2},{2,0},{5,1},{9,5},... | collective-permute-start | bytes 688136 | tf_op jit(solution)/shard_map/ppermute | solution.py:171
  43.4 4.6 %collective-permute-done.17 = bf16[32,3584]{1,0:T(8,128)(2,1)S(1)} collective-permute-done((bf16[32,3584]{1,0:T(8,128)(2,1)S(1)}, bf16[32,3584]{1,0:T(8,128)(2,1)S(1)}, u32[]{:S(2)}, u32[]{:S(2)}) %collective-permute-start.17) | collective-permute-done | bytes 229408 | tf_op jit(solution)/shard_map/ppermute | solution.py:171
  48.0 0.1 add_convert_fusion.4
  48.1 2.5 %collective-permute-start.19 = (bf16[32,3584]{1,0:T(8,128)(2,1)S(1)}, bf16[32,3584]{1,0:T(8,128)(2,1)S(1)}, u32[]{:S(2)}, u32[]{:S(2)}) collective-permute-start(bf16[32,3584]{1,0:T(8,128)(2,1)S(1)} %add_convert_fusion.4), channel_id=1, source_target_pairs={{0,4},{4,8},{8,12},{12,14},{14,10},{10,6},{6,2},{2,0},{5,1},{9,5},... | collective-permute-start | bytes 688136 | tf_op jit(solution)/shard_map/ppermute | solution.py:171
  50.6 0.1 add_convert_fusion.3
  50.7 2.4 %collective-permute-start.23 = (bf16[32,3584]{1,0:T(8,128)(2,1)S(1)}, bf16[32,3584]{1,0:T(8,128)(2,1)S(1)}, u32[]{:S(2)}, u32[]{:S(2)}) collective-permute-start(bf16[32,3584]{1,0:T(8,128)(2,1)S(1)} %add_convert_fusion.3), channel_id=1, source_target_pairs={{0,4},{4,8},{8,12},{12,14},{14,10},{10,6},{6,2},{2,0},{5,1},{9,5},... | collective-permute-start | bytes 688136 | tf_op jit(solution)/shard_map/ppermute | solution.py:171
  53.1 1.0 %collective-permute-done.19 = bf16[32,3584]{1,0:T(8,128)(2,1)S(1)} collective-permute-done((bf16[32,3584]{1,0:T(8,128)(2,1)S(1)}, bf16[32,3584]{1,0:T(8,128)(2,1)S(1)}, u32[]{:S(2)}, u32[]{:S(2)}) %collective-permute-start.19) | collective-permute-done | bytes 229408 | tf_op jit(solution)/shard_map/ppermute | solution.py:171
  54.2 0.1 add_convert_fusion.2
  54.2 2.5 %collective-permute-start.22 = (bf16[32,3584]{1,0:T(8,128)(2,1)S(1)}, bf16[32,3584]{1,0:T(8,128)(2,1)S(1)}, u32[]{:S(2)}, u32[]{:S(2)}) collective-permute-start(bf16[32,3584]{1,0:T(8,128)(2,1)S(1)} %add_convert_fusion.2), channel_id=1, source_target_pairs={{0,4},{4,8},{8,12},{12,14},{14,10},{10,6},{6,2},{2,0},{5,1},{9,5},... | collective-permute-start | bytes 688136 | tf_op jit(solution)/shard_map/ppermute | solution.py:171
  56.8 0.0 collective-permute-done.23
  56.8 0.1 add_convert_fusion.1
  56.9 2.4 %collective-permute-start.25 = (bf16[32,3584]{1,0:T(8,128)(2,1)S(1)}, bf16[32,3584]{1,0:T(8,128)(2,1)S(1)}, u32[]{:S(2)}, u32[]{:S(2)}) collective-permute-start(bf16[32,3584]{1,0:T(8,128)(2,1)S(1)} %add_convert_fusion.1), channel_id=1, source_target_pairs={{0,4},{4,8},{8,12},{12,14},{14,10},{10,6},{6,2},{2,0},{5,1},{9,5},... | collective-permute-start | bytes 688136 | tf_op jit(solution)/shard_map/ppermute | solution.py:171
  59.3 1.0 %collective-permute-done.22 = bf16[32,3584]{1,0:T(8,128)(2,1)S(1)} collective-permute-done((bf16[32,3584]{1,0:T(8,128)(2,1)S(1)}, bf16[32,3584]{1,0:T(8,128)(2,1)S(1)}, u32[]{:S(2)}, u32[]{:S(2)}) %collective-permute-start.22) | collective-permute-done | bytes 229408 | tf_op jit(solution)/shard_map/ppermute | solution.py:171
  60.3 2.7 %collective-permute-done.25 = bf16[32,3584]{1,0:T(8,128)(2,1)S(1)} collective-permute-done((bf16[32,3584]{1,0:T(8,128)(2,1)S(1)}, bf16[32,3584]{1,0:T(8,128)(2,1)S(1)}, u32[]{:S(2)}, u32[]{:S(2)}) %collective-permute-start.25) | collective-permute-done | bytes 229408 | tf_op jit(solution)/shard_map/ppermute | solution.py:171
  63.0 0.1 convert_add_fusion
  63.0 0.7 %add_convert_fusion = bf16[32,3584]{1,0:T(8,128)(2,1)} fusion(f32[32,3584]{1,0:T(8,128)S(1)} %convert_add_fusion, bf16[32,3584]{1,0:T(8,128)(2,1)S(1)} %collective-permute-done.24), kind=kLoop, calls=%fused_computation | loop fusion | flops 344064 | bytes 917504 | tf_op jit(solution)/shard_map/convert_element_type | solution.py:246
  (31 shorter events, 0.2 us)
Async XLA Ops:
  0.0 22.7 %slice-start = ((s8[7340032]{0:T(1024)(128)(4,1)}), s8[4194304]{0:T(1024)(128)(4,1)S(1)}, s32[]{:S(2)}) async-start(s8[7340032]{0:T(1024)(128)(4,1)} %bitcast.2), calls=%async_computation | async-start | bytes 8388608
  0.0 22.7 %slice-start.2 = ((s8[7340032]{0:T(1024)(128)(4,1)}), s8[4194304]{0:T(1024)(128)(4,1)S(1)}, s32[]{:S(2)}) async-start(s8[7340032]{0:T(1024)(128)(4,1)} %bitcast.4), calls=%async_computation.2 | async-start | bytes 8388608
  0.0 22.7 %slice-start.1 = ((s8[7340032]{0:T(1024)(128)(4,1)}), s8[3145728]{0:T(1024)(128)(4,1)S(1)}, s32[]{:S(2)}) async-start(s8[7340032]{0:T(1024)(128)(4,1)} %bitcast.2), calls=%async_computation.1 | async-start | bytes 6291456
  0.0 22.7 %slice-start.3 = ((s8[7340032]{0:T(1024)(128)(4,1)}), s8[3145728]{0:T(1024)(128)(4,1)S(1)}, s32[]{:S(2)}) async-start(s8[7340032]{0:T(1024)(128)(4,1)} %bitcast.4), calls=%async_computation.3 | async-start | bytes 6291456
  1.2 3.2 %collective-permute-start.2 = (bf16[32,3712]{1,0:T(8,128)(2,1)S(1)}, bf16[32,3712]{1,0:T(8,128)(2,1)S(1)}, u32[]{:S(2)}, u32[]{:S(2)}) collective-permute-start(bf16[32,3712]{1,0:T(8,128)(2,1)S(1)} %shard_map.64.refs_2_), channel_id=1, source_target_pairs={{0,1},{1,0},{2,3},{3,2},{4,5},{5,4},{6,7},{7,6},{8,9},{9,8},{10,11... | collective-permute-start | bytes 712712 | tf_op jit(solution)/shard_map/ppermute | solution.py:173
  1.7 6.7 %collective-permute-start = (bf16[32,3712]{1,0:T(8,128)(2,1)S(1)}, bf16[32,3712]{1,0:T(8,128)(2,1)S(1)}, u32[]{:S(2)}, u32[]{:S(2)}) collective-permute-start(bf16[32,3712]{1,0:T(8,128)(2,1)S(1)} %shard_map.64.refs_2_), channel_id=1, source_target_pairs={{0,4},{4,8},{8,12},{12,14},{14,10},{10,6},{6,2},{2,0},{5,1},{9,5},... | collective-permute-start | bytes 712712 | tf_op jit(solution)/shard_map/ppermute | solution.py:171
  4.3 6.6 %collective-permute-start.3 = (bf16[32,3712]{1,0:T(8,128)(2,1)S(1)}, bf16[32,3712]{1,0:T(8,128)(2,1)S(1)}, u32[]{:S(2)}, u32[]{:S(2)}) collective-permute-start(bf16[32,3712]{1,0:T(8,128)(2,1)S(1)} %collective-permute-done.2.refs_7_), channel_id=1, source_target_pairs={{0,4},{4,8},{8,12},{12,14},{14,10},{10,6},{6,2},{2,0},{5,1},{9,5},... | collective-permute-start | bytes 712712 | tf_op jit(solution)/shard_map/ppermute | solution.py:171
  8.4 6.1 %collective-permute-start.5 = (bf16[32,3712]{1,0:T(8,128)(2,1)S(1)}, bf16[32,3712]{1,0:T(8,128)(2,1)S(1)}, u32[]{:S(2)}, u32[]{:S(2)}) collective-permute-start(bf16[32,3712]{1,0:T(8,128)(2,1)S(1)} %collective-permute-done.refs_5_), channel_id=1, source_target_pairs={{0,4},{4,8},{8,12},{12,14},{14,10},{10,6},{6,2},{2,0},{5,1},{9,5},... | collective-permute-start | bytes 712712 | tf_op jit(solution)/shard_map/ppermute | solution.py:171
  10.9 6.2 %collective-permute-start.6 = (bf16[32,3712]{1,0:T(8,128)(2,1)S(1)}, bf16[32,3712]{1,0:T(8,128)(2,1)S(1)}, u32[]{:S(2)}, u32[]{:S(2)}) collective-permute-start(bf16[32,3712]{1,0:T(8,128)(2,1)S(1)} %collective-permute-done.3.refs_6_), channel_id=1, source_target_pairs={{0,4},{4,8},{8,12},{12,14},{14,10},{10,6},{6,2},{2,0},{5,1},{9,5},... | collective-permute-start | bytes 712712 | tf_op jit(solution)/shard_map/ppermute | solution.py:171
  13.0 4.1 %collective-permute-start.1 = (bf16[32,3712]{1,0:T(8,128)(2,1)S(1)}, bf16[32,3712]{1,0:T(8,128)(2,1)S(1)}, u32[]{:S(2)}, u32[]{:S(2)}) collective-permute-start(bf16[32,3712]{1,0:T(8,128)(2,1)S(1)} %collective-permute-done.refs_5_), channel_id=1, source_target_pairs={{0,1},{1,0},{2,3},{3,2},{4,5},{5,4},{6,7},{7,6},{8,9},{9,8},{10,11... | collective-permute-start | bytes 712712 | tf_op jit(solution)/shard_map/ppermute | solution.py:173
  14.5 6.1 %collective-permute-start.7 = (bf16[32,3712]{1,0:T(8,128)(2,1)S(1)}, bf16[32,3712]{1,0:T(8,128)(2,1)S(1)}, u32[]{:S(2)}, u32[]{:S(2)}) collective-permute-start(bf16[32,3712]{1,0:T(8,128)(2,1)S(1)} %collective-permute-done.5.refs_3_), channel_id=1, source_target_pairs={{0,4},{4,8},{8,12},{12,14},{14,10},{10,6},{6,2},{2,0},{5,1},{9,5},... | collective-permute-start | bytes 712712 | tf_op jit(solution)/shard_map/ppermute | solution.py:171
  16.5 4.0 %collective-permute-start.4 = (bf16[32,3712]{1,0:T(8,128)(2,1)S(1)}, bf16[32,3712]{1,0:T(8,128)(2,1)S(1)}, u32[]{:S(2)}, u32[]{:S(2)}) collective-permute-start(bf16[32,3712]{1,0:T(8,128)(2,1)S(1)} %collective-permute-done.3.refs_6_), channel_id=1, source_target_pairs={{0,1},{1,0},{2,3},{3,2},{4,5},{5,4},{6,7},{7,6},{8,9},{9,8},{10,11... | collective-permute-start | bytes 712712 | tf_op jit(solution)/shard_map/ppermute | solution.py:173
  16.6 10.3 %collective-permute-start.11 = (bf16[32,3712]{1,0:T(8,128)(2,1)S(1)}, bf16[32,3712]{1,0:T(8,128)(2,1)S(1)}, u32[]{:S(2)}, u32[]{:S(2)}) collective-permute-start(bf16[32,3712]{1,0:T(8,128)(2,1)S(1)} %collective-permute-done.5.refs_3_), channel_id=1, source_target_pairs={{0,1},{1,0},{2,3},{3,2},{4,5},{5,4},{6,7},{7,6},{8,9},{9,8},{10,11... | collective-permute-start | bytes 712712 | tf_op jit(solution)/shard_map/ppermute | solution.py:173
  17.1 9.8 %collective-permute-start.12 = (bf16[32,3712]{1,0:T(8,128)(2,1)S(1)}, bf16[32,3712]{1,0:T(8,128)(2,1)S(1)}, u32[]{:S(2)}, u32[]{:S(2)}) collective-permute-start(bf16[32,3712]{1,0:T(8,128)(2,1)S(1)} %collective-permute-done.6.refs_4_), channel_id=1, source_target_pairs={{0,1},{1,0},{2,3},{3,2},{4,5},{5,4},{6,7},{7,6},{8,9},{9,8},{10,11... | collective-permute-start | bytes 712712 | tf_op jit(solution)/shard_map/ppermute | solution.py:173
  17.1 9.8 %collective-permute-start.9 = (bf16[32,3712]{1,0:T(8,128)(2,1)S(1)}, bf16[32,3712]{1,0:T(8,128)(2,1)S(1)}, u32[]{:S(2)}, u32[]{:S(2)}) collective-permute-start(bf16[32,3712]{1,0:T(8,128)(2,1)S(1)} %collective-permute-done.6.refs_4_), channel_id=1, source_target_pairs={{0,4},{4,8},{8,12},{12,14},{14,10},{10,6},{6,2},{2,0},{5,1},{9,5},... | collective-permute-start | bytes 712712 | tf_op jit(solution)/shard_map/ppermute | solution.py:171
  20.6 6.3 %collective-permute-start.10 = (bf16[32,3712]{1,0:T(8,128)(2,1)S(1)}, bf16[32,3712]{1,0:T(8,128)(2,1)S(1)}, u32[]{:S(2)}, u32[]{:S(2)}) collective-permute-start(bf16[32,3712]{1,0:T(8,128)(2,1)S(1)} %collective-permute-done.7.refs_1_), channel_id=1, source_target_pairs={{0,1},{1,0},{2,3},{3,2},{4,5},{5,4},{6,7},{7,6},{8,9},{9,8},{10,11... | collective-permute-start | bytes 712712 | tf_op jit(solution)/shard_map/ppermute | solution.py:173
  20.6 6.3 %collective-permute-start.8 = (bf16[32,3712]{1,0:T(8,128)(2,1)S(1)}, bf16[32,3712]{1,0:T(8,128)(2,1)S(1)}, u32[]{:S(2)}, u32[]{:S(2)}) collective-permute-start(bf16[32,3712]{1,0:T(8,128)(2,1)S(1)} %collective-permute-done.7.refs_1_), channel_id=1, source_target_pairs={{0,4},{4,8},{8,12},{12,14},{14,10},{10,6},{6,2},{2,0},{5,1},{9,5},... | collective-permute-start | bytes 712712 | tf_op jit(solution)/shard_map/ppermute | solution.py:171
  22.7 4.8 %copy-start = (bf16[1,1024,3584]{2,1,0:T(8,128)(2,1)S(1)}, bf16[1,1024,3584]{2,1,0:T(8,128)(2,1)}, u32[]{:S(2)}) copy-start(bf16[1,1024,3584]{2,1,0:T(8,128)(2,1)} %refs_6_.1) | copy-start | bytes 22020100
  26.9 2.7 %collective-permute-start.13 = (bf16[32,3712]{1,0:T(8,128)(2,1)S(1)}, bf16[32,3712]{1,0:T(8,128)(2,1)S(1)}, u32[]{:S(2)}, u32[]{:S(2)}) collective-permute-start(bf16[32,3712]{1,0:T(8,128)(2,1)S(1)} %collective-permute-done.8.refs_3_.refs_0_), channel_id=1, source_target_pairs={{0,1},{1,0},{2,3},{3,2},{4,5},{5,4},{6,7},{7,6},{8,9},{9,8},{10,11... | collective-permute-start | bytes 712712 | tf_op jit(solution)/shard_map/ppermute | solution.py:173
  27.1 2.4 %collective-permute-start.14 = (bf16[32,3712]{1,0:T(8,128)(2,1)S(1)}, bf16[32,3712]{1,0:T(8,128)(2,1)S(1)}, u32[]{:S(2)}, u32[]{:S(2)}) collective-permute-start(bf16[32,3712]{1,0:T(8,128)(2,1)S(1)} %collective-permute-done.9.refs_2_), channel_id=1, source_target_pairs={{0,1},{1,0},{2,3},{3,2},{4,5},{5,4},{6,7},{7,6},{8,9},{9,8},{10,11... | collective-permute-start | bytes 712712 | tf_op jit(solution)/shard_map/ppermute | solution.py:173
  29.6 7.7 %collective-permute-start.15 = (bf16[160,3584]{1,0:T(8,128)(2,1)S(1)}, bf16[160,3584]{1,0:T(8,128)(2,1)S(1)}, u32[]{:S(2)}, u32[]{:S(2)}) collective-permute-start(bf16[160,3584]{1,0:T(8,128)(2,1)S(1)} %get-tuple-element.53), channel_id=1, source_target_pairs={{0,1},{1,0},{2,3},{3,2},{4,5},{5,4},{6,7},{7,6},{8,9},{9,8},{10,11... | collective-permute-start | bytes 3440648 | tf_op jit(solution)/shard_map/ppermute | solution.py:173
  35.3 2.0 %collective-permute-start.16 = (bf16[64,3584]{1,0:T(8,128)(2,1)S(1)}, bf16[64,3584]{1,0:T(8,128)(2,1)S(1)}, u32[]{:S(2)}, u32[]{:S(2)}) collective-permute-start(bf16[64,3584]{1,0:T(8,128)(2,1)S(1)} %get-tuple-element.56), channel_id=1, source_target_pairs={{0,1},{1,0},{2,3},{3,2},{4,5},{5,4},{6,7},{7,6},{8,9},{9,8},{10,11... | collective-permute-start | bytes 1376264 | tf_op jit(solution)/shard_map/ppermute | solution.py:173
  35.7 6.1 %collective-permute-start.18 = (bf16[32,3584]{1,0:T(8,128)(2,1)S(1)}, bf16[32,3584]{1,0:T(8,128)(2,1)S(1)}, u32[]{:S(2)}, u32[]{:S(2)}) collective-permute-start(bf16[32,3584]{1,0:T(8,128)(2,1)S(1)} %get-tuple-element.59), channel_id=1, source_target_pairs={{0,1},{1,0},{2,3},{3,2},{4,5},{5,4},{6,7},{7,6},{8,9},{9,8},{10,11... | collective-permute-start | bytes 688136 | tf_op jit(solution)/shard_map/ppermute | solution.py:173
  37.4 13.3 %collective-permute-start.20 = (bf16[32,3584]{1,0:T(8,128)(2,1)S(1)}, bf16[32,3584]{1,0:T(8,128)(2,1)S(1)}, u32[]{:S(2)}, u32[]{:S(2)}) collective-permute-start(bf16[32,3584]{1,0:T(8,128)(2,1)S(1)} %add_convert_fusion.7), channel_id=1, source_target_pairs={{0,8},{4,12},{8,14},{12,10},{14,6},{10,2},{6,0},{2,4},{5,3},{9,1},... | collective-permute-start | bytes 688136 | tf_op jit(solution)/shard_map/ppermute | solution.py:172
  40.2 7.8 %collective-permute-start.17 = (bf16[32,3584]{1,0:T(8,128)(2,1)S(1)}, bf16[32,3584]{1,0:T(8,128)(2,1)S(1)}, u32[]{:S(2)}, u32[]{:S(2)}) collective-permute-start(bf16[32,3584]{1,0:T(8,128)(2,1)S(1)} %add_convert_fusion.6), channel_id=1, source_target_pairs={{0,4},{4,8},{8,12},{12,14},{14,10},{10,6},{6,2},{2,0},{5,1},{9,5},... | collective-permute-start | bytes 688136 | tf_op jit(solution)/shard_map/ppermute | solution.py:171
  41.9 8.8 %collective-permute-start.21 = (bf16[32,3584]{1,0:T(8,128)(2,1)S(1)}, bf16[32,3584]{1,0:T(8,128)(2,1)S(1)}, u32[]{:S(2)}, u32[]{:S(2)}) collective-permute-start(bf16[32,3584]{1,0:T(8,128)(2,1)S(1)} %add_convert_fusion.5), channel_id=1, source_target_pairs={{0,4},{4,8},{8,12},{12,14},{14,10},{10,6},{6,2},{2,0},{5,1},{9,5},... | collective-permute-start | bytes 688136 | tf_op jit(solution)/shard_map/ppermute | solution.py:171
  48.1 6.1 %collective-permute-start.19 = (bf16[32,3584]{1,0:T(8,128)(2,1)S(1)}, bf16[32,3584]{1,0:T(8,128)(2,1)S(1)}, u32[]{:S(2)}, u32[]{:S(2)}) collective-permute-start(bf16[32,3584]{1,0:T(8,128)(2,1)S(1)} %add_convert_fusion.4), channel_id=1, source_target_pairs={{0,4},{4,8},{8,12},{12,14},{14,10},{10,6},{6,2},{2,0},{5,1},{9,5},... | collective-permute-start | bytes 688136 | tf_op jit(solution)/shard_map/ppermute | solution.py:171
  50.7 6.1 %collective-permute-start.23 = (bf16[32,3584]{1,0:T(8,128)(2,1)S(1)}, bf16[32,3584]{1,0:T(8,128)(2,1)S(1)}, u32[]{:S(2)}, u32[]{:S(2)}) collective-permute-start(bf16[32,3584]{1,0:T(8,128)(2,1)S(1)} %add_convert_fusion.3), channel_id=1, source_target_pairs={{0,4},{4,8},{8,12},{12,14},{14,10},{10,6},{6,2},{2,0},{5,1},{9,5},... | collective-permute-start | bytes 688136 | tf_op jit(solution)/shard_map/ppermute | solution.py:171
  54.2 6.1 %collective-permute-start.22 = (bf16[32,3584]{1,0:T(8,128)(2,1)S(1)}, bf16[32,3584]{1,0:T(8,128)(2,1)S(1)}, u32[]{:S(2)}, u32[]{:S(2)}) collective-permute-start(bf16[32,3584]{1,0:T(8,128)(2,1)S(1)} %add_convert_fusion.2), channel_id=1, source_target_pairs={{0,4},{4,8},{8,12},{12,14},{14,10},{10,6},{6,2},{2,0},{5,1},{9,5},... | collective-permute-start | bytes 688136 | tf_op jit(solution)/shard_map/ppermute | solution.py:171
  56.9 6.1 %collective-permute-start.25 = (bf16[32,3584]{1,0:T(8,128)(2,1)S(1)}, bf16[32,3584]{1,0:T(8,128)(2,1)S(1)}, u32[]{:S(2)}, u32[]{:S(2)}) collective-permute-start(bf16[32,3584]{1,0:T(8,128)(2,1)S(1)} %add_convert_fusion.1), channel_id=1, source_target_pairs={{0,4},{4,8},{8,12},{12,14},{14,10},{10,6},{6,2},{2,0},{5,1},{9,5},... | collective-permute-start | bytes 688136 | tf_op jit(solution)/shard_map/ppermute | solution.py:171
  60.3 2.7 %collective-permute-start.24 = (bf16[32,3584]{1,0:T(8,128)(2,1)S(1)}, bf16[32,3584]{1,0:T(8,128)(2,1)S(1)}, u32[]{:S(2)}, u32[]{:S(2)}) collective-permute-start(bf16[32,3584]{1,0:T(8,128)(2,1)S(1)} %collective-permute-done.22), channel_id=1, source_target_pairs={{0,1},{1,0},{2,3},{3,2},{4,5},{5,4},{6,7},{7,6},{8,9},{9,8},{10,11... | collective-permute-start | bytes 688136 | tf_op jit(solution)/shard_map/ppermute | solution.py:173

commit v18 on v16

--- a/solution.py
+++ b/solution.py
@@ -201,7 +201,8 @@
     h, kept[0], given[2], others = together((h, kept[0], given[2], others))
     kept[1], kept[3 : end - 2] = others[0], others[1:]
     given[0], kept[2] = sibling(kept[0]), sibling(given[2])
-    near, near_given = output(blocks, h, 0, [(3, F32), (5, BF16)], experts, w_down)
+    (near_given,) = output(blocks[3:], h, 3, [(5, BF16)], experts, w_down)
+    h_near, near_blocks = h, blocks[:3]
     given[0], kept[2], near_given = together((given[0], kept[2], near_given))
     near_sent = sibling(near_given)
 
@@ -213,7 +214,7 @@
     sent = [sibling(p) for p in pieces]
     (out,) = output(kept_blocks, h, len(give_last), [(len(keep_last), F32)], experts, w_down)
     out, near_sent = together((out, near_sent))
-    note(keep, near, give, [near_sent])
+    theirs.update({j: (near_sent, at) for at, j in enumerate(give)})
     note(keep_last, out, give_last, sent)
 
     def add(j, *arrived):
@@ -231,6 +232,11 @@
     sums_twin = []
     for j in range(1, end, 2):
         sums_twin = [send(add(j, *sums_twin))]
+        if j == 1:
+            h_near, _ = together((h_near, last))
+            (near,) = output(near_blocks, h_near, 0, [(3, F32)], experts, w_down)
+            near, sums = together((near, sums))
+            mine.update({k: (near, at) for at, k in enumerate(keep)})
         sums = send(add(j + 1, sums))
     piece, sums = together((theirs[end][0], sums))
     total = block(*mine[end]) + block(piece, theirs[end][1]).astype(F32) + sums.astype(F32)

time: 62.8 us -> 62.2 us (level)
  waiting for transfers between devices: 17.7 us -> 16.3 us
  Pallas kernels: 14.2 us -> 14.9 us
    ppermute x14, waiting for transfers between devices: 17.7 us -> 16.3 us  [local(): send = lambda a: lax.ppermute(a, 'node', spin)]
    pallas_call x3 -> x4, Pallas kernels: 4.81 us -> 5.45 us  [output(): pl.pallas_call(functools.partial(output_kernel, count, experts, tiles(wid...]
  transfers between devices with their start and end apart: 26 -> 26, of which waited for: 11 -> 11; matrix products, arithmetic and copies ran while one was open for 1% -> 1% of each run, Pallas kernels for 21% -> 22%
where the time goes in v18:
time: 62.2 us; the launch traced here: 62.1 us
  starting transfers between devices  29.3 us (47%)
  waiting for transfers between devices  16.3 us (26%)
  Pallas kernels  14.9 us (24%)
  other arithmetic  1.35 us (2%)
    ppermute x14, starting transfers between devices, local(): send = lambda a: lax.ppermute(a, 'node', spin)  26.9 us
    ppermute x14, waiting for transfers between devices, local(): send = lambda a: lax.ppermute(a, 'node', spin)  16.3 us
    pallas_call x2, Pallas kernels, hidden(): pl.pallas_call(functools.partial(hidden_kernel, count, tiles(width, ff)[0...  8.27 us
    pallas_call x4, Pallas kernels, output(): pl.pallas_call(functools.partial(output_kernel, count, experts, tiles(wid...  5.45 us
    ppermute x12, starting transfers between devices, local(): sibling = lambda a: lax.ppermute(a, 'node', swap)  2.43 us
  transfers between devices with their start and end apart: 26, of which 11 were waited for; matrix products, arithmetic and copies ran while one was open for 1% of the time, Pallas kernels for 22%

profile of v18, /device:TPU:0, one launch (start us, length us, event | category | flops | bytes accessed | tf_op | source)
XLA Modules:
  0.0 62.1 jit_solution(16938555053750236105)
XLA Ops:
  0.0 1.1 %shard_map.64.refs_2_ = bf16[32,3712]{1,0:T(8,128)(2,1)S(1)} custom-call(bf16[32,3584]{1,0:T(8,128)(2,1)} %tok_hbm.1, s32[8,32]{1,0:T(8,128)} %bitcast.6, f32[8,32]{1,0:T(8,128)} %bitcast.7), custom_call_target="tpu_custom_call" | custom-call | flops 10737418240 | tf_op jit(solution)/shard_map/pallas_call | solution.py:59
  1.2 0.5 collective-permute-start.2
  1.7 2.6 %collective-permute-start = (bf16[32,3712]{1,0:T(8,128)(2,1)S(1)}, bf16[32,3712]{1,0:T(8,128)(2,1)S(1)}, u32[]{:S(2)}, u32[]{:S(2)}) collective-permute-start(bf16[32,3712]{1,0:T(8,128)(2,1)S(1)} %shard_map.64.refs_2_), channel_id=1, source_target_pairs={{0,4},{4,8},{8,12},{12,14},{14,10},{10,6},{6,2},{2,0},{5,1},{9,5},... | collective-permute-start | bytes 712712 | tf_op jit(solution)/shard_map/ppermute | solution.py:170
  4.3 1.6 %collective-permute-start.3 = (bf16[32,3712]{1,0:T(8,128)(2,1)S(1)}, bf16[32,3712]{1,0:T(8,128)(2,1)S(1)}, u32[]{:S(2)}, u32[]{:S(2)}) collective-permute-start(bf16[32,3712]{1,0:T(8,128)(2,1)S(1)} %collective-permute-done.2.refs_7_.refs_4_), channel_id=1, source_target_pairs={{0,4},{4,8},{8,12},{12,14},{14,10},{10,6},{6,2},{2,0},{5,1},{9,5},... | collective-permute-start | bytes 712712 | tf_op jit(solution)/shard_map/ppermute | solution.py:170
  5.9 2.5 %collective-permute-done.refs_5_.refs_2_ = bf16[32,3712]{1,0:T(8,128)(2,1)S(1)} collective-permute-done((bf16[32,3712]{1,0:T(8,128)(2,1)S(1)}, bf16[32,3712]{1,0:T(8,128)(2,1)S(1)}, u32[]{:S(2)}, u32[]{:S(2)}) %collective-permute-start) | collective-permute-done | bytes 237600 | tf_op jit(solution)/shard_map/ppermute | solution.py:170
  8.4 2.1 %collective-permute-start.5 = (bf16[32,3712]{1,0:T(8,128)(2,1)S(1)}, bf16[32,3712]{1,0:T(8,128)(2,1)S(1)}, u32[]{:S(2)}, u32[]{:S(2)}) collective-permute-start(bf16[32,3712]{1,0:T(8,128)(2,1)S(1)} %collective-permute-done.refs_5_.refs_2_), channel_id=1, source_target_pairs={{0,4},{4,8},{8,12},{12,14},{14,10},{10,6},{6,2},{2,0},{5,1},{9,5},... | collective-permute-start | bytes 712712 | tf_op jit(solution)/shard_map/ppermute | solution.py:170
  10.4 0.5 collective-permute-done.3.refs_6_.refs_3_
  10.9 2.1 %collective-permute-start.6 = (bf16[32,3712]{1,0:T(8,128)(2,1)S(1)}, bf16[32,3712]{1,0:T(8,128)(2,1)S(1)}, u32[]{:S(2)}, u32[]{:S(2)}) collective-permute-start(bf16[32,3712]{1,0:T(8,128)(2,1)S(1)} %collective-permute-done.3.refs_6_.refs_3_), channel_id=1, source_target_pairs={{0,4},{4,8},{8,12},{12,14},{14,10},{10,6},{6,2},{2,0},{5,1},{9,5},... | collective-permute-start | bytes 712712 | tf_op jit(solution)/shard_map/ppermute | solution.py:170
  13.0 1.5 %collective-permute-done.5.refs_3_.refs_0_ = bf16[32,3712]{1,0:T(8,128)(2,1)S(1)} collective-permute-done((bf16[32,3712]{1,0:T(8,128)(2,1)S(1)}, bf16[32,3712]{1,0:T(8,128)(2,1)S(1)}, u32[]{:S(2)}, u32[]{:S(2)}) %collective-permute-start.5) | collective-permute-done | bytes 237600 | tf_op jit(solution)/shard_map/ppermute | solution.py:170
  14.5 2.1 %collective-permute-start.7 = (bf16[32,3712]{1,0:T(8,128)(2,1)S(1)}, bf16[32,3712]{1,0:T(8,128)(2,1)S(1)}, u32[]{:S(2)}, u32[]{:S(2)}) collective-permute-start(bf16[32,3712]{1,0:T(8,128)(2,1)S(1)} %collective-permute-done.5.refs_3_.refs_0_), channel_id=1, source_target_pairs={{0,4},{4,8},{8,12},{12,14},{14,10},{10,6},{6,2},{2,0},{5,1},{9,5},... | collective-permute-start | bytes 712712 | tf_op jit(solution)/shard_map/ppermute | solution.py:170
  16.6 0.5 collective-permute-start.11
  17.1 2.0 %collective-permute-start.9 = (bf16[32,3712]{1,0:T(8,128)(2,1)S(1)}, bf16[32,3712]{1,0:T(8,128)(2,1)S(1)}, u32[]{:S(2)}, u32[]{:S(2)}) collective-permute-start(bf16[32,3712]{1,0:T(8,128)(2,1)S(1)} %collective-permute-done.6.refs_4_.refs_1_), channel_id=1, source_target_pairs={{0,4},{4,8},{8,12},{12,14},{14,10},{10,6},{6,2},{2,0},{5,1},{9,5},... | collective-permute-start | bytes 712712 | tf_op jit(solution)/shard_map/ppermute | solution.py:170
  19.1 1.5 %collective-permute-done.7.refs_1_ = bf16[32,3712]{1,0:T(8,128)(2,1)S(1)} collective-permute-done((bf16[32,3712]{1,0:T(8,128)(2,1)S(1)}, bf16[32,3712]{1,0:T(8,128)(2,1)S(1)}, u32[]{:S(2)}, u32[]{:S(2)}) %collective-permute-start.7) | collective-permute-done | bytes 237600 | tf_op jit(solution)/shard_map/ppermute | solution.py:170
  20.6 2.1 %collective-permute-start.8 = (bf16[32,3712]{1,0:T(8,128)(2,1)S(1)}, bf16[32,3712]{1,0:T(8,128)(2,1)S(1)}, u32[]{:S(2)}, u32[]{:S(2)}) collective-permute-start(bf16[32,3712]{1,0:T(8,128)(2,1)S(1)} %collective-permute-done.7.refs_1_), channel_id=1, source_target_pairs={{0,4},{4,8},{8,12},{12,14},{14,10},{10,6},{6,2},{2,0},{5,1},{9,5},... | collective-permute-start | bytes 712712 | tf_op jit(solution)/shard_map/ppermute | solution.py:170
  22.7 0.0 copy-start
  22.7 4.1 %shard_map.65.refs_5_.refs_3_ = bf16[256,1024]{1,0:T(8,128)(2,1)S(1)} custom-call(bf16[32,3712]{1,0:T(8,128)(2,1)S(1)} %collective-permute-done.1.refs_0_, bf16[32,3712]{1,0:T(8,128)(2,1)S(1)} %collective-permute-done.4.refs_1_, bf16[32,3712]{1,0:T(8,128)(2,1)S(1)} %shard_map.64.refs_2_, bf16[32,3712]{1,0:T(8,128)(2,1)S(1)} %collective-permute-done.5.refs_3_.refs_0_, ...), custom_call_target="tpu_custom_call" | custom-call | flops 3758096384 | tf_op jit(solution)/shard_map/pallas_call | solution.py:126
  26.9 0.2 collective-permute-start.13
  27.1 0.3 collective-permute-start.14
  27.5 1.4 %shard_map.66 = bf16[160,3584]{1,0:T(8,128)(2,1)S(1)} custom-call(bf16[32,3712]{1,0:T(8,128)(2,1)S(1)} %collective-permute-done.5.refs_3_.refs_0_, bf16[32,3712]{1,0:T(8,128)(2,1)S(1)} %collective-permute-done.6.refs_4_.refs_1_, bf16[32,3712]{1,0:T(8,128)(2,1)S(1)} %collective-permute-done.refs_5_.refs_2_, ...), custom_call_target="tpu_custom_call" | custom-call | flops 1879048192 | tf_op jit(solution)/shard_map/pallas_call | solution.py:150
  28.9 0.2 collective-permute-start.15
  29.1 4.1 %shard_map.67.refs_3_.refs_5_ = bf16[256,1024]{1,0:T(8,128)(2,1)S(1)} custom-call(bf16[32,3712]{1,0:T(8,128)(2,1)S(1)} %collective-permute-done.13.refs_0_, bf16[32,3712]{1,0:T(8,128)(2,1)S(1)} %collective-permute-done.7.refs_1_, bf16[32,3712]{1,0:T(8,128)(2,1)S(1)} %collective-permute-done.9.refs_2_, ...), custom_call_target="tpu_custom_call" | custom-call | flops 3758096384 | tf_op jit(solution)/shard_map/pallas_call | solution.py:126
  33.3 1.3 %shard_map.68 = (bf16[64,3584]{1,0:T(8,128)(2,1)S(1)}, bf16[32,3584]{1,0:T(8,128)(2,1)S(1)}) custom-call(bf16[32,3712]{1,0:T(8,128)(2,1)S(1)} %collective-permute-done.13.refs_0_, bf16[32,3712]{1,0:T(8,128)(2,1)S(1)} %collective-permute-done.7.refs_1_, bf16[32,3712]{1,0:T(8,128)(2,1)S(1)} %collective-permute-done.9.refs_2_, ...), custom_call_target="tpu_custom_call" | custom-call | flops 1879048192 | tf_op jit(solution)/shard_map/pallas_call | solution.py:150
  34.6 0.4 collective-permute-start.16
  35.0 0.2 collective-permute-start.19
  35.2 1.4 %shard_map.69 = f32[160,3584]{1,0:T(8,128)S(1)} custom-call(bf16[32,3712]{1,0:T(8,128)(2,1)S(1)} %collective-permute-done.8.refs_3_.refs_0_, bf16[32,3712]{1,0:T(8,128)(2,1)S(1)} %collective-permute-done.10.refs_4_.refs_1_, bf16[32,3712]{1,0:T(8,128)(2,1)S(1)} %collective-permute-done.14.refs_5_.refs_2_, ...), custom_call_target="tpu_custom_call" | custom-call | flops 1879048192 | tf_op jit(solution)/shard_map/pallas_call | solution.py:150
  36.6 0.1 add_convert_fusion.7
  36.7 1.8 %collective-permute-start.17 = (bf16[32,3584]{1,0:T(8,128)(2,1)S(1)}, bf16[32,3584]{1,0:T(8,128)(2,1)S(1)}, u32[]{:S(2)}, u32[]{:S(2)}) collective-permute-start(bf16[32,3584]{1,0:T(8,128)(2,1)S(1)} %add_convert_fusion.7), channel_id=1, source_target_pairs={{0,4},{4,8},{8,12},{12,14},{14,10},{10,6},{6,2},{2,0},{5,1},{9,5},... | collective-permute-start | bytes 688136 | tf_op jit(solution)/shard_map/ppermute | solution.py:170
  38.5 1.6 %collective-permute-start.18 = (bf16[32,3584]{1,0:T(8,128)(2,1)S(1)}, bf16[32,3584]{1,0:T(8,128)(2,1)S(1)}, u32[]{:S(2)}, u32[]{:S(2)}) collective-permute-start(bf16[32,3584]{1,0:T(8,128)(2,1)S(1)} %add_convert_fusion.6), channel_id=1, source_target_pairs={{0,4},{4,8},{8,12},{12,14},{14,10},{10,6},{6,2},{2,0},{5,1},{9,5},... | collective-permute-start | bytes 688136 | tf_op jit(solution)/shard_map/ppermute | solution.py:170
  40.1 1.3 %shard_map.70 = f32[96,3584]{1,0:T(8,128)S(1)} custom-call(bf16[32,3712]{1,0:T(8,128)(2,1)S(1)} %collective-permute-done.1.refs_0_, bf16[32,3712]{1,0:T(8,128)(2,1)S(1)} %collective-permute-done.4.refs_1_, bf16[32,3712]{1,0:T(8,128)(2,1)S(1)} %shard_map.64.refs_2_, bf16[256,1024]{1,0:T(8,128)(2,1)S(1)} %shard_map.65.refs_5_.refs_3_, ...), custom_call_target="tpu_custom_call" | custom-call | flops 1879048192 | tf_op jit(solution)/shard_map/pallas_call | solution.py:150
  41.4 1.3 %collective-permute-done.17 = bf16[32,3584]{1,0:T(8,128)(2,1)S(1)} collective-permute-done((bf16[32,3584]{1,0:T(8,128)(2,1)S(1)}, bf16[32,3584]{1,0:T(8,128)(2,1)S(1)}, u32[]{:S(2)}, u32[]{:S(2)}) %collective-permute-start.17) | collective-permute-done | bytes 229408 | tf_op jit(solution)/shard_map/ppermute | solution.py:170
  42.7 0.1 add_convert_fusion.5
  42.8 1.8 %collective-permute-start.21 = (bf16[32,3584]{1,0:T(8,128)(2,1)S(1)}, bf16[32,3584]{1,0:T(8,128)(2,1)S(1)}, u32[]{:S(2)}, u32[]{:S(2)}) collective-permute-start(bf16[32,3584]{1,0:T(8,128)(2,1)S(1)} %add_convert_fusion.5), channel_id=1, source_target_pairs={{0,4},{4,8},{8,12},{12,14},{14,10},{10,6},{6,2},{2,0},{5,1},{9,5},... | collective-permute-start | bytes 688136 | tf_op jit(solution)/shard_map/ppermute | solution.py:170
  44.6 0.6 collective-permute-done.18
  45.2 0.1 add_convert_fusion.4
  45.3 1.8 %collective-permute-start.20 = (bf16[32,3584]{1,0:T(8,128)(2,1)S(1)}, bf16[32,3584]{1,0:T(8,128)(2,1)S(1)}, u32[]{:S(2)}, u32[]{:S(2)}) collective-permute-start(bf16[32,3584]{1,0:T(8,128)(2,1)S(1)} %add_convert_fusion.4), channel_id=1, source_target_pairs={{0,4},{4,8},{8,12},{12,14},{14,10},{10,6},{6,2},{2,0},{5,1},{9,5},... | collective-permute-start | bytes 688136 | tf_op jit(solution)/shard_map/ppermute | solution.py:170
  47.1 1.8 %collective-permute-done.21 = bf16[32,3584]{1,0:T(8,128)(2,1)S(1)} collective-permute-done((bf16[32,3584]{1,0:T(8,128)(2,1)S(1)}, bf16[32,3584]{1,0:T(8,128)(2,1)S(1)}, u32[]{:S(2)}, u32[]{:S(2)}) %collective-permute-start.21) | collective-permute-done | bytes 229408 | tf_op jit(solution)/shard_map/ppermute | solution.py:170
  48.9 0.1 add_convert_fusion.3
  49.0 1.8 %collective-permute-start.24 = (bf16[32,3584]{1,0:T(8,128)(2,1)S(1)}, bf16[32,3584]{1,0:T(8,128)(2,1)S(1)}, u32[]{:S(2)}, u32[]{:S(2)}) collective-permute-start(bf16[32,3584]{1,0:T(8,128)(2,1)S(1)} %add_convert_fusion.3), channel_id=1, source_target_pairs={{0,4},{4,8},{8,12},{12,14},{14,10},{10,6},{6,2},{2,0},{5,1},{9,5},... | collective-permute-start | bytes 688136 | tf_op jit(solution)/shard_map/ppermute | solution.py:170
  50.8 0.6 collective-permute-done.20
  51.4 0.1 add_convert_fusion.2
  51.5 1.8 %collective-permute-start.22 = (bf16[32,3584]{1,0:T(8,128)(2,1)S(1)}, bf16[32,3584]{1,0:T(8,128)(2,1)S(1)}, u32[]{:S(2)}, u32[]{:S(2)}) collective-permute-start(bf16[32,3584]{1,0:T(8,128)(2,1)S(1)} %add_convert_fusion.2), channel_id=1, source_target_pairs={{0,4},{4,8},{8,12},{12,14},{14,10},{10,6},{6,2},{2,0},{5,1},{9,5},... | collective-permute-start | bytes 688136 | tf_op jit(solution)/shard_map/ppermute | solution.py:170
  53.2 1.8 %collective-permute-done.24 = bf16[32,3584]{1,0:T(8,128)(2,1)S(1)} collective-permute-done((bf16[32,3584]{1,0:T(8,128)(2,1)S(1)}, bf16[32,3584]{1,0:T(8,128)(2,1)S(1)}, u32[]{:S(2)}, u32[]{:S(2)}) %collective-permute-start.24) | collective-permute-done | bytes 229408 | tf_op jit(solution)/shard_map/ppermute | solution.py:170
  55.1 0.1 add_convert_fusion.1
  55.2 1.8 %collective-permute-start.25 = (bf16[32,3584]{1,0:T(8,128)(2,1)S(1)}, bf16[32,3584]{1,0:T(8,128)(2,1)S(1)}, u32[]{:S(2)}, u32[]{:S(2)}) collective-permute-start(bf16[32,3584]{1,0:T(8,128)(2,1)S(1)} %add_convert_fusion.1), channel_id=1, source_target_pairs={{0,4},{4,8},{8,12},{12,14},{14,10},{10,6},{6,2},{2,0},{5,1},{9,5},... | collective-permute-start | bytes 688136 | tf_op jit(solution)/shard_map/ppermute | solution.py:170
  56.9 0.6 collective-permute-done.22
  57.5 3.7 %collective-permute-done.25 = bf16[32,3584]{1,0:T(8,128)(2,1)S(1)} collective-permute-done((bf16[32,3584]{1,0:T(8,128)(2,1)S(1)}, bf16[32,3584]{1,0:T(8,128)(2,1)S(1)}, u32[]{:S(2)}, u32[]{:S(2)}) %collective-permute-start.25) | collective-permute-done | bytes 229408 | tf_op jit(solution)/shard_map/ppermute | solution.py:170
  61.2 0.1 convert_add_fusion
  61.3 0.7 %add_convert_fusion = bf16[32,3584]{1,0:T(8,128)(2,1)} fusion(f32[32,3584]{1,0:T(8,128)S(1)} %convert_add_fusion, bf16[32,3584]{1,0:T(8,128)(2,1)S(1)} %collective-permute-done.23), kind=kLoop, calls=%fused_computation | loop fusion | flops 344064 | bytes 917504 | tf_op jit(solution)/shard_map/convert_element_type | solution.py:246
  (32 shorter events, 0.1 us)
Async XLA Ops:
  0.0 22.7 %slice-start = ((s8[7340032]{0:T(1024)(128)(4,1)}), s8[4194304]{0:T(1024)(128)(4,1)S(1)}, s32[]{:S(2)}) async-start(s8[7340032]{0:T(1024)(128)(4,1)} %bitcast.2), calls=%async_computation | async-start | bytes 8388608
  0.0 22.7 %slice-start.2 = ((s8[7340032]{0:T(1024)(128)(4,1)}), s8[4194304]{0:T(1024)(128)(4,1)S(1)}, s32[]{:S(2)}) async-start(s8[7340032]{0:T(1024)(128)(4,1)} %bitcast.4), calls=%async_computation.2 | async-start | bytes 8388608
  0.0 22.7 %slice-start.1 = ((s8[7340032]{0:T(1024)(128)(4,1)}), s8[3145728]{0:T(1024)(128)(4,1)S(1)}, s32[]{:S(2)}) async-start(s8[7340032]{0:T(1024)(128)(4,1)} %bitcast.2), calls=%async_computation.1 | async-start | bytes 6291456
  0.0 22.7 %slice-start.3 = ((s8[7340032]{0:T(1024)(128)(4,1)}), s8[3145728]{0:T(1024)(128)(4,1)S(1)}, s32[]{:S(2)}) async-start(s8[7340032]{0:T(1024)(128)(4,1)} %bitcast.4), calls=%async_computation.3 | async-start | bytes 6291456
  1.2 3.2 %collective-permute-start.2 = (bf16[32,3712]{1,0:T(8,128)(2,1)S(1)}, bf16[32,3712]{1,0:T(8,128)(2,1)S(1)}, u32[]{:S(2)}, u32[]{:S(2)}) collective-permute-start(bf16[32,3712]{1,0:T(8,128)(2,1)S(1)} %shard_map.64.refs_2_), channel_id=1, source_target_pairs={{0,1},{1,0},{2,3},{3,2},{4,5},{5,4},{6,7},{7,6},{8,9},{9,8},{10,11... | collective-permute-start | bytes 712712 | tf_op jit(solution)/shard_map/ppermute | solution.py:171
  1.7 6.7 %collective-permute-start = (bf16[32,3712]{1,0:T(8,128)(2,1)S(1)}, bf16[32,3712]{1,0:T(8,128)(2,1)S(1)}, u32[]{:S(2)}, u32[]{:S(2)}) collective-permute-start(bf16[32,3712]{1,0:T(8,128)(2,1)S(1)} %shard_map.64.refs_2_), channel_id=1, source_target_pairs={{0,4},{4,8},{8,12},{12,14},{14,10},{10,6},{6,2},{2,0},{5,1},{9,5},... | collective-permute-start | bytes 712712 | tf_op jit(solution)/shard_map/ppermute | solution.py:170
  4.3 6.6 %collective-permute-start.3 = (bf16[32,3712]{1,0:T(8,128)(2,1)S(1)}, bf16[32,3712]{1,0:T(8,128)(2,1)S(1)}, u32[]{:S(2)}, u32[]{:S(2)}) collective-permute-start(bf16[32,3712]{1,0:T(8,128)(2,1)S(1)} %collective-permute-done.2.refs_7_.refs_4_), channel_id=1, source_target_pairs={{0,4},{4,8},{8,12},{12,14},{14,10},{10,6},{6,2},{2,0},{5,1},{9,5},... | collective-permute-start | bytes 712712 | tf_op jit(solution)/shard_map/ppermute | solution.py:170
  8.4 6.1 %collective-permute-start.5 = (bf16[32,3712]{1,0:T(8,128)(2,1)S(1)}, bf16[32,3712]{1,0:T(8,128)(2,1)S(1)}, u32[]{:S(2)}, u32[]{:S(2)}) collective-permute-start(bf16[32,3712]{1,0:T(8,128)(2,1)S(1)} %collective-permute-done.refs_5_.refs_2_), channel_id=1, source_target_pairs={{0,4},{4,8},{8,12},{12,14},{14,10},{10,6},{6,2},{2,0},{5,1},{9,5},... | collective-permute-start | bytes 712712 | tf_op jit(solution)/shard_map/ppermute | solution.py:170
  10.9 6.2 %collective-permute-start.6 = (bf16[32,3712]{1,0:T(8,128)(2,1)S(1)}, bf16[32,3712]{1,0:T(8,128)(2,1)S(1)}, u32[]{:S(2)}, u32[]{:S(2)}) collective-permute-start(bf16[32,3712]{1,0:T(8,128)(2,1)S(1)} %collective-permute-done.3.refs_6_.refs_3_), channel_id=1, source_target_pairs={{0,4},{4,8},{8,12},{12,14},{14,10},{10,6},{6,2},{2,0},{5,1},{9,5},... | collective-permute-start | bytes 712712 | tf_op jit(solution)/shard_map/ppermute | solution.py:170
  13.0 4.1 %collective-permute-start.1 = (bf16[32,3712]{1,0:T(8,128)(2,1)S(1)}, bf16[32,3712]{1,0:T(8,128)(2,1)S(1)}, u32[]{:S(2)}, u32[]{:S(2)}) collective-permute-start(bf16[32,3712]{1,0:T(8,128)(2,1)S(1)} %collective-permute-done.refs_5_.refs_2_), channel_id=1, source_target_pairs={{0,1},{1,0},{2,3},{3,2},{4,5},{5,4},{6,7},{7,6},{8,9},{9,8},{10,11... | collective-permute-start | bytes 712712 | tf_op jit(solution)/shard_map/ppermute | solution.py:171
  14.5 6.1 %collective-permute-start.7 = (bf16[32,3712]{1,0:T(8,128)(2,1)S(1)}, bf16[32,3712]{1,0:T(8,128)(2,1)S(1)}, u32[]{:S(2)}, u32[]{:S(2)}) collective-permute-start(bf16[32,3712]{1,0:T(8,128)(2,1)S(1)} %collective-permute-done.5.refs_3_.refs_0_), channel_id=1, source_target_pairs={{0,4},{4,8},{8,12},{12,14},{14,10},{10,6},{6,2},{2,0},{5,1},{9,5},... | collective-permute-start | bytes 712712 | tf_op jit(solution)/shard_map/ppermute | solution.py:170
  16.5 4.0 %collective-permute-start.4 = (bf16[32,3712]{1,0:T(8,128)(2,1)S(1)}, bf16[32,3712]{1,0:T(8,128)(2,1)S(1)}, u32[]{:S(2)}, u32[]{:S(2)}) collective-permute-start(bf16[32,3712]{1,0:T(8,128)(2,1)S(1)} %collective-permute-done.3.refs_6_.refs_3_), channel_id=1, source_target_pairs={{0,1},{1,0},{2,3},{3,2},{4,5},{5,4},{6,7},{7,6},{8,9},{9,8},{10,11... | collective-permute-start | bytes 712712 | tf_op jit(solution)/shard_map/ppermute | solution.py:171
  16.6 10.3 %collective-permute-start.11 = (bf16[32,3712]{1,0:T(8,128)(2,1)S(1)}, bf16[32,3712]{1,0:T(8,128)(2,1)S(1)}, u32[]{:S(2)}, u32[]{:S(2)}) collective-permute-start(bf16[32,3712]{1,0:T(8,128)(2,1)S(1)} %collective-permute-done.5.refs_3_.refs_0_), channel_id=1, source_target_pairs={{0,1},{1,0},{2,3},{3,2},{4,5},{5,4},{6,7},{7,6},{8,9},{9,8},{10,11... | collective-permute-start | bytes 712712 | tf_op jit(solution)/shard_map/ppermute | solution.py:171
  17.1 9.8 %collective-permute-start.12 = (bf16[32,3712]{1,0:T(8,128)(2,1)S(1)}, bf16[32,3712]{1,0:T(8,128)(2,1)S(1)}, u32[]{:S(2)}, u32[]{:S(2)}) collective-permute-start(bf16[32,3712]{1,0:T(8,128)(2,1)S(1)} %collective-permute-done.6.refs_4_.refs_1_), channel_id=1, source_target_pairs={{0,1},{1,0},{2,3},{3,2},{4,5},{5,4},{6,7},{7,6},{8,9},{9,8},{10,11... | collective-permute-start | bytes 712712 | tf_op jit(solution)/shard_map/ppermute | solution.py:171
  17.1 9.8 %collective-permute-start.9 = (bf16[32,3712]{1,0:T(8,128)(2,1)S(1)}, bf16[32,3712]{1,0:T(8,128)(2,1)S(1)}, u32[]{:S(2)}, u32[]{:S(2)}) collective-permute-start(bf16[32,3712]{1,0:T(8,128)(2,1)S(1)} %collective-permute-done.6.refs_4_.refs_1_), channel_id=1, source_target_pairs={{0,4},{4,8},{8,12},{12,14},{14,10},{10,6},{6,2},{2,0},{5,1},{9,5},... | collective-permute-start | bytes 712712 | tf_op jit(solution)/shard_map/ppermute | solution.py:170
  20.6 6.3 %collective-permute-start.10 = (bf16[32,3712]{1,0:T(8,128)(2,1)S(1)}, bf16[32,3712]{1,0:T(8,128)(2,1)S(1)}, u32[]{:S(2)}, u32[]{:S(2)}) collective-permute-start(bf16[32,3712]{1,0:T(8,128)(2,1)S(1)} %collective-permute-done.7.refs_1_), channel_id=1, source_target_pairs={{0,1},{1,0},{2,3},{3,2},{4,5},{5,4},{6,7},{7,6},{8,9},{9,8},{10,11... | collective-permute-start | bytes 712712 | tf_op jit(solution)/shard_map/ppermute | solution.py:171
  20.6 6.3 %collective-permute-start.8 = (bf16[32,3712]{1,0:T(8,128)(2,1)S(1)}, bf16[32,3712]{1,0:T(8,128)(2,1)S(1)}, u32[]{:S(2)}, u32[]{:S(2)}) collective-permute-start(bf16[32,3712]{1,0:T(8,128)(2,1)S(1)} %collective-permute-done.7.refs_1_), channel_id=1, source_target_pairs={{0,4},{4,8},{8,12},{12,14},{14,10},{10,6},{6,2},{2,0},{5,1},{9,5},... | collective-permute-start | bytes 712712 | tf_op jit(solution)/shard_map/ppermute | solution.py:170
  22.7 4.8 %copy-start = (bf16[1,1024,3584]{2,1,0:T(8,128)(2,1)S(1)}, bf16[1,1024,3584]{2,1,0:T(8,128)(2,1)}, u32[]{:S(2)}) copy-start(bf16[1,1024,3584]{2,1,0:T(8,128)(2,1)} %refs_4_.3) | copy-start | bytes 22020100
  26.9 2.0 %collective-permute-start.13 = (bf16[32,3712]{1,0:T(8,128)(2,1)S(1)}, bf16[32,3712]{1,0:T(8,128)(2,1)S(1)}, u32[]{:S(2)}, u32[]{:S(2)}) collective-permute-start(bf16[32,3712]{1,0:T(8,128)(2,1)S(1)} %collective-permute-done.8.refs_3_.refs_0_), channel_id=1, source_target_pairs={{0,1},{1,0},{2,3},{3,2},{4,5},{5,4},{6,7},{7,6},{8,9},{9,8},{10,11... | collective-permute-start | bytes 712712 | tf_op jit(solution)/shard_map/ppermute | solution.py:171
  27.1 1.8 %collective-permute-start.14 = (bf16[32,3712]{1,0:T(8,128)(2,1)S(1)}, bf16[32,3712]{1,0:T(8,128)(2,1)S(1)}, u32[]{:S(2)}, u32[]{:S(2)}) collective-permute-start(bf16[32,3712]{1,0:T(8,128)(2,1)S(1)} %collective-permute-done.9.refs_2_), channel_id=1, source_target_pairs={{0,1},{1,0},{2,3},{3,2},{4,5},{5,4},{6,7},{7,6},{8,9},{9,8},{10,11... | collective-permute-start | bytes 712712 | tf_op jit(solution)/shard_map/ppermute | solution.py:171
  28.9 7.7 %collective-permute-start.15 = (bf16[160,3584]{1,0:T(8,128)(2,1)S(1)}, bf16[160,3584]{1,0:T(8,128)(2,1)S(1)}, u32[]{:S(2)}, u32[]{:S(2)}) collective-permute-start(bf16[160,3584]{1,0:T(8,128)(2,1)S(1)} %shard_map.66), channel_id=1, source_target_pairs={{0,1},{1,0},{2,3},{3,2},{4,5},{5,4},{6,7},{7,6},{8,9},{9,8},{10,11... | collective-permute-start | bytes 3440648 | tf_op jit(solution)/shard_map/ppermute | solution.py:171
  34.6 2.0 %collective-permute-start.16 = (bf16[64,3584]{1,0:T(8,128)(2,1)S(1)}, bf16[64,3584]{1,0:T(8,128)(2,1)S(1)}, u32[]{:S(2)}, u32[]{:S(2)}) collective-permute-start(bf16[64,3584]{1,0:T(8,128)(2,1)S(1)} %get-tuple-element.53), channel_id=1, source_target_pairs={{0,1},{1,0},{2,3},{3,2},{4,5},{5,4},{6,7},{7,6},{8,9},{9,8},{10,11... | collective-permute-start | bytes 1376264 | tf_op jit(solution)/shard_map/ppermute | solution.py:171
  35.0 7.7 %collective-permute-start.19 = (bf16[32,3584]{1,0:T(8,128)(2,1)S(1)}, bf16[32,3584]{1,0:T(8,128)(2,1)S(1)}, u32[]{:S(2)}, u32[]{:S(2)}) collective-permute-start(bf16[32,3584]{1,0:T(8,128)(2,1)S(1)} %get-tuple-element.59), channel_id=1, source_target_pairs={{0,1},{1,0},{2,3},{3,2},{4,5},{5,4},{6,7},{7,6},{8,9},{9,8},{10,11... | collective-permute-start | bytes 688136 | tf_op jit(solution)/shard_map/ppermute | solution.py:171
  36.7 6.1 %collective-permute-start.17 = (bf16[32,3584]{1,0:T(8,128)(2,1)S(1)}, bf16[32,3584]{1,0:T(8,128)(2,1)S(1)}, u32[]{:S(2)}, u32[]{:S(2)}) collective-permute-start(bf16[32,3584]{1,0:T(8,128)(2,1)S(1)} %add_convert_fusion.7), channel_id=1, source_target_pairs={{0,4},{4,8},{8,12},{12,14},{14,10},{10,6},{6,2},{2,0},{5,1},{9,5},... | collective-permute-start | bytes 688136 | tf_op jit(solution)/shard_map/ppermute | solution.py:170
  38.5 6.7 %collective-permute-start.18 = (bf16[32,3584]{1,0:T(8,128)(2,1)S(1)}, bf16[32,3584]{1,0:T(8,128)(2,1)S(1)}, u32[]{:S(2)}, u32[]{:S(2)}) collective-permute-start(bf16[32,3584]{1,0:T(8,128)(2,1)S(1)} %add_convert_fusion.6), channel_id=1, source_target_pairs={{0,4},{4,8},{8,12},{12,14},{14,10},{10,6},{6,2},{2,0},{5,1},{9,5},... | collective-permute-start | bytes 688136 | tf_op jit(solution)/shard_map/ppermute | solution.py:170
  42.8 6.1 %collective-permute-start.21 = (bf16[32,3584]{1,0:T(8,128)(2,1)S(1)}, bf16[32,3584]{1,0:T(8,128)(2,1)S(1)}, u32[]{:S(2)}, u32[]{:S(2)}) collective-permute-start(bf16[32,3584]{1,0:T(8,128)(2,1)S(1)} %add_convert_fusion.5), channel_id=1, source_target_pairs={{0,4},{4,8},{8,12},{12,14},{14,10},{10,6},{6,2},{2,0},{5,1},{9,5},... | collective-permute-start | bytes 688136 | tf_op jit(solution)/shard_map/ppermute | solution.py:170
  45.3 6.1 %collective-permute-start.20 = (bf16[32,3584]{1,0:T(8,128)(2,1)S(1)}, bf16[32,3584]{1,0:T(8,128)(2,1)S(1)}, u32[]{:S(2)}, u32[]{:S(2)}) collective-permute-start(bf16[32,3584]{1,0:T(8,128)(2,1)S(1)} %add_convert_fusion.4), channel_id=1, source_target_pairs={{0,4},{4,8},{8,12},{12,14},{14,10},{10,6},{6,2},{2,0},{5,1},{9,5},... | collective-permute-start | bytes 688136 | tf_op jit(solution)/shard_map/ppermute | solution.py:170
  49.0 6.1 %collective-permute-start.24 = (bf16[32,3584]{1,0:T(8,128)(2,1)S(1)}, bf16[32,3584]{1,0:T(8,128)(2,1)S(1)}, u32[]{:S(2)}, u32[]{:S(2)}) collective-permute-start(bf16[32,3584]{1,0:T(8,128)(2,1)S(1)} %add_convert_fusion.3), channel_id=1, source_target_pairs={{0,4},{4,8},{8,12},{12,14},{14,10},{10,6},{6,2},{2,0},{5,1},{9,5},... | collective-permute-start | bytes 688136 | tf_op jit(solution)/shard_map/ppermute | solution.py:170
  51.5 6.1 %collective-permute-start.22 = (bf16[32,3584]{1,0:T(8,128)(2,1)S(1)}, bf16[32,3584]{1,0:T(8,128)(2,1)S(1)}, u32[]{:S(2)}, u32[]{:S(2)}) collective-permute-start(bf16[32,3584]{1,0:T(8,128)(2,1)S(1)} %add_convert_fusion.2), channel_id=1, source_target_pairs={{0,4},{4,8},{8,12},{12,14},{14,10},{10,6},{6,2},{2,0},{5,1},{9,5},... | collective-permute-start | bytes 688136 | tf_op jit(solution)/shard_map/ppermute | solution.py:170
  55.2 6.1 %collective-permute-start.25 = (bf16[32,3584]{1,0:T(8,128)(2,1)S(1)}, bf16[32,3584]{1,0:T(8,128)(2,1)S(1)}, u32[]{:S(2)}, u32[]{:S(2)}) collective-permute-start(bf16[32,3584]{1,0:T(8,128)(2,1)S(1)} %add_convert_fusion.1), channel_id=1, source_target_pairs={{0,4},{4,8},{8,12},{12,14},{14,10},{10,6},{6,2},{2,0},{5,1},{9,5},... | collective-permute-start | bytes 688136 | tf_op jit(solution)/shard_map/ppermute | solution.py:170
  57.5 3.8 %collective-permute-start.23 = (bf16[32,3584]{1,0:T(8,128)(2,1)S(1)}, bf16[32,3584]{1,0:T(8,128)(2,1)S(1)}, u32[]{:S(2)}, u32[]{:S(2)}) collective-permute-start(bf16[32,3584]{1,0:T(8,128)(2,1)S(1)} %collective-permute-done.22), channel_id=1, source_target_pairs={{0,1},{1,0},{2,3},{3,2},{4,5},{5,4},{6,7},{7,6},{8,9},{9,8},{10,11... | collective-permute-start | bytes 688136 | tf_op jit(solution)/shard_map/ppermute | solution.py:171
